TPU v7x, 32 devices: a whole 2x2x4 slice. The times are simulated.
32 devices in a mesh: grp: 2 (over y), bl: 16 (over z, x, core).
Axes of the slice: x: 2, y: 2, z: 4, core: 2. Of those that a mesh axis runs over, the one named last changes fastest.
Arguments:
- measured_correlation: float32 [2, 480, 32, 128], P(None, ('grp', 'bl')), parts along dimension 1, may hold values from -6 to 6
- model_response: bfloat16 [40, 2, 480, 32, 128], P(None, None, ('grp', 'bl')), parts along dimension 2, may hold values from -1 to 1
- validity_mask: int32 [480, 32, 128], P(('grp', 'bl')), parts along dimension 0, may hold values from 0 to 1, as said below
- leading_station_index: int32 [480], P(('grp', 'bl')), parts along dimension 0, may hold values from 0 to 62, as said below
- trailing_station_index: int32 [480], P(('grp', 'bl')), parts along dimension 0, may hold values from 1 to 63, as said below
- gain_real_part: float32 [5120, 128], P(('grp', 'bl')), parts along dimension 0, may hold values from 0.5 to 1.5
- gain_imaginary: float32 [5120, 128], P(('grp', 'bl')), parts along dimension 0, may hold values from -1.5 to 1.5
Outputs:
- gains: float32 [2, 5120, 128], P(None, ('grp', 'bl')), parts along dimension 1
- residual: float32 [2, 480, 32, 128], P(None, ('grp', 'bl')), parts along dimension 1
There are 2 independent parts, one for each index of `grp`. A program takes and returns all parts, laid end to end along the dimension named above; each array names one. Nothing has to cross between parts.
Inputs may be any that keep to these rules, and one draw needn't show every extreme that they name: leading_station_index[b] < trailing_station_index[b]; no pair of stations appears twice; stations 0 and 63 form a baseline. `trailing_station_index`: see leading_station_index. `validity_mask`: whole time samples of a baseline may be flagged, at rates that differ between the baselines of different devices.
All inputs are finite; a program needn't handle non-finite values.
Results may differ from a plain program's by a relative error of at most 0.0003.
Values sent between devices are 32-bit elements; how exact they have to be, the bound alone decides.
No kernel may reach another device: no remote copies, remote signals or barrier semaphores. Data moves between devices by JAX's collectives and lax.ppermute only.
A program may use at most 64 MiB of HBM per device.

v0:
```python
import jax
import jax.numpy as jnp
from jax import lax
from jax.sharding import PartitionSpec as P

STATIONS = 64
SOURCE_COUNT = 40
ITERS = 2


ridge = 1.0


def block_pass(full_re, full_im, vis_blk, coh_blk, weight, first, second, want_sums):
    ar = jnp.transpose(full_re[first], (1, 0, 2))
    ai = jnp.transpose(full_im[first], (1, 0, 2))
    br = jnp.transpose(full_re[second], (1, 0, 2))
    bi = jnp.transpose(full_im[second], (1, 0, 2))
    mr = coh_blk[:, 0].astype(jnp.float32)
    mi = coh_blk[:, 1].astype(jnp.float32)
    hr = (ar * br + ai * bi)[:, :, None]
    hi = (ai * br - ar * bi)[:, :, None]
    pred_re = hr * mr - hi * mi
    pred_im = hr * mi + hi * mr
    res_re = weight * (vis_blk[0] - jnp.sum(pred_re, 0))
    res_im = weight * (vis_blk[1] - jnp.sum(pred_im, 0))
    residual = jnp.stack([res_re, res_im])
    if not want_sums:
        return (residual, None)
    x_re = res_re[None] + weight[None] * pred_re
    x_im = res_im[None] + weight[None] * pred_im
    bre = br[:, :, None]
    bim = bi[:, :, None]
    are = ar[:, :, None]
    aim = ai[:, :, None]
    z_re = mr * bre + mi * bim
    z_im = mi * bre - mr * bim
    first_re = jnp.sum(z_re * x_re + z_im * x_im, 2)
    first_im = jnp.sum(z_re * x_im - z_im * x_re, 2)
    u_re = mr * are - mi * aim
    u_im = mr * aim + mi * are
    second_re = jnp.sum(u_re * x_re + u_im * x_im, 2)
    second_im = jnp.sum(u_im * x_re - u_re * x_im, 2)
    power = jnp.sum(weight[None] * (mr * mr + mi * mi), 2)
    den_first = power * (br * br + bi * bi)
    den_second = power * (ar * ar + ai * ai)
    stations = jnp.arange(STATIONS, dtype=jnp.int32)
    onehot_first = (first[:, None] == stations[None, :]).astype(jnp.float32)
    onehot_second = (second[:, None] == stations[None, :]).astype(jnp.float32)
    terms_first = jnp.stack([first_re, first_im, den_first])
    terms_second = jnp.stack([second_re, second_im, den_second])
    sums = jnp.einsum("bs,cdbf->csdf", onehot_first, terms_first, precision=lax.Precision.HIGHEST)
    sums = sums + jnp.einsum(
        "bs,cdbf->csdf", onehot_second, terms_second, precision=lax.Precision.HIGHEST
    )
    return (residual, sums)


def update(gre, gim, sums):
    denom = sums[2] + ridge
    return (0.5 * (gre + sums[0] / denom), 0.5 * (gim + sums[1] / denom))


def body(
    measured_correlation,
    model_response,
    validity_mask,
    leading_station_index,
    trailing_station_index,
    gain_real_part,
    gain_imaginary,
):
    weight = validity_mask.astype(jnp.float32)
    rows = gain_real_part.shape[0]
    channels = gain_real_part.shape[1]
    full_re, full_im = (
        lax.all_gather(gain_real_part, "bl", axis=0, tiled=True),
        lax.all_gather(gain_imaginary, "bl", axis=0, tiled=True),
    )
    own_re, own_im = (gain_real_part, gain_imaginary)
    for step in range(ITERS):
        unused, sums = block_pass(
            full_re.reshape(STATIONS, SOURCE_COUNT, channels),
            full_im.reshape(STATIONS, SOURCE_COUNT, channels),
            measured_correlation,
            model_response,
            weight,
            leading_station_index,
            trailing_station_index,
            True,
        )
        sums = sums.reshape(3, STATIONS * SOURCE_COUNT, channels)
        totals = lax.psum(sums, "bl")
        full_re, full_im = update(full_re, full_im, totals)
        offset = lax.axis_index("bl") * rows
        own_re = lax.dynamic_slice_in_dim(full_re, offset, rows, 0)
        own_im = lax.dynamic_slice_in_dim(full_im, offset, rows, 0)
    residual, unused = block_pass(
        full_re.reshape(STATIONS, SOURCE_COUNT, channels),
        full_im.reshape(STATIONS, SOURCE_COUNT, channels),
        measured_correlation,
        model_response,
        weight,
        leading_station_index,
        trailing_station_index,
        False,
    )
    return (jnp.stack([own_re, own_im]), residual)


def solution(mesh):
    in_specs = (
        P(None, ("grp", "bl"), None, None),
        P(None, None, ("grp", "bl"), None, None),
        P(("grp", "bl"), None, None),
        P(("grp", "bl")),
        P(("grp", "bl")),
        P(("grp", "bl"), None),
        P(("grp", "bl"), None),
    )
    out_specs = (P(None, ("grp", "bl"), None), P(None, ("grp", "bl"), None, None))
    return jax.shard_map(body, mesh=mesh, in_specs=in_specs, out_specs=out_specs, check_vma=False)
```

profile of v0, /device:TPU:9, one launch (start us, length us, event | category | flops | bytes accessed | tf_op | source)
XLA Modules:
  0.0 426.4 jit_solution(15628050966828318752)
XLA Ops:
  7.2 0.7 all-gather.3.cloned.1.call-update
  8.0 0.7 all-gather.5.cloned.1.call-update
  8.7 1.8 convert_element_type.27
  10.5 0.7 compare_select_fusion
  11.2 38.6 %all-gather.3.cloned.1.call-done = f32[2560,128]{1,0:T(8,128)} async-done(((f32[160,128]{1,0:T(8,128)}), f32[2560,128]{1,0:T(8,128)}) %all-gather.3.cloned.1.call-update) | async-done | bytes 1310736 | tf_op jit(solution)/shard_map/all_gather | solution.py:77
  49.8 1.9 gather_fusion
  51.7 38.0 %all-gather.5.cloned.1.call-done = f32[2560,128]{1,0:T(8,128)} async-done(((f32[160,128]{1,0:T(8,128)}), f32[2560,128]{1,0:T(8,128)}) %all-gather.5.cloned.1.call-update) | async-done | bytes 1310736 | tf_op jit(solution)/shard_map/all_gather | solution.py:78
  89.7 1.9 gather_fusion.1
  91.6 1.9 gather_fusion.2
  93.5 1.9 gather_fusion.3
  95.6 0.2 multiply_add_fusion.5
  95.9 7.1 %fusion.22 = (f32[15,32,128]{2,1,0:T(8,128)S(1)}, f32[15,32,128]{2,1,0:T(8,128)S(1)}) fusion(f32[40,15,128]{2,1,0:T(8,128)S(1)} %get-tuple-element.30, f32[40,15,128]{2,1,0:T(8,128)S(1)} %get-tuple-element.29, bf16[40,2,15,32,128]{4,3,2,1,0:T(8,128)(2,1)} %param.8), kind=kLoop, calls=%fused_computation.76 | loop fusion | flops 24453120 | bytes 10936320 | tf_op jit(solution)/shard_map/reduce_sum | solution.py:25
  103.1 0.1 fusion.61
  103.2 20.8 %add_reduce_fusion.2 = (f32[40,15,128]{2,1,0:T(8,128)S(1)}, f32[40,15,128]{2,1,0:T(8,128)S(1)}, f32[40,15,128]{2,1,0:T(8,128)S(1)}, f32[40,15,128]{2,1,0:T(8,128)S(1)}, f32[40,15,128]{2,1,0:T(8,128)S(1)}) fusion(f32[40,15,128]{2,1,0:T(8,128)S(1)} %bitcast.230, f32[40,15,128]{2,1,0:T(8,128)S(1)} %bitcast.231, f32[15,32,128]{2,1,0:T(8,128)S(1)} %get-tuple-element.36, ...), kind=kLoop, calls=%fused_computation.68 | loop fusion | flops 110208000 | bytes 13946880 | tf_op jit(solution)/shard_map/reduce_sum | solution.py:42
  124.0 0.2 multiply_bitcast_fusion.2
  124.3 0.5 copy-done.3
  124.8 1.8 fusion.35
  126.6 2.0 add_bitcast_fusion.1
  128.7 4.2 copy.17
  132.9 107.0 %all-reduce.3.cloned.1.call-done = f32[3,2560,128]{2,1,0:T(8,128)} async-done(((f32[3,2560,128]{2,1,0:T(8,128)}), f32[3,2560,128]{2,1,0:T(8,128)}) %all-reduce.3.cloned.1.call-update) | async-done | bytes 3932176 | tf_op jit(solution)/shard_map/psum | solution.py:93
  240.0 4.0 fusion.34
  244.0 2.7 gather_fusion.5
  246.7 2.6 gather_fusion.7
  249.3 1.3 gather_fusion.6
  250.6 1.3 gather_fusion.4
  251.8 1.1 copy.84
  252.9 1.0 copy.85
  254.0 1.0 copy.86
  255.0 1.7 multiply_add_fusion.4
  256.7 1.0 copy.87
  257.8 6.5 %fusion.20 = (f32[15,32,128]{2,1,0:T(8,128)S(1)}, f32[15,32,128]{2,1,0:T(8,128)S(1)}) fusion(f32[40,15,128]{2,1,0:T(8,128)S(1)} %get-tuple-element.28, f32[40,15,128]{2,1,0:T(8,128)S(1)} %get-tuple-element.27, bf16[40,2,15,32,128]{4,3,2,1,0:T(8,128)(2,1)} %param.8), kind=kLoop, calls=%fused_computation.74 | loop fusion | flops 24453120 | bytes 10936320 | tf_op jit(solution)/shard_map/reduce_sum | solution.py:25
  264.3 0.1 fusion.62
  264.5 18.4 %add_reduce_fusion = (f32[40,15,128]{2,1,0:T(8,128)S(1)}, f32[40,15,128]{2,1,0:T(8,128)S(1)}, f32[40,15,128]{2,1,0:T(8,128)S(1)}, f32[40,15,128]{2,1,0:T(8,128)S(1)}) fusion(f32[40,15,128]{2,1,0:T(8,128)S(1)} %bitcast.238, f32[40,15,128]{2,1,0:T(8,128)S(1)} %bitcast.239, f32[15,32,128]{2,1,0:T(8,128)S(1)} %get-tuple-element.34, ...), kind=kLoop, calls=%fused_computation.62 | loop fusion | flops 97996800 | bytes 13639680 | tf_op jit(solution)/shard_map/reduce_sum | solution.py:42
  282.8 1.8 fusion.46
  284.7 2.0 add_bitcast_fusion
  286.8 4.2 copy.22
  291.0 107.5 %all-reduce.5.cloned.1.call-done = f32[3,2560,128]{2,1,0:T(8,128)} async-done(((f32[3,2560,128]{2,1,0:T(8,128)}), f32[3,2560,128]{2,1,0:T(8,128)}) %all-reduce.5.cloned.1.call-update) | async-done | bytes 3932176 | tf_op jit(solution)/shard_map/psum | solution.py:93
  398.5 3.9 fusion.28
  402.4 1.9 gather_fusion.10
  404.3 1.9 gather_fusion.11
  406.2 1.9 gather_fusion.8
  408.1 1.9 gather_fusion.9
  410.0 0.9 dynamic-slice_bitcast_fusion.1
  410.9 0.9 dynamic-slice_bitcast_fusion
  412.0 6.2 %fusion.16 = (f32[15,32,128]{2,1,0:T(8,128)S(1)}, f32[15,32,128]{2,1,0:T(8,128)S(1)}) fusion(f32[40,15,128]{2,1,0:T(8,128)S(1)} %copy.24, f32[40,15,128]{2,1,0:T(8,128)S(1)} %copy.23, bf16[40,2,15,32,128]{4,3,2,1,0:T(8,128)(2,1)} %param.8), kind=kLoop, calls=%fused_computation.58 | loop fusion | flops 24453120 | bytes 10936320 | tf_op jit(solution)/shard_map/reduce_sum | solution.py:25
  418.2 0.1 fusion.64
  418.3 0.8 pad_maximum_fusion
  419.2 0.7 pad_maximum_fusion.1
  (46 shorter events, 0.8 us)
Async XLA Ops:
  7.2 95.9 %copy-start.2 = (s32[15,32,128]{2,1,0:T(8,128)S(1)}, s32[15,32,128]{2,1,0:T(8,128)}, u32[]{:S(2)}) copy-start(s32[15,32,128]{2,1,0:T(8,128)} %param.9) | copy-start | bytes 737284
  7.2 95.9 %copy-start.1 = (f32[2,15,32,128]{3,2,1,0:T(8,128)S(1)}, f32[2,15,32,128]{3,2,1,0:T(8,128)}, u32[]{:S(2)}) copy-start(f32[2,15,32,128]{3,2,1,0:T(8,128)} %param.7) | copy-start | bytes 1474564
  7.2 42.6 %all-gather.3.cloned.1.call-start = ((), (), s32[]{:S(2)}) async-start(), calls=%async_computation | async-start | bytes 1392640 | tf_op jit(solution)/shard_map/all_gather | solution.py:77
  7.9 81.8 %all-gather.5.cloned.1.call-start = ((), (), s32[]{:S(2)}) async-start(), calls=%async_computation.1 | async-start | bytes 1392640 | tf_op jit(solution)/shard_map/all_gather | solution.py:78
  8.7 231.3 %all-reduce.3.cloned.1.call-start = ((), (), s32[]{:S(2)}) async-start(), calls=%async_computation.2 | async-start | bytes 7864320 | tf_op jit(solution)/shard_map/psum | solution.py:93
  8.7 94.5 %slice-start = ((s8[9830400]{0:T(1024)(128)(4,1)}), s8[1441792]{0:T(1024)(128)(4,1)S(1)}, s32[]{:S(2)}) async-start(s8[9830400]{0:T(1024)(128)(4,1)} %bitcast.208), calls=%async_computation.4 | async-start | bytes 2883584
  95.4 7.8 %copy-start.5 = (f32[15,32,128]{2,1,0:T(8,128)S(1)}, f32[15,32,128]{2,1,0:T(8,128)}, u32[]{:S(2)}) copy-start(f32[15,32,128]{2,1,0:T(8,128)} %convert_element_type.27) | copy-start | bytes 737284
  95.6 7.6 %slice-start.1 = ((s8[9830400]{0:T(1024)(128)(4,1)}), s8[4194304]{0:T(1024)(128)(4,1)S(1)}, s32[]{:S(2)}) async-start(s8[9830400]{0:T(1024)(128)(4,1)} %bitcast.208), calls=%async_computation.5 | async-start | bytes 8388608
  95.9 7.3 %slice-start.2 = ((s8[9830400]{0:T(1024)(128)(4,1)}), s8[4194304]{0:T(1024)(128)(4,1)S(1)}, s32[]{:S(2)}) async-start(s8[9830400]{0:T(1024)(128)(4,1)} %bitcast.208), calls=%async_computation.6 | async-start | bytes 8388608
  103.0 21.7 %copy-start.7 = (s32[15]{0:T(128)S(1)}, s32[15]{0:T(128)}, u32[]{:S(2)}) copy-start(s32[15]{0:T(128)} %param.10) | copy-start | bytes 184
  103.2 23.4 %copy-start.8 = (s32[15]{0:T(128)S(1)}, s32[15]{0:T(128)}, u32[]{:S(2)}) copy-start(s32[15]{0:T(128)} %param.11) | copy-start | bytes 184
  124.0 0.7 copy-start.3
  126.6 113.4 %copy-start.4 = (f32[2560,128]{1,0:T(8,128)S(1)}, f32[2560,128]{1,0:T(8,128)}, u32[]{:S(2)}) copy-start(f32[2560,128]{1,0:T(8,128)} %all-gather.3.cloned.1.call-done) | copy-start | bytes 3932164
  132.9 265.6 %all-reduce.5.cloned.1.call-start = ((), (), s32[]{:S(2)}) async-start(), calls=%async_computation.3 | async-start | bytes 7864320 | tf_op jit(solution)/shard_map/psum | solution.py:93
  244.0 20.4 %slice-start.3 = ((s8[9830400]{0:T(1024)(128)(4,1)}), s8[1441792]{0:T(1024)(128)(4,1)S(1)}, s32[]{:S(2)}) async-start(s8[9830400]{0:T(1024)(128)(4,1)} %bitcast.210), calls=%async_computation.7 | async-start | bytes 2883584
  251.8 12.6 %copy-start.6 = (f32[15,32,128]{2,1,0:T(8,128)S(1)}, f32[15,32,128]{2,1,0:T(8,128)}, u32[]{:S(2)}) copy-start(f32[15,32,128]{2,1,0:T(8,128)} %convert_element_type.27) | copy-start | bytes 737284
  255.0 9.5 %slice-start.4 = ((s8[9830400]{0:T(1024)(128)(4,1)}), s8[4194304]{0:T(1024)(128)(4,1)S(1)}, s32[]{:S(2)}) async-start(s8[9830400]{0:T(1024)(128)(4,1)} %bitcast.210), calls=%async_computation.8 | async-start | bytes 8388608
  257.8 6.7 %slice-start.5 = ((s8[9830400]{0:T(1024)(128)(4,1)}), s8[4194304]{0:T(1024)(128)(4,1)S(1)}, s32[]{:S(2)}) async-start(s8[9830400]{0:T(1024)(128)(4,1)} %bitcast.210), calls=%async_computation.9 | async-start | bytes 8388608
  284.7 113.8 %copy-start = (f32[2560,128]{1,0:T(8,128)S(1)}, f32[2560,128]{1,0:T(8,128)}, u32[]{:S(2)}) copy-start(f32[2560,128]{1,0:T(8,128)} %get-tuple-element.24) | copy-start | bytes 3932164
Sparse Core Ops, SparseCore 0:
  10.3 39.4 all-gather.2
  52.1 37.6 all-gather.4
  133.0 106.9 all-reduce.2
  291.1 107.3 all-reduce.4
where the time goes:
time: 430 us; the launch traced here: 426 us
  waiting for transfers between devices  293 us (68%)
  other arithmetic  73.4 us (17%)
  local copies, waits for them, and re-layouts  38.2 us (9%)
  between operations  14.2 us (3%)
  matrix products  7.78 us (2%)
    psum x2, waiting for transfers between devices, body(): totals = lax.psum(sums, 'bl')  215 us
    reduce_sum x2, other arithmetic, block_pass(): second_re = jnp.sum(u_re * x_re + u_im * x_im, 2)  39.1 us
    all_gather x1, waiting for transfers between devices, body(): lax.all_gather(gain_real_part, 'bl', axis=0, tiled=True)  38.6 us
    all_gather x1, waiting for transfers between devices, body(): lax.all_gather(gain_imaginary, 'bl', axis=0, tiled=True)  38 us
    reduce_sum x3, other arithmetic, block_pass(): res_re = weight * (vis_blk[0] - jnp.sum(pred_re, 0))  19.7 us
  transfers between devices with their start and end apart: 4, of which 4 were waited for; matrix products, arithmetic and copies ran while one was open for 1% of the time, Pallas kernels for 0%

commit v1 on v0

v1 whole, which is shorter than its diff:
```python
import functools

import jax
import jax.numpy as jnp
from jax import lax
from jax.experimental import pallas as pl
from jax.experimental.pallas import tpu as pltpu
from jax.sharding import PartitionSpec as P

STATIONS = 64
SOURCE_COUNT = 40
ITERS = 2
ROWS = 16

ridge = 1.0
F32 = jnp.float32
BF16 = jnp.bfloat16
VMEM_LIMIT = 48 * 1024 * 1024


def swap(x):
    return pltpu.roll(x, x.shape[-1] // 2, axis=x.ndim - 1)


def lower(shape):
    return lax.broadcasted_iota(jnp.int32, shape, len(shape) - 1) < shape[-1] // 2


def cross(a, b):
    lo = lower(a.shape)
    return jnp.where(lo, a, swap(b)), jnp.where(lo, swap(a), b)


def three(x):
    hi = x.astype(BF16)
    rest = x - hi.astype(F32)
    mid = rest.astype(BF16)
    return hi, mid, (rest - mid.astype(F32)).astype(BF16)


def pick(onehot, x, dims):
    return sum(
        lax.dot_general(onehot, part, (dims, ((), ())), preferred_element_type=F32)
        for part in three(x)
    )


def pack_kernel(n, dpc, me_ref, first_ref, second_ref, re_ref, im_ref, *rest):
    outs, halves = rest[:n], rest[n]
    per = re_ref.shape[0] // SOURCE_COUNT
    me = me_ref[0]
    a, b = cross(re_ref[...], im_ref[...])
    halves[0] = a
    halves[1] = b
    base = lax.rem(me, 2) * per
    lane = lax.broadcasted_iota(jnp.int32, (1, dpc * 128), 1)
    sub = lax.broadcasted_iota(jnp.int32, (2 * per, 128), 0)
    count = first_ref.shape[0]
    for o in range(n):
        peer = jnp.bitwise_xor(me, o)
        k, c = lax.div(peer, 2), lax.rem(peer, 2)
        marks = jnp.zeros((1, dpc * 128), F32)
        for r in range(count):
            marks = jnp.where(lane == o * 2 * ROWS + r, (first_ref[r] + 1).astype(F32), marks)
            marks = jnp.where(lane == o * 2 * ROWS + ROWS + r, (second_ref[r] + 1).astype(F32), marks)
        for dd in range(dpc):
            cols = slice(dd * 128, (dd + 1) * 128)
            block = jnp.where(sub == per - base, marks[:, cols], 0.0)
            for s in range(per):
                row = halves[c, pl.ds(s * SOURCE_COUNT + k * dpc + dd, 1), :]
                block = jnp.where(sub == base + s, row, block)
            outs[o][:, cols] = block


def power_kernel(n, dpc, me_ref, model_ref, mask_ref, *rest):
    outs, local, = rest[:n], rest[n]
    b = pl.program_id(0)

    @pl.when(b == 0)
    def _():
        local[...] = jnp.zeros_like(local)

    weight = mask_ref[0].astype(F32)
    for d in range(SOURCE_COUNT):
        mr = model_ref[d, 0, 0].astype(F32)
        mi = model_ref[d, 1, 0].astype(F32)
        local[d, pl.ds(b, 1), :] = jnp.sum(weight * (mr * mr + mi * mi), axis=0, keepdims=True)

    @pl.when(b == pl.num_programs(0) - 1)
    def _():
        me = me_ref[0]
        for o in range(n):
            peer = jnp.bitwise_xor(me, o)
            k, c = lax.div(peer, 2), lax.rem(peer, 2)
            for dd in range(dpc):
                full = local[k * dpc + dd]
                x0, x1 = cross(full[:8], full[8:])
                outs[o][:, dd * 128 : (dd + 1) * 128] = jnp.where(c == 0, x0, x1)


def own_first_kernel(n, dpc, me_ref, *rest):
    ins, (g_ref, onehot_ref), outs = rest[:n], rest[n : n + 2], rest[n + 2 :]
    me = me_ref[0]
    width = dpc * 128
    per = STATIONS // n
    row = lax.broadcasted_iota(jnp.int32, (2 * per, width), 0)
    marks = jnp.zeros((2 * per, width), F32)
    for m in range(n // 2):
        total = jnp.zeros((2 * per, width), F32)
        for o in (2 * m, 2 * m + 1):
            peer = jnp.bitwise_xor(me, o)
            mine = lax.div(row, per) == lax.rem(peer, 2)
            x = ins[o][...]
            total = total + jnp.where(mine, x, 0.0)
            marks = marks + jnp.where(mine, 0.0, x)
        chip = lax.div(jnp.bitwise_xor(me, 2 * m), 2)
        g_ref[pl.ds(pl.multiple_of(chip * 2 * per, 2 * per), 2 * per), :] = total
    marks = jnp.sum(marks, axis=0, keepdims=True)[:, : n * 2 * ROWS]
    station = lax.broadcasted_iota(jnp.int32, (STATIONS, n * 2 * ROWS), 0)
    onehot = jnp.where(station + 1 == marks.astype(jnp.int32), 1.0, 0.0).astype(BF16)
    onehot_ref[...] = onehot
    sel = pick(onehot, g_ref[...], ((0,), (0,)))
    for o in range(n):
        outs[o][...] = sel[o * 2 * ROWS : (o + 1) * 2 * ROWS]


def own_kernel(n, dpc, last, me_ref, g_in, onehot_ref, *rest):
    sums, powers, sels = rest[:n], rest[n : 2 * n], rest[2 * n : 3 * n]
    rest = rest[3 * n :]
    g_out, outs, terms = rest[0], rest[1 : n + 1], rest[n + 1]
    width = dpc * 128
    lo = lower((ROWS, 128))
    lo8 = lower((8, 128))
    sign = jnp.where(lo, -1.0, 1.0)
    for o in range(n):
        for dd in range(dpc):
            cols = slice(dd * 128, (dd + 1) * 128)
            B = sums[o][:, cols]
            W = powers[o][:, cols]
            Wx = swap(W)
            W = jnp.concatenate([jnp.where(lo8, W, Wx), jnp.where(lo8, Wx, W)], 0)
            p = sels[o][:ROWS, cols]
            q = sels[o][ROWS:, cols]
            Bx, px, qx = swap(B), swap(p), swap(q)
            Brr, Bii = jnp.where(lo, B, Bx), jnp.where(lo, Bx, B)
            first = Brr * q + sign * Bii * qx
            second = Brr * p - sign * Bii * px
            q2, p2 = q * q, p * p
            r = o * 2 * ROWS
            terms[r : r + ROWS, cols] = first
            terms[r + ROWS : r + 2 * ROWS, cols] = second
            dcols = slice(width + dd * 128, width + (dd + 1) * 128)
            terms[r : r + ROWS, dcols] = W * (q2 + swap(q2))
            terms[r + ROWS : r + 2 * ROWS, dcols] = W * (p2 + swap(p2))
    onehot = onehot_ref[...]
    total = pick(onehot, terms[...], ((1,), (0,)))
    g = 0.5 * (g_in[...] + total[:, :width] / (total[:, width:] + ridge))
    g_out[...] = g
    sel = pick(onehot, g, ((0,), (0,)))
    for o in range(n):
        outs[o][: 2 * ROWS, :] = sel[o * 2 * ROWS : (o + 1) * 2 * ROWS]
    if last:
        per = STATIONS // n
        line = lax.broadcasted_iota(jnp.int32, (n * 8, STATIONS), 0)
        col = lax.broadcasted_iota(jnp.int32, (n * 8, STATIONS), 1)
        slot, r = lax.div(line, 8), lax.rem(line, 8)
        want = jnp.bitwise_xor(me_ref[0], slot) * per + r
        mine = jnp.where((col == want) & (r < per), 1.0, 0.0).astype(BF16)
        own = pick(mine, g, ((1,), (0,)))
        for o in range(n):
            outs[o][2 * ROWS :, :] = own[o * 8 : (o + 1) * 8]


def unpack_rows(me, ins, m, rows, cols):
    even = lax.rem(me, 2) == 0
    a, b = ins[2 * m][rows, cols], ins[2 * m + 1][rows, cols]
    return cross(jnp.where(even, a, b), jnp.where(even, b, a))


def load_products(n, dpc, me, ins, hre, him):
    for m in range(n // 2):
        k = lax.div(jnp.bitwise_xor(me, 2 * m), 2)
        for dd in range(dpc):
            cols = slice(dd * 128, (dd + 1) * 128)
            pr, pi = unpack_rows(me, ins, m, slice(0, ROWS), cols)
            qr, qi = unpack_rows(me, ins, m, slice(ROWS, 2 * ROWS), cols)
            hre[k * dpc + dd] = pr * qr + pi * qi
            him[k * dpc + dd] = pi * qr - pr * qi


def predict(b, model_ref, vis_ref, mask_ref, hre, him):
    acc_re = vis_ref[0, 0]
    acc_im = vis_ref[1, 0]

    def step(i, acc):
        acc_re, acc_im = acc
        for u in range(8):
            d = i * 8 + u
            mr = model_ref[d, 0, 0].astype(F32)
            mi = model_ref[d, 1, 0].astype(F32)
            hr = hre[d, pl.ds(b, 1), :]
            hi = him[d, pl.ds(b, 1), :]
            acc_re = acc_re - (hr * mr - hi * mi)
            acc_im = acc_im - (hr * mi + hi * mr)
        return acc_re, acc_im

    acc_re, acc_im = lax.fori_loop(0, SOURCE_COUNT // 8, step, (acc_re, acc_im))
    weight = mask_ref[0].astype(F32)
    return weight * acc_re, weight * acc_im


def pass_kernel(n, dpc, me_ref, model_ref, vis_ref, mask_ref, power_ref, *rest):
    ins, outs = rest[:n], rest[n : 2 * n]
    hre, him, cre, cim, halves = rest[2 * n :]
    b = pl.program_id(0)
    me = me_ref[0]

    @pl.when(b == 0)
    def _():
        load_products(n, dpc, me, ins, hre, him)
        cre[...] = jnp.zeros_like(cre)
        cim[...] = jnp.zeros_like(cim)

    res_re, res_im = predict(b, model_ref, vis_ref, mask_ref, hre, him)

    def step(i, carry):
        for u in range(8):
            d = i * 8 + u
            mr = model_ref[d, 0, 0].astype(F32)
            mi = model_ref[d, 1, 0].astype(F32)
            cre[d, pl.ds(b, 1), :] = jnp.sum(mr * res_re + mi * res_im, axis=0, keepdims=True)
            cim[d, pl.ds(b, 1), :] = jnp.sum(mr * res_im - mi * res_re, axis=0, keepdims=True)
        return carry

    lax.fori_loop(0, SOURCE_COUNT // 8, step, 0)

    @pl.when(b == pl.num_programs(0) - 1)
    def _():
        for d in range(SOURCE_COUNT):
            w = power_ref[d]
            x0, x1 = cross(cre[d] + hre[d] * w, cim[d] + him[d] * w)
            halves[0, d] = x0
            halves[1, d] = x1
        for o in range(n):
            peer = jnp.bitwise_xor(me, o)
            k, c = lax.div(peer, 2), lax.rem(peer, 2)
            for dd in range(dpc):
                outs[o][:, dd * 128 : (dd + 1) * 128] = halves[c, k * dpc + dd]


def last_kernel(n, dpc, me_ref, model_ref, vis_ref, mask_ref, *rest):
    ins, (res_ref, gains_ref), (hre, him) = rest[:n], rest[n : n + 2], rest[n + 2 :]
    b = pl.program_id(0)
    me = me_ref[0]

    @pl.when(b == 0)
    def _():
        load_products(n, dpc, me, ins, hre, him)
        per = STATIONS // n
        for m in range(n // 2):
            k = lax.div(jnp.bitwise_xor(me, 2 * m), 2)
            for dd in range(dpc):
                cols = slice(dd * 128, (dd + 1) * 128)
                re, im = unpack_rows(me, ins, m, slice(2 * ROWS, 2 * ROWS + 8), cols)
                for s in range(per):
                    at = s * SOURCE_COUNT + k * dpc + dd
                    gains_ref[0, pl.ds(at, 1), :] = re[s : s + 1]
                    gains_ref[1, pl.ds(at, 1), :] = im[s : s + 1]

    res_re, res_im = predict(b, model_ref, vis_ref, mask_ref, hre, him)
    res_ref[0, 0] = res_re
    res_ref[1, 0] = res_im


SMEM = pl.BlockSpec(memory_space=pltpu.SMEM)


def whole(shape):
    return pl.BlockSpec(shape, lambda *_: (0,) * len(shape))


def spec_like(x):
    return whole(x.shape)


def shape(*dims, dtype=F32):
    return jax.ShapeDtypeStruct(dims, dtype)


def exchange(n, parts):
    done = [parts[0]]
    for o in range(1, n):
        done.append(lax.ppermute(parts[o], "bl", [(i, i ^ o) for i in range(n)]))
    return done


def fast_body(n, vis, model, mask, first, second, gre, gim):
    dpc = SOURCE_COUNT // (n // 2)
    width = dpc * 128
    pairs, times, channels = mask.shape
    me = lax.axis_index("bl").astype(jnp.int32).reshape(1)
    params = pltpu.CompilerParams(vmem_limit_bytes=VMEM_LIMIT)
    plane = (SOURCE_COUNT, ROWS, channels)

    per_model = pl.BlockSpec((SOURCE_COUNT, 2, 1, times, channels), lambda b: (0, 0, b, 0, 0))
    per_vis = pl.BlockSpec((2, 1, times, channels), lambda b: (0, b, 0, 0))
    per_mask = pl.BlockSpec((1, times, channels), lambda b: (b, 0, 0))

    def call(kernel, args, specs, outs, scratch=(), grid=()):
        out_specs = [o[1] if isinstance(o, tuple) else whole(o.shape) for o in outs]
        out_shape = [o[0] if isinstance(o, tuple) else o for o in outs]
        return pl.pallas_call(
            functools.partial(kernel, n, dpc),
            grid=grid,
            in_specs=specs,
            out_specs=out_specs,
            out_shape=out_shape,
            scratch_shapes=list(scratch),
            compiler_params=params,
        )(*args)

    start_rows = 2 * STATIONS // n
    packed = call(
        pack_kernel,
        (me, first, second, gre, gim),
        [SMEM, SMEM, SMEM, spec_like(gre), spec_like(gim)],
        [shape(start_rows, width)] * n,
        [pltpu.VMEM((2,) + gre.shape, F32)],
    )
    packed = exchange(n, packed)
    power = call(
        power_kernel,
        (me, model, mask),
        [SMEM, per_model, per_mask],
        [shape(8, width)] * n + [shape(*plane)],
        grid=(pairs,),
    )
    powers, power = exchange(n, power[:n]), power[n]
    out = call(
        own_first_kernel,
        (me, *packed),
        [SMEM] + [spec_like(x) for x in packed],
        [shape(STATIONS, width), shape(STATIONS, n * 2 * ROWS, dtype=BF16)]
        + [shape(2 * ROWS, width)] * n,
    )
    g, onehot, sels = out[0], out[1], out[2:]
    full = [pltpu.VMEM(plane, F32)] * 2
    for step in range(ITERS):
        got = exchange(n, sels)
        sums = call(
            pass_kernel,
            (me, model, vis, mask, power, *got),
            [SMEM, per_model, per_vis, per_mask, whole(plane)] + [spec_like(x) for x in got],
            [shape(ROWS, width)] * n,
            full * 2 + [pltpu.VMEM((2,) + plane, F32)],
            grid=(pairs,),
        )
        sums = exchange(n, sums)
        last = step == ITERS - 1
        args = (me, g, onehot, *sums, *powers, *sels)
        out = call(
            lambda n, dpc, *refs: own_kernel(n, dpc, last, *refs),
            args,
            [SMEM] + [spec_like(x) for x in args[1:]],
            [shape(STATIONS, width)] + [shape(2 * ROWS + (8 if last else 0), width)] * n,
            [pltpu.VMEM((n * 2 * ROWS, 2 * width), F32)],
        )
        g, sels = out[0], out[1:]
    got = exchange(n, sels)
    residual, gains = call(
        last_kernel,
        (me, model, vis, mask, *got),
        [SMEM, per_model, per_vis, per_mask] + [spec_like(x) for x in got],
        [(shape(*vis.shape), per_vis), shape(2, *gre.shape)],
        full,
        grid=(pairs,),
    )
    return gains, residual


def block_pass(full_re, full_im, vis_blk, coh_blk, weight, first, second, want_sums):
    ar = jnp.transpose(full_re[first], (1, 0, 2))
    ai = jnp.transpose(full_im[first], (1, 0, 2))
    br = jnp.transpose(full_re[second], (1, 0, 2))
    bi = jnp.transpose(full_im[second], (1, 0, 2))
    mr = coh_blk[:, 0].astype(F32)
    mi = coh_blk[:, 1].astype(F32)
    hr = ar * br + ai * bi
    hi = ai * br - ar * bi
    hr_t, hi_t = hr[:, :, None], hi[:, :, None]
    res_re = weight * (vis_blk[0] - jnp.sum(hr_t * mr - hi_t * mi, 0))
    res_im = weight * (vis_blk[1] - jnp.sum(hr_t * mi + hi_t * mr, 0))
    residual = jnp.stack([res_re, res_im])
    if not want_sums:
        return (residual, None)
    power = jnp.sum(weight[None] * (mr * mr + mi * mi), 2)
    sum_re = jnp.sum(mr * res_re + mi * res_im, 2) + hr * power
    sum_im = jnp.sum(mr * res_im - mi * res_re, 2) + hi * power
    terms_first = jnp.stack([br * sum_re - bi * sum_im, br * sum_im + bi * sum_re, power * (br * br + bi * bi)])
    terms_second = jnp.stack([ar * sum_re + ai * sum_im, ai * sum_re - ar * sum_im, power * (ar * ar + ai * ai)])
    stations = jnp.arange(STATIONS, dtype=jnp.int32)
    onehot_first = (first[:, None] == stations[None, :]).astype(F32)
    onehot_second = (second[:, None] == stations[None, :]).astype(F32)
    exact = lax.Precision.HIGHEST
    sums = jnp.einsum("bs,cdbf->csdf", onehot_first, terms_first, precision=exact)
    sums = sums + jnp.einsum("bs,cdbf->csdf", onehot_second, terms_second, precision=exact)
    return (residual, sums)


def plain_body(vis, model, mask, first, second, gre, gim):
    weight = mask.astype(F32)
    rows, channels = gre.shape
    shaped = (STATIONS, SOURCE_COUNT, channels)
    full_re = lax.all_gather(gre, "bl", axis=0, tiled=True).reshape(shaped)
    full_im = lax.all_gather(gim, "bl", axis=0, tiled=True).reshape(shaped)
    for step in range(ITERS):
        unused, sums = block_pass(full_re, full_im, vis, model, weight, first, second, True)
        totals = lax.psum(sums, "bl")
        denom = totals[2] + ridge
        full_re = 0.5 * (full_re + totals[0] / denom)
        full_im = 0.5 * (full_im + totals[1] / denom)
    residual, unused = block_pass(full_re, full_im, vis, model, weight, first, second, False)
    both = jnp.stack([full_re, full_im]).reshape(2, STATIONS * SOURCE_COUNT, channels)
    return lax.dynamic_slice_in_dim(both, lax.axis_index("bl") * rows, rows, 1), residual


def solution(mesh):
    n = mesh.shape["bl"]
    split = n % 2 == 0 and SOURCE_COUNT % (n // 2) == 0 and STATIONS == 4 * n

    def body(vis, model, mask, first, second, gre, gim):
        if split and mask.shape[0] <= ROWS:
            return fast_body(n, vis, model, mask, first, second, gre, gim)
        return plain_body(vis, model, mask, first, second, gre, gim)

    in_specs = (
        P(None, ("grp", "bl"), None, None),
        P(None, None, ("grp", "bl"), None, None),
        P(("grp", "bl"), None, None),
        P(("grp", "bl")),
        P(("grp", "bl")),
        P(("grp", "bl"), None),
        P(("grp", "bl"), None),
    )
    out_specs = (P(None, ("grp", "bl"), None), P(None, ("grp", "bl"), None, None))
    return jax.shard_map(body, mesh=mesh, in_specs=in_specs, out_specs=out_specs, check_vma=False)
```

time: 430 us -> 272 us (0.63)
  waiting for transfers between devices: 293 us -> 64 us
  starting transfers between devices: 0.16 us -> 144 us
  other arithmetic: 73.4 us -> 0 us
  Pallas kernels: 0 us -> 58.1 us
  local copies, waits for them, and re-layouts: 38.2 us -> 4.08 us
  between operations: 14.2 us -> 0.85 us
  matrix products: 7.78 us -> 0 us
    psum x2 -> x0, waiting for transfers between devices: 215 us -> none  [body(): totals = lax.psum(sums, 'bl')]
    ppermute x0 -> x105, starting transfers between devices: none -> 144 us  [exchange(): done.append(lax.ppermute(parts[o], 'bl', [(i, i ^ o) for i in range(n)]))]
    all_gather x2 -> x0, waiting for transfers between devices: 76.7 us -> none  [the longest x1 38.6 us: body(): lax.all_gather(gain_real_part, 'bl', axis=0, tiled=True)]
    ppermute x0 -> x105, waiting for transfers between devices: none -> 64 us  [exchange(): done.append(lax.ppermute(parts[o], 'bl', [(i, i ^ o) for i in range(n)]))]
    reduce_sum x5 -> x0, other arithmetic: 58.9 us -> none  [the longest x2 39.1 us: block_pass(): second_re = jnp.sum(u_re * x_re + u_im * x_im, 2)]
    pallas_call x0 -> x8, Pallas kernels: none -> 58.1 us  [call(): pl.pallas_call(functools.partial(kernel, n, dpc), grid=grid, in_specs=spe...]
    gather x20 -> x0, local copies, waits for them, and re-layouts: 27.4 us -> none  [the longest x5 7.57 us: block_pass(): bi = jnp.transpose(full_im[second], (1, 0, 2))]
    add x3 -> x0, local copies, waits for them, and re-layouts: 8.42 us -> none  [the longest x2 8.36 us: block_pass(): sums + jnp.einsum('bs,cdbf->csdf', onehot_second, terms_second, precision...]
  transfers between devices with their start and end apart: 4 -> 105, of which waited for: 4 -> 30; matrix products, arithmetic and copies ran while one was open for 1% -> 0% of each run, Pallas kernels for 0% -> 9%
where the time goes in v1:
time: 272 us; the launch traced here: 271 us
  starting transfers between devices  144 us (53%)
  waiting for transfers between devices  64 us (24%)
  Pallas kernels  58.1 us (21%)
  local copies, waits for them, and re-layouts  4.08 us (2%)
    ppermute x105, starting transfers between devices, exchange(): done.append(lax.ppermute(parts[o], 'bl', [(i, i ^ o) for i in range(n)]))  144 us
    ppermute x105, waiting for transfers between devices, exchange(): done.append(lax.ppermute(parts[o], 'bl', [(i, i ^ o) for i in range(n)]))  64 us
    pallas_call x8, Pallas kernels, call(): pl.pallas_call(functools.partial(kernel, n, dpc), grid=grid, in_specs=spe...  58.1 us
  transfers between devices with their start and end apart: 105, of which 30 were waited for; matrix products, arithmetic and copies ran while one was open for 0% of the time, Pallas kernels for 9%

profile of v1, /device:TPU:9, one launch (start us, length us, event | category | flops | bytes accessed | tf_op | source)
XLA Modules:
  0.0 271.0 jit_solution(10216150179855451855)
XLA Ops:
  7.1 1.8 collective-permute-start.4
  11.5 2.3 collective-permute-start.7
  14.2 3.2 %collective-permute-start.9 = (f32[8,640]{1,0:T(8,128)S(1)}, f32[8,640]{1,0:T(8,128)S(1)}, u32[]{:S(2)}, u32[]{:S(2)}) collective-permute-start(f32[8,640]{1,0:T(8,128)S(1)} %get-tuple-element.130), channel_id=1, source_target_pairs={{0,10},{1,11},{2,8},{3,9},{4,14},{5,15},{6,12},{7,13},{8,2},{9,3},... | collective-permute-start | bytes 61448 | tf_op jit(solution)/shard_map/ppermute | solution.py:293
  19.6 2.2 collective-permute-start.13
  23.1 10.9 %shard_map.88 = (f32[8,640]{1,0:T(8,128)S(1)}, f32[8,640]{1,0:T(8,128)S(1)}, f32[8,640]{1,0:T(8,128)S(1)}, f32[8,640]{1,0:T(8,128)S(1)}, f32[8,640]{1,0:T(8,128)...) custom-call(s32[1]{0:T(128)} %bitcast.me_ref.refs_0_, ...), custom_call_target="tpu_custom_call" | custom-call | tf_op jit(solution)/shard_map/pallas_call | solution.py:312
  36.2 3.9 %collective-permute-start.48 = (f32[8,640]{1,0:T(8,128)S(1)}, f32[8,640]{1,0:T(8,128)S(1)}, u32[]{:S(2)}, u32[]{:S(2)}) collective-permute-start(f32[8,640]{1,0:T(8,128)S(1)} %get-tuple-element.175), channel_id=1, source_target_pairs={{0,4},{1,5},{2,6},{3,7},{4,0},{5,1},{6,2},{7,3},{8,12},{9,13},{10,... | collective-permute-start | bytes 61448 | tf_op jit(solution)/shard_map/ppermute | solution.py:293
  40.1 2.4 collective-permute-start.50
  43.3 3.2 %collective-permute-start.52 = (f32[8,640]{1,0:T(8,128)S(1)}, f32[8,640]{1,0:T(8,128)S(1)}, u32[]{:S(2)}, u32[]{:S(2)}) collective-permute-start(f32[8,640]{1,0:T(8,128)S(1)} %get-tuple-element.179), channel_id=1, source_target_pairs={{0,8},{1,9},{2,10},{3,11},{4,12},{5,13},{6,14},{7,15},{8,0},{9,1},... | collective-permute-start | bytes 61448 | tf_op jit(solution)/shard_map/ppermute | solution.py:293
  46.5 3.3 %collective-permute-start.54 = (f32[8,640]{1,0:T(8,128)S(1)}, f32[8,640]{1,0:T(8,128)S(1)}, u32[]{:S(2)}, u32[]{:S(2)}) collective-permute-start(f32[8,640]{1,0:T(8,128)S(1)} %get-tuple-element.181), channel_id=1, source_target_pairs={{0,10},{1,11},{2,8},{3,9},{4,14},{5,15},{6,12},{7,13},{8,2},{9,3},... | collective-permute-start | bytes 61448 | tf_op jit(solution)/shard_map/ppermute | solution.py:293
  55.3 2.1 collective-permute-start.21
  57.8 2.3 collective-permute-start.23
  61.2 2.6 collective-permute-start.25
  63.9 6.6 %collective-permute-start.27 = (f32[32,640]{1,0:T(8,128)S(1)}, f32[32,640]{1,0:T(8,128)S(1)}, u32[]{:S(2)}, u32[]{:S(2)}) collective-permute-start(f32[32,640]{1,0:T(8,128)S(1)} %get-tuple-element.152.refs_48_), channel_id=1, source_target_pairs={{0,13},{1,12},{2,15},{3,14},{4,9},{5,8},{6,11},{7,10},{8,5},{9,4},... | collective-permute-start | bytes 245768 | tf_op jit(solution)/shard_map/ppermute | solution.py:293
  70.4 2.4 collective-permute-start.28
  76.2 4.3 %collective-permute-start.55 = (f32[8,640]{1,0:T(8,128)S(1)}, f32[8,640]{1,0:T(8,128)S(1)}, u32[]{:S(2)}, u32[]{:S(2)}) collective-permute-start(f32[8,640]{1,0:T(8,128)S(1)} %get-tuple-element.182), channel_id=1, source_target_pairs={{0,11},{1,10},{2,9},{3,8},{4,15},{5,14},{6,13},{7,12},{8,3},{9,2},... | collective-permute-start | bytes 61448 | tf_op jit(solution)/shard_map/ppermute | solution.py:293
  81.9 4.2 %collective-permute-done.27.rest_13_ = f32[32,640]{1,0:T(8,128)S(1)} collective-permute-done((f32[32,640]{1,0:T(8,128)S(1)}, f32[32,640]{1,0:T(8,128)S(1)}, u32[]{:S(2)}, u32[]{:S(2)}) %collective-permute-start.27) | collective-permute-done | bytes 81952 | tf_op jit(solution)/shard_map/ppermute | solution.py:293
  86.6 2.5 collective-permute-done.28.rest_14_
  91.8 14.1 %shard_map.89 = (f32[16,640]{1,0:T(8,128)S(1)}, f32[16,640]{1,0:T(8,128)S(1)}, f32[16,640]{1,0:T(8,128)S(1)}, f32[16,640]{1,0:T(8,128)S(1)}, f32[16,640]{1,0:T(8...) custom-call(s32[1]{0:T(128)} %bitcast.me_ref.refs_0_, ...), custom_call_target="tpu_custom_call" | custom-call | tf_op jit(solution)/shard_map/pallas_call | solution.py:312
  108.6 1.8 collective-permute-start.34
  110.4 2.6 collective-permute-start.36
  116.9 2.3 collective-permute-start.40
  124.6 2.2 collective-permute-done.42.refs_16_
  126.8 2.2 collective-permute-done.43.refs_17_
  129.9 2.3 shard_map.90
  134.4 2.1 collective-permute-start.63
  136.6 2.0 collective-permute-start.65
  142.1 2.0 collective-permute-start.69
  144.1 4.5 %collective-permute-start.70 = (f32[32,640]{1,0:T(8,128)S(1)}, f32[32,640]{1,0:T(8,128)S(1)}, u32[]{:S(2)}, u32[]{:S(2)}) collective-permute-start(f32[32,640]{1,0:T(8,128)S(1)} %get-tuple-element.199.refs_46_), channel_id=1, source_target_pairs={{0,11},{1,10},{2,9},{3,8},{4,15},{5,14},{6,13},{7,12},{8,3},{9,2},... | collective-permute-start | bytes 245768 | tf_op jit(solution)/shard_map/ppermute | solution.py:293
  149.1 5.7 %collective-permute-start.72 = (f32[32,640]{1,0:T(8,128)S(1)}, f32[32,640]{1,0:T(8,128)S(1)}, u32[]{:S(2)}, u32[]{:S(2)}) collective-permute-start(f32[32,640]{1,0:T(8,128)S(1)} %get-tuple-element.201.refs_48_), channel_id=1, source_target_pairs={{0,13},{1,12},{2,15},{3,14},{4,9},{5,8},{6,11},{7,10},{8,5},{9,4},... | collective-permute-start | bytes 245768 | tf_op jit(solution)/shard_map/ppermute | solution.py:293
  156.2 2.0 collective-permute-start.74
  158.7 5.4 %collective-permute-done.71.rest_12_ = f32[32,640]{1,0:T(8,128)S(1)} collective-permute-done((f32[32,640]{1,0:T(8,128)S(1)}, f32[32,640]{1,0:T(8,128)S(1)}, u32[]{:S(2)}, u32[]{:S(2)}) %collective-permute-start.71) | collective-permute-done | bytes 81952 | tf_op jit(solution)/shard_map/ppermute | solution.py:293
  164.2 4.1 %collective-permute-done.72.rest_13_ = f32[32,640]{1,0:T(8,128)S(1)} collective-permute-done((f32[32,640]{1,0:T(8,128)S(1)}, f32[32,640]{1,0:T(8,128)S(1)}, u32[]{:S(2)}, u32[]{:S(2)}) %collective-permute-start.72) | collective-permute-done | bytes 81952 | tf_op jit(solution)/shard_map/ppermute | solution.py:293
  169.7 1.9 collective-permute-done.74.rest_15_
  171.6 14.3 %shard_map.91 = (f32[16,640]{1,0:T(8,128)S(1)}, f32[16,640]{1,0:T(8,128)S(1)}, f32[16,640]{1,0:T(8,128)S(1)}, f32[16,640]{1,0:T(8,128)S(1)}, f32[16,640]{1,0:T(8...) custom-call(s32[1]{0:T(128)} %bitcast.me_ref.refs_0_, ...), custom_call_target="tpu_custom_call" | custom-call | tf_op jit(solution)/shard_map/pallas_call | solution.py:312
  190.3 2.3 collective-permute-start.81
  192.8 2.3 collective-permute-start.83
  195.7 3.1 %collective-permute-start.85 = (f32[16,640]{1,0:T(8,128)S(1)}, f32[16,640]{1,0:T(8,128)S(1)}, u32[]{:S(2)}, u32[]{:S(2)}) collective-permute-start(f32[16,640]{1,0:T(8,128)S(1)} %get-tuple-element.215), channel_id=1, source_target_pairs={{0,11},{1,10},{2,9},{3,8},{4,15},{5,14},{6,13},{7,12},{8,3},{9,2},... | collective-permute-start | bytes 122888 | tf_op jit(solution)/shard_map/ppermute | solution.py:293
  205.7 2.4 collective-permute-done.88.refs_17_
  209.9 2.4 shard_map.92
  217.6 2.1 collective-permute-start.96
  222.4 2.0 collective-permute-start.99
  224.4 5.8 %collective-permute-start.100 = (f32[40,640]{1,0:T(8,128)S(1)}, f32[40,640]{1,0:T(8,128)S(1)}, u32[]{:S(2)}, u32[]{:S(2)}) collective-permute-start(f32[40,640]{1,0:T(8,128)S(1)} %get-tuple-element.231), channel_id=1, source_target_pairs={{0,11},{1,10},{2,9},{3,8},{4,15},{5,14},{6,13},{7,12},{8,3},{9,2},... | collective-permute-start | bytes 307208 | tf_op jit(solution)/shard_map/ppermute | solution.py:293
  230.7 8.7 %collective-permute-done.98.rest_9_ = f32[40,640]{1,0:T(8,128)S(1)} collective-permute-done((f32[40,640]{1,0:T(8,128)S(1)}, f32[40,640]{1,0:T(8,128)S(1)}, u32[]{:S(2)}, u32[]{:S(2)}) %collective-permute-start.98) | collective-permute-done | bytes 102432 | tf_op jit(solution)/shard_map/ppermute | solution.py:293
  243.8 7.8 %collective-permute-done.101.rest_12_ = f32[40,640]{1,0:T(8,128)S(1)} collective-permute-done((f32[40,640]{1,0:T(8,128)S(1)}, f32[40,640]{1,0:T(8,128)S(1)}, u32[]{:S(2)}, u32[]{:S(2)}) %collective-permute-start.101) | collective-permute-done | bytes 102432 | tf_op jit(solution)/shard_map/ppermute | solution.py:293
  251.6 2.5 collective-permute-done.102.rest_13_
  254.1 2.2 collective-permute-done.103.rest_14_
  256.3 2.2 collective-permute-done.104.rest_15_
  258.5 12.4 %shard_map.93 = (f32[2,15,32,128]{3,2,1,0:T(8,128)}, f32[2,160,128]{2,1,0:T(8,128)}) custom-call(s32[1]{0:T(128)} %bitcast.me_ref.refs_0_, bf16[40,2,15,32,128]{4,3,2,1,0:T(8,128)(2,1)} %model_ref.7, f32[2,15,32,128]{3,2,1,0:T(8,128)S(1)} %copy-done, s32[15,32,128]{2,1,0:T(8,128)S(1)} %copy-done.2, f32[40,640]{1,0:T(8,128)S(1)} %get-tuple-element.220.rest_0_, ...), custom_call_target="tpu_custom_call" | custom-call | tf_op jit(solution)/shard_map/pallas_call | solution.py:312
  (184 shorter events, 79.9 us)
Async XLA Ops:
  8.9 8.5 %collective-permute-start.5 = (f32[8,640]{1,0:T(8,128)S(1)}, f32[8,640]{1,0:T(8,128)S(1)}, u32[]{:S(2)}, u32[]{:S(2)}) collective-permute-start(f32[8,640]{1,0:T(8,128)S(1)} %get-tuple-element.126), channel_id=1, source_target_pairs={{0,6},{1,7},{2,4},{3,5},{4,2},{5,3},{6,0},{7,1},{8,14},{9,15},{10,... | collective-permute-start | bytes 61448 | tf_op jit(solution)/shard_map/ppermute | solution.py:293
  17.5 16.5 %collective-permute-start.10 = (f32[8,640]{1,0:T(8,128)S(1)}, f32[8,640]{1,0:T(8,128)S(1)}, u32[]{:S(2)}, u32[]{:S(2)}) collective-permute-start(f32[8,640]{1,0:T(8,128)S(1)} %get-tuple-element.131), channel_id=1, source_target_pairs={{0,11},{1,10},{2,9},{3,8},{4,15},{5,14},{6,13},{7,12},{8,3},{9,2},... | collective-permute-start | bytes 61448 | tf_op jit(solution)/shard_map/ppermute | solution.py:293
  17.8 16.5 %collective-permute-start.11 = (f32[8,640]{1,0:T(8,128)S(1)}, f32[8,640]{1,0:T(8,128)S(1)}, u32[]{:S(2)}, u32[]{:S(2)}) collective-permute-start(f32[8,640]{1,0:T(8,128)S(1)} %get-tuple-element.132), channel_id=1, source_target_pairs={{0,12},{1,13},{2,14},{3,15},{4,8},{5,9},{6,10},{7,11},{8,4},{9,5},... | collective-permute-start | bytes 61448 | tf_op jit(solution)/shard_map/ppermute | solution.py:293
  19.1 16.4 %collective-permute-start.12 = (f32[8,640]{1,0:T(8,128)S(1)}, f32[8,640]{1,0:T(8,128)S(1)}, u32[]{:S(2)}, u32[]{:S(2)}) collective-permute-start(f32[8,640]{1,0:T(8,128)S(1)} %get-tuple-element.133), channel_id=1, source_target_pairs={{0,13},{1,12},{2,15},{3,14},{4,9},{5,8},{6,11},{7,10},{8,5},{9,4},... | collective-permute-start | bytes 61448 | tf_op jit(solution)/shard_map/ppermute | solution.py:293
  19.6 16.6 %collective-permute-start.13 = (f32[8,640]{1,0:T(8,128)S(1)}, f32[8,640]{1,0:T(8,128)S(1)}, u32[]{:S(2)}, u32[]{:S(2)}) collective-permute-start(f32[8,640]{1,0:T(8,128)S(1)} %get-tuple-element.134), channel_id=1, source_target_pairs={{0,14},{1,15},{2,12},{3,13},{4,10},{5,11},{6,8},{7,9},{8,6},{9,7},... | collective-permute-start | bytes 61448 | tf_op jit(solution)/shard_map/ppermute | solution.py:293
  21.8 18.4 %collective-permute-start.14 = (f32[8,640]{1,0:T(8,128)S(1)}, f32[8,640]{1,0:T(8,128)S(1)}, u32[]{:S(2)}, u32[]{:S(2)}) collective-permute-start(f32[8,640]{1,0:T(8,128)S(1)} %get-tuple-element.135), channel_id=1, source_target_pairs={{0,15},{1,14},{2,13},{3,12},{4,11},{5,10},{6,9},{7,8},{8,7},{9,6},... | collective-permute-start | bytes 61448 | tf_op jit(solution)/shard_map/ppermute | solution.py:293
  34.2 8.2 %collective-permute-start.46 = (f32[8,640]{1,0:T(8,128)S(1)}, f32[8,640]{1,0:T(8,128)S(1)}, u32[]{:S(2)}, u32[]{:S(2)}) collective-permute-start(f32[8,640]{1,0:T(8,128)S(1)} %get-tuple-element.173), channel_id=1, source_target_pairs={{0,2},{1,3},{2,0},{3,1},{4,6},{5,7},{6,4},{7,5},{8,10},{9,11},{10,... | collective-permute-start | bytes 61448 | tf_op jit(solution)/shard_map/ppermute | solution.py:293
  35.4 7.8 %collective-permute-start.47 = (f32[8,640]{1,0:T(8,128)S(1)}, f32[8,640]{1,0:T(8,128)S(1)}, u32[]{:S(2)}, u32[]{:S(2)}) collective-permute-start(f32[8,640]{1,0:T(8,128)S(1)} %get-tuple-element.174), channel_id=1, source_target_pairs={{0,3},{1,2},{2,1},{3,0},{4,7},{5,6},{6,5},{7,4},{8,11},{9,10},{10,... | collective-permute-start | bytes 61448 | tf_op jit(solution)/shard_map/ppermute | solution.py:293
  36.2 10.3 %collective-permute-start.48 = (f32[8,640]{1,0:T(8,128)S(1)}, f32[8,640]{1,0:T(8,128)S(1)}, u32[]{:S(2)}, u32[]{:S(2)}) collective-permute-start(f32[8,640]{1,0:T(8,128)S(1)} %get-tuple-element.175), channel_id=1, source_target_pairs={{0,4},{1,5},{2,6},{3,7},{4,0},{5,1},{6,2},{7,3},{8,12},{9,13},{10,... | collective-permute-start | bytes 61448 | tf_op jit(solution)/shard_map/ppermute | solution.py:293
  40.1 10.5 %collective-permute-start.50 = (f32[8,640]{1,0:T(8,128)S(1)}, f32[8,640]{1,0:T(8,128)S(1)}, u32[]{:S(2)}, u32[]{:S(2)}) collective-permute-start(f32[8,640]{1,0:T(8,128)S(1)} %get-tuple-element.177), channel_id=1, source_target_pairs={{0,6},{1,7},{2,4},{3,5},{4,2},{5,3},{6,0},{7,1},{8,14},{9,15},{10,... | collective-permute-start | bytes 61448 | tf_op jit(solution)/shard_map/ppermute | solution.py:293
  42.5 8.8 %collective-permute-start.51 = (f32[8,640]{1,0:T(8,128)S(1)}, f32[8,640]{1,0:T(8,128)S(1)}, u32[]{:S(2)}, u32[]{:S(2)}) collective-permute-start(f32[8,640]{1,0:T(8,128)S(1)} %get-tuple-element.178), channel_id=1, source_target_pairs={{0,7},{1,6},{2,5},{3,4},{4,3},{5,2},{6,1},{7,0},{8,15},{9,14},{10,... | collective-permute-start | bytes 61448 | tf_op jit(solution)/shard_map/ppermute | solution.py:293
  43.3 8.3 %collective-permute-start.52 = (f32[8,640]{1,0:T(8,128)S(1)}, f32[8,640]{1,0:T(8,128)S(1)}, u32[]{:S(2)}, u32[]{:S(2)}) collective-permute-start(f32[8,640]{1,0:T(8,128)S(1)} %get-tuple-element.179), channel_id=1, source_target_pairs={{0,8},{1,9},{2,10},{3,11},{4,12},{5,13},{6,14},{7,15},{8,0},{9,1},... | collective-permute-start | bytes 61448 | tf_op jit(solution)/shard_map/ppermute | solution.py:293
  55.3 8.4 %collective-permute-start.21 = (f32[32,640]{1,0:T(8,128)S(1)}, f32[32,640]{1,0:T(8,128)S(1)}, u32[]{:S(2)}, u32[]{:S(2)}) collective-permute-start(f32[32,640]{1,0:T(8,128)S(1)} %get-tuple-element.146.refs_42_), channel_id=1, source_target_pairs={{0,7},{1,6},{2,5},{3,4},{4,3},{5,2},{6,1},{7,0},{8,15},{9,14},{10,... | collective-permute-start | bytes 245768 | tf_op jit(solution)/shard_map/ppermute | solution.py:293
  57.8 12.6 %collective-permute-start.23 = (f32[32,640]{1,0:T(8,128)S(1)}, f32[32,640]{1,0:T(8,128)S(1)}, u32[]{:S(2)}, u32[]{:S(2)}) collective-permute-start(f32[32,640]{1,0:T(8,128)S(1)} %get-tuple-element.148.refs_44_), channel_id=1, source_target_pairs={{0,9},{1,8},{2,11},{3,10},{4,13},{5,12},{6,15},{7,14},{8,1},{9,0},... | collective-permute-start | bytes 245768 | tf_op jit(solution)/shard_map/ppermute | solution.py:293
  60.1 13.4 %collective-permute-start.24 = (f32[32,640]{1,0:T(8,128)S(1)}, f32[32,640]{1,0:T(8,128)S(1)}, u32[]{:S(2)}, u32[]{:S(2)}) collective-permute-start(f32[32,640]{1,0:T(8,128)S(1)} %get-tuple-element.149.refs_45_), channel_id=1, source_target_pairs={{0,10},{1,11},{2,8},{3,9},{4,14},{5,15},{6,12},{7,13},{8,2},{9,3},... | collective-permute-start | bytes 245768 | tf_op jit(solution)/shard_map/ppermute | solution.py:293
  61.2 15.0 %collective-permute-start.25 = (f32[32,640]{1,0:T(8,128)S(1)}, f32[32,640]{1,0:T(8,128)S(1)}, u32[]{:S(2)}, u32[]{:S(2)}) collective-permute-start(f32[32,640]{1,0:T(8,128)S(1)} %get-tuple-element.150.refs_46_), channel_id=1, source_target_pairs={{0,11},{1,10},{2,9},{3,8},{4,15},{5,14},{6,13},{7,12},{8,3},{9,2},... | collective-permute-start | bytes 245768 | tf_op jit(solution)/shard_map/ppermute | solution.py:293
  63.7 17.4 %collective-permute-start.26 = (f32[32,640]{1,0:T(8,128)S(1)}, f32[32,640]{1,0:T(8,128)S(1)}, u32[]{:S(2)}, u32[]{:S(2)}) collective-permute-start(f32[32,640]{1,0:T(8,128)S(1)} %get-tuple-element.151.refs_47_), channel_id=1, source_target_pairs={{0,12},{1,13},{2,14},{3,15},{4,8},{5,9},{6,10},{7,11},{8,4},{9,5},... | collective-permute-start | bytes 245768 | tf_op jit(solution)/shard_map/ppermute | solution.py:293
  63.9 22.2 %collective-permute-start.27 = (f32[32,640]{1,0:T(8,128)S(1)}, f32[32,640]{1,0:T(8,128)S(1)}, u32[]{:S(2)}, u32[]{:S(2)}) collective-permute-start(f32[32,640]{1,0:T(8,128)S(1)} %get-tuple-element.152.refs_48_), channel_id=1, source_target_pairs={{0,13},{1,12},{2,15},{3,14},{4,9},{5,8},{6,11},{7,10},{8,5},{9,4},... | collective-permute-start | bytes 245768 | tf_op jit(solution)/shard_map/ppermute | solution.py:293
  70.4 18.6 %collective-permute-start.28 = (f32[32,640]{1,0:T(8,128)S(1)}, f32[32,640]{1,0:T(8,128)S(1)}, u32[]{:S(2)}, u32[]{:S(2)}) collective-permute-start(f32[32,640]{1,0:T(8,128)S(1)} %get-tuple-element.153.refs_49_), channel_id=1, source_target_pairs={{0,14},{1,15},{2,12},{3,13},{4,10},{5,11},{6,8},{7,9},{8,6},{9,7},... | collective-permute-start | bytes 245768 | tf_op jit(solution)/shard_map/ppermute | solution.py:293
  73.5 17.3 %collective-permute-start.29 = (f32[32,640]{1,0:T(8,128)S(1)}, f32[32,640]{1,0:T(8,128)S(1)}, u32[]{:S(2)}, u32[]{:S(2)}) collective-permute-start(f32[32,640]{1,0:T(8,128)S(1)} %get-tuple-element.154.refs_50_), channel_id=1, source_target_pairs={{0,15},{1,14},{2,13},{3,12},{4,11},{5,10},{6,9},{7,8},{8,7},{9,6},... | collective-permute-start | bytes 245768 | tf_op jit(solution)/shard_map/ppermute | solution.py:293
  76.2 29.8 %collective-permute-start.55 = (f32[8,640]{1,0:T(8,128)S(1)}, f32[8,640]{1,0:T(8,128)S(1)}, u32[]{:S(2)}, u32[]{:S(2)}) collective-permute-start(f32[8,640]{1,0:T(8,128)S(1)} %get-tuple-element.182), channel_id=1, source_target_pairs={{0,11},{1,10},{2,9},{3,8},{4,15},{5,14},{6,13},{7,12},{8,3},{9,2},... | collective-permute-start | bytes 61448 | tf_op jit(solution)/shard_map/ppermute | solution.py:293
  81.1 25.7 %collective-permute-start.56 = (f32[8,640]{1,0:T(8,128)S(1)}, f32[8,640]{1,0:T(8,128)S(1)}, u32[]{:S(2)}, u32[]{:S(2)}) collective-permute-start(f32[8,640]{1,0:T(8,128)S(1)} %get-tuple-element.183), channel_id=1, source_target_pairs={{0,12},{1,13},{2,14},{3,15},{4,8},{5,9},{6,10},{7,11},{8,4},{9,5},... | collective-permute-start | bytes 61448 | tf_op jit(solution)/shard_map/ppermute | solution.py:293
  86.1 20.9 %collective-permute-start.57 = (f32[8,640]{1,0:T(8,128)S(1)}, f32[8,640]{1,0:T(8,128)S(1)}, u32[]{:S(2)}, u32[]{:S(2)}) collective-permute-start(f32[8,640]{1,0:T(8,128)S(1)} %get-tuple-element.184), channel_id=1, source_target_pairs={{0,13},{1,12},{2,15},{3,14},{4,9},{5,8},{6,11},{7,10},{8,5},{9,4},... | collective-permute-start | bytes 61448 | tf_op jit(solution)/shard_map/ppermute | solution.py:293
  89.1 19.5 %collective-permute-start.58 = (f32[8,640]{1,0:T(8,128)S(1)}, f32[8,640]{1,0:T(8,128)S(1)}, u32[]{:S(2)}, u32[]{:S(2)}) collective-permute-start(f32[8,640]{1,0:T(8,128)S(1)} %get-tuple-element.185), channel_id=1, source_target_pairs={{0,14},{1,15},{2,12},{3,13},{4,10},{5,11},{6,8},{7,9},{8,6},{9,7},... | collective-permute-start | bytes 61448 | tf_op jit(solution)/shard_map/ppermute | solution.py:293
  90.8 17.8 %collective-permute-start.59 = (f32[8,640]{1,0:T(8,128)S(1)}, f32[8,640]{1,0:T(8,128)S(1)}, u32[]{:S(2)}, u32[]{:S(2)}) collective-permute-start(f32[8,640]{1,0:T(8,128)S(1)} %get-tuple-element.186), channel_id=1, source_target_pairs={{0,15},{1,14},{2,13},{3,12},{4,11},{5,10},{6,9},{7,8},{8,7},{9,6},... | collective-permute-start | bytes 61448 | tf_op jit(solution)/shard_map/ppermute | solution.py:293
  110.4 8.8 %collective-permute-start.36 = (f32[16,640]{1,0:T(8,128)S(1)}, f32[16,640]{1,0:T(8,128)S(1)}, u32[]{:S(2)}, u32[]{:S(2)}) collective-permute-start(f32[16,640]{1,0:T(8,128)S(1)} %get-tuple-element.162), channel_id=1, source_target_pairs={{0,7},{1,6},{2,5},{3,4},{4,3},{5,2},{6,1},{7,0},{8,15},{9,14},{10,... | collective-permute-start | bytes 122888 | tf_op jit(solution)/shard_map/ppermute | solution.py:293
  121.0 8.0 %collective-permute-start.43 = (f32[16,640]{1,0:T(8,128)S(1)}, f32[16,640]{1,0:T(8,128)S(1)}, u32[]{:S(2)}, u32[]{:S(2)}) collective-permute-start(f32[16,640]{1,0:T(8,128)S(1)} %get-tuple-element.169), channel_id=1, source_target_pairs={{0,14},{1,15},{2,12},{3,13},{4,10},{5,11},{6,8},{7,9},{8,6},{9,7},... | collective-permute-start | bytes 122888 | tf_op jit(solution)/shard_map/ppermute | solution.py:293
  138.7 9.9 %collective-permute-start.66 = (f32[32,640]{1,0:T(8,128)S(1)}, f32[32,640]{1,0:T(8,128)S(1)}, u32[]{:S(2)}, u32[]{:S(2)}) collective-permute-start(f32[32,640]{1,0:T(8,128)S(1)} %get-tuple-element.195.refs_42_), channel_id=1, source_target_pairs={{0,7},{1,6},{2,5},{3,4},{4,3},{5,2},{6,1},{7,0},{8,15},{9,14},{10,... | collective-permute-start | bytes 245768 | tf_op jit(solution)/shard_map/ppermute | solution.py:293
  140.4 8.8 %collective-permute-start.67 = (f32[32,640]{1,0:T(8,128)S(1)}, f32[32,640]{1,0:T(8,128)S(1)}, u32[]{:S(2)}, u32[]{:S(2)}) collective-permute-start(f32[32,640]{1,0:T(8,128)S(1)} %get-tuple-element.196.refs_43_), channel_id=1, source_target_pairs={{0,8},{1,9},{2,10},{3,11},{4,12},{5,13},{6,14},{7,15},{8,0},{9,1},... | collective-permute-start | bytes 245768 | tf_op jit(solution)/shard_map/ppermute | solution.py:293
  141.2 13.6 %collective-permute-start.68 = (f32[32,640]{1,0:T(8,128)S(1)}, f32[32,640]{1,0:T(8,128)S(1)}, u32[]{:S(2)}, u32[]{:S(2)}) collective-permute-start(f32[32,640]{1,0:T(8,128)S(1)} %get-tuple-element.197.refs_44_), channel_id=1, source_target_pairs={{0,9},{1,8},{2,11},{3,10},{4,13},{5,12},{6,15},{7,14},{8,1},{9,0},... | collective-permute-start | bytes 245768 | tf_op jit(solution)/shard_map/ppermute | solution.py:293
  142.1 14.1 %collective-permute-start.69 = (f32[32,640]{1,0:T(8,128)S(1)}, f32[32,640]{1,0:T(8,128)S(1)}, u32[]{:S(2)}, u32[]{:S(2)}) collective-permute-start(f32[32,640]{1,0:T(8,128)S(1)} %get-tuple-element.198.refs_45_), channel_id=1, source_target_pairs={{0,10},{1,11},{2,8},{3,9},{4,14},{5,15},{6,12},{7,13},{8,2},{9,3},... | collective-permute-start | bytes 245768 | tf_op jit(solution)/shard_map/ppermute | solution.py:293
  144.1 14.6 %collective-permute-start.70 = (f32[32,640]{1,0:T(8,128)S(1)}, f32[32,640]{1,0:T(8,128)S(1)}, u32[]{:S(2)}, u32[]{:S(2)}) collective-permute-start(f32[32,640]{1,0:T(8,128)S(1)} %get-tuple-element.199.refs_46_), channel_id=1, source_target_pairs={{0,11},{1,10},{2,9},{3,8},{4,15},{5,14},{6,13},{7,12},{8,3},{9,2},... | collective-permute-start | bytes 245768 | tf_op jit(solution)/shard_map/ppermute | solution.py:293
  148.6 15.6 %collective-permute-start.71 = (f32[32,640]{1,0:T(8,128)S(1)}, f32[32,640]{1,0:T(8,128)S(1)}, u32[]{:S(2)}, u32[]{:S(2)}) collective-permute-start(f32[32,640]{1,0:T(8,128)S(1)} %get-tuple-element.200.refs_47_), channel_id=1, source_target_pairs={{0,12},{1,13},{2,14},{3,15},{4,8},{5,9},{6,10},{7,11},{8,4},{9,5},... | collective-permute-start | bytes 245768 | tf_op jit(solution)/shard_map/ppermute | solution.py:293
  149.1 19.2 %collective-permute-start.72 = (f32[32,640]{1,0:T(8,128)S(1)}, f32[32,640]{1,0:T(8,128)S(1)}, u32[]{:S(2)}, u32[]{:S(2)}) collective-permute-start(f32[32,640]{1,0:T(8,128)S(1)} %get-tuple-element.201.refs_48_), channel_id=1, source_target_pairs={{0,13},{1,12},{2,15},{3,14},{4,9},{5,8},{6,11},{7,10},{8,5},{9,4},... | collective-permute-start | bytes 245768 | tf_op jit(solution)/shard_map/ppermute | solution.py:293
  154.8 14.9 %collective-permute-start.73 = (f32[32,640]{1,0:T(8,128)S(1)}, f32[32,640]{1,0:T(8,128)S(1)}, u32[]{:S(2)}, u32[]{:S(2)}) collective-permute-start(f32[32,640]{1,0:T(8,128)S(1)} %get-tuple-element.202.refs_49_), channel_id=1, source_target_pairs={{0,14},{1,15},{2,12},{3,13},{4,10},{5,11},{6,8},{7,9},{8,6},{9,7},... | collective-permute-start | bytes 245768 | tf_op jit(solution)/shard_map/ppermute | solution.py:293
  156.2 15.4 %collective-permute-start.74 = (f32[32,640]{1,0:T(8,128)S(1)}, f32[32,640]{1,0:T(8,128)S(1)}, u32[]{:S(2)}, u32[]{:S(2)}) collective-permute-start(f32[32,640]{1,0:T(8,128)S(1)} %get-tuple-element.203.refs_50_), channel_id=1, source_target_pairs={{0,15},{1,14},{2,13},{3,12},{4,11},{5,10},{6,9},{7,8},{8,7},{9,6},... | collective-permute-start | bytes 245768 | tf_op jit(solution)/shard_map/ppermute | solution.py:293
  190.3 8.5 %collective-permute-start.81 = (f32[16,640]{1,0:T(8,128)S(1)}, f32[16,640]{1,0:T(8,128)S(1)}, u32[]{:S(2)}, u32[]{:S(2)}) collective-permute-start(f32[16,640]{1,0:T(8,128)S(1)} %get-tuple-element.211), channel_id=1, source_target_pairs={{0,7},{1,6},{2,5},{3,4},{4,3},{5,2},{6,1},{7,0},{8,15},{9,14},{10,... | collective-permute-start | bytes 122888 | tf_op jit(solution)/shard_map/ppermute | solution.py:293
  201.4 8.5 %collective-permute-start.89 = (f32[16,640]{1,0:T(8,128)S(1)}, f32[16,640]{1,0:T(8,128)S(1)}, u32[]{:S(2)}, u32[]{:S(2)}) collective-permute-start(f32[16,640]{1,0:T(8,128)S(1)} %get-tuple-element.219), channel_id=1, source_target_pairs={{0,15},{1,14},{2,13},{3,12},{4,11},{5,10},{6,9},{7,8},{8,7},{9,6},... | collective-permute-start | bytes 122888 | tf_op jit(solution)/shard_map/ppermute | solution.py:293
  216.3 8.1 %collective-permute-start.95 = (f32[40,640]{1,0:T(8,128)S(1)}, f32[40,640]{1,0:T(8,128)S(1)}, u32[]{:S(2)}, u32[]{:S(2)}) collective-permute-start(f32[40,640]{1,0:T(8,128)S(1)} %get-tuple-element.226), channel_id=1, source_target_pairs={{0,6},{1,7},{2,4},{3,5},{4,2},{5,3},{6,0},{7,1},{8,14},{9,15},{10,... | collective-permute-start | bytes 307208 | tf_op jit(solution)/shard_map/ppermute | solution.py:293
  217.6 12.5 %collective-permute-start.96 = (f32[40,640]{1,0:T(8,128)S(1)}, f32[40,640]{1,0:T(8,128)S(1)}, u32[]{:S(2)}, u32[]{:S(2)}) collective-permute-start(f32[40,640]{1,0:T(8,128)S(1)} %get-tuple-element.227), channel_id=1, source_target_pairs={{0,7},{1,6},{2,5},{3,4},{4,3},{5,2},{6,1},{7,0},{8,15},{9,14},{10,... | collective-permute-start | bytes 307208 | tf_op jit(solution)/shard_map/ppermute | solution.py:293
  219.9 10.7 %collective-permute-start.97 = (f32[40,640]{1,0:T(8,128)S(1)}, f32[40,640]{1,0:T(8,128)S(1)}, u32[]{:S(2)}, u32[]{:S(2)}) collective-permute-start(f32[40,640]{1,0:T(8,128)S(1)} %get-tuple-element.228), channel_id=1, source_target_pairs={{0,8},{1,9},{2,10},{3,11},{4,12},{5,13},{6,14},{7,15},{8,0},{9,1},... | collective-permute-start | bytes 307208 | tf_op jit(solution)/shard_map/ppermute | solution.py:293
  221.6 17.8 %collective-permute-start.98 = (f32[40,640]{1,0:T(8,128)S(1)}, f32[40,640]{1,0:T(8,128)S(1)}, u32[]{:S(2)}, u32[]{:S(2)}) collective-permute-start(f32[40,640]{1,0:T(8,128)S(1)} %get-tuple-element.229), channel_id=1, source_target_pairs={{0,9},{1,8},{2,11},{3,10},{4,13},{5,12},{6,15},{7,14},{8,1},{9,0},... | collective-permute-start | bytes 307208 | tf_op jit(solution)/shard_map/ppermute | solution.py:293
  222.4 19.2 %collective-permute-start.99 = (f32[40,640]{1,0:T(8,128)S(1)}, f32[40,640]{1,0:T(8,128)S(1)}, u32[]{:S(2)}, u32[]{:S(2)}) collective-permute-start(f32[40,640]{1,0:T(8,128)S(1)} %get-tuple-element.230), channel_id=1, source_target_pairs={{0,10},{1,11},{2,8},{3,9},{4,14},{5,15},{6,12},{7,13},{8,2},{9,3},... | collective-permute-start | bytes 307208 | tf_op jit(solution)/shard_map/ppermute | solution.py:293
  224.4 19.4 %collective-permute-start.100 = (f32[40,640]{1,0:T(8,128)S(1)}, f32[40,640]{1,0:T(8,128)S(1)}, u32[]{:S(2)}, u32[]{:S(2)}) collective-permute-start(f32[40,640]{1,0:T(8,128)S(1)} %get-tuple-element.231), channel_id=1, source_target_pairs={{0,11},{1,10},{2,9},{3,8},{4,15},{5,14},{6,13},{7,12},{8,3},{9,2},... | collective-permute-start | bytes 307208 | tf_op jit(solution)/shard_map/ppermute | solution.py:293
  230.2 21.4 %collective-permute-start.101 = (f32[40,640]{1,0:T(8,128)S(1)}, f32[40,640]{1,0:T(8,128)S(1)}, u32[]{:S(2)}, u32[]{:S(2)}) collective-permute-start(f32[40,640]{1,0:T(8,128)S(1)} %get-tuple-element.232), channel_id=1, source_target_pairs={{0,12},{1,13},{2,14},{3,15},{4,8},{5,9},{6,10},{7,11},{8,4},{9,5},... | collective-permute-start | bytes 307208 | tf_op jit(solution)/shard_map/ppermute | solution.py:293
  230.7 23.4 %collective-permute-start.102 = (f32[40,640]{1,0:T(8,128)S(1)}, f32[40,640]{1,0:T(8,128)S(1)}, u32[]{:S(2)}, u32[]{:S(2)}) collective-permute-start(f32[40,640]{1,0:T(8,128)S(1)} %get-tuple-element.233), channel_id=1, source_target_pairs={{0,13},{1,12},{2,15},{3,14},{4,9},{5,8},{6,11},{7,10},{8,5},{9,4},... | collective-permute-start | bytes 307208 | tf_op jit(solution)/shard_map/ppermute | solution.py:293
  239.4 16.9 %collective-permute-start.103 = (f32[40,640]{1,0:T(8,128)S(1)}, f32[40,640]{1,0:T(8,128)S(1)}, u32[]{:S(2)}, u32[]{:S(2)}) collective-permute-start(f32[40,640]{1,0:T(8,128)S(1)} %get-tuple-element.234), channel_id=1, source_target_pairs={{0,14},{1,15},{2,12},{3,13},{4,10},{5,11},{6,8},{7,9},{8,6},{9,7},... | collective-permute-start | bytes 307208 | tf_op jit(solution)/shard_map/ppermute | solution.py:293
  241.6 17.0 %collective-permute-start.104 = (f32[40,640]{1,0:T(8,128)S(1)}, f32[40,640]{1,0:T(8,128)S(1)}, u32[]{:S(2)}, u32[]{:S(2)}) collective-permute-start(f32[40,640]{1,0:T(8,128)S(1)} %get-tuple-element.235), channel_id=1, source_target_pairs={{0,15},{1,14},{2,13},{3,12},{4,11},{5,10},{6,9},{7,8},{8,7},{9,6},... | collective-permute-start | bytes 307208 | tf_op jit(solution)/shard_map/ppermute | solution.py:293
  (64 other events, 510.6 us)

commit v2 on v1

v2 whole, which is shorter than its diff:
```python
import functools

import jax
import jax.numpy as jnp
from jax import lax
from jax.experimental import pallas as pl
from jax.experimental.pallas import tpu as pltpu
from jax.sharding import PartitionSpec as P

STATIONS = 64
SOURCE_COUNT = 40
ITERS = 2
ROWS = 16

ridge = 1.0
F32 = jnp.float32
BF16 = jnp.bfloat16
VMEM_LIMIT = 16 * 1024 * 1024


def swap(x):
    return pltpu.roll(x, x.shape[-1] // 2, axis=x.ndim - 1)


def lower(shape):
    return lax.broadcasted_iota(jnp.int32, shape, len(shape) - 1) < shape[-1] // 2


def cross(a, b):
    lo = lower(a.shape)
    return jnp.where(lo, a, swap(b)), jnp.where(lo, swap(a), b)


def three(x):
    hi = x.astype(BF16)
    rest = x - hi.astype(F32)
    mid = rest.astype(BF16)
    return hi, mid, (rest - mid.astype(F32)).astype(BF16)


def pick(onehot, x, dims):
    return sum(
        lax.dot_general(onehot, part, (dims, ((), ())), preferred_element_type=F32)
        for part in three(x)
    )


def pack_kernel(n, dpc, me_ref, first_ref, second_ref, re_ref, im_ref, *rest):
    outs, halves = rest
    per = re_ref.shape[0] // SOURCE_COUNT
    me = me_ref[0]
    a, b = cross(re_ref[...], im_ref[...])
    halves[0] = a
    halves[1] = b
    base = lax.rem(me, 2) * per
    lane = lax.broadcasted_iota(jnp.int32, (1, dpc * 128), 1)
    sub = lax.broadcasted_iota(jnp.int32, (2 * per, 128), 0)
    count = first_ref.shape[0]
    at = me * 2 * ROWS
    marks = jnp.zeros((1, dpc * 128), F32)
    for r in range(count):
        marks = jnp.where(lane == at + r, (first_ref[r] + 1).astype(F32), marks)
        marks = jnp.where(lane == at + ROWS + r, (second_ref[r] + 1).astype(F32), marks)
    for o in range(n):
        k, c = o // 2, o % 2
        for dd in range(dpc):
            cols = slice(dd * 128, (dd + 1) * 128)
            block = jnp.where(sub == per - base, marks[:, cols], 0.0)
            for s in range(per):
                at = s * SOURCE_COUNT + k * dpc + dd
                row = halves[c, at : at + 1, :]
                block = jnp.where(sub == base + s, row, block)
            outs[o, :, cols] = block


def power_kernel(n, dpc, model_ref, mask_ref, out_ref, local):
    local[...] = jnp.zeros_like(local)

    def pair(b, carry):
        weight = mask_ref[b].astype(F32)
        for d in range(SOURCE_COUNT):
            mr = model_ref[d, 0, b].astype(F32)
            mi = model_ref[d, 1, b].astype(F32)
            local[d, pl.ds(b, 1), :] = jnp.sum(weight * (mr * mr + mi * mi), axis=0, keepdims=True)
        return carry

    lax.fori_loop(0, mask_ref.shape[0], pair, 0)
    for k in range(n // 2):
        for dd in range(dpc):
            full = local[k * dpc + dd]
            x0, x1 = cross(full[:8], full[8:])
            out_ref[2 * k, :, dd * 128 : (dd + 1) * 128] = x0
            out_ref[2 * k + 1, :, dd * 128 : (dd + 1) * 128] = x1


def own_first_kernel(n, dpc, ins, g_ref, onehot_ref, outs):
    width = dpc * 128
    per = STATIONS // n
    row = lax.broadcasted_iota(jnp.int32, (2 * per, width), 0)
    marks = jnp.zeros((2 * per, width), F32)
    for m in range(n // 2):
        total = jnp.zeros((2 * per, width), F32)
        for o in (2 * m, 2 * m + 1):
            mine = lax.div(row, per) == o % 2
            x = ins[o]
            total = total + jnp.where(mine, x, 0.0)
            marks = marks + jnp.where(mine, 0.0, x)
        g_ref[m * 2 * per : (m + 1) * 2 * per, :] = total
    marks = jnp.sum(marks, axis=0, keepdims=True)[:, : n * 2 * ROWS]
    station = lax.broadcasted_iota(jnp.int32, (STATIONS, n * 2 * ROWS), 0)
    onehot = jnp.where(station + 1 == marks.astype(jnp.int32), 1.0, 0.0).astype(BF16)
    onehot_ref[...] = onehot
    sel = pick(onehot, g_ref[...], ((0,), (0,)))
    for o in range(n):
        outs[o] = sel[o * 2 * ROWS : (o + 1) * 2 * ROWS]


def own_kernel(n, dpc, last, g_in, onehot_ref, sums, powers, sels, g_out, outs, terms):
    width = dpc * 128
    lo = lower((ROWS, 128))
    lo8 = lower((8, 128))
    sign = jnp.where(lo, -1.0, 1.0)
    for o in range(n):
        for dd in range(dpc):
            cols = slice(dd * 128, (dd + 1) * 128)
            B = sums[o, :, cols]
            W = powers[o, :, cols]
            Wx = swap(W)
            W = jnp.concatenate([jnp.where(lo8, W, Wx), jnp.where(lo8, Wx, W)], 0)
            p = sels[o, :ROWS, cols]
            q = sels[o, ROWS:, cols]
            Bx, px, qx = swap(B), swap(p), swap(q)
            Brr, Bii = jnp.where(lo, B, Bx), jnp.where(lo, Bx, B)
            first = Brr * q + sign * Bii * qx
            second = Brr * p - sign * Bii * px
            q2, p2 = q * q, p * p
            r = o * 2 * ROWS
            terms[r : r + ROWS, cols] = first
            terms[r + ROWS : r + 2 * ROWS, cols] = second
            dcols = slice(width + dd * 128, width + (dd + 1) * 128)
            terms[r : r + ROWS, dcols] = W * (q2 + swap(q2))
            terms[r + ROWS : r + 2 * ROWS, dcols] = W * (p2 + swap(p2))
    onehot = onehot_ref[...]
    total = pick(onehot, terms[...], ((1,), (0,)))
    g = 0.5 * (g_in[...] + total[:, :width] / (total[:, width:] + ridge))
    g_out[...] = g
    sel = pick(onehot, g, ((0,), (0,)))
    for o in range(n):
        outs[o, : 2 * ROWS, :] = sel[o * 2 * ROWS : (o + 1) * 2 * ROWS]
    if last:
        per = STATIONS // n
        line = lax.broadcasted_iota(jnp.int32, (n * 8, STATIONS), 0)
        col = lax.broadcasted_iota(jnp.int32, (n * 8, STATIONS), 1)
        slot, r = lax.div(line, 8), lax.rem(line, 8)
        want = slot * per + r
        mine = jnp.where((col == want) & (r < per), 1.0, 0.0).astype(BF16)
        own = pick(mine, g, ((1,), (0,)))
        for o in range(n):
            outs[o, 2 * ROWS :, :] = own[o * 8 : (o + 1) * 8]


def load_products(n, dpc, ins, hre, him):
    for k in range(n // 2):
        for dd in range(dpc):
            cols = slice(dd * 128, (dd + 1) * 128)
            pr, pi = cross(ins[2 * k, :ROWS, cols], ins[2 * k + 1, :ROWS, cols])
            qr, qi = cross(ins[2 * k, ROWS : 2 * ROWS, cols], ins[2 * k + 1, ROWS : 2 * ROWS, cols])
            hre[k * dpc + dd] = pr * qr + pi * qi
            him[k * dpc + dd] = pi * qr - pr * qi


def predict(b, model_ref, vis_ref, mask_ref, hre, him):
    def step(i, acc):
        acc_re, acc_im = acc
        for u in range(8):
            d = i * 8 + u
            mr = model_ref[d, 0, b].astype(F32)
            mi = model_ref[d, 1, b].astype(F32)
            hr = hre[d, pl.ds(b, 1), :]
            hi = him[d, pl.ds(b, 1), :]
            acc_re = acc_re - (hr * mr - hi * mi)
            acc_im = acc_im - (hr * mi + hi * mr)
        return acc_re, acc_im

    acc = lax.fori_loop(0, SOURCE_COUNT // 8, step, (vis_ref[0, b], vis_ref[1, b]))
    weight = mask_ref[b].astype(F32)
    return weight * acc[0], weight * acc[1]


def pass_kernel(n, dpc, model_ref, vis_ref, mask_ref, power_ref, ins, out_ref, hre, him, cre, cim):
    load_products(n, dpc, ins, hre, him)
    cre[...] = jnp.zeros_like(cre)
    cim[...] = jnp.zeros_like(cim)

    def pair(b, carry):
        res_re, res_im = predict(b, model_ref, vis_ref, mask_ref, hre, him)

        def step(i, carry):
            for u in range(8):
                d = i * 8 + u
                mr = model_ref[d, 0, b].astype(F32)
                mi = model_ref[d, 1, b].astype(F32)
                cre[d, pl.ds(b, 1), :] = jnp.sum(mr * res_re + mi * res_im, axis=0, keepdims=True)
                cim[d, pl.ds(b, 1), :] = jnp.sum(mr * res_im - mi * res_re, axis=0, keepdims=True)
            return carry

        return lax.fori_loop(0, SOURCE_COUNT // 8, step, carry)

    lax.fori_loop(0, mask_ref.shape[0], pair, 0)
    for k in range(n // 2):
        for dd in range(dpc):
            d = k * dpc + dd
            w = power_ref[d]
            x0, x1 = cross(cre[d] + hre[d] * w, cim[d] + him[d] * w)
            out_ref[2 * k, :, dd * 128 : (dd + 1) * 128] = x0
            out_ref[2 * k + 1, :, dd * 128 : (dd + 1) * 128] = x1


def last_kernel(n, dpc, model_ref, vis_ref, mask_ref, ins, res_ref, gains_ref, hre, him):
    load_products(n, dpc, ins, hre, him)
    for k in range(n // 2):
        for dd in range(dpc):
            cols = slice(dd * 128, (dd + 1) * 128)
            re, im = cross(ins[2 * k, 2 * ROWS :, cols], ins[2 * k + 1, 2 * ROWS :, cols])
            for s in range(STATIONS // n):
                at = s * SOURCE_COUNT + k * dpc + dd
                gains_ref[0, at : at + 1, :] = re[s : s + 1]
                gains_ref[1, at : at + 1, :] = im[s : s + 1]

    def pair(b, carry):
        res_re, res_im = predict(b, model_ref, vis_ref, mask_ref, hre, him)
        res_ref[0, b] = res_re
        res_ref[1, b] = res_im
        return carry

    lax.fori_loop(0, mask_ref.shape[0], pair, 0)


SMEM = pl.BlockSpec(memory_space=pltpu.SMEM)
VMEM = pl.BlockSpec(memory_space=pltpu.VMEM)


def shape(*dims, dtype=F32):
    return jax.ShapeDtypeStruct(dims, dtype)


def exchange(x):
    return lax.all_to_all(x, "bl", split_axis=0, concat_axis=0, tiled=True)


def fast_body(n, vis, model, mask, first, second, gre, gim):
    dpc = SOURCE_COUNT // (n // 2)
    width = dpc * 128
    pairs, times, channels = mask.shape
    me = lax.axis_index("bl").astype(jnp.int32).reshape(1)
    params = pltpu.CompilerParams(vmem_limit_bytes=VMEM_LIMIT)
    plane = (SOURCE_COUNT, ROWS, channels)

    def call(kernel, args, outs, scratch=()):
        return pl.pallas_call(
            functools.partial(kernel, n, dpc),
            in_specs=[SMEM if x.ndim == 1 else VMEM for x in args],
            out_specs=[VMEM for o in outs],
            out_shape=outs,
            scratch_shapes=[pltpu.VMEM(x, F32) for x in scratch],
            compiler_params=params,
        )(*args)

    start_rows = 2 * STATIONS // n
    (packed,) = call(
        pack_kernel, (me, first, second, gre, gim), [shape(n, start_rows, width)], [(2,) + gre.shape]
    )
    packed = exchange(packed)
    powers, power = call(power_kernel, (model, mask), [shape(n, 8, width), shape(*plane)])
    powers = exchange(powers)
    g, onehot, sels = call(
        own_first_kernel,
        (packed,),
        [shape(STATIONS, width), shape(STATIONS, n * 2 * ROWS, dtype=BF16), shape(n, 2 * ROWS, width)],
    )
    for step in range(ITERS):
        last = step == ITERS - 1
        got = exchange(sels)
        (sums,) = call(
            pass_kernel, (model, vis, mask, power, got), [shape(n, ROWS, width)], [plane] * 4
        )
        sums = exchange(sums)
        g, sels = call(
            lambda n, dpc, *refs: own_kernel(n, dpc, last, *refs),
            (g, onehot, sums, powers, sels),
            [shape(STATIONS, width), shape(n, 2 * ROWS + (8 if last else 0), width)],
            [(n * 2 * ROWS, 2 * width)],
        )
    got = exchange(sels)
    residual, gains = call(
        last_kernel, (model, vis, mask, got), [shape(*vis.shape), shape(2, *gre.shape)], [plane] * 2
    )
    return gains, residual


def block_pass(full_re, full_im, vis_blk, coh_blk, weight, first, second, want_sums):
    ar = jnp.transpose(full_re[first], (1, 0, 2))
    ai = jnp.transpose(full_im[first], (1, 0, 2))
    br = jnp.transpose(full_re[second], (1, 0, 2))
    bi = jnp.transpose(full_im[second], (1, 0, 2))
    mr = coh_blk[:, 0].astype(F32)
    mi = coh_blk[:, 1].astype(F32)
    hr = ar * br + ai * bi
    hi = ai * br - ar * bi
    hr_t, hi_t = hr[:, :, None], hi[:, :, None]
    res_re = weight * (vis_blk[0] - jnp.sum(hr_t * mr - hi_t * mi, 0))
    res_im = weight * (vis_blk[1] - jnp.sum(hr_t * mi + hi_t * mr, 0))
    residual = jnp.stack([res_re, res_im])
    if not want_sums:
        return (residual, None)
    power = jnp.sum(weight[None] * (mr * mr + mi * mi), 2)
    sum_re = jnp.sum(mr * res_re + mi * res_im, 2) + hr * power
    sum_im = jnp.sum(mr * res_im - mi * res_re, 2) + hi * power
    terms_first = jnp.stack([br * sum_re - bi * sum_im, br * sum_im + bi * sum_re, power * (br * br + bi * bi)])
    terms_second = jnp.stack([ar * sum_re + ai * sum_im, ai * sum_re - ar * sum_im, power * (ar * ar + ai * ai)])
    stations = jnp.arange(STATIONS, dtype=jnp.int32)
    onehot_first = (first[:, None] == stations[None, :]).astype(F32)
    onehot_second = (second[:, None] == stations[None, :]).astype(F32)
    exact = lax.Precision.HIGHEST
    sums = jnp.einsum("bs,cdbf->csdf", onehot_first, terms_first, precision=exact)
    sums = sums + jnp.einsum("bs,cdbf->csdf", onehot_second, terms_second, precision=exact)
    return (residual, sums)


def plain_body(vis, model, mask, first, second, gre, gim):
    weight = mask.astype(F32)
    rows, channels = gre.shape
    shaped = (STATIONS, SOURCE_COUNT, channels)
    full_re = lax.all_gather(gre, "bl", axis=0, tiled=True).reshape(shaped)
    full_im = lax.all_gather(gim, "bl", axis=0, tiled=True).reshape(shaped)
    for step in range(ITERS):
        unused, sums = block_pass(full_re, full_im, vis, model, weight, first, second, True)
        totals = lax.psum(sums, "bl")
        denom = totals[2] + ridge
        full_re = 0.5 * (full_re + totals[0] / denom)
        full_im = 0.5 * (full_im + totals[1] / denom)
    residual, unused = block_pass(full_re, full_im, vis, model, weight, first, second, False)
    both = jnp.stack([full_re, full_im]).reshape(2, STATIONS * SOURCE_COUNT, channels)
    return lax.dynamic_slice_in_dim(both, lax.axis_index("bl") * rows, rows, 1), residual


def solution(mesh):
    n = mesh.shape["bl"]
    split = n % 2 == 0 and SOURCE_COUNT % (n // 2) == 0 and STATIONS == 4 * n

    def body(vis, model, mask, first, second, gre, gim):
        if split and mask.shape[0] <= ROWS:
            return fast_body(n, vis, model, mask, first, second, gre, gim)
        return plain_body(vis, model, mask, first, second, gre, gim)

    in_specs = (
        P(None, ("grp", "bl"), None, None),
        P(None, None, ("grp", "bl"), None, None),
        P(("grp", "bl"), None, None),
        P(("grp", "bl")),
        P(("grp", "bl")),
        P(("grp", "bl"), None),
        P(("grp", "bl"), None),
    )
    out_specs = (P(None, ("grp", "bl"), None), P(None, ("grp", "bl"), None, None))
    return jax.shard_map(body, mesh=mesh, in_specs=in_specs, out_specs=out_specs, check_vma=False)
```

time: 272 us -> 229 us (0.84)
  blocking collectives: 0 us -> 139 us
  starting transfers between devices: 144 us -> 10 us
  waiting for transfers between devices: 64 us -> 22.8 us
  Pallas kernels: 58.1 us -> 35 us
  local copies, waits for them, and re-layouts: 4.08 us -> 18.9 us
    ppermute x105 -> x0, starting transfers between devices: 144 us -> none  [exchange(): done.append(lax.ppermute(parts[o], 'bl', [(i, i ^ o) for i in range(n)]))]
    all_to_all x0 -> x5, blocking collectives: none -> 139 us  [exchange(): return lax.all_to_all(x, 'bl', split_axis=0, concat_axis=0, tiled=True)]
    ppermute x105 -> x0, waiting for transfers between devices: 64 us -> none  [exchange(): done.append(lax.ppermute(parts[o], 'bl', [(i, i ^ o) for i in range(n)]))]
    pallas_call x8, Pallas kernels: 58.1 us -> 35 us  [call(): pl.pallas_call(functools.partial(kernel, n, dpc), in_specs=[SMEM if x.ndi...]
    all_to_all x0 -> x2, waiting for transfers between devices: none -> 22.8 us  [exchange(): return lax.all_to_all(x, 'bl', split_axis=0, concat_axis=0, tiled=True)]
    unnamed x14 -> x24, local copies, waits for them, and re-layouts: 4.08 us -> 18.9 us
    all_to_all x0 -> x2, starting transfers between devices: none -> 10 us  [exchange(): return lax.all_to_all(x, 'bl', split_axis=0, concat_axis=0, tiled=True)]
  transfers between devices with their start and end apart: 105 -> 2, of which waited for: 30 -> 1; matrix products, arithmetic and copies ran while one was open for 0% -> 0% of each run, Pallas kernels for 9% -> 6%
where the time goes in v2:
time: 229 us; the launch traced here: 226 us
  blocking collectives  139 us (61%)
  Pallas kernels  35 us (15%)
  waiting for transfers between devices  22.8 us (10%)
  local copies, waits for them, and re-layouts  18.9 us (8%)
  starting transfers between devices  10 us (4%)
    all_to_all x5, blocking collectives, exchange(): return lax.all_to_all(x, 'bl', split_axis=0, concat_axis=0, tiled=True)  139 us
    pallas_call x8, Pallas kernels, call(): pl.pallas_call(functools.partial(kernel, n, dpc), in_specs=[SMEM if x.ndi...  35 us
    all_to_all x2, waiting for transfers between devices, exchange(): return lax.all_to_all(x, 'bl', split_axis=0, concat_axis=0, tiled=True)  22.8 us
    unnamed x24, local copies, waits for them, and re-layouts  18.9 us
    all_to_all x2, starting transfers between devices, exchange(): return lax.all_to_all(x, 'bl', split_axis=0, concat_axis=0, tiled=True)  10 us
  transfers between devices with their start and end apart: 2, of which 1 were waited for; matrix products, arithmetic and copies ran while one was open for 0% of the time, Pallas kernels for 6%

profile of v2, /device:TPU:9, one launch (start us, length us, event | category | flops | bytes accessed | tf_op | source)
XLA Modules:
  0.0 226.1 jit_solution(12519209629472384481)
XLA Ops:
  0.6 0.0 copy-start.8
  0.6 0.9 copy-done.8
  1.5 0.0 copy-start.9
  1.5 0.9 copy-done.9
  2.4 0.0 copy-start.10
  2.4 0.7 copy-done.10
  3.1 0.0 copy-start.11
  3.1 0.7 copy-done.11
  3.7 0.7 shard_map.86
  4.5 16.4 %all_to_all.35.ins = f32[16,8,640]{2,1,0:T(8,128)S(1)} all-to-all(f32[16,8,640]{2,1,0:T(8,128)S(1)} %shard_map.86), channel_id=1, replica_groups=mesh['grp'=2,'bl'=16] {'bl'}, dimensions={0} | all-to-all | bytes 655360 | tf_op jit(solution)/shard_map/all_to_all | solution.py:248
  20.9 1.8 shard_map.87
  22.7 0.0 copy-start.6
  22.7 0.7 copy-done.6
  23.4 0.0 copy-start.5
  23.4 4.8 %all-to-all-start.1 = ((f32[16,32,640]{2,1,0:T(8,128)}), f32[16,32,640]{2,1,0:T(8,128)S(1)}, u32[]{:S(2)}, u32[]{:S(2)}) async-start(f32[16,32,640]{2,1,0:T(8,128)} %get-tuple-element.15.refs_4_), calls=%async_computation.1 | async-start | bytes 2621440 | tf_op jit(solution)/shard_map/all_to_all | solution.py:248
  28.2 0.0 copy-done.5
  28.2 0.0 copy-start
  28.2 3.8 %copy-done = bf16[40,2,15,32,128]{4,3,2,1,0:T(8,128)(2,1)S(1)} copy-done((bf16[40,2,15,32,128]{4,3,2,1,0:T(8,128)(2,1)S(1)}, bf16[40,2,15,32,128]{4,3,2,1,0:T(8,128)(2,1)}, u32[]{:S(2)}) %copy-start) | copy-done | bytes 9830424
  32.0 0.0 copy-start.4
  32.0 3.7 %shard_map.88 = (f32[16,8,640]{2,1,0:T(8,128)}, f32[40,16,128]{2,1,0:T(8,128)S(1)}) custom-call(bf16[40,2,15,32,128]{4,3,2,1,0:T(8,128)(2,1)S(1)} %copy-done, s32[15,32,128]{2,1,0:T(8,128)S(1)} %copy-done.5), custom_call_target="tpu_custom_call" | custom-call | tf_op jit(solution)/shard_map/pallas_call | solution.py:260
  35.6 22.7 %all-to-all-done.1.ins = f32[16,32,640]{2,1,0:T(8,128)S(1)} async-done(((f32[16,32,640]{2,1,0:T(8,128)}), f32[16,32,640]{2,1,0:T(8,128)S(1)}, u32[]{:S(2)}, u32[]{:S(2)}) %all-to-all-start.1) | async-done | bytes 1310752 | tf_op jit(solution)/shard_map/all_to_all | solution.py:248
  58.4 5.2 %all-to-all-start.3 = ((f32[16,8,640]{2,1,0:T(8,128)}), f32[16,8,640]{2,1,0:T(8,128)S(1)}, u32[]{:S(2)}, u32[]{:S(2)}) async-start(f32[16,8,640]{2,1,0:T(8,128)} %get-tuple-element.16), calls=%async_computation.3 | async-start | bytes 655360 | tf_op jit(solution)/shard_map/all_to_all | solution.py:248
  63.6 0.0 copy-done.4
  63.6 0.0 copy-start.1
  63.6 3.8 %copy-done.1 = bf16[40,2,15,32,128]{4,3,2,1,0:T(8,128)(2,1)S(1)} copy-done((bf16[40,2,15,32,128]{4,3,2,1,0:T(8,128)(2,1)S(1)}, bf16[40,2,15,32,128]{4,3,2,1,0:T(8,128)(2,1)}, u32[]{:S(2)}) %copy-start.1) | copy-done | bytes 9830424
  67.4 8.9 %shard_map.89 = f32[16,16,640]{2,1,0:T(8,128)S(1)} custom-call(bf16[40,2,15,32,128]{4,3,2,1,0:T(8,128)(2,1)S(1)} %copy-done.1, f32[2,15,32,128]{3,2,1,0:T(8,128)S(1)} %copy-done.4, s32[15,32,128]{2,1,0:T(8,128)S(1)} %copy-done.5, f32[40,16,128]{2,1,0:T(8,128)S(1)} %get-tuple-element.14.power_ref, f32[16,32,640]{2,1,0:T(8,128)S(1)} %all-to-all-done.1.ins), custom_call_target="tpu_custom_call" | custom-call | tf_op jit(solution)/shard_map/pallas_call | solution.py:260
  76.4 0.0 copy-start.7
  76.4 0.0 all-to-all-done.3.refs_3_
  76.4 23.2 %all_to_all.36.refs_2_ = f32[16,16,640]{2,1,0:T(8,128)S(1)} all-to-all(f32[16,16,640]{2,1,0:T(8,128)S(1)} %shard_map.89), channel_id=1, replica_groups=mesh['grp'=2,'bl'=16] {'bl'}, dimensions={0} | all-to-all | bytes 1310720 | tf_op jit(solution)/shard_map/all_to_all | solution.py:248
  99.5 0.0 copy-done.7
  99.5 3.6 %shard_map.90 = (f32[64,640]{1,0:T(8,128)S(1)}, f32[16,32,640]{2,1,0:T(8,128)S(1)}) custom-call(f32[64,640]{1,0:T(8,128)S(1)} %copy-done.7, bf16[64,512]{1,0:T(8,128)(2,1)S(1)} %get-tuple-element.13.refs_1_, f32[16,16,640]{2,1,0:T(8,128)S(1)} %all_to_all.36.refs_2_, f32[16,8,640]{2,1,0:T(8,128)S(1)} %all-to-all-done.3.refs_3_, ...), custom_call_target="tpu_custom_call" | custom-call | tf_op jit(solution)/shard_map/pallas_call | solution.py:260
  103.1 35.3 %all_to_all.37.ins = f32[16,32,640]{2,1,0:T(8,128)S(1)} all-to-all(f32[16,32,640]{2,1,0:T(8,128)S(1)} %get-tuple-element.18.refs_4_), channel_id=1, replica_groups=mesh['grp'=2,'bl'=16] {'bl'}, dimensions={0} | all-to-all | bytes 2621440 | tf_op jit(solution)/shard_map/all_to_all | solution.py:248
  138.4 0.0 copy-start.2
  138.4 3.8 %copy-done.2 = bf16[40,2,15,32,128]{4,3,2,1,0:T(8,128)(2,1)S(1)} copy-done((bf16[40,2,15,32,128]{4,3,2,1,0:T(8,128)(2,1)S(1)}, bf16[40,2,15,32,128]{4,3,2,1,0:T(8,128)(2,1)}, u32[]{:S(2)}) %copy-start.2) | copy-done | bytes 9830424
  142.2 8.9 %shard_map.91 = f32[16,16,640]{2,1,0:T(8,128)S(1)} custom-call(bf16[40,2,15,32,128]{4,3,2,1,0:T(8,128)(2,1)S(1)} %copy-done.2, f32[2,15,32,128]{3,2,1,0:T(8,128)S(1)} %copy-done.4, s32[15,32,128]{2,1,0:T(8,128)S(1)} %copy-done.5, f32[40,16,128]{2,1,0:T(8,128)S(1)} %get-tuple-element.14.power_ref, f32[16,32,640]{2,1,0:T(8,128)S(1)} %all_to_all.37.ins), custom_call_target="tpu_custom_call" | custom-call | tf_op jit(solution)/shard_map/pallas_call | solution.py:260
  151.2 21.3 %all_to_all.38.refs_2_ = f32[16,16,640]{2,1,0:T(8,128)S(1)} all-to-all(f32[16,16,640]{2,1,0:T(8,128)S(1)} %shard_map.91), channel_id=1, replica_groups=mesh['grp'=2,'bl'=16] {'bl'}, dimensions={0} | all-to-all | bytes 1310720 | tf_op jit(solution)/shard_map/all_to_all | solution.py:248
  172.5 2.3 %shard_map.92 = (f32[64,640]{1,0:T(8,128)}, f32[16,40,640]{2,1,0:T(8,128)S(1)}) custom-call(f32[64,640]{1,0:T(8,128)S(1)} %get-tuple-element.17.refs_0_, bf16[64,512]{1,0:T(8,128)(2,1)S(1)} %get-tuple-element.13.refs_1_, f32[16,16,640]{2,1,0:T(8,128)S(1)} %all_to_all.38.refs_2_, f32[16,8,640]{2,1,0:T(8,128)S(1)} %all-to-all-done.3.refs_3_, ...), custom_call_target="tpu_custom_call" | custom-call | tf_op jit(solution)/shard_map/pallas_call | solution.py:260
  174.8 42.5 %all_to_all.39.ins = f32[16,40,640]{2,1,0:T(8,128)S(1)} all-to-all(f32[16,40,640]{2,1,0:T(8,128)S(1)} %get-tuple-element.19), channel_id=1, replica_groups=mesh['grp'=2,'bl'=16] {'bl'}, dimensions={0} | all-to-all | bytes 3276800 | tf_op jit(solution)/shard_map/all_to_all | solution.py:248
  217.4 0.0 copy-start.3
  217.4 3.8 %copy-done.3 = bf16[40,2,15,32,128]{4,3,2,1,0:T(8,128)(2,1)S(1)} copy-done((bf16[40,2,15,32,128]{4,3,2,1,0:T(8,128)(2,1)S(1)}, bf16[40,2,15,32,128]{4,3,2,1,0:T(8,128)(2,1)}, u32[]{:S(2)}) %copy-start.3) | copy-done | bytes 9830424
  221.2 5.0 %shard_map.93 = (f32[2,15,32,128]{3,2,1,0:T(8,128)}, f32[2,160,128]{2,1,0:T(8,128)}) custom-call(bf16[40,2,15,32,128]{4,3,2,1,0:T(8,128)(2,1)S(1)} %copy-done.3, f32[2,15,32,128]{3,2,1,0:T(8,128)S(1)} %copy-done.4, s32[15,32,128]{2,1,0:T(8,128)S(1)} %copy-done.5, f32[16,40,640]{2,1,0:T(8,128)S(1)} %all_to_all.39.ins), custom_call_target="tpu_custom_call" | custom-call | tf_op jit(solution)/shard_map/pallas_call | solution.py:260
Async XLA Ops:
  0.6 0.9 copy-start.8
  1.5 0.9 copy-start.9
  2.4 0.7 copy-start.10
  3.1 0.7 copy-start.11
  22.7 0.7 copy-start.6
  23.4 4.8 %copy-start.5 = (s32[15,32,128]{2,1,0:T(8,128)S(1)}, s32[15,32,128]{2,1,0:T(8,128)}, u32[]{:S(2)}) copy-start(s32[15,32,128]{2,1,0:T(8,128)} %mask_ref.7) | copy-start | bytes 737284
  23.4 35.0 %all-to-all-start.1 = ((f32[16,32,640]{2,1,0:T(8,128)}), f32[16,32,640]{2,1,0:T(8,128)S(1)}, u32[]{:S(2)}, u32[]{:S(2)}) async-start(f32[16,32,640]{2,1,0:T(8,128)} %get-tuple-element.15.refs_4_), calls=%async_computation.1 | async-start | bytes 2621440 | tf_op jit(solution)/shard_map/all_to_all | solution.py:248
  28.2 3.8 %copy-start = (bf16[40,2,15,32,128]{4,3,2,1,0:T(8,128)(2,1)S(1)}, bf16[40,2,15,32,128]{4,3,2,1,0:T(8,128)(2,1)}, u32[]{:S(2)}) copy-start(bf16[40,2,15,32,128]{4,3,2,1,0:T(8,128)(2,1)} %model_ref.7) | copy-start | bytes 29491204
  32.0 31.6 %copy-start.4 = (f32[2,15,32,128]{3,2,1,0:T(8,128)S(1)}, f32[2,15,32,128]{3,2,1,0:T(8,128)}, u32[]{:S(2)}) copy-start(f32[2,15,32,128]{3,2,1,0:T(8,128)} %vis_ref.5) | copy-start | bytes 1474564
  58.4 18.0 %all-to-all-start.3 = ((f32[16,8,640]{2,1,0:T(8,128)}), f32[16,8,640]{2,1,0:T(8,128)S(1)}, u32[]{:S(2)}, u32[]{:S(2)}) async-start(f32[16,8,640]{2,1,0:T(8,128)} %get-tuple-element.16), calls=%async_computation.3 | async-start | bytes 655360 | tf_op jit(solution)/shard_map/all_to_all | solution.py:248
  63.6 3.8 %copy-start.1 = (bf16[40,2,15,32,128]{4,3,2,1,0:T(8,128)(2,1)S(1)}, bf16[40,2,15,32,128]{4,3,2,1,0:T(8,128)(2,1)}, u32[]{:S(2)}) copy-start(bf16[40,2,15,32,128]{4,3,2,1,0:T(8,128)(2,1)} %model_ref.7) | copy-start | bytes 29491204
  76.4 23.2 %copy-start.7 = (f32[64,640]{1,0:T(8,128)S(1)}, f32[64,640]{1,0:T(8,128)}, u32[]{:S(2)}) copy-start(f32[64,640]{1,0:T(8,128)} %copy-done.6) | copy-start | bytes 491524
  138.4 3.8 %copy-start.2 = (bf16[40,2,15,32,128]{4,3,2,1,0:T(8,128)(2,1)S(1)}, bf16[40,2,15,32,128]{4,3,2,1,0:T(8,128)(2,1)}, u32[]{:S(2)}) copy-start(bf16[40,2,15,32,128]{4,3,2,1,0:T(8,128)(2,1)} %model_ref.7) | copy-start | bytes 29491204
  217.4 3.8 %copy-start.3 = (bf16[40,2,15,32,128]{4,3,2,1,0:T(8,128)(2,1)S(1)}, bf16[40,2,15,32,128]{4,3,2,1,0:T(8,128)(2,1)}, u32[]{:S(2)}) copy-start(bf16[40,2,15,32,128]{4,3,2,1,0:T(8,128)(2,1)} %model_ref.7) | copy-start | bytes 29491204

commit v3 on v2

v3 whole, which is shorter than its diff:
```python
import functools

import jax
import jax.numpy as jnp
from jax import lax
from jax.experimental import pallas as pl
from jax.experimental.pallas import tpu as pltpu
from jax.sharding import PartitionSpec as P

STATIONS = 64
SOURCE_COUNT = 40
ITERS = 2
ROWS = 16

ridge = 1.0
F32 = jnp.float32
BF16 = jnp.bfloat16
VMEM_LIMIT = 16 * 1024 * 1024


def swap(x):
    return pltpu.roll(x, x.shape[-1] // 2, axis=x.ndim - 1)


def lower(shape):
    return lax.broadcasted_iota(jnp.int32, shape, len(shape) - 1) < shape[-1] // 2


def cross(a, b):
    lo = lower(a.shape)
    return jnp.where(lo, a, swap(b)), jnp.where(lo, swap(a), b)


def three(x):
    hi = x.astype(BF16)
    rest = x - hi.astype(F32)
    mid = rest.astype(BF16)
    return hi, mid, (rest - mid.astype(F32)).astype(BF16)


def pick(onehot, x, dims):
    return sum(
        lax.dot_general(onehot, part, (dims, ((), ())), preferred_element_type=F32)
        for part in three(x)
    )


def pack_kernel(n, dpc, first_ref, second_ref, re_ref, im_ref, out_ref):
    rows = re_ref.shape[0]
    out_ref[:rows] = re_ref[...]
    out_ref[rows : 2 * rows] = im_ref[...]
    lane = lax.broadcasted_iota(jnp.int32, (8, 128), 1)
    marks = jnp.zeros((8, 128), F32)
    for r in range(first_ref.shape[0]):
        marks = jnp.where(lane == r, (first_ref[r] + 1).astype(F32), marks)
        marks = jnp.where(lane == ROWS + r, (second_ref[r] + 1).astype(F32), marks)
    out_ref[2 * rows :] = marks


def power_kernel(n, dpc, model_ref, mask_ref, local):
    local[...] = jnp.zeros_like(local)

    def pair(b, carry):
        weight = mask_ref[b].astype(F32)
        for d in range(SOURCE_COUNT):
            mr = model_ref[d, 0, b].astype(F32)
            mi = model_ref[d, 1, b].astype(F32)
            local[d, pl.ds(b, 1), :] = jnp.sum(weight * (mr * mr + mi * mi), axis=0, keepdims=True)
        return carry

    lax.fori_loop(0, mask_ref.shape[0], pair, 0)


def wide(ref):
    return jnp.concatenate([ref[dd] for dd in range(ref.shape[0])], axis=1)


def first_own_kernel(n, dpc, me_ref, *rest):
    ins, (g_ref, onehot_ref, sel_ref, lines) = rest[:n], rest[n:]
    me = me_ref[0]
    k, c = lax.div(me, 2), lax.rem(me, 2)
    per = STATIONS // n
    rows = per * SOURCE_COUNT
    for o in range(n):
        peer = jnp.bitwise_xor(me, o)
        lines[pl.ds(peer, 1), :] = ins[o][2 * rows : 2 * rows + 1, :]
        for s in range(per):
            for dd in range(dpc):
                at = s * SOURCE_COUNT + k * dpc + dd
                x0, x1 = cross(ins[o][pl.ds(at, 1), :], ins[o][pl.ds(rows + at, 1), :])
                g_ref[dd, pl.ds(peer * per + s, 1), :] = jnp.where(c == 0, x0, x1)
    across = 128 // (2 * ROWS)
    station = lax.broadcasted_iota(jnp.int32, (STATIONS, 128), 0)
    for group in range(n // across):
        marks = jnp.zeros((1, 128), F32)
        for i in range(across):
            row = lines[group * across + i : group * across + i + 1, :]
            marks = marks + (pltpu.roll(row, i * 2 * ROWS, axis=1) if i else row)
        hit = station + 1 == marks.astype(jnp.int32)
        onehot_ref[:, group * 128 : (group + 1) * 128] = jnp.where(hit, 1.0, 0.0).astype(BF16)
    sel_ref[...] = pick(onehot_ref[...], wide(g_ref), ((0,), (0,)))


def power_rows(sums, o, cols):
    lo8 = lower((8, 128))
    W = sums[o, ROWS:, cols]
    Wx = swap(W)
    return jnp.concatenate([jnp.where(lo8, W, Wx), jnp.where(lo8, Wx, W)], 0)


def fill_powers(n, dpc, sums, sel_ref, terms, base):
    for o in range(n):
        r = o * 2 * ROWS
        for dd in range(dpc):
            cols = slice(dd * 128, (dd + 1) * 128)
            dcols = slice(base + dd * 128, base + (dd + 1) * 128)
            W = power_rows(sums, o, cols)
            p = sel_ref[r : r + ROWS, cols]
            q = sel_ref[r + ROWS : r + 2 * ROWS, cols]
            p2, q2 = p * p, q * q
            terms[r : r + ROWS, dcols] = W * (q2 + swap(q2))
            terms[r + ROWS : r + 2 * ROWS, dcols] = W * (p2 + swap(p2))


def fill_sums(n, dpc, sums, sel_ref, terms):
    lo = lower((ROWS, 128))
    sign = jnp.where(lo, -1.0, 1.0)
    for o in range(n):
        r = o * 2 * ROWS
        for dd in range(dpc):
            cols = slice(dd * 128, (dd + 1) * 128)
            B = sums[o, :ROWS, cols]
            p = sel_ref[r : r + ROWS, cols]
            q = sel_ref[r + ROWS : r + 2 * ROWS, cols]
            Bx = swap(B)
            Brr, Bii = jnp.where(lo, B, Bx), jnp.where(lo, Bx, B)
            terms[r : r + ROWS, cols] = Brr * q + sign * Bii * swap(q)
            terms[r + ROWS : r + 2 * ROWS, cols] = Brr * p - sign * Bii * swap(p)


def own_kernel(n, dpc, g_in, onehot_ref, sel_ref, sums, g_out, terms):
    width = dpc * 128
    fill_sums(n, dpc, sums, sel_ref, terms)
    fill_powers(n, dpc, sums, sel_ref, terms, width)
    total = pick(onehot_ref[...], terms[...], ((1,), (0,)))
    step = total[:, :width] / (total[:, width:] + ridge)
    for dd in range(dpc):
        g_out[dd] = 0.5 * (g_in[dd] + step[:, dd * 128 : (dd + 1) * 128])


def prepare_kernel(n, dpc, g_ref, onehot_ref, sums, sel_ref, den_ref, terms):
    sel_ref[...] = pick(onehot_ref[...], wide(g_ref), ((0,), (0,)))
    fill_powers(n, dpc, sums, sel_ref, terms, 0)
    den_ref[...] = pick(onehot_ref[...], terms[...], ((1,), (0,))) + ridge


def later_own_kernel(n, dpc, g_in, onehot_ref, sel_ref, den_ref, sums, g_out, terms):
    fill_sums(n, dpc, sums, sel_ref, terms)
    total = pick(onehot_ref[...], terms[...], ((1,), (0,)))
    step = total / den_ref[...]
    for dd in range(dpc):
        g_out[dd] = 0.5 * (g_in[dd] + step[:, dd * 128 : (dd + 1) * 128])


def products_first(n, dpc, me, first_ref, second_ref, ins, hre, him, stack):
    per = STATIONS // n
    rows = per * SOURCE_COUNT
    for o in range(n):
        stack[jnp.bitwise_xor(me, o)] = ins[o][: 2 * rows, :]

    def block(station, part):
        at = lax.rem(station, per) * SOURCE_COUNT + part * rows
        return stack[lax.div(station, per), pl.ds(pl.multiple_of(at, 8), SOURCE_COUNT), :]

    def pair(b, carry):
        p, q = first_ref[b], second_ref[b]
        pr, pi, qr, qi = block(p, 0), block(p, 1), block(q, 0), block(q, 1)
        re, im = pr * qr + pi * qi, pi * qr - pr * qi
        for d in range(SOURCE_COUNT):
            hre[d, pl.ds(b, 1), :] = re[d : d + 1]
            him[d, pl.ds(b, 1), :] = im[d : d + 1]
        return carry

    lax.fori_loop(0, first_ref.shape[0], pair, 0)


def products(n, dpc, me, first_ref, second_ref, ins, hre, him, gp, gq):
    def pair(b, carry):
        p, q = first_ref[b], second_ref[b]
        for o in range(n):
            for dd in range(dpc):
                gp[o * dpc + dd, pl.ds(b, 1), :] = ins[o][dd, pl.ds(p, 1), :]
                gq[o * dpc + dd, pl.ds(b, 1), :] = ins[o][dd, pl.ds(q, 1), :]
        return carry

    lax.fori_loop(0, first_ref.shape[0], pair, 0)
    even = lax.rem(me, 2) == 0
    for m in range(n // 2):
        k = lax.div(jnp.bitwise_xor(me, 2 * m), 2)
        for dd in range(dpc):
            a, b = 2 * m * dpc + dd, (2 * m + 1) * dpc + dd
            pr, pi = cross(jnp.where(even, gp[a], gp[b]), jnp.where(even, gp[b], gp[a]))
            qr, qi = cross(jnp.where(even, gq[a], gq[b]), jnp.where(even, gq[b], gq[a]))
            hre[k * dpc + dd] = pr * qr + pi * qi
            him[k * dpc + dd] = pi * qr - pr * qi


def predict(b, model_ref, vis_ref, mask_ref, hre, him):
    def step(i, acc):
        acc_re, acc_im = acc
        for u in range(8):
            d = i * 8 + u
            mr = model_ref[d, 0, b].astype(F32)
            mi = model_ref[d, 1, b].astype(F32)
            hr = hre[d, pl.ds(b, 1), :]
            hi = him[d, pl.ds(b, 1), :]
            acc_re = acc_re - (hr * mr - hi * mi)
            acc_im = acc_im - (hr * mi + hi * mr)
        return acc_re, acc_im

    acc = lax.fori_loop(0, SOURCE_COUNT // 8, step, (vis_ref[0, b], vis_ref[1, b]))
    weight = mask_ref[b].astype(F32)
    return weight * acc[0], weight * acc[1]


def pass_kernel(n, dpc, start, me_ref, first_ref, second_ref, model_ref, vis_ref, mask_ref, power_ref, *rest):
    ins, (out_ref, hre, him, cre, cim), work = rest[:n], rest[n : n + 5], rest[n + 5 :]
    build = products_first if start else products
    build(n, dpc, me_ref[0], first_ref, second_ref, ins, hre, him, *work)
    cre[...] = jnp.zeros_like(cre)
    cim[...] = jnp.zeros_like(cim)

    def pair(b, carry):
        res_re, res_im = predict(b, model_ref, vis_ref, mask_ref, hre, him)

        def step(i, carry):
            for u in range(8):
                d = i * 8 + u
                mr = model_ref[d, 0, b].astype(F32)
                mi = model_ref[d, 1, b].astype(F32)
                cre[d, pl.ds(b, 1), :] = jnp.sum(mr * res_re + mi * res_im, axis=0, keepdims=True)
                cim[d, pl.ds(b, 1), :] = jnp.sum(mr * res_im - mi * res_re, axis=0, keepdims=True)
            return carry

        return lax.fori_loop(0, SOURCE_COUNT // 8, step, carry)

    lax.fori_loop(0, mask_ref.shape[0], pair, 0)
    pairs = mask_ref.shape[0]
    real = lax.broadcasted_iota(jnp.int32, (ROWS, 128), 0) < pairs
    for k in range(n // 2):
        for dd in range(dpc):
            d = k * dpc + dd
            cols = slice(dd * 128, (dd + 1) * 128)
            w = power_ref[d]
            re = jnp.where(real, cre[d] + hre[d] * w, 0.0)
            im = jnp.where(real, cim[d] + him[d] * w, 0.0)
            out_ref[2 * k, :ROWS, cols], out_ref[2 * k + 1, :ROWS, cols] = cross(re, im)
            if start:
                out_ref[2 * k, ROWS:, cols], out_ref[2 * k + 1, ROWS:, cols] = cross(w[:8], w[8:])


def last_kernel(n, dpc, me_ref, first_ref, second_ref, model_ref, vis_ref, mask_ref, *rest):
    ins, (res_ref, gains_ref, hre, him), work = rest[:n], rest[n : n + 4], rest[n + 4 :]
    me = me_ref[0]
    per = STATIONS // n
    even = lax.rem(me, 2) == 0
    for m in range(n // 2):
        k = lax.div(jnp.bitwise_xor(me, 2 * m), 2)
        for dd in range(dpc):
            for s in range(per):
                a = ins[2 * m][dd, pl.ds(me * per + s, 1), :]
                b = ins[2 * m + 1][dd, pl.ds(me * per + s, 1), :]
                re, im = cross(jnp.where(even, a, b), jnp.where(even, b, a))
                at = s * SOURCE_COUNT + k * dpc + dd
                gains_ref[0, pl.ds(at, 1), :] = re
                gains_ref[1, pl.ds(at, 1), :] = im
    products(n, dpc, me, first_ref, second_ref, ins, hre, him, *work)

    def pair(b, carry):
        res_re, res_im = predict(b, model_ref, vis_ref, mask_ref, hre, him)
        res_ref[0, b] = res_re
        res_ref[1, b] = res_im
        return carry

    lax.fori_loop(0, mask_ref.shape[0], pair, 0)


SMEM = pl.BlockSpec(memory_space=pltpu.SMEM)
VMEM = pl.BlockSpec(memory_space=pltpu.VMEM)


def shape(*dims, dtype=F32):
    return jax.ShapeDtypeStruct(dims, dtype)


def exchange(x):
    return lax.all_to_all(x, "bl", split_axis=0, concat_axis=0, tiled=True)


def gather(n, piece):
    def send(x, o):
        return lax.ppermute(x, "bl", [(i, i ^ o) for i in range(n)])

    got = {0: piece}
    got[4], got[12] = send(piece, 4), send(piece, 12)
    got[2] = send(piece, 2)
    got[8] = send(got[12], 4)
    for o in (4, 12, 8):
        got[o + 2] = send(got[o], 2)
    for o in (0, 2, 4, 12, 6, 14, 8, 10):
        got[o + 1] = send(got[o], 1)
    return [got[o] for o in range(n)]


def fast_body(n, vis, model, mask, first, second, gre, gim):
    dpc = SOURCE_COUNT // (n // 2)
    width = dpc * 128
    pairs, times, channels = mask.shape
    me = lax.axis_index("bl").astype(jnp.int32).reshape(1)
    params = pltpu.CompilerParams(vmem_limit_bytes=VMEM_LIMIT)
    plane = (SOURCE_COUNT, ROWS, channels)
    picked = (n * dpc, ROWS, channels)
    lots = n * 2 * ROWS
    mine = (dpc, STATIONS, channels)

    def call(kernel, args, outs, scratch=()):
        return pl.pallas_call(
            functools.partial(kernel, n, dpc),
            in_specs=[SMEM if x.ndim == 1 else VMEM for x in args],
            out_specs=[VMEM for o in outs],
            out_shape=outs,
            scratch_shapes=[pltpu.VMEM(x, F32) for x in scratch],
            compiler_params=params,
        )(*args)

    (piece,) = call(pack_kernel, (first, second, gre, gim), [shape(2 * gre.shape[0] + 8, channels)])
    got = gather(n, piece)
    (power,) = call(power_kernel, (model, mask), [shape(*plane)])
    g, onehot, sel = call(
        first_own_kernel,
        (me, *got),
        [shape(*mine), shape(STATIONS, lots, dtype=BF16), shape(lots, width)],
        [(n, channels)],
    )
    for step in range(ITERS):
        start = step == 0
        work = [(n, 2 * gre.shape[0], channels)] if start else [picked] * 2
        (sums,) = call(
            lambda n, dpc, *refs: pass_kernel(n, dpc, start, *refs),
            (me, first, second, model, vis, mask, power, *got),
            [shape(n, ROWS + (8 if start else 0), width)],
            [plane] * 4 + work,
        )
        sums = exchange(sums)
        if start:
            powers = sums
            (g,) = call(
                own_kernel, (g, onehot, sel, sums), [shape(*mine)], [(lots, 2 * width)]
            )
        else:
            (g,) = call(
                later_own_kernel, (g, onehot, sel, den, sums), [shape(*mine)], [(lots, width)]
            )
        got = gather(n, g)
        if step < ITERS - 1:
            sel, den = call(
                prepare_kernel,
                (g, onehot, powers),
                [shape(lots, width), shape(STATIONS, width)],
                [(lots, width)],
            )
    residual, gains = call(
        last_kernel,
        (me, first, second, model, vis, mask, *got),
        [shape(*vis.shape), shape(2, *gre.shape)],
        [plane] * 2 + [picked] * 2,
    )
    return gains, residual


def block_pass(full_re, full_im, vis_blk, coh_blk, weight, first, second, want_sums):
    ar = jnp.transpose(full_re[first], (1, 0, 2))
    ai = jnp.transpose(full_im[first], (1, 0, 2))
    br = jnp.transpose(full_re[second], (1, 0, 2))
    bi = jnp.transpose(full_im[second], (1, 0, 2))
    mr = coh_blk[:, 0].astype(F32)
    mi = coh_blk[:, 1].astype(F32)
    hr = ar * br + ai * bi
    hi = ai * br - ar * bi
    hr_t, hi_t = hr[:, :, None], hi[:, :, None]
    res_re = weight * (vis_blk[0] - jnp.sum(hr_t * mr - hi_t * mi, 0))
    res_im = weight * (vis_blk[1] - jnp.sum(hr_t * mi + hi_t * mr, 0))
    residual = jnp.stack([res_re, res_im])
    if not want_sums:
        return (residual, None)
    power = jnp.sum(weight[None] * (mr * mr + mi * mi), 2)
    sum_re = jnp.sum(mr * res_re + mi * res_im, 2) + hr * power
    sum_im = jnp.sum(mr * res_im - mi * res_re, 2) + hi * power
    terms_first = jnp.stack([br * sum_re - bi * sum_im, br * sum_im + bi * sum_re, power * (br * br + bi * bi)])
    terms_second = jnp.stack([ar * sum_re + ai * sum_im, ai * sum_re - ar * sum_im, power * (ar * ar + ai * ai)])
    stations = jnp.arange(STATIONS, dtype=jnp.int32)
    onehot_first = (first[:, None] == stations[None, :]).astype(F32)
    onehot_second = (second[:, None] == stations[None, :]).astype(F32)
    exact = lax.Precision.HIGHEST
    sums = jnp.einsum("bs,cdbf->csdf", onehot_first, terms_first, precision=exact)
    sums = sums + jnp.einsum("bs,cdbf->csdf", onehot_second, terms_second, precision=exact)
    return (residual, sums)


def plain_body(vis, model, mask, first, second, gre, gim):
    weight = mask.astype(F32)
    rows, channels = gre.shape
    shaped = (STATIONS, SOURCE_COUNT, channels)
    full_re = lax.all_gather(gre, "bl", axis=0, tiled=True).reshape(shaped)
    full_im = lax.all_gather(gim, "bl", axis=0, tiled=True).reshape(shaped)
    for step in range(ITERS):
        unused, sums = block_pass(full_re, full_im, vis, model, weight, first, second, True)
        totals = lax.psum(sums, "bl")
        denom = totals[2] + ridge
        full_re = 0.5 * (full_re + totals[0] / denom)
        full_im = 0.5 * (full_im + totals[1] / denom)
    residual, unused = block_pass(full_re, full_im, vis, model, weight, first, second, False)
    both = jnp.stack([full_re, full_im]).reshape(2, STATIONS * SOURCE_COUNT, channels)
    return lax.dynamic_slice_in_dim(both, lax.axis_index("bl") * rows, rows, 1), residual


def solution(mesh):
    n = mesh.shape["bl"]
    split = n == 16

    def body(vis, model, mask, first, second, gre, gim):
        if split and mask.shape[0] <= ROWS:
            return fast_body(n, vis, model, mask, first, second, gre, gim)
        return plain_body(vis, model, mask, first, second, gre, gim)

    in_specs = (
        P(None, ("grp", "bl"), None, None),
        P(None, None, ("grp", "bl"), None, None),
        P(("grp", "bl"), None, None),
        P(("grp", "bl")),
        P(("grp", "bl")),
        P(("grp", "bl"), None),
        P(("grp", "bl"), None),
    )
    out_specs = (P(None, ("grp", "bl"), None), P(None, ("grp", "bl"), None, None))
    return jax.shard_map(body, mesh=mesh, in_specs=in_specs, out_specs=out_specs, check_vma=False)
```

time: 229 us -> 188 us (0.82)
  blocking collectives: 139 us -> 0 us
  starting transfers between devices: 10 us -> 52.5 us
  waiting for transfers between devices: 22.8 us -> 56.5 us
  local copies, waits for them, and re-layouts: 18.9 us -> 33.9 us
  Pallas kernels: 35 us -> 40.4 us
    all_to_all x5 -> x0, blocking collectives: 139 us -> none  [exchange(): return lax.all_to_all(x, 'bl', split_axis=0, concat_axis=0, tiled=True)]
    ppermute x0 -> x45, starting transfers between devices: none -> 42.7 us  [send(): return lax.ppermute(x, 'bl', [(i, i ^ o) for i in range(n)])]
    ppermute x0 -> x45, waiting for transfers between devices: none -> 34.3 us  [send(): return lax.ppermute(x, 'bl', [(i, i ^ o) for i in range(n)])]
    unnamed x24 -> x92, local copies, waits for them, and re-layouts: 18.9 us -> 33.9 us
    pallas_call x8 -> x9, Pallas kernels: 35 us -> 40.4 us  [call(): pl.pallas_call(functools.partial(kernel, n, dpc), in_specs=[SMEM if x.ndi...]
  transfers between devices with their start and end apart: 2 -> 47, of which waited for: 1 -> 18; matrix products, arithmetic and copies ran while one was open for 0% -> 0% of each run, Pallas kernels for 6% -> 4%
where the time goes in v3:
time: 188 us; the launch traced here: 184 us
  waiting for transfers between devices  56.5 us (30%)
  starting transfers between devices  52.5 us (28%)
  Pallas kernels  40.4 us (21%)
  local copies, waits for them, and re-layouts  33.9 us (18%)
    ppermute x45, starting transfers between devices, send(): return lax.ppermute(x, 'bl', [(i, i ^ o) for i in range(n)])  42.7 us
    pallas_call x9, Pallas kernels, call(): pl.pallas_call(functools.partial(kernel, n, dpc), in_specs=[SMEM if x.ndi...  40.4 us
    ppermute x45, waiting for transfers between devices, send(): return lax.ppermute(x, 'bl', [(i, i ^ o) for i in range(n)])  34.3 us
    unnamed x92, local copies, waits for them, and re-layouts  33.9 us
    all_to_all x2, waiting for transfers between devices, exchange(): return lax.all_to_all(x, 'bl', split_axis=0, concat_axis=0, tiled=True)  22.2 us
    all_to_all x2, starting transfers between devices, exchange(): return lax.all_to_all(x, 'bl', split_axis=0, concat_axis=0, tiled=True)  9.85 us
  transfers between devices with their start and end apart: 47, of which 18 were waited for; matrix products, arithmetic and copies ran while one was open for 0% of the time, Pallas kernels for 4%

profile of v3, /device:TPU:9, one launch (start us, length us, event | category | flops | bytes accessed | tf_op | source)
XLA Modules:
  0.0 184.3 jit_solution(8064174689401678817)
XLA Ops:
  4.3 1.4 collective-permute-start.7
  5.7 1.2 collective-permute-start.1
  6.9 2.2 %collective-permute-start.3 = (f32[328,128]{1,0:T(8,128)S(1)}, f32[328,128]{1,0:T(8,128)S(1)}, u32[]{:S(2)}, u32[]{:S(2)}) collective-permute-start(f32[328,128]{1,0:T(8,128)S(1)} %shard_map.86.rest_0_.refs_7_), channel_id=1, source_target_pairs={{0,4},{1,5},{2,6},{3,7},{4,0},{5,1},{6,2},{7,3},{8,12},{9,13},{10,... | collective-permute-start | bytes 503816 | tf_op jit(solution)/shard_map/ppermute | solution.py:302
  9.1 1.5 collective-permute-start
  10.6 2.7 %collective-permute-done.7.rest_12_.refs_19_ = f32[328,128]{1,0:T(8,128)S(1)} collective-permute-done((f32[328,128]{1,0:T(8,128)S(1)}, f32[328,128]{1,0:T(8,128)S(1)}, u32[]{:S(2)}, u32[]{:S(2)}) %collective-permute-start.7) | collective-permute-done | bytes 167968 | tf_op jit(solution)/shard_map/ppermute | solution.py:302
  13.3 1.4 collective-permute-start.2
  15.2 1.8 collective-permute-start.4
  17.0 1.2 collective-permute-start.5
  18.5 1.2 collective-permute-start.10
  19.7 2.1 %collective-permute-start.12 = (f32[328,128]{1,0:T(8,128)S(1)}, f32[328,128]{1,0:T(8,128)S(1)}, u32[]{:S(2)}, u32[]{:S(2)}) collective-permute-start(f32[328,128]{1,0:T(8,128)S(1)} %collective-permute-done.7.rest_12_.refs_19_), channel_id=1, source_target_pairs={{0,1},{1,0},{2,3},{3,2},{4,5},{5,4},{6,7},{7,6},{8,9},{9,8},{10,11... | collective-permute-start | bytes 503816 | tf_op jit(solution)/shard_map/ppermute | solution.py:302
  22.9 1.2 collective-permute-start.6
  24.1 2.4 %collective-permute-done.13.rest_14_.refs_21_ = f32[328,128]{1,0:T(8,128)S(1)} collective-permute-done((f32[328,128]{1,0:T(8,128)S(1)}, f32[328,128]{1,0:T(8,128)S(1)}, u32[]{:S(2)}, u32[]{:S(2)}) %collective-permute-start.13) | collective-permute-done | bytes 167968 | tf_op jit(solution)/shard_map/ppermute | solution.py:302
  26.5 1.2 collective-permute-start.14
  27.7 2.4 %collective-permute-done.10.rest_10_.refs_17_ = f32[328,128]{1,0:T(8,128)S(1)} collective-permute-done((f32[328,128]{1,0:T(8,128)S(1)}, f32[328,128]{1,0:T(8,128)S(1)}, u32[]{:S(2)}, u32[]{:S(2)}) %collective-permute-start.10) | collective-permute-done | bytes 167968 | tf_op jit(solution)/shard_map/ppermute | solution.py:302
  30.9 3.8 %copy-done = bf16[40,2,15,32,128]{4,3,2,1,0:T(8,128)(2,1)S(1)} copy-done((bf16[40,2,15,32,128]{4,3,2,1,0:T(8,128)(2,1)S(1)}, bf16[40,2,15,32,128]{4,3,2,1,0:T(8,128)(2,1)}, u32[]{:S(2)}) %copy-start) | copy-done | bytes 9830424
  35.7 2.8 %shard_map.88.refs_6_ = f32[40,16,128]{2,1,0:T(8,128)S(1)} custom-call(bf16[40,2,15,32,128]{4,3,2,1,0:T(8,128)(2,1)S(1)} %copy-done, s32[15,32,128]{2,1,0:T(8,128)S(1)} %copy-done.5), custom_call_target="tpu_custom_call" | custom-call | tf_op jit(solution)/shard_map/pallas_call | solution.py:327
  39.7 11.4 %shard_map.89 = f32[16,24,640]{2,1,0:T(8,128)} custom-call(s32[1]{0:T(128)} %bitcast.me_ref.refs_0_, s32[15]{0:T(128)S(1)} %copy-done.43, s32[15]{0:T(128)S(1)} %copy-done.45, bf16[40,2,15,32,128]{4,3,2,1,0:T(8,128)(2,1)S(1)} %copy-done.1, f32[2,15,32,128]{3,2,1,0:T(8,128)S(1)} %copy-done.4, s32[15,32,128]{2,1,0:T(8,128)S(1)} %copy-done.5, ...), custom_call_target="tpu_custom_call" | custom-call | tf_op jit(solution)/shard_map/pallas_call | solution.py:327
  51.1 4.8 %all-to-all-start = ((f32[16,24,640]{2,1,0:T(8,128)}), f32[16,24,640]{2,1,0:T(8,128)S(1)}, u32[]{:S(2)}, u32[]{:S(2)}) async-start(f32[16,24,640]{2,1,0:T(8,128)} %shard_map.89), calls=%async_computation | async-start | bytes 1966080 | tf_op jit(solution)/shard_map/all_to_all | solution.py:297
  67.8 2.4 %shard_map.87 = (f32[5,64,128]{2,1,0:T(8,128)S(1)}, bf16[64,512]{1,0:T(8,128)(2,1)S(1)}, f32[512,640]{1,0:T(8,128)S(1)}) custom-call(s32[1]{0:T(128)} %bitcast.me_ref.refs_0_, f32[328,128]{1,0:T(8,128)S(1)} %shard_map.86.rest_0_.refs_7_, f32[328,128]{1,0:T(8,128)S(1)} %copy-done.16, f32[328,128]{1,0:T(8,128)S(1)} %copy-done.12, f32[328,128]{1,0:T(8,128)S(1)} %copy-done.20, ...), custom_call_target="tpu_custom_call" | custom-call | tf_op jit(solution)/shard_map/pallas_call | solution.py:327
  71.6 7.8 %all-to-all-done.sums = f32[16,24,640]{2,1,0:T(8,128)S(1)} async-done(((f32[16,24,640]{2,1,0:T(8,128)}), f32[16,24,640]{2,1,0:T(8,128)S(1)}, u32[]{:S(2)}, u32[]{:S(2)}) %all-to-all-start) | async-done | bytes 983072 | tf_op jit(solution)/shard_map/all_to_all | solution.py:297
  81.2 1.5 shard_map.90.g_ref.refs_7_.g_in
  84.0 2.3 %collective-permute-start.18 = (f32[5,64,128]{2,1,0:T(8,128)S(1)}, f32[5,64,128]{2,1,0:T(8,128)S(1)}, u32[]{:S(2)}, u32[]{:S(2)}) collective-permute-start(f32[5,64,128]{2,1,0:T(8,128)S(1)} %shard_map.90.g_ref.refs_7_.g_in), channel_id=1, source_target_pairs={{0,4},{1,5},{2,6},{3,7},{4,0},{5,1},{6,2},{7,3},{8,12},{9,13},{10,... | collective-permute-start | bytes 491528 | tf_op jit(solution)/shard_map/ppermute | solution.py:302
  86.3 1.1 collective-permute-start.15
  87.3 4.3 %collective-permute-done.22.refs_19_ = f32[5,64,128]{2,1,0:T(8,128)S(1)} collective-permute-done((f32[5,64,128]{2,1,0:T(8,128)S(1)}, f32[5,64,128]{2,1,0:T(8,128)S(1)}, u32[]{:S(2)}, u32[]{:S(2)}) %collective-permute-start.22) | collective-permute-done | bytes 163872 | tf_op jit(solution)/shard_map/ppermute | solution.py:302
  93.0 2.0 %collective-permute-start.20 = (f32[5,64,128]{2,1,0:T(8,128)S(1)}, f32[5,64,128]{2,1,0:T(8,128)S(1)}, u32[]{:S(2)}, u32[]{:S(2)}) collective-permute-start(f32[5,64,128]{2,1,0:T(8,128)S(1)} %collective-permute-done.18.refs_11_), channel_id=1, source_target_pairs={{0,2},{1,3},{2,0},{3,1},{4,6},{5,7},{6,4},{7,5},{8,10},{9,11},{10,... | collective-permute-start | bytes 491528 | tf_op jit(solution)/shard_map/ppermute | solution.py:302
  95.0 2.0 %collective-permute-done.23.refs_15_ = f32[5,64,128]{2,1,0:T(8,128)S(1)} collective-permute-done((f32[5,64,128]{2,1,0:T(8,128)S(1)}, f32[5,64,128]{2,1,0:T(8,128)S(1)}, u32[]{:S(2)}, u32[]{:S(2)}) %collective-permute-start.23) | collective-permute-done | bytes 163872 | tf_op jit(solution)/shard_map/ppermute | solution.py:302
  97.0 1.6 collective-permute-start.25
  98.6 1.6 collective-permute-start.27
  100.7 2.3 %collective-permute-done.28.refs_21_ = f32[5,64,128]{2,1,0:T(8,128)S(1)} collective-permute-done((f32[5,64,128]{2,1,0:T(8,128)S(1)}, f32[5,64,128]{2,1,0:T(8,128)S(1)}, u32[]{:S(2)}, u32[]{:S(2)}) %collective-permute-start.28) | collective-permute-done | bytes 163872 | tf_op jit(solution)/shard_map/ppermute | solution.py:302
  103.8 2.7 %collective-permute-done.25.refs_17_ = f32[5,64,128]{2,1,0:T(8,128)S(1)} collective-permute-done((f32[5,64,128]{2,1,0:T(8,128)S(1)}, f32[5,64,128]{2,1,0:T(8,128)S(1)}, u32[]{:S(2)}, u32[]{:S(2)}) %collective-permute-start.25) | collective-permute-done | bytes 163872 | tf_op jit(solution)/shard_map/ppermute | solution.py:302
  108.2 3.8 %copy-done.2 = bf16[40,2,15,32,128]{4,3,2,1,0:T(8,128)(2,1)S(1)} copy-done((bf16[40,2,15,32,128]{4,3,2,1,0:T(8,128)(2,1)S(1)}, bf16[40,2,15,32,128]{4,3,2,1,0:T(8,128)(2,1)}, u32[]{:S(2)}) %copy-start.2) | copy-done | bytes 9830424
  112.0 11.9 %shard_map.92 = f32[16,16,640]{2,1,0:T(8,128)} custom-call(s32[1]{0:T(128)} %bitcast.me_ref.refs_0_, s32[15]{0:T(128)S(1)} %copy-done.43, s32[15]{0:T(128)S(1)} %copy-done.45, bf16[40,2,15,32,128]{4,3,2,1,0:T(8,128)(2,1)S(1)} %copy-done.2, f32[2,15,32,128]{3,2,1,0:T(8,128)S(1)} %copy-done.4, s32[15,32,128]{2,1,0:T(8,128)S(1)} %copy-done.6, ...), custom_call_target="tpu_custom_call" | custom-call | tf_op jit(solution)/shard_map/pallas_call | solution.py:327
  123.9 5.1 %all-to-all-start.1 = ((f32[16,16,640]{2,1,0:T(8,128)}), f32[16,16,640]{2,1,0:T(8,128)S(1)}, u32[]{:S(2)}, u32[]{:S(2)}) async-start(f32[16,16,640]{2,1,0:T(8,128)} %shard_map.92), calls=%async_computation.1 | async-start | bytes 1310720 | tf_op jit(solution)/shard_map/all_to_all | solution.py:297
  129.0 1.4 shard_map.91
  130.4 1.1 copy-done.7
  131.5 14.4 %all-to-all-done.1.sums = f32[16,16,640]{2,1,0:T(8,128)S(1)} async-done(((f32[16,16,640]{2,1,0:T(8,128)}), f32[16,16,640]{2,1,0:T(8,128)S(1)}, u32[]{:S(2)}, u32[]{:S(2)}) %all-to-all-start.1) | async-done | bytes 655392 | tf_op jit(solution)/shard_map/all_to_all | solution.py:297
  145.8 1.3 copy-done.8
  149.0 2.3 %collective-permute-start.33 = (f32[5,64,128]{2,1,0:T(8,128)S(1)}, f32[5,64,128]{2,1,0:T(8,128)S(1)}, u32[]{:S(2)}, u32[]{:S(2)}) collective-permute-start(f32[5,64,128]{2,1,0:T(8,128)S(1)} %shard_map.93.rest_0_), channel_id=1, source_target_pairs={{0,4},{1,5},{2,6},{3,7},{4,0},{5,1},{6,2},{7,3},{8,12},{9,13},{10,... | collective-permute-start | bytes 491528 | tf_op jit(solution)/shard_map/ppermute | solution.py:302
  152.3 5.4 %collective-permute-done.37.rest_12_ = f32[5,64,128]{2,1,0:T(8,128)S(1)} collective-permute-done((f32[5,64,128]{2,1,0:T(8,128)S(1)}, f32[5,64,128]{2,1,0:T(8,128)S(1)}, u32[]{:S(2)}, u32[]{:S(2)}) %collective-permute-start.37) | collective-permute-done | bytes 163872 | tf_op jit(solution)/shard_map/ppermute | solution.py:302
  158.4 1.6 collective-permute-start.35
  160.0 2.9 %collective-permute-done.38.rest_8_ = f32[5,64,128]{2,1,0:T(8,128)S(1)} collective-permute-done((f32[5,64,128]{2,1,0:T(8,128)S(1)}, f32[5,64,128]{2,1,0:T(8,128)S(1)}, u32[]{:S(2)}, u32[]{:S(2)}) %collective-permute-start.38) | collective-permute-done | bytes 163872 | tf_op jit(solution)/shard_map/ppermute | solution.py:302
  162.9 2.1 %collective-permute-start.42 = (f32[5,64,128]{2,1,0:T(8,128)S(1)}, f32[5,64,128]{2,1,0:T(8,128)S(1)}, u32[]{:S(2)}, u32[]{:S(2)}) collective-permute-start(f32[5,64,128]{2,1,0:T(8,128)S(1)} %collective-permute-done.37.rest_12_), channel_id=1, source_target_pairs={{0,1},{1,0},{2,3},{3,2},{4,5},{5,4},{6,7},{7,6},{8,9},{9,8},{10,11... | collective-permute-start | bytes 491528 | tf_op jit(solution)/shard_map/ppermute | solution.py:302
  165.9 1.6 collective-permute-done.43.rest_14_
  167.5 1.9 %collective-permute-start.44 = (f32[5,64,128]{2,1,0:T(8,128)S(1)}, f32[5,64,128]{2,1,0:T(8,128)S(1)}, u32[]{:S(2)}, u32[]{:S(2)}) collective-permute-start(f32[5,64,128]{2,1,0:T(8,128)S(1)} %collective-permute-done.43.rest_14_), channel_id=1, source_target_pairs={{0,1},{1,0},{2,3},{3,2},{4,5},{5,4},{6,7},{7,6},{8,9},{9,8},{10,11... | collective-permute-start | bytes 491528 | tf_op jit(solution)/shard_map/ppermute | solution.py:302
  169.4 1.6 collective-permute-done.40.rest_10_
  171.0 1.2 collective-permute-start.41
  173.2 3.8 %copy-done.3 = bf16[40,2,15,32,128]{4,3,2,1,0:T(8,128)(2,1)S(1)} copy-done((bf16[40,2,15,32,128]{4,3,2,1,0:T(8,128)(2,1)S(1)}, bf16[40,2,15,32,128]{4,3,2,1,0:T(8,128)(2,1)}, u32[]{:S(2)}) %copy-start.3) | copy-done | bytes 9830424
  177.0 7.3 %shard_map.94 = (f32[2,15,32,128]{3,2,1,0:T(8,128)}, f32[2,160,128]{2,1,0:T(8,128)}) custom-call(s32[1]{0:T(128)} %bitcast.me_ref.refs_0_, s32[15]{0:T(128)S(1)} %copy-done.43, s32[15]{0:T(128)S(1)} %copy-done.45, bf16[40,2,15,32,128]{4,3,2,1,0:T(8,128)(2,1)S(1)} %copy-done.3, f32[2,15,32,128]{3,2,1,0:T(8,128)S(1)} %copy-done.4, ...), custom_call_target="tpu_custom_call" | custom-call | tf_op jit(solution)/shard_map/pallas_call | solution.py:327
  (147 shorter events, 34.3 us)
Async XLA Ops:
  4.3 9.0 %collective-permute-start.7 = (f32[328,128]{1,0:T(8,128)S(1)}, f32[328,128]{1,0:T(8,128)S(1)}, u32[]{:S(2)}, u32[]{:S(2)}) collective-permute-start(f32[328,128]{1,0:T(8,128)S(1)} %shard_map.86.rest_0_.refs_7_), channel_id=1, source_target_pairs={{0,12},{1,13},{2,14},{3,15},{4,8},{5,9},{6,10},{7,11},{8,4},{9,5},... | collective-permute-start | bytes 503816 | tf_op jit(solution)/shard_map/ppermute | solution.py:302
  5.7 7.7 %collective-permute-start.1 = (f32[328,128]{1,0:T(8,128)S(1)}, f32[328,128]{1,0:T(8,128)S(1)}, u32[]{:S(2)}, u32[]{:S(2)}) collective-permute-start(f32[328,128]{1,0:T(8,128)S(1)} %shard_map.86.rest_0_.refs_7_), channel_id=1, source_target_pairs={{0,2},{1,3},{2,0},{3,1},{4,6},{5,7},{6,4},{7,5},{8,10},{9,11},{10,... | collective-permute-start | bytes 503816 | tf_op jit(solution)/shard_map/ppermute | solution.py:302
  6.9 8.4 %collective-permute-start.3 = (f32[328,128]{1,0:T(8,128)S(1)}, f32[328,128]{1,0:T(8,128)S(1)}, u32[]{:S(2)}, u32[]{:S(2)}) collective-permute-start(f32[328,128]{1,0:T(8,128)S(1)} %shard_map.86.rest_0_.refs_7_), channel_id=1, source_target_pairs={{0,4},{1,5},{2,6},{3,7},{4,0},{5,1},{6,2},{7,3},{8,12},{9,13},{10,... | collective-permute-start | bytes 503816 | tf_op jit(solution)/shard_map/ppermute | solution.py:302
  9.1 9.1 %collective-permute-start = (f32[328,128]{1,0:T(8,128)S(1)}, f32[328,128]{1,0:T(8,128)S(1)}, u32[]{:S(2)}, u32[]{:S(2)}) collective-permute-start(f32[328,128]{1,0:T(8,128)S(1)} %shard_map.86.rest_0_.refs_7_), channel_id=1, source_target_pairs={{0,1},{1,0},{2,3},{3,2},{4,5},{5,4},{6,7},{7,6},{8,9},{9,8},{10,11... | collective-permute-start | bytes 503816 | tf_op jit(solution)/shard_map/ppermute | solution.py:302
  13.3 5.2 %collective-permute-start.8 = (f32[328,128]{1,0:T(8,128)S(1)}, f32[328,128]{1,0:T(8,128)S(1)}, u32[]{:S(2)}, u32[]{:S(2)}) collective-permute-start(f32[328,128]{1,0:T(8,128)S(1)} %collective-permute-done.7.rest_12_.refs_19_), channel_id=1, source_target_pairs={{0,4},{1,5},{2,6},{3,7},{4,0},{5,1},{6,2},{7,3},{8,12},{9,13},{10,... | collective-permute-start | bytes 503816 | tf_op jit(solution)/shard_map/ppermute | solution.py:302
  13.3 6.4 %collective-permute-start.2 = (f32[328,128]{1,0:T(8,128)S(1)}, f32[328,128]{1,0:T(8,128)S(1)}, u32[]{:S(2)}, u32[]{:S(2)}) collective-permute-start(f32[328,128]{1,0:T(8,128)S(1)} %collective-permute-done.1.rest_2_.refs_9_), channel_id=1, source_target_pairs={{0,1},{1,0},{2,3},{3,2},{4,5},{5,4},{6,7},{7,6},{8,9},{9,8},{10,11... | collective-permute-start | bytes 503816 | tf_op jit(solution)/shard_map/ppermute | solution.py:302
  15.2 6.6 %collective-permute-start.4 = (f32[328,128]{1,0:T(8,128)S(1)}, f32[328,128]{1,0:T(8,128)S(1)}, u32[]{:S(2)}, u32[]{:S(2)}) collective-permute-start(f32[328,128]{1,0:T(8,128)S(1)} %collective-permute-done.3.rest_4_.refs_11_), channel_id=1, source_target_pairs={{0,1},{1,0},{2,3},{3,2},{4,5},{5,4},{6,7},{7,6},{8,9},{9,8},{10,11... | collective-permute-start | bytes 503816 | tf_op jit(solution)/shard_map/ppermute | solution.py:302
  17.0 5.9 %collective-permute-start.5 = (f32[328,128]{1,0:T(8,128)S(1)}, f32[328,128]{1,0:T(8,128)S(1)}, u32[]{:S(2)}, u32[]{:S(2)}) collective-permute-start(f32[328,128]{1,0:T(8,128)S(1)} %collective-permute-done.3.rest_4_.refs_11_), channel_id=1, source_target_pairs={{0,2},{1,3},{2,0},{3,1},{4,6},{5,7},{6,4},{7,5},{8,10},{9,11},{10,... | collective-permute-start | bytes 503816 | tf_op jit(solution)/shard_map/ppermute | solution.py:302
  18.2 8.3 %collective-permute-start.13 = (f32[328,128]{1,0:T(8,128)S(1)}, f32[328,128]{1,0:T(8,128)S(1)}, u32[]{:S(2)}, u32[]{:S(2)}) collective-permute-start(f32[328,128]{1,0:T(8,128)S(1)} %collective-permute-done.7.rest_12_.refs_19_), channel_id=1, source_target_pairs={{0,2},{1,3},{2,0},{3,1},{4,6},{5,7},{6,4},{7,5},{8,10},{9,11},{10,... | collective-permute-start | bytes 503816 | tf_op jit(solution)/shard_map/ppermute | solution.py:302
  18.5 11.6 %collective-permute-start.10 = (f32[328,128]{1,0:T(8,128)S(1)}, f32[328,128]{1,0:T(8,128)S(1)}, u32[]{:S(2)}, u32[]{:S(2)}) collective-permute-start(f32[328,128]{1,0:T(8,128)S(1)} %collective-permute-done.8.rest_8_.refs_15_), channel_id=1, source_target_pairs={{0,2},{1,3},{2,0},{3,1},{4,6},{5,7},{6,4},{7,5},{8,10},{9,11},{10,... | collective-permute-start | bytes 503816 | tf_op jit(solution)/shard_map/ppermute | solution.py:302
  19.7 18.7 %collective-permute-start.12 = (f32[328,128]{1,0:T(8,128)S(1)}, f32[328,128]{1,0:T(8,128)S(1)}, u32[]{:S(2)}, u32[]{:S(2)}) collective-permute-start(f32[328,128]{1,0:T(8,128)S(1)} %collective-permute-done.7.rest_12_.refs_19_), channel_id=1, source_target_pairs={{0,1},{1,0},{2,3},{3,2},{4,5},{5,4},{6,7},{7,6},{8,9},{9,8},{10,11... | collective-permute-start | bytes 503816 | tf_op jit(solution)/shard_map/ppermute | solution.py:302
  21.8 16.6 %collective-permute-start.9 = (f32[328,128]{1,0:T(8,128)S(1)}, f32[328,128]{1,0:T(8,128)S(1)}, u32[]{:S(2)}, u32[]{:S(2)}) collective-permute-start(f32[328,128]{1,0:T(8,128)S(1)} %collective-permute-done.8.rest_8_.refs_15_), channel_id=1, source_target_pairs={{0,1},{1,0},{2,3},{3,2},{4,5},{5,4},{6,7},{7,6},{8,9},{9,8},{10,11... | collective-permute-start | bytes 503816 | tf_op jit(solution)/shard_map/ppermute | solution.py:302
  22.9 15.5 %collective-permute-start.6 = (f32[328,128]{1,0:T(8,128)S(1)}, f32[328,128]{1,0:T(8,128)S(1)}, u32[]{:S(2)}, u32[]{:S(2)}) collective-permute-start(f32[328,128]{1,0:T(8,128)S(1)} %collective-permute-done.5.rest_6_.refs_13_), channel_id=1, source_target_pairs={{0,1},{1,0},{2,3},{3,2},{4,5},{5,4},{6,7},{7,6},{8,9},{9,8},{10,11... | collective-permute-start | bytes 503816 | tf_op jit(solution)/shard_map/ppermute | solution.py:302
  26.5 12.0 %collective-permute-start.14 = (f32[328,128]{1,0:T(8,128)S(1)}, f32[328,128]{1,0:T(8,128)}, u32[]{:S(2)}, u32[]{:S(2)}) collective-permute-start(f32[328,128]{1,0:T(8,128)S(1)} %collective-permute-done.13.rest_14_.refs_21_), channel_id=1, source_target_pairs={{0,1},{1,0},{2,3},{3,2},{4,5},{5,4},{6,7},{7,6},{8,9},{9,8},{10,11... | collective-permute-start | bytes 503816 | tf_op jit(solution)/shard_map/ppermute | solution.py:302
  30.1 8.4 %collective-permute-start.11 = (f32[328,128]{1,0:T(8,128)S(1)}, f32[328,128]{1,0:T(8,128)}, u32[]{:S(2)}, u32[]{:S(2)}) collective-permute-start(f32[328,128]{1,0:T(8,128)S(1)} %collective-permute-done.10.rest_10_.refs_17_), channel_id=1, source_target_pairs={{0,1},{1,0},{2,3},{3,2},{4,5},{5,4},{6,7},{7,6},{8,9},{9,8},{10,11... | collective-permute-start | bytes 503816 | tf_op jit(solution)/shard_map/ppermute | solution.py:302
  51.1 28.3 %all-to-all-start = ((f32[16,24,640]{2,1,0:T(8,128)}), f32[16,24,640]{2,1,0:T(8,128)S(1)}, u32[]{:S(2)}, u32[]{:S(2)}) async-start(f32[16,24,640]{2,1,0:T(8,128)} %shard_map.89), calls=%async_computation | async-start | bytes 1966080 | tf_op jit(solution)/shard_map/all_to_all | solution.py:297
  81.2 27.0 %copy-start.6 = (s32[15,32,128]{2,1,0:T(8,128)S(1)}, s32[15,32,128]{2,1,0:T(8,128)}, u32[]{:S(2)}) copy-start(s32[15,32,128]{2,1,0:T(8,128)} %mask_ref.3) | copy-start | bytes 737284
  82.7 8.9 %collective-permute-start.22 = (f32[5,64,128]{2,1,0:T(8,128)S(1)}, f32[5,64,128]{2,1,0:T(8,128)S(1)}, u32[]{:S(2)}, u32[]{:S(2)}) collective-permute-start(f32[5,64,128]{2,1,0:T(8,128)S(1)} %shard_map.90.g_ref.refs_7_.g_in), channel_id=1, source_target_pairs={{0,12},{1,13},{2,14},{3,15},{4,8},{5,9},{6,10},{7,11},{8,4},{9,5},... | collective-permute-start | bytes 491528 | tf_op jit(solution)/shard_map/ppermute | solution.py:302
  83.7 7.9 %collective-permute-start.16 = (f32[5,64,128]{2,1,0:T(8,128)S(1)}, f32[5,64,128]{2,1,0:T(8,128)S(1)}, u32[]{:S(2)}, u32[]{:S(2)}) collective-permute-start(f32[5,64,128]{2,1,0:T(8,128)S(1)} %shard_map.90.g_ref.refs_7_.g_in), channel_id=1, source_target_pairs={{0,2},{1,3},{2,0},{3,1},{4,6},{5,7},{6,4},{7,5},{8,10},{9,11},{10,... | collective-permute-start | bytes 491528 | tf_op jit(solution)/shard_map/ppermute | solution.py:302
  84.0 8.4 %collective-permute-start.18 = (f32[5,64,128]{2,1,0:T(8,128)S(1)}, f32[5,64,128]{2,1,0:T(8,128)S(1)}, u32[]{:S(2)}, u32[]{:S(2)}) collective-permute-start(f32[5,64,128]{2,1,0:T(8,128)S(1)} %shard_map.90.g_ref.refs_7_.g_in), channel_id=1, source_target_pairs={{0,4},{1,5},{2,6},{3,7},{4,0},{5,1},{6,2},{7,3},{8,12},{9,13},{10,... | collective-permute-start | bytes 491528 | tf_op jit(solution)/shard_map/ppermute | solution.py:302
  86.3 8.7 %collective-permute-start.15 = (f32[5,64,128]{2,1,0:T(8,128)S(1)}, f32[5,64,128]{2,1,0:T(8,128)S(1)}, u32[]{:S(2)}, u32[]{:S(2)}) collective-permute-start(f32[5,64,128]{2,1,0:T(8,128)S(1)} %shard_map.90.g_ref.refs_7_.g_in), channel_id=1, source_target_pairs={{0,1},{1,0},{2,3},{3,2},{4,5},{5,4},{6,7},{7,6},{8,9},{9,8},{10,11... | collective-permute-start | bytes 491528 | tf_op jit(solution)/shard_map/ppermute | solution.py:302
  91.6 5.3 %collective-permute-start.23 = (f32[5,64,128]{2,1,0:T(8,128)S(1)}, f32[5,64,128]{2,1,0:T(8,128)S(1)}, u32[]{:S(2)}, u32[]{:S(2)}) collective-permute-start(f32[5,64,128]{2,1,0:T(8,128)S(1)} %collective-permute-done.22.refs_19_), channel_id=1, source_target_pairs={{0,4},{1,5},{2,6},{3,7},{4,0},{5,1},{6,2},{7,3},{8,12},{9,13},{10,... | collective-permute-start | bytes 491528 | tf_op jit(solution)/shard_map/ppermute | solution.py:302
  91.6 7.0 %collective-permute-start.17 = (f32[5,64,128]{2,1,0:T(8,128)S(1)}, f32[5,64,128]{2,1,0:T(8,128)S(1)}, u32[]{:S(2)}, u32[]{:S(2)}) collective-permute-start(f32[5,64,128]{2,1,0:T(8,128)S(1)} %collective-permute-done.16.refs_9_), channel_id=1, source_target_pairs={{0,1},{1,0},{2,3},{3,2},{4,5},{5,4},{6,7},{7,6},{8,9},{9,8},{10,11... | collective-permute-start | bytes 491528 | tf_op jit(solution)/shard_map/ppermute | solution.py:302
  92.4 7.8 %collective-permute-start.19 = (f32[5,64,128]{2,1,0:T(8,128)S(1)}, f32[5,64,128]{2,1,0:T(8,128)S(1)}, u32[]{:S(2)}, u32[]{:S(2)}) collective-permute-start(f32[5,64,128]{2,1,0:T(8,128)S(1)} %collective-permute-done.18.refs_11_), channel_id=1, source_target_pairs={{0,1},{1,0},{2,3},{3,2},{4,5},{5,4},{6,7},{7,6},{8,9},{9,8},{10,11... | collective-permute-start | bytes 491528 | tf_op jit(solution)/shard_map/ppermute | solution.py:302
  93.0 7.3 %collective-permute-start.20 = (f32[5,64,128]{2,1,0:T(8,128)S(1)}, f32[5,64,128]{2,1,0:T(8,128)S(1)}, u32[]{:S(2)}, u32[]{:S(2)}) collective-permute-start(f32[5,64,128]{2,1,0:T(8,128)S(1)} %collective-permute-done.18.refs_11_), channel_id=1, source_target_pairs={{0,2},{1,3},{2,0},{3,1},{4,6},{5,7},{6,4},{7,5},{8,10},{9,11},{10,... | collective-permute-start | bytes 491528 | tf_op jit(solution)/shard_map/ppermute | solution.py:302
  95.0 8.1 %collective-permute-start.28 = (f32[5,64,128]{2,1,0:T(8,128)S(1)}, f32[5,64,128]{2,1,0:T(8,128)S(1)}, u32[]{:S(2)}, u32[]{:S(2)}) collective-permute-start(f32[5,64,128]{2,1,0:T(8,128)S(1)} %collective-permute-done.22.refs_19_), channel_id=1, source_target_pairs={{0,2},{1,3},{2,0},{3,1},{4,6},{5,7},{6,4},{7,5},{8,10},{9,11},{10,... | collective-permute-start | bytes 491528 | tf_op jit(solution)/shard_map/ppermute | solution.py:302
  97.0 9.6 %collective-permute-start.25 = (f32[5,64,128]{2,1,0:T(8,128)S(1)}, f32[5,64,128]{2,1,0:T(8,128)S(1)}, u32[]{:S(2)}, u32[]{:S(2)}) collective-permute-start(f32[5,64,128]{2,1,0:T(8,128)S(1)} %collective-permute-done.23.refs_15_), channel_id=1, source_target_pairs={{0,2},{1,3},{2,0},{3,1},{4,6},{5,7},{6,4},{7,5},{8,10},{9,11},{10,... | collective-permute-start | bytes 491528 | tf_op jit(solution)/shard_map/ppermute | solution.py:302
  98.6 8.5 %collective-permute-start.27 = (f32[5,64,128]{2,1,0:T(8,128)S(1)}, f32[5,64,128]{2,1,0:T(8,128)S(1)}, u32[]{:S(2)}, u32[]{:S(2)}) collective-permute-start(f32[5,64,128]{2,1,0:T(8,128)S(1)} %collective-permute-done.22.refs_19_), channel_id=1, source_target_pairs={{0,1},{1,0},{2,3},{3,2},{4,5},{5,4},{6,7},{7,6},{8,9},{9,8},{10,11... | collective-permute-start | bytes 491528 | tf_op jit(solution)/shard_map/ppermute | solution.py:302
  100.2 7.0 %collective-permute-start.24 = (f32[5,64,128]{2,1,0:T(8,128)S(1)}, f32[5,64,128]{2,1,0:T(8,128)S(1)}, u32[]{:S(2)}, u32[]{:S(2)}) collective-permute-start(f32[5,64,128]{2,1,0:T(8,128)S(1)} %collective-permute-done.23.refs_15_), channel_id=1, source_target_pairs={{0,1},{1,0},{2,3},{3,2},{4,5},{5,4},{6,7},{7,6},{8,9},{9,8},{10,11... | collective-permute-start | bytes 491528 | tf_op jit(solution)/shard_map/ppermute | solution.py:302
  100.3 6.9 %collective-permute-start.21 = (f32[5,64,128]{2,1,0:T(8,128)S(1)}, f32[5,64,128]{2,1,0:T(8,128)S(1)}, u32[]{:S(2)}, u32[]{:S(2)}) collective-permute-start(f32[5,64,128]{2,1,0:T(8,128)S(1)} %collective-permute-done.20.refs_13_), channel_id=1, source_target_pairs={{0,1},{1,0},{2,3},{3,2},{4,5},{5,4},{6,7},{7,6},{8,9},{9,8},{10,11... | collective-permute-start | bytes 491528 | tf_op jit(solution)/shard_map/ppermute | solution.py:302
  103.1 4.1 %collective-permute-start.29 = (f32[5,64,128]{2,1,0:T(8,128)S(1)}, f32[5,64,128]{2,1,0:T(8,128)S(1)}, u32[]{:S(2)}, u32[]{:S(2)}) collective-permute-start(f32[5,64,128]{2,1,0:T(8,128)S(1)} %collective-permute-done.28.refs_21_), channel_id=1, source_target_pairs={{0,1},{1,0},{2,3},{3,2},{4,5},{5,4},{6,7},{7,6},{8,9},{9,8},{10,11... | collective-permute-start | bytes 491528 | tf_op jit(solution)/shard_map/ppermute | solution.py:302
  106.6 1.6 collective-permute-start.26
  123.9 21.9 %all-to-all-start.1 = ((f32[16,16,640]{2,1,0:T(8,128)}), f32[16,16,640]{2,1,0:T(8,128)S(1)}, u32[]{:S(2)}, u32[]{:S(2)}) async-start(f32[16,16,640]{2,1,0:T(8,128)} %shard_map.92), calls=%async_computation.1 | async-start | bytes 1310720 | tf_op jit(solution)/shard_map/all_to_all | solution.py:297
  148.1 9.6 %collective-permute-start.37 = (f32[5,64,128]{2,1,0:T(8,128)S(1)}, f32[5,64,128]{2,1,0:T(8,128)S(1)}, u32[]{:S(2)}, u32[]{:S(2)}) collective-permute-start(f32[5,64,128]{2,1,0:T(8,128)S(1)} %shard_map.93.rest_0_), channel_id=1, source_target_pairs={{0,12},{1,13},{2,14},{3,15},{4,8},{5,9},{6,10},{7,11},{8,4},{9,5},... | collective-permute-start | bytes 491528 | tf_op jit(solution)/shard_map/ppermute | solution.py:302
  148.4 9.3 %collective-permute-start.31 = (f32[5,64,128]{2,1,0:T(8,128)S(1)}, f32[5,64,128]{2,1,0:T(8,128)S(1)}, u32[]{:S(2)}, u32[]{:S(2)}) collective-permute-start(f32[5,64,128]{2,1,0:T(8,128)S(1)} %shard_map.93.rest_0_), channel_id=1, source_target_pairs={{0,2},{1,3},{2,0},{3,1},{4,6},{5,7},{6,4},{7,5},{8,10},{9,11},{10,... | collective-permute-start | bytes 491528 | tf_op jit(solution)/shard_map/ppermute | solution.py:302
  149.0 9.3 %collective-permute-start.33 = (f32[5,64,128]{2,1,0:T(8,128)S(1)}, f32[5,64,128]{2,1,0:T(8,128)S(1)}, u32[]{:S(2)}, u32[]{:S(2)}) collective-permute-start(f32[5,64,128]{2,1,0:T(8,128)S(1)} %shard_map.93.rest_0_), channel_id=1, source_target_pairs={{0,4},{1,5},{2,6},{3,7},{4,0},{5,1},{6,2},{7,3},{8,12},{9,13},{10,... | collective-permute-start | bytes 491528 | tf_op jit(solution)/shard_map/ppermute | solution.py:302
  151.3 8.7 %collective-permute-start.30 = (f32[5,64,128]{2,1,0:T(8,128)S(1)}, f32[5,64,128]{2,1,0:T(8,128)S(1)}, u32[]{:S(2)}, u32[]{:S(2)}) collective-permute-start(f32[5,64,128]{2,1,0:T(8,128)S(1)} %shard_map.93.rest_0_), channel_id=1, source_target_pairs={{0,1},{1,0},{2,3},{3,2},{4,5},{5,4},{6,7},{7,6},{8,9},{9,8},{10,11... | collective-permute-start | bytes 491528 | tf_op jit(solution)/shard_map/ppermute | solution.py:302
  157.7 5.2 %collective-permute-start.38 = (f32[5,64,128]{2,1,0:T(8,128)S(1)}, f32[5,64,128]{2,1,0:T(8,128)S(1)}, u32[]{:S(2)}, u32[]{:S(2)}) collective-permute-start(f32[5,64,128]{2,1,0:T(8,128)S(1)} %collective-permute-done.37.rest_12_), channel_id=1, source_target_pairs={{0,4},{1,5},{2,6},{3,7},{4,0},{5,1},{6,2},{7,3},{8,12},{9,13},{10,... | collective-permute-start | bytes 491528 | tf_op jit(solution)/shard_map/ppermute | solution.py:302
  157.7 5.2 %collective-permute-start.32 = (f32[5,64,128]{2,1,0:T(8,128)S(1)}, f32[5,64,128]{2,1,0:T(8,128)S(1)}, u32[]{:S(2)}, u32[]{:S(2)}) collective-permute-start(f32[5,64,128]{2,1,0:T(8,128)S(1)} %collective-permute-done.31.rest_2_), channel_id=1, source_target_pairs={{0,1},{1,0},{2,3},{3,2},{4,5},{5,4},{6,7},{7,6},{8,9},{9,8},{10,11... | collective-permute-start | bytes 491528 | tf_op jit(solution)/shard_map/ppermute | solution.py:302
  158.3 6.7 %collective-permute-start.34 = (f32[5,64,128]{2,1,0:T(8,128)S(1)}, f32[5,64,128]{2,1,0:T(8,128)S(1)}, u32[]{:S(2)}, u32[]{:S(2)}) collective-permute-start(f32[5,64,128]{2,1,0:T(8,128)S(1)} %collective-permute-done.33.rest_4_), channel_id=1, source_target_pairs={{0,1},{1,0},{2,3},{3,2},{4,5},{5,4},{6,7},{7,6},{8,9},{9,8},{10,11... | collective-permute-start | bytes 491528 | tf_op jit(solution)/shard_map/ppermute | solution.py:302
  158.4 6.6 %collective-permute-start.35 = (f32[5,64,128]{2,1,0:T(8,128)S(1)}, f32[5,64,128]{2,1,0:T(8,128)S(1)}, u32[]{:S(2)}, u32[]{:S(2)}) collective-permute-start(f32[5,64,128]{2,1,0:T(8,128)S(1)} %collective-permute-done.33.rest_4_), channel_id=1, source_target_pairs={{0,2},{1,3},{2,0},{3,1},{4,6},{5,7},{6,4},{7,5},{8,10},{9,11},{10,... | collective-permute-start | bytes 491528 | tf_op jit(solution)/shard_map/ppermute | solution.py:302
  160.0 7.5 %collective-permute-start.43 = (f32[5,64,128]{2,1,0:T(8,128)S(1)}, f32[5,64,128]{2,1,0:T(8,128)S(1)}, u32[]{:S(2)}, u32[]{:S(2)}) collective-permute-start(f32[5,64,128]{2,1,0:T(8,128)S(1)} %collective-permute-done.37.rest_12_), channel_id=1, source_target_pairs={{0,2},{1,3},{2,0},{3,1},{4,6},{5,7},{6,4},{7,5},{8,10},{9,11},{10,... | collective-permute-start | bytes 491528 | tf_op jit(solution)/shard_map/ppermute | solution.py:302
  162.9 8.1 %collective-permute-start.40 = (f32[5,64,128]{2,1,0:T(8,128)S(1)}, f32[5,64,128]{2,1,0:T(8,128)S(1)}, u32[]{:S(2)}, u32[]{:S(2)}) collective-permute-start(f32[5,64,128]{2,1,0:T(8,128)S(1)} %collective-permute-done.38.rest_8_), channel_id=1, source_target_pairs={{0,2},{1,3},{2,0},{3,1},{4,6},{5,7},{6,4},{7,5},{8,10},{9,11},{10,... | collective-permute-start | bytes 491528 | tf_op jit(solution)/shard_map/ppermute | solution.py:302
  162.9 9.2 %collective-permute-start.42 = (f32[5,64,128]{2,1,0:T(8,128)S(1)}, f32[5,64,128]{2,1,0:T(8,128)S(1)}, u32[]{:S(2)}, u32[]{:S(2)}) collective-permute-start(f32[5,64,128]{2,1,0:T(8,128)S(1)} %collective-permute-done.37.rest_12_), channel_id=1, source_target_pairs={{0,1},{1,0},{2,3},{3,2},{4,5},{5,4},{6,7},{7,6},{8,9},{9,8},{10,11... | collective-permute-start | bytes 491528 | tf_op jit(solution)/shard_map/ppermute | solution.py:302
  165.0 7.2 %collective-permute-start.39 = (f32[5,64,128]{2,1,0:T(8,128)S(1)}, f32[5,64,128]{2,1,0:T(8,128)S(1)}, u32[]{:S(2)}, u32[]{:S(2)}) collective-permute-start(f32[5,64,128]{2,1,0:T(8,128)S(1)} %collective-permute-done.38.rest_8_), channel_id=1, source_target_pairs={{0,1},{1,0},{2,3},{3,2},{4,5},{5,4},{6,7},{7,6},{8,9},{9,8},{10,11... | collective-permute-start | bytes 491528 | tf_op jit(solution)/shard_map/ppermute | solution.py:302
  165.1 7.1 %collective-permute-start.36 = (f32[5,64,128]{2,1,0:T(8,128)S(1)}, f32[5,64,128]{2,1,0:T(8,128)S(1)}, u32[]{:S(2)}, u32[]{:S(2)}) collective-permute-start(f32[5,64,128]{2,1,0:T(8,128)S(1)} %collective-permute-done.35.rest_6_), channel_id=1, source_target_pairs={{0,1},{1,0},{2,3},{3,2},{4,5},{5,4},{6,7},{7,6},{8,9},{9,8},{10,11... | collective-permute-start | bytes 491528 | tf_op jit(solution)/shard_map/ppermute | solution.py:302
  167.5 4.7 %collective-permute-start.44 = (f32[5,64,128]{2,1,0:T(8,128)S(1)}, f32[5,64,128]{2,1,0:T(8,128)S(1)}, u32[]{:S(2)}, u32[]{:S(2)}) collective-permute-start(f32[5,64,128]{2,1,0:T(8,128)S(1)} %collective-permute-done.43.rest_14_), channel_id=1, source_target_pairs={{0,1},{1,0},{2,3},{3,2},{4,5},{5,4},{6,7},{7,6},{8,9},{9,8},{10,11... | collective-permute-start | bytes 491528 | tf_op jit(solution)/shard_map/ppermute | solution.py:302
  171.0 2.2 %collective-permute-start.41 = (f32[5,64,128]{2,1,0:T(8,128)S(1)}, f32[5,64,128]{2,1,0:T(8,128)S(1)}, u32[]{:S(2)}, u32[]{:S(2)}) collective-permute-start(f32[5,64,128]{2,1,0:T(8,128)S(1)} %collective-permute-done.40.rest_10_), channel_id=1, source_target_pairs={{0,1},{1,0},{2,3},{3,2},{4,5},{5,4},{6,7},{7,6},{8,9},{9,8},{10,11... | collective-permute-start | bytes 491528 | tf_op jit(solution)/shard_map/ppermute | solution.py:302
  (45 other events, 277.8 us)

commit v4 on v3

v4 whole, which is shorter than its diff:
```python
import functools

import jax
import jax.numpy as jnp
from jax import lax
from jax.experimental import pallas as pl
from jax.experimental.pallas import tpu as pltpu
from jax.sharding import PartitionSpec as P

STATIONS = 64
SOURCE_COUNT = 40
ITERS = 2
ROWS = 16

ridge = 1.0
F32 = jnp.float32
BF16 = jnp.bfloat16
VMEM_LIMIT = 24 * 1024 * 1024


def swap(x):
    return pltpu.roll(x, x.shape[-1] // 2, axis=x.ndim - 1)


def lower(shape):
    return lax.broadcasted_iota(jnp.int32, shape, len(shape) - 1) < shape[-1] // 2


def cross(a, b):
    lo = lower(a.shape)
    return jnp.where(lo, a, swap(b)), jnp.where(lo, swap(a), b)


def three(x):
    hi = x.astype(BF16)
    rest = x - hi.astype(F32)
    mid = rest.astype(BF16)
    return hi, mid, (rest - mid.astype(F32)).astype(BF16)


def pick(onehot, x, dims):
    return sum(
        lax.dot_general(onehot, part, (dims, ((), ())), preferred_element_type=F32)
        for part in three(x)
    )


TILE = 8


def pack_kernel(n, dpc, first_ref, second_ref, re_ref, im_ref, out_ref, sems):
    rows = re_ref.shape[0]
    copies = [
        pltpu.make_async_copy(re_ref, out_ref.at[pl.ds(0, rows)], sems.at[0]),
        pltpu.make_async_copy(im_ref, out_ref.at[pl.ds(rows, rows)], sems.at[1]),
    ]
    for copy in copies:
        copy.start()
    lane = lax.broadcasted_iota(jnp.int32, (TILE, 128), 1)
    marks = jnp.zeros((TILE, 128), F32)
    for r in range(first_ref.shape[0]):
        marks = jnp.where(lane == r, (first_ref[r] + 1).astype(F32), marks)
        marks = jnp.where(lane == ROWS + r, (second_ref[r] + 1).astype(F32), marks)
    out_ref[2 * rows :] = marks
    for copy in copies:
        copy.wait()


class Fetch:
    def __init__(self, model, held, sems):
        pairs = held.shape[2]
        parts = 3 if pairs % 3 == 0 else 1
        self.size = pairs // parts
        self.copies = []
        for i in range(parts):
            part = pl.ds(i * self.size, self.size)
            self.copies.append(
                pltpu.make_async_copy(model.at[:, :, part], held.at[:, :, part], sems.at[i])
            )
        for copy in self.copies:
            copy.start()

    def each(self, body):
        for i, copy in enumerate(self.copies):
            copy.wait()
            lax.fori_loop(i * self.size, (i + 1) * self.size, body, 0)


def power_kernel(n, dpc, model_hbm, mask_ref, unused_in, out_ref, unused_out, model_ref, sems):
    fetch = Fetch(model_hbm, model_ref, sems)
    out_ref[...] = jnp.zeros_like(out_ref)

    def pair(b, carry):
        weight = mask_ref[b].astype(F32)
        for d in range(SOURCE_COUNT):
            mr = model_ref[d, 0, b].astype(F32)
            mi = model_ref[d, 1, b].astype(F32)
            row = d // dpc * TILE + d % dpc
            out_ref[b, row : row + 1, :] = jnp.sum(weight * (mr * mr + mi * mi), axis=0, keepdims=True)
        return carry

    fetch.each(pair)


def wide(ref, dpc):
    return jnp.concatenate([ref[pl.ds(dd, STATIONS, stride=dpc), :] for dd in range(dpc)], axis=1)


def put(ref, value, dpc):
    for dd in range(dpc):
        ref[pl.ds(dd, STATIONS, stride=dpc), :] = value[:, dd * 128 : (dd + 1) * 128]
    ref[STATIONS * dpc :, :] = jnp.zeros((TILE, 128), F32)


def first_own_kernel(n, dpc, me_ref, *rest):
    ins, (g_ref, onehot_ref, sel_ref, split, lines) = rest[:n], rest[n:]
    me = me_ref[0]
    k, c = lax.div(me, 2), lax.rem(me, 2)
    per = STATIONS // n
    rows = per * SOURCE_COUNT
    for o in range(n):
        peer = jnp.bitwise_xor(me, o)
        lines[pl.ds(peer, 1), :] = ins[o][2 * rows : 2 * rows + 1, :]
        for s in range(per):
            at = s * SOURCE_COUNT + k * dpc
            x0, x1 = cross(ins[o][pl.ds(at, TILE), :], ins[o][pl.ds(rows + at, TILE), :])
            to = pl.multiple_of((peer * per + s) * TILE, TILE)
            split[pl.ds(to, TILE), :] = jnp.where(c == 0, x0, x1)
    g = jnp.concatenate([split[pl.ds(dd, STATIONS, stride=TILE), :] for dd in range(dpc)], axis=1)
    put(g_ref, g, dpc)
    across = 128 // (2 * ROWS)
    station = lax.broadcasted_iota(jnp.int32, (STATIONS, 128), 0)
    for group in range(n // across):
        marks = jnp.zeros((1, 128), F32)
        for i in range(across):
            row = lines[group * across + i : group * across + i + 1, :]
            marks = marks + (pltpu.roll(row, i * 2 * ROWS, axis=1) if i else row)
        hit = station + 1 == marks.astype(jnp.int32)
        onehot_ref[:, group * 128 : (group + 1) * 128] = jnp.where(hit, 1.0, 0.0).astype(BF16)
    sel_ref[...] = pick(onehot_ref[...], g, ((0,), (0,)))


def fill_powers(n, dpc, sums, sel_ref, terms, base):
    lo = lower((TILE, 128))
    for o in range(n):
        r = o * 2 * ROWS
        for dd in range(dpc):
            cols = slice(dd * 128, (dd + 1) * 128)
            dcols = slice(base + dd * 128, base + (dd + 1) * 128)
            W = sums[o, pl.ds(ROWS * dpc + dd, TILE, stride=dpc), :]
            Wx = swap(W)
            W = jnp.concatenate([jnp.where(lo, W, Wx), jnp.where(lo, Wx, W)], 0)
            p = sel_ref[r : r + ROWS, cols]
            q = sel_ref[r + ROWS : r + 2 * ROWS, cols]
            p2, q2 = p * p, q * q
            terms[r : r + ROWS, dcols] = W * (q2 + swap(q2))
            terms[r + ROWS : r + 2 * ROWS, dcols] = W * (p2 + swap(p2))


def fill_sums(n, dpc, sums, sel_ref, terms):
    lo = lower((ROWS, 128))
    sign = jnp.where(lo, -1.0, 1.0)
    for o in range(n):
        r = o * 2 * ROWS
        for dd in range(dpc):
            cols = slice(dd * 128, (dd + 1) * 128)
            B = sums[o, pl.ds(dd, ROWS, stride=dpc), :]
            p = sel_ref[r : r + ROWS, cols]
            q = sel_ref[r + ROWS : r + 2 * ROWS, cols]
            Bx = swap(B)
            Brr, Bii = jnp.where(lo, B, Bx), sign * jnp.where(lo, Bx, B)
            terms[r : r + ROWS, cols] = Brr * q + Bii * swap(q)
            terms[r + ROWS : r + 2 * ROWS, cols] = Brr * p - Bii * swap(p)


def own_kernel(n, dpc, g_in, onehot_ref, sel_ref, sums, g_out, terms):
    width = dpc * 128
    fill_sums(n, dpc, sums, sel_ref, terms)
    fill_powers(n, dpc, sums, sel_ref, terms, width)
    total = pick(onehot_ref[...], terms[...], ((1,), (0,)))
    put(g_out, 0.5 * (wide(g_in, dpc) + total[:, :width] / (total[:, width:] + ridge)), dpc)


def prepare_kernel(n, dpc, g_ref, onehot_ref, sums, sel_ref, den_ref, terms):
    sel_ref[...] = pick(onehot_ref[...], wide(g_ref, dpc), ((0,), (0,)))
    fill_powers(n, dpc, sums, sel_ref, terms, 0)
    den_ref[...] = pick(onehot_ref[...], terms[...], ((1,), (0,))) + ridge


def later_own_kernel(n, dpc, g_in, onehot_ref, sel_ref, den_ref, sums, g_out, terms):
    fill_sums(n, dpc, sums, sel_ref, terms)
    total = pick(onehot_ref[...], terms[...], ((1,), (0,)))
    put(g_out, 0.5 * (wide(g_in, dpc) + total / den_ref[...]), dpc)


def products_first(n, dpc, me, first_ref, second_ref, ins, hre, him, stack):
    per = STATIONS // n
    rows = per * SOURCE_COUNT
    for o in range(n):
        stack[jnp.bitwise_xor(me, o)] = ins[o][...]

    def pair(b, carry):
        p, q = first_ref[b], second_ref[b]

        def block(station, k, part):
            at = lax.rem(station, per) * SOURCE_COUNT + k * dpc + part * rows
            return stack[lax.div(station, per), pl.ds(at, TILE), :]

        for k in range(n // 2):
            pr, pi, qr, qi = block(p, k, 0), block(p, k, 1), block(q, k, 0), block(q, k, 1)
            hre[b, k * TILE : (k + 1) * TILE, :] = pr * qr + pi * qi
            him[b, k * TILE : (k + 1) * TILE, :] = pi * qr - pr * qi
        return carry

    lax.fori_loop(0, first_ref.shape[0], pair, 0)


def piece_pair(dpc, even, ins, m, station):
    a = ins[2 * m][pl.ds(station * dpc, TILE), :]
    b = ins[2 * m + 1][pl.ds(station * dpc, TILE), :]
    return cross(jnp.where(even, a, b), jnp.where(even, b, a))


def products(n, dpc, me, first_ref, second_ref, ins, hre, him):
    even = lax.rem(me, 2) == 0

    def pair(b, carry):
        p, q = first_ref[b], second_ref[b]
        for m in range(n // 2):
            k = lax.div(jnp.bitwise_xor(me, 2 * m), 2)
            pr, pi = piece_pair(dpc, even, ins, m, p)
            qr, qi = piece_pair(dpc, even, ins, m, q)
            rows = pl.ds(pl.multiple_of(k * TILE, TILE), TILE)
            hre[b, rows, :] = pr * qr + pi * qi
            him[b, rows, :] = pi * qr - pr * qi
        return carry

    lax.fori_loop(0, first_ref.shape[0], pair, 0)


def predict(n, dpc, b, model_ref, vis_ref, mask_ref, hre, him):
    def step(k, acc):
        acc_re, acc_im = acc
        for dd in range(dpc):
            mr = model_ref[k * dpc + dd, 0, b].astype(F32)
            mi = model_ref[k * dpc + dd, 1, b].astype(F32)
            hr = hre[b, pl.ds(k * TILE + dd, 1), :]
            hi = him[b, pl.ds(k * TILE + dd, 1), :]
            acc_re = acc_re - (hr * mr - hi * mi)
            acc_im = acc_im - (hr * mi + hi * mr)
        return acc_re, acc_im

    acc = lax.fori_loop(0, n // 2, step, (vis_ref[0, b], vis_ref[1, b]))
    weight = mask_ref[b].astype(F32)
    return weight * acc[0], weight * acc[1]


def pass_kernel(
    n, dpc, start, me_ref, first_ref, second_ref, model_hbm, vis_ref, mask_ref, power_ref, *rest
):
    ins, (out_ref, model_ref, sems, hre, him, cre, cim), work = rest[:n], rest[n : n + 7], rest[n + 7 :]
    fetch = Fetch(model_hbm, model_ref, sems)
    build = products_first if start else products
    build(n, dpc, me_ref[0], first_ref, second_ref, ins, hre, him, *work)

    def pair(b, carry):
        res_re, res_im = predict(n, dpc, b, model_ref, vis_ref, mask_ref, hre, him)

        def step(k, carry):
            for dd in range(dpc):
                mr = model_ref[k * dpc + dd, 0, b].astype(F32)
                mi = model_ref[k * dpc + dd, 1, b].astype(F32)
                row = pl.ds(k * TILE + dd, 1)
                cre[b, row, :] = jnp.sum(mr * res_re + mi * res_im, axis=0, keepdims=True)
                cim[b, row, :] = jnp.sum(mr * res_im - mi * res_re, axis=0, keepdims=True)
            return carry

        return lax.fori_loop(0, n // 2, step, carry)

    fetch.each(pair)
    pairs = mask_ref.shape[0]
    for k in range(n // 2):
        tile = slice(k * TILE, (k + 1) * TILE)
        for b in range(pairs):
            w = power_ref[b, tile, :]
            x0, x1 = cross(cre[b, tile, :] + hre[b, tile, :] * w, cim[b, tile, :] + him[b, tile, :] * w)
            out_ref[2 * k, b * dpc : (b + 1) * dpc, :] = x0[:dpc]
            out_ref[2 * k + 1, b * dpc : (b + 1) * dpc, :] = x1[:dpc]
        if pairs < ROWS:
            empty = jnp.zeros(((ROWS - pairs) * dpc, 128), F32)
            out_ref[2 * k, pairs * dpc : ROWS * dpc, :] = empty
            out_ref[2 * k + 1, pairs * dpc : ROWS * dpc, :] = empty
        if start:
            for r in range(TILE):
                x0, x1 = cross(power_ref[r, tile, :], power_ref[r + TILE, tile, :])
                to = (ROWS + r) * dpc
                out_ref[2 * k, to : to + dpc, :] = x0[:dpc]
                out_ref[2 * k + 1, to : to + dpc, :] = x1[:dpc]


def last_kernel(n, dpc, me_ref, first_ref, second_ref, model_hbm, vis_ref, mask_ref, *rest):
    ins, (res_ref, gains_ref, model_ref, sems, hre, him) = rest[:n], rest[n:]
    fetch = Fetch(model_hbm, model_ref, sems)
    me = me_ref[0]
    per = STATIONS // n
    even = lax.rem(me, 2) == 0
    for m in range(n // 2):
        k = lax.div(jnp.bitwise_xor(me, 2 * m), 2)
        for s in range(per):
            re, im = piece_pair(dpc, even, ins, m, me * per + s)
            for dd in range(dpc):
                at = s * SOURCE_COUNT + k * dpc + dd
                gains_ref[0, pl.ds(at, 1), :] = re[dd : dd + 1]
                gains_ref[1, pl.ds(at, 1), :] = im[dd : dd + 1]
    products(n, dpc, me, first_ref, second_ref, ins, hre, him)

    def pair(b, carry):
        res_re, res_im = predict(n, dpc, b, model_ref, vis_ref, mask_ref, hre, him)
        res_ref[0, b] = res_re
        res_ref[1, b] = res_im
        return carry

    fetch.each(pair)


SMEM = pl.BlockSpec(memory_space=pltpu.SMEM)
VMEM = pl.BlockSpec(memory_space=pltpu.VMEM)
HBM = pl.BlockSpec(memory_space=pltpu.HBM)


def shape(*dims, dtype=F32):
    return jax.ShapeDtypeStruct(dims, dtype)


def exchange(x):
    return lax.all_to_all(x, "bl", split_axis=0, concat_axis=0, tiled=True)


def gather(n, piece, beside=lambda x: x):
    def send(x, o):
        return lax.ppermute(x, "bl", [(i, i ^ o) for i in range(n)])

    got = {0: piece}
    got[4], got[12] = send(piece, 4), send(piece, 12)
    got[2] = send(piece, 2)
    got[4] = beside(got[4])
    got[8] = send(got[12], 4)
    for o in (4, 12, 8):
        got[o + 2] = send(got[o], 2)
    for o in (0, 2, 4, 12, 6, 14, 8, 10):
        got[o + 1] = send(got[o], 1)
    return [got[o] for o in range(n)]


def fast_body(n, vis, model, mask, first, second, gre, gim):
    model, gre, gim = (pltpu.with_memory_space_constraint(x, pltpu.HBM) for x in (model, gre, gim))
    dpc = SOURCE_COUNT // (n // 2)
    width = dpc * 128
    pairs, times, channels = mask.shape
    me = lax.axis_index("bl").astype(jnp.int32).reshape(1)
    params = pltpu.CompilerParams(vmem_limit_bytes=VMEM_LIMIT)
    plane = (ROWS, n // 2 * TILE, channels)
    lots = n * 2 * ROWS
    mine = (STATIONS * dpc + TILE, channels)
    held = [pltpu.VMEM(model.shape, BF16), pltpu.SemaphoreType.DMA((3,))]

    def call(kernel, args, outs, scratch=(), micros=1, aliases={}):
        def place(x):
            if x is model or x is gre or x is gim:
                return HBM
            return SMEM if x.ndim == 1 else VMEM

        return pl.pallas_call(
            functools.partial(kernel, n, dpc),
            in_specs=[place(x) for x in args],
            out_specs=[VMEM for o in outs],
            out_shape=outs,
            scratch_shapes=[pltpu.VMEM(x, F32) if isinstance(x, tuple) else x for x in scratch],
            compiler_params=params,
            input_output_aliases=aliases,
            cost_estimate=pl.CostEstimate(
                flops=0, bytes_accessed=int(micros * 3.69e6), transcendentals=0
            ),
        )(*args)

    (piece,) = call(
        pack_kernel,
        (first, second, gre, gim),
        [shape(2 * gre.shape[0] + TILE, channels)],
        [pltpu.SemaphoreType.DMA((2,))],
    )
    power = None

    def powers_beside(x):
        nonlocal power
        power, x = call(
            power_kernel, (model, mask, x), [shape(*plane), shape(*x.shape)], held, micros=6, aliases={2: 1}
        )
        return x

    got = gather(n, piece, powers_beside)
    g, onehot, sel = call(
        first_own_kernel,
        (me, *got),
        [shape(*mine), shape(STATIONS, lots, dtype=BF16), shape(lots, width)],
        [(STATIONS * TILE, channels), (n, channels)],
        micros=2,
    )
    for step in range(ITERS):
        start = step == 0
        work = [(n,) + piece.shape] if start else []
        (sums,) = call(
            lambda n, dpc, *refs: pass_kernel(n, dpc, start, *refs),
            (me, first, second, model, vis, mask, power, *got),
            [shape(n, (ROWS + (TILE if start else 0)) * dpc, channels)],
            held + [plane] * 4 + work,
            micros=9,
        )
        sums = exchange(sums)
        if start:
            powers = sums
            (g,) = call(own_kernel, (g, onehot, sel, sums), [shape(*mine)], [(lots, 2 * width)])
        else:
            (g,) = call(later_own_kernel, (g, onehot, sel, den, sums), [shape(*mine)], [(lots, width)])
        got = gather(n, g)
        if step < ITERS - 1:
            sel, den = call(
                prepare_kernel,
                (g, onehot, powers),
                [shape(lots, width), shape(STATIONS, width)],
                [(lots, width)],
                micros=2,
            )
    residual, gains = call(
        last_kernel,
        (me, first, second, model, vis, mask, *got),
        [shape(*vis.shape), shape(2, *gre.shape)],
        held + [plane] * 2,
        micros=6,
    )
    return gains, residual


def block_pass(full_re, full_im, vis_blk, coh_blk, weight, first, second, want_sums):
    ar = jnp.transpose(full_re[first], (1, 0, 2))
    ai = jnp.transpose(full_im[first], (1, 0, 2))
    br = jnp.transpose(full_re[second], (1, 0, 2))
    bi = jnp.transpose(full_im[second], (1, 0, 2))
    mr = coh_blk[:, 0].astype(F32)
    mi = coh_blk[:, 1].astype(F32)
    hr = ar * br + ai * bi
    hi = ai * br - ar * bi
    hr_t, hi_t = hr[:, :, None], hi[:, :, None]
    res_re = weight * (vis_blk[0] - jnp.sum(hr_t * mr - hi_t * mi, 0))
    res_im = weight * (vis_blk[1] - jnp.sum(hr_t * mi + hi_t * mr, 0))
    residual = jnp.stack([res_re, res_im])
    if not want_sums:
        return (residual, None)
    power = jnp.sum(weight[None] * (mr * mr + mi * mi), 2)
    sum_re = jnp.sum(mr * res_re + mi * res_im, 2) + hr * power
    sum_im = jnp.sum(mr * res_im - mi * res_re, 2) + hi * power
    terms_first = jnp.stack([br * sum_re - bi * sum_im, br * sum_im + bi * sum_re, power * (br * br + bi * bi)])
    terms_second = jnp.stack([ar * sum_re + ai * sum_im, ai * sum_re - ar * sum_im, power * (ar * ar + ai * ai)])
    stations = jnp.arange(STATIONS, dtype=jnp.int32)
    onehot_first = (first[:, None] == stations[None, :]).astype(F32)
    onehot_second = (second[:, None] == stations[None, :]).astype(F32)
    exact = lax.Precision.HIGHEST
    sums = jnp.einsum("bs,cdbf->csdf", onehot_first, terms_first, precision=exact)
    sums = sums + jnp.einsum("bs,cdbf->csdf", onehot_second, terms_second, precision=exact)
    return (residual, sums)


def plain_body(vis, model, mask, first, second, gre, gim):
    weight = mask.astype(F32)
    rows, channels = gre.shape
    shaped = (STATIONS, SOURCE_COUNT, channels)
    full_re = lax.all_gather(gre, "bl", axis=0, tiled=True).reshape(shaped)
    full_im = lax.all_gather(gim, "bl", axis=0, tiled=True).reshape(shaped)
    for step in range(ITERS):
        unused, sums = block_pass(full_re, full_im, vis, model, weight, first, second, True)
        totals = lax.psum(sums, "bl")
        denom = totals[2] + ridge
        full_re = 0.5 * (full_re + totals[0] / denom)
        full_im = 0.5 * (full_im + totals[1] / denom)
    residual, unused = block_pass(full_re, full_im, vis, model, weight, first, second, False)
    both = jnp.stack([full_re, full_im]).reshape(2, STATIONS * SOURCE_COUNT, channels)
    return lax.dynamic_slice_in_dim(both, lax.axis_index("bl") * rows, rows, 1), residual


def solution(mesh):
    n = mesh.shape["bl"]
    split = n == 16

    def body(vis, model, mask, first, second, gre, gim):
        if split and mask.shape[0] <= ROWS:
            return fast_body(n, vis, model, mask, first, second, gre, gim)
        return plain_body(vis, model, mask, first, second, gre, gim)

    in_specs = (
        P(None, ("grp", "bl"), None, None),
        P(None, None, ("grp", "bl"), None, None),
        P(("grp", "bl"), None, None),
        P(("grp", "bl")),
        P(("grp", "bl")),
        P(("grp", "bl"), None),
        P(("grp", "bl"), None),
    )
    out_specs = (P(None, ("grp", "bl"), None), P(None, ("grp", "bl"), None, None))
    return jax.shard_map(body, mesh=mesh, in_specs=in_specs, out_specs=out_specs, check_vma=False)
```

time: 188 us -> 183 us (0.973)
  local copies, waits for them, and re-layouts: 33.9 us -> 13.2 us
  waiting for transfers between devices: 56.5 us -> 66.8 us
  Pallas kernels: 40.4 us -> 46.8 us
    unnamed x92 -> x46, local copies, waits for them, and re-layouts: 33.9 us -> 13.2 us
    all_to_all x2, waiting for transfers between devices: 22.2 us -> 29.5 us  [exchange(): return lax.all_to_all(x, 'bl', split_axis=0, concat_axis=0, tiled=True)]
    pallas_call x9, Pallas kernels: 40.4 us -> 46.8 us  [call(): pl.pallas_call(functools.partial(kernel, n, dpc), in_specs=[place(x) for...]
    ppermute x45, waiting for transfers between devices: 34.3 us -> 37.4 us  [send(): return lax.ppermute(x, 'bl', [(i, i ^ o) for i in range(n)])]
  transfers between devices with their start and end apart: 47 -> 47, of which waited for: 18 -> 19; matrix products, arithmetic and copies ran while one was open for 0% -> 0% of each run, Pallas kernels for 4% -> 5%
where the time goes in v4:
time: 183 us; the launch traced here: 179 us
  waiting for transfers between devices  66.8 us (37%)
  starting transfers between devices  51.8 us (28%)
  Pallas kernels  46.8 us (26%)
  local copies, waits for them, and re-layouts  13.2 us (7%)
    pallas_call x9, Pallas kernels, call(): pl.pallas_call(functools.partial(kernel, n, dpc), in_specs=[place(x) for...  46.8 us
    ppermute x45, starting transfers between devices, send(): return lax.ppermute(x, 'bl', [(i, i ^ o) for i in range(n)])  41.8 us
    ppermute x45, waiting for transfers between devices, send(): return lax.ppermute(x, 'bl', [(i, i ^ o) for i in range(n)])  37.4 us
    all_to_all x2, waiting for transfers between devices, exchange(): return lax.all_to_all(x, 'bl', split_axis=0, concat_axis=0, tiled=True)  29.5 us
    unnamed x46, local copies, waits for them, and re-layouts  13.2 us
    all_to_all x2, starting transfers between devices, exchange(): return lax.all_to_all(x, 'bl', split_axis=0, concat_axis=0, tiled=True)  9.98 us
  transfers between devices with their start and end apart: 47, of which 19 were waited for; matrix products, arithmetic and copies ran while one was open for 0% of the time, Pallas kernels for 5%

profile of v4, /device:TPU:9, one launch (start us, length us, event | category | flops | bytes accessed | tf_op | source)
XLA Modules:
  0.0 179.5 jit_solution(2411206293548804573)
XLA Ops:
  1.9 1.5 shard_map.86.rest_0_.refs_7_
  3.5 1.4 collective-permute-start.7
  4.8 1.2 collective-permute-start.1
  6.0 2.2 %collective-permute-start.3 = (f32[328,128]{1,0:T(8,128)S(1)}, f32[328,128]{1,0:T(8,128)S(1)}, u32[]{:S(2)}, u32[]{:S(2)}) collective-permute-start(f32[328,128]{1,0:T(8,128)S(1)} %shard_map.86.rest_0_.refs_7_), channel_id=1, source_target_pairs={{0,4},{1,5},{2,6},{3,7},{4,0},{5,1},{6,2},{7,3},{8,12},{9,13},{10,... | collective-permute-start | bytes 503816 | tf_op jit(solution)/shard_map/ppermute | solution.py:341
  8.2 1.5 collective-permute-start
  9.7 2.7 %collective-permute-done.7.rest_12_.refs_19_ = f32[328,128]{1,0:T(8,128)S(1)} collective-permute-done((f32[328,128]{1,0:T(8,128)S(1)}, f32[328,128]{1,0:T(8,128)S(1)}, u32[]{:S(2)}, u32[]{:S(2)}) %collective-permute-start.7) | collective-permute-done | bytes 167968 | tf_op jit(solution)/shard_map/ppermute | solution.py:341
  12.5 1.4 collective-permute-start.2
  15.3 4.8 %shard_map.87 = (f32[16,64,128]{2,1,0:T(8,128)S(1)}, f32[328,128]{1,0:T(8,128)S(1)}) custom-call(bf16[40,2,15,32,128]{4,3,2,1,0:T(8,128)(2,1)} %model_hbm.3, s32[15,32,128]{2,1,0:T(8,128)S(1)} %copy-done.1, f32[328,128]{1,0:T(8,128)S(1)} %collective-permute-done.3.unused_in), custom_call_target="tpu_custom_call", output_to_operand_aliasing={{1}: (2, {})} | custom-call | bytes 22140000 | tf_op jit(solution)/shard_map/pallas_call | solution.py:373
  20.2 1.8 %collective-permute-start.4 = (f32[328,128]{1,0:T(8,128)S(1)}, f32[328,128]{1,0:T(8,128)S(1)}, u32[]{:S(2)}, u32[]{:S(2)}) collective-permute-start(f32[328,128]{1,0:T(8,128)S(1)} %get-tuple-element.11.rest_4_.refs_11_), channel_id=1, source_target_pairs={{0,1},{1,0},{2,3},{3,2},{4,5},{5,4},{6,7},{7,6},{8,9},{9,8},{10,11... | collective-permute-start | bytes 503816 | tf_op jit(solution)/shard_map/ppermute | solution.py:341
  22.0 1.2 collective-permute-start.5
  23.5 1.2 collective-permute-start.10
  25.7 2.2 %collective-permute-done.5.rest_6_.refs_13_ = f32[328,128]{1,0:T(8,128)S(1)} collective-permute-done((f32[328,128]{1,0:T(8,128)S(1)}, f32[328,128]{1,0:T(8,128)S(1)}, u32[]{:S(2)}, u32[]{:S(2)}) %collective-permute-start.5) | collective-permute-done | bytes 167968 | tf_op jit(solution)/shard_map/ppermute | solution.py:341
  27.9 1.3 collective-permute-start.6
  29.2 2.3 %collective-permute-done.13.rest_14_.refs_21_ = f32[328,128]{1,0:T(8,128)S(1)} collective-permute-done((f32[328,128]{1,0:T(8,128)S(1)}, f32[328,128]{1,0:T(8,128)S(1)}, u32[]{:S(2)}, u32[]{:S(2)}) %collective-permute-start.13) | collective-permute-done | bytes 167968 | tf_op jit(solution)/shard_map/ppermute | solution.py:341
  31.5 1.3 collective-permute-start.14
  32.8 2.3 %collective-permute-done.10.rest_10_.refs_17_ = f32[328,128]{1,0:T(8,128)S(1)} collective-permute-done((f32[328,128]{1,0:T(8,128)S(1)}, f32[328,128]{1,0:T(8,128)S(1)}, u32[]{:S(2)}, u32[]{:S(2)}) %collective-permute-start.10) | collective-permute-done | bytes 167968 | tf_op jit(solution)/shard_map/ppermute | solution.py:341
  36.0 1.1 collective-permute-done.11.rest_11_.refs_18_
  37.1 14.0 %shard_map.89 = f32[16,120,128]{2,1,0:T(8,128)} custom-call(s32[1]{0:T(128)} %bitcast.me_ref.refs_0_, s32[15]{0:T(128)S(1)} %copy-done.20, s32[15]{0:T(128)S(1)} %copy-done.22, bf16[40,2,15,32,128]{4,3,2,1,0:T(8,128)(2,1)} %model_hbm.3, f32[2,15,32,128]{3,2,1,0:T(8,128)S(1)} %copy-done, s32[15,32,128]{2,1,0:T(8,128)S(1)} %copy-done.2, ...), custom_call_target="tpu_custom_call" | custom-call | bytes 33210000 | tf_op jit(solution)/shard_map/pallas_call | solution.py:373
  51.2 5.1 %all-to-all-start = ((f32[16,120,128]{2,1,0:T(8,128)}), f32[16,120,128]{2,1,0:T(8,128)S(1)}, u32[]{:S(2)}, u32[]{:S(2)}) async-start(f32[16,120,128]{2,1,0:T(8,128)} %shard_map.89), calls=%async_computation | async-start | bytes 1966080 | tf_op jit(solution)/shard_map/all_to_all | solution.py:336
  60.8 2.1 %shard_map.88 = (f32[328,128]{1,0:T(8,128)S(1)}, bf16[64,512]{1,0:T(8,128)(2,1)S(1)}, f32[512,640]{1,0:T(8,128)S(1)}) custom-call(s32[1]{0:T(128)} %bitcast.me_ref.refs_0_, f32[328,128]{1,0:T(8,128)S(1)} %shard_map.86.rest_0_.refs_7_, f32[328,128]{1,0:T(8,128)S(1)} %collective-permute-done.rest_1_.refs_8_, ...), custom_call_target="tpu_custom_call" | custom-call | bytes 7380000 | tf_op jit(solution)/shard_map/pallas_call | solution.py:373
  62.9 1.1 copy-done.3
  64.6 15.1 %all-to-all-done.sums = f32[16,120,128]{2,1,0:T(8,128)S(1)} async-done(((f32[16,120,128]{2,1,0:T(8,128)}), f32[16,120,128]{2,1,0:T(8,128)S(1)}, u32[]{:S(2)}, u32[]{:S(2)}) %all-to-all-start) | async-done | bytes 983072 | tf_op jit(solution)/shard_map/all_to_all | solution.py:336
  79.7 1.3 copy-done.4
  82.0 1.6 shard_map.90.g_ref.refs_7_.g_in
  84.8 2.3 %collective-permute-start.18 = (f32[328,128]{1,0:T(8,128)S(1)}, f32[328,128]{1,0:T(8,128)S(1)}, u32[]{:S(2)}, u32[]{:S(2)}) collective-permute-start(f32[328,128]{1,0:T(8,128)S(1)} %shard_map.90.g_ref.refs_7_.g_in), channel_id=1, source_target_pairs={{0,4},{1,5},{2,6},{3,7},{4,0},{5,1},{6,2},{7,3},{8,12},{9,13},{10,... | collective-permute-start | bytes 503816 | tf_op jit(solution)/shard_map/ppermute | solution.py:341
  88.1 4.5 %collective-permute-done.22.refs_19_ = f32[328,128]{1,0:T(8,128)S(1)} collective-permute-done((f32[328,128]{1,0:T(8,128)S(1)}, f32[328,128]{1,0:T(8,128)S(1)}, u32[]{:S(2)}, u32[]{:S(2)}) %collective-permute-start.22) | collective-permute-done | bytes 167968 | tf_op jit(solution)/shard_map/ppermute | solution.py:341
  94.0 2.0 %collective-permute-start.20 = (f32[328,128]{1,0:T(8,128)S(1)}, f32[328,128]{1,0:T(8,128)S(1)}, u32[]{:S(2)}, u32[]{:S(2)}) collective-permute-start(f32[328,128]{1,0:T(8,128)S(1)} %collective-permute-done.18.refs_11_), channel_id=1, source_target_pairs={{0,2},{1,3},{2,0},{3,1},{4,6},{5,7},{6,4},{7,5},{8,10},{9,11},{10,... | collective-permute-start | bytes 503816 | tf_op jit(solution)/shard_map/ppermute | solution.py:341
  96.0 2.0 %collective-permute-done.23.refs_15_ = f32[328,128]{1,0:T(8,128)S(1)} collective-permute-done((f32[328,128]{1,0:T(8,128)S(1)}, f32[328,128]{1,0:T(8,128)S(1)}, u32[]{:S(2)}, u32[]{:S(2)}) %collective-permute-start.23) | collective-permute-done | bytes 167968 | tf_op jit(solution)/shard_map/ppermute | solution.py:341
  98.0 1.6 collective-permute-start.25
  99.7 1.6 collective-permute-start.27
  101.8 2.4 %collective-permute-done.28.refs_21_ = f32[328,128]{1,0:T(8,128)S(1)} collective-permute-done((f32[328,128]{1,0:T(8,128)S(1)}, f32[328,128]{1,0:T(8,128)S(1)}, u32[]{:S(2)}, u32[]{:S(2)}) %collective-permute-start.28) | collective-permute-done | bytes 167968 | tf_op jit(solution)/shard_map/ppermute | solution.py:341
  105.0 2.8 %collective-permute-done.25.refs_17_ = f32[328,128]{1,0:T(8,128)S(1)} collective-permute-done((f32[328,128]{1,0:T(8,128)S(1)}, f32[328,128]{1,0:T(8,128)S(1)}, u32[]{:S(2)}, u32[]{:S(2)}) %collective-permute-start.25) | collective-permute-done | bytes 167968 | tf_op jit(solution)/shard_map/ppermute | solution.py:341
  109.4 13.1 %shard_map.92 = f32[16,80,128]{2,1,0:T(8,128)} custom-call(s32[1]{0:T(128)} %bitcast.me_ref.refs_0_, s32[15]{0:T(128)S(1)} %copy-done.20, s32[15]{0:T(128)S(1)} %copy-done.22, bf16[40,2,15,32,128]{4,3,2,1,0:T(8,128)(2,1)} %model_hbm.3, f32[2,15,32,128]{3,2,1,0:T(8,128)S(1)} %copy-done, s32[15,32,128]{2,1,0:T(8,128)S(1)} %copy-done.2, ...), custom_call_target="tpu_custom_call" | custom-call | bytes 33210000 | tf_op jit(solution)/shard_map/pallas_call | solution.py:373
  122.5 4.9 %all-to-all-start.1 = ((f32[16,80,128]{2,1,0:T(8,128)}), f32[16,80,128]{2,1,0:T(8,128)S(1)}, u32[]{:S(2)}, u32[]{:S(2)}) async-start(f32[16,80,128]{2,1,0:T(8,128)} %shard_map.92), calls=%async_computation.1 | async-start | bytes 1310720 | tf_op jit(solution)/shard_map/all_to_all | solution.py:336
  127.4 1.4 shard_map.91
  128.9 1.1 copy-done.5
  130.0 14.4 %all-to-all-done.1.sums = f32[16,80,128]{2,1,0:T(8,128)S(1)} async-done(((f32[16,80,128]{2,1,0:T(8,128)}), f32[16,80,128]{2,1,0:T(8,128)S(1)}, u32[]{:S(2)}, u32[]{:S(2)}) %all-to-all-start.1) | async-done | bytes 655392 | tf_op jit(solution)/shard_map/all_to_all | solution.py:336
  144.3 1.3 copy-done.6
  147.5 2.3 %collective-permute-start.33 = (f32[328,128]{1,0:T(8,128)S(1)}, f32[328,128]{1,0:T(8,128)S(1)}, u32[]{:S(2)}, u32[]{:S(2)}) collective-permute-start(f32[328,128]{1,0:T(8,128)S(1)} %shard_map.93.rest_0_), channel_id=1, source_target_pairs={{0,4},{1,5},{2,6},{3,7},{4,0},{5,1},{6,2},{7,3},{8,12},{9,13},{10,... | collective-permute-start | bytes 503816 | tf_op jit(solution)/shard_map/ppermute | solution.py:341
  150.8 5.6 %collective-permute-done.37.rest_12_ = f32[328,128]{1,0:T(8,128)S(1)} collective-permute-done((f32[328,128]{1,0:T(8,128)S(1)}, f32[328,128]{1,0:T(8,128)S(1)}, u32[]{:S(2)}, u32[]{:S(2)}) %collective-permute-start.37) | collective-permute-done | bytes 167968 | tf_op jit(solution)/shard_map/ppermute | solution.py:341
  157.1 1.6 collective-permute-start.35
  158.7 3.0 %collective-permute-done.38.rest_8_ = f32[328,128]{1,0:T(8,128)S(1)} collective-permute-done((f32[328,128]{1,0:T(8,128)S(1)}, f32[328,128]{1,0:T(8,128)S(1)}, u32[]{:S(2)}, u32[]{:S(2)}) %collective-permute-start.38) | collective-permute-done | bytes 167968 | tf_op jit(solution)/shard_map/ppermute | solution.py:341
  161.7 2.0 %collective-permute-start.42 = (f32[328,128]{1,0:T(8,128)S(1)}, f32[328,128]{1,0:T(8,128)S(1)}, u32[]{:S(2)}, u32[]{:S(2)}) collective-permute-start(f32[328,128]{1,0:T(8,128)S(1)} %collective-permute-done.37.rest_12_), channel_id=1, source_target_pairs={{0,1},{1,0},{2,3},{3,2},{4,5},{5,4},{6,7},{7,6},{8,9},{9,8},{10,11... | collective-permute-start | bytes 503816 | tf_op jit(solution)/shard_map/ppermute | solution.py:341
  164.6 1.7 collective-permute-done.43.rest_14_
  166.3 1.9 %collective-permute-start.44 = (f32[328,128]{1,0:T(8,128)S(1)}, f32[328,128]{1,0:T(8,128)S(1)}, u32[]{:S(2)}, u32[]{:S(2)}) collective-permute-start(f32[328,128]{1,0:T(8,128)S(1)} %collective-permute-done.43.rest_14_), channel_id=1, source_target_pairs={{0,1},{1,0},{2,3},{3,2},{4,5},{5,4},{6,7},{7,6},{8,9},{9,8},{10,11... | collective-permute-start | bytes 503816 | tf_op jit(solution)/shard_map/ppermute | solution.py:341
  168.2 1.7 collective-permute-done.40.rest_10_
  169.9 1.2 collective-permute-start.41
  172.1 7.3 %shard_map.94 = (f32[2,15,32,128]{3,2,1,0:T(8,128)}, f32[2,160,128]{2,1,0:T(8,128)}) custom-call(s32[1]{0:T(128)} %bitcast.me_ref.refs_0_, s32[15]{0:T(128)S(1)} %copy-done.20, s32[15]{0:T(128)S(1)} %copy-done.22, bf16[40,2,15,32,128]{4,3,2,1,0:T(8,128)(2,1)} %model_hbm.3, f32[2,15,32,128]{3,2,1,0:T(8,128)S(1)} %copy-done, s32[15,32,128]{2,1,0:T(8,128)S(1)} %copy-done.2, ...), custom_call_target="tpu_custom_call" | custom-call | bytes 22140000 | tf_op jit(solution)/shard_map/pallas_call | solution.py:373
  (101 shorter events, 23.2 us)
Async XLA Ops:
  1.9 35.2 %copy-start.22 = (s32[15]{0:T(128)S(1)}, s32[15]{0:T(128)}, u32[]{:S(2)}) copy-start(s32[15]{0:T(128)} %second_ref.3) | copy-start | bytes 184
  3.5 9.0 %collective-permute-start.7 = (f32[328,128]{1,0:T(8,128)S(1)}, f32[328,128]{1,0:T(8,128)S(1)}, u32[]{:S(2)}, u32[]{:S(2)}) collective-permute-start(f32[328,128]{1,0:T(8,128)S(1)} %shard_map.86.rest_0_.refs_7_), channel_id=1, source_target_pairs={{0,12},{1,13},{2,14},{3,15},{4,8},{5,9},{6,10},{7,11},{8,4},{9,5},... | collective-permute-start | bytes 503816 | tf_op jit(solution)/shard_map/ppermute | solution.py:341
  4.8 7.7 %collective-permute-start.1 = (f32[328,128]{1,0:T(8,128)S(1)}, f32[328,128]{1,0:T(8,128)S(1)}, u32[]{:S(2)}, u32[]{:S(2)}) collective-permute-start(f32[328,128]{1,0:T(8,128)S(1)} %shard_map.86.rest_0_.refs_7_), channel_id=1, source_target_pairs={{0,2},{1,3},{2,0},{3,1},{4,6},{5,7},{6,4},{7,5},{8,10},{9,11},{10,... | collective-permute-start | bytes 503816 | tf_op jit(solution)/shard_map/ppermute | solution.py:341
  6.0 8.4 %collective-permute-start.3 = (f32[328,128]{1,0:T(8,128)S(1)}, f32[328,128]{1,0:T(8,128)S(1)}, u32[]{:S(2)}, u32[]{:S(2)}) collective-permute-start(f32[328,128]{1,0:T(8,128)S(1)} %shard_map.86.rest_0_.refs_7_), channel_id=1, source_target_pairs={{0,4},{1,5},{2,6},{3,7},{4,0},{5,1},{6,2},{7,3},{8,12},{9,13},{10,... | collective-permute-start | bytes 503816 | tf_op jit(solution)/shard_map/ppermute | solution.py:341
  8.2 15.0 %collective-permute-start = (f32[328,128]{1,0:T(8,128)S(1)}, f32[328,128]{1,0:T(8,128)S(1)}, u32[]{:S(2)}, u32[]{:S(2)}) collective-permute-start(f32[328,128]{1,0:T(8,128)S(1)} %shard_map.86.rest_0_.refs_7_), channel_id=1, source_target_pairs={{0,1},{1,0},{2,3},{3,2},{4,5},{5,4},{6,7},{7,6},{8,9},{9,8},{10,11... | collective-permute-start | bytes 503816 | tf_op jit(solution)/shard_map/ppermute | solution.py:341
  12.5 11.0 %collective-permute-start.8 = (f32[328,128]{1,0:T(8,128)S(1)}, f32[328,128]{1,0:T(8,128)S(1)}, u32[]{:S(2)}, u32[]{:S(2)}) collective-permute-start(f32[328,128]{1,0:T(8,128)S(1)} %collective-permute-done.7.rest_12_.refs_19_), channel_id=1, source_target_pairs={{0,4},{1,5},{2,6},{3,7},{4,0},{5,1},{6,2},{7,3},{8,12},{9,13},{10,... | collective-permute-start | bytes 503816 | tf_op jit(solution)/shard_map/ppermute | solution.py:341
  12.5 12.2 %collective-permute-start.2 = (f32[328,128]{1,0:T(8,128)S(1)}, f32[328,128]{1,0:T(8,128)S(1)}, u32[]{:S(2)}, u32[]{:S(2)}) collective-permute-start(f32[328,128]{1,0:T(8,128)S(1)} %collective-permute-done.1.rest_2_.refs_9_), channel_id=1, source_target_pairs={{0,1},{1,0},{2,3},{3,2},{4,5},{5,4},{6,7},{7,6},{8,9},{9,8},{10,11... | collective-permute-start | bytes 503816 | tf_op jit(solution)/shard_map/ppermute | solution.py:341
  20.2 5.4 %collective-permute-start.4 = (f32[328,128]{1,0:T(8,128)S(1)}, f32[328,128]{1,0:T(8,128)S(1)}, u32[]{:S(2)}, u32[]{:S(2)}) collective-permute-start(f32[328,128]{1,0:T(8,128)S(1)} %get-tuple-element.11.rest_4_.refs_11_), channel_id=1, source_target_pairs={{0,1},{1,0},{2,3},{3,2},{4,5},{5,4},{6,7},{7,6},{8,9},{9,8},{10,11... | collective-permute-start | bytes 503816 | tf_op jit(solution)/shard_map/ppermute | solution.py:341
  22.0 5.9 %collective-permute-start.5 = (f32[328,128]{1,0:T(8,128)S(1)}, f32[328,128]{1,0:T(8,128)S(1)}, u32[]{:S(2)}, u32[]{:S(2)}) collective-permute-start(f32[328,128]{1,0:T(8,128)S(1)} %get-tuple-element.11.rest_4_.refs_11_), channel_id=1, source_target_pairs={{0,2},{1,3},{2,0},{3,1},{4,6},{5,7},{6,4},{7,5},{8,10},{9,11},{10,... | collective-permute-start | bytes 503816 | tf_op jit(solution)/shard_map/ppermute | solution.py:341
  23.2 8.2 %collective-permute-start.13 = (f32[328,128]{1,0:T(8,128)S(1)}, f32[328,128]{1,0:T(8,128)S(1)}, u32[]{:S(2)}, u32[]{:S(2)}) collective-permute-start(f32[328,128]{1,0:T(8,128)S(1)} %collective-permute-done.7.rest_12_.refs_19_), channel_id=1, source_target_pairs={{0,2},{1,3},{2,0},{3,1},{4,6},{5,7},{6,4},{7,5},{8,10},{9,11},{10,... | collective-permute-start | bytes 503816 | tf_op jit(solution)/shard_map/ppermute | solution.py:341
  23.5 11.6 %collective-permute-start.10 = (f32[328,128]{1,0:T(8,128)S(1)}, f32[328,128]{1,0:T(8,128)S(1)}, u32[]{:S(2)}, u32[]{:S(2)}) collective-permute-start(f32[328,128]{1,0:T(8,128)S(1)} %collective-permute-done.8.rest_8_.refs_15_), channel_id=1, source_target_pairs={{0,2},{1,3},{2,0},{3,1},{4,6},{5,7},{6,4},{7,5},{8,10},{9,11},{10,... | collective-permute-start | bytes 503816 | tf_op jit(solution)/shard_map/ppermute | solution.py:341
  24.7 11.2 %collective-permute-start.12 = (f32[328,128]{1,0:T(8,128)S(1)}, f32[328,128]{1,0:T(8,128)S(1)}, u32[]{:S(2)}, u32[]{:S(2)}) collective-permute-start(f32[328,128]{1,0:T(8,128)S(1)} %collective-permute-done.7.rest_12_.refs_19_), channel_id=1, source_target_pairs={{0,1},{1,0},{2,3},{3,2},{4,5},{5,4},{6,7},{7,6},{8,9},{9,8},{10,11... | collective-permute-start | bytes 503816 | tf_op jit(solution)/shard_map/ppermute | solution.py:341
  25.6 10.3 %collective-permute-start.9 = (f32[328,128]{1,0:T(8,128)S(1)}, f32[328,128]{1,0:T(8,128)}, u32[]{:S(2)}, u32[]{:S(2)}) collective-permute-start(f32[328,128]{1,0:T(8,128)S(1)} %collective-permute-done.8.rest_8_.refs_15_), channel_id=1, source_target_pairs={{0,1},{1,0},{2,3},{3,2},{4,5},{5,4},{6,7},{7,6},{8,9},{9,8},{10,11... | collective-permute-start | bytes 503816 | tf_op jit(solution)/shard_map/ppermute | solution.py:341
  27.9 8.1 %collective-permute-start.6 = (f32[328,128]{1,0:T(8,128)S(1)}, f32[328,128]{1,0:T(8,128)}, u32[]{:S(2)}, u32[]{:S(2)}) collective-permute-start(f32[328,128]{1,0:T(8,128)S(1)} %collective-permute-done.5.rest_6_.refs_13_), channel_id=1, source_target_pairs={{0,1},{1,0},{2,3},{3,2},{4,5},{5,4},{6,7},{7,6},{8,9},{9,8},{10,11... | collective-permute-start | bytes 503816 | tf_op jit(solution)/shard_map/ppermute | solution.py:341
  31.5 4.5 %collective-permute-start.14 = (f32[328,128]{1,0:T(8,128)S(1)}, f32[328,128]{1,0:T(8,128)}, u32[]{:S(2)}, u32[]{:S(2)}) collective-permute-start(f32[328,128]{1,0:T(8,128)S(1)} %collective-permute-done.13.rest_14_.refs_21_), channel_id=1, source_target_pairs={{0,1},{1,0},{2,3},{3,2},{4,5},{5,4},{6,7},{7,6},{8,9},{9,8},{10,11... | collective-permute-start | bytes 503816 | tf_op jit(solution)/shard_map/ppermute | solution.py:341
  35.1 2.0 %collective-permute-start.11 = (f32[328,128]{1,0:T(8,128)S(1)}, f32[328,128]{1,0:T(8,128)}, u32[]{:S(2)}, u32[]{:S(2)}) collective-permute-start(f32[328,128]{1,0:T(8,128)S(1)} %collective-permute-done.10.rest_10_.refs_17_), channel_id=1, source_target_pairs={{0,1},{1,0},{2,3},{3,2},{4,5},{5,4},{6,7},{7,6},{8,9},{9,8},{10,11... | collective-permute-start | bytes 503816 | tf_op jit(solution)/shard_map/ppermute | solution.py:341
  51.2 28.6 %all-to-all-start = ((f32[16,120,128]{2,1,0:T(8,128)}), f32[16,120,128]{2,1,0:T(8,128)S(1)}, u32[]{:S(2)}, u32[]{:S(2)}) async-start(f32[16,120,128]{2,1,0:T(8,128)} %shard_map.89), calls=%async_computation | async-start | bytes 1966080 | tf_op jit(solution)/shard_map/all_to_all | solution.py:336
  83.5 9.1 %collective-permute-start.22 = (f32[328,128]{1,0:T(8,128)S(1)}, f32[328,128]{1,0:T(8,128)S(1)}, u32[]{:S(2)}, u32[]{:S(2)}) collective-permute-start(f32[328,128]{1,0:T(8,128)S(1)} %shard_map.90.g_ref.refs_7_.g_in), channel_id=1, source_target_pairs={{0,12},{1,13},{2,14},{3,15},{4,8},{5,9},{6,10},{7,11},{8,4},{9,5},... | collective-permute-start | bytes 503816 | tf_op jit(solution)/shard_map/ppermute | solution.py:341
  84.5 8.1 %collective-permute-start.16 = (f32[328,128]{1,0:T(8,128)S(1)}, f32[328,128]{1,0:T(8,128)S(1)}, u32[]{:S(2)}, u32[]{:S(2)}) collective-permute-start(f32[328,128]{1,0:T(8,128)S(1)} %shard_map.90.g_ref.refs_7_.g_in), channel_id=1, source_target_pairs={{0,2},{1,3},{2,0},{3,1},{4,6},{5,7},{6,4},{7,5},{8,10},{9,11},{10,... | collective-permute-start | bytes 503816 | tf_op jit(solution)/shard_map/ppermute | solution.py:341
  84.8 8.6 %collective-permute-start.18 = (f32[328,128]{1,0:T(8,128)S(1)}, f32[328,128]{1,0:T(8,128)S(1)}, u32[]{:S(2)}, u32[]{:S(2)}) collective-permute-start(f32[328,128]{1,0:T(8,128)S(1)} %shard_map.90.g_ref.refs_7_.g_in), channel_id=1, source_target_pairs={{0,4},{1,5},{2,6},{3,7},{4,0},{5,1},{6,2},{7,3},{8,12},{9,13},{10,... | collective-permute-start | bytes 503816 | tf_op jit(solution)/shard_map/ppermute | solution.py:341
  87.1 8.9 %collective-permute-start.15 = (f32[328,128]{1,0:T(8,128)S(1)}, f32[328,128]{1,0:T(8,128)S(1)}, u32[]{:S(2)}, u32[]{:S(2)}) collective-permute-start(f32[328,128]{1,0:T(8,128)S(1)} %shard_map.90.g_ref.refs_7_.g_in), channel_id=1, source_target_pairs={{0,1},{1,0},{2,3},{3,2},{4,5},{5,4},{6,7},{7,6},{8,9},{9,8},{10,11... | collective-permute-start | bytes 503816 | tf_op jit(solution)/shard_map/ppermute | solution.py:341
  92.6 5.4 %collective-permute-start.23 = (f32[328,128]{1,0:T(8,128)S(1)}, f32[328,128]{1,0:T(8,128)S(1)}, u32[]{:S(2)}, u32[]{:S(2)}) collective-permute-start(f32[328,128]{1,0:T(8,128)S(1)} %collective-permute-done.22.refs_19_), channel_id=1, source_target_pairs={{0,4},{1,5},{2,6},{3,7},{4,0},{5,1},{6,2},{7,3},{8,12},{9,13},{10,... | collective-permute-start | bytes 503816 | tf_op jit(solution)/shard_map/ppermute | solution.py:341
  92.6 7.1 %collective-permute-start.17 = (f32[328,128]{1,0:T(8,128)S(1)}, f32[328,128]{1,0:T(8,128)S(1)}, u32[]{:S(2)}, u32[]{:S(2)}) collective-permute-start(f32[328,128]{1,0:T(8,128)S(1)} %collective-permute-done.16.refs_9_), channel_id=1, source_target_pairs={{0,1},{1,0},{2,3},{3,2},{4,5},{5,4},{6,7},{7,6},{8,9},{9,8},{10,11... | collective-permute-start | bytes 503816 | tf_op jit(solution)/shard_map/ppermute | solution.py:341
  93.4 7.9 %collective-permute-start.19 = (f32[328,128]{1,0:T(8,128)S(1)}, f32[328,128]{1,0:T(8,128)S(1)}, u32[]{:S(2)}, u32[]{:S(2)}) collective-permute-start(f32[328,128]{1,0:T(8,128)S(1)} %collective-permute-done.18.refs_11_), channel_id=1, source_target_pairs={{0,1},{1,0},{2,3},{3,2},{4,5},{5,4},{6,7},{7,6},{8,9},{9,8},{10,11... | collective-permute-start | bytes 503816 | tf_op jit(solution)/shard_map/ppermute | solution.py:341
  94.0 7.4 %collective-permute-start.20 = (f32[328,128]{1,0:T(8,128)S(1)}, f32[328,128]{1,0:T(8,128)S(1)}, u32[]{:S(2)}, u32[]{:S(2)}) collective-permute-start(f32[328,128]{1,0:T(8,128)S(1)} %collective-permute-done.18.refs_11_), channel_id=1, source_target_pairs={{0,2},{1,3},{2,0},{3,1},{4,6},{5,7},{6,4},{7,5},{8,10},{9,11},{10,... | collective-permute-start | bytes 503816 | tf_op jit(solution)/shard_map/ppermute | solution.py:341
  96.0 8.2 %collective-permute-start.28 = (f32[328,128]{1,0:T(8,128)S(1)}, f32[328,128]{1,0:T(8,128)S(1)}, u32[]{:S(2)}, u32[]{:S(2)}) collective-permute-start(f32[328,128]{1,0:T(8,128)S(1)} %collective-permute-done.22.refs_19_), channel_id=1, source_target_pairs={{0,2},{1,3},{2,0},{3,1},{4,6},{5,7},{6,4},{7,5},{8,10},{9,11},{10,... | collective-permute-start | bytes 503816 | tf_op jit(solution)/shard_map/ppermute | solution.py:341
  98.0 9.8 %collective-permute-start.25 = (f32[328,128]{1,0:T(8,128)S(1)}, f32[328,128]{1,0:T(8,128)S(1)}, u32[]{:S(2)}, u32[]{:S(2)}) collective-permute-start(f32[328,128]{1,0:T(8,128)S(1)} %collective-permute-done.23.refs_15_), channel_id=1, source_target_pairs={{0,2},{1,3},{2,0},{3,1},{4,6},{5,7},{6,4},{7,5},{8,10},{9,11},{10,... | collective-permute-start | bytes 503816 | tf_op jit(solution)/shard_map/ppermute | solution.py:341
  99.7 8.7 %collective-permute-start.27 = (f32[328,128]{1,0:T(8,128)S(1)}, f32[328,128]{1,0:T(8,128)S(1)}, u32[]{:S(2)}, u32[]{:S(2)}) collective-permute-start(f32[328,128]{1,0:T(8,128)S(1)} %collective-permute-done.22.refs_19_), channel_id=1, source_target_pairs={{0,1},{1,0},{2,3},{3,2},{4,5},{5,4},{6,7},{7,6},{8,9},{9,8},{10,11... | collective-permute-start | bytes 503816 | tf_op jit(solution)/shard_map/ppermute | solution.py:341
  101.3 7.1 %collective-permute-start.24 = (f32[328,128]{1,0:T(8,128)S(1)}, f32[328,128]{1,0:T(8,128)S(1)}, u32[]{:S(2)}, u32[]{:S(2)}) collective-permute-start(f32[328,128]{1,0:T(8,128)S(1)} %collective-permute-done.23.refs_15_), channel_id=1, source_target_pairs={{0,1},{1,0},{2,3},{3,2},{4,5},{5,4},{6,7},{7,6},{8,9},{9,8},{10,11... | collective-permute-start | bytes 503816 | tf_op jit(solution)/shard_map/ppermute | solution.py:341
  101.3 7.1 %collective-permute-start.21 = (f32[328,128]{1,0:T(8,128)S(1)}, f32[328,128]{1,0:T(8,128)S(1)}, u32[]{:S(2)}, u32[]{:S(2)}) collective-permute-start(f32[328,128]{1,0:T(8,128)S(1)} %collective-permute-done.20.refs_13_), channel_id=1, source_target_pairs={{0,1},{1,0},{2,3},{3,2},{4,5},{5,4},{6,7},{7,6},{8,9},{9,8},{10,11... | collective-permute-start | bytes 503816 | tf_op jit(solution)/shard_map/ppermute | solution.py:341
  104.2 4.2 %collective-permute-start.29 = (f32[328,128]{1,0:T(8,128)S(1)}, f32[328,128]{1,0:T(8,128)S(1)}, u32[]{:S(2)}, u32[]{:S(2)}) collective-permute-start(f32[328,128]{1,0:T(8,128)S(1)} %collective-permute-done.28.refs_21_), channel_id=1, source_target_pairs={{0,1},{1,0},{2,3},{3,2},{4,5},{5,4},{6,7},{7,6},{8,9},{9,8},{10,11... | collective-permute-start | bytes 503816 | tf_op jit(solution)/shard_map/ppermute | solution.py:341
  107.8 1.6 collective-permute-start.26
  122.5 21.8 %all-to-all-start.1 = ((f32[16,80,128]{2,1,0:T(8,128)}), f32[16,80,128]{2,1,0:T(8,128)S(1)}, u32[]{:S(2)}, u32[]{:S(2)}) async-start(f32[16,80,128]{2,1,0:T(8,128)} %shard_map.92), calls=%async_computation.1 | async-start | bytes 1310720 | tf_op jit(solution)/shard_map/all_to_all | solution.py:336
  146.6 9.8 %collective-permute-start.37 = (f32[328,128]{1,0:T(8,128)S(1)}, f32[328,128]{1,0:T(8,128)S(1)}, u32[]{:S(2)}, u32[]{:S(2)}) collective-permute-start(f32[328,128]{1,0:T(8,128)S(1)} %shard_map.93.rest_0_), channel_id=1, source_target_pairs={{0,12},{1,13},{2,14},{3,15},{4,8},{5,9},{6,10},{7,11},{8,4},{9,5},... | collective-permute-start | bytes 503816 | tf_op jit(solution)/shard_map/ppermute | solution.py:341
  146.9 9.5 %collective-permute-start.31 = (f32[328,128]{1,0:T(8,128)S(1)}, f32[328,128]{1,0:T(8,128)S(1)}, u32[]{:S(2)}, u32[]{:S(2)}) collective-permute-start(f32[328,128]{1,0:T(8,128)S(1)} %shard_map.93.rest_0_), channel_id=1, source_target_pairs={{0,2},{1,3},{2,0},{3,1},{4,6},{5,7},{6,4},{7,5},{8,10},{9,11},{10,... | collective-permute-start | bytes 503816 | tf_op jit(solution)/shard_map/ppermute | solution.py:341
  147.5 9.5 %collective-permute-start.33 = (f32[328,128]{1,0:T(8,128)S(1)}, f32[328,128]{1,0:T(8,128)S(1)}, u32[]{:S(2)}, u32[]{:S(2)}) collective-permute-start(f32[328,128]{1,0:T(8,128)S(1)} %shard_map.93.rest_0_), channel_id=1, source_target_pairs={{0,4},{1,5},{2,6},{3,7},{4,0},{5,1},{6,2},{7,3},{8,12},{9,13},{10,... | collective-permute-start | bytes 503816 | tf_op jit(solution)/shard_map/ppermute | solution.py:341
  149.8 8.9 %collective-permute-start.30 = (f32[328,128]{1,0:T(8,128)S(1)}, f32[328,128]{1,0:T(8,128)S(1)}, u32[]{:S(2)}, u32[]{:S(2)}) collective-permute-start(f32[328,128]{1,0:T(8,128)S(1)} %shard_map.93.rest_0_), channel_id=1, source_target_pairs={{0,1},{1,0},{2,3},{3,2},{4,5},{5,4},{6,7},{7,6},{8,9},{9,8},{10,11... | collective-permute-start | bytes 503816 | tf_op jit(solution)/shard_map/ppermute | solution.py:341
  156.4 5.3 %collective-permute-start.38 = (f32[328,128]{1,0:T(8,128)S(1)}, f32[328,128]{1,0:T(8,128)S(1)}, u32[]{:S(2)}, u32[]{:S(2)}) collective-permute-start(f32[328,128]{1,0:T(8,128)S(1)} %collective-permute-done.37.rest_12_), channel_id=1, source_target_pairs={{0,4},{1,5},{2,6},{3,7},{4,0},{5,1},{6,2},{7,3},{8,12},{9,13},{10,... | collective-permute-start | bytes 503816 | tf_op jit(solution)/shard_map/ppermute | solution.py:341
  156.4 5.3 %collective-permute-start.32 = (f32[328,128]{1,0:T(8,128)S(1)}, f32[328,128]{1,0:T(8,128)S(1)}, u32[]{:S(2)}, u32[]{:S(2)}) collective-permute-start(f32[328,128]{1,0:T(8,128)S(1)} %collective-permute-done.31.rest_2_), channel_id=1, source_target_pairs={{0,1},{1,0},{2,3},{3,2},{4,5},{5,4},{6,7},{7,6},{8,9},{9,8},{10,11... | collective-permute-start | bytes 503816 | tf_op jit(solution)/shard_map/ppermute | solution.py:341
  157.0 6.7 %collective-permute-start.34 = (f32[328,128]{1,0:T(8,128)S(1)}, f32[328,128]{1,0:T(8,128)S(1)}, u32[]{:S(2)}, u32[]{:S(2)}) collective-permute-start(f32[328,128]{1,0:T(8,128)S(1)} %collective-permute-done.33.rest_4_), channel_id=1, source_target_pairs={{0,1},{1,0},{2,3},{3,2},{4,5},{5,4},{6,7},{7,6},{8,9},{9,8},{10,11... | collective-permute-start | bytes 503816 | tf_op jit(solution)/shard_map/ppermute | solution.py:341
  157.1 6.7 %collective-permute-start.35 = (f32[328,128]{1,0:T(8,128)S(1)}, f32[328,128]{1,0:T(8,128)S(1)}, u32[]{:S(2)}, u32[]{:S(2)}) collective-permute-start(f32[328,128]{1,0:T(8,128)S(1)} %collective-permute-done.33.rest_4_), channel_id=1, source_target_pairs={{0,2},{1,3},{2,0},{3,1},{4,6},{5,7},{6,4},{7,5},{8,10},{9,11},{10,... | collective-permute-start | bytes 503816 | tf_op jit(solution)/shard_map/ppermute | solution.py:341
  158.6 7.7 %collective-permute-start.43 = (f32[328,128]{1,0:T(8,128)S(1)}, f32[328,128]{1,0:T(8,128)S(1)}, u32[]{:S(2)}, u32[]{:S(2)}) collective-permute-start(f32[328,128]{1,0:T(8,128)S(1)} %collective-permute-done.37.rest_12_), channel_id=1, source_target_pairs={{0,2},{1,3},{2,0},{3,1},{4,6},{5,7},{6,4},{7,5},{8,10},{9,11},{10,... | collective-permute-start | bytes 503816 | tf_op jit(solution)/shard_map/ppermute | solution.py:341
  161.7 8.2 %collective-permute-start.40 = (f32[328,128]{1,0:T(8,128)S(1)}, f32[328,128]{1,0:T(8,128)S(1)}, u32[]{:S(2)}, u32[]{:S(2)}) collective-permute-start(f32[328,128]{1,0:T(8,128)S(1)} %collective-permute-done.38.rest_8_), channel_id=1, source_target_pairs={{0,2},{1,3},{2,0},{3,1},{4,6},{5,7},{6,4},{7,5},{8,10},{9,11},{10,... | collective-permute-start | bytes 503816 | tf_op jit(solution)/shard_map/ppermute | solution.py:341
  161.7 9.4 %collective-permute-start.42 = (f32[328,128]{1,0:T(8,128)S(1)}, f32[328,128]{1,0:T(8,128)S(1)}, u32[]{:S(2)}, u32[]{:S(2)}) collective-permute-start(f32[328,128]{1,0:T(8,128)S(1)} %collective-permute-done.37.rest_12_), channel_id=1, source_target_pairs={{0,1},{1,0},{2,3},{3,2},{4,5},{5,4},{6,7},{7,6},{8,9},{9,8},{10,11... | collective-permute-start | bytes 503816 | tf_op jit(solution)/shard_map/ppermute | solution.py:341
  163.7 7.3 %collective-permute-start.39 = (f32[328,128]{1,0:T(8,128)S(1)}, f32[328,128]{1,0:T(8,128)S(1)}, u32[]{:S(2)}, u32[]{:S(2)}) collective-permute-start(f32[328,128]{1,0:T(8,128)S(1)} %collective-permute-done.38.rest_8_), channel_id=1, source_target_pairs={{0,1},{1,0},{2,3},{3,2},{4,5},{5,4},{6,7},{7,6},{8,9},{9,8},{10,11... | collective-permute-start | bytes 503816 | tf_op jit(solution)/shard_map/ppermute | solution.py:341
  163.8 7.3 %collective-permute-start.36 = (f32[328,128]{1,0:T(8,128)S(1)}, f32[328,128]{1,0:T(8,128)S(1)}, u32[]{:S(2)}, u32[]{:S(2)}) collective-permute-start(f32[328,128]{1,0:T(8,128)S(1)} %collective-permute-done.35.rest_6_), channel_id=1, source_target_pairs={{0,1},{1,0},{2,3},{3,2},{4,5},{5,4},{6,7},{7,6},{8,9},{9,8},{10,11... | collective-permute-start | bytes 503816 | tf_op jit(solution)/shard_map/ppermute | solution.py:341
  166.3 4.8 %collective-permute-start.44 = (f32[328,128]{1,0:T(8,128)S(1)}, f32[328,128]{1,0:T(8,128)S(1)}, u32[]{:S(2)}, u32[]{:S(2)}) collective-permute-start(f32[328,128]{1,0:T(8,128)S(1)} %collective-permute-done.43.rest_14_), channel_id=1, source_target_pairs={{0,1},{1,0},{2,3},{3,2},{4,5},{5,4},{6,7},{7,6},{8,9},{9,8},{10,11... | collective-permute-start | bytes 503816 | tf_op jit(solution)/shard_map/ppermute | solution.py:341
  169.9 2.2 %collective-permute-start.41 = (f32[328,128]{1,0:T(8,128)S(1)}, f32[328,128]{1,0:T(8,128)S(1)}, u32[]{:S(2)}, u32[]{:S(2)}) collective-permute-start(f32[328,128]{1,0:T(8,128)S(1)} %collective-permute-done.40.rest_10_), channel_id=1, source_target_pairs={{0,1},{1,0},{2,3},{3,2},{4,5},{5,4},{6,7},{7,6},{8,9},{9,8},{10,11... | collective-permute-start | bytes 503816 | tf_op jit(solution)/shard_map/ppermute | solution.py:341
  (22 other events, 216.9 us)

commit v5 on v4

--- a/solution.py
+++ b/solution.py
@@ -67,22 +67,30 @@
 
 
 class Fetch:
-    def __init__(self, model, held, sems):
-        pairs = held.shape[2]
+    def __init__(self, model, held, sems, firsts=(0,)):
+        count, pairs = held.shape[0] // len(firsts), held.shape[2]
         parts = 3 if pairs % 3 == 0 else 1
         self.size = pairs // parts
         self.copies = []
         for i in range(parts):
             part = pl.ds(i * self.size, self.size)
-            self.copies.append(
-                pltpu.make_async_copy(model.at[:, :, part], held.at[:, :, part], sems.at[i])
-            )
-        for copy in self.copies:
-            copy.start()
+            self.copies.append([])
+            for j, first in enumerate(firsts):
+                self.copies[i].append(
+                    pltpu.make_async_copy(
+                        model.at[pl.ds(first, count), :, part],
+                        held.at[pl.ds(j * count, count), :, part],
+                        sems.at[i, j],
+                    )
+                )
+        for copies in self.copies:
+            for copy in copies:
+                copy.start()
 
     def each(self, body):
-        for i, copy in enumerate(self.copies):
-            copy.wait()
+        for i, copies in enumerate(self.copies):
+            for copy in copies:
+                copy.wait()
             lax.fori_loop(i * self.size, (i + 1) * self.size, body, 0)
 
 
@@ -221,69 +229,59 @@
     return cross(jnp.where(even, a, b), jnp.where(even, b, a))
 
 
-def products(n, dpc, me, first_ref, second_ref, ins, hre, him):
+def products(dpc, me, first_ref, second_ref, ins, hre, him):
     even = lax.rem(me, 2) == 0
 
     def pair(b, carry):
         p, q = first_ref[b], second_ref[b]
-        for m in range(n // 2):
-            k = lax.div(jnp.bitwise_xor(me, 2 * m), 2)
+        for m in range(len(ins) // 2):
             pr, pi = piece_pair(dpc, even, ins, m, p)
             qr, qi = piece_pair(dpc, even, ins, m, q)
-            rows = pl.ds(pl.multiple_of(k * TILE, TILE), TILE)
-            hre[b, rows, :] = pr * qr + pi * qi
-            him[b, rows, :] = pi * qr - pr * qi
+            hre[b, m * TILE : (m + 1) * TILE, :] = pr * qr + pi * qi
+            him[b, m * TILE : (m + 1) * TILE, :] = pi * qr - pr * qi
         return carry
 
     lax.fori_loop(0, first_ref.shape[0], pair, 0)
 
 
-def predict(n, dpc, b, model_ref, vis_ref, mask_ref, hre, him):
-    def step(k, acc):
-        acc_re, acc_im = acc
+def predict(dpc, b, acc, chips, model_ref, hre, him):
+    acc_re, acc_im = acc
+    for m, k in enumerate(chips):
         for dd in range(dpc):
             mr = model_ref[k * dpc + dd, 0, b].astype(F32)
             mi = model_ref[k * dpc + dd, 1, b].astype(F32)
-            hr = hre[b, pl.ds(k * TILE + dd, 1), :]
-            hi = him[b, pl.ds(k * TILE + dd, 1), :]
+            row = m * TILE + dd
+            hr = hre[b, row : row + 1, :]
+            hi = him[b, row : row + 1, :]
             acc_re = acc_re - (hr * mr - hi * mi)
             acc_im = acc_im - (hr * mi + hi * mr)
-        return acc_re, acc_im
-
-    acc = lax.fori_loop(0, n // 2, step, (vis_ref[0, b], vis_ref[1, b]))
+    return acc_re, acc_im
+
+
+def weighted(b, acc, mask_ref):
     weight = mask_ref[b].astype(F32)
     return weight * acc[0], weight * acc[1]
 
 
-def pass_kernel(
-    n, dpc, start, me_ref, first_ref, second_ref, model_hbm, vis_ref, mask_ref, power_ref, *rest
-):
-    ins, (out_ref, model_ref, sems, hre, him, cre, cim), work = rest[:n], rest[n : n + 7], rest[n + 7 :]
-    fetch = Fetch(model_hbm, model_ref, sems)
-    build = products_first if start else products
-    build(n, dpc, me_ref[0], first_ref, second_ref, ins, hre, him, *work)
-
-    def pair(b, carry):
-        res_re, res_im = predict(n, dpc, b, model_ref, vis_ref, mask_ref, hre, him)
-
-        def step(k, carry):
-            for dd in range(dpc):
-                mr = model_ref[k * dpc + dd, 0, b].astype(F32)
-                mi = model_ref[k * dpc + dd, 1, b].astype(F32)
-                row = pl.ds(k * TILE + dd, 1)
-                cre[b, row, :] = jnp.sum(mr * res_re + mi * res_im, axis=0, keepdims=True)
-                cim[b, row, :] = jnp.sum(mr * res_im - mi * res_re, axis=0, keepdims=True)
-            return carry
-
-        return lax.fori_loop(0, n // 2, step, carry)
-
-    fetch.each(pair)
-    pairs = mask_ref.shape[0]
-    for k in range(n // 2):
-        tile = slice(k * TILE, (k + 1) * TILE)
+def correlate(dpc, b, res, chips, model_ref, cre, cim):
+    res_re, res_im = res
+    for m, k in enumerate(chips):
+        for dd in range(dpc):
+            mr = model_ref[k * dpc + dd, 0, b].astype(F32)
+            mi = model_ref[k * dpc + dd, 1, b].astype(F32)
+            row = m * TILE + dd
+            cre[b, row : row + 1, :] = jnp.sum(mr * res_re + mi * res_im, axis=0, keepdims=True)
+            cim[b, row : row + 1, :] = jnp.sum(mr * res_im - mi * res_re, axis=0, keepdims=True)
+
+
+def write_sums(dpc, pairs, chips, cre, cim, tiles, power_ref, out_ref, start):
+    for m, k in enumerate(chips):
+        tile = slice(m * TILE, (m + 1) * TILE)
+        strong = pl.ds(k * TILE, TILE)
         for b in range(pairs):
-            w = power_ref[b, tile, :]
-            x0, x1 = cross(cre[b, tile, :] + hre[b, tile, :] * w, cim[b, tile, :] + him[b, tile, :] * w)
+            hr, hi = tiles(b, m)
+            w = power_ref[b, strong, :]
+            x0, x1 = cross(cre[b, tile, :] + hr * w, cim[b, tile, :] + hi * w)
             out_ref[2 * k, b * dpc : (b + 1) * dpc, :] = x0[:dpc]
             out_ref[2 * k + 1, b * dpc : (b + 1) * dpc, :] = x1[:dpc]
         if pairs < ROWS:
@@ -292,32 +290,100 @@
             out_ref[2 * k + 1, pairs * dpc : ROWS * dpc, :] = empty
         if start:
             for r in range(TILE):
-                x0, x1 = cross(power_ref[r, tile, :], power_ref[r + TILE, tile, :])
+                x0, x1 = cross(power_ref[r, strong, :], power_ref[r + TILE, strong, :])
                 to = (ROWS + r) * dpc
                 out_ref[2 * k, to : to + dpc, :] = x0[:dpc]
                 out_ref[2 * k + 1, to : to + dpc, :] = x1[:dpc]
 
 
-def last_kernel(n, dpc, me_ref, first_ref, second_ref, model_hbm, vis_ref, mask_ref, *rest):
-    ins, (res_ref, gains_ref, model_ref, sems, hre, him) = rest[:n], rest[n:]
+def first_pass_kernel(
+    n, dpc, me_ref, first_ref, second_ref, model_hbm, vis_ref, mask_ref, power_ref, *rest
+):
+    ins, (out_ref, model_ref, sems, hre, him, cre, cim, stack) = rest[:n], rest[n:]
+    fetch = Fetch(model_hbm, model_ref, sems)
+    products_first(n, dpc, me_ref[0], first_ref, second_ref, ins, hre, him, stack)
+    chips = range(n // 2)
+
+    def pair(b, carry):
+        acc = predict(dpc, b, (vis_ref[0, b], vis_ref[1, b]), chips, model_ref, hre, him)
+        correlate(dpc, b, weighted(b, acc, mask_ref), chips, model_ref, cre, cim)
+        return carry
+
+    fetch.each(pair)
+
+    def tiles(b, m):
+        tile = slice(m * TILE, (m + 1) * TILE)
+        return hre[b, tile, :], him[b, tile, :]
+
+    write_sums(dpc, mask_ref.shape[0], chips, cre, cim, tiles, power_ref, out_ref, True)
+
+
+NEAR, FAR = (0, 1, 2, 6), (3, 4, 5, 7)
+
+
+def chips_of(me, pairs):
+    return [jnp.bitwise_xor(lax.div(me, 2), m) for m in pairs]
+
+
+def early_kernel(n, dpc, me_ref, first_ref, second_ref, model_hbm, vis_ref, unused_in, *rest):
+    ins, (acc_ref, hre, him, unused_out, model_ref, sems) = rest[: 2 * len(NEAR)], rest[2 * len(NEAR) :]
+    me = me_ref[0]
+    fetch = Fetch(model_hbm, model_ref, sems, [k * dpc for k in chips_of(me, NEAR)])
+    products(dpc, me, first_ref, second_ref, ins, hre, him)
+
+    def pair(b, carry):
+        acc = vis_ref[0, b], vis_ref[1, b]
+        acc_ref[0, b], acc_ref[1, b] = predict(dpc, b, acc, range(len(NEAR)), model_ref, hre, him)
+        return carry
+
+    fetch.each(pair)
+
+
+def later_pass_kernel(
+    n, dpc, me_ref, first_ref, second_ref, model_hbm, mask_ref, power_ref, acc_ref, near_re, near_im, *rest
+):
+    ins, (out_ref, model_ref, sems, hre, him, cre, cim) = rest[: 2 * len(FAR)], rest[2 * len(FAR) :]
     fetch = Fetch(model_hbm, model_ref, sems)
     me = me_ref[0]
+    products(dpc, me, first_ref, second_ref, ins, hre, him)
+    far = chips_of(me, FAR)
+    chips = chips_of(me, NEAR) + far
+
+    def pair(b, carry):
+        acc = predict(dpc, b, (acc_ref[0, b], acc_ref[1, b]), far, model_ref, hre, him)
+        correlate(dpc, b, weighted(b, acc, mask_ref), chips, model_ref, cre, cim)
+        return carry
+
+    fetch.each(pair)
+
+    def tiles(b, m):
+        re, im = (near_re, near_im) if m < len(NEAR) else (hre, him)
+        m = m % len(NEAR)
+        tile = slice(m * TILE, (m + 1) * TILE)
+        return re[b, tile, :], im[b, tile, :]
+
+    write_sums(dpc, mask_ref.shape[0], chips, cre, cim, tiles, power_ref, out_ref, False)
+
+
+def last_kernel(n, dpc, me_ref, first_ref, second_ref, model_hbm, mask_ref, acc_ref, *rest):
+    ins, (res_ref, gains_ref, model_ref, sems, hre, him) = rest[:n], rest[n:]
+    me = me_ref[0]
+    fetch = Fetch(model_hbm, model_ref, sems, [k * dpc for k in chips_of(me, FAR)])
+    products(dpc, me, first_ref, second_ref, ins[: 2 * len(FAR)], hre, him)
     per = STATIONS // n
     even = lax.rem(me, 2) == 0
-    for m in range(n // 2):
-        k = lax.div(jnp.bitwise_xor(me, 2 * m), 2)
+    for m, k in enumerate(chips_of(me, FAR + NEAR)):
         for s in range(per):
             re, im = piece_pair(dpc, even, ins, m, me * per + s)
             for dd in range(dpc):
                 at = s * SOURCE_COUNT + k * dpc + dd
                 gains_ref[0, pl.ds(at, 1), :] = re[dd : dd + 1]
                 gains_ref[1, pl.ds(at, 1), :] = im[dd : dd + 1]
-    products(n, dpc, me, first_ref, second_ref, ins, hre, him)
 
     def pair(b, carry):
-        res_re, res_im = predict(n, dpc, b, model_ref, vis_ref, mask_ref, hre, him)
-        res_ref[0, b] = res_re
-        res_ref[1, b] = res_im
+        acc = acc_ref[0, b], acc_ref[1, b]
+        acc = predict(dpc, b, acc, range(len(FAR)), model_ref, hre, him)
+        res_ref[0, b], res_ref[1, b] = weighted(b, acc, mask_ref)
         return carry
 
     fetch.each(pair)
@@ -336,18 +402,20 @@
     return lax.all_to_all(x, "bl", split_axis=0, concat_axis=0, tiled=True)
 
 
-def gather(n, piece, beside=lambda x: x):
+def gather(n, piece, beside):
     def send(x, o):
         return lax.ppermute(x, "bl", [(i, i ^ o) for i in range(n)])
 
     got = {0: piece}
     got[4], got[12] = send(piece, 4), send(piece, 12)
     got[2] = send(piece, 2)
-    got[4] = beside(got[4])
+    got[6] = send(got[4], 2)
     got[8] = send(got[12], 4)
-    for o in (4, 12, 8):
-        got[o + 2] = send(got[o], 2)
-    for o in (0, 2, 4, 12, 6, 14, 8, 10):
+    got[14], got[10] = send(got[12], 2), send(got[8], 2)
+    for o in (0, 2, 4, 12):
+        got[o + 1] = send(got[o], 1)
+    got[6] = beside(got[6], got)
+    for o in (6, 14, 8, 10):
         got[o + 1] = send(got[o], 1)
     return [got[o] for o in range(n)]
 
@@ -360,9 +428,12 @@
     me = lax.axis_index("bl").astype(jnp.int32).reshape(1)
     params = pltpu.CompilerParams(vmem_limit_bytes=VMEM_LIMIT)
     plane = (ROWS, n // 2 * TILE, channels)
+    half = (ROWS, n // 4 * TILE, channels)
     lots = n * 2 * ROWS
     mine = (STATIONS * dpc + TILE, channels)
-    held = [pltpu.VMEM(model.shape, BF16), pltpu.SemaphoreType.DMA((3,))]
+    sems = pltpu.SemaphoreType.DMA((3, n // 4))
+    held = [pltpu.VMEM(model.shape, BF16), sems]
+    held_half = [pltpu.VMEM((SOURCE_COUNT // 2,) + model.shape[1:], BF16), sems]
 
     def call(kernel, args, outs, scratch=(), micros=1, aliases={}):
         def place(x):
@@ -391,10 +462,10 @@
     )
     power = None
 
-    def powers_beside(x):
+    def powers_beside(x, got):
         nonlocal power
         power, x = call(
-            power_kernel, (model, mask, x), [shape(*plane), shape(*x.shape)], held, micros=6, aliases={2: 1}
+            power_kernel, (model, mask, x), [shape(*plane), shape(*x.shape)], held, micros=20, aliases={2: 1}
         )
         return x
 
@@ -406,37 +477,57 @@
         [(STATIONS * TILE, channels), (n, channels)],
         micros=2,
     )
-    for step in range(ITERS):
-        start = step == 0
-        work = [(n,) + piece.shape] if start else []
+    (sums,) = call(
+        first_pass_kernel,
+        (me, first, second, model, vis, mask, power, *got),
+        [shape(n, (ROWS + TILE) * dpc, channels)],
+        held + [plane] * 4 + [(n,) + piece.shape],
+        micros=9,
+    )
+    powers = exchange(sums)
+    (g,) = call(own_kernel, (g, onehot, sel, powers), [shape(*mine)], [(lots, 2 * width)])
+
+    def slots(got, pairs):
+        return [got[2 * m + c] for m in pairs for c in (0, 1)]
+
+    def gather_near(g):
+        near = None
+
+        def beside(x, got):
+            nonlocal near
+            args = (me, first, second, model, vis, x, *slots(got, NEAR))
+            outs = [shape(*vis.shape), shape(*half), shape(*half), shape(*x.shape)]
+            *near, x = call(early_kernel, args, outs, held_half, micros=20, aliases={5: 3})
+            return x
+
+        got = gather(n, g, beside)
+        return near, slots(got, NEAR), slots(got, FAR)
+
+    for step in range(1, ITERS):
+        near, _, far_slots = gather_near(g)
+        sel, den = call(
+            prepare_kernel,
+            (g, onehot, powers),
+            [shape(lots, width), shape(STATIONS, width)],
+            [(lots, width)],
+            micros=2,
+        )
         (sums,) = call(
-            lambda n, dpc, *refs: pass_kernel(n, dpc, start, *refs),
-            (me, first, second, model, vis, mask, power, *got),
-            [shape(n, (ROWS + (TILE if start else 0)) * dpc, channels)],
-            held + [plane] * 4 + work,
-            micros=9,
+            later_pass_kernel,
+            (me, first, second, model, mask, power, *near, *far_slots),
+            [shape(n, ROWS * dpc, channels)],
+            held + [half] * 2 + [plane] * 2,
+            micros=7,
         )
         sums = exchange(sums)
-        if start:
-            powers = sums
-            (g,) = call(own_kernel, (g, onehot, sel, sums), [shape(*mine)], [(lots, 2 * width)])
-        else:
-            (g,) = call(later_own_kernel, (g, onehot, sel, den, sums), [shape(*mine)], [(lots, width)])
-        got = gather(n, g)
-        if step < ITERS - 1:
-            sel, den = call(
-                prepare_kernel,
-                (g, onehot, powers),
-                [shape(lots, width), shape(STATIONS, width)],
-                [(lots, width)],
-                micros=2,
-            )
+        (g,) = call(later_own_kernel, (g, onehot, sel, den, sums), [shape(*mine)], [(lots, width)])
+    near, near_slots, far_slots = gather_near(g)
     residual, gains = call(
         last_kernel,
-        (me, first, second, model, vis, mask, *got),
+        (me, first, second, model, mask, near[0], *far_slots, *near_slots),
         [shape(*vis.shape), shape(2, *gre.shape)],
-        held + [plane] * 2,
-        micros=6,
+        held_half + [half] * 2,
+        micros=4,
     )
     return gains, residual
 

time: 183 us -> 164 us (0.90)
  waiting for transfers between devices: 66.8 us -> 40.7 us
  starting transfers between devices: 51.8 us -> 58.8 us
    ppermute x45, waiting for transfers between devices: 37.4 us -> 11.3 us  [send(): return lax.ppermute(x, 'bl', [(i, i ^ o) for i in range(n)])]
    ppermute x45, starting transfers between devices: 41.8 us -> 48.5 us  [send(): return lax.ppermute(x, 'bl', [(i, i ^ o) for i in range(n)])]
    pallas_call x9 -> x11, Pallas kernels: 46.8 us -> 47.6 us  [call(): pl.pallas_call(functools.partial(kernel, n, dpc), in_specs=[place(x) for...]
  transfers between devices with their start and end apart: 47 -> 47, of which waited for: 19 -> 15; matrix products, arithmetic and copies ran while one was open for 0% -> 0% of each run, Pallas kernels for 5% -> 11%
where the time goes in v5:
time: 164 us; the launch traced here: 161 us
  starting transfers between devices  58.8 us (36%)
  Pallas kernels  47.6 us (29%)
  waiting for transfers between devices  40.7 us (25%)
  local copies, waits for them, and re-layouts  13.2 us (8%)
    ppermute x45, starting transfers between devices, send(): return lax.ppermute(x, 'bl', [(i, i ^ o) for i in range(n)])  48.5 us
    pallas_call x11, Pallas kernels, call(): pl.pallas_call(functools.partial(kernel, n, dpc), in_specs=[place(x) for...  47.6 us
    all_to_all x2, waiting for transfers between devices, exchange(): return lax.all_to_all(x, 'bl', split_axis=0, concat_axis=0, tiled=True)  29.4 us
    unnamed x46, local copies, waits for them, and re-layouts  13.2 us
    ppermute x45, waiting for transfers between devices, send(): return lax.ppermute(x, 'bl', [(i, i ^ o) for i in range(n)])  11.3 us
    all_to_all x2, starting transfers between devices, exchange(): return lax.all_to_all(x, 'bl', split_axis=0, concat_axis=0, tiled=True)  10.4 us
  transfers between devices with their start and end apart: 47, of which 15 were waited for; matrix products, arithmetic and copies ran while one was open for 0% of the time, Pallas kernels for 11%

profile of v5, /device:TPU:9, one launch (start us, length us, event | category | flops | bytes accessed | tf_op | source)
XLA Modules:
  0.0 161.4 jit_solution(3618324790861954299)
XLA Ops:
  1.9 1.5 shard_map.86.rest_0_
  3.5 2.6 %collective-permute-start.7 = (f32[328,128]{1,0:T(8,128)S(1)}, f32[328,128]{1,0:T(8,128)S(1)}, u32[]{:S(2)}, u32[]{:S(2)}) collective-permute-start(f32[328,128]{1,0:T(8,128)S(1)} %shard_map.86.rest_0_), channel_id=1, source_target_pairs={{0,12},{1,13},{2,14},{3,15},{4,8},{5,9},{6,10},{7,11},{8,4},{9,5},... | collective-permute-start | bytes 503816 | tf_op jit(solution)/shard_map/ppermute | solution.py:407
  6.1 1.2 collective-permute-start.1
  7.3 1.4 collective-permute-done.3.rest_4_
  8.7 1.2 collective-permute-start.5
  9.9 4.6 %collective-permute-start.8 = (f32[328,128]{1,0:T(8,128)S(1)}, f32[328,128]{1,0:T(8,128)S(1)}, u32[]{:S(2)}, u32[]{:S(2)}) collective-permute-start(f32[328,128]{1,0:T(8,128)S(1)} %collective-permute-done.7.rest_12_), channel_id=1, source_target_pairs={{0,4},{1,5},{2,6},{3,7},{4,0},{5,1},{6,2},{7,3},{8,12},{9,13},{10,... | collective-permute-start | bytes 503816 | tf_op jit(solution)/shard_map/ppermute | solution.py:407
  14.5 1.9 %collective-permute-start = (f32[328,128]{1,0:T(8,128)S(1)}, f32[328,128]{1,0:T(8,128)S(1)}, u32[]{:S(2)}, u32[]{:S(2)}) collective-permute-start(f32[328,128]{1,0:T(8,128)S(1)} %shard_map.86.rest_0_), channel_id=1, source_target_pairs={{0,1},{1,0},{2,3},{3,2},{4,5},{5,4},{6,7},{7,6},{8,9},{9,8},{10,11... | collective-permute-start | bytes 503816 | tf_op jit(solution)/shard_map/ppermute | solution.py:407
  16.9 1.2 collective-permute-start.13
  18.5 0.9 copy-done.1
  19.4 4.9 %shard_map.87 = (f32[16,64,128]{2,1,0:T(8,128)S(1)}, f32[328,128]{1,0:T(8,128)S(1)}) custom-call(bf16[40,2,15,32,128]{4,3,2,1,0:T(8,128)(2,1)} %model_hbm.11, s32[15,32,128]{2,1,0:T(8,128)S(1)} %copy-done.1, f32[328,128]{1,0:T(8,128)S(1)} %collective-permute-done.5.unused_in), custom_call_target="tpu_custom_call", output_to_operand_aliasing={{1}: (2, {})} | custom-call | bytes 73800000 | tf_op jit(solution)/shard_map/pallas_call | solution.py:444
  24.4 3.4 %collective-permute-start.12 = (f32[328,128]{1,0:T(8,128)S(1)}, f32[328,128]{1,0:T(8,128)S(1)}, u32[]{:S(2)}, u32[]{:S(2)}) collective-permute-start(f32[328,128]{1,0:T(8,128)S(1)} %collective-permute-done.7.rest_12_), channel_id=1, source_target_pairs={{0,1},{1,0},{2,3},{3,2},{4,5},{5,4},{6,7},{7,6},{8,9},{9,8},{10,11... | collective-permute-start | bytes 503816 | tf_op jit(solution)/shard_map/ppermute | solution.py:407
  30.1 12.0 %shard_map.89 = f32[16,120,128]{2,1,0:T(8,128)} custom-call(s32[1]{0:T(128)} %bitcast.me_ref, s32[15]{0:T(128)S(1)} %copy-done.20, s32[15]{0:T(128)S(1)} %copy-done.22, bf16[40,2,15,32,128]{4,3,2,1,0:T(8,128)(2,1)} %model_hbm.11, f32[2,15,32,128]{3,2,1,0:T(8,128)S(1)} %copy-done, s32[15,32,128]{2,1,0:T(8,128)S(1)} %copy-done.2, ...), custom_call_target="tpu_custom_call" | custom-call | bytes 33210000 | tf_op jit(solution)/shard_map/pallas_call | solution.py:444
  42.1 5.6 %all-to-all-start = ((f32[16,120,128]{2,1,0:T(8,128)}), f32[16,120,128]{2,1,0:T(8,128)S(1)}, u32[]{:S(2)}, u32[]{:S(2)}) async-start(f32[16,120,128]{2,1,0:T(8,128)} %shard_map.89), calls=%async_computation | async-start | bytes 1966080 | tf_op jit(solution)/shard_map/all_to_all | solution.py:402
  48.6 0.9 copy-done.10
  49.6 0.9 copy-done.12
  50.5 0.9 copy-done.14
  52.3 2.1 %shard_map.88 = (f32[328,128]{1,0:T(8,128)S(1)}, bf16[64,512]{1,0:T(8,128)(2,1)S(1)}, f32[512,640]{1,0:T(8,128)S(1)}) custom-call(s32[1]{0:T(128)} %bitcast.me_ref, f32[328,128]{1,0:T(8,128)S(1)} %shard_map.86.rest_0_, f32[328,128]{1,0:T(8,128)S(1)} %collective-permute-done.rest_1_, f32[328,128]{1,0:T(8,128)S(1)} %collective-permute-done.1.rest_2_, ...), custom_call_target="tpu_custom_call" | custom-call | bytes 7380000 | tf_op jit(solution)/shard_map/pallas_call | solution.py:444
  54.4 1.1 copy-done.3
  56.1 15.1 %all-to-all-done.sums = f32[16,120,128]{2,1,0:T(8,128)S(1)} async-done(((f32[16,120,128]{2,1,0:T(8,128)}), f32[16,120,128]{2,1,0:T(8,128)S(1)}, u32[]{:S(2)}, u32[]{:S(2)}) %all-to-all-start) | async-done | bytes 983072 | tf_op jit(solution)/shard_map/all_to_all | solution.py:402
  71.2 1.3 copy-done.4
  72.5 0.9 copy-done.18
  73.5 1.6 shard_map.90.g_ref.rest_0_.g_in
  75.1 1.0 collective-permute-start.21
  76.1 1.6 collective-permute-start.18
  77.7 1.1 collective-permute-start.17
  78.7 2.5 %collective-permute-done.15.rest_4_ = f32[328,128]{1,0:T(8,128)S(1)} collective-permute-done((f32[328,128]{1,0:T(8,128)S(1)}, f32[328,128]{1,0:T(8,128)S(1)}, u32[]{:S(2)}, u32[]{:S(2)}) %collective-permute-start.15) | collective-permute-done | bytes 167968 | tf_op jit(solution)/shard_map/ppermute | solution.py:407
  81.9 3.5 %collective-permute-start.24 = (f32[328,128]{1,0:T(8,128)S(1)}, f32[328,128]{1,0:T(8,128)S(1)}, u32[]{:S(2)}, u32[]{:S(2)}) collective-permute-start(f32[328,128]{1,0:T(8,128)S(1)} %collective-permute-done.21.rest_6_), channel_id=1, source_target_pairs={{0,4},{1,5},{2,6},{3,7},{4,0},{5,1},{6,2},{7,3},{8,12},{9,13},{10,... | collective-permute-start | bytes 503816 | tf_op jit(solution)/shard_map/ppermute | solution.py:407
  85.5 2.1 %collective-permute-start.20 = (f32[328,128]{1,0:T(8,128)S(1)}, f32[328,128]{1,0:T(8,128)S(1)}, u32[]{:S(2)}, u32[]{:S(2)}) collective-permute-start(f32[328,128]{1,0:T(8,128)S(1)} %collective-permute-done.15.rest_4_), channel_id=1, source_target_pairs={{0,1},{1,0},{2,3},{3,2},{4,5},{5,4},{6,7},{7,6},{8,9},{9,8},{10,11... | collective-permute-start | bytes 503816 | tf_op jit(solution)/shard_map/ppermute | solution.py:407
  88.3 1.2 collective-permute-start.26
  89.5 4.2 %shard_map.92 = (f32[2,15,32,128]{3,2,1,0:T(8,128)S(1)}, f32[16,32,128]{2,1,0:T(8,128)S(1)}, f32[16,32,128]{2,1,0:T(8,128)S(1)}, f32[328,128]{1,0:T(8,128)S(1)}) custom-call(s32[1]{0:T(128)} %bitcast.me_ref, s32[15]{0:T(128)S(1)} %copy-done.20, s32[15]{0:T(128)S(1)} %copy-done.22, ...), custom_call_target="tpu_custom_call", output_to_operand_aliasing={{3}: (5, {})} | custom-call | bytes 73800000 | tf_op jit(solution)/shard_map/pallas_call | solution.py:444
  93.7 2.8 %collective-permute-start.23 = (f32[328,128]{1,0:T(8,128)S(1)}, f32[328,128]{1,0:T(8,128)S(1)}, u32[]{:S(2)}, u32[]{:S(2)}) collective-permute-start(f32[328,128]{1,0:T(8,128)S(1)} %get-tuple-element.27.rest_0_), channel_id=1, source_target_pairs={{0,1},{1,0},{2,3},{3,2},{4,5},{5,4},{6,7},{7,6},{8,9},{9,8},{10,11... | collective-permute-start | bytes 503816 | tf_op jit(solution)/shard_map/ppermute | solution.py:407
  98.4 1.0 collective-permute-done.27.rest_5_
  99.4 9.5 %shard_map.93 = f32[16,80,128]{2,1,0:T(8,128)} custom-call(s32[1]{0:T(128)} %bitcast.me_ref, s32[15]{0:T(128)S(1)} %copy-done.20, s32[15]{0:T(128)S(1)} %copy-done.22, bf16[40,2,15,32,128]{4,3,2,1,0:T(8,128)(2,1)} %model_hbm.11, s32[15,32,128]{2,1,0:T(8,128)S(1)} %copy-done.2, f32[16,64,128]{2,1,0:T(8,128)S(1)} %get-tuple-element.21.power_ref, ...), custom_call_target="tpu_custom_call" | custom-call | bytes 25830000 | tf_op jit(solution)/shard_map/pallas_call | solution.py:444
  108.9 4.8 %all-to-all-start.1 = ((f32[16,80,128]{2,1,0:T(8,128)}), f32[16,80,128]{2,1,0:T(8,128)S(1)}, u32[]{:S(2)}, u32[]{:S(2)}) async-start(f32[16,80,128]{2,1,0:T(8,128)} %shard_map.93), calls=%async_computation.1 | async-start | bytes 1310720 | tf_op jit(solution)/shard_map/all_to_all | solution.py:402
  113.6 1.4 shard_map.91
  115.1 1.1 copy-done.5
  116.2 14.4 %all-to-all-done.1.sums = f32[16,80,128]{2,1,0:T(8,128)S(1)} async-done(((f32[16,80,128]{2,1,0:T(8,128)}), f32[16,80,128]{2,1,0:T(8,128)S(1)}, u32[]{:S(2)}, u32[]{:S(2)}) %all-to-all-start.1) | async-done | bytes 655392 | tf_op jit(solution)/shard_map/all_to_all | solution.py:402
  130.5 1.3 copy-done.6
  131.8 1.0 shard_map.94.rest_0_.rest_8_
  133.4 1.6 %collective-permute-start.33 = (f32[328,128]{1,0:T(8,128)S(1)}, f32[328,128]{1,0:T(8,128)S(1)}, u32[]{:S(2)}, u32[]{:S(2)}) collective-permute-start(f32[328,128]{1,0:T(8,128)S(1)} %shard_map.94.rest_0_.rest_8_), channel_id=1, source_target_pairs={{0,2},{1,3},{2,0},{3,1},{4,6},{5,7},{6,4},{7,5},{8,10},{9,11},{10,... | collective-permute-start | bytes 503816 | tf_op jit(solution)/shard_map/ppermute | solution.py:407
  135.1 1.1 collective-permute-start.32
  136.1 2.8 %collective-permute-done.30.rest_4_.rest_12_ = f32[328,128]{1,0:T(8,128)S(1)} collective-permute-done((f32[328,128]{1,0:T(8,128)S(1)}, f32[328,128]{1,0:T(8,128)S(1)}, u32[]{:S(2)}, u32[]{:S(2)}) %collective-permute-start.30) | collective-permute-done | bytes 167968 | tf_op jit(solution)/shard_map/ppermute | solution.py:407
  140.0 2.4 %collective-permute-start.39 = (f32[328,128]{1,0:T(8,128)S(1)}, f32[328,128]{1,0:T(8,128)S(1)}, u32[]{:S(2)}, u32[]{:S(2)}) collective-permute-start(f32[328,128]{1,0:T(8,128)S(1)} %collective-permute-done.36.rest_6_.rest_14_), channel_id=1, source_target_pairs={{0,4},{1,5},{2,6},{3,7},{4,0},{5,1},{6,2},{7,3},{8,12},{9,13},{10,... | collective-permute-start | bytes 503816 | tf_op jit(solution)/shard_map/ppermute | solution.py:407
  142.4 2.2 %collective-permute-start.35 = (f32[328,128]{1,0:T(8,128)S(1)}, f32[328,128]{1,0:T(8,128)S(1)}, u32[]{:S(2)}, u32[]{:S(2)}) collective-permute-start(f32[328,128]{1,0:T(8,128)S(1)} %collective-permute-done.30.rest_4_.rest_12_), channel_id=1, source_target_pairs={{0,1},{1,0},{2,3},{3,2},{4,5},{5,4},{6,7},{7,6},{8,9},{9,8},{10,11... | collective-permute-start | bytes 503816 | tf_op jit(solution)/shard_map/ppermute | solution.py:407
  145.7 1.0 collective-permute-start.41
  146.7 4.7 %shard_map.95 = (f32[2,15,32,128]{3,2,1,0:T(8,128)S(1)}, f32[16,32,128]{2,1,0:T(8,128)}, f32[16,32,128]{2,1,0:T(8,128)}, f32[328,128]{1,0:T(8,128)S(1)}) custom-call(s32[1]{0:T(128)} %bitcast.me_ref, s32[15]{0:T(128)S(1)} %copy-done.20, s32[15]{0:T(128)S(1)} %copy-done.22, bf16[40,2,15,32,128]{4,3,2,1,0:T(8,128)(2,1)} %model_hbm.11, ...), custom_call_target="tpu_custom_call", output_to_operand_aliasing={{3}: (5, {})} | custom-call | bytes 73800000 | tf_op jit(solution)/shard_map/pallas_call | solution.py:444
  151.5 3.0 %collective-permute-start.38 = (f32[328,128]{1,0:T(8,128)S(1)}, f32[328,128]{1,0:T(8,128)S(1)}, u32[]{:S(2)}, u32[]{:S(2)}) collective-permute-start(f32[328,128]{1,0:T(8,128)S(1)} %get-tuple-element.29.rest_0_), channel_id=1, source_target_pairs={{0,1},{1,0},{2,3},{3,2},{4,5},{5,4},{6,7},{7,6},{8,9},{9,8},{10,11... | collective-permute-start | bytes 503816 | tf_op jit(solution)/shard_map/ppermute | solution.py:407
  156.5 4.8 %shard_map.96 = (f32[2,15,32,128]{3,2,1,0:T(8,128)}, f32[2,160,128]{2,1,0:T(8,128)}) custom-call(s32[1]{0:T(128)} %bitcast.me_ref, s32[15]{0:T(128)S(1)} %copy-done.20, s32[15]{0:T(128)S(1)} %copy-done.22, bf16[40,2,15,32,128]{4,3,2,1,0:T(8,128)(2,1)} %model_hbm.11, s32[15,32,128]{2,1,0:T(8,128)S(1)} %copy-done.2, ...), custom_call_target="tpu_custom_call" | custom-call | bytes 14760000 | tf_op jit(solution)/shard_map/pallas_call | solution.py:444
  (103 shorter events, 15.3 us)
Async XLA Ops:
  1.9 28.1 %copy-start.22 = (s32[15]{0:T(128)S(1)}, s32[15]{0:T(128)}, u32[]{:S(2)}) copy-start(s32[15]{0:T(128)} %second_ref.11) | copy-start | bytes 184
  3.5 5.2 %collective-permute-start.3 = (f32[328,128]{1,0:T(8,128)S(1)}, f32[328,128]{1,0:T(8,128)S(1)}, u32[]{:S(2)}, u32[]{:S(2)}) collective-permute-start(f32[328,128]{1,0:T(8,128)S(1)} %shard_map.86.rest_0_), channel_id=1, source_target_pairs={{0,4},{1,5},{2,6},{3,7},{4,0},{5,1},{6,2},{7,3},{8,12},{9,13},{10,... | collective-permute-start | bytes 503816 | tf_op jit(solution)/shard_map/ppermute | solution.py:407
  3.5 6.4 %collective-permute-start.7 = (f32[328,128]{1,0:T(8,128)S(1)}, f32[328,128]{1,0:T(8,128)S(1)}, u32[]{:S(2)}, u32[]{:S(2)}) collective-permute-start(f32[328,128]{1,0:T(8,128)S(1)} %shard_map.86.rest_0_), channel_id=1, source_target_pairs={{0,12},{1,13},{2,14},{3,15},{4,8},{5,9},{6,10},{7,11},{8,4},{9,5},... | collective-permute-start | bytes 503816 | tf_op jit(solution)/shard_map/ppermute | solution.py:407
  6.1 10.3 %collective-permute-start.1 = (f32[328,128]{1,0:T(8,128)S(1)}, f32[328,128]{1,0:T(8,128)S(1)}, u32[]{:S(2)}, u32[]{:S(2)}) collective-permute-start(f32[328,128]{1,0:T(8,128)S(1)} %shard_map.86.rest_0_), channel_id=1, source_target_pairs={{0,2},{1,3},{2,0},{3,1},{4,6},{5,7},{6,4},{7,5},{8,10},{9,11},{10,... | collective-permute-start | bytes 503816 | tf_op jit(solution)/shard_map/ppermute | solution.py:407
  8.7 8.2 %collective-permute-start.5 = (f32[328,128]{1,0:T(8,128)S(1)}, f32[328,128]{1,0:T(8,128)S(1)}, u32[]{:S(2)}, u32[]{:S(2)}) collective-permute-start(f32[328,128]{1,0:T(8,128)S(1)} %collective-permute-done.3.rest_4_), channel_id=1, source_target_pairs={{0,2},{1,3},{2,0},{3,1},{4,6},{5,7},{6,4},{7,5},{8,10},{9,11},{10,... | collective-permute-start | bytes 503816 | tf_op jit(solution)/shard_map/ppermute | solution.py:407
  9.9 8.2 %collective-permute-start.8 = (f32[328,128]{1,0:T(8,128)S(1)}, f32[328,128]{1,0:T(8,128)S(1)}, u32[]{:S(2)}, u32[]{:S(2)}) collective-permute-start(f32[328,128]{1,0:T(8,128)S(1)} %collective-permute-done.7.rest_12_), channel_id=1, source_target_pairs={{0,4},{1,5},{2,6},{3,7},{4,0},{5,1},{6,2},{7,3},{8,12},{9,13},{10,... | collective-permute-start | bytes 503816 | tf_op jit(solution)/shard_map/ppermute | solution.py:407
  14.5 9.8 %collective-permute-start = (f32[328,128]{1,0:T(8,128)S(1)}, f32[328,128]{1,0:T(8,128)S(1)}, u32[]{:S(2)}, u32[]{:S(2)}) collective-permute-start(f32[328,128]{1,0:T(8,128)S(1)} %shard_map.86.rest_0_), channel_id=1, source_target_pairs={{0,1},{1,0},{2,3},{3,2},{4,5},{5,4},{6,7},{7,6},{8,9},{9,8},{10,11... | collective-permute-start | bytes 503816 | tf_op jit(solution)/shard_map/ppermute | solution.py:407
  16.4 11.4 %collective-permute-start.2 = (f32[328,128]{1,0:T(8,128)S(1)}, f32[328,128]{1,0:T(8,128)S(1)}, u32[]{:S(2)}, u32[]{:S(2)}) collective-permute-start(f32[328,128]{1,0:T(8,128)S(1)} %collective-permute-done.1.rest_2_), channel_id=1, source_target_pairs={{0,1},{1,0},{2,3},{3,2},{4,5},{5,4},{6,7},{7,6},{8,9},{9,8},{10,11... | collective-permute-start | bytes 503816 | tf_op jit(solution)/shard_map/ppermute | solution.py:407
  16.4 11.5 %collective-permute-start.4 = (f32[328,128]{1,0:T(8,128)S(1)}, f32[328,128]{1,0:T(8,128)S(1)}, u32[]{:S(2)}, u32[]{:S(2)}) collective-permute-start(f32[328,128]{1,0:T(8,128)S(1)} %collective-permute-done.3.rest_4_), channel_id=1, source_target_pairs={{0,1},{1,0},{2,3},{3,2},{4,5},{5,4},{6,7},{7,6},{8,9},{9,8},{10,11... | collective-permute-start | bytes 503816 | tf_op jit(solution)/shard_map/ppermute | solution.py:407
  16.9 11.4 %collective-permute-start.13 = (f32[328,128]{1,0:T(8,128)S(1)}, f32[328,128]{1,0:T(8,128)S(1)}, u32[]{:S(2)}, u32[]{:S(2)}) collective-permute-start(f32[328,128]{1,0:T(8,128)S(1)} %collective-permute-done.7.rest_12_), channel_id=1, source_target_pairs={{0,2},{1,3},{2,0},{3,1},{4,6},{5,7},{6,4},{7,5},{8,10},{9,11},{10,... | collective-permute-start | bytes 503816 | tf_op jit(solution)/shard_map/ppermute | solution.py:407
  18.1 10.2 %collective-permute-start.10 = (f32[328,128]{1,0:T(8,128)S(1)}, f32[328,128]{1,0:T(8,128)S(1)}, u32[]{:S(2)}, u32[]{:S(2)}) collective-permute-start(f32[328,128]{1,0:T(8,128)S(1)} %collective-permute-done.8.rest_8_), channel_id=1, source_target_pairs={{0,2},{1,3},{2,0},{3,1},{4,6},{5,7},{6,4},{7,5},{8,10},{9,11},{10,... | collective-permute-start | bytes 503816 | tf_op jit(solution)/shard_map/ppermute | solution.py:407
  24.4 4.4 %collective-permute-start.12 = (f32[328,128]{1,0:T(8,128)S(1)}, f32[328,128]{1,0:T(8,128)S(1)}, u32[]{:S(2)}, u32[]{:S(2)}) collective-permute-start(f32[328,128]{1,0:T(8,128)S(1)} %collective-permute-done.7.rest_12_), channel_id=1, source_target_pairs={{0,1},{1,0},{2,3},{3,2},{4,5},{5,4},{6,7},{7,6},{8,9},{9,8},{10,11... | collective-permute-start | bytes 503816 | tf_op jit(solution)/shard_map/ppermute | solution.py:407
  27.8 1.5 collective-permute-start.6
  27.9 1.7 %collective-permute-start.9 = (f32[328,128]{1,0:T(8,128)S(1)}, f32[328,128]{1,0:T(8,128)}, u32[]{:S(2)}, u32[]{:S(2)}) collective-permute-start(f32[328,128]{1,0:T(8,128)S(1)} %collective-permute-done.8.rest_8_), channel_id=1, source_target_pairs={{0,1},{1,0},{2,3},{3,2},{4,5},{5,4},{6,7},{7,6},{8,9},{9,8},{10,11... | collective-permute-start | bytes 503816 | tf_op jit(solution)/shard_map/ppermute | solution.py:407
  28.3 1.5 collective-permute-start.14
  28.4 1.7 %collective-permute-start.11 = (f32[328,128]{1,0:T(8,128)S(1)}, f32[328,128]{1,0:T(8,128)}, u32[]{:S(2)}, u32[]{:S(2)}) collective-permute-start(f32[328,128]{1,0:T(8,128)S(1)} %collective-permute-done.10.rest_10_), channel_id=1, source_target_pairs={{0,1},{1,0},{2,3},{3,2},{4,5},{5,4},{6,7},{7,6},{8,9},{9,8},{10,11... | collective-permute-start | bytes 503816 | tf_op jit(solution)/shard_map/ppermute | solution.py:407
  42.1 29.1 %all-to-all-start = ((f32[16,120,128]{2,1,0:T(8,128)}), f32[16,120,128]{2,1,0:T(8,128)S(1)}, u32[]{:S(2)}, u32[]{:S(2)}) async-start(f32[16,120,128]{2,1,0:T(8,128)} %shard_map.89), calls=%async_computation | async-start | bytes 1966080 | tf_op jit(solution)/shard_map/all_to_all | solution.py:402
  75.0 6.2 %collective-permute-start.15 = (f32[328,128]{1,0:T(8,128)S(1)}, f32[328,128]{1,0:T(8,128)S(1)}, u32[]{:S(2)}, u32[]{:S(2)}) collective-permute-start(f32[328,128]{1,0:T(8,128)S(1)} %shard_map.90.g_ref.rest_0_.g_in), channel_id=1, source_target_pairs={{0,4},{1,5},{2,6},{3,7},{4,0},{5,1},{6,2},{7,3},{8,12},{9,13},{10,... | collective-permute-start | bytes 503816 | tf_op jit(solution)/shard_map/ppermute | solution.py:407
  75.1 6.8 %collective-permute-start.21 = (f32[328,128]{1,0:T(8,128)S(1)}, f32[328,128]{1,0:T(8,128)S(1)}, u32[]{:S(2)}, u32[]{:S(2)}) collective-permute-start(f32[328,128]{1,0:T(8,128)S(1)} %shard_map.90.g_ref.rest_0_.g_in), channel_id=1, source_target_pairs={{0,12},{1,13},{2,14},{3,15},{4,8},{5,9},{6,10},{7,11},{8,4},{9,5},... | collective-permute-start | bytes 503816 | tf_op jit(solution)/shard_map/ppermute | solution.py:407
  76.1 11.4 %collective-permute-start.18 = (f32[328,128]{1,0:T(8,128)S(1)}, f32[328,128]{1,0:T(8,128)S(1)}, u32[]{:S(2)}, u32[]{:S(2)}) collective-permute-start(f32[328,128]{1,0:T(8,128)S(1)} %shard_map.90.g_ref.rest_0_.g_in), channel_id=1, source_target_pairs={{0,2},{1,3},{2,0},{3,1},{4,6},{5,7},{6,4},{7,5},{8,10},{9,11},{10,... | collective-permute-start | bytes 503816 | tf_op jit(solution)/shard_map/ppermute | solution.py:407
  77.7 9.8 %collective-permute-start.17 = (f32[328,128]{1,0:T(8,128)S(1)}, f32[328,128]{1,0:T(8,128)S(1)}, u32[]{:S(2)}, u32[]{:S(2)}) collective-permute-start(f32[328,128]{1,0:T(8,128)S(1)} %shard_map.90.g_ref.rest_0_.g_in), channel_id=1, source_target_pairs={{0,1},{1,0},{2,3},{3,2},{4,5},{5,4},{6,7},{7,6},{8,9},{9,8},{10,11... | collective-permute-start | bytes 503816 | tf_op jit(solution)/shard_map/ppermute | solution.py:407
  81.2 6.8 %collective-permute-start.16 = (f32[328,128]{1,0:T(8,128)S(1)}, f32[328,128]{1,0:T(8,128)S(1)}, u32[]{:S(2)}, u32[]{:S(2)}) collective-permute-start(f32[328,128]{1,0:T(8,128)S(1)} %collective-permute-done.15.rest_4_), channel_id=1, source_target_pairs={{0,2},{1,3},{2,0},{3,1},{4,6},{5,7},{6,4},{7,5},{8,10},{9,11},{10,... | collective-permute-start | bytes 503816 | tf_op jit(solution)/shard_map/ppermute | solution.py:407
  81.9 6.4 %collective-permute-start.24 = (f32[328,128]{1,0:T(8,128)S(1)}, f32[328,128]{1,0:T(8,128)S(1)}, u32[]{:S(2)}, u32[]{:S(2)}) collective-permute-start(f32[328,128]{1,0:T(8,128)S(1)} %collective-permute-done.21.rest_6_), channel_id=1, source_target_pairs={{0,4},{1,5},{2,6},{3,7},{4,0},{5,1},{6,2},{7,3},{8,12},{9,13},{10,... | collective-permute-start | bytes 503816 | tf_op jit(solution)/shard_map/ppermute | solution.py:407
  85.5 4.1 %collective-permute-start.20 = (f32[328,128]{1,0:T(8,128)S(1)}, f32[328,128]{1,0:T(8,128)S(1)}, u32[]{:S(2)}, u32[]{:S(2)}) collective-permute-start(f32[328,128]{1,0:T(8,128)S(1)} %collective-permute-done.15.rest_4_), channel_id=1, source_target_pairs={{0,1},{1,0},{2,3},{3,2},{4,5},{5,4},{6,7},{7,6},{8,9},{9,8},{10,11... | collective-permute-start | bytes 503816 | tf_op jit(solution)/shard_map/ppermute | solution.py:407
  87.5 2.0 %collective-permute-start.19 = (f32[328,128]{1,0:T(8,128)S(1)}, f32[328,128]{1,0:T(8,128)S(1)}, u32[]{:S(2)}, u32[]{:S(2)}) collective-permute-start(f32[328,128]{1,0:T(8,128)S(1)} %collective-permute-done.18.rest_2_), channel_id=1, source_target_pairs={{0,1},{1,0},{2,3},{3,2},{4,5},{5,4},{6,7},{7,6},{8,9},{9,8},{10,11... | collective-permute-start | bytes 503816 | tf_op jit(solution)/shard_map/ppermute | solution.py:407
  87.5 2.0 %collective-permute-start.22 = (f32[328,128]{1,0:T(8,128)S(1)}, f32[328,128]{1,0:T(8,128)S(1)}, u32[]{:S(2)}, u32[]{:S(2)}) collective-permute-start(f32[328,128]{1,0:T(8,128)S(1)} %collective-permute-done.21.rest_6_), channel_id=1, source_target_pairs={{0,1},{1,0},{2,3},{3,2},{4,5},{5,4},{6,7},{7,6},{8,9},{9,8},{10,11... | collective-permute-start | bytes 503816 | tf_op jit(solution)/shard_map/ppermute | solution.py:407
  88.0 8.5 %collective-permute-start.28 = (f32[328,128]{1,0:T(8,128)S(1)}, f32[328,128]{1,0:T(8,128)S(1)}, u32[]{:S(2)}, u32[]{:S(2)}) collective-permute-start(f32[328,128]{1,0:T(8,128)S(1)} %collective-permute-done.21.rest_6_), channel_id=1, source_target_pairs={{0,2},{1,3},{2,0},{3,1},{4,6},{5,7},{6,4},{7,5},{8,10},{9,11},{10,... | collective-permute-start | bytes 503816 | tf_op jit(solution)/shard_map/ppermute | solution.py:407
  88.3 9.1 %collective-permute-start.26 = (f32[328,128]{1,0:T(8,128)S(1)}, f32[328,128]{1,0:T(8,128)S(1)}, u32[]{:S(2)}, u32[]{:S(2)}) collective-permute-start(f32[328,128]{1,0:T(8,128)S(1)} %collective-permute-done.24.rest_2_), channel_id=1, source_target_pairs={{0,2},{1,3},{2,0},{3,1},{4,6},{5,7},{6,4},{7,5},{8,10},{9,11},{10,... | collective-permute-start | bytes 503816 | tf_op jit(solution)/shard_map/ppermute | solution.py:407
  93.7 4.7 %collective-permute-start.23 = (f32[328,128]{1,0:T(8,128)S(1)}, f32[328,128]{1,0:T(8,128)S(1)}, u32[]{:S(2)}, u32[]{:S(2)}) collective-permute-start(f32[328,128]{1,0:T(8,128)S(1)} %get-tuple-element.27.rest_0_), channel_id=1, source_target_pairs={{0,1},{1,0},{2,3},{3,2},{4,5},{5,4},{6,7},{7,6},{8,9},{9,8},{10,11... | collective-permute-start | bytes 503816 | tf_op jit(solution)/shard_map/ppermute | solution.py:407
  96.5 1.9 %collective-permute-start.25 = (f32[328,128]{1,0:T(8,128)S(1)}, f32[328,128]{1,0:T(8,128)S(1)}, u32[]{:S(2)}, u32[]{:S(2)}) collective-permute-start(f32[328,128]{1,0:T(8,128)S(1)} %collective-permute-done.24.rest_2_), channel_id=1, source_target_pairs={{0,1},{1,0},{2,3},{3,2},{4,5},{5,4},{6,7},{7,6},{8,9},{9,8},{10,11... | collective-permute-start | bytes 503816 | tf_op jit(solution)/shard_map/ppermute | solution.py:407
  96.6 1.8 %collective-permute-start.29 = (f32[328,128]{1,0:T(8,128)S(1)}, f32[328,128]{1,0:T(8,128)S(1)}, u32[]{:S(2)}, u32[]{:S(2)}) collective-permute-start(f32[328,128]{1,0:T(8,128)S(1)} %collective-permute-done.28.rest_6_), channel_id=1, source_target_pairs={{0,1},{1,0},{2,3},{3,2},{4,5},{5,4},{6,7},{7,6},{8,9},{9,8},{10,11... | collective-permute-start | bytes 503816 | tf_op jit(solution)/shard_map/ppermute | solution.py:407
  97.5 1.9 %collective-permute-start.27 = (f32[328,128]{1,0:T(8,128)S(1)}, f32[328,128]{1,0:T(8,128)S(1)}, u32[]{:S(2)}, u32[]{:S(2)}) collective-permute-start(f32[328,128]{1,0:T(8,128)S(1)} %collective-permute-done.26.rest_4_), channel_id=1, source_target_pairs={{0,1},{1,0},{2,3},{3,2},{4,5},{5,4},{6,7},{7,6},{8,9},{9,8},{10,11... | collective-permute-start | bytes 503816 | tf_op jit(solution)/shard_map/ppermute | solution.py:407
  108.9 21.7 %all-to-all-start.1 = ((f32[16,80,128]{2,1,0:T(8,128)}), f32[16,80,128]{2,1,0:T(8,128)S(1)}, u32[]{:S(2)}, u32[]{:S(2)}) async-start(f32[16,80,128]{2,1,0:T(8,128)} %shard_map.93), calls=%async_computation.1 | async-start | bytes 1310720 | tf_op jit(solution)/shard_map/all_to_all | solution.py:402
  132.8 6.1 %collective-permute-start.30 = (f32[328,128]{1,0:T(8,128)S(1)}, f32[328,128]{1,0:T(8,128)S(1)}, u32[]{:S(2)}, u32[]{:S(2)}) collective-permute-start(f32[328,128]{1,0:T(8,128)S(1)} %shard_map.94.rest_0_.rest_8_), channel_id=1, source_target_pairs={{0,4},{1,5},{2,6},{3,7},{4,0},{5,1},{6,2},{7,3},{8,12},{9,13},{10,... | collective-permute-start | bytes 503816 | tf_op jit(solution)/shard_map/ppermute | solution.py:407
  132.9 7.1 %collective-permute-start.36 = (f32[328,128]{1,0:T(8,128)S(1)}, f32[328,128]{1,0:T(8,128)S(1)}, u32[]{:S(2)}, u32[]{:S(2)}) collective-permute-start(f32[328,128]{1,0:T(8,128)S(1)} %shard_map.94.rest_0_.rest_8_), channel_id=1, source_target_pairs={{0,12},{1,13},{2,14},{3,15},{4,8},{5,9},{6,10},{7,11},{8,4},{9,5},... | collective-permute-start | bytes 503816 | tf_op jit(solution)/shard_map/ppermute | solution.py:407
  133.4 11.2 %collective-permute-start.33 = (f32[328,128]{1,0:T(8,128)S(1)}, f32[328,128]{1,0:T(8,128)S(1)}, u32[]{:S(2)}, u32[]{:S(2)}) collective-permute-start(f32[328,128]{1,0:T(8,128)S(1)} %shard_map.94.rest_0_.rest_8_), channel_id=1, source_target_pairs={{0,2},{1,3},{2,0},{3,1},{4,6},{5,7},{6,4},{7,5},{8,10},{9,11},{10,... | collective-permute-start | bytes 503816 | tf_op jit(solution)/shard_map/ppermute | solution.py:407
  135.1 9.6 %collective-permute-start.32 = (f32[328,128]{1,0:T(8,128)S(1)}, f32[328,128]{1,0:T(8,128)S(1)}, u32[]{:S(2)}, u32[]{:S(2)}) collective-permute-start(f32[328,128]{1,0:T(8,128)S(1)} %shard_map.94.rest_0_.rest_8_), channel_id=1, source_target_pairs={{0,1},{1,0},{2,3},{3,2},{4,5},{5,4},{6,7},{7,6},{8,9},{9,8},{10,11... | collective-permute-start | bytes 503816 | tf_op jit(solution)/shard_map/ppermute | solution.py:407
  138.9 6.2 %collective-permute-start.31 = (f32[328,128]{1,0:T(8,128)S(1)}, f32[328,128]{1,0:T(8,128)S(1)}, u32[]{:S(2)}, u32[]{:S(2)}) collective-permute-start(f32[328,128]{1,0:T(8,128)S(1)} %collective-permute-done.30.rest_4_.rest_12_), channel_id=1, source_target_pairs={{0,2},{1,3},{2,0},{3,1},{4,6},{5,7},{6,4},{7,5},{8,10},{9,11},{10,... | collective-permute-start | bytes 503816 | tf_op jit(solution)/shard_map/ppermute | solution.py:407
  140.0 5.7 %collective-permute-start.39 = (f32[328,128]{1,0:T(8,128)S(1)}, f32[328,128]{1,0:T(8,128)S(1)}, u32[]{:S(2)}, u32[]{:S(2)}) collective-permute-start(f32[328,128]{1,0:T(8,128)S(1)} %collective-permute-done.36.rest_6_.rest_14_), channel_id=1, source_target_pairs={{0,4},{1,5},{2,6},{3,7},{4,0},{5,1},{6,2},{7,3},{8,12},{9,13},{10,... | collective-permute-start | bytes 503816 | tf_op jit(solution)/shard_map/ppermute | solution.py:407
  142.4 4.4 %collective-permute-start.35 = (f32[328,128]{1,0:T(8,128)S(1)}, f32[328,128]{1,0:T(8,128)S(1)}, u32[]{:S(2)}, u32[]{:S(2)}) collective-permute-start(f32[328,128]{1,0:T(8,128)S(1)} %collective-permute-done.30.rest_4_.rest_12_), channel_id=1, source_target_pairs={{0,1},{1,0},{2,3},{3,2},{4,5},{5,4},{6,7},{7,6},{8,9},{9,8},{10,11... | collective-permute-start | bytes 503816 | tf_op jit(solution)/shard_map/ppermute | solution.py:407
  144.6 2.1 %collective-permute-start.34 = (f32[328,128]{1,0:T(8,128)S(1)}, f32[328,128]{1,0:T(8,128)S(1)}, u32[]{:S(2)}, u32[]{:S(2)}) collective-permute-start(f32[328,128]{1,0:T(8,128)S(1)} %collective-permute-done.33.rest_2_.rest_10_), channel_id=1, source_target_pairs={{0,1},{1,0},{2,3},{3,2},{4,5},{5,4},{6,7},{7,6},{8,9},{9,8},{10,11... | collective-permute-start | bytes 503816 | tf_op jit(solution)/shard_map/ppermute | solution.py:407
  144.6 2.1 %collective-permute-start.37 = (f32[328,128]{1,0:T(8,128)S(1)}, f32[328,128]{1,0:T(8,128)S(1)}, u32[]{:S(2)}, u32[]{:S(2)}) collective-permute-start(f32[328,128]{1,0:T(8,128)S(1)} %collective-permute-done.36.rest_6_.rest_14_), channel_id=1, source_target_pairs={{0,1},{1,0},{2,3},{3,2},{4,5},{5,4},{6,7},{7,6},{8,9},{9,8},{10,11... | collective-permute-start | bytes 503816 | tf_op jit(solution)/shard_map/ppermute | solution.py:407
  145.1 9.4 %collective-permute-start.43 = (f32[328,128]{1,0:T(8,128)S(1)}, f32[328,128]{1,0:T(8,128)S(1)}, u32[]{:S(2)}, u32[]{:S(2)}) collective-permute-start(f32[328,128]{1,0:T(8,128)S(1)} %collective-permute-done.36.rest_6_.rest_14_), channel_id=1, source_target_pairs={{0,2},{1,3},{2,0},{3,1},{4,6},{5,7},{6,4},{7,5},{8,10},{9,11},{10,... | collective-permute-start | bytes 503816 | tf_op jit(solution)/shard_map/ppermute | solution.py:407
  145.7 9.3 %collective-permute-start.41 = (f32[328,128]{1,0:T(8,128)S(1)}, f32[328,128]{1,0:T(8,128)S(1)}, u32[]{:S(2)}, u32[]{:S(2)}) collective-permute-start(f32[328,128]{1,0:T(8,128)S(1)} %collective-permute-done.39.rest_2_), channel_id=1, source_target_pairs={{0,2},{1,3},{2,0},{3,1},{4,6},{5,7},{6,4},{7,5},{8,10},{9,11},{10,... | collective-permute-start | bytes 503816 | tf_op jit(solution)/shard_map/ppermute | solution.py:407
  151.5 4.0 %collective-permute-start.38 = (f32[328,128]{1,0:T(8,128)S(1)}, f32[328,128]{1,0:T(8,128)S(1)}, u32[]{:S(2)}, u32[]{:S(2)}) collective-permute-start(f32[328,128]{1,0:T(8,128)S(1)} %get-tuple-element.29.rest_0_), channel_id=1, source_target_pairs={{0,1},{1,0},{2,3},{3,2},{4,5},{5,4},{6,7},{7,6},{8,9},{9,8},{10,11... | collective-permute-start | bytes 503816 | tf_op jit(solution)/shard_map/ppermute | solution.py:407
  154.4 1.4 collective-permute-start.40
  154.5 1.6 collective-permute-start.44
  155.0 1.5 collective-permute-start.42
  (22 other events, 165.4 us)

commit v6 on v5

--- a/solution.py
+++ b/solution.py
@@ -46,6 +46,7 @@
 
 
 TILE = 8
+PARTS = (1, 3, 7, ROWS)
 
 
 def pack_kernel(n, dpc, first_ref, second_ref, re_ref, im_ref, out_ref, sems):
@@ -69,11 +70,10 @@
 class Fetch:
     def __init__(self, model, held, sems, firsts=(0,)):
         count, pairs = held.shape[0] // len(firsts), held.shape[2]
-        parts = 3 if pairs % 3 == 0 else 1
-        self.size = pairs // parts
         self.copies = []
-        for i in range(parts):
-            part = pl.ds(i * self.size, self.size)
+        self.ends = [0] + [min(end, pairs) for end in PARTS]
+        for i in range(len(PARTS)):
+            part = pl.ds(self.ends[i], self.ends[i + 1] - self.ends[i])
             self.copies.append([])
             for j, first in enumerate(firsts):
                 self.copies[i].append(
@@ -91,7 +91,7 @@
         for i, copies in enumerate(self.copies):
             for copy in copies:
                 copy.wait()
-            lax.fori_loop(i * self.size, (i + 1) * self.size, body, 0)
+            lax.fori_loop(self.ends[i], self.ends[i + 1], body, 0)
 
 
 def power_kernel(n, dpc, model_hbm, mask_ref, unused_in, out_ref, unused_out, model_ref, sems):
@@ -103,8 +103,8 @@
         for d in range(SOURCE_COUNT):
             mr = model_ref[d, 0, b].astype(F32)
             mi = model_ref[d, 1, b].astype(F32)
-            row = d // dpc * TILE + d % dpc
-            out_ref[b, row : row + 1, :] = jnp.sum(weight * (mr * mr + mi * mi), axis=0, keepdims=True)
+            row = pl.ds(b * dpc + d % dpc, 1)
+            out_ref[d // dpc, row, :] = jnp.sum(weight * (mr * mr + mi * mi), axis=0, keepdims=True)
         return carry
 
     fetch.each(pair)
@@ -201,6 +201,13 @@
     put(g_out, 0.5 * (wide(g_in, dpc) + total / den_ref[...]), dpc)
 
 
+def clear(dpc, pairs, *refs):
+    for ref in refs:
+        chips, rows, _ = ref.shape
+        for m in range(chips):
+            ref[m, pairs * dpc :, :] = jnp.zeros((rows - pairs * dpc, 128), F32)
+
+
 def products_first(n, dpc, me, first_ref, second_ref, ins, hre, him, stack):
     per = STATIONS // n
     rows = per * SOURCE_COUNT
@@ -216,11 +223,12 @@
 
         for k in range(n // 2):
             pr, pi, qr, qi = block(p, k, 0), block(p, k, 1), block(q, k, 0), block(q, k, 1)
-            hre[b, k * TILE : (k + 1) * TILE, :] = pr * qr + pi * qi
-            him[b, k * TILE : (k + 1) * TILE, :] = pi * qr - pr * qi
+            hre[k, pl.ds(b * dpc, TILE), :] = pr * qr + pi * qi
+            him[k, pl.ds(b * dpc, TILE), :] = pi * qr - pr * qi
         return carry
 
     lax.fori_loop(0, first_ref.shape[0], pair, 0)
+    clear(dpc, first_ref.shape[0], hre, him)
 
 
 def piece_pair(dpc, even, ins, m, station):
@@ -237,11 +245,12 @@
         for m in range(len(ins) // 2):
             pr, pi = piece_pair(dpc, even, ins, m, p)
             qr, qi = piece_pair(dpc, even, ins, m, q)
-            hre[b, m * TILE : (m + 1) * TILE, :] = pr * qr + pi * qi
-            him[b, m * TILE : (m + 1) * TILE, :] = pi * qr - pr * qi
+            hre[m, pl.ds(b * dpc, TILE), :] = pr * qr + pi * qi
+            him[m, pl.ds(b * dpc, TILE), :] = pi * qr - pr * qi
         return carry
 
     lax.fori_loop(0, first_ref.shape[0], pair, 0)
+    clear(dpc, first_ref.shape[0], hre, him)
 
 
 def predict(dpc, b, acc, chips, model_ref, hre, him):
@@ -250,9 +259,8 @@
         for dd in range(dpc):
             mr = model_ref[k * dpc + dd, 0, b].astype(F32)
             mi = model_ref[k * dpc + dd, 1, b].astype(F32)
-            row = m * TILE + dd
-            hr = hre[b, row : row + 1, :]
-            hi = him[b, row : row + 1, :]
+            row = pl.ds(b * dpc + dd, 1)
+            hr, hi = hre[m, row, :], him[m, row, :]
             acc_re = acc_re - (hr * mr - hi * mi)
             acc_im = acc_im - (hr * mi + hi * mr)
     return acc_re, acc_im
@@ -269,31 +277,29 @@
         for dd in range(dpc):
             mr = model_ref[k * dpc + dd, 0, b].astype(F32)
             mi = model_ref[k * dpc + dd, 1, b].astype(F32)
-            row = m * TILE + dd
-            cre[b, row : row + 1, :] = jnp.sum(mr * res_re + mi * res_im, axis=0, keepdims=True)
-            cim[b, row : row + 1, :] = jnp.sum(mr * res_im - mi * res_re, axis=0, keepdims=True)
-
-
-def write_sums(dpc, pairs, chips, cre, cim, tiles, power_ref, out_ref, start):
+            row = pl.ds(b * dpc + dd, 1)
+            cre[m, row, :] = jnp.sum(mr * res_re + mi * res_im, axis=0, keepdims=True)
+            cim[m, row, :] = jnp.sum(mr * res_im - mi * res_re, axis=0, keepdims=True)
+
+
+def write_sums(dpc, chips, cre, cim, tiles, power_ref, out_ref, start):
     for m, k in enumerate(chips):
-        tile = slice(m * TILE, (m + 1) * TILE)
-        strong = pl.ds(k * TILE, TILE)
-        for b in range(pairs):
-            hr, hi = tiles(b, m)
-            w = power_ref[b, strong, :]
-            x0, x1 = cross(cre[b, tile, :] + hr * w, cim[b, tile, :] + hi * w)
-            out_ref[2 * k, b * dpc : (b + 1) * dpc, :] = x0[:dpc]
-            out_ref[2 * k + 1, b * dpc : (b + 1) * dpc, :] = x1[:dpc]
-        if pairs < ROWS:
-            empty = jnp.zeros(((ROWS - pairs) * dpc, 128), F32)
-            out_ref[2 * k, pairs * dpc : ROWS * dpc, :] = empty
-            out_ref[2 * k + 1, pairs * dpc : ROWS * dpc, :] = empty
+        re, im, at = tiles(m)
+        for t in range(ROWS * dpc // TILE):
+            rows = slice(t * TILE, (t + 1) * TILE)
+            w = power_ref[k, rows, :]
+            x0, x1 = cross(cre[m, rows, :] + re[at, rows, :] * w, cim[m, rows, :] + im[at, rows, :] * w)
+            out_ref[2 * k, rows, :] = x0
+            out_ref[2 * k + 1, rows, :] = x1
         if start:
-            for r in range(TILE):
-                x0, x1 = cross(power_ref[r, strong, :], power_ref[r + TILE, strong, :])
-                to = (ROWS + r) * dpc
-                out_ref[2 * k, to : to + dpc, :] = x0[:dpc]
-                out_ref[2 * k + 1, to : to + dpc, :] = x1[:dpc]
+            for t in range(dpc):
+                x0, x1 = cross(
+                    power_ref[k, t * TILE : (t + 1) * TILE, :],
+                    power_ref[k, (t + dpc) * TILE : (t + dpc + 1) * TILE, :],
+                )
+                rows = slice(ROWS * dpc + t * TILE, ROWS * dpc + (t + 1) * TILE)
+                out_ref[2 * k, rows, :] = x0
+                out_ref[2 * k + 1, rows, :] = x1
 
 
 def first_pass_kernel(
@@ -311,11 +317,8 @@
 
     fetch.each(pair)
 
-    def tiles(b, m):
-        tile = slice(m * TILE, (m + 1) * TILE)
-        return hre[b, tile, :], him[b, tile, :]
-
-    write_sums(dpc, mask_ref.shape[0], chips, cre, cim, tiles, power_ref, out_ref, True)
+    clear(dpc, mask_ref.shape[0], cre, cim)
+    write_sums(dpc, chips, cre, cim, lambda m: (hre, him, m), power_ref, out_ref, True)
 
 
 NEAR, FAR = (0, 1, 2, 6), (3, 4, 5, 7)
@@ -356,13 +359,11 @@
 
     fetch.each(pair)
 
-    def tiles(b, m):
-        re, im = (near_re, near_im) if m < len(NEAR) else (hre, him)
-        m = m % len(NEAR)
-        tile = slice(m * TILE, (m + 1) * TILE)
-        return re[b, tile, :], im[b, tile, :]
-
-    write_sums(dpc, mask_ref.shape[0], chips, cre, cim, tiles, power_ref, out_ref, False)
+    def tiles(m):
+        return (near_re, near_im, m) if m < len(NEAR) else (hre, him, m - len(NEAR))
+
+    clear(dpc, mask_ref.shape[0], cre, cim)
+    write_sums(dpc, chips, cre, cim, tiles, power_ref, out_ref, False)
 
 
 def last_kernel(n, dpc, me_ref, first_ref, second_ref, model_hbm, mask_ref, acc_ref, *rest):
@@ -402,7 +403,7 @@
     return lax.all_to_all(x, "bl", split_axis=0, concat_axis=0, tiled=True)
 
 
-def gather(n, piece, beside):
+def gather(n, piece, beside, at):
     def send(x, o):
         return lax.ppermute(x, "bl", [(i, i ^ o) for i in range(n)])
 
@@ -412,10 +413,9 @@
     got[6] = send(got[4], 2)
     got[8] = send(got[12], 4)
     got[14], got[10] = send(got[12], 2), send(got[8], 2)
-    for o in (0, 2, 4, 12):
-        got[o + 1] = send(got[o], 1)
-    got[6] = beside(got[6], got)
-    for o in (6, 14, 8, 10):
+    for o in (0, 2, 4, 12, 6, 14, 8, 10):
+        if o == at:
+            got[o] = beside(got[o], got)
         got[o + 1] = send(got[o], 1)
     return [got[o] for o in range(n)]
 
@@ -427,11 +427,11 @@
     pairs, times, channels = mask.shape
     me = lax.axis_index("bl").astype(jnp.int32).reshape(1)
     params = pltpu.CompilerParams(vmem_limit_bytes=VMEM_LIMIT)
-    plane = (ROWS, n // 2 * TILE, channels)
-    half = (ROWS, n // 4 * TILE, channels)
+    plane = (n // 2, ROWS * dpc + TILE, channels)
+    half = (n // 4, ROWS * dpc + TILE, channels)
     lots = n * 2 * ROWS
     mine = (STATIONS * dpc + TILE, channels)
-    sems = pltpu.SemaphoreType.DMA((3, n // 4))
+    sems = pltpu.SemaphoreType.DMA((len(PARTS), n // 4))
     held = [pltpu.VMEM(model.shape, BF16), sems]
     held_half = [pltpu.VMEM((SOURCE_COUNT // 2,) + model.shape[1:], BF16), sems]
 
@@ -469,7 +469,7 @@
         )
         return x
 
-    got = gather(n, piece, powers_beside)
+    got = gather(n, piece, powers_beside, 14)
     g, onehot, sel = call(
         first_own_kernel,
         (me, *got),
@@ -485,7 +485,12 @@
         micros=9,
     )
     powers = exchange(sums)
-    (g,) = call(own_kernel, (g, onehot, sel, powers), [shape(*mine)], [(lots, 2 * width)])
+    (g,) = call(
+        own_kernel,
+        (g, onehot, sel, powers),
+        [shape(*mine)],
+        [(lots, 2 * width)],
+    )
 
     def slots(got, pairs):
         return [got[2 * m + c] for m in pairs for c in (0, 1)]
@@ -500,7 +505,7 @@
             *near, x = call(early_kernel, args, outs, held_half, micros=20, aliases={5: 3})
             return x
 
-        got = gather(n, g, beside)
+        got = gather(n, g, beside, 14)
         return near, slots(got, NEAR), slots(got, FAR)
 
     for step in range(1, ITERS):
@@ -520,7 +525,12 @@
             micros=7,
         )
         sums = exchange(sums)
-        (g,) = call(later_own_kernel, (g, onehot, sel, den, sums), [shape(*mine)], [(lots, width)])
+        (g,) = call(
+            later_own_kernel,
+            (g, onehot, sel, den, sums),
+            [shape(*mine)],
+            [(lots, width)],
+        )
     near, near_slots, far_slots = gather_near(g)
     residual, gains = call(
         last_kernel,

time: 164 us -> 166 us (1.012); the launches traced: 161 us -> 165 us
  waiting for transfers between devices: 40.7 us -> 55.2 us
  starting transfers between devices: 58.8 us -> 48.9 us
    ppermute x45, waiting for transfers between devices: 11.3 us -> 25.7 us  [send(): return lax.ppermute(x, 'bl', [(i, i ^ o) for i in range(n)])]
    ppermute x45, starting transfers between devices: 48.5 us -> 38.9 us  [send(): return lax.ppermute(x, 'bl', [(i, i ^ o) for i in range(n)])]
  transfers between devices with their start and end apart: 47 -> 47, of which waited for: 15 -> 13; matrix products, arithmetic and copies ran while one was open for 0% -> 0% of each run, Pallas kernels for 11% -> 11%
where the time goes in v6:
time: 166 us; the launch traced here: 165 us
  waiting for transfers between devices  55.2 us (33%)
  starting transfers between devices  48.9 us (29%)
  Pallas kernels  47 us (28%)
  local copies, waits for them, and re-layouts  13.2 us (8%)
    pallas_call x11, Pallas kernels, call(): pl.pallas_call(functools.partial(kernel, n, dpc), in_specs=[place(x) for...  47 us
    ppermute x45, starting transfers between devices, send(): return lax.ppermute(x, 'bl', [(i, i ^ o) for i in range(n)])  38.9 us
    all_to_all x2, waiting for transfers between devices, exchange(): return lax.all_to_all(x, 'bl', split_axis=0, concat_axis=0, tiled=True)  29.5 us
    ppermute x45, waiting for transfers between devices, send(): return lax.ppermute(x, 'bl', [(i, i ^ o) for i in range(n)])  25.7 us
    unnamed x46, local copies, waits for them, and re-layouts  13.2 us
    all_to_all x2, starting transfers between devices, exchange(): return lax.all_to_all(x, 'bl', split_axis=0, concat_axis=0, tiled=True)  9.99 us
  transfers between devices with their start and end apart: 47, of which 13 were waited for; matrix products, arithmetic and copies ran while one was open for 0% of the time, Pallas kernels for 11%

profile of v6, /device:TPU:9, one launch (start us, length us, event | category | flops | bytes accessed | tf_op | source)
XLA Modules:
  0.0 165.4 jit_solution(4747123147316603383)
XLA Ops:
  1.9 1.5 shard_map.86.rest_0_
  3.5 1.4 collective-permute-start.7
  4.8 1.2 collective-permute-start.1
  6.0 2.2 %collective-permute-start.3 = (f32[328,128]{1,0:T(8,128)S(1)}, f32[328,128]{1,0:T(8,128)S(1)}, u32[]{:S(2)}, u32[]{:S(2)}) collective-permute-start(f32[328,128]{1,0:T(8,128)S(1)} %shard_map.86.rest_0_), channel_id=1, source_target_pairs={{0,4},{1,5},{2,6},{3,7},{4,0},{5,1},{6,2},{7,3},{8,12},{9,13},{10,... | collective-permute-start | bytes 503816 | tf_op jit(solution)/shard_map/ppermute | solution.py:408
  8.2 4.2 %collective-permute-done.7.rest_12_ = f32[328,128]{1,0:T(8,128)S(1)} collective-permute-done((f32[328,128]{1,0:T(8,128)S(1)}, f32[328,128]{1,0:T(8,128)S(1)}, u32[]{:S(2)}, u32[]{:S(2)}) %collective-permute-start.7) | collective-permute-done | bytes 167968 | tf_op jit(solution)/shard_map/ppermute | solution.py:408
  12.5 1.2 collective-permute-start.13
  13.7 1.6 collective-permute-start
  15.7 1.9 %collective-permute-done.8.rest_8_ = f32[328,128]{1,0:T(8,128)S(1)} collective-permute-done((f32[328,128]{1,0:T(8,128)S(1)}, f32[328,128]{1,0:T(8,128)S(1)}, u32[]{:S(2)}, u32[]{:S(2)}) %collective-permute-start.8) | collective-permute-done | bytes 167968 | tf_op jit(solution)/shard_map/ppermute | solution.py:408
  17.5 2.0 %collective-permute-start.4 = (f32[328,128]{1,0:T(8,128)S(1)}, f32[328,128]{1,0:T(8,128)S(1)}, u32[]{:S(2)}, u32[]{:S(2)}) collective-permute-start(f32[328,128]{1,0:T(8,128)S(1)} %collective-permute-done.3.rest_4_), channel_id=1, source_target_pairs={{0,1},{1,0},{2,3},{3,2},{4,5},{5,4},{6,7},{7,6},{8,9},{9,8},{10,11... | collective-permute-start | bytes 503816 | tf_op jit(solution)/shard_map/ppermute | solution.py:408
  19.5 1.2 collective-permute-start.10
  21.7 5.5 %shard_map.87 = (f32[8,88,128]{2,1,0:T(8,128)S(1)}, f32[328,128]{1,0:T(8,128)S(1)}) custom-call(bf16[40,2,15,32,128]{4,3,2,1,0:T(8,128)(2,1)} %model_hbm.11, s32[15,32,128]{2,1,0:T(8,128)S(1)} %copy-done.1, f32[328,128]{1,0:T(8,128)S(1)} %collective-permute-done.13.unused_in), custom_call_target="tpu_custom_call", output_to_operand_aliasing={{1}: (2, {})} | custom-call | bytes 73800000 | tf_op jit(solution)/shard_map/pallas_call | solution.py:444
  27.2 1.7 %collective-permute-start.12 = (f32[328,128]{1,0:T(8,128)S(1)}, f32[328,128]{1,0:T(8,128)S(1)}, u32[]{:S(2)}, u32[]{:S(2)}) collective-permute-start(f32[328,128]{1,0:T(8,128)S(1)} %collective-permute-done.7.rest_12_), channel_id=1, source_target_pairs={{0,1},{1,0},{2,3},{3,2},{4,5},{5,4},{6,7},{7,6},{8,9},{9,8},{10,11... | collective-permute-start | bytes 503816 | tf_op jit(solution)/shard_map/ppermute | solution.py:408
  31.2 11.0 %shard_map.89 = f32[16,120,128]{2,1,0:T(8,128)} custom-call(s32[1]{0:T(128)} %bitcast.me_ref, s32[15]{0:T(128)S(1)} %copy-done.20, s32[15]{0:T(128)S(1)} %copy-done.22, bf16[40,2,15,32,128]{4,3,2,1,0:T(8,128)(2,1)} %model_hbm.11, f32[2,15,32,128]{3,2,1,0:T(8,128)S(1)} %copy-done, s32[15,32,128]{2,1,0:T(8,128)S(1)} %copy-done.2, ...), custom_call_target="tpu_custom_call" | custom-call | bytes 33210000 | tf_op jit(solution)/shard_map/pallas_call | solution.py:444
  42.2 5.7 %all-to-all-start = ((f32[16,120,128]{2,1,0:T(8,128)}), f32[16,120,128]{2,1,0:T(8,128)S(1)}, u32[]{:S(2)}, u32[]{:S(2)}) async-start(f32[16,120,128]{2,1,0:T(8,128)} %shard_map.89), calls=%async_computation | async-start | bytes 1966080 | tf_op jit(solution)/shard_map/all_to_all | solution.py:403
  52.5 2.0 %shard_map.88 = (f32[328,128]{1,0:T(8,128)S(1)}, bf16[64,512]{1,0:T(8,128)(2,1)S(1)}, f32[512,640]{1,0:T(8,128)S(1)}) custom-call(s32[1]{0:T(128)} %bitcast.me_ref, f32[328,128]{1,0:T(8,128)S(1)} %shard_map.86.rest_0_, f32[328,128]{1,0:T(8,128)S(1)} %collective-permute-done.rest_1_, f32[328,128]{1,0:T(8,128)S(1)} %collective-permute-done.1.rest_2_, ...), custom_call_target="tpu_custom_call" | custom-call | bytes 7380000 | tf_op jit(solution)/shard_map/pallas_call | solution.py:444
  54.5 1.1 copy-done.3
  56.3 15.2 %all-to-all-done.sums = f32[16,120,128]{2,1,0:T(8,128)S(1)} async-done(((f32[16,120,128]{2,1,0:T(8,128)}), f32[16,120,128]{2,1,0:T(8,128)S(1)}, u32[]{:S(2)}, u32[]{:S(2)}) %all-to-all-start) | async-done | bytes 983072 | tf_op jit(solution)/shard_map/all_to_all | solution.py:403
  71.5 1.3 copy-done.4
  73.7 1.6 shard_map.90.g_ref.rest_0_.g_in
  75.3 1.0 collective-permute-start.15
  76.5 2.3 %collective-permute-start.20 = (f32[328,128]{1,0:T(8,128)S(1)}, f32[328,128]{1,0:T(8,128)S(1)}, u32[]{:S(2)}, u32[]{:S(2)}) collective-permute-start(f32[328,128]{1,0:T(8,128)S(1)} %shard_map.90.g_ref.rest_0_.g_in), channel_id=1, source_target_pairs={{0,4},{1,5},{2,6},{3,7},{4,0},{5,1},{6,2},{7,3},{8,12},{9,13},{10,... | collective-permute-start | bytes 503816 | tf_op jit(solution)/shard_map/ppermute | solution.py:408
  78.8 1.0 collective-permute-start.17
  79.9 4.5 %collective-permute-done.15.rest_6_ = f32[328,128]{1,0:T(8,128)S(1)} collective-permute-done((f32[328,128]{1,0:T(8,128)S(1)}, f32[328,128]{1,0:T(8,128)S(1)}, u32[]{:S(2)}, u32[]{:S(2)}) %collective-permute-start.15) | collective-permute-done | bytes 167968 | tf_op jit(solution)/shard_map/ppermute | solution.py:408
  84.4 1.7 %collective-permute-start.16 = (f32[328,128]{1,0:T(8,128)S(1)}, f32[328,128]{1,0:T(8,128)S(1)}, u32[]{:S(2)}, u32[]{:S(2)}) collective-permute-start(f32[328,128]{1,0:T(8,128)S(1)} %collective-permute-done.15.rest_6_), channel_id=1, source_target_pairs={{0,2},{1,3},{2,0},{3,1},{4,6},{5,7},{6,4},{7,5},{8,10},{9,11},{10,... | collective-permute-start | bytes 503816 | tf_op jit(solution)/shard_map/ppermute | solution.py:408
  87.3 2.9 %collective-permute-done.16.unused_in = f32[328,128]{1,0:T(8,128)S(1)} collective-permute-done((f32[328,128]{1,0:T(8,128)S(1)}, f32[328,128]{1,0:T(8,128)S(1)}, u32[]{:S(2)}, u32[]{:S(2)}) %collective-permute-start.16) | collective-permute-done | bytes 167968 | tf_op jit(solution)/shard_map/ppermute | solution.py:408
  90.2 1.2 collective-permute-start.23
  91.7 4.3 %shard_map.92 = (f32[2,15,32,128]{3,2,1,0:T(8,128)S(1)}, f32[4,88,128]{2,1,0:T(8,128)S(1)}, f32[4,88,128]{2,1,0:T(8,128)S(1)}, f32[328,128]{1,0:T(8,128)S(1)}) custom-call(s32[1]{0:T(128)} %bitcast.me_ref, s32[15]{0:T(128)S(1)} %copy-done.20, s32[15]{0:T(128)S(1)} %copy-done.22, ...), custom_call_target="tpu_custom_call", output_to_operand_aliasing={{3}: (5, {})} | custom-call | bytes 73800000 | tf_op jit(solution)/shard_map/pallas_call | solution.py:444
  96.0 1.7 %collective-permute-start.29 = (f32[328,128]{1,0:T(8,128)S(1)}, f32[328,128]{1,0:T(8,128)S(1)}, u32[]{:S(2)}, u32[]{:S(2)}) collective-permute-start(f32[328,128]{1,0:T(8,128)S(1)} %get-tuple-element.27.rest_6_), channel_id=1, source_target_pairs={{0,1},{1,0},{2,3},{3,2},{4,5},{5,4},{6,7},{7,6},{8,9},{9,8},{10,11... | collective-permute-start | bytes 503816 | tf_op jit(solution)/shard_map/ppermute | solution.py:408
  98.5 2.0 %collective-permute-start.28 = (f32[328,128]{1,0:T(8,128)S(1)}, f32[328,128]{1,0:T(8,128)S(1)}, u32[]{:S(2)}, u32[]{:S(2)}) collective-permute-start(f32[328,128]{1,0:T(8,128)S(1)} %collective-permute-done.27.rest_4_), channel_id=1, source_target_pairs={{0,1},{1,0},{2,3},{3,2},{4,5},{5,4},{6,7},{7,6},{8,9},{9,8},{10,11... | collective-permute-start | bytes 503816 | tf_op jit(solution)/shard_map/ppermute | solution.py:408
  100.5 1.0 collective-permute-done.28.rest_5_
  101.5 8.9 %shard_map.93 = f32[16,80,128]{2,1,0:T(8,128)} custom-call(s32[1]{0:T(128)} %bitcast.me_ref, s32[15]{0:T(128)S(1)} %copy-done.20, s32[15]{0:T(128)S(1)} %copy-done.22, bf16[40,2,15,32,128]{4,3,2,1,0:T(8,128)(2,1)} %model_hbm.11, s32[15,32,128]{2,1,0:T(8,128)S(1)} %copy-done.2, f32[8,88,128]{2,1,0:T(8,128)S(1)} %get-tuple-element.21.power_ref, ...), custom_call_target="tpu_custom_call" | custom-call | bytes 25830000 | tf_op jit(solution)/shard_map/pallas_call | solution.py:444
  110.4 4.3 %all-to-all-start.1 = ((f32[16,80,128]{2,1,0:T(8,128)}), f32[16,80,128]{2,1,0:T(8,128)S(1)}, u32[]{:S(2)}, u32[]{:S(2)}) async-start(f32[16,80,128]{2,1,0:T(8,128)} %shard_map.93), calls=%async_computation.1 | async-start | bytes 1310720 | tf_op jit(solution)/shard_map/all_to_all | solution.py:403
  114.7 1.4 shard_map.91
  116.1 1.1 copy-done.5
  117.2 14.4 %all-to-all-done.1.sums = f32[16,80,128]{2,1,0:T(8,128)S(1)} async-done(((f32[16,80,128]{2,1,0:T(8,128)}), f32[16,80,128]{2,1,0:T(8,128)S(1)}, u32[]{:S(2)}, u32[]{:S(2)}) %all-to-all-start.1) | async-done | bytes 655392 | tf_op jit(solution)/shard_map/all_to_all | solution.py:403
  131.6 1.3 copy-done.6
  132.9 1.0 shard_map.94.rest_0_.rest_8_
  134.7 2.3 %collective-permute-start.35 = (f32[328,128]{1,0:T(8,128)S(1)}, f32[328,128]{1,0:T(8,128)S(1)}, u32[]{:S(2)}, u32[]{:S(2)}) collective-permute-start(f32[328,128]{1,0:T(8,128)S(1)} %shard_map.94.rest_0_.rest_8_), channel_id=1, source_target_pairs={{0,4},{1,5},{2,6},{3,7},{4,0},{5,1},{6,2},{7,3},{8,12},{9,13},{10,... | collective-permute-start | bytes 503816 | tf_op jit(solution)/shard_map/ppermute | solution.py:408
  137.0 1.1 collective-permute-start.32
  138.1 5.6 %collective-permute-done.30.rest_6_.rest_14_ = f32[328,128]{1,0:T(8,128)S(1)} collective-permute-done((f32[328,128]{1,0:T(8,128)S(1)}, f32[328,128]{1,0:T(8,128)S(1)}, u32[]{:S(2)}, u32[]{:S(2)}) %collective-permute-start.30) | collective-permute-done | bytes 167968 | tf_op jit(solution)/shard_map/ppermute | solution.py:408
  144.0 1.2 collective-permute-start.34
  145.8 3.2 %collective-permute-done.31.unused_in = f32[328,128]{1,0:T(8,128)S(1)} collective-permute-done((f32[328,128]{1,0:T(8,128)S(1)}, f32[328,128]{1,0:T(8,128)S(1)}, u32[]{:S(2)}, u32[]{:S(2)}) %collective-permute-start.31) | collective-permute-done | bytes 167968 | tf_op jit(solution)/shard_map/ppermute | solution.py:408
  148.9 1.5 collective-permute-start.42
  150.4 4.9 %shard_map.95 = (f32[2,15,32,128]{3,2,1,0:T(8,128)S(1)}, f32[4,88,128]{2,1,0:T(8,128)}, f32[4,88,128]{2,1,0:T(8,128)}, f32[328,128]{1,0:T(8,128)S(1)}) custom-call(s32[1]{0:T(128)} %bitcast.me_ref, s32[15]{0:T(128)S(1)} %copy-done.20, s32[15]{0:T(128)S(1)} %copy-done.22, bf16[40,2,15,32,128]{4,3,2,1,0:T(8,128)(2,1)} %model_hbm.11, ...), custom_call_target="tpu_custom_call", output_to_operand_aliasing={{3}: (5, {})} | custom-call | bytes 73800000 | tf_op jit(solution)/shard_map/pallas_call | solution.py:444
  155.4 2.1 %collective-permute-start.44 = (f32[328,128]{1,0:T(8,128)S(1)}, f32[328,128]{1,0:T(8,128)S(1)}, u32[]{:S(2)}, u32[]{:S(2)}) collective-permute-start(f32[328,128]{1,0:T(8,128)S(1)} %get-tuple-element.29.rest_6_), channel_id=1, source_target_pairs={{0,1},{1,0},{2,3},{3,2},{4,5},{5,4},{6,7},{7,6},{8,9},{9,8},{10,11... | collective-permute-start | bytes 503816 | tf_op jit(solution)/shard_map/ppermute | solution.py:408
  157.9 1.3 collective-permute-start.43
  159.3 1.0 collective-permute-done.43.rest_5_
  160.3 5.0 %shard_map.96 = (f32[2,15,32,128]{3,2,1,0:T(8,128)}, f32[2,160,128]{2,1,0:T(8,128)}) custom-call(s32[1]{0:T(128)} %bitcast.me_ref, s32[15]{0:T(128)S(1)} %copy-done.20, s32[15]{0:T(128)S(1)} %copy-done.22, bf16[40,2,15,32,128]{4,3,2,1,0:T(8,128)(2,1)} %model_hbm.11, s32[15,32,128]{2,1,0:T(8,128)S(1)} %copy-done.2, ...), custom_call_target="tpu_custom_call" | custom-call | bytes 14760000 | tf_op jit(solution)/shard_map/pallas_call | solution.py:444
  (103 shorter events, 15.9 us)
Async XLA Ops:
  1.9 29.3 %copy-start.22 = (s32[15]{0:T(128)S(1)}, s32[15]{0:T(128)}, u32[]{:S(2)}) copy-start(s32[15]{0:T(128)} %second_ref.11) | copy-start | bytes 184
  3.5 9.0 %collective-permute-start.7 = (f32[328,128]{1,0:T(8,128)S(1)}, f32[328,128]{1,0:T(8,128)S(1)}, u32[]{:S(2)}, u32[]{:S(2)}) collective-permute-start(f32[328,128]{1,0:T(8,128)S(1)} %shard_map.86.rest_0_), channel_id=1, source_target_pairs={{0,12},{1,13},{2,14},{3,15},{4,8},{5,9},{6,10},{7,11},{8,4},{9,5},... | collective-permute-start | bytes 503816 | tf_op jit(solution)/shard_map/ppermute | solution.py:408
  4.8 10.5 %collective-permute-start.1 = (f32[328,128]{1,0:T(8,128)S(1)}, f32[328,128]{1,0:T(8,128)S(1)}, u32[]{:S(2)}, u32[]{:S(2)}) collective-permute-start(f32[328,128]{1,0:T(8,128)S(1)} %shard_map.86.rest_0_), channel_id=1, source_target_pairs={{0,2},{1,3},{2,0},{3,1},{4,6},{5,7},{6,4},{7,5},{8,10},{9,11},{10,... | collective-permute-start | bytes 503816 | tf_op jit(solution)/shard_map/ppermute | solution.py:408
  6.0 9.3 %collective-permute-start.3 = (f32[328,128]{1,0:T(8,128)S(1)}, f32[328,128]{1,0:T(8,128)S(1)}, u32[]{:S(2)}, u32[]{:S(2)}) collective-permute-start(f32[328,128]{1,0:T(8,128)S(1)} %shard_map.86.rest_0_), channel_id=1, source_target_pairs={{0,4},{1,5},{2,6},{3,7},{4,0},{5,1},{6,2},{7,3},{8,12},{9,13},{10,... | collective-permute-start | bytes 503816 | tf_op jit(solution)/shard_map/ppermute | solution.py:408
  12.5 5.1 %collective-permute-start.8 = (f32[328,128]{1,0:T(8,128)S(1)}, f32[328,128]{1,0:T(8,128)S(1)}, u32[]{:S(2)}, u32[]{:S(2)}) collective-permute-start(f32[328,128]{1,0:T(8,128)S(1)} %collective-permute-done.7.rest_12_), channel_id=1, source_target_pairs={{0,4},{1,5},{2,6},{3,7},{4,0},{5,1},{6,2},{7,3},{8,12},{9,13},{10,... | collective-permute-start | bytes 503816 | tf_op jit(solution)/shard_map/ppermute | solution.py:408
  12.5 7.0 %collective-permute-start.13 = (f32[328,128]{1,0:T(8,128)S(1)}, f32[328,128]{1,0:T(8,128)S(1)}, u32[]{:S(2)}, u32[]{:S(2)}) collective-permute-start(f32[328,128]{1,0:T(8,128)S(1)} %collective-permute-done.7.rest_12_), channel_id=1, source_target_pairs={{0,2},{1,3},{2,0},{3,1},{4,6},{5,7},{6,4},{7,5},{8,10},{9,11},{10,... | collective-permute-start | bytes 503816 | tf_op jit(solution)/shard_map/ppermute | solution.py:408
  13.7 13.5 %collective-permute-start = (f32[328,128]{1,0:T(8,128)S(1)}, f32[328,128]{1,0:T(8,128)S(1)}, u32[]{:S(2)}, u32[]{:S(2)}) collective-permute-start(f32[328,128]{1,0:T(8,128)S(1)} %shard_map.86.rest_0_), channel_id=1, source_target_pairs={{0,1},{1,0},{2,3},{3,2},{4,5},{5,4},{6,7},{7,6},{8,9},{9,8},{10,11... | collective-permute-start | bytes 503816 | tf_op jit(solution)/shard_map/ppermute | solution.py:408
  15.3 13.6 %collective-permute-start.2 = (f32[328,128]{1,0:T(8,128)S(1)}, f32[328,128]{1,0:T(8,128)S(1)}, u32[]{:S(2)}, u32[]{:S(2)}) collective-permute-start(f32[328,128]{1,0:T(8,128)S(1)} %collective-permute-done.1.rest_2_), channel_id=1, source_target_pairs={{0,1},{1,0},{2,3},{3,2},{4,5},{5,4},{6,7},{7,6},{8,9},{9,8},{10,11... | collective-permute-start | bytes 503816 | tf_op jit(solution)/shard_map/ppermute | solution.py:408
  15.3 13.7 %collective-permute-start.5 = (f32[328,128]{1,0:T(8,128)S(1)}, f32[328,128]{1,0:T(8,128)S(1)}, u32[]{:S(2)}, u32[]{:S(2)}) collective-permute-start(f32[328,128]{1,0:T(8,128)S(1)} %collective-permute-done.3.rest_4_), channel_id=1, source_target_pairs={{0,2},{1,3},{2,0},{3,1},{4,6},{5,7},{6,4},{7,5},{8,10},{9,11},{10,... | collective-permute-start | bytes 503816 | tf_op jit(solution)/shard_map/ppermute | solution.py:408
  17.5 11.9 %collective-permute-start.4 = (f32[328,128]{1,0:T(8,128)S(1)}, f32[328,128]{1,0:T(8,128)S(1)}, u32[]{:S(2)}, u32[]{:S(2)}) collective-permute-start(f32[328,128]{1,0:T(8,128)S(1)} %collective-permute-done.3.rest_4_), channel_id=1, source_target_pairs={{0,1},{1,0},{2,3},{3,2},{4,5},{5,4},{6,7},{7,6},{8,9},{9,8},{10,11... | collective-permute-start | bytes 503816 | tf_op jit(solution)/shard_map/ppermute | solution.py:408
  19.5 10.0 %collective-permute-start.10 = (f32[328,128]{1,0:T(8,128)S(1)}, f32[328,128]{1,0:T(8,128)S(1)}, u32[]{:S(2)}, u32[]{:S(2)}) collective-permute-start(f32[328,128]{1,0:T(8,128)S(1)} %collective-permute-done.8.rest_8_), channel_id=1, source_target_pairs={{0,2},{1,3},{2,0},{3,1},{4,6},{5,7},{6,4},{7,5},{8,10},{9,11},{10,... | collective-permute-start | bytes 503816 | tf_op jit(solution)/shard_map/ppermute | solution.py:408
  27.2 2.7 %collective-permute-start.12 = (f32[328,128]{1,0:T(8,128)S(1)}, f32[328,128]{1,0:T(8,128)S(1)}, u32[]{:S(2)}, u32[]{:S(2)}) collective-permute-start(f32[328,128]{1,0:T(8,128)S(1)} %collective-permute-done.7.rest_12_), channel_id=1, source_target_pairs={{0,1},{1,0},{2,3},{3,2},{4,5},{5,4},{6,7},{7,6},{8,9},{9,8},{10,11... | collective-permute-start | bytes 503816 | tf_op jit(solution)/shard_map/ppermute | solution.py:408
  28.9 2.1 %collective-permute-start.14 = (f32[328,128]{1,0:T(8,128)S(1)}, f32[328,128]{1,0:T(8,128)S(1)}, u32[]{:S(2)}, u32[]{:S(2)}) collective-permute-start(f32[328,128]{1,0:T(8,128)S(1)} %get-tuple-element.17.rest_14_), channel_id=1, source_target_pairs={{0,1},{1,0},{2,3},{3,2},{4,5},{5,4},{6,7},{7,6},{8,9},{9,8},{10,11... | collective-permute-start | bytes 503816 | tf_op jit(solution)/shard_map/ppermute | solution.py:408
  29.0 1.7 %collective-permute-start.6 = (f32[328,128]{1,0:T(8,128)S(1)}, f32[328,128]{1,0:T(8,128)}, u32[]{:S(2)}, u32[]{:S(2)}) collective-permute-start(f32[328,128]{1,0:T(8,128)S(1)} %collective-permute-done.5.rest_6_), channel_id=1, source_target_pairs={{0,1},{1,0},{2,3},{3,2},{4,5},{5,4},{6,7},{7,6},{8,9},{9,8},{10,11... | collective-permute-start | bytes 503816 | tf_op jit(solution)/shard_map/ppermute | solution.py:408
  29.4 1.5 collective-permute-start.9
  29.5 1.7 %collective-permute-start.11 = (f32[328,128]{1,0:T(8,128)S(1)}, f32[328,128]{1,0:T(8,128)}, u32[]{:S(2)}, u32[]{:S(2)}) collective-permute-start(f32[328,128]{1,0:T(8,128)S(1)} %collective-permute-done.10.rest_10_), channel_id=1, source_target_pairs={{0,1},{1,0},{2,3},{3,2},{4,5},{5,4},{6,7},{7,6},{8,9},{9,8},{10,11... | collective-permute-start | bytes 503816 | tf_op jit(solution)/shard_map/ppermute | solution.py:408
  42.2 29.2 %all-to-all-start = ((f32[16,120,128]{2,1,0:T(8,128)}), f32[16,120,128]{2,1,0:T(8,128)S(1)}, u32[]{:S(2)}, u32[]{:S(2)}) async-start(f32[16,120,128]{2,1,0:T(8,128)} %shard_map.89), calls=%async_computation | async-start | bytes 1966080 | tf_op jit(solution)/shard_map/all_to_all | solution.py:403
  75.3 9.1 %collective-permute-start.15 = (f32[328,128]{1,0:T(8,128)S(1)}, f32[328,128]{1,0:T(8,128)S(1)}, u32[]{:S(2)}, u32[]{:S(2)}) collective-permute-start(f32[328,128]{1,0:T(8,128)S(1)} %shard_map.90.g_ref.rest_0_.g_in), channel_id=1, source_target_pairs={{0,12},{1,13},{2,14},{3,15},{4,8},{5,9},{6,10},{7,11},{8,4},{9,5},... | collective-permute-start | bytes 503816 | tf_op jit(solution)/shard_map/ppermute | solution.py:408
  76.3 9.7 %collective-permute-start.18 = (f32[328,128]{1,0:T(8,128)S(1)}, f32[328,128]{1,0:T(8,128)S(1)}, u32[]{:S(2)}, u32[]{:S(2)}) collective-permute-start(f32[328,128]{1,0:T(8,128)S(1)} %shard_map.90.g_ref.rest_0_.g_in), channel_id=1, source_target_pairs={{0,2},{1,3},{2,0},{3,1},{4,6},{5,7},{6,4},{7,5},{8,10},{9,11},{10,... | collective-permute-start | bytes 503816 | tf_op jit(solution)/shard_map/ppermute | solution.py:408
  76.5 10.2 %collective-permute-start.20 = (f32[328,128]{1,0:T(8,128)S(1)}, f32[328,128]{1,0:T(8,128)S(1)}, u32[]{:S(2)}, u32[]{:S(2)}) collective-permute-start(f32[328,128]{1,0:T(8,128)S(1)} %shard_map.90.g_ref.rest_0_.g_in), channel_id=1, source_target_pairs={{0,4},{1,5},{2,6},{3,7},{4,0},{5,1},{6,2},{7,3},{8,12},{9,13},{10,... | collective-permute-start | bytes 503816 | tf_op jit(solution)/shard_map/ppermute | solution.py:408
  78.8 8.0 %collective-permute-start.17 = (f32[328,128]{1,0:T(8,128)S(1)}, f32[328,128]{1,0:T(8,128)S(1)}, u32[]{:S(2)}, u32[]{:S(2)}) collective-permute-start(f32[328,128]{1,0:T(8,128)S(1)} %shard_map.90.g_ref.rest_0_.g_in), channel_id=1, source_target_pairs={{0,1},{1,0},{2,3},{3,2},{4,5},{5,4},{6,7},{7,6},{8,9},{9,8},{10,11... | collective-permute-start | bytes 503816 | tf_op jit(solution)/shard_map/ppermute | solution.py:408
  84.4 5.8 %collective-permute-start.16 = (f32[328,128]{1,0:T(8,128)S(1)}, f32[328,128]{1,0:T(8,128)S(1)}, u32[]{:S(2)}, u32[]{:S(2)}) collective-permute-start(f32[328,128]{1,0:T(8,128)S(1)} %collective-permute-done.15.rest_6_), channel_id=1, source_target_pairs={{0,2},{1,3},{2,0},{3,1},{4,6},{5,7},{6,4},{7,5},{8,10},{9,11},{10,... | collective-permute-start | bytes 503816 | tf_op jit(solution)/shard_map/ppermute | solution.py:408
  86.0 5.4 %collective-permute-start.25 = (f32[328,128]{1,0:T(8,128)S(1)}, f32[328,128]{1,0:T(8,128)S(1)}, u32[]{:S(2)}, u32[]{:S(2)}) collective-permute-start(f32[328,128]{1,0:T(8,128)S(1)} %collective-permute-done.15.rest_6_), channel_id=1, source_target_pairs={{0,4},{1,5},{2,6},{3,7},{4,0},{5,1},{6,2},{7,3},{8,12},{9,13},{10,... | collective-permute-start | bytes 503816 | tf_op jit(solution)/shard_map/ppermute | solution.py:408
  86.0 5.6 %collective-permute-start.19 = (f32[328,128]{1,0:T(8,128)S(1)}, f32[328,128]{1,0:T(8,128)S(1)}, u32[]{:S(2)}, u32[]{:S(2)}) collective-permute-start(f32[328,128]{1,0:T(8,128)S(1)} %collective-permute-done.18.rest_2_), channel_id=1, source_target_pairs={{0,1},{1,0},{2,3},{3,2},{4,5},{5,4},{6,7},{7,6},{8,9},{9,8},{10,11... | collective-permute-start | bytes 503816 | tf_op jit(solution)/shard_map/ppermute | solution.py:408
  86.8 4.9 %collective-permute-start.21 = (f32[328,128]{1,0:T(8,128)S(1)}, f32[328,128]{1,0:T(8,128)S(1)}, u32[]{:S(2)}, u32[]{:S(2)}) collective-permute-start(f32[328,128]{1,0:T(8,128)S(1)} %collective-permute-done.20.rest_4_), channel_id=1, source_target_pairs={{0,1},{1,0},{2,3},{3,2},{4,5},{5,4},{6,7},{7,6},{8,9},{9,8},{10,11... | collective-permute-start | bytes 503816 | tf_op jit(solution)/shard_map/ppermute | solution.py:408
  86.9 4.8 %collective-permute-start.22 = (f32[328,128]{1,0:T(8,128)S(1)}, f32[328,128]{1,0:T(8,128)S(1)}, u32[]{:S(2)}, u32[]{:S(2)}) collective-permute-start(f32[328,128]{1,0:T(8,128)S(1)} %collective-permute-done.15.rest_6_), channel_id=1, source_target_pairs={{0,1},{1,0},{2,3},{3,2},{4,5},{5,4},{6,7},{7,6},{8,9},{9,8},{10,11... | collective-permute-start | bytes 503816 | tf_op jit(solution)/shard_map/ppermute | solution.py:408
  90.2 7.5 %collective-permute-start.23 = (f32[328,128]{1,0:T(8,128)S(1)}, f32[328,128]{1,0:T(8,128)S(1)}, u32[]{:S(2)}, u32[]{:S(2)}) collective-permute-start(f32[328,128]{1,0:T(8,128)S(1)} %collective-permute-done.20.rest_4_), channel_id=1, source_target_pairs={{0,2},{1,3},{2,0},{3,1},{4,6},{5,7},{6,4},{7,5},{8,10},{9,11},{10,... | collective-permute-start | bytes 503816 | tf_op jit(solution)/shard_map/ppermute | solution.py:408
  91.4 7.1 %collective-permute-start.27 = (f32[328,128]{1,0:T(8,128)S(1)}, f32[328,128]{1,0:T(8,128)S(1)}, u32[]{:S(2)}, u32[]{:S(2)}) collective-permute-start(f32[328,128]{1,0:T(8,128)S(1)} %collective-permute-done.25.rest_2_), channel_id=1, source_target_pairs={{0,2},{1,3},{2,0},{3,1},{4,6},{5,7},{6,4},{7,5},{8,10},{9,11},{10,... | collective-permute-start | bytes 503816 | tf_op jit(solution)/shard_map/ppermute | solution.py:408
  96.0 4.5 %collective-permute-start.29 = (f32[328,128]{1,0:T(8,128)S(1)}, f32[328,128]{1,0:T(8,128)S(1)}, u32[]{:S(2)}, u32[]{:S(2)}) collective-permute-start(f32[328,128]{1,0:T(8,128)S(1)} %get-tuple-element.27.rest_6_), channel_id=1, source_target_pairs={{0,1},{1,0},{2,3},{3,2},{4,5},{5,4},{6,7},{7,6},{8,9},{9,8},{10,11... | collective-permute-start | bytes 503816 | tf_op jit(solution)/shard_map/ppermute | solution.py:408
  97.7 2.8 %collective-permute-start.24 = (f32[328,128]{1,0:T(8,128)S(1)}, f32[328,128]{1,0:T(8,128)S(1)}, u32[]{:S(2)}, u32[]{:S(2)}) collective-permute-start(f32[328,128]{1,0:T(8,128)S(1)} %collective-permute-done.23.rest_0_), channel_id=1, source_target_pairs={{0,1},{1,0},{2,3},{3,2},{4,5},{5,4},{6,7},{7,6},{8,9},{9,8},{10,11... | collective-permute-start | bytes 503816 | tf_op jit(solution)/shard_map/ppermute | solution.py:408
  98.5 2.0 %collective-permute-start.26 = (f32[328,128]{1,0:T(8,128)S(1)}, f32[328,128]{1,0:T(8,128)S(1)}, u32[]{:S(2)}, u32[]{:S(2)}) collective-permute-start(f32[328,128]{1,0:T(8,128)S(1)} %collective-permute-done.25.rest_2_), channel_id=1, source_target_pairs={{0,1},{1,0},{2,3},{3,2},{4,5},{5,4},{6,7},{7,6},{8,9},{9,8},{10,11... | collective-permute-start | bytes 503816 | tf_op jit(solution)/shard_map/ppermute | solution.py:408
  98.5 3.0 %collective-permute-start.28 = (f32[328,128]{1,0:T(8,128)S(1)}, f32[328,128]{1,0:T(8,128)S(1)}, u32[]{:S(2)}, u32[]{:S(2)}) collective-permute-start(f32[328,128]{1,0:T(8,128)S(1)} %collective-permute-done.27.rest_4_), channel_id=1, source_target_pairs={{0,1},{1,0},{2,3},{3,2},{4,5},{5,4},{6,7},{7,6},{8,9},{9,8},{10,11... | collective-permute-start | bytes 503816 | tf_op jit(solution)/shard_map/ppermute | solution.py:408
  110.4 21.2 %all-to-all-start.1 = ((f32[16,80,128]{2,1,0:T(8,128)}), f32[16,80,128]{2,1,0:T(8,128)S(1)}, u32[]{:S(2)}, u32[]{:S(2)}) async-start(f32[16,80,128]{2,1,0:T(8,128)} %shard_map.93), calls=%async_computation.1 | async-start | bytes 1310720 | tf_op jit(solution)/shard_map/all_to_all | solution.py:403
  133.9 9.8 %collective-permute-start.30 = (f32[328,128]{1,0:T(8,128)S(1)}, f32[328,128]{1,0:T(8,128)S(1)}, u32[]{:S(2)}, u32[]{:S(2)}) collective-permute-start(f32[328,128]{1,0:T(8,128)S(1)} %shard_map.94.rest_0_.rest_8_), channel_id=1, source_target_pairs={{0,12},{1,13},{2,14},{3,15},{4,8},{5,9},{6,10},{7,11},{8,4},{9,5},... | collective-permute-start | bytes 503816 | tf_op jit(solution)/shard_map/ppermute | solution.py:408
  134.1 9.9 %collective-permute-start.33 = (f32[328,128]{1,0:T(8,128)S(1)}, f32[328,128]{1,0:T(8,128)S(1)}, u32[]{:S(2)}, u32[]{:S(2)}) collective-permute-start(f32[328,128]{1,0:T(8,128)S(1)} %shard_map.94.rest_0_.rest_8_), channel_id=1, source_target_pairs={{0,2},{1,3},{2,0},{3,1},{4,6},{5,7},{6,4},{7,5},{8,10},{9,11},{10,... | collective-permute-start | bytes 503816 | tf_op jit(solution)/shard_map/ppermute | solution.py:408
  134.7 10.5 %collective-permute-start.35 = (f32[328,128]{1,0:T(8,128)S(1)}, f32[328,128]{1,0:T(8,128)S(1)}, u32[]{:S(2)}, u32[]{:S(2)}) collective-permute-start(f32[328,128]{1,0:T(8,128)S(1)} %shard_map.94.rest_0_.rest_8_), channel_id=1, source_target_pairs={{0,4},{1,5},{2,6},{3,7},{4,0},{5,1},{6,2},{7,3},{8,12},{9,13},{10,... | collective-permute-start | bytes 503816 | tf_op jit(solution)/shard_map/ppermute | solution.py:408
  137.0 8.3 %collective-permute-start.32 = (f32[328,128]{1,0:T(8,128)S(1)}, f32[328,128]{1,0:T(8,128)S(1)}, u32[]{:S(2)}, u32[]{:S(2)}) collective-permute-start(f32[328,128]{1,0:T(8,128)S(1)} %shard_map.94.rest_0_.rest_8_), channel_id=1, source_target_pairs={{0,1},{1,0},{2,3},{3,2},{4,5},{5,4},{6,7},{7,6},{8,9},{9,8},{10,11... | collective-permute-start | bytes 503816 | tf_op jit(solution)/shard_map/ppermute | solution.py:408
  143.7 5.3 %collective-permute-start.31 = (f32[328,128]{1,0:T(8,128)S(1)}, f32[328,128]{1,0:T(8,128)S(1)}, u32[]{:S(2)}, u32[]{:S(2)}) collective-permute-start(f32[328,128]{1,0:T(8,128)S(1)} %collective-permute-done.30.rest_6_.rest_14_), channel_id=1, source_target_pairs={{0,2},{1,3},{2,0},{3,1},{4,6},{5,7},{6,4},{7,5},{8,10},{9,11},{10,... | collective-permute-start | bytes 503816 | tf_op jit(solution)/shard_map/ppermute | solution.py:408
  144.0 4.9 %collective-permute-start.40 = (f32[328,128]{1,0:T(8,128)S(1)}, f32[328,128]{1,0:T(8,128)S(1)}, u32[]{:S(2)}, u32[]{:S(2)}) collective-permute-start(f32[328,128]{1,0:T(8,128)S(1)} %collective-permute-done.30.rest_6_.rest_14_), channel_id=1, source_target_pairs={{0,4},{1,5},{2,6},{3,7},{4,0},{5,1},{6,2},{7,3},{8,12},{9,13},{10,... | collective-permute-start | bytes 503816 | tf_op jit(solution)/shard_map/ppermute | solution.py:408
  144.0 6.4 %collective-permute-start.34 = (f32[328,128]{1,0:T(8,128)S(1)}, f32[328,128]{1,0:T(8,128)S(1)}, u32[]{:S(2)}, u32[]{:S(2)}) collective-permute-start(f32[328,128]{1,0:T(8,128)S(1)} %collective-permute-done.33.rest_2_.rest_10_), channel_id=1, source_target_pairs={{0,1},{1,0},{2,3},{3,2},{4,5},{5,4},{6,7},{7,6},{8,9},{9,8},{10,11... | collective-permute-start | bytes 503816 | tf_op jit(solution)/shard_map/ppermute | solution.py:408
  145.3 5.2 %collective-permute-start.36 = (f32[328,128]{1,0:T(8,128)S(1)}, f32[328,128]{1,0:T(8,128)S(1)}, u32[]{:S(2)}, u32[]{:S(2)}) collective-permute-start(f32[328,128]{1,0:T(8,128)S(1)} %collective-permute-done.35.rest_4_.rest_12_), channel_id=1, source_target_pairs={{0,1},{1,0},{2,3},{3,2},{4,5},{5,4},{6,7},{7,6},{8,9},{9,8},{10,11... | collective-permute-start | bytes 503816 | tf_op jit(solution)/shard_map/ppermute | solution.py:408
  145.3 5.1 %collective-permute-start.37 = (f32[328,128]{1,0:T(8,128)S(1)}, f32[328,128]{1,0:T(8,128)S(1)}, u32[]{:S(2)}, u32[]{:S(2)}) collective-permute-start(f32[328,128]{1,0:T(8,128)S(1)} %collective-permute-done.30.rest_6_.rest_14_), channel_id=1, source_target_pairs={{0,1},{1,0},{2,3},{3,2},{4,5},{5,4},{6,7},{7,6},{8,9},{9,8},{10,11... | collective-permute-start | bytes 503816 | tf_op jit(solution)/shard_map/ppermute | solution.py:408
  148.9 8.5 %collective-permute-start.38 = (f32[328,128]{1,0:T(8,128)S(1)}, f32[328,128]{1,0:T(8,128)S(1)}, u32[]{:S(2)}, u32[]{:S(2)}) collective-permute-start(f32[328,128]{1,0:T(8,128)S(1)} %collective-permute-done.35.rest_4_.rest_12_), channel_id=1, source_target_pairs={{0,2},{1,3},{2,0},{3,1},{4,6},{5,7},{6,4},{7,5},{8,10},{9,11},{10,... | collective-permute-start | bytes 503816 | tf_op jit(solution)/shard_map/ppermute | solution.py:408
  148.9 9.0 %collective-permute-start.42 = (f32[328,128]{1,0:T(8,128)S(1)}, f32[328,128]{1,0:T(8,128)S(1)}, u32[]{:S(2)}, u32[]{:S(2)}) collective-permute-start(f32[328,128]{1,0:T(8,128)S(1)} %collective-permute-done.40.rest_2_), channel_id=1, source_target_pairs={{0,2},{1,3},{2,0},{3,1},{4,6},{5,7},{6,4},{7,5},{8,10},{9,11},{10,... | collective-permute-start | bytes 503816 | tf_op jit(solution)/shard_map/ppermute | solution.py:408
  155.4 3.9 %collective-permute-start.44 = (f32[328,128]{1,0:T(8,128)S(1)}, f32[328,128]{1,0:T(8,128)S(1)}, u32[]{:S(2)}, u32[]{:S(2)}) collective-permute-start(f32[328,128]{1,0:T(8,128)S(1)} %get-tuple-element.29.rest_6_), channel_id=1, source_target_pairs={{0,1},{1,0},{2,3},{3,2},{4,5},{5,4},{6,7},{7,6},{8,9},{9,8},{10,11... | collective-permute-start | bytes 503816 | tf_op jit(solution)/shard_map/ppermute | solution.py:408
  157.4 1.8 %collective-permute-start.39 = (f32[328,128]{1,0:T(8,128)S(1)}, f32[328,128]{1,0:T(8,128)S(1)}, u32[]{:S(2)}, u32[]{:S(2)}) collective-permute-start(f32[328,128]{1,0:T(8,128)S(1)} %collective-permute-done.38.rest_0_), channel_id=1, source_target_pairs={{0,1},{1,0},{2,3},{3,2},{4,5},{5,4},{6,7},{7,6},{8,9},{9,8},{10,11... | collective-permute-start | bytes 503816 | tf_op jit(solution)/shard_map/ppermute | solution.py:408
  157.5 1.8 %collective-permute-start.41 = (f32[328,128]{1,0:T(8,128)S(1)}, f32[328,128]{1,0:T(8,128)S(1)}, u32[]{:S(2)}, u32[]{:S(2)}) collective-permute-start(f32[328,128]{1,0:T(8,128)S(1)} %collective-permute-done.40.rest_2_), channel_id=1, source_target_pairs={{0,1},{1,0},{2,3},{3,2},{4,5},{5,4},{6,7},{7,6},{8,9},{9,8},{10,11... | collective-permute-start | bytes 503816 | tf_op jit(solution)/shard_map/ppermute | solution.py:408
  157.9 2.4 %collective-permute-start.43 = (f32[328,128]{1,0:T(8,128)S(1)}, f32[328,128]{1,0:T(8,128)S(1)}, u32[]{:S(2)}, u32[]{:S(2)}) collective-permute-start(f32[328,128]{1,0:T(8,128)S(1)} %collective-permute-done.42.rest_4_), channel_id=1, source_target_pairs={{0,1},{1,0},{2,3},{3,2},{4,5},{5,4},{6,7},{7,6},{8,9},{9,8},{10,11... | collective-permute-start | bytes 503816 | tf_op jit(solution)/shard_map/ppermute | solution.py:408
  (22 other events, 161.8 us)

commit v7 on v6

--- a/solution.py
+++ b/solution.py
@@ -121,7 +121,7 @@
 
 
 def first_own_kernel(n, dpc, me_ref, *rest):
-    ins, (g_ref, onehot_ref, sel_ref, split, lines) = rest[:n], rest[n:]
+    ins, (g_ref, onehot_ref, split, lines) = rest[:n], rest[n:]
     me = me_ref[0]
     k, c = lax.div(me, 2), lax.rem(me, 2)
     per = STATIONS // n
@@ -145,7 +145,6 @@
             marks = marks + (pltpu.roll(row, i * 2 * ROWS, axis=1) if i else row)
         hit = station + 1 == marks.astype(jnp.int32)
         onehot_ref[:, group * 128 : (group + 1) * 128] = jnp.where(hit, 1.0, 0.0).astype(BF16)
-    sel_ref[...] = pick(onehot_ref[...], g, ((0,), (0,)))
 
 
 def fill_powers(n, dpc, sums, sel_ref, terms, base):
@@ -181,21 +180,23 @@
             terms[r + ROWS : r + 2 * ROWS, cols] = Brr * p - Bii * swap(p)
 
 
-def own_kernel(n, dpc, g_in, onehot_ref, sel_ref, sums, g_out, terms):
+def own_kernel(n, dpc, g_in, onehot_ref, sums, g_out, terms, sel_ref):
     width = dpc * 128
+    sel_ref[...] = pick(onehot_ref[...], wide(g_in, dpc), ((0,), (0,)))
     fill_sums(n, dpc, sums, sel_ref, terms)
     fill_powers(n, dpc, sums, sel_ref, terms, width)
     total = pick(onehot_ref[...], terms[...], ((1,), (0,)))
     put(g_out, 0.5 * (wide(g_in, dpc) + total[:, :width] / (total[:, width:] + ridge)), dpc)
 
 
-def prepare_kernel(n, dpc, g_ref, onehot_ref, sums, sel_ref, den_ref, terms):
+def prepare_kernel(n, dpc, g_ref, onehot_ref, sums, den_ref, terms, sel_ref):
     sel_ref[...] = pick(onehot_ref[...], wide(g_ref, dpc), ((0,), (0,)))
     fill_powers(n, dpc, sums, sel_ref, terms, 0)
     den_ref[...] = pick(onehot_ref[...], terms[...], ((1,), (0,))) + ridge
 
 
-def later_own_kernel(n, dpc, g_in, onehot_ref, sel_ref, den_ref, sums, g_out, terms):
+def later_own_kernel(n, dpc, g_in, onehot_ref, den_ref, sums, g_out, terms, sel_ref):
+    sel_ref[...] = pick(onehot_ref[...], wide(g_in, dpc), ((0,), (0,)))
     fill_sums(n, dpc, sums, sel_ref, terms)
     total = pick(onehot_ref[...], terms[...], ((1,), (0,)))
     put(g_out, 0.5 * (wide(g_in, dpc) + total / den_ref[...]), dpc)
@@ -271,15 +272,42 @@
     return weight * acc[0], weight * acc[1]
 
 
+def fold(a, b, step):
+    if a is None:
+        return None
+    if b is None:
+        return a + pltpu.roll(a, step, axis=0)
+    mine = (lax.broadcasted_iota(jnp.int32, a.shape, 0) & step) == 0
+    return jnp.where(mine, a, b) + pltpu.roll(jnp.where(mine, b, a), step, axis=0)
+
+
+def row_sums(values):
+    values = list(values) + [None] * (TILE - len(values))
+    step = 1
+    while step < TILE:
+        values = [fold(a, b, step) for a, b in zip(values[::2], values[1::2])]
+        step *= 2
+    return values[0]
+
+
+def tile_sum(x):
+    total = x[:TILE]
+    for t in range(1, x.shape[0] // TILE):
+        total = total + x[t * TILE : (t + 1) * TILE]
+    return total
+
+
 def correlate(dpc, b, res, chips, model_ref, cre, cim):
     res_re, res_im = res
     for m, k in enumerate(chips):
+        re, im = [], []
         for dd in range(dpc):
             mr = model_ref[k * dpc + dd, 0, b].astype(F32)
             mi = model_ref[k * dpc + dd, 1, b].astype(F32)
-            row = pl.ds(b * dpc + dd, 1)
-            cre[m, row, :] = jnp.sum(mr * res_re + mi * res_im, axis=0, keepdims=True)
-            cim[m, row, :] = jnp.sum(mr * res_im - mi * res_re, axis=0, keepdims=True)
+            re.append(tile_sum(mr * res_re + mi * res_im))
+            im.append(tile_sum(mr * res_im - mi * res_re))
+        cre[m, pl.ds(b * dpc, TILE), :] = row_sums(re)
+        cim[m, pl.ds(b * dpc, TILE), :] = row_sums(im)
 
 
 def write_sums(dpc, chips, cre, cim, tiles, power_ref, out_ref, start):
@@ -321,36 +349,50 @@
     write_sums(dpc, chips, cre, cim, lambda m: (hre, him, m), power_ref, out_ref, True)
 
 
-NEAR, FAR = (0, 1, 2, 6), (3, 4, 5, 7)
+OWN, NEAR, FAR = (0,), (1, 2, 6), (3, 4, 5, 7)
 
 
 def chips_of(me, pairs):
     return [jnp.bitwise_xor(lax.div(me, 2), m) for m in pairs]
 
 
-def early_kernel(n, dpc, me_ref, first_ref, second_ref, model_hbm, vis_ref, unused_in, *rest):
-    ins, (acc_ref, hre, him, unused_out, model_ref, sems) = rest[: 2 * len(NEAR)], rest[2 * len(NEAR) :]
+def early_kernel(n, dpc, pairs, me_ref, first_ref, second_ref, model_hbm, acc_in, handed, *rest):
+    ins, (acc_ref, hre, him, handed_out, model_ref, sems) = rest[: 2 * len(pairs)], rest[2 * len(pairs) :]
     me = me_ref[0]
-    fetch = Fetch(model_hbm, model_ref, sems, [k * dpc for k in chips_of(me, NEAR)])
+    fetch = Fetch(model_hbm, model_ref, sems, [k * dpc for k in chips_of(me, pairs)])
+    handed_out[...] = handed[...]
     products(dpc, me, first_ref, second_ref, ins, hre, him)
 
     def pair(b, carry):
-        acc = vis_ref[0, b], vis_ref[1, b]
-        acc_ref[0, b], acc_ref[1, b] = predict(dpc, b, acc, range(len(NEAR)), model_ref, hre, him)
+        acc = acc_in[0, b], acc_in[1, b]
+        acc_ref[0, b], acc_ref[1, b] = predict(dpc, b, acc, range(len(pairs)), model_ref, hre, him)
         return carry
 
     fetch.each(pair)
 
 
 def later_pass_kernel(
-    n, dpc, me_ref, first_ref, second_ref, model_hbm, mask_ref, power_ref, acc_ref, near_re, near_im, *rest
+    n,
+    dpc,
+    me_ref,
+    first_ref,
+    second_ref,
+    model_hbm,
+    mask_ref,
+    power_ref,
+    acc_ref,
+    own_re,
+    own_im,
+    near_re,
+    near_im,
+    *rest,
 ):
     ins, (out_ref, model_ref, sems, hre, him, cre, cim) = rest[: 2 * len(FAR)], rest[2 * len(FAR) :]
     fetch = Fetch(model_hbm, model_ref, sems)
     me = me_ref[0]
     products(dpc, me, first_ref, second_ref, ins, hre, him)
     far = chips_of(me, FAR)
-    chips = chips_of(me, NEAR) + far
+    chips = chips_of(me, OWN + NEAR) + far
 
     def pair(b, carry):
         acc = predict(dpc, b, (acc_ref[0, b], acc_ref[1, b]), far, model_ref, hre, him)
@@ -360,7 +402,10 @@
     fetch.each(pair)
 
     def tiles(m):
-        return (near_re, near_im, m) if m < len(NEAR) else (hre, him, m - len(NEAR))
+        for re, im, pairs in ((own_re, own_im, OWN), (near_re, near_im, NEAR), (hre, him, FAR)):
+            if m < len(pairs):
+                return re, im, m
+            m -= len(pairs)
 
     clear(dpc, mask_ref.shape[0], cre, cim)
     write_sums(dpc, chips, cre, cim, tiles, power_ref, out_ref, False)
@@ -373,7 +418,7 @@
     products(dpc, me, first_ref, second_ref, ins[: 2 * len(FAR)], hre, him)
     per = STATIONS // n
     even = lax.rem(me, 2) == 0
-    for m, k in enumerate(chips_of(me, FAR + NEAR)):
+    for m, k in enumerate(chips_of(me, FAR + NEAR + OWN)):
         for s in range(per):
             re, im = piece_pair(dpc, even, ins, m, me * per + s)
             for dd in range(dpc):
@@ -403,18 +448,16 @@
     return lax.all_to_all(x, "bl", split_axis=0, concat_axis=0, tiled=True)
 
 
-def gather(n, piece, beside, at):
+def gather(n, piece, beside, early=None):
     def send(x, o):
         return lax.ppermute(x, "bl", [(i, i ^ o) for i in range(n)])
 
     got = {0: piece}
-    got[4], got[12] = send(piece, 4), send(piece, 12)
-    got[2] = send(piece, 2)
-    got[6] = send(got[4], 2)
-    got[8] = send(got[12], 4)
-    got[14], got[10] = send(got[12], 2), send(got[8], 2)
-    for o in (0, 2, 4, 12, 6, 14, 8, 10):
-        if o == at:
+    got[12], got[2], got[4], got[1] = (send(piece, o) for o in (12, 2, 4, 1))
+    got[8] = send(early(piece, got), 8) if early else send(got[12], 4)
+    got[6], got[14], got[10] = send(got[4], 2), send(got[12], 2), send(got[8], 2)
+    for o in (2, 4, 12, 6, 14, 8, 10):
+        if o == 6:
             got[o] = beside(got[o], got)
         got[o + 1] = send(got[o], 1)
     return [got[o] for o in range(n)]
@@ -428,7 +471,7 @@
     me = lax.axis_index("bl").astype(jnp.int32).reshape(1)
     params = pltpu.CompilerParams(vmem_limit_bytes=VMEM_LIMIT)
     plane = (n // 2, ROWS * dpc + TILE, channels)
-    half = (n // 4, ROWS * dpc + TILE, channels)
+    half = (len(FAR), ROWS * dpc + TILE, channels)
     lots = n * 2 * ROWS
     mine = (STATIONS * dpc + TILE, channels)
     sems = pltpu.SemaphoreType.DMA((len(PARTS), n // 4))
@@ -469,11 +512,11 @@
         )
         return x
 
-    got = gather(n, piece, powers_beside, 14)
-    g, onehot, sel = call(
+    got = gather(n, piece, powers_beside)
+    g, onehot = call(
         first_own_kernel,
         (me, *got),
-        [shape(*mine), shape(STATIONS, lots, dtype=BF16), shape(lots, width)],
+        [shape(*mine), shape(STATIONS, lots, dtype=BF16)],
         [(STATIONS * TILE, channels), (n, channels)],
         micros=2,
     )
@@ -487,39 +530,46 @@
     powers = exchange(sums)
     (g,) = call(
         own_kernel,
-        (g, onehot, sel, powers),
+        (g, onehot, powers),
         [shape(*mine)],
-        [(lots, 2 * width)],
+        [(lots, 2 * width), (lots, width)],
     )
 
     def slots(got, pairs):
         return [got[2 * m + c] for m in pairs for c in (0, 1)]
 
     def gather_near(g):
-        near = None
-
-        def beside(x, got):
-            nonlocal near
-            args = (me, first, second, model, vis, x, *slots(got, NEAR))
-            outs = [shape(*vis.shape), shape(*half), shape(*half), shape(*x.shape)]
-            *near, x = call(early_kernel, args, outs, held_half, micros=20, aliases={5: 3})
-            return x
-
-        got = gather(n, g, beside, 14)
-        return near, slots(got, NEAR), slots(got, FAR)
+        acc, products = vis, []
+
+        def work(pairs):
+            def beside(x, got):
+                nonlocal acc
+                args = (me, first, second, model, acc, x, *slots(got, pairs))
+                size = (len(pairs),) + plane[1:]
+                outs = [shape(*vis.shape), shape(*size), shape(*size), shape(*x.shape)]
+                part = pltpu.VMEM((len(pairs) * dpc,) + model.shape[1:], BF16)
+                kernel = lambda n, dpc, *refs: early_kernel(n, dpc, pairs, *refs)
+                acc, re, im, x = call(kernel, args, outs, [part, sems])
+                products.extend([re, im])
+                return x
+
+            return beside
+
+        got = gather(n, g, work(NEAR), work(OWN))
+        return acc, products, slots(got, FAR + NEAR + OWN)
 
     for step in range(1, ITERS):
-        near, _, far_slots = gather_near(g)
-        sel, den = call(
+        acc, products, got = gather_near(g)
+        (den,) = call(
             prepare_kernel,
             (g, onehot, powers),
-            [shape(lots, width), shape(STATIONS, width)],
-            [(lots, width)],
+            [shape(STATIONS, width)],
+            [(lots, width)] * 2,
             micros=2,
         )
         (sums,) = call(
             later_pass_kernel,
-            (me, first, second, model, mask, power, *near, *far_slots),
+            (me, first, second, model, mask, power, acc, *products, *got[: 2 * len(FAR)]),
             [shape(n, ROWS * dpc, channels)],
             held + [half] * 2 + [plane] * 2,
             micros=7,
@@ -527,14 +577,14 @@
         sums = exchange(sums)
         (g,) = call(
             later_own_kernel,
-            (g, onehot, sel, den, sums),
+            (g, onehot, den, sums),
             [shape(*mine)],
-            [(lots, width)],
+            [(lots, width)] * 2,
         )
-    near, near_slots, far_slots = gather_near(g)
+    acc, products, got = gather_near(g)
     residual, gains = call(
         last_kernel,
-        (me, first, second, model, mask, near[0], *far_slots, *near_slots),
+        (me, first, second, model, mask, acc, *got),
         [shape(*vis.shape), shape(2, *gre.shape)],
         held_half + [half] * 2,
         micros=4,

time: 166 us -> 167 us (level)
  starting transfers between devices: 48.9 us -> 63.1 us
  waiting for transfers between devices: 55.2 us -> 41 us
  local copies, waits for them, and re-layouts: 13.2 us -> 8.44 us
  Pallas kernels: 47 us -> 51.2 us
    ppermute x45, waiting for transfers between devices: 25.7 us -> 8.68 us  [send(): return lax.ppermute(x, 'bl', [(i, i ^ o) for i in range(n)])]
    ppermute x45, starting transfers between devices: 38.9 us -> 52.2 us  [send(): return lax.ppermute(x, 'bl', [(i, i ^ o) for i in range(n)])]
    unnamed x46 -> x38, local copies, waits for them, and re-layouts: 13.2 us -> 8.44 us
    pallas_call x11 -> x13, Pallas kernels: 47 us -> 51.2 us  [call(): pl.pallas_call(functools.partial(kernel, n, dpc), in_specs=[place(x) for...]
    all_to_all x2, waiting for transfers between devices: 29.5 us -> 32.3 us  [exchange(): return lax.all_to_all(x, 'bl', split_axis=0, concat_axis=0, tiled=True)]
  transfers between devices with their start and end apart: 47 -> 47, of which waited for: 13 -> 14; matrix products, arithmetic and copies ran while one was open for 0% -> 0% of each run, Pallas kernels for 11% -> 13%
where the time goes in v7:
time: 167 us; the launch traced here: 165 us
  starting transfers between devices  63.1 us (38%)
  Pallas kernels  51.2 us (31%)
  waiting for transfers between devices  41 us (25%)
  local copies, waits for them, and re-layouts  8.44 us (5%)
    ppermute x45, starting transfers between devices, send(): return lax.ppermute(x, 'bl', [(i, i ^ o) for i in range(n)])  52.2 us
    pallas_call x13, Pallas kernels, call(): pl.pallas_call(functools.partial(kernel, n, dpc), in_specs=[place(x) for...  51.2 us
    all_to_all x2, waiting for transfers between devices, exchange(): return lax.all_to_all(x, 'bl', split_axis=0, concat_axis=0, tiled=True)  32.3 us
    all_to_all x2, starting transfers between devices, exchange(): return lax.all_to_all(x, 'bl', split_axis=0, concat_axis=0, tiled=True)  10.9 us
    ppermute x45, waiting for transfers between devices, send(): return lax.ppermute(x, 'bl', [(i, i ^ o) for i in range(n)])  8.68 us
    unnamed x38, local copies, waits for them, and re-layouts  8.44 us
  transfers between devices with their start and end apart: 47, of which 14 were waited for; matrix products, arithmetic and copies ran while one was open for 0% of the time, Pallas kernels for 13%

profile of v7, /device:TPU:9, one launch (start us, length us, event | category | flops | bytes accessed | tf_op | source)
XLA Modules:
  0.0 164.8 jit_solution(9934091797512524394)
XLA Ops:
  1.9 1.5 shard_map.86.rest_0_
  3.5 2.6 %collective-permute-start.7 = (f32[328,128]{1,0:T(8,128)S(1)}, f32[328,128]{1,0:T(8,128)S(1)}, u32[]{:S(2)}, u32[]{:S(2)}) collective-permute-start(f32[328,128]{1,0:T(8,128)S(1)} %shard_map.86.rest_0_), channel_id=1, source_target_pairs={{0,12},{1,13},{2,14},{3,15},{4,8},{5,9},{6,10},{7,11},{8,4},{9,5},... | collective-permute-start | bytes 503816 | tf_op jit(solution)/shard_map/ppermute | solution.py:453
  6.1 1.2 collective-permute-start.1
  7.3 1.4 collective-permute-done.3.rest_4_
  8.7 1.2 collective-permute-start.5
  9.9 4.6 %collective-permute-start.8 = (f32[328,128]{1,0:T(8,128)S(1)}, f32[328,128]{1,0:T(8,128)S(1)}, u32[]{:S(2)}, u32[]{:S(2)}) collective-permute-start(f32[328,128]{1,0:T(8,128)S(1)} %collective-permute-done.7.rest_12_), channel_id=1, source_target_pairs={{0,4},{1,5},{2,6},{3,7},{4,0},{5,1},{6,2},{7,3},{8,12},{9,13},{10,... | collective-permute-start | bytes 503816 | tf_op jit(solution)/shard_map/ppermute | solution.py:453
  14.5 1.9 %collective-permute-start = (f32[328,128]{1,0:T(8,128)S(1)}, f32[328,128]{1,0:T(8,128)S(1)}, u32[]{:S(2)}, u32[]{:S(2)}) collective-permute-start(f32[328,128]{1,0:T(8,128)S(1)} %shard_map.86.rest_0_), channel_id=1, source_target_pairs={{0,1},{1,0},{2,3},{3,2},{4,5},{5,4},{6,7},{7,6},{8,9},{9,8},{10,11... | collective-permute-start | bytes 503816 | tf_op jit(solution)/shard_map/ppermute | solution.py:453
  16.9 1.2 collective-permute-start.13
  18.5 0.9 copy-done.1
  19.4 5.6 %shard_map.87 = (f32[8,88,128]{2,1,0:T(8,128)S(1)}, f32[328,128]{1,0:T(8,128)S(1)}) custom-call(bf16[40,2,15,32,128]{4,3,2,1,0:T(8,128)(2,1)} %model_hbm.7, s32[15,32,128]{2,1,0:T(8,128)S(1)} %copy-done.1, f32[328,128]{1,0:T(8,128)S(1)} %collective-permute-done.5.unused_in), custom_call_target="tpu_custom_call", output_to_operand_aliasing={{1}: (2, {})} | custom-call | bytes 73800000 | tf_op jit(solution)/shard_map/pallas_call | solution.py:487
  25.0 3.4 %collective-permute-start.12 = (f32[328,128]{1,0:T(8,128)S(1)}, f32[328,128]{1,0:T(8,128)S(1)}, u32[]{:S(2)}, u32[]{:S(2)}) collective-permute-start(f32[328,128]{1,0:T(8,128)S(1)} %collective-permute-done.7.rest_12_), channel_id=1, source_target_pairs={{0,1},{1,0},{2,3},{3,2},{4,5},{5,4},{6,7},{7,6},{8,9},{9,8},{10,11... | collective-permute-start | bytes 503816 | tf_op jit(solution)/shard_map/ppermute | solution.py:453
  30.7 10.8 %shard_map.89 = f32[16,120,128]{2,1,0:T(8,128)} custom-call(s32[1]{0:T(128)} %bitcast.me_ref.refs_0_, s32[15]{0:T(128)S(1)} %copy-done.16, s32[15]{0:T(128)S(1)} %copy-done.18, bf16[40,2,15,32,128]{4,3,2,1,0:T(8,128)(2,1)} %model_hbm.7, f32[2,15,32,128]{3,2,1,0:T(8,128)S(1)} %copy-done, s32[15,32,128]{2,1,0:T(8,128)S(1)} %copy-done.2, ...), custom_call_target="tpu_custom_call" | custom-call | bytes 33210000 | tf_op jit(solution)/shard_map/pallas_call | solution.py:487
  41.5 5.6 %all-to-all-start = ((f32[16,120,128]{2,1,0:T(8,128)}), f32[16,120,128]{2,1,0:T(8,128)S(1)}, u32[]{:S(2)}, u32[]{:S(2)}) async-start(f32[16,120,128]{2,1,0:T(8,128)} %shard_map.89), calls=%async_computation | async-start | bytes 1966080 | tf_op jit(solution)/shard_map/all_to_all | solution.py:448
  48.1 0.9 copy-done.6
  49.9 0.9 copy-done.10
  51.7 1.3 shard_map.88
  53.8 16.9 %all-to-all-done.sums = f32[16,120,128]{2,1,0:T(8,128)S(1)} async-done(((f32[16,120,128]{2,1,0:T(8,128)}), f32[16,120,128]{2,1,0:T(8,128)S(1)}, u32[]{:S(2)}, u32[]{:S(2)}) %all-to-all-start) | async-done | bytes 983072 | tf_op jit(solution)/shard_map/all_to_all | solution.py:448
  70.7 0.9 copy-done.14
  71.6 2.2 %shard_map.90.g_ref.refs_5_.refs_6_.g_in = f32[328,128]{1,0:T(8,128)S(1)} custom-call(f32[328,128]{1,0:T(8,128)S(1)} %copy-done.14, bf16[64,512]{1,0:T(8,128)(2,1)S(1)} %get-tuple-element.22.onehot_ref, f32[16,120,128]{2,1,0:T(8,128)S(1)} %all-to-all-done.sums), custom_call_target="tpu_custom_call" | custom-call | bytes 3690000 | tf_op jit(solution)/shard_map/pallas_call | solution.py:487
  73.9 1.2 collective-permute-start.18
  75.1 1.5 collective-permute-start.21
  76.6 2.4 %shard_map.92 = (f32[2,15,32,128]{3,2,1,0:T(8,128)S(1)}, f32[1,88,128]{2,1,0:T(8,128)S(1)}, f32[1,88,128]{2,1,0:T(8,128)S(1)}, f32[328,128]{1,0:T(8,128)S(1)}) custom-call(s32[1]{0:T(128)} %bitcast.me_ref.refs_0_, s32[15]{0:T(128)S(1)} %copy-done.16, s32[15]{0:T(128)S(1)} %copy-done.18, bf16[40,2,15,32,128]{4,3,2,1,0:T(8,128)(2,1)} %model_hbm.7, ...), custom_call_target="tpu_custom_call" | custom-call | bytes 3690000 | tf_op jit(solution)/shard_map/pallas_call | solution.py:487
  79.3 1.4 collective-permute-start.17
  80.7 1.2 collective-permute-start.24
  81.9 1.7 %collective-permute-start.20 = (f32[328,128]{1,0:T(8,128)S(1)}, f32[328,128]{1,0:T(8,128)S(1)}, u32[]{:S(2)}, u32[]{:S(2)}) collective-permute-start(f32[328,128]{1,0:T(8,128)S(1)} %collective-permute-done.16.refs_8_), channel_id=1, source_target_pairs={{0,1},{1,0},{2,3},{3,2},{4,5},{5,4},{6,7},{7,6},{8,9},{9,8},{10,11... | collective-permute-start | bytes 503816 | tf_op jit(solution)/shard_map/ppermute | solution.py:453
  83.6 6.0 %collective-permute-start.22 = (f32[328,128]{1,0:T(8,128)S(1)}, f32[328,128]{1,0:T(8,128)S(1)}, u32[]{:S(2)}, u32[]{:S(2)}) collective-permute-start(f32[328,128]{1,0:T(8,128)S(1)} %collective-permute-done.21.refs_10_), channel_id=1, source_target_pairs={{0,1},{1,0},{2,3},{3,2},{4,5},{5,4},{6,7},{7,6},{8,9},{9,8},{10,11... | collective-permute-start | bytes 503816 | tf_op jit(solution)/shard_map/ppermute | solution.py:453
  90.2 1.2 collective-permute-start.26
  91.4 3.7 %shard_map.93 = (f32[2,15,32,128]{3,2,1,0:T(8,128)S(1)}, f32[3,88,128]{2,1,0:T(8,128)S(1)}, f32[3,88,128]{2,1,0:T(8,128)S(1)}, f32[328,128]{1,0:T(8,128)S(1)}) custom-call(s32[1]{0:T(128)} %bitcast.me_ref.refs_0_, s32[15]{0:T(128)S(1)} %copy-done.16, s32[15]{0:T(128)S(1)} %copy-done.18, bf16[40,2,15,32,128]{4,3,2,1,0:T(8,128)(2,1)} %model_hbm.7, ...), custom_call_target="tpu_custom_call" | custom-call | bytes 3690000 | tf_op jit(solution)/shard_map/pallas_call | solution.py:487
  95.1 1.3 collective-permute-start.23
  96.9 2.2 %collective-permute-done.26.rest_4_ = f32[328,128]{1,0:T(8,128)S(1)} collective-permute-done((f32[328,128]{1,0:T(8,128)S(1)}, f32[328,128]{1,0:T(8,128)S(1)}, u32[]{:S(2)}, u32[]{:S(2)}) %collective-permute-start.26) | collective-permute-done | bytes 167968 | tf_op jit(solution)/shard_map/ppermute | solution.py:453
  99.9 1.0 collective-permute-done.27.rest_5_
  100.9 8.6 %shard_map.94 = f32[16,80,128]{2,1,0:T(8,128)} custom-call(s32[1]{0:T(128)} %bitcast.me_ref.refs_0_, s32[15]{0:T(128)S(1)} %copy-done.16, s32[15]{0:T(128)S(1)} %copy-done.18, bf16[40,2,15,32,128]{4,3,2,1,0:T(8,128)(2,1)} %model_hbm.7, s32[15,32,128]{2,1,0:T(8,128)S(1)} %copy-done.2, f32[8,88,128]{2,1,0:T(8,128)S(1)} %get-tuple-element.23.power_ref, ...), custom_call_target="tpu_custom_call" | custom-call | bytes 25830000 | tf_op jit(solution)/shard_map/pallas_call | solution.py:487
  109.6 5.3 %all-to-all-start.1 = ((f32[16,80,128]{2,1,0:T(8,128)}), f32[16,80,128]{2,1,0:T(8,128)S(1)}, u32[]{:S(2)}, u32[]{:S(2)}) async-start(f32[16,80,128]{2,1,0:T(8,128)} %shard_map.94), calls=%async_computation.1 | async-start | bytes 1310720 | tf_op jit(solution)/shard_map/all_to_all | solution.py:448
  114.8 1.4 shard_map.91.den_ref
  116.3 15.4 %all-to-all-done.1.sums = f32[16,80,128]{2,1,0:T(8,128)S(1)} async-done(((f32[16,80,128]{2,1,0:T(8,128)}), f32[16,80,128]{2,1,0:T(8,128)S(1)}, u32[]{:S(2)}, u32[]{:S(2)}) %all-to-all-start.1) | async-done | bytes 655392 | tf_op jit(solution)/shard_map/all_to_all | solution.py:448
  131.7 1.5 shard_map.95.refs_5_.refs_6_.rest_14_
  134.2 1.4 collective-permute-start.36
  135.7 3.0 %shard_map.96 = (f32[2,15,32,128]{3,2,1,0:T(8,128)S(1)}, f32[1,88,128]{2,1,0:T(8,128)}, f32[1,88,128]{2,1,0:T(8,128)}, f32[328,128]{1,0:T(8,128)S(1)}) custom-call(s32[1]{0:T(128)} %bitcast.me_ref.refs_0_, s32[15]{0:T(128)S(1)} %copy-done.16, s32[15]{0:T(128)S(1)} %copy-done.18, bf16[40,2,15,32,128]{4,3,2,1,0:T(8,128)(2,1)} %model_hbm.7, ...), custom_call_target="tpu_custom_call" | custom-call | bytes 3690000 | tf_op jit(solution)/shard_map/pallas_call | solution.py:487
  138.8 1.0 collective-permute-start.32
  139.8 1.7 %collective-permute-start.39 = (f32[328,128]{1,0:T(8,128)S(1)}, f32[328,128]{1,0:T(8,128)S(1)}, u32[]{:S(2)}, u32[]{:S(2)}) collective-permute-start(f32[328,128]{1,0:T(8,128)S(1)} %get-tuple-element.35), channel_id=1, source_target_pairs={{0,8},{1,9},{2,10},{3,11},{4,12},{5,13},{6,14},{7,15},{8,0},{9,1},... | collective-permute-start | bytes 503816 | tf_op jit(solution)/shard_map/ppermute | solution.py:453
  141.5 1.8 %collective-permute-start.35 = (f32[328,128]{1,0:T(8,128)S(1)}, f32[328,128]{1,0:T(8,128)S(1)}, u32[]{:S(2)}, u32[]{:S(2)}) collective-permute-start(f32[328,128]{1,0:T(8,128)S(1)} %collective-permute-done.31.refs_8_.rest_10_), channel_id=1, source_target_pairs={{0,1},{1,0},{2,3},{3,2},{4,5},{5,4},{6,7},{7,6},{8,9},{9,8},{10,11... | collective-permute-start | bytes 503816 | tf_op jit(solution)/shard_map/ppermute | solution.py:453
  143.3 5.0 %collective-permute-start.37 = (f32[328,128]{1,0:T(8,128)S(1)}, f32[328,128]{1,0:T(8,128)S(1)}, u32[]{:S(2)}, u32[]{:S(2)}) collective-permute-start(f32[328,128]{1,0:T(8,128)S(1)} %collective-permute-done.36.refs_10_.rest_12_), channel_id=1, source_target_pairs={{0,1},{1,0},{2,3},{3,2},{4,5},{5,4},{6,7},{7,6},{8,9},{9,8},{10,11... | collective-permute-start | bytes 503816 | tf_op jit(solution)/shard_map/ppermute | solution.py:453
  148.4 1.3 collective-permute-start.43
  150.5 4.3 %shard_map.97 = (f32[2,15,32,128]{3,2,1,0:T(8,128)S(1)}, f32[3,88,128]{2,1,0:T(8,128)}, f32[3,88,128]{2,1,0:T(8,128)}, f32[328,128]{1,0:T(8,128)S(1)}) custom-call(s32[1]{0:T(128)} %bitcast.me_ref.refs_0_, s32[15]{0:T(128)S(1)} %copy-done.16, s32[15]{0:T(128)S(1)} %copy-done.18, bf16[40,2,15,32,128]{4,3,2,1,0:T(8,128)(2,1)} %model_hbm.7, ...), custom_call_target="tpu_custom_call" | custom-call | bytes 3690000 | tf_op jit(solution)/shard_map/pallas_call | solution.py:487
  154.8 1.3 collective-permute-start.38
  156.6 1.3 collective-permute-done.41.rest_4_
  158.7 1.0 collective-permute-done.42.rest_5_
  159.7 5.0 %shard_map.98 = (f32[2,15,32,128]{3,2,1,0:T(8,128)}, f32[2,160,128]{2,1,0:T(8,128)}) custom-call(s32[1]{0:T(128)} %bitcast.me_ref.refs_0_, s32[15]{0:T(128)S(1)} %copy-done.16, s32[15]{0:T(128)S(1)} %copy-done.18, bf16[40,2,15,32,128]{4,3,2,1,0:T(8,128)(2,1)} %model_hbm.7, s32[15,32,128]{2,1,0:T(8,128)S(1)} %copy-done.2, ...), custom_call_target="tpu_custom_call" | custom-call | bytes 14760000 | tf_op jit(solution)/shard_map/pallas_call | solution.py:487
  (97 shorter events, 13.7 us)
Async XLA Ops:
  1.9 28.8 %copy-start = (f32[2,15,32,128]{3,2,1,0:T(8,128)S(1)}, f32[2,15,32,128]{3,2,1,0:T(8,128)}, u32[]{:S(2)}) copy-start(f32[2,15,32,128]{3,2,1,0:T(8,128)} %refs_4_.3) | copy-start | bytes 1474564
  3.4 5.2 %collective-permute-start.3 = (f32[328,128]{1,0:T(8,128)S(1)}, f32[328,128]{1,0:T(8,128)S(1)}, u32[]{:S(2)}, u32[]{:S(2)}) collective-permute-start(f32[328,128]{1,0:T(8,128)S(1)} %shard_map.86.rest_0_), channel_id=1, source_target_pairs={{0,4},{1,5},{2,6},{3,7},{4,0},{5,1},{6,2},{7,3},{8,12},{9,13},{10,... | collective-permute-start | bytes 503816 | tf_op jit(solution)/shard_map/ppermute | solution.py:453
  3.5 6.4 %collective-permute-start.7 = (f32[328,128]{1,0:T(8,128)S(1)}, f32[328,128]{1,0:T(8,128)S(1)}, u32[]{:S(2)}, u32[]{:S(2)}) collective-permute-start(f32[328,128]{1,0:T(8,128)S(1)} %shard_map.86.rest_0_), channel_id=1, source_target_pairs={{0,12},{1,13},{2,14},{3,15},{4,8},{5,9},{6,10},{7,11},{8,4},{9,5},... | collective-permute-start | bytes 503816 | tf_op jit(solution)/shard_map/ppermute | solution.py:453
  6.1 10.3 %collective-permute-start.1 = (f32[328,128]{1,0:T(8,128)S(1)}, f32[328,128]{1,0:T(8,128)S(1)}, u32[]{:S(2)}, u32[]{:S(2)}) collective-permute-start(f32[328,128]{1,0:T(8,128)S(1)} %shard_map.86.rest_0_), channel_id=1, source_target_pairs={{0,2},{1,3},{2,0},{3,1},{4,6},{5,7},{6,4},{7,5},{8,10},{9,11},{10,... | collective-permute-start | bytes 503816 | tf_op jit(solution)/shard_map/ppermute | solution.py:453
  8.7 8.2 %collective-permute-start.5 = (f32[328,128]{1,0:T(8,128)S(1)}, f32[328,128]{1,0:T(8,128)S(1)}, u32[]{:S(2)}, u32[]{:S(2)}) collective-permute-start(f32[328,128]{1,0:T(8,128)S(1)} %collective-permute-done.3.rest_4_), channel_id=1, source_target_pairs={{0,2},{1,3},{2,0},{3,1},{4,6},{5,7},{6,4},{7,5},{8,10},{9,11},{10,... | collective-permute-start | bytes 503816 | tf_op jit(solution)/shard_map/ppermute | solution.py:453
  9.9 8.2 %collective-permute-start.8 = (f32[328,128]{1,0:T(8,128)S(1)}, f32[328,128]{1,0:T(8,128)S(1)}, u32[]{:S(2)}, u32[]{:S(2)}) collective-permute-start(f32[328,128]{1,0:T(8,128)S(1)} %collective-permute-done.7.rest_12_), channel_id=1, source_target_pairs={{0,4},{1,5},{2,6},{3,7},{4,0},{5,1},{6,2},{7,3},{8,12},{9,13},{10,... | collective-permute-start | bytes 503816 | tf_op jit(solution)/shard_map/ppermute | solution.py:453
  14.5 10.5 %collective-permute-start = (f32[328,128]{1,0:T(8,128)S(1)}, f32[328,128]{1,0:T(8,128)S(1)}, u32[]{:S(2)}, u32[]{:S(2)}) collective-permute-start(f32[328,128]{1,0:T(8,128)S(1)} %shard_map.86.rest_0_), channel_id=1, source_target_pairs={{0,1},{1,0},{2,3},{3,2},{4,5},{5,4},{6,7},{7,6},{8,9},{9,8},{10,11... | collective-permute-start | bytes 503816 | tf_op jit(solution)/shard_map/ppermute | solution.py:453
  16.4 12.0 %collective-permute-start.2 = (f32[328,128]{1,0:T(8,128)S(1)}, f32[328,128]{1,0:T(8,128)S(1)}, u32[]{:S(2)}, u32[]{:S(2)}) collective-permute-start(f32[328,128]{1,0:T(8,128)S(1)} %collective-permute-done.1.rest_2_), channel_id=1, source_target_pairs={{0,1},{1,0},{2,3},{3,2},{4,5},{5,4},{6,7},{7,6},{8,9},{9,8},{10,11... | collective-permute-start | bytes 503816 | tf_op jit(solution)/shard_map/ppermute | solution.py:453
  16.4 12.1 %collective-permute-start.4 = (f32[328,128]{1,0:T(8,128)S(1)}, f32[328,128]{1,0:T(8,128)S(1)}, u32[]{:S(2)}, u32[]{:S(2)}) collective-permute-start(f32[328,128]{1,0:T(8,128)S(1)} %collective-permute-done.3.rest_4_), channel_id=1, source_target_pairs={{0,1},{1,0},{2,3},{3,2},{4,5},{5,4},{6,7},{7,6},{8,9},{9,8},{10,11... | collective-permute-start | bytes 503816 | tf_op jit(solution)/shard_map/ppermute | solution.py:453
  16.9 12.0 %collective-permute-start.13 = (f32[328,128]{1,0:T(8,128)S(1)}, f32[328,128]{1,0:T(8,128)S(1)}, u32[]{:S(2)}, u32[]{:S(2)}) collective-permute-start(f32[328,128]{1,0:T(8,128)S(1)} %collective-permute-done.7.rest_12_), channel_id=1, source_target_pairs={{0,2},{1,3},{2,0},{3,1},{4,6},{5,7},{6,4},{7,5},{8,10},{9,11},{10,... | collective-permute-start | bytes 503816 | tf_op jit(solution)/shard_map/ppermute | solution.py:453
  18.1 10.9 %collective-permute-start.10 = (f32[328,128]{1,0:T(8,128)S(1)}, f32[328,128]{1,0:T(8,128)S(1)}, u32[]{:S(2)}, u32[]{:S(2)}) collective-permute-start(f32[328,128]{1,0:T(8,128)S(1)} %collective-permute-done.8.rest_8_), channel_id=1, source_target_pairs={{0,2},{1,3},{2,0},{3,1},{4,6},{5,7},{6,4},{7,5},{8,10},{9,11},{10,... | collective-permute-start | bytes 503816 | tf_op jit(solution)/shard_map/ppermute | solution.py:453
  25.0 4.4 %collective-permute-start.12 = (f32[328,128]{1,0:T(8,128)S(1)}, f32[328,128]{1,0:T(8,128)S(1)}, u32[]{:S(2)}, u32[]{:S(2)}) collective-permute-start(f32[328,128]{1,0:T(8,128)S(1)} %collective-permute-done.7.rest_12_), channel_id=1, source_target_pairs={{0,1},{1,0},{2,3},{3,2},{4,5},{5,4},{6,7},{7,6},{8,9},{9,8},{10,11... | collective-permute-start | bytes 503816 | tf_op jit(solution)/shard_map/ppermute | solution.py:453
  28.4 1.4 collective-permute-start.6
  28.5 1.7 %collective-permute-start.9 = (f32[328,128]{1,0:T(8,128)S(1)}, f32[328,128]{1,0:T(8,128)}, u32[]{:S(2)}, u32[]{:S(2)}) collective-permute-start(f32[328,128]{1,0:T(8,128)S(1)} %collective-permute-done.8.rest_8_), channel_id=1, source_target_pairs={{0,1},{1,0},{2,3},{3,2},{4,5},{5,4},{6,7},{7,6},{8,9},{9,8},{10,11... | collective-permute-start | bytes 503816 | tf_op jit(solution)/shard_map/ppermute | solution.py:453
  28.9 1.5 collective-permute-start.14
  29.0 1.7 %collective-permute-start.11 = (f32[328,128]{1,0:T(8,128)S(1)}, f32[328,128]{1,0:T(8,128)}, u32[]{:S(2)}, u32[]{:S(2)}) collective-permute-start(f32[328,128]{1,0:T(8,128)S(1)} %collective-permute-done.10.rest_10_), channel_id=1, source_target_pairs={{0,1},{1,0},{2,3},{3,2},{4,5},{5,4},{6,7},{7,6},{8,9},{9,8},{10,11... | collective-permute-start | bytes 503816 | tf_op jit(solution)/shard_map/ppermute | solution.py:453
  41.5 29.1 %all-to-all-start = ((f32[16,120,128]{2,1,0:T(8,128)}), f32[16,120,128]{2,1,0:T(8,128)S(1)}, u32[]{:S(2)}, u32[]{:S(2)}) async-start(f32[16,120,128]{2,1,0:T(8,128)} %shard_map.89), calls=%async_computation | async-start | bytes 1966080 | tf_op jit(solution)/shard_map/all_to_all | solution.py:448
  73.7 2.9 %collective-permute-start.15 = (f32[328,128]{1,0:T(8,128)S(1)}, f32[328,128]{1,0:T(8,128)S(1)}, u32[]{:S(2)}, u32[]{:S(2)}) collective-permute-start(f32[328,128]{1,0:T(8,128)S(1)} %shard_map.90.g_ref.refs_5_.refs_6_.g_in), channel_id=1, source_target_pairs={{0,1},{1,0},{2,3},{3,2},{4,5},{5,4},{6,7},{7,6},{8,9},{9,8},{10,11... | collective-permute-start | bytes 503816 | tf_op jit(solution)/shard_map/ppermute | solution.py:453
  73.8 5.5 %collective-permute-start.16 = (f32[328,128]{1,0:T(8,128)S(1)}, f32[328,128]{1,0:T(8,128)S(1)}, u32[]{:S(2)}, u32[]{:S(2)}) collective-permute-start(f32[328,128]{1,0:T(8,128)S(1)} %shard_map.90.g_ref.refs_5_.refs_6_.g_in), channel_id=1, source_target_pairs={{0,4},{1,5},{2,6},{3,7},{4,0},{5,1},{6,2},{7,3},{8,12},{9,13},{10,... | collective-permute-start | bytes 503816 | tf_op jit(solution)/shard_map/ppermute | solution.py:453
  73.9 9.7 %collective-permute-start.18 = (f32[328,128]{1,0:T(8,128)S(1)}, f32[328,128]{1,0:T(8,128)S(1)}, u32[]{:S(2)}, u32[]{:S(2)}) collective-permute-start(f32[328,128]{1,0:T(8,128)S(1)} %shard_map.90.g_ref.refs_5_.refs_6_.g_in), channel_id=1, source_target_pairs={{0,2},{1,3},{2,0},{3,1},{4,6},{5,7},{6,4},{7,5},{8,10},{9,11},{10,... | collective-permute-start | bytes 503816 | tf_op jit(solution)/shard_map/ppermute | solution.py:453
  75.1 8.4 %collective-permute-start.21 = (f32[328,128]{1,0:T(8,128)S(1)}, f32[328,128]{1,0:T(8,128)S(1)}, u32[]{:S(2)}, u32[]{:S(2)}) collective-permute-start(f32[328,128]{1,0:T(8,128)S(1)} %shard_map.90.g_ref.refs_5_.refs_6_.g_in), channel_id=1, source_target_pairs={{0,12},{1,13},{2,14},{3,15},{4,8},{5,9},{6,10},{7,11},{8,4},{9,5},... | collective-permute-start | bytes 503816 | tf_op jit(solution)/shard_map/ppermute | solution.py:453
  79.3 10.3 %collective-permute-start.17 = (f32[328,128]{1,0:T(8,128)S(1)}, f32[328,128]{1,0:T(8,128)S(1)}, u32[]{:S(2)}, u32[]{:S(2)}) collective-permute-start(f32[328,128]{1,0:T(8,128)S(1)} %collective-permute-done.16.refs_8_), channel_id=1, source_target_pairs={{0,2},{1,3},{2,0},{3,1},{4,6},{5,7},{6,4},{7,5},{8,10},{9,11},{10,... | collective-permute-start | bytes 503816 | tf_op jit(solution)/shard_map/ppermute | solution.py:453
  80.7 9.5 %collective-permute-start.24 = (f32[328,128]{1,0:T(8,128)S(1)}, f32[328,128]{1,0:T(8,128)S(1)}, u32[]{:S(2)}, u32[]{:S(2)}) collective-permute-start(f32[328,128]{1,0:T(8,128)S(1)} %get-tuple-element.31), channel_id=1, source_target_pairs={{0,8},{1,9},{2,10},{3,11},{4,12},{5,13},{6,14},{7,15},{8,0},{9,1},... | collective-permute-start | bytes 503816 | tf_op jit(solution)/shard_map/ppermute | solution.py:453
  81.9 9.5 %collective-permute-start.20 = (f32[328,128]{1,0:T(8,128)S(1)}, f32[328,128]{1,0:T(8,128)S(1)}, u32[]{:S(2)}, u32[]{:S(2)}) collective-permute-start(f32[328,128]{1,0:T(8,128)S(1)} %collective-permute-done.16.refs_8_), channel_id=1, source_target_pairs={{0,1},{1,0},{2,3},{3,2},{4,5},{5,4},{6,7},{7,6},{8,9},{9,8},{10,11... | collective-permute-start | bytes 503816 | tf_op jit(solution)/shard_map/ppermute | solution.py:453
  83.6 7.8 %collective-permute-start.19 = (f32[328,128]{1,0:T(8,128)S(1)}, f32[328,128]{1,0:T(8,128)S(1)}, u32[]{:S(2)}, u32[]{:S(2)}) collective-permute-start(f32[328,128]{1,0:T(8,128)S(1)} %collective-permute-done.18.refs_6_), channel_id=1, source_target_pairs={{0,1},{1,0},{2,3},{3,2},{4,5},{5,4},{6,7},{7,6},{8,9},{9,8},{10,11... | collective-permute-start | bytes 503816 | tf_op jit(solution)/shard_map/ppermute | solution.py:453
  83.6 7.8 %collective-permute-start.22 = (f32[328,128]{1,0:T(8,128)S(1)}, f32[328,128]{1,0:T(8,128)S(1)}, u32[]{:S(2)}, u32[]{:S(2)}) collective-permute-start(f32[328,128]{1,0:T(8,128)S(1)} %collective-permute-done.21.refs_10_), channel_id=1, source_target_pairs={{0,1},{1,0},{2,3},{3,2},{4,5},{5,4},{6,7},{7,6},{8,9},{9,8},{10,11... | collective-permute-start | bytes 503816 | tf_op jit(solution)/shard_map/ppermute | solution.py:453
  89.6 6.9 %collective-permute-start.28 = (f32[328,128]{1,0:T(8,128)S(1)}, f32[328,128]{1,0:T(8,128)S(1)}, u32[]{:S(2)}, u32[]{:S(2)}) collective-permute-start(f32[328,128]{1,0:T(8,128)S(1)} %collective-permute-done.21.refs_10_), channel_id=1, source_target_pairs={{0,2},{1,3},{2,0},{3,1},{4,6},{5,7},{6,4},{7,5},{8,10},{9,11},{10,... | collective-permute-start | bytes 503816 | tf_op jit(solution)/shard_map/ppermute | solution.py:453
  90.2 8.9 %collective-permute-start.26 = (f32[328,128]{1,0:T(8,128)S(1)}, f32[328,128]{1,0:T(8,128)S(1)}, u32[]{:S(2)}, u32[]{:S(2)}) collective-permute-start(f32[328,128]{1,0:T(8,128)S(1)} %collective-permute-done.24.rest_2_), channel_id=1, source_target_pairs={{0,2},{1,3},{2,0},{3,1},{4,6},{5,7},{6,4},{7,5},{8,10},{9,11},{10,... | collective-permute-start | bytes 503816 | tf_op jit(solution)/shard_map/ppermute | solution.py:453
  95.1 4.8 %collective-permute-start.23 = (f32[328,128]{1,0:T(8,128)S(1)}, f32[328,128]{1,0:T(8,128)S(1)}, u32[]{:S(2)}, u32[]{:S(2)}) collective-permute-start(f32[328,128]{1,0:T(8,128)S(1)} %get-tuple-element.30.rest_0_), channel_id=1, source_target_pairs={{0,1},{1,0},{2,3},{3,2},{4,5},{5,4},{6,7},{7,6},{8,9},{9,8},{10,11... | collective-permute-start | bytes 503816 | tf_op jit(solution)/shard_map/ppermute | solution.py:453
  96.4 3.5 %collective-permute-start.25 = (f32[328,128]{1,0:T(8,128)S(1)}, f32[328,128]{1,0:T(8,128)S(1)}, u32[]{:S(2)}, u32[]{:S(2)}) collective-permute-start(f32[328,128]{1,0:T(8,128)S(1)} %collective-permute-done.24.rest_2_), channel_id=1, source_target_pairs={{0,1},{1,0},{2,3},{3,2},{4,5},{5,4},{6,7},{7,6},{8,9},{9,8},{10,11... | collective-permute-start | bytes 503816 | tf_op jit(solution)/shard_map/ppermute | solution.py:453
  96.5 3.4 %collective-permute-start.29 = (f32[328,128]{1,0:T(8,128)S(1)}, f32[328,128]{1,0:T(8,128)S(1)}, u32[]{:S(2)}, u32[]{:S(2)}) collective-permute-start(f32[328,128]{1,0:T(8,128)S(1)} %collective-permute-done.28.rest_6_), channel_id=1, source_target_pairs={{0,1},{1,0},{2,3},{3,2},{4,5},{5,4},{6,7},{7,6},{8,9},{9,8},{10,11... | collective-permute-start | bytes 503816 | tf_op jit(solution)/shard_map/ppermute | solution.py:453
  99.1 1.8 %collective-permute-start.27 = (f32[328,128]{1,0:T(8,128)S(1)}, f32[328,128]{1,0:T(8,128)S(1)}, u32[]{:S(2)}, u32[]{:S(2)}) collective-permute-start(f32[328,128]{1,0:T(8,128)S(1)} %collective-permute-done.26.rest_4_), channel_id=1, source_target_pairs={{0,1},{1,0},{2,3},{3,2},{4,5},{5,4},{6,7},{7,6},{8,9},{9,8},{10,11... | collective-permute-start | bytes 503816 | tf_op jit(solution)/shard_map/ppermute | solution.py:453
  109.6 22.1 %all-to-all-start.1 = ((f32[16,80,128]{2,1,0:T(8,128)}), f32[16,80,128]{2,1,0:T(8,128)S(1)}, u32[]{:S(2)}, u32[]{:S(2)}) async-start(f32[16,80,128]{2,1,0:T(8,128)} %shard_map.94), calls=%async_computation.1 | async-start | bytes 1310720 | tf_op jit(solution)/shard_map/all_to_all | solution.py:448
  133.2 2.5 %collective-permute-start.30 = (f32[328,128]{1,0:T(8,128)S(1)}, f32[328,128]{1,0:T(8,128)S(1)}, u32[]{:S(2)}, u32[]{:S(2)}) collective-permute-start(f32[328,128]{1,0:T(8,128)S(1)} %shard_map.95.refs_5_.refs_6_.rest_14_), channel_id=1, source_target_pairs={{0,1},{1,0},{2,3},{3,2},{4,5},{5,4},{6,7},{7,6},{8,9},{9,8},{10,11... | collective-permute-start | bytes 503816 | tf_op jit(solution)/shard_map/ppermute | solution.py:453
  133.3 5.5 %collective-permute-start.31 = (f32[328,128]{1,0:T(8,128)S(1)}, f32[328,128]{1,0:T(8,128)S(1)}, u32[]{:S(2)}, u32[]{:S(2)}) collective-permute-start(f32[328,128]{1,0:T(8,128)S(1)} %shard_map.95.refs_5_.refs_6_.rest_14_), channel_id=1, source_target_pairs={{0,4},{1,5},{2,6},{3,7},{4,0},{5,1},{6,2},{7,3},{8,12},{9,13},{10,... | collective-permute-start | bytes 503816 | tf_op jit(solution)/shard_map/ppermute | solution.py:453
  133.4 9.9 %collective-permute-start.33 = (f32[328,128]{1,0:T(8,128)S(1)}, f32[328,128]{1,0:T(8,128)S(1)}, u32[]{:S(2)}, u32[]{:S(2)}) collective-permute-start(f32[328,128]{1,0:T(8,128)S(1)} %shard_map.95.refs_5_.refs_6_.rest_14_), channel_id=1, source_target_pairs={{0,2},{1,3},{2,0},{3,1},{4,6},{5,7},{6,4},{7,5},{8,10},{9,11},{10,... | collective-permute-start | bytes 503816 | tf_op jit(solution)/shard_map/ppermute | solution.py:453
  134.2 9.1 %collective-permute-start.36 = (f32[328,128]{1,0:T(8,128)S(1)}, f32[328,128]{1,0:T(8,128)S(1)}, u32[]{:S(2)}, u32[]{:S(2)}) collective-permute-start(f32[328,128]{1,0:T(8,128)S(1)} %shard_map.95.refs_5_.refs_6_.rest_14_), channel_id=1, source_target_pairs={{0,12},{1,13},{2,14},{3,15},{4,8},{5,9},{6,10},{7,11},{8,4},{9,5},... | collective-permute-start | bytes 503816 | tf_op jit(solution)/shard_map/ppermute | solution.py:453
  138.8 9.5 %collective-permute-start.32 = (f32[328,128]{1,0:T(8,128)S(1)}, f32[328,128]{1,0:T(8,128)S(1)}, u32[]{:S(2)}, u32[]{:S(2)}) collective-permute-start(f32[328,128]{1,0:T(8,128)S(1)} %collective-permute-done.31.refs_8_.rest_10_), channel_id=1, source_target_pairs={{0,2},{1,3},{2,0},{3,1},{4,6},{5,7},{6,4},{7,5},{8,10},{9,11},{10,... | collective-permute-start | bytes 503816 | tf_op jit(solution)/shard_map/ppermute | solution.py:453
  139.8 9.8 %collective-permute-start.39 = (f32[328,128]{1,0:T(8,128)S(1)}, f32[328,128]{1,0:T(8,128)S(1)}, u32[]{:S(2)}, u32[]{:S(2)}) collective-permute-start(f32[328,128]{1,0:T(8,128)S(1)} %get-tuple-element.35), channel_id=1, source_target_pairs={{0,8},{1,9},{2,10},{3,11},{4,12},{5,13},{6,14},{7,15},{8,0},{9,1},... | collective-permute-start | bytes 503816 | tf_op jit(solution)/shard_map/ppermute | solution.py:453
  141.5 9.0 %collective-permute-start.35 = (f32[328,128]{1,0:T(8,128)S(1)}, f32[328,128]{1,0:T(8,128)S(1)}, u32[]{:S(2)}, u32[]{:S(2)}) collective-permute-start(f32[328,128]{1,0:T(8,128)S(1)} %collective-permute-done.31.refs_8_.rest_10_), channel_id=1, source_target_pairs={{0,1},{1,0},{2,3},{3,2},{4,5},{5,4},{6,7},{7,6},{8,9},{9,8},{10,11... | collective-permute-start | bytes 503816 | tf_op jit(solution)/shard_map/ppermute | solution.py:453
  143.3 7.2 %collective-permute-start.34 = (f32[328,128]{1,0:T(8,128)S(1)}, f32[328,128]{1,0:T(8,128)S(1)}, u32[]{:S(2)}, u32[]{:S(2)}) collective-permute-start(f32[328,128]{1,0:T(8,128)S(1)} %collective-permute-done.33.refs_6_.rest_8_), channel_id=1, source_target_pairs={{0,1},{1,0},{2,3},{3,2},{4,5},{5,4},{6,7},{7,6},{8,9},{9,8},{10,11... | collective-permute-start | bytes 503816 | tf_op jit(solution)/shard_map/ppermute | solution.py:453
  143.3 7.2 %collective-permute-start.37 = (f32[328,128]{1,0:T(8,128)S(1)}, f32[328,128]{1,0:T(8,128)S(1)}, u32[]{:S(2)}, u32[]{:S(2)}) collective-permute-start(f32[328,128]{1,0:T(8,128)S(1)} %collective-permute-done.36.refs_10_.rest_12_), channel_id=1, source_target_pairs={{0,1},{1,0},{2,3},{3,2},{4,5},{5,4},{6,7},{7,6},{8,9},{9,8},{10,11... | collective-permute-start | bytes 503816 | tf_op jit(solution)/shard_map/ppermute | solution.py:453
  148.4 7.8 %collective-permute-start.43 = (f32[328,128]{1,0:T(8,128)S(1)}, f32[328,128]{1,0:T(8,128)S(1)}, u32[]{:S(2)}, u32[]{:S(2)}) collective-permute-start(f32[328,128]{1,0:T(8,128)S(1)} %collective-permute-done.36.refs_10_.rest_12_), channel_id=1, source_target_pairs={{0,2},{1,3},{2,0},{3,1},{4,6},{5,7},{6,4},{7,5},{8,10},{9,11},{10,... | collective-permute-start | bytes 503816 | tf_op jit(solution)/shard_map/ppermute | solution.py:453
  149.6 8.2 %collective-permute-start.41 = (f32[328,128]{1,0:T(8,128)S(1)}, f32[328,128]{1,0:T(8,128)S(1)}, u32[]{:S(2)}, u32[]{:S(2)}) collective-permute-start(f32[328,128]{1,0:T(8,128)S(1)} %collective-permute-done.39.rest_2_), channel_id=1, source_target_pairs={{0,2},{1,3},{2,0},{3,1},{4,6},{5,7},{6,4},{7,5},{8,10},{9,11},{10,... | collective-permute-start | bytes 503816 | tf_op jit(solution)/shard_map/ppermute | solution.py:453
  154.8 3.8 %collective-permute-start.38 = (f32[328,128]{1,0:T(8,128)S(1)}, f32[328,128]{1,0:T(8,128)S(1)}, u32[]{:S(2)}, u32[]{:S(2)}) collective-permute-start(f32[328,128]{1,0:T(8,128)S(1)} %get-tuple-element.34.rest_0_), channel_id=1, source_target_pairs={{0,1},{1,0},{2,3},{3,2},{4,5},{5,4},{6,7},{7,6},{8,9},{9,8},{10,11... | collective-permute-start | bytes 503816 | tf_op jit(solution)/shard_map/ppermute | solution.py:453
  156.1 2.6 %collective-permute-start.40 = (f32[328,128]{1,0:T(8,128)S(1)}, f32[328,128]{1,0:T(8,128)S(1)}, u32[]{:S(2)}, u32[]{:S(2)}) collective-permute-start(f32[328,128]{1,0:T(8,128)S(1)} %collective-permute-done.39.rest_2_), channel_id=1, source_target_pairs={{0,1},{1,0},{2,3},{3,2},{4,5},{5,4},{6,7},{7,6},{8,9},{9,8},{10,11... | collective-permute-start | bytes 503816 | tf_op jit(solution)/shard_map/ppermute | solution.py:453
  156.2 2.5 %collective-permute-start.44 = (f32[328,128]{1,0:T(8,128)S(1)}, f32[328,128]{1,0:T(8,128)S(1)}, u32[]{:S(2)}, u32[]{:S(2)}) collective-permute-start(f32[328,128]{1,0:T(8,128)S(1)} %collective-permute-done.43.rest_6_), channel_id=1, source_target_pairs={{0,1},{1,0},{2,3},{3,2},{4,5},{5,4},{6,7},{7,6},{8,9},{9,8},{10,11... | collective-permute-start | bytes 503816 | tf_op jit(solution)/shard_map/ppermute | solution.py:453
  157.9 1.8 %collective-permute-start.42 = (f32[328,128]{1,0:T(8,128)S(1)}, f32[328,128]{1,0:T(8,128)S(1)}, u32[]{:S(2)}, u32[]{:S(2)}) collective-permute-start(f32[328,128]{1,0:T(8,128)S(1)} %collective-permute-done.41.rest_4_), channel_id=1, source_target_pairs={{0,1},{1,0},{2,3},{3,2},{4,5},{5,4},{6,7},{7,6},{8,9},{9,8},{10,11... | collective-permute-start | bytes 503816 | tf_op jit(solution)/shard_map/ppermute | solution.py:453
  (18 other events, 104.2 us)

commit v8 on v7

--- a/solution.py
+++ b/solution.py
@@ -31,17 +31,15 @@
     return jnp.where(lo, a, swap(b)), jnp.where(lo, swap(a), b)
 
 
-def three(x):
+def halves_of(x):
     hi = x.astype(BF16)
-    rest = x - hi.astype(F32)
-    mid = rest.astype(BF16)
-    return hi, mid, (rest - mid.astype(F32)).astype(BF16)
+    return hi, (x - hi.astype(F32)).astype(BF16)
 
 
 def pick(onehot, x, dims):
     return sum(
         lax.dot_general(onehot, part, (dims, ((), ())), preferred_element_type=F32)
-        for part in three(x)
+        for part in halves_of(x)
     )
 
 
@@ -255,16 +253,18 @@
 
 
 def predict(dpc, b, acc, chips, model_ref, hre, him):
-    acc_re, acc_im = acc
+    tiles = [slice(t, t + TILE) for t in range(0, acc[0].shape[0], TILE)]
+    acc_re, acc_im = ([x[t] for t in tiles] for x in acc)
     for m, k in enumerate(chips):
         for dd in range(dpc):
             mr = model_ref[k * dpc + dd, 0, b].astype(F32)
             mi = model_ref[k * dpc + dd, 1, b].astype(F32)
-            row = pl.ds(b * dpc + dd, 1)
+            row = pl.ds(b * dpc + dd, TILE, stride=0)
             hr, hi = hre[m, row, :], him[m, row, :]
-            acc_re = acc_re - (hr * mr - hi * mi)
-            acc_im = acc_im - (hr * mi + hi * mr)
-    return acc_re, acc_im
+            for i, t in enumerate(tiles):
+                acc_re[i] = acc_re[i] - (hr * mr[t] - hi * mi[t])
+                acc_im[i] = acc_im[i] - (hr * mi[t] + hi * mr[t])
+    return jnp.concatenate(acc_re, 0), jnp.concatenate(acc_im, 0)
 
 
 def weighted(b, acc, mask_ref):
@@ -349,23 +349,22 @@
     write_sums(dpc, chips, cre, cim, lambda m: (hre, him, m), power_ref, out_ref, True)
 
 
-OWN, NEAR, FAR = (0,), (1, 2, 6), (3, 4, 5, 7)
+NEAR, FAR = (0, 1, 2, 6), (3, 4, 5, 7)
 
 
 def chips_of(me, pairs):
     return [jnp.bitwise_xor(lax.div(me, 2), m) for m in pairs]
 
 
-def early_kernel(n, dpc, pairs, me_ref, first_ref, second_ref, model_hbm, acc_in, handed, *rest):
-    ins, (acc_ref, hre, him, handed_out, model_ref, sems) = rest[: 2 * len(pairs)], rest[2 * len(pairs) :]
+def early_kernel(n, dpc, me_ref, first_ref, second_ref, model_hbm, vis_ref, unused_in, *rest):
+    ins, (acc_ref, hre, him, unused_out, model_ref, sems) = rest[: 2 * len(NEAR)], rest[2 * len(NEAR) :]
     me = me_ref[0]
-    fetch = Fetch(model_hbm, model_ref, sems, [k * dpc for k in chips_of(me, pairs)])
-    handed_out[...] = handed[...]
+    fetch = Fetch(model_hbm, model_ref, sems, [k * dpc for k in chips_of(me, NEAR)])
     products(dpc, me, first_ref, second_ref, ins, hre, him)
 
     def pair(b, carry):
-        acc = acc_in[0, b], acc_in[1, b]
-        acc_ref[0, b], acc_ref[1, b] = predict(dpc, b, acc, range(len(pairs)), model_ref, hre, him)
+        acc = vis_ref[0, b], vis_ref[1, b]
+        acc_ref[0, b], acc_ref[1, b] = predict(dpc, b, acc, range(len(NEAR)), model_ref, hre, him)
         return carry
 
     fetch.each(pair)
@@ -381,8 +380,6 @@
     mask_ref,
     power_ref,
     acc_ref,
-    own_re,
-    own_im,
     near_re,
     near_im,
     *rest,
@@ -392,7 +389,7 @@
     me = me_ref[0]
     products(dpc, me, first_ref, second_ref, ins, hre, him)
     far = chips_of(me, FAR)
-    chips = chips_of(me, OWN + NEAR) + far
+    chips = chips_of(me, NEAR) + far
 
     def pair(b, carry):
         acc = predict(dpc, b, (acc_ref[0, b], acc_ref[1, b]), far, model_ref, hre, him)
@@ -402,7 +399,7 @@
     fetch.each(pair)
 
     def tiles(m):
-        for re, im, pairs in ((own_re, own_im, OWN), (near_re, near_im, NEAR), (hre, him, FAR)):
+        for re, im, pairs in ((near_re, near_im, NEAR), (hre, him, FAR)):
             if m < len(pairs):
                 return re, im, m
             m -= len(pairs)
@@ -418,7 +415,7 @@
     products(dpc, me, first_ref, second_ref, ins[: 2 * len(FAR)], hre, him)
     per = STATIONS // n
     even = lax.rem(me, 2) == 0
-    for m, k in enumerate(chips_of(me, FAR + NEAR + OWN)):
+    for m, k in enumerate(chips_of(me, FAR + NEAR)):
         for s in range(per):
             re, im = piece_pair(dpc, even, ins, m, me * per + s)
             for dd in range(dpc):
@@ -448,13 +445,13 @@
     return lax.all_to_all(x, "bl", split_axis=0, concat_axis=0, tiled=True)
 
 
-def gather(n, piece, beside, early=None):
+def gather(n, piece, beside):
     def send(x, o):
         return lax.ppermute(x, "bl", [(i, i ^ o) for i in range(n)])
 
     got = {0: piece}
     got[12], got[2], got[4], got[1] = (send(piece, o) for o in (12, 2, 4, 1))
-    got[8] = send(early(piece, got), 8) if early else send(got[12], 4)
+    got[8] = send(got[12], 4)
     got[6], got[14], got[10] = send(got[4], 2), send(got[12], 2), send(got[8], 2)
     for o in (2, 4, 12, 6, 14, 8, 10):
         if o == 6:
@@ -539,27 +536,20 @@
         return [got[2 * m + c] for m in pairs for c in (0, 1)]
 
     def gather_near(g):
-        acc, products = vis, []
-
-        def work(pairs):
-            def beside(x, got):
-                nonlocal acc
-                args = (me, first, second, model, acc, x, *slots(got, pairs))
-                size = (len(pairs),) + plane[1:]
-                outs = [shape(*vis.shape), shape(*size), shape(*size), shape(*x.shape)]
-                part = pltpu.VMEM((len(pairs) * dpc,) + model.shape[1:], BF16)
-                kernel = lambda n, dpc, *refs: early_kernel(n, dpc, pairs, *refs)
-                acc, re, im, x = call(kernel, args, outs, [part, sems])
-                products.extend([re, im])
-                return x
-
-            return beside
-
-        got = gather(n, g, work(NEAR), work(OWN))
-        return acc, products, slots(got, FAR + NEAR + OWN)
+        near = None
+
+        def beside(x, got):
+            nonlocal near
+            args = (me, first, second, model, vis, x, *slots(got, NEAR))
+            outs = [shape(*vis.shape), shape(*half), shape(*half), shape(*x.shape)]
+            *near, x = call(early_kernel, args, outs, held_half, aliases={5: 3})
+            return x
+
+        got = gather(n, g, beside)
+        return near, slots(got, FAR + NEAR)
 
     for step in range(1, ITERS):
-        acc, products, got = gather_near(g)
+        near, got = gather_near(g)
         (den,) = call(
             prepare_kernel,
             (g, onehot, powers),
@@ -569,7 +559,7 @@
         )
         (sums,) = call(
             later_pass_kernel,
-            (me, first, second, model, mask, power, acc, *products, *got[: 2 * len(FAR)]),
+            (me, first, second, model, mask, power, *near, *got[: 2 * len(FAR)]),
             [shape(n, ROWS * dpc, channels)],
             held + [half] * 2 + [plane] * 2,
             micros=7,
@@ -581,10 +571,10 @@
             [shape(*mine)],
             [(lots, width)] * 2,
         )
-    acc, products, got = gather_near(g)
+    near, got = gather_near(g)
     residual, gains = call(
         last_kernel,
-        (me, first, second, model, mask, acc, *got),
+        (me, first, second, model, mask, near[0], *got),
         [shape(*vis.shape), shape(2, *gre.shape)],
         held_half + [half] * 2,
         micros=4,

time: 167 us -> 161 us (0.964)
  Pallas kernels: 51.2 us -> 45.6 us
  starting transfers between devices: 63.1 us -> 58.8 us
  waiting for transfers between devices: 41 us -> 43.9 us
    pallas_call x13 -> x11, Pallas kernels: 51.2 us -> 45.6 us  [call(): pl.pallas_call(functools.partial(kernel, n, dpc), in_specs=[place(x) for...]
    ppermute x45, starting transfers between devices: 52.2 us -> 48.3 us  [send(): return lax.ppermute(x, 'bl', [(i, i ^ o) for i in range(n)])]
    ppermute x45, waiting for transfers between devices: 8.68 us -> 11.2 us  [send(): return lax.ppermute(x, 'bl', [(i, i ^ o) for i in range(n)])]
  transfers between devices with their start and end apart: 47 -> 47, of which waited for: 14 -> 16; matrix products, arithmetic and copies ran while one was open for 0% -> 0% of each run, Pallas kernels for 13% -> 11%
where the time goes in v8:
time: 161 us; the launch traced here: 158 us
  starting transfers between devices  58.8 us (37%)
  Pallas kernels  45.6 us (28%)
  waiting for transfers between devices  43.9 us (27%)
  local copies, waits for them, and re-layouts  8.44 us (5%)
    ppermute x45, starting transfers between devices, send(): return lax.ppermute(x, 'bl', [(i, i ^ o) for i in range(n)])  48.3 us
    pallas_call x11, Pallas kernels, call(): pl.pallas_call(functools.partial(kernel, n, dpc), in_specs=[place(x) for...  45.6 us
    all_to_all x2, waiting for transfers between devices, exchange(): return lax.all_to_all(x, 'bl', split_axis=0, concat_axis=0, tiled=True)  32.7 us
    ppermute x45, waiting for transfers between devices, send(): return lax.ppermute(x, 'bl', [(i, i ^ o) for i in range(n)])  11.2 us
    all_to_all x2, starting transfers between devices, exchange(): return lax.all_to_all(x, 'bl', split_axis=0, concat_axis=0, tiled=True)  10.5 us
    unnamed x38, local copies, waits for them, and re-layouts  8.44 us
  transfers between devices with their start and end apart: 47, of which 16 were waited for; matrix products, arithmetic and copies ran while one was open for 0% of the time, Pallas kernels for 11%

profile of v8, /device:TPU:9, one launch (start us, length us, event | category | flops | bytes accessed | tf_op | source)
XLA Modules:
  0.0 157.8 jit_solution(12845725652526669116)
XLA Ops:
  1.9 1.5 shard_map.86.rest_0_
  3.5 2.6 %collective-permute-start.7 = (f32[328,128]{1,0:T(8,128)S(1)}, f32[328,128]{1,0:T(8,128)S(1)}, u32[]{:S(2)}, u32[]{:S(2)}) collective-permute-start(f32[328,128]{1,0:T(8,128)S(1)} %shard_map.86.rest_0_), channel_id=1, source_target_pairs={{0,12},{1,13},{2,14},{3,15},{4,8},{5,9},{6,10},{7,11},{8,4},{9,5},... | collective-permute-start | bytes 503816 | tf_op jit(solution)/shard_map/ppermute | solution.py:450
  6.1 1.2 collective-permute-start.1
  7.3 1.4 collective-permute-done.3.rest_4_
  8.7 1.2 collective-permute-start.5
  9.9 4.6 %collective-permute-start.8 = (f32[328,128]{1,0:T(8,128)S(1)}, f32[328,128]{1,0:T(8,128)S(1)}, u32[]{:S(2)}, u32[]{:S(2)}) collective-permute-start(f32[328,128]{1,0:T(8,128)S(1)} %collective-permute-done.7.rest_12_), channel_id=1, source_target_pairs={{0,4},{1,5},{2,6},{3,7},{4,0},{5,1},{6,2},{7,3},{8,12},{9,13},{10,... | collective-permute-start | bytes 503816 | tf_op jit(solution)/shard_map/ppermute | solution.py:450
  14.5 1.9 %collective-permute-start = (f32[328,128]{1,0:T(8,128)S(1)}, f32[328,128]{1,0:T(8,128)S(1)}, u32[]{:S(2)}, u32[]{:S(2)}) collective-permute-start(f32[328,128]{1,0:T(8,128)S(1)} %shard_map.86.rest_0_), channel_id=1, source_target_pairs={{0,1},{1,0},{2,3},{3,2},{4,5},{5,4},{6,7},{7,6},{8,9},{9,8},{10,11... | collective-permute-start | bytes 503816 | tf_op jit(solution)/shard_map/ppermute | solution.py:450
  16.9 1.2 collective-permute-start.13
  18.5 0.9 copy-done.1
  19.4 5.6 %shard_map.87 = (f32[8,88,128]{2,1,0:T(8,128)S(1)}, f32[328,128]{1,0:T(8,128)S(1)}) custom-call(bf16[40,2,15,32,128]{4,3,2,1,0:T(8,128)(2,1)} %model_hbm.11, s32[15,32,128]{2,1,0:T(8,128)S(1)} %copy-done.1, f32[328,128]{1,0:T(8,128)S(1)} %collective-permute-done.5.unused_in), custom_call_target="tpu_custom_call", output_to_operand_aliasing={{1}: (2, {})} | custom-call | bytes 73800000 | tf_op jit(solution)/shard_map/pallas_call | solution.py:484
  25.0 3.4 %collective-permute-start.12 = (f32[328,128]{1,0:T(8,128)S(1)}, f32[328,128]{1,0:T(8,128)S(1)}, u32[]{:S(2)}, u32[]{:S(2)}) collective-permute-start(f32[328,128]{1,0:T(8,128)S(1)} %collective-permute-done.7.rest_12_), channel_id=1, source_target_pairs={{0,1},{1,0},{2,3},{3,2},{4,5},{5,4},{6,7},{7,6},{8,9},{9,8},{10,11... | collective-permute-start | bytes 503816 | tf_op jit(solution)/shard_map/ppermute | solution.py:450
  30.7 10.7 %shard_map.89 = f32[16,120,128]{2,1,0:T(8,128)} custom-call(s32[1]{0:T(128)} %bitcast.me_ref, s32[15]{0:T(128)S(1)} %copy-done.16, s32[15]{0:T(128)S(1)} %copy-done.18, bf16[40,2,15,32,128]{4,3,2,1,0:T(8,128)(2,1)} %model_hbm.11, f32[2,15,32,128]{3,2,1,0:T(8,128)S(1)} %copy-done, s32[15,32,128]{2,1,0:T(8,128)S(1)} %copy-done.2, ...), custom_call_target="tpu_custom_call" | custom-call | bytes 33210000 | tf_op jit(solution)/shard_map/pallas_call | solution.py:484
  41.5 5.6 %all-to-all-start = ((f32[16,120,128]{2,1,0:T(8,128)}), f32[16,120,128]{2,1,0:T(8,128)S(1)}, u32[]{:S(2)}, u32[]{:S(2)}) async-start(f32[16,120,128]{2,1,0:T(8,128)} %shard_map.89), calls=%async_computation | async-start | bytes 1966080 | tf_op jit(solution)/shard_map/all_to_all | solution.py:445
  47.1 0.9 copy-done.4
  48.0 0.9 copy-done.6
  48.9 0.9 copy-done.8
  49.9 0.9 copy-done.10
  50.8 0.9 copy-done.12
  51.7 1.3 shard_map.88
  53.7 16.9 %all-to-all-done.sums = f32[16,120,128]{2,1,0:T(8,128)S(1)} async-done(((f32[16,120,128]{2,1,0:T(8,128)}), f32[16,120,128]{2,1,0:T(8,128)S(1)}, u32[]{:S(2)}, u32[]{:S(2)}) %all-to-all-start) | async-done | bytes 983072 | tf_op jit(solution)/shard_map/all_to_all | solution.py:445
  70.6 0.9 copy-done.14
  71.5 1.5 shard_map.90.g_ref.rest_0_.g_in
  73.2 1.0 collective-permute-start.21
  74.2 1.6 collective-permute-start.18
  75.7 1.1 collective-permute-start.17
  76.8 2.5 %collective-permute-done.15.rest_4_ = f32[328,128]{1,0:T(8,128)S(1)} collective-permute-done((f32[328,128]{1,0:T(8,128)S(1)}, f32[328,128]{1,0:T(8,128)S(1)}, u32[]{:S(2)}, u32[]{:S(2)}) %collective-permute-start.15) | collective-permute-done | bytes 167968 | tf_op jit(solution)/shard_map/ppermute | solution.py:450
  80.0 3.6 %collective-permute-start.24 = (f32[328,128]{1,0:T(8,128)S(1)}, f32[328,128]{1,0:T(8,128)S(1)}, u32[]{:S(2)}, u32[]{:S(2)}) collective-permute-start(f32[328,128]{1,0:T(8,128)S(1)} %collective-permute-done.21.rest_6_), channel_id=1, source_target_pairs={{0,4},{1,5},{2,6},{3,7},{4,0},{5,1},{6,2},{7,3},{8,12},{9,13},{10,... | collective-permute-start | bytes 503816 | tf_op jit(solution)/shard_map/ppermute | solution.py:450
  83.5 2.1 %collective-permute-start.20 = (f32[328,128]{1,0:T(8,128)S(1)}, f32[328,128]{1,0:T(8,128)S(1)}, u32[]{:S(2)}, u32[]{:S(2)}) collective-permute-start(f32[328,128]{1,0:T(8,128)S(1)} %collective-permute-done.15.rest_4_), channel_id=1, source_target_pairs={{0,1},{1,0},{2,3},{3,2},{4,5},{5,4},{6,7},{7,6},{8,9},{9,8},{10,11... | collective-permute-start | bytes 503816 | tf_op jit(solution)/shard_map/ppermute | solution.py:450
  86.4 1.2 collective-permute-start.26
  87.6 4.3 %shard_map.92 = (f32[2,15,32,128]{3,2,1,0:T(8,128)S(1)}, f32[4,88,128]{2,1,0:T(8,128)S(1)}, f32[4,88,128]{2,1,0:T(8,128)S(1)}, f32[328,128]{1,0:T(8,128)S(1)}) custom-call(s32[1]{0:T(128)} %bitcast.me_ref, s32[15]{0:T(128)S(1)} %copy-done.16, s32[15]{0:T(128)S(1)} %copy-done.18, ...), custom_call_target="tpu_custom_call", output_to_operand_aliasing={{3}: (5, {})} | custom-call | bytes 3690000 | tf_op jit(solution)/shard_map/pallas_call | solution.py:484
  91.9 2.8 %collective-permute-start.23 = (f32[328,128]{1,0:T(8,128)S(1)}, f32[328,128]{1,0:T(8,128)S(1)}, u32[]{:S(2)}, u32[]{:S(2)}) collective-permute-start(f32[328,128]{1,0:T(8,128)S(1)} %get-tuple-element.21.rest_0_), channel_id=1, source_target_pairs={{0,1},{1,0},{2,3},{3,2},{4,5},{5,4},{6,7},{7,6},{8,9},{9,8},{10,11... | collective-permute-start | bytes 503816 | tf_op jit(solution)/shard_map/ppermute | solution.py:450
  95.5 0.9 collective-permute-start.27
  96.4 1.0 collective-permute-done.27.rest_5_
  97.4 8.7 %shard_map.93 = f32[16,80,128]{2,1,0:T(8,128)} custom-call(s32[1]{0:T(128)} %bitcast.me_ref, s32[15]{0:T(128)S(1)} %copy-done.16, s32[15]{0:T(128)S(1)} %copy-done.18, bf16[40,2,15,32,128]{4,3,2,1,0:T(8,128)(2,1)} %model_hbm.11, s32[15,32,128]{2,1,0:T(8,128)S(1)} %copy-done.2, f32[8,88,128]{2,1,0:T(8,128)S(1)} %get-tuple-element.17.power_ref, ...), custom_call_target="tpu_custom_call" | custom-call | bytes 25830000 | tf_op jit(solution)/shard_map/pallas_call | solution.py:484
  106.1 4.9 %all-to-all-start.1 = ((f32[16,80,128]{2,1,0:T(8,128)}), f32[16,80,128]{2,1,0:T(8,128)S(1)}, u32[]{:S(2)}, u32[]{:S(2)}) async-start(f32[16,80,128]{2,1,0:T(8,128)} %shard_map.93), calls=%async_computation.1 | async-start | bytes 1310720 | tf_op jit(solution)/shard_map/all_to_all | solution.py:445
  111.0 1.0 shard_map.91.den_ref
  112.0 15.8 %all-to-all-done.1.sums = f32[16,80,128]{2,1,0:T(8,128)S(1)} async-done(((f32[16,80,128]{2,1,0:T(8,128)}), f32[16,80,128]{2,1,0:T(8,128)S(1)}, u32[]{:S(2)}, u32[]{:S(2)}) %all-to-all-start.1) | async-done | bytes 655392 | tf_op jit(solution)/shard_map/all_to_all | solution.py:445
  127.9 1.0 shard_map.94.rest_0_.rest_8_
  129.6 1.6 %collective-permute-start.33 = (f32[328,128]{1,0:T(8,128)S(1)}, f32[328,128]{1,0:T(8,128)S(1)}, u32[]{:S(2)}, u32[]{:S(2)}) collective-permute-start(f32[328,128]{1,0:T(8,128)S(1)} %shard_map.94.rest_0_.rest_8_), channel_id=1, source_target_pairs={{0,2},{1,3},{2,0},{3,1},{4,6},{5,7},{6,4},{7,5},{8,10},{9,11},{10,... | collective-permute-start | bytes 503816 | tf_op jit(solution)/shard_map/ppermute | solution.py:450
  131.2 1.1 collective-permute-start.32
  132.2 2.8 %collective-permute-done.30.rest_4_.rest_12_ = f32[328,128]{1,0:T(8,128)S(1)} collective-permute-done((f32[328,128]{1,0:T(8,128)S(1)}, f32[328,128]{1,0:T(8,128)S(1)}, u32[]{:S(2)}, u32[]{:S(2)}) %collective-permute-start.30) | collective-permute-done | bytes 167968 | tf_op jit(solution)/shard_map/ppermute | solution.py:450
  135.4 0.7 collective-permute-done.36.rest_6_.rest_14_
  136.1 2.4 %collective-permute-start.39 = (f32[328,128]{1,0:T(8,128)S(1)}, f32[328,128]{1,0:T(8,128)S(1)}, u32[]{:S(2)}, u32[]{:S(2)}) collective-permute-start(f32[328,128]{1,0:T(8,128)S(1)} %collective-permute-done.36.rest_6_.rest_14_), channel_id=1, source_target_pairs={{0,4},{1,5},{2,6},{3,7},{4,0},{5,1},{6,2},{7,3},{8,12},{9,13},{10,... | collective-permute-start | bytes 503816 | tf_op jit(solution)/shard_map/ppermute | solution.py:450
  138.5 2.2 %collective-permute-start.35 = (f32[328,128]{1,0:T(8,128)S(1)}, f32[328,128]{1,0:T(8,128)S(1)}, u32[]{:S(2)}, u32[]{:S(2)}) collective-permute-start(f32[328,128]{1,0:T(8,128)S(1)} %collective-permute-done.30.rest_4_.rest_12_), channel_id=1, source_target_pairs={{0,1},{1,0},{2,3},{3,2},{4,5},{5,4},{6,7},{7,6},{8,9},{9,8},{10,11... | collective-permute-start | bytes 503816 | tf_op jit(solution)/shard_map/ppermute | solution.py:450
  141.8 1.0 collective-permute-start.41
  142.9 4.9 %shard_map.95 = (f32[2,15,32,128]{3,2,1,0:T(8,128)S(1)}, f32[4,88,128]{2,1,0:T(8,128)}, f32[4,88,128]{2,1,0:T(8,128)}, f32[328,128]{1,0:T(8,128)S(1)}) custom-call(s32[1]{0:T(128)} %bitcast.me_ref, s32[15]{0:T(128)S(1)} %copy-done.16, s32[15]{0:T(128)S(1)} %copy-done.18, bf16[40,2,15,32,128]{4,3,2,1,0:T(8,128)(2,1)} %model_hbm.11, ...), custom_call_target="tpu_custom_call", output_to_operand_aliasing={{3}: (5, {})} | custom-call | bytes 3690000 | tf_op jit(solution)/shard_map/pallas_call | solution.py:484
  147.8 3.0 %collective-permute-start.38 = (f32[328,128]{1,0:T(8,128)S(1)}, f32[328,128]{1,0:T(8,128)S(1)}, u32[]{:S(2)}, u32[]{:S(2)}) collective-permute-start(f32[328,128]{1,0:T(8,128)S(1)} %get-tuple-element.23.rest_0_), channel_id=1, source_target_pairs={{0,1},{1,0},{2,3},{3,2},{4,5},{5,4},{6,7},{7,6},{8,9},{9,8},{10,11... | collective-permute-start | bytes 503816 | tf_op jit(solution)/shard_map/ppermute | solution.py:450
  152.7 5.0 %shard_map.96 = (f32[2,15,32,128]{3,2,1,0:T(8,128)}, f32[2,160,128]{2,1,0:T(8,128)}) custom-call(s32[1]{0:T(128)} %bitcast.me_ref, s32[15]{0:T(128)S(1)} %copy-done.16, s32[15]{0:T(128)S(1)} %copy-done.18, bf16[40,2,15,32,128]{4,3,2,1,0:T(8,128)(2,1)} %model_hbm.11, s32[15,32,128]{2,1,0:T(8,128)S(1)} %copy-done.2, ...), custom_call_target="tpu_custom_call" | custom-call | bytes 14760000 | tf_op jit(solution)/shard_map/pallas_call | solution.py:484
  (95 shorter events, 11.6 us)
Async XLA Ops:
  1.9 28.8 %copy-start = (f32[2,15,32,128]{3,2,1,0:T(8,128)S(1)}, f32[2,15,32,128]{3,2,1,0:T(8,128)}, u32[]{:S(2)}) copy-start(f32[2,15,32,128]{3,2,1,0:T(8,128)} %vis_ref.5) | copy-start | bytes 1474564
  3.4 5.2 %collective-permute-start.3 = (f32[328,128]{1,0:T(8,128)S(1)}, f32[328,128]{1,0:T(8,128)S(1)}, u32[]{:S(2)}, u32[]{:S(2)}) collective-permute-start(f32[328,128]{1,0:T(8,128)S(1)} %shard_map.86.rest_0_), channel_id=1, source_target_pairs={{0,4},{1,5},{2,6},{3,7},{4,0},{5,1},{6,2},{7,3},{8,12},{9,13},{10,... | collective-permute-start | bytes 503816 | tf_op jit(solution)/shard_map/ppermute | solution.py:450
  3.5 6.4 %collective-permute-start.7 = (f32[328,128]{1,0:T(8,128)S(1)}, f32[328,128]{1,0:T(8,128)S(1)}, u32[]{:S(2)}, u32[]{:S(2)}) collective-permute-start(f32[328,128]{1,0:T(8,128)S(1)} %shard_map.86.rest_0_), channel_id=1, source_target_pairs={{0,12},{1,13},{2,14},{3,15},{4,8},{5,9},{6,10},{7,11},{8,4},{9,5},... | collective-permute-start | bytes 503816 | tf_op jit(solution)/shard_map/ppermute | solution.py:450
  6.1 10.3 %collective-permute-start.1 = (f32[328,128]{1,0:T(8,128)S(1)}, f32[328,128]{1,0:T(8,128)S(1)}, u32[]{:S(2)}, u32[]{:S(2)}) collective-permute-start(f32[328,128]{1,0:T(8,128)S(1)} %shard_map.86.rest_0_), channel_id=1, source_target_pairs={{0,2},{1,3},{2,0},{3,1},{4,6},{5,7},{6,4},{7,5},{8,10},{9,11},{10,... | collective-permute-start | bytes 503816 | tf_op jit(solution)/shard_map/ppermute | solution.py:450
  8.7 8.2 %collective-permute-start.5 = (f32[328,128]{1,0:T(8,128)S(1)}, f32[328,128]{1,0:T(8,128)S(1)}, u32[]{:S(2)}, u32[]{:S(2)}) collective-permute-start(f32[328,128]{1,0:T(8,128)S(1)} %collective-permute-done.3.rest_4_), channel_id=1, source_target_pairs={{0,2},{1,3},{2,0},{3,1},{4,6},{5,7},{6,4},{7,5},{8,10},{9,11},{10,... | collective-permute-start | bytes 503816 | tf_op jit(solution)/shard_map/ppermute | solution.py:450
  9.9 8.2 %collective-permute-start.8 = (f32[328,128]{1,0:T(8,128)S(1)}, f32[328,128]{1,0:T(8,128)S(1)}, u32[]{:S(2)}, u32[]{:S(2)}) collective-permute-start(f32[328,128]{1,0:T(8,128)S(1)} %collective-permute-done.7.rest_12_), channel_id=1, source_target_pairs={{0,4},{1,5},{2,6},{3,7},{4,0},{5,1},{6,2},{7,3},{8,12},{9,13},{10,... | collective-permute-start | bytes 503816 | tf_op jit(solution)/shard_map/ppermute | solution.py:450
  14.5 10.5 %collective-permute-start = (f32[328,128]{1,0:T(8,128)S(1)}, f32[328,128]{1,0:T(8,128)S(1)}, u32[]{:S(2)}, u32[]{:S(2)}) collective-permute-start(f32[328,128]{1,0:T(8,128)S(1)} %shard_map.86.rest_0_), channel_id=1, source_target_pairs={{0,1},{1,0},{2,3},{3,2},{4,5},{5,4},{6,7},{7,6},{8,9},{9,8},{10,11... | collective-permute-start | bytes 503816 | tf_op jit(solution)/shard_map/ppermute | solution.py:450
  16.4 12.0 %collective-permute-start.2 = (f32[328,128]{1,0:T(8,128)S(1)}, f32[328,128]{1,0:T(8,128)S(1)}, u32[]{:S(2)}, u32[]{:S(2)}) collective-permute-start(f32[328,128]{1,0:T(8,128)S(1)} %collective-permute-done.1.rest_2_), channel_id=1, source_target_pairs={{0,1},{1,0},{2,3},{3,2},{4,5},{5,4},{6,7},{7,6},{8,9},{9,8},{10,11... | collective-permute-start | bytes 503816 | tf_op jit(solution)/shard_map/ppermute | solution.py:450
  16.4 12.1 %collective-permute-start.4 = (f32[328,128]{1,0:T(8,128)S(1)}, f32[328,128]{1,0:T(8,128)S(1)}, u32[]{:S(2)}, u32[]{:S(2)}) collective-permute-start(f32[328,128]{1,0:T(8,128)S(1)} %collective-permute-done.3.rest_4_), channel_id=1, source_target_pairs={{0,1},{1,0},{2,3},{3,2},{4,5},{5,4},{6,7},{7,6},{8,9},{9,8},{10,11... | collective-permute-start | bytes 503816 | tf_op jit(solution)/shard_map/ppermute | solution.py:450
  16.9 12.0 %collective-permute-start.13 = (f32[328,128]{1,0:T(8,128)S(1)}, f32[328,128]{1,0:T(8,128)S(1)}, u32[]{:S(2)}, u32[]{:S(2)}) collective-permute-start(f32[328,128]{1,0:T(8,128)S(1)} %collective-permute-done.7.rest_12_), channel_id=1, source_target_pairs={{0,2},{1,3},{2,0},{3,1},{4,6},{5,7},{6,4},{7,5},{8,10},{9,11},{10,... | collective-permute-start | bytes 503816 | tf_op jit(solution)/shard_map/ppermute | solution.py:450
  18.1 10.9 %collective-permute-start.10 = (f32[328,128]{1,0:T(8,128)S(1)}, f32[328,128]{1,0:T(8,128)S(1)}, u32[]{:S(2)}, u32[]{:S(2)}) collective-permute-start(f32[328,128]{1,0:T(8,128)S(1)} %collective-permute-done.8.rest_8_), channel_id=1, source_target_pairs={{0,2},{1,3},{2,0},{3,1},{4,6},{5,7},{6,4},{7,5},{8,10},{9,11},{10,... | collective-permute-start | bytes 503816 | tf_op jit(solution)/shard_map/ppermute | solution.py:450
  25.0 4.4 %collective-permute-start.12 = (f32[328,128]{1,0:T(8,128)S(1)}, f32[328,128]{1,0:T(8,128)S(1)}, u32[]{:S(2)}, u32[]{:S(2)}) collective-permute-start(f32[328,128]{1,0:T(8,128)S(1)} %collective-permute-done.7.rest_12_), channel_id=1, source_target_pairs={{0,1},{1,0},{2,3},{3,2},{4,5},{5,4},{6,7},{7,6},{8,9},{9,8},{10,11... | collective-permute-start | bytes 503816 | tf_op jit(solution)/shard_map/ppermute | solution.py:450
  28.4 1.4 collective-permute-start.6
  28.5 1.7 %collective-permute-start.9 = (f32[328,128]{1,0:T(8,128)S(1)}, f32[328,128]{1,0:T(8,128)}, u32[]{:S(2)}, u32[]{:S(2)}) collective-permute-start(f32[328,128]{1,0:T(8,128)S(1)} %collective-permute-done.8.rest_8_), channel_id=1, source_target_pairs={{0,1},{1,0},{2,3},{3,2},{4,5},{5,4},{6,7},{7,6},{8,9},{9,8},{10,11... | collective-permute-start | bytes 503816 | tf_op jit(solution)/shard_map/ppermute | solution.py:450
  28.9 1.5 collective-permute-start.14
  29.0 1.7 %collective-permute-start.11 = (f32[328,128]{1,0:T(8,128)S(1)}, f32[328,128]{1,0:T(8,128)}, u32[]{:S(2)}, u32[]{:S(2)}) collective-permute-start(f32[328,128]{1,0:T(8,128)S(1)} %collective-permute-done.10.rest_10_), channel_id=1, source_target_pairs={{0,1},{1,0},{2,3},{3,2},{4,5},{5,4},{6,7},{7,6},{8,9},{9,8},{10,11... | collective-permute-start | bytes 503816 | tf_op jit(solution)/shard_map/ppermute | solution.py:450
  41.5 29.1 %all-to-all-start = ((f32[16,120,128]{2,1,0:T(8,128)}), f32[16,120,128]{2,1,0:T(8,128)S(1)}, u32[]{:S(2)}, u32[]{:S(2)}) async-start(f32[16,120,128]{2,1,0:T(8,128)} %shard_map.89), calls=%async_computation | async-start | bytes 1966080 | tf_op jit(solution)/shard_map/all_to_all | solution.py:445
  73.1 6.2 %collective-permute-start.15 = (f32[328,128]{1,0:T(8,128)S(1)}, f32[328,128]{1,0:T(8,128)S(1)}, u32[]{:S(2)}, u32[]{:S(2)}) collective-permute-start(f32[328,128]{1,0:T(8,128)S(1)} %shard_map.90.g_ref.rest_0_.g_in), channel_id=1, source_target_pairs={{0,4},{1,5},{2,6},{3,7},{4,0},{5,1},{6,2},{7,3},{8,12},{9,13},{10,... | collective-permute-start | bytes 503816 | tf_op jit(solution)/shard_map/ppermute | solution.py:450
  73.2 6.8 %collective-permute-start.21 = (f32[328,128]{1,0:T(8,128)S(1)}, f32[328,128]{1,0:T(8,128)S(1)}, u32[]{:S(2)}, u32[]{:S(2)}) collective-permute-start(f32[328,128]{1,0:T(8,128)S(1)} %shard_map.90.g_ref.rest_0_.g_in), channel_id=1, source_target_pairs={{0,12},{1,13},{2,14},{3,15},{4,8},{5,9},{6,10},{7,11},{8,4},{9,5},... | collective-permute-start | bytes 503816 | tf_op jit(solution)/shard_map/ppermute | solution.py:450
  74.2 11.4 %collective-permute-start.18 = (f32[328,128]{1,0:T(8,128)S(1)}, f32[328,128]{1,0:T(8,128)S(1)}, u32[]{:S(2)}, u32[]{:S(2)}) collective-permute-start(f32[328,128]{1,0:T(8,128)S(1)} %shard_map.90.g_ref.rest_0_.g_in), channel_id=1, source_target_pairs={{0,2},{1,3},{2,0},{3,1},{4,6},{5,7},{6,4},{7,5},{8,10},{9,11},{10,... | collective-permute-start | bytes 503816 | tf_op jit(solution)/shard_map/ppermute | solution.py:450
  75.7 9.8 %collective-permute-start.17 = (f32[328,128]{1,0:T(8,128)S(1)}, f32[328,128]{1,0:T(8,128)S(1)}, u32[]{:S(2)}, u32[]{:S(2)}) collective-permute-start(f32[328,128]{1,0:T(8,128)S(1)} %shard_map.90.g_ref.rest_0_.g_in), channel_id=1, source_target_pairs={{0,1},{1,0},{2,3},{3,2},{4,5},{5,4},{6,7},{7,6},{8,9},{9,8},{10,11... | collective-permute-start | bytes 503816 | tf_op jit(solution)/shard_map/ppermute | solution.py:450
  79.3 6.8 %collective-permute-start.16 = (f32[328,128]{1,0:T(8,128)S(1)}, f32[328,128]{1,0:T(8,128)S(1)}, u32[]{:S(2)}, u32[]{:S(2)}) collective-permute-start(f32[328,128]{1,0:T(8,128)S(1)} %collective-permute-done.15.rest_4_), channel_id=1, source_target_pairs={{0,2},{1,3},{2,0},{3,1},{4,6},{5,7},{6,4},{7,5},{8,10},{9,11},{10,... | collective-permute-start | bytes 503816 | tf_op jit(solution)/shard_map/ppermute | solution.py:450
  80.0 6.4 %collective-permute-start.24 = (f32[328,128]{1,0:T(8,128)S(1)}, f32[328,128]{1,0:T(8,128)S(1)}, u32[]{:S(2)}, u32[]{:S(2)}) collective-permute-start(f32[328,128]{1,0:T(8,128)S(1)} %collective-permute-done.21.rest_6_), channel_id=1, source_target_pairs={{0,4},{1,5},{2,6},{3,7},{4,0},{5,1},{6,2},{7,3},{8,12},{9,13},{10,... | collective-permute-start | bytes 503816 | tf_op jit(solution)/shard_map/ppermute | solution.py:450
  83.5 4.1 %collective-permute-start.20 = (f32[328,128]{1,0:T(8,128)S(1)}, f32[328,128]{1,0:T(8,128)S(1)}, u32[]{:S(2)}, u32[]{:S(2)}) collective-permute-start(f32[328,128]{1,0:T(8,128)S(1)} %collective-permute-done.15.rest_4_), channel_id=1, source_target_pairs={{0,1},{1,0},{2,3},{3,2},{4,5},{5,4},{6,7},{7,6},{8,9},{9,8},{10,11... | collective-permute-start | bytes 503816 | tf_op jit(solution)/shard_map/ppermute | solution.py:450
  85.6 2.0 %collective-permute-start.19 = (f32[328,128]{1,0:T(8,128)S(1)}, f32[328,128]{1,0:T(8,128)S(1)}, u32[]{:S(2)}, u32[]{:S(2)}) collective-permute-start(f32[328,128]{1,0:T(8,128)S(1)} %collective-permute-done.18.rest_2_), channel_id=1, source_target_pairs={{0,1},{1,0},{2,3},{3,2},{4,5},{5,4},{6,7},{7,6},{8,9},{9,8},{10,11... | collective-permute-start | bytes 503816 | tf_op jit(solution)/shard_map/ppermute | solution.py:450
  85.6 2.0 %collective-permute-start.22 = (f32[328,128]{1,0:T(8,128)S(1)}, f32[328,128]{1,0:T(8,128)S(1)}, u32[]{:S(2)}, u32[]{:S(2)}) collective-permute-start(f32[328,128]{1,0:T(8,128)S(1)} %collective-permute-done.21.rest_6_), channel_id=1, source_target_pairs={{0,1},{1,0},{2,3},{3,2},{4,5},{5,4},{6,7},{7,6},{8,9},{9,8},{10,11... | collective-permute-start | bytes 503816 | tf_op jit(solution)/shard_map/ppermute | solution.py:450
  86.1 8.7 %collective-permute-start.28 = (f32[328,128]{1,0:T(8,128)S(1)}, f32[328,128]{1,0:T(8,128)S(1)}, u32[]{:S(2)}, u32[]{:S(2)}) collective-permute-start(f32[328,128]{1,0:T(8,128)S(1)} %collective-permute-done.21.rest_6_), channel_id=1, source_target_pairs={{0,2},{1,3},{2,0},{3,1},{4,6},{5,7},{6,4},{7,5},{8,10},{9,11},{10,... | collective-permute-start | bytes 503816 | tf_op jit(solution)/shard_map/ppermute | solution.py:450
  86.4 9.1 %collective-permute-start.26 = (f32[328,128]{1,0:T(8,128)S(1)}, f32[328,128]{1,0:T(8,128)S(1)}, u32[]{:S(2)}, u32[]{:S(2)}) collective-permute-start(f32[328,128]{1,0:T(8,128)S(1)} %collective-permute-done.24.rest_2_), channel_id=1, source_target_pairs={{0,2},{1,3},{2,0},{3,1},{4,6},{5,7},{6,4},{7,5},{8,10},{9,11},{10,... | collective-permute-start | bytes 503816 | tf_op jit(solution)/shard_map/ppermute | solution.py:450
  91.9 4.5 %collective-permute-start.23 = (f32[328,128]{1,0:T(8,128)S(1)}, f32[328,128]{1,0:T(8,128)S(1)}, u32[]{:S(2)}, u32[]{:S(2)}) collective-permute-start(f32[328,128]{1,0:T(8,128)S(1)} %get-tuple-element.21.rest_0_), channel_id=1, source_target_pairs={{0,1},{1,0},{2,3},{3,2},{4,5},{5,4},{6,7},{7,6},{8,9},{9,8},{10,11... | collective-permute-start | bytes 503816 | tf_op jit(solution)/shard_map/ppermute | solution.py:450
  94.7 1.7 %collective-permute-start.25 = (f32[328,128]{1,0:T(8,128)S(1)}, f32[328,128]{1,0:T(8,128)S(1)}, u32[]{:S(2)}, u32[]{:S(2)}) collective-permute-start(f32[328,128]{1,0:T(8,128)S(1)} %collective-permute-done.24.rest_2_), channel_id=1, source_target_pairs={{0,1},{1,0},{2,3},{3,2},{4,5},{5,4},{6,7},{7,6},{8,9},{9,8},{10,11... | collective-permute-start | bytes 503816 | tf_op jit(solution)/shard_map/ppermute | solution.py:450
  94.8 1.6 %collective-permute-start.29 = (f32[328,128]{1,0:T(8,128)S(1)}, f32[328,128]{1,0:T(8,128)S(1)}, u32[]{:S(2)}, u32[]{:S(2)}) collective-permute-start(f32[328,128]{1,0:T(8,128)S(1)} %collective-permute-done.28.rest_6_), channel_id=1, source_target_pairs={{0,1},{1,0},{2,3},{3,2},{4,5},{5,4},{6,7},{7,6},{8,9},{9,8},{10,11... | collective-permute-start | bytes 503816 | tf_op jit(solution)/shard_map/ppermute | solution.py:450
  95.5 1.9 %collective-permute-start.27 = (f32[328,128]{1,0:T(8,128)S(1)}, f32[328,128]{1,0:T(8,128)S(1)}, u32[]{:S(2)}, u32[]{:S(2)}) collective-permute-start(f32[328,128]{1,0:T(8,128)S(1)} %collective-permute-done.26.rest_4_), channel_id=1, source_target_pairs={{0,1},{1,0},{2,3},{3,2},{4,5},{5,4},{6,7},{7,6},{8,9},{9,8},{10,11... | collective-permute-start | bytes 503816 | tf_op jit(solution)/shard_map/ppermute | solution.py:450
  106.1 21.8 %all-to-all-start.1 = ((f32[16,80,128]{2,1,0:T(8,128)}), f32[16,80,128]{2,1,0:T(8,128)S(1)}, u32[]{:S(2)}, u32[]{:S(2)}) async-start(f32[16,80,128]{2,1,0:T(8,128)} %shard_map.93), calls=%async_computation.1 | async-start | bytes 1310720 | tf_op jit(solution)/shard_map/all_to_all | solution.py:445
  128.9 6.1 %collective-permute-start.30 = (f32[328,128]{1,0:T(8,128)S(1)}, f32[328,128]{1,0:T(8,128)S(1)}, u32[]{:S(2)}, u32[]{:S(2)}) collective-permute-start(f32[328,128]{1,0:T(8,128)S(1)} %shard_map.94.rest_0_.rest_8_), channel_id=1, source_target_pairs={{0,4},{1,5},{2,6},{3,7},{4,0},{5,1},{6,2},{7,3},{8,12},{9,13},{10,... | collective-permute-start | bytes 503816 | tf_op jit(solution)/shard_map/ppermute | solution.py:450
  129.0 7.1 %collective-permute-start.36 = (f32[328,128]{1,0:T(8,128)S(1)}, f32[328,128]{1,0:T(8,128)S(1)}, u32[]{:S(2)}, u32[]{:S(2)}) collective-permute-start(f32[328,128]{1,0:T(8,128)S(1)} %shard_map.94.rest_0_.rest_8_), channel_id=1, source_target_pairs={{0,12},{1,13},{2,14},{3,15},{4,8},{5,9},{6,10},{7,11},{8,4},{9,5},... | collective-permute-start | bytes 503816 | tf_op jit(solution)/shard_map/ppermute | solution.py:450
  129.6 11.2 %collective-permute-start.33 = (f32[328,128]{1,0:T(8,128)S(1)}, f32[328,128]{1,0:T(8,128)S(1)}, u32[]{:S(2)}, u32[]{:S(2)}) collective-permute-start(f32[328,128]{1,0:T(8,128)S(1)} %shard_map.94.rest_0_.rest_8_), channel_id=1, source_target_pairs={{0,2},{1,3},{2,0},{3,1},{4,6},{5,7},{6,4},{7,5},{8,10},{9,11},{10,... | collective-permute-start | bytes 503816 | tf_op jit(solution)/shard_map/ppermute | solution.py:450
  131.2 9.6 %collective-permute-start.32 = (f32[328,128]{1,0:T(8,128)S(1)}, f32[328,128]{1,0:T(8,128)S(1)}, u32[]{:S(2)}, u32[]{:S(2)}) collective-permute-start(f32[328,128]{1,0:T(8,128)S(1)} %shard_map.94.rest_0_.rest_8_), channel_id=1, source_target_pairs={{0,1},{1,0},{2,3},{3,2},{4,5},{5,4},{6,7},{7,6},{8,9},{9,8},{10,11... | collective-permute-start | bytes 503816 | tf_op jit(solution)/shard_map/ppermute | solution.py:450
  135.1 6.2 %collective-permute-start.31 = (f32[328,128]{1,0:T(8,128)S(1)}, f32[328,128]{1,0:T(8,128)S(1)}, u32[]{:S(2)}, u32[]{:S(2)}) collective-permute-start(f32[328,128]{1,0:T(8,128)S(1)} %collective-permute-done.30.rest_4_.rest_12_), channel_id=1, source_target_pairs={{0,2},{1,3},{2,0},{3,1},{4,6},{5,7},{6,4},{7,5},{8,10},{9,11},{10,... | collective-permute-start | bytes 503816 | tf_op jit(solution)/shard_map/ppermute | solution.py:450
  136.1 5.7 %collective-permute-start.39 = (f32[328,128]{1,0:T(8,128)S(1)}, f32[328,128]{1,0:T(8,128)S(1)}, u32[]{:S(2)}, u32[]{:S(2)}) collective-permute-start(f32[328,128]{1,0:T(8,128)S(1)} %collective-permute-done.36.rest_6_.rest_14_), channel_id=1, source_target_pairs={{0,4},{1,5},{2,6},{3,7},{4,0},{5,1},{6,2},{7,3},{8,12},{9,13},{10,... | collective-permute-start | bytes 503816 | tf_op jit(solution)/shard_map/ppermute | solution.py:450
  138.5 4.4 %collective-permute-start.35 = (f32[328,128]{1,0:T(8,128)S(1)}, f32[328,128]{1,0:T(8,128)S(1)}, u32[]{:S(2)}, u32[]{:S(2)}) collective-permute-start(f32[328,128]{1,0:T(8,128)S(1)} %collective-permute-done.30.rest_4_.rest_12_), channel_id=1, source_target_pairs={{0,1},{1,0},{2,3},{3,2},{4,5},{5,4},{6,7},{7,6},{8,9},{9,8},{10,11... | collective-permute-start | bytes 503816 | tf_op jit(solution)/shard_map/ppermute | solution.py:450
  140.7 2.1 %collective-permute-start.34 = (f32[328,128]{1,0:T(8,128)S(1)}, f32[328,128]{1,0:T(8,128)S(1)}, u32[]{:S(2)}, u32[]{:S(2)}) collective-permute-start(f32[328,128]{1,0:T(8,128)S(1)} %collective-permute-done.33.rest_2_.rest_10_), channel_id=1, source_target_pairs={{0,1},{1,0},{2,3},{3,2},{4,5},{5,4},{6,7},{7,6},{8,9},{9,8},{10,11... | collective-permute-start | bytes 503816 | tf_op jit(solution)/shard_map/ppermute | solution.py:450
  140.7 2.1 %collective-permute-start.37 = (f32[328,128]{1,0:T(8,128)S(1)}, f32[328,128]{1,0:T(8,128)S(1)}, u32[]{:S(2)}, u32[]{:S(2)}) collective-permute-start(f32[328,128]{1,0:T(8,128)S(1)} %collective-permute-done.36.rest_6_.rest_14_), channel_id=1, source_target_pairs={{0,1},{1,0},{2,3},{3,2},{4,5},{5,4},{6,7},{7,6},{8,9},{9,8},{10,11... | collective-permute-start | bytes 503816 | tf_op jit(solution)/shard_map/ppermute | solution.py:450
  141.3 9.6 %collective-permute-start.43 = (f32[328,128]{1,0:T(8,128)S(1)}, f32[328,128]{1,0:T(8,128)S(1)}, u32[]{:S(2)}, u32[]{:S(2)}) collective-permute-start(f32[328,128]{1,0:T(8,128)S(1)} %collective-permute-done.36.rest_6_.rest_14_), channel_id=1, source_target_pairs={{0,2},{1,3},{2,0},{3,1},{4,6},{5,7},{6,4},{7,5},{8,10},{9,11},{10,... | collective-permute-start | bytes 503816 | tf_op jit(solution)/shard_map/ppermute | solution.py:450
  141.8 9.4 %collective-permute-start.41 = (f32[328,128]{1,0:T(8,128)S(1)}, f32[328,128]{1,0:T(8,128)S(1)}, u32[]{:S(2)}, u32[]{:S(2)}) collective-permute-start(f32[328,128]{1,0:T(8,128)S(1)} %collective-permute-done.39.rest_2_), channel_id=1, source_target_pairs={{0,2},{1,3},{2,0},{3,1},{4,6},{5,7},{6,4},{7,5},{8,10},{9,11},{10,... | collective-permute-start | bytes 503816 | tf_op jit(solution)/shard_map/ppermute | solution.py:450
  147.8 4.0 %collective-permute-start.38 = (f32[328,128]{1,0:T(8,128)S(1)}, f32[328,128]{1,0:T(8,128)S(1)}, u32[]{:S(2)}, u32[]{:S(2)}) collective-permute-start(f32[328,128]{1,0:T(8,128)S(1)} %get-tuple-element.23.rest_0_), channel_id=1, source_target_pairs={{0,1},{1,0},{2,3},{3,2},{4,5},{5,4},{6,7},{7,6},{8,9},{9,8},{10,11... | collective-permute-start | bytes 503816 | tf_op jit(solution)/shard_map/ppermute | solution.py:450
  150.7 1.4 collective-permute-start.40
  150.8 1.6 collective-permute-start.44
  151.3 1.4 collective-permute-start.42
  (18 other events, 104.0 us)

commit v9 on v8

--- a/solution.py
+++ b/solution.py
@@ -15,7 +15,7 @@
 ridge = 1.0
 F32 = jnp.float32
 BF16 = jnp.bfloat16
-VMEM_LIMIT = 24 * 1024 * 1024
+VMEM_LIMIT = 16 * 1024 * 1024
 
 
 def swap(x):
@@ -44,7 +44,7 @@
 
 
 TILE = 8
-PARTS = (1, 3, 7, ROWS)
+PARTS = (1, 2, 4, 6, 8, 10, 12, ROWS)
 
 
 def pack_kernel(n, dpc, first_ref, second_ref, re_ref, im_ref, out_ref, sems):
@@ -66,29 +66,21 @@
 
 
 class Fetch:
-    def __init__(self, model, held, sems, firsts=(0,)):
-        count, pairs = held.shape[0] // len(firsts), held.shape[2]
+    def __init__(self, model, held, sems):
+        pairs = held.shape[2]
+        self.ends = [0] + [min(end, pairs) for end in PARTS]
         self.copies = []
-        self.ends = [0] + [min(end, pairs) for end in PARTS]
         for i in range(len(PARTS)):
             part = pl.ds(self.ends[i], self.ends[i + 1] - self.ends[i])
-            self.copies.append([])
-            for j, first in enumerate(firsts):
-                self.copies[i].append(
-                    pltpu.make_async_copy(
-                        model.at[pl.ds(first, count), :, part],
-                        held.at[pl.ds(j * count, count), :, part],
-                        sems.at[i, j],
-                    )
-                )
-        for copies in self.copies:
-            for copy in copies:
-                copy.start()
+            self.copies.append(
+                pltpu.make_async_copy(model.at[:, :, part], held.at[:, :, part], sems.at[i])
+            )
+        for copy in self.copies:
+            copy.start()
 
     def each(self, body):
-        for i, copies in enumerate(self.copies):
-            for copy in copies:
-                copy.wait()
+        for i, copy in enumerate(self.copies):
+            copy.wait()
             lax.fori_loop(self.ends[i], self.ends[i + 1], body, 0)
 
 
@@ -331,10 +323,9 @@
 
 
 def first_pass_kernel(
-    n, dpc, me_ref, first_ref, second_ref, model_hbm, vis_ref, mask_ref, power_ref, *rest
+    n, dpc, me_ref, first_ref, second_ref, model_ref, vis_ref, mask_ref, power_ref, *rest
 ):
-    ins, (out_ref, model_ref, sems, hre, him, cre, cim, stack) = rest[:n], rest[n:]
-    fetch = Fetch(model_hbm, model_ref, sems)
+    ins, (out_ref, hre, him, cre, cim, stack) = rest[:n], rest[n:]
     products_first(n, dpc, me_ref[0], first_ref, second_ref, ins, hre, him, stack)
     chips = range(n // 2)
 
@@ -343,7 +334,7 @@
         correlate(dpc, b, weighted(b, acc, mask_ref), chips, model_ref, cre, cim)
         return carry
 
-    fetch.each(pair)
+    lax.fori_loop(0, mask_ref.shape[0], pair, 0)
 
     clear(dpc, mask_ref.shape[0], cre, cim)
     write_sums(dpc, chips, cre, cim, lambda m: (hre, him, m), power_ref, out_ref, True)
@@ -356,18 +347,18 @@
     return [jnp.bitwise_xor(lax.div(me, 2), m) for m in pairs]
 
 
-def early_kernel(n, dpc, me_ref, first_ref, second_ref, model_hbm, vis_ref, unused_in, *rest):
-    ins, (acc_ref, hre, him, unused_out, model_ref, sems) = rest[: 2 * len(NEAR)], rest[2 * len(NEAR) :]
+def early_kernel(n, dpc, me_ref, first_ref, second_ref, model_ref, vis_ref, unused_in, *rest):
+    ins, (acc_ref, hre, him, unused_out) = rest[: 2 * len(NEAR)], rest[2 * len(NEAR) :]
     me = me_ref[0]
-    fetch = Fetch(model_hbm, model_ref, sems, [k * dpc for k in chips_of(me, NEAR)])
+    chips = chips_of(me, NEAR)
     products(dpc, me, first_ref, second_ref, ins, hre, him)
 
     def pair(b, carry):
         acc = vis_ref[0, b], vis_ref[1, b]
-        acc_ref[0, b], acc_ref[1, b] = predict(dpc, b, acc, range(len(NEAR)), model_ref, hre, him)
+        acc_ref[0, b], acc_ref[1, b] = predict(dpc, b, acc, chips, model_ref, hre, him)
         return carry
 
-    fetch.each(pair)
+    lax.fori_loop(0, vis_ref.shape[1], pair, 0)
 
 
 def later_pass_kernel(
@@ -376,7 +367,7 @@
     me_ref,
     first_ref,
     second_ref,
-    model_hbm,
+    model_ref,
     mask_ref,
     power_ref,
     acc_ref,
@@ -384,8 +375,7 @@
     near_im,
     *rest,
 ):
-    ins, (out_ref, model_ref, sems, hre, him, cre, cim) = rest[: 2 * len(FAR)], rest[2 * len(FAR) :]
-    fetch = Fetch(model_hbm, model_ref, sems)
+    ins, (out_ref, hre, him, cre, cim) = rest[: 2 * len(FAR)], rest[2 * len(FAR) :]
     me = me_ref[0]
     products(dpc, me, first_ref, second_ref, ins, hre, him)
     far = chips_of(me, FAR)
@@ -396,7 +386,7 @@
         correlate(dpc, b, weighted(b, acc, mask_ref), chips, model_ref, cre, cim)
         return carry
 
-    fetch.each(pair)
+    lax.fori_loop(0, mask_ref.shape[0], pair, 0)
 
     def tiles(m):
         for re, im, pairs in ((near_re, near_im, NEAR), (hre, him, FAR)):
@@ -408,10 +398,10 @@
     write_sums(dpc, chips, cre, cim, tiles, power_ref, out_ref, False)
 
 
-def last_kernel(n, dpc, me_ref, first_ref, second_ref, model_hbm, mask_ref, acc_ref, *rest):
-    ins, (res_ref, gains_ref, model_ref, sems, hre, him) = rest[:n], rest[n:]
+def last_kernel(n, dpc, me_ref, first_ref, second_ref, model_ref, mask_ref, acc_ref, *rest):
+    ins, (res_ref, gains_ref, hre, him) = rest[:n], rest[n:]
     me = me_ref[0]
-    fetch = Fetch(model_hbm, model_ref, sems, [k * dpc for k in chips_of(me, FAR)])
+    far = chips_of(me, FAR)
     products(dpc, me, first_ref, second_ref, ins[: 2 * len(FAR)], hre, him)
     per = STATIONS // n
     even = lax.rem(me, 2) == 0
@@ -425,11 +415,11 @@
 
     def pair(b, carry):
         acc = acc_ref[0, b], acc_ref[1, b]
-        acc = predict(dpc, b, acc, range(len(FAR)), model_ref, hre, him)
+        acc = predict(dpc, b, acc, far, model_ref, hre, him)
         res_ref[0, b], res_ref[1, b] = weighted(b, acc, mask_ref)
         return carry
 
-    fetch.each(pair)
+    lax.fori_loop(0, mask_ref.shape[0], pair, 0)
 
 
 SMEM = pl.BlockSpec(memory_space=pltpu.SMEM)
@@ -471,9 +461,7 @@
     half = (len(FAR), ROWS * dpc + TILE, channels)
     lots = n * 2 * ROWS
     mine = (STATIONS * dpc + TILE, channels)
-    sems = pltpu.SemaphoreType.DMA((len(PARTS), n // 4))
-    held = [pltpu.VMEM(model.shape, BF16), sems]
-    held_half = [pltpu.VMEM((SOURCE_COUNT // 2,) + model.shape[1:], BF16), sems]
+    sems = pltpu.SemaphoreType.DMA((len(PARTS),))
 
     def call(kernel, args, outs, scratch=(), micros=1, aliases={}):
         def place(x):
@@ -500,13 +488,12 @@
         [shape(2 * gre.shape[0] + TILE, channels)],
         [pltpu.SemaphoreType.DMA((2,))],
     )
-    power = None
+    power = held = None
 
     def powers_beside(x, got):
-        nonlocal power
-        power, x = call(
-            power_kernel, (model, mask, x), [shape(*plane), shape(*x.shape)], held, micros=20, aliases={2: 1}
-        )
+        nonlocal power, held
+        outs = [shape(*plane), shape(*x.shape), pltpu.VMEM(model.shape, BF16)]
+        power, x, held = call(power_kernel, (model, mask, x), outs, [sems], aliases={2: 1})
         return x
 
     got = gather(n, piece, powers_beside)
@@ -519,9 +506,9 @@
     )
     (sums,) = call(
         first_pass_kernel,
-        (me, first, second, model, vis, mask, power, *got),
+        (me, first, second, held, vis, mask, power, *got),
         [shape(n, (ROWS + TILE) * dpc, channels)],
-        held + [plane] * 4 + [(n,) + piece.shape],
+        [plane] * 4 + [(n,) + piece.shape],
         micros=9,
     )
     powers = exchange(sums)
@@ -540,9 +527,9 @@
 
         def beside(x, got):
             nonlocal near
-            args = (me, first, second, model, vis, x, *slots(got, NEAR))
+            args = (me, first, second, held, vis, x, *slots(got, NEAR))
             outs = [shape(*vis.shape), shape(*half), shape(*half), shape(*x.shape)]
-            *near, x = call(early_kernel, args, outs, held_half, aliases={5: 3})
+            *near, x = call(early_kernel, args, outs, aliases={5: 3})
             return x
 
         got = gather(n, g, beside)
@@ -559,9 +546,9 @@
         )
         (sums,) = call(
             later_pass_kernel,
-            (me, first, second, model, mask, power, *near, *got[: 2 * len(FAR)]),
+            (me, first, second, held, mask, power, *near, *got[: 2 * len(FAR)]),
             [shape(n, ROWS * dpc, channels)],
-            held + [half] * 2 + [plane] * 2,
+            [half] * 2 + [plane] * 2,
             micros=7,
         )
         sums = exchange(sums)
@@ -574,9 +561,9 @@
     near, got = gather_near(g)
     residual, gains = call(
         last_kernel,
-        (me, first, second, model, mask, near[0], *got),
+        (me, first, second, held, mask, near[0], *got),
         [shape(*vis.shape), shape(2, *gre.shape)],
-        held_half + [half] * 2,
+        [half] * 2,
         micros=4,
     )
     return gains, residual

time: 161 us -> 174 us (1.081)
  local copies, waits for them, and re-layouts: 8.44 us -> 23.7 us
    unnamed x38 -> x50, local copies, waits for them, and re-layouts: 8.44 us -> 23.7 us
  transfers between devices with their start and end apart: 47 -> 47, of which waited for: 16 -> 18; matrix products, arithmetic and copies ran while one was open for 0% -> 0% of each run, Pallas kernels for 11% -> 9%
where the time goes in v9:
time: 174 us; the launch traced here: 171 us
  starting transfers between devices  58.5 us (34%)
  Pallas kernels  44.1 us (25%)
  waiting for transfers between devices  44.1 us (25%)
  local copies, waits for them, and re-layouts  23.7 us (14%)
    ppermute x45, starting transfers between devices, send(): return lax.ppermute(x, 'bl', [(i, i ^ o) for i in range(n)])  47.2 us
    pallas_call x11, Pallas kernels, call(): pl.pallas_call(functools.partial(kernel, n, dpc), in_specs=[place(x) for...  44.1 us
    all_to_all x2, waiting for transfers between devices, exchange(): return lax.all_to_all(x, 'bl', split_axis=0, concat_axis=0, tiled=True)  32.7 us
    unnamed x50, local copies, waits for them, and re-layouts  23.7 us
    ppermute x45, waiting for transfers between devices, send(): return lax.ppermute(x, 'bl', [(i, i ^ o) for i in range(n)])  11.4 us
    all_to_all x2, starting transfers between devices, exchange(): return lax.all_to_all(x, 'bl', split_axis=0, concat_axis=0, tiled=True)  11.3 us
  transfers between devices with their start and end apart: 47, of which 18 were waited for; matrix products, arithmetic and copies ran while one was open for 0% of the time, Pallas kernels for 9%

profile of v9, /device:TPU:9, one launch (start us, length us, event | category | flops | bytes accessed | tf_op | source)
XLA Modules:
  0.0 171.2 jit_solution(16569613485113544373)
XLA Ops:
  1.9 1.5 shard_map.86.rest_0_
  3.5 2.6 %collective-permute-start.7 = (f32[328,128]{1,0:T(8,128)S(1)}, f32[328,128]{1,0:T(8,128)S(1)}, u32[]{:S(2)}, u32[]{:S(2)}) collective-permute-start(f32[328,128]{1,0:T(8,128)S(1)} %shard_map.86.rest_0_), channel_id=1, source_target_pairs={{0,12},{1,13},{2,14},{3,15},{4,8},{5,9},{6,10},{7,11},{8,4},{9,5},... | collective-permute-start | bytes 503816 | tf_op jit(solution)/shard_map/ppermute | solution.py:440
  6.1 1.2 collective-permute-start.3
  7.3 1.4 collective-permute-done.rest_4_
  8.7 1.2 collective-permute-start.1
  9.9 4.6 %collective-permute-start.8 = (f32[328,128]{1,0:T(8,128)S(1)}, f32[328,128]{1,0:T(8,128)S(1)}, u32[]{:S(2)}, u32[]{:S(2)}) collective-permute-start(f32[328,128]{1,0:T(8,128)S(1)} %collective-permute-done.7.rest_12_), channel_id=1, source_target_pairs={{0,4},{1,5},{2,6},{3,7},{4,0},{5,1},{6,2},{7,3},{8,12},{9,13},{10,... | collective-permute-start | bytes 503816 | tf_op jit(solution)/shard_map/ppermute | solution.py:440
  14.5 1.9 %collective-permute-start.2 = (f32[328,128]{1,0:T(8,128)S(1)}, f32[328,128]{1,0:T(8,128)S(1)}, u32[]{:S(2)}, u32[]{:S(2)}) collective-permute-start(f32[328,128]{1,0:T(8,128)S(1)} %shard_map.86.rest_0_), channel_id=1, source_target_pairs={{0,1},{1,0},{2,3},{3,2},{4,5},{5,4},{6,7},{7,6},{8,9},{9,8},{10,11... | collective-permute-start | bytes 503816 | tf_op jit(solution)/shard_map/ppermute | solution.py:440
  16.9 1.2 collective-permute-start.13
  18.5 0.9 copy-done.7
  19.4 4.6 %shard_map.87 = (f32[8,88,128]{2,1,0:T(8,128)S(1)}, f32[328,128]{1,0:T(8,128)S(1)}, bf16[40,2,15,32,128]{4,3,2,1,0:T(8,128)(2,1)S(1)}) custom-call(bf16[40,2,15,32,128]{4,3,2,1,0:T(8,128)(2,1)} %model_hbm.1, s32[15,32,128]{2,1,0:T(8,128)S(1)} %copy-done.7, f32[328,128]{1,0:T(8,128)S(1)} %collective-permute-done.1.unused_in), custom_call_target="tpu_custom_call", output_to_operand_aliasing={{1}: (2, {})} | custom-call | bytes 3690000 | tf_op jit(solution)/shard_map/pallas_call | solution.py:472
  24.0 3.8 %copy-done = bf16[40,2,15,32,128]{4,3,2,1,0:T(8,128)(2,1)} copy-done((bf16[40,2,15,32,128]{4,3,2,1,0:T(8,128)(2,1)}, bf16[40,2,15,32,128]{4,3,2,1,0:T(8,128)(2,1)S(1)}, u32[]{:S(2)}) %copy-start) | copy-done | bytes 9830424
  27.9 3.3 %collective-permute-start.12 = (f32[328,128]{1,0:T(8,128)S(1)}, f32[328,128]{1,0:T(8,128)S(1)}, u32[]{:S(2)}, u32[]{:S(2)}) collective-permute-start(f32[328,128]{1,0:T(8,128)S(1)} %collective-permute-done.7.rest_12_), channel_id=1, source_target_pairs={{0,1},{1,0},{2,3},{3,2},{4,5},{5,4},{6,7},{7,6},{8,9},{9,8},{10,11... | collective-permute-start | bytes 503816 | tf_op jit(solution)/shard_map/ppermute | solution.py:440
  33.5 3.8 %copy-done.1 = bf16[40,2,15,32,128]{4,3,2,1,0:T(8,128)(2,1)S(1)} copy-done((bf16[40,2,15,32,128]{4,3,2,1,0:T(8,128)(2,1)S(1)}, bf16[40,2,15,32,128]{4,3,2,1,0:T(8,128)(2,1)}, u32[]{:S(2)}) %copy-start.1) | copy-done | bytes 9830424
  37.3 10.3 %shard_map.89 = f32[16,120,128]{2,1,0:T(8,128)} custom-call(s32[1]{0:T(128)} %bitcast.me_ref, s32[15]{0:T(128)S(1)} %copy-done.22, s32[15]{0:T(128)S(1)} %copy-done.24, bf16[40,2,15,32,128]{4,3,2,1,0:T(8,128)(2,1)S(1)} %copy-done.1, f32[2,15,32,128]{3,2,1,0:T(8,128)S(1)} %copy-done.6, s32[15,32,128]{2,1,0:T(8,128)S(1)} %copy-done.8, ...), custom_call_target="tpu_custom_call" | custom-call | bytes 33210000 | tf_op jit(solution)/shard_map/pallas_call | solution.py:472
  47.6 5.6 %all-to-all-start = ((f32[16,120,128]{2,1,0:T(8,128)}), f32[16,120,128]{2,1,0:T(8,128)S(1)}, u32[]{:S(2)}, u32[]{:S(2)}) async-start(f32[16,120,128]{2,1,0:T(8,128)} %shard_map.89), calls=%async_computation | async-start | bytes 1966080 | tf_op jit(solution)/shard_map/all_to_all | solution.py:435
  54.1 0.9 copy-done.12
  55.1 0.9 copy-done.14
  56.0 0.9 copy-done.16
  56.9 0.9 copy-done.18
  57.8 1.3 shard_map.88
  59.8 16.9 %all-to-all-done.sums = f32[16,120,128]{2,1,0:T(8,128)S(1)} async-done(((f32[16,120,128]{2,1,0:T(8,128)}), f32[16,120,128]{2,1,0:T(8,128)S(1)}, u32[]{:S(2)}, u32[]{:S(2)}) %all-to-all-start) | async-done | bytes 983072 | tf_op jit(solution)/shard_map/all_to_all | solution.py:435
  76.7 0.9 copy-done.20
  77.6 1.5 shard_map.90.g_ref.rest_0_.g_in
  79.3 1.0 collective-permute-start.21
  80.3 1.6 collective-permute-start.18
  81.8 1.1 collective-permute-start.17
  82.9 2.5 %collective-permute-done.15.rest_4_ = f32[328,128]{1,0:T(8,128)S(1)} collective-permute-done((f32[328,128]{1,0:T(8,128)S(1)}, f32[328,128]{1,0:T(8,128)S(1)}, u32[]{:S(2)}, u32[]{:S(2)}) %collective-permute-start.15) | collective-permute-done | bytes 167968 | tf_op jit(solution)/shard_map/ppermute | solution.py:440
  86.1 3.5 %collective-permute-start.24 = (f32[328,128]{1,0:T(8,128)S(1)}, f32[328,128]{1,0:T(8,128)S(1)}, u32[]{:S(2)}, u32[]{:S(2)}) collective-permute-start(f32[328,128]{1,0:T(8,128)S(1)} %collective-permute-done.21.rest_6_), channel_id=1, source_target_pairs={{0,4},{1,5},{2,6},{3,7},{4,0},{5,1},{6,2},{7,3},{8,12},{9,13},{10,... | collective-permute-start | bytes 503816 | tf_op jit(solution)/shard_map/ppermute | solution.py:440
  89.6 2.1 %collective-permute-start.20 = (f32[328,128]{1,0:T(8,128)S(1)}, f32[328,128]{1,0:T(8,128)S(1)}, u32[]{:S(2)}, u32[]{:S(2)}) collective-permute-start(f32[328,128]{1,0:T(8,128)S(1)} %collective-permute-done.15.rest_4_), channel_id=1, source_target_pairs={{0,1},{1,0},{2,3},{3,2},{4,5},{5,4},{6,7},{7,6},{8,9},{9,8},{10,11... | collective-permute-start | bytes 503816 | tf_op jit(solution)/shard_map/ppermute | solution.py:440
  92.5 1.2 collective-permute-start.26
  93.7 3.8 %copy-done.2 = bf16[40,2,15,32,128]{4,3,2,1,0:T(8,128)(2,1)S(1)} copy-done((bf16[40,2,15,32,128]{4,3,2,1,0:T(8,128)(2,1)S(1)}, bf16[40,2,15,32,128]{4,3,2,1,0:T(8,128)(2,1)}, u32[]{:S(2)}) %copy-start.2) | copy-done | bytes 9830424
  97.5 4.0 %shard_map.92 = (f32[2,15,32,128]{3,2,1,0:T(8,128)S(1)}, f32[4,88,128]{2,1,0:T(8,128)S(1)}, f32[4,88,128]{2,1,0:T(8,128)S(1)}, f32[328,128]{1,0:T(8,128)S(1)}) custom-call(s32[1]{0:T(128)} %bitcast.me_ref, s32[15]{0:T(128)S(1)} %copy-done.22, s32[15]{0:T(128)S(1)} %copy-done.24, ...), custom_call_target="tpu_custom_call", output_to_operand_aliasing={{3}: (5, {})} | custom-call | bytes 3690000 | tf_op jit(solution)/shard_map/pallas_call | solution.py:472
  101.5 2.8 %collective-permute-start.23 = (f32[328,128]{1,0:T(8,128)S(1)}, f32[328,128]{1,0:T(8,128)S(1)}, u32[]{:S(2)}, u32[]{:S(2)}) collective-permute-start(f32[328,128]{1,0:T(8,128)S(1)} %get-tuple-element.23.rest_0_), channel_id=1, source_target_pairs={{0,1},{1,0},{2,3},{3,2},{4,5},{5,4},{6,7},{7,6},{8,9},{9,8},{10,11... | collective-permute-start | bytes 503816 | tf_op jit(solution)/shard_map/ppermute | solution.py:440
  106.3 9.0 %shard_map.93 = f32[16,80,128]{2,1,0:T(8,128)} custom-call(s32[1]{0:T(128)} %bitcast.me_ref, s32[15]{0:T(128)S(1)} %copy-done.22, s32[15]{0:T(128)S(1)} %copy-done.24, bf16[40,2,15,32,128]{4,3,2,1,0:T(8,128)(2,1)S(1)} %copy-done.3, s32[15,32,128]{2,1,0:T(8,128)S(1)} %copy-done.8, f32[8,88,128]{2,1,0:T(8,128)S(1)} %get-tuple-element.19.power_ref, ...), custom_call_target="tpu_custom_call" | custom-call | bytes 25830000 | tf_op jit(solution)/shard_map/pallas_call | solution.py:472
  115.2 5.7 %all-to-all-start.1 = ((f32[16,80,128]{2,1,0:T(8,128)}), f32[16,80,128]{2,1,0:T(8,128)S(1)}, u32[]{:S(2)}, u32[]{:S(2)}) async-start(f32[16,80,128]{2,1,0:T(8,128)} %shard_map.93), calls=%async_computation.1 | async-start | bytes 1310720 | tf_op jit(solution)/shard_map/all_to_all | solution.py:435
  120.9 1.0 shard_map.91.den_ref
  122.0 15.8 %all-to-all-done.1.sums = f32[16,80,128]{2,1,0:T(8,128)S(1)} async-done(((f32[16,80,128]{2,1,0:T(8,128)}), f32[16,80,128]{2,1,0:T(8,128)S(1)}, u32[]{:S(2)}, u32[]{:S(2)}) %all-to-all-start.1) | async-done | bytes 655392 | tf_op jit(solution)/shard_map/all_to_all | solution.py:435
  137.8 1.0 shard_map.94.rest_0_.rest_8_
  139.5 1.6 collective-permute-start.33
  141.1 1.1 collective-permute-start.32
  142.2 2.8 %collective-permute-done.30.rest_4_.rest_12_ = f32[328,128]{1,0:T(8,128)S(1)} collective-permute-done((f32[328,128]{1,0:T(8,128)S(1)}, f32[328,128]{1,0:T(8,128)S(1)}, u32[]{:S(2)}, u32[]{:S(2)}) %collective-permute-start.30) | collective-permute-done | bytes 167968 | tf_op jit(solution)/shard_map/ppermute | solution.py:440
  146.1 2.4 %collective-permute-start.39 = (f32[328,128]{1,0:T(8,128)S(1)}, f32[328,128]{1,0:T(8,128)S(1)}, u32[]{:S(2)}, u32[]{:S(2)}) collective-permute-start(f32[328,128]{1,0:T(8,128)S(1)} %collective-permute-done.36.rest_6_.rest_14_), channel_id=1, source_target_pairs={{0,4},{1,5},{2,6},{3,7},{4,0},{5,1},{6,2},{7,3},{8,12},{9,13},{10,... | collective-permute-start | bytes 503816 | tf_op jit(solution)/shard_map/ppermute | solution.py:440
  148.4 2.2 %collective-permute-start.35 = (f32[328,128]{1,0:T(8,128)S(1)}, f32[328,128]{1,0:T(8,128)S(1)}, u32[]{:S(2)}, u32[]{:S(2)}) collective-permute-start(f32[328,128]{1,0:T(8,128)S(1)} %collective-permute-done.30.rest_4_.rest_12_), channel_id=1, source_target_pairs={{0,1},{1,0},{2,3},{3,2},{4,5},{5,4},{6,7},{7,6},{8,9},{9,8},{10,11... | collective-permute-start | bytes 503816 | tf_op jit(solution)/shard_map/ppermute | solution.py:440
  151.8 1.0 collective-permute-start.41
  152.8 3.8 %copy-done.4 = bf16[40,2,15,32,128]{4,3,2,1,0:T(8,128)(2,1)S(1)} copy-done((bf16[40,2,15,32,128]{4,3,2,1,0:T(8,128)(2,1)S(1)}, bf16[40,2,15,32,128]{4,3,2,1,0:T(8,128)(2,1)}, u32[]{:S(2)}) %copy-start.4) | copy-done | bytes 9830424
  156.6 4.7 %shard_map.95 = (f32[2,15,32,128]{3,2,1,0:T(8,128)S(1)}, f32[4,88,128]{2,1,0:T(8,128)}, f32[4,88,128]{2,1,0:T(8,128)}, f32[328,128]{1,0:T(8,128)S(1)}) custom-call(s32[1]{0:T(128)} %bitcast.me_ref, s32[15]{0:T(128)S(1)} %copy-done.22, s32[15]{0:T(128)S(1)} %copy-done.24, ...), custom_call_target="tpu_custom_call", output_to_operand_aliasing={{3}: (5, {})} | custom-call | bytes 3690000 | tf_op jit(solution)/shard_map/pallas_call | solution.py:472
  161.4 2.9 %collective-permute-start.38 = (f32[328,128]{1,0:T(8,128)S(1)}, f32[328,128]{1,0:T(8,128)S(1)}, u32[]{:S(2)}, u32[]{:S(2)}) collective-permute-start(f32[328,128]{1,0:T(8,128)S(1)} %get-tuple-element.25.rest_0_), channel_id=1, source_target_pairs={{0,1},{1,0},{2,3},{3,2},{4,5},{5,4},{6,7},{7,6},{8,9},{9,8},{10,11... | collective-permute-start | bytes 503816 | tf_op jit(solution)/shard_map/ppermute | solution.py:440
  166.2 5.0 %shard_map.96 = (f32[2,15,32,128]{3,2,1,0:T(8,128)}, f32[2,160,128]{2,1,0:T(8,128)}) custom-call(s32[1]{0:T(128)} %bitcast.me_ref, s32[15]{0:T(128)S(1)} %copy-done.22, s32[15]{0:T(128)S(1)} %copy-done.24, bf16[40,2,15,32,128]{4,3,2,1,0:T(8,128)(2,1)S(1)} %copy-done.5, s32[15,32,128]{2,1,0:T(8,128)S(1)} %copy-done.8, ...), custom_call_target="tpu_custom_call" | custom-call | bytes 14760000 | tf_op jit(solution)/shard_map/pallas_call | solution.py:472
  (107 shorter events, 14.4 us)
Async XLA Ops:
  1.9 31.5 %copy-start.6 = (f32[2,15,32,128]{3,2,1,0:T(8,128)S(1)}, f32[2,15,32,128]{3,2,1,0:T(8,128)}, u32[]{:S(2)}) copy-start(f32[2,15,32,128]{3,2,1,0:T(8,128)} %vis_ref.5) | copy-start | bytes 1474564
  3.4 5.2 %collective-permute-start = (f32[328,128]{1,0:T(8,128)S(1)}, f32[328,128]{1,0:T(8,128)S(1)}, u32[]{:S(2)}, u32[]{:S(2)}) collective-permute-start(f32[328,128]{1,0:T(8,128)S(1)} %shard_map.86.rest_0_), channel_id=1, source_target_pairs={{0,4},{1,5},{2,6},{3,7},{4,0},{5,1},{6,2},{7,3},{8,12},{9,13},{10,... | collective-permute-start | bytes 503816 | tf_op jit(solution)/shard_map/ppermute | solution.py:440
  3.5 6.4 %collective-permute-start.7 = (f32[328,128]{1,0:T(8,128)S(1)}, f32[328,128]{1,0:T(8,128)S(1)}, u32[]{:S(2)}, u32[]{:S(2)}) collective-permute-start(f32[328,128]{1,0:T(8,128)S(1)} %shard_map.86.rest_0_), channel_id=1, source_target_pairs={{0,12},{1,13},{2,14},{3,15},{4,8},{5,9},{6,10},{7,11},{8,4},{9,5},... | collective-permute-start | bytes 503816 | tf_op jit(solution)/shard_map/ppermute | solution.py:440
  6.1 10.3 %collective-permute-start.3 = (f32[328,128]{1,0:T(8,128)S(1)}, f32[328,128]{1,0:T(8,128)S(1)}, u32[]{:S(2)}, u32[]{:S(2)}) collective-permute-start(f32[328,128]{1,0:T(8,128)S(1)} %shard_map.86.rest_0_), channel_id=1, source_target_pairs={{0,2},{1,3},{2,0},{3,1},{4,6},{5,7},{6,4},{7,5},{8,10},{9,11},{10,... | collective-permute-start | bytes 503816 | tf_op jit(solution)/shard_map/ppermute | solution.py:440
  8.7 8.2 %collective-permute-start.1 = (f32[328,128]{1,0:T(8,128)S(1)}, f32[328,128]{1,0:T(8,128)S(1)}, u32[]{:S(2)}, u32[]{:S(2)}) collective-permute-start(f32[328,128]{1,0:T(8,128)S(1)} %collective-permute-done.rest_4_), channel_id=1, source_target_pairs={{0,2},{1,3},{2,0},{3,1},{4,6},{5,7},{6,4},{7,5},{8,10},{9,11},{10,... | collective-permute-start | bytes 503816 | tf_op jit(solution)/shard_map/ppermute | solution.py:440
  9.9 8.2 %collective-permute-start.8 = (f32[328,128]{1,0:T(8,128)S(1)}, f32[328,128]{1,0:T(8,128)S(1)}, u32[]{:S(2)}, u32[]{:S(2)}) collective-permute-start(f32[328,128]{1,0:T(8,128)S(1)} %collective-permute-done.7.rest_12_), channel_id=1, source_target_pairs={{0,4},{1,5},{2,6},{3,7},{4,0},{5,1},{6,2},{7,3},{8,12},{9,13},{10,... | collective-permute-start | bytes 503816 | tf_op jit(solution)/shard_map/ppermute | solution.py:440
  14.5 13.4 %collective-permute-start.2 = (f32[328,128]{1,0:T(8,128)S(1)}, f32[328,128]{1,0:T(8,128)S(1)}, u32[]{:S(2)}, u32[]{:S(2)}) collective-permute-start(f32[328,128]{1,0:T(8,128)S(1)} %shard_map.86.rest_0_), channel_id=1, source_target_pairs={{0,1},{1,0},{2,3},{3,2},{4,5},{5,4},{6,7},{7,6},{8,9},{9,8},{10,11... | collective-permute-start | bytes 503816 | tf_op jit(solution)/shard_map/ppermute | solution.py:440
  16.4 14.8 %collective-permute-start.4 = (f32[328,128]{1,0:T(8,128)S(1)}, f32[328,128]{1,0:T(8,128)S(1)}, u32[]{:S(2)}, u32[]{:S(2)}) collective-permute-start(f32[328,128]{1,0:T(8,128)S(1)} %collective-permute-done.3.rest_2_), channel_id=1, source_target_pairs={{0,1},{1,0},{2,3},{3,2},{4,5},{5,4},{6,7},{7,6},{8,9},{9,8},{10,11... | collective-permute-start | bytes 503816 | tf_op jit(solution)/shard_map/ppermute | solution.py:440
  16.4 14.9 %collective-permute-start.5 = (f32[328,128]{1,0:T(8,128)S(1)}, f32[328,128]{1,0:T(8,128)S(1)}, u32[]{:S(2)}, u32[]{:S(2)}) collective-permute-start(f32[328,128]{1,0:T(8,128)S(1)} %collective-permute-done.rest_4_), channel_id=1, source_target_pairs={{0,1},{1,0},{2,3},{3,2},{4,5},{5,4},{6,7},{7,6},{8,9},{9,8},{10,11... | collective-permute-start | bytes 503816 | tf_op jit(solution)/shard_map/ppermute | solution.py:440
  16.9 14.8 %collective-permute-start.13 = (f32[328,128]{1,0:T(8,128)S(1)}, f32[328,128]{1,0:T(8,128)S(1)}, u32[]{:S(2)}, u32[]{:S(2)}) collective-permute-start(f32[328,128]{1,0:T(8,128)S(1)} %collective-permute-done.7.rest_12_), channel_id=1, source_target_pairs={{0,2},{1,3},{2,0},{3,1},{4,6},{5,7},{6,4},{7,5},{8,10},{9,11},{10,... | collective-permute-start | bytes 503816 | tf_op jit(solution)/shard_map/ppermute | solution.py:440
  18.1 13.7 %collective-permute-start.10 = (f32[328,128]{1,0:T(8,128)S(1)}, f32[328,128]{1,0:T(8,128)S(1)}, u32[]{:S(2)}, u32[]{:S(2)}) collective-permute-start(f32[328,128]{1,0:T(8,128)S(1)} %collective-permute-done.8.rest_8_), channel_id=1, source_target_pairs={{0,2},{1,3},{2,0},{3,1},{4,6},{5,7},{6,4},{7,5},{8,10},{9,11},{10,... | collective-permute-start | bytes 503816 | tf_op jit(solution)/shard_map/ppermute | solution.py:440
  27.9 4.4 %collective-permute-start.12 = (f32[328,128]{1,0:T(8,128)S(1)}, f32[328,128]{1,0:T(8,128)S(1)}, u32[]{:S(2)}, u32[]{:S(2)}) collective-permute-start(f32[328,128]{1,0:T(8,128)S(1)} %collective-permute-done.7.rest_12_), channel_id=1, source_target_pairs={{0,1},{1,0},{2,3},{3,2},{4,5},{5,4},{6,7},{7,6},{8,9},{9,8},{10,11... | collective-permute-start | bytes 503816 | tf_op jit(solution)/shard_map/ppermute | solution.py:440
  31.2 1.4 collective-permute-start.6
  31.3 1.7 collective-permute-start.9
  31.7 1.5 collective-permute-start.14
  31.8 1.7 collective-permute-start.11
  47.6 29.1 %all-to-all-start = ((f32[16,120,128]{2,1,0:T(8,128)}), f32[16,120,128]{2,1,0:T(8,128)S(1)}, u32[]{:S(2)}, u32[]{:S(2)}) async-start(f32[16,120,128]{2,1,0:T(8,128)} %shard_map.89), calls=%async_computation | async-start | bytes 1966080 | tf_op jit(solution)/shard_map/all_to_all | solution.py:435
  79.2 6.2 %collective-permute-start.15 = (f32[328,128]{1,0:T(8,128)S(1)}, f32[328,128]{1,0:T(8,128)S(1)}, u32[]{:S(2)}, u32[]{:S(2)}) collective-permute-start(f32[328,128]{1,0:T(8,128)S(1)} %shard_map.90.g_ref.rest_0_.g_in), channel_id=1, source_target_pairs={{0,4},{1,5},{2,6},{3,7},{4,0},{5,1},{6,2},{7,3},{8,12},{9,13},{10,... | collective-permute-start | bytes 503816 | tf_op jit(solution)/shard_map/ppermute | solution.py:440
  79.3 6.8 %collective-permute-start.21 = (f32[328,128]{1,0:T(8,128)S(1)}, f32[328,128]{1,0:T(8,128)S(1)}, u32[]{:S(2)}, u32[]{:S(2)}) collective-permute-start(f32[328,128]{1,0:T(8,128)S(1)} %shard_map.90.g_ref.rest_0_.g_in), channel_id=1, source_target_pairs={{0,12},{1,13},{2,14},{3,15},{4,8},{5,9},{6,10},{7,11},{8,4},{9,5},... | collective-permute-start | bytes 503816 | tf_op jit(solution)/shard_map/ppermute | solution.py:440
  80.3 11.4 %collective-permute-start.18 = (f32[328,128]{1,0:T(8,128)S(1)}, f32[328,128]{1,0:T(8,128)S(1)}, u32[]{:S(2)}, u32[]{:S(2)}) collective-permute-start(f32[328,128]{1,0:T(8,128)S(1)} %shard_map.90.g_ref.rest_0_.g_in), channel_id=1, source_target_pairs={{0,2},{1,3},{2,0},{3,1},{4,6},{5,7},{6,4},{7,5},{8,10},{9,11},{10,... | collective-permute-start | bytes 503816 | tf_op jit(solution)/shard_map/ppermute | solution.py:440
  81.8 9.8 %collective-permute-start.17 = (f32[328,128]{1,0:T(8,128)S(1)}, f32[328,128]{1,0:T(8,128)S(1)}, u32[]{:S(2)}, u32[]{:S(2)}) collective-permute-start(f32[328,128]{1,0:T(8,128)S(1)} %shard_map.90.g_ref.rest_0_.g_in), channel_id=1, source_target_pairs={{0,1},{1,0},{2,3},{3,2},{4,5},{5,4},{6,7},{7,6},{8,9},{9,8},{10,11... | collective-permute-start | bytes 503816 | tf_op jit(solution)/shard_map/ppermute | solution.py:440
  85.4 6.8 %collective-permute-start.16 = (f32[328,128]{1,0:T(8,128)S(1)}, f32[328,128]{1,0:T(8,128)S(1)}, u32[]{:S(2)}, u32[]{:S(2)}) collective-permute-start(f32[328,128]{1,0:T(8,128)S(1)} %collective-permute-done.15.rest_4_), channel_id=1, source_target_pairs={{0,2},{1,3},{2,0},{3,1},{4,6},{5,7},{6,4},{7,5},{8,10},{9,11},{10,... | collective-permute-start | bytes 503816 | tf_op jit(solution)/shard_map/ppermute | solution.py:440
  86.1 6.4 %collective-permute-start.24 = (f32[328,128]{1,0:T(8,128)S(1)}, f32[328,128]{1,0:T(8,128)S(1)}, u32[]{:S(2)}, u32[]{:S(2)}) collective-permute-start(f32[328,128]{1,0:T(8,128)S(1)} %collective-permute-done.21.rest_6_), channel_id=1, source_target_pairs={{0,4},{1,5},{2,6},{3,7},{4,0},{5,1},{6,2},{7,3},{8,12},{9,13},{10,... | collective-permute-start | bytes 503816 | tf_op jit(solution)/shard_map/ppermute | solution.py:440
  89.6 4.1 %collective-permute-start.20 = (f32[328,128]{1,0:T(8,128)S(1)}, f32[328,128]{1,0:T(8,128)S(1)}, u32[]{:S(2)}, u32[]{:S(2)}) collective-permute-start(f32[328,128]{1,0:T(8,128)S(1)} %collective-permute-done.15.rest_4_), channel_id=1, source_target_pairs={{0,1},{1,0},{2,3},{3,2},{4,5},{5,4},{6,7},{7,6},{8,9},{9,8},{10,11... | collective-permute-start | bytes 503816 | tf_op jit(solution)/shard_map/ppermute | solution.py:440
  91.7 2.0 %collective-permute-start.19 = (f32[328,128]{1,0:T(8,128)S(1)}, f32[328,128]{1,0:T(8,128)S(1)}, u32[]{:S(2)}, u32[]{:S(2)}) collective-permute-start(f32[328,128]{1,0:T(8,128)S(1)} %collective-permute-done.18.rest_2_), channel_id=1, source_target_pairs={{0,1},{1,0},{2,3},{3,2},{4,5},{5,4},{6,7},{7,6},{8,9},{9,8},{10,11... | collective-permute-start | bytes 503816 | tf_op jit(solution)/shard_map/ppermute | solution.py:440
  91.7 2.0 %collective-permute-start.22 = (f32[328,128]{1,0:T(8,128)S(1)}, f32[328,128]{1,0:T(8,128)S(1)}, u32[]{:S(2)}, u32[]{:S(2)}) collective-permute-start(f32[328,128]{1,0:T(8,128)S(1)} %collective-permute-done.21.rest_6_), channel_id=1, source_target_pairs={{0,1},{1,0},{2,3},{3,2},{4,5},{5,4},{6,7},{7,6},{8,9},{9,8},{10,11... | collective-permute-start | bytes 503816 | tf_op jit(solution)/shard_map/ppermute | solution.py:440
  92.2 12.2 %collective-permute-start.28 = (f32[328,128]{1,0:T(8,128)S(1)}, f32[328,128]{1,0:T(8,128)S(1)}, u32[]{:S(2)}, u32[]{:S(2)}) collective-permute-start(f32[328,128]{1,0:T(8,128)S(1)} %collective-permute-done.21.rest_6_), channel_id=1, source_target_pairs={{0,2},{1,3},{2,0},{3,1},{4,6},{5,7},{6,4},{7,5},{8,10},{9,11},{10,... | collective-permute-start | bytes 503816 | tf_op jit(solution)/shard_map/ppermute | solution.py:440
  92.5 12.4 %collective-permute-start.26 = (f32[328,128]{1,0:T(8,128)S(1)}, f32[328,128]{1,0:T(8,128)S(1)}, u32[]{:S(2)}, u32[]{:S(2)}) collective-permute-start(f32[328,128]{1,0:T(8,128)S(1)} %collective-permute-done.24.rest_2_), channel_id=1, source_target_pairs={{0,2},{1,3},{2,0},{3,1},{4,6},{5,7},{6,4},{7,5},{8,10},{9,11},{10,... | collective-permute-start | bytes 503816 | tf_op jit(solution)/shard_map/ppermute | solution.py:440
  101.5 3.8 %collective-permute-start.23 = (f32[328,128]{1,0:T(8,128)S(1)}, f32[328,128]{1,0:T(8,128)S(1)}, u32[]{:S(2)}, u32[]{:S(2)}) collective-permute-start(f32[328,128]{1,0:T(8,128)S(1)} %get-tuple-element.23.rest_0_), channel_id=1, source_target_pairs={{0,1},{1,0},{2,3},{3,2},{4,5},{5,4},{6,7},{7,6},{8,9},{9,8},{10,11... | collective-permute-start | bytes 503816 | tf_op jit(solution)/shard_map/ppermute | solution.py:440
  104.3 1.4 collective-permute-start.25
  104.4 1.6 collective-permute-start.29
  104.9 1.4 collective-permute-start.27
  115.2 22.6 %all-to-all-start.1 = ((f32[16,80,128]{2,1,0:T(8,128)}), f32[16,80,128]{2,1,0:T(8,128)S(1)}, u32[]{:S(2)}, u32[]{:S(2)}) async-start(f32[16,80,128]{2,1,0:T(8,128)} %shard_map.93), calls=%async_computation.1 | async-start | bytes 1310720 | tf_op jit(solution)/shard_map/all_to_all | solution.py:435
  138.9 6.1 %collective-permute-start.30 = (f32[328,128]{1,0:T(8,128)S(1)}, f32[328,128]{1,0:T(8,128)S(1)}, u32[]{:S(2)}, u32[]{:S(2)}) collective-permute-start(f32[328,128]{1,0:T(8,128)S(1)} %shard_map.94.rest_0_.rest_8_), channel_id=1, source_target_pairs={{0,4},{1,5},{2,6},{3,7},{4,0},{5,1},{6,2},{7,3},{8,12},{9,13},{10,... | collective-permute-start | bytes 503816 | tf_op jit(solution)/shard_map/ppermute | solution.py:440
  139.0 7.1 %collective-permute-start.36 = (f32[328,128]{1,0:T(8,128)S(1)}, f32[328,128]{1,0:T(8,128)S(1)}, u32[]{:S(2)}, u32[]{:S(2)}) collective-permute-start(f32[328,128]{1,0:T(8,128)S(1)} %shard_map.94.rest_0_.rest_8_), channel_id=1, source_target_pairs={{0,12},{1,13},{2,14},{3,15},{4,8},{5,9},{6,10},{7,11},{8,4},{9,5},... | collective-permute-start | bytes 503816 | tf_op jit(solution)/shard_map/ppermute | solution.py:440
  139.5 11.2 %collective-permute-start.33 = (f32[328,128]{1,0:T(8,128)S(1)}, f32[328,128]{1,0:T(8,128)S(1)}, u32[]{:S(2)}, u32[]{:S(2)}) collective-permute-start(f32[328,128]{1,0:T(8,128)S(1)} %shard_map.94.rest_0_.rest_8_), channel_id=1, source_target_pairs={{0,2},{1,3},{2,0},{3,1},{4,6},{5,7},{6,4},{7,5},{8,10},{9,11},{10,... | collective-permute-start | bytes 503816 | tf_op jit(solution)/shard_map/ppermute | solution.py:440
  141.1 9.6 %collective-permute-start.32 = (f32[328,128]{1,0:T(8,128)S(1)}, f32[328,128]{1,0:T(8,128)S(1)}, u32[]{:S(2)}, u32[]{:S(2)}) collective-permute-start(f32[328,128]{1,0:T(8,128)S(1)} %shard_map.94.rest_0_.rest_8_), channel_id=1, source_target_pairs={{0,1},{1,0},{2,3},{3,2},{4,5},{5,4},{6,7},{7,6},{8,9},{9,8},{10,11... | collective-permute-start | bytes 503816 | tf_op jit(solution)/shard_map/ppermute | solution.py:440
  145.0 6.2 %collective-permute-start.31 = (f32[328,128]{1,0:T(8,128)S(1)}, f32[328,128]{1,0:T(8,128)S(1)}, u32[]{:S(2)}, u32[]{:S(2)}) collective-permute-start(f32[328,128]{1,0:T(8,128)S(1)} %collective-permute-done.30.rest_4_.rest_12_), channel_id=1, source_target_pairs={{0,2},{1,3},{2,0},{3,1},{4,6},{5,7},{6,4},{7,5},{8,10},{9,11},{10,... | collective-permute-start | bytes 503816 | tf_op jit(solution)/shard_map/ppermute | solution.py:440
  146.1 5.7 %collective-permute-start.39 = (f32[328,128]{1,0:T(8,128)S(1)}, f32[328,128]{1,0:T(8,128)S(1)}, u32[]{:S(2)}, u32[]{:S(2)}) collective-permute-start(f32[328,128]{1,0:T(8,128)S(1)} %collective-permute-done.36.rest_6_.rest_14_), channel_id=1, source_target_pairs={{0,4},{1,5},{2,6},{3,7},{4,0},{5,1},{6,2},{7,3},{8,12},{9,13},{10,... | collective-permute-start | bytes 503816 | tf_op jit(solution)/shard_map/ppermute | solution.py:440
  148.4 4.4 %collective-permute-start.35 = (f32[328,128]{1,0:T(8,128)S(1)}, f32[328,128]{1,0:T(8,128)S(1)}, u32[]{:S(2)}, u32[]{:S(2)}) collective-permute-start(f32[328,128]{1,0:T(8,128)S(1)} %collective-permute-done.30.rest_4_.rest_12_), channel_id=1, source_target_pairs={{0,1},{1,0},{2,3},{3,2},{4,5},{5,4},{6,7},{7,6},{8,9},{9,8},{10,11... | collective-permute-start | bytes 503816 | tf_op jit(solution)/shard_map/ppermute | solution.py:440
  150.7 2.1 %collective-permute-start.34 = (f32[328,128]{1,0:T(8,128)S(1)}, f32[328,128]{1,0:T(8,128)S(1)}, u32[]{:S(2)}, u32[]{:S(2)}) collective-permute-start(f32[328,128]{1,0:T(8,128)S(1)} %collective-permute-done.33.rest_2_.rest_10_), channel_id=1, source_target_pairs={{0,1},{1,0},{2,3},{3,2},{4,5},{5,4},{6,7},{7,6},{8,9},{9,8},{10,11... | collective-permute-start | bytes 503816 | tf_op jit(solution)/shard_map/ppermute | solution.py:440
  150.7 2.1 %collective-permute-start.37 = (f32[328,128]{1,0:T(8,128)S(1)}, f32[328,128]{1,0:T(8,128)S(1)}, u32[]{:S(2)}, u32[]{:S(2)}) collective-permute-start(f32[328,128]{1,0:T(8,128)S(1)} %collective-permute-done.36.rest_6_.rest_14_), channel_id=1, source_target_pairs={{0,1},{1,0},{2,3},{3,2},{4,5},{5,4},{6,7},{7,6},{8,9},{9,8},{10,11... | collective-permute-start | bytes 503816 | tf_op jit(solution)/shard_map/ppermute | solution.py:440
  151.2 13.1 %collective-permute-start.43 = (f32[328,128]{1,0:T(8,128)S(1)}, f32[328,128]{1,0:T(8,128)S(1)}, u32[]{:S(2)}, u32[]{:S(2)}) collective-permute-start(f32[328,128]{1,0:T(8,128)S(1)} %collective-permute-done.36.rest_6_.rest_14_), channel_id=1, source_target_pairs={{0,2},{1,3},{2,0},{3,1},{4,6},{5,7},{6,4},{7,5},{8,10},{9,11},{10,... | collective-permute-start | bytes 503816 | tf_op jit(solution)/shard_map/ppermute | solution.py:440
  151.8 13.0 %collective-permute-start.41 = (f32[328,128]{1,0:T(8,128)S(1)}, f32[328,128]{1,0:T(8,128)S(1)}, u32[]{:S(2)}, u32[]{:S(2)}) collective-permute-start(f32[328,128]{1,0:T(8,128)S(1)} %collective-permute-done.39.rest_2_), channel_id=1, source_target_pairs={{0,2},{1,3},{2,0},{3,1},{4,6},{5,7},{6,4},{7,5},{8,10},{9,11},{10,... | collective-permute-start | bytes 503816 | tf_op jit(solution)/shard_map/ppermute | solution.py:440
  161.4 3.9 %collective-permute-start.38 = (f32[328,128]{1,0:T(8,128)S(1)}, f32[328,128]{1,0:T(8,128)S(1)}, u32[]{:S(2)}, u32[]{:S(2)}) collective-permute-start(f32[328,128]{1,0:T(8,128)S(1)} %get-tuple-element.25.rest_0_), channel_id=1, source_target_pairs={{0,1},{1,0},{2,3},{3,2},{4,5},{5,4},{6,7},{7,6},{8,9},{9,8},{10,11... | collective-permute-start | bytes 503816 | tf_op jit(solution)/shard_map/ppermute | solution.py:440
  164.2 1.4 collective-permute-start.40
  164.3 1.6 collective-permute-start.44
  164.8 1.4 collective-permute-start.42
  (24 other events, 162.6 us)

commit v10 on v8

--- a/solution.py
+++ b/solution.py
@@ -44,66 +44,69 @@
 
 
 TILE = 8
-PARTS = (1, 3, 7, ROWS)
-
-
-def pack_kernel(n, dpc, first_ref, second_ref, re_ref, im_ref, out_ref, sems):
-    rows = re_ref.shape[0]
+
+
+def pack_kernel(n, dpc, first_hbm, second_hbm, re_hbm, im_hbm, out_ref, first_ref, second_ref, sems):
+    rows = re_hbm.shape[0]
     copies = [
-        pltpu.make_async_copy(re_ref, out_ref.at[pl.ds(0, rows)], sems.at[0]),
-        pltpu.make_async_copy(im_ref, out_ref.at[pl.ds(rows, rows)], sems.at[1]),
+        pltpu.make_async_copy(first_hbm, first_ref, sems.at[0]),
+        pltpu.make_async_copy(second_hbm, second_ref, sems.at[1]),
+        pltpu.make_async_copy(re_hbm, out_ref.at[pl.ds(0, rows)], sems.at[2]),
+        pltpu.make_async_copy(im_hbm, out_ref.at[pl.ds(rows, rows)], sems.at[3]),
     ]
     for copy in copies:
         copy.start()
-    lane = lax.broadcasted_iota(jnp.int32, (TILE, 128), 1)
-    marks = jnp.zeros((TILE, 128), F32)
-    for r in range(first_ref.shape[0]):
-        marks = jnp.where(lane == r, (first_ref[r] + 1).astype(F32), marks)
-        marks = jnp.where(lane == ROWS + r, (second_ref[r] + 1).astype(F32), marks)
-    out_ref[2 * rows :] = marks
+    out_ref[2 * rows :] = jnp.zeros((TILE, 128), F32)
     for copy in copies:
         copy.wait()
+    pairs = first_ref.shape[1]
+    out_ref[2 * rows : 2 * rows + 1, :pairs] = (first_ref[...] + 1).astype(F32)
+    out_ref[2 * rows : 2 * rows + 1, ROWS : ROWS + pairs] = (second_ref[...] + 1).astype(F32)
 
 
 class Fetch:
     def __init__(self, model, held, sems, firsts=(0,)):
-        count, pairs = held.shape[0] // len(firsts), held.shape[2]
-        self.copies = []
-        self.ends = [0] + [min(end, pairs) for end in PARTS]
-        for i in range(len(PARTS)):
-            part = pl.ds(self.ends[i], self.ends[i + 1] - self.ends[i])
-            self.copies.append([])
-            for j, first in enumerate(firsts):
-                self.copies[i].append(
-                    pltpu.make_async_copy(
-                        model.at[pl.ds(first, count), :, part],
-                        held.at[pl.ds(j * count, count), :, part],
-                        sems.at[i, j],
-                    )
-                )
-        for copies in self.copies:
-            for copy in copies:
+        self.model, self.held, self.sems, self.firsts = model, held, sems, firsts
+        self.pairs = held.shape[2]
+        self.size = 3 if self.pairs % 3 == 0 else 1
+        for i in range(self.pairs // self.size):
+            for copy in self.part(i):
                 copy.start()
 
+    def part(self, i):
+        count = self.held.shape[0] // len(self.firsts)
+        pairs = pl.ds(i * self.size, self.size)
+        return [
+            pltpu.make_async_copy(
+                self.model.at[pl.ds(first, count), :, pairs],
+                self.held.at[pl.ds(j * count, count), :, pairs],
+                self.sems.at[i, j],
+            )
+            for j, first in enumerate(self.firsts)
+        ]
+
     def each(self, body):
-        for i, copies in enumerate(self.copies):
-            for copy in copies:
+        def part(i, carry):
+            for copy in self.part(i):
                 copy.wait()
-            lax.fori_loop(self.ends[i], self.ends[i + 1], body, 0)
+            for u in range(self.size):
+                body(i * self.size + u)
+            return carry
+
+        lax.fori_loop(0, self.pairs // self.size, part, 0)
 
 
 def power_kernel(n, dpc, model_hbm, mask_ref, unused_in, out_ref, unused_out, model_ref, sems):
     fetch = Fetch(model_hbm, model_ref, sems)
     out_ref[...] = jnp.zeros_like(out_ref)
 
-    def pair(b, carry):
+    def pair(b):
         weight = mask_ref[b].astype(F32)
         for d in range(SOURCE_COUNT):
             mr = model_ref[d, 0, b].astype(F32)
             mi = model_ref[d, 1, b].astype(F32)
             row = pl.ds(b * dpc + d % dpc, 1)
             out_ref[d // dpc, row, :] = jnp.sum(weight * (mr * mr + mi * mi), axis=0, keepdims=True)
-        return carry
 
     fetch.each(pair)
 
@@ -118,9 +121,9 @@
     ref[STATIONS * dpc :, :] = jnp.zeros((TILE, 128), F32)
 
 
-def first_own_kernel(n, dpc, me_ref, *rest):
+def first_own_kernel(n, dpc, *rest):
     ins, (g_ref, onehot_ref, split, lines) = rest[:n], rest[n:]
-    me = me_ref[0]
+    me = lax.axis_index("bl")
     k, c = lax.div(me, 2), lax.rem(me, 2)
     per = STATIONS // n
     rows = per * SOURCE_COUNT
@@ -207,14 +210,14 @@
             ref[m, pairs * dpc :, :] = jnp.zeros((rows - pairs * dpc, 128), F32)
 
 
-def products_first(n, dpc, me, first_ref, second_ref, ins, hre, him, stack):
+def products_first(n, dpc, me, pairs, ends_ref, ins, hre, him, stack):
     per = STATIONS // n
     rows = per * SOURCE_COUNT
     for o in range(n):
         stack[jnp.bitwise_xor(me, o)] = ins[o][...]
 
     def pair(b, carry):
-        p, q = first_ref[b], second_ref[b]
+        p, q = ends_ref[b], ends_ref[pairs + b]
 
         def block(station, k, part):
             at = lax.rem(station, per) * SOURCE_COUNT + k * dpc + part * rows
@@ -226,8 +229,8 @@
             him[k, pl.ds(b * dpc, TILE), :] = pi * qr - pr * qi
         return carry
 
-    lax.fori_loop(0, first_ref.shape[0], pair, 0)
-    clear(dpc, first_ref.shape[0], hre, him)
+    lax.fori_loop(0, pairs, pair, 0, unroll=5 if pairs % 5 == 0 else 1)
+    clear(dpc, pairs, hre, him)
 
 
 def piece_pair(dpc, even, ins, m, station):
@@ -236,11 +239,11 @@
     return cross(jnp.where(even, a, b), jnp.where(even, b, a))
 
 
-def products(dpc, me, first_ref, second_ref, ins, hre, him):
+def products(dpc, me, pairs, ends_ref, ins, hre, him):
     even = lax.rem(me, 2) == 0
 
     def pair(b, carry):
-        p, q = first_ref[b], second_ref[b]
+        p, q = ends_ref[b], ends_ref[pairs + b]
         for m in range(len(ins) // 2):
             pr, pi = piece_pair(dpc, even, ins, m, p)
             qr, qi = piece_pair(dpc, even, ins, m, q)
@@ -248,8 +251,8 @@
             him[m, pl.ds(b * dpc, TILE), :] = pi * qr - pr * qi
         return carry
 
-    lax.fori_loop(0, first_ref.shape[0], pair, 0)
-    clear(dpc, first_ref.shape[0], hre, him)
+    lax.fori_loop(0, pairs, pair, 0, unroll=5 if pairs % 5 == 0 else 1)
+    clear(dpc, pairs, hre, him)
 
 
 def predict(dpc, b, acc, chips, model_ref, hre, him):
@@ -330,18 +333,15 @@
                 out_ref[2 * k + 1, rows, :] = x1
 
 
-def first_pass_kernel(
-    n, dpc, me_ref, first_ref, second_ref, model_hbm, vis_ref, mask_ref, power_ref, *rest
-):
+def first_pass_kernel(n, dpc, ends_ref, model_hbm, vis_ref, mask_ref, power_ref, *rest):
     ins, (out_ref, model_ref, sems, hre, him, cre, cim, stack) = rest[:n], rest[n:]
     fetch = Fetch(model_hbm, model_ref, sems)
-    products_first(n, dpc, me_ref[0], first_ref, second_ref, ins, hre, him, stack)
+    products_first(n, dpc, lax.axis_index("bl"), mask_ref.shape[0], ends_ref, ins, hre, him, stack)
     chips = range(n // 2)
 
-    def pair(b, carry):
+    def pair(b):
         acc = predict(dpc, b, (vis_ref[0, b], vis_ref[1, b]), chips, model_ref, hre, him)
         correlate(dpc, b, weighted(b, acc, mask_ref), chips, model_ref, cre, cim)
-        return carry
 
     fetch.each(pair)
 
@@ -356,16 +356,15 @@
     return [jnp.bitwise_xor(lax.div(me, 2), m) for m in pairs]
 
 
-def early_kernel(n, dpc, me_ref, first_ref, second_ref, model_hbm, vis_ref, unused_in, *rest):
+def early_kernel(n, dpc, ends_ref, model_hbm, vis_ref, unused_in, *rest):
     ins, (acc_ref, hre, him, unused_out, model_ref, sems) = rest[: 2 * len(NEAR)], rest[2 * len(NEAR) :]
-    me = me_ref[0]
+    me = lax.axis_index("bl")
     fetch = Fetch(model_hbm, model_ref, sems, [k * dpc for k in chips_of(me, NEAR)])
-    products(dpc, me, first_ref, second_ref, ins, hre, him)
-
-    def pair(b, carry):
+    products(dpc, me, model_hbm.shape[2], ends_ref, ins, hre, him)
+
+    def pair(b):
         acc = vis_ref[0, b], vis_ref[1, b]
         acc_ref[0, b], acc_ref[1, b] = predict(dpc, b, acc, range(len(NEAR)), model_ref, hre, him)
-        return carry
 
     fetch.each(pair)
 
@@ -373,9 +372,7 @@
 def later_pass_kernel(
     n,
     dpc,
-    me_ref,
-    first_ref,
-    second_ref,
+    ends_ref,
     model_hbm,
     mask_ref,
     power_ref,
@@ -386,15 +383,14 @@
 ):
     ins, (out_ref, model_ref, sems, hre, him, cre, cim) = rest[: 2 * len(FAR)], rest[2 * len(FAR) :]
     fetch = Fetch(model_hbm, model_ref, sems)
-    me = me_ref[0]
-    products(dpc, me, first_ref, second_ref, ins, hre, him)
+    me = lax.axis_index("bl")
+    products(dpc, me, model_hbm.shape[2], ends_ref, ins, hre, him)
     far = chips_of(me, FAR)
     chips = chips_of(me, NEAR) + far
 
-    def pair(b, carry):
+    def pair(b):
         acc = predict(dpc, b, (acc_ref[0, b], acc_ref[1, b]), far, model_ref, hre, him)
         correlate(dpc, b, weighted(b, acc, mask_ref), chips, model_ref, cre, cim)
-        return carry
 
     fetch.each(pair)
 
@@ -408,11 +404,11 @@
     write_sums(dpc, chips, cre, cim, tiles, power_ref, out_ref, False)
 
 
-def last_kernel(n, dpc, me_ref, first_ref, second_ref, model_hbm, mask_ref, acc_ref, *rest):
+def last_kernel(n, dpc, ends_ref, model_hbm, mask_ref, acc_ref, *rest):
     ins, (res_ref, gains_ref, model_ref, sems, hre, him) = rest[:n], rest[n:]
-    me = me_ref[0]
+    me = lax.axis_index("bl")
     fetch = Fetch(model_hbm, model_ref, sems, [k * dpc for k in chips_of(me, FAR)])
-    products(dpc, me, first_ref, second_ref, ins[: 2 * len(FAR)], hre, him)
+    products(dpc, me, model_hbm.shape[2], ends_ref, ins[: 2 * len(FAR)], hre, him)
     per = STATIONS // n
     even = lax.rem(me, 2) == 0
     for m, k in enumerate(chips_of(me, FAR + NEAR)):
@@ -423,11 +419,10 @@
                 gains_ref[0, pl.ds(at, 1), :] = re[dd : dd + 1]
                 gains_ref[1, pl.ds(at, 1), :] = im[dd : dd + 1]
 
-    def pair(b, carry):
+    def pair(b):
         acc = acc_ref[0, b], acc_ref[1, b]
         acc = predict(dpc, b, acc, range(len(FAR)), model_ref, hre, him)
         res_ref[0, b], res_ref[1, b] = weighted(b, acc, mask_ref)
-        return carry
 
     fetch.each(pair)
 
@@ -461,23 +456,24 @@
 
 
 def fast_body(n, vis, model, mask, first, second, gre, gim):
-    model, gre, gim = (pltpu.with_memory_space_constraint(x, pltpu.HBM) for x in (model, gre, gim))
+    ends = jnp.concatenate([first, second])
+    starts = (first.reshape(1, -1), second.reshape(1, -1), gre, gim)
+    model, *starts = (pltpu.with_memory_space_constraint(x, pltpu.HBM) for x in (model, *starts))
     dpc = SOURCE_COUNT // (n // 2)
     width = dpc * 128
     pairs, times, channels = mask.shape
-    me = lax.axis_index("bl").astype(jnp.int32).reshape(1)
     params = pltpu.CompilerParams(vmem_limit_bytes=VMEM_LIMIT)
     plane = (n // 2, ROWS * dpc + TILE, channels)
     half = (len(FAR), ROWS * dpc + TILE, channels)
     lots = n * 2 * ROWS
     mine = (STATIONS * dpc + TILE, channels)
-    sems = pltpu.SemaphoreType.DMA((len(PARTS), n // 4))
+    sems = pltpu.SemaphoreType.DMA((pairs, n // 4))
     held = [pltpu.VMEM(model.shape, BF16), sems]
     held_half = [pltpu.VMEM((SOURCE_COUNT // 2,) + model.shape[1:], BF16), sems]
 
     def call(kernel, args, outs, scratch=(), micros=1, aliases={}):
         def place(x):
-            if x is model or x is gre or x is gim:
+            if x is model or any(x is y for y in starts):
                 return HBM
             return SMEM if x.ndim == 1 else VMEM
 
@@ -496,9 +492,9 @@
 
     (piece,) = call(
         pack_kernel,
-        (first, second, gre, gim),
+        starts,
         [shape(2 * gre.shape[0] + TILE, channels)],
-        [pltpu.SemaphoreType.DMA((2,))],
+        [pltpu.VMEM((1, pairs), jnp.int32)] * 2 + [pltpu.SemaphoreType.DMA((4,))],
     )
     power = None
 
@@ -512,14 +508,14 @@
     got = gather(n, piece, powers_beside)
     g, onehot = call(
         first_own_kernel,
-        (me, *got),
+        got,
         [shape(*mine), shape(STATIONS, lots, dtype=BF16)],
         [(STATIONS * TILE, channels), (n, channels)],
         micros=2,
     )
     (sums,) = call(
         first_pass_kernel,
-        (me, first, second, model, vis, mask, power, *got),
+        (ends, model, vis, mask, power, *got),
         [shape(n, (ROWS + TILE) * dpc, channels)],
         held + [plane] * 4 + [(n,) + piece.shape],
         micros=9,
@@ -540,9 +536,9 @@
 
         def beside(x, got):
             nonlocal near
-            args = (me, first, second, model, vis, x, *slots(got, NEAR))
+            args = (ends, model, vis, x, *slots(got, NEAR))
             outs = [shape(*vis.shape), shape(*half), shape(*half), shape(*x.shape)]
-            *near, x = call(early_kernel, args, outs, held_half, aliases={5: 3})
+            *near, x = call(early_kernel, args, outs, held_half, aliases={3: 3})
             return x
 
         got = gather(n, g, beside)
@@ -559,7 +555,7 @@
         )
         (sums,) = call(
             later_pass_kernel,
-            (me, first, second, model, mask, power, *near, *got[: 2 * len(FAR)]),
+            (ends, model, mask, power, *near, *got[: 2 * len(FAR)]),
             [shape(n, ROWS * dpc, channels)],
             held + [half] * 2 + [plane] * 2,
             micros=7,
@@ -574,7 +570,7 @@
     near, got = gather_near(g)
     residual, gains = call(
         last_kernel,
-        (me, first, second, model, mask, near[0], *got),
+        (ends, model, mask, near[0], *got),
         [shape(*vis.shape), shape(2, *gre.shape)],
         held_half + [half] * 2,
         micros=4,

time: 161 us -> 164 us (1.019)
  local copies, waits for them, and re-layouts: 8.44 us -> 15.2 us
  waiting for transfers between devices: 43.9 us -> 41.8 us
    unnamed x38 -> x46, local copies, waits for them, and re-layouts: 8.44 us -> 15.2 us
    all_to_all x2, waiting for transfers between devices: 32.7 us -> 31.1 us  [exchange(): return lax.all_to_all(x, 'bl', split_axis=0, concat_axis=0, tiled=True)]
  transfers between devices with their start and end apart: 47 -> 47, of which waited for: 16 -> 17; matrix products, arithmetic and copies ran while one was open for 0% -> 0% of each run, Pallas kernels for 11% -> 10%
where the time goes in v10:
time: 164 us; the launch traced here: 162 us
  starting transfers between devices  59.1 us (36%)
  Pallas kernels  44.4 us (27%)
  waiting for transfers between devices  41.8 us (25%)
  local copies, waits for them, and re-layouts  15.2 us (9%)
    ppermute x45, starting transfers between devices, send(): return lax.ppermute(x, 'bl', [(i, i ^ o) for i in range(n)])  48.4 us
    pallas_call x11, Pallas kernels, call(): pl.pallas_call(functools.partial(kernel, n, dpc), in_specs=[place(x) for...  44.4 us
    all_to_all x2, waiting for transfers between devices, exchange(): return lax.all_to_all(x, 'bl', split_axis=0, concat_axis=0, tiled=True)  31.1 us
    unnamed x46, local copies, waits for them, and re-layouts  15.2 us
    all_to_all x2, starting transfers between devices, exchange(): return lax.all_to_all(x, 'bl', split_axis=0, concat_axis=0, tiled=True)  10.7 us
    ppermute x45, waiting for transfers between devices, send(): return lax.ppermute(x, 'bl', [(i, i ^ o) for i in range(n)])  10.7 us
  transfers between devices with their start and end apart: 47, of which 17 were waited for; matrix products, arithmetic and copies ran while one was open for 0% of the time, Pallas kernels for 10%

profile of v10, /device:TPU:9, one launch (start us, length us, event | category | flops | bytes accessed | tf_op | source)
XLA Modules:
  0.0 161.5 jit_solution(12295236577687858190)
XLA Ops:
  0.6 1.1 shard_map.86.rest_0_
  1.8 2.6 %collective-permute-start.7 = (f32[328,128]{1,0:T(8,128)S(1)}, f32[328,128]{1,0:T(8,128)S(1)}, u32[]{:S(2)}, u32[]{:S(2)}) collective-permute-start(f32[328,128]{1,0:T(8,128)S(1)} %shard_map.86.rest_0_), channel_id=1, source_target_pairs={{0,12},{1,13},{2,14},{3,15},{4,8},{5,9},{6,10},{7,11},{8,4},{9,5},... | collective-permute-start | bytes 503816 | tf_op jit(solution)/shard_map/ppermute | solution.py:445
  4.4 1.2 collective-permute-start.1
  5.6 1.4 collective-permute-done.3.rest_4_
  7.0 1.2 collective-permute-start.5
  8.2 4.6 %collective-permute-start.8 = (f32[328,128]{1,0:T(8,128)S(1)}, f32[328,128]{1,0:T(8,128)S(1)}, u32[]{:S(2)}, u32[]{:S(2)}) collective-permute-start(f32[328,128]{1,0:T(8,128)S(1)} %collective-permute-done.7.rest_12_), channel_id=1, source_target_pairs={{0,4},{1,5},{2,6},{3,7},{4,0},{5,1},{6,2},{7,3},{8,12},{9,13},{10,... | collective-permute-start | bytes 503816 | tf_op jit(solution)/shard_map/ppermute | solution.py:445
  12.8 1.9 %collective-permute-start = (f32[328,128]{1,0:T(8,128)S(1)}, f32[328,128]{1,0:T(8,128)S(1)}, u32[]{:S(2)}, u32[]{:S(2)}) collective-permute-start(f32[328,128]{1,0:T(8,128)S(1)} %shard_map.86.rest_0_), channel_id=1, source_target_pairs={{0,1},{1,0},{2,3},{3,2},{4,5},{5,4},{6,7},{7,6},{8,9},{9,8},{10,11... | collective-permute-start | bytes 503816 | tf_op jit(solution)/shard_map/ppermute | solution.py:445
  15.2 1.2 collective-permute-start.13
  16.8 0.9 copy-done.1
  17.7 5.0 %shard_map.87 = (f32[8,88,128]{2,1,0:T(8,128)S(1)}, f32[328,128]{1,0:T(8,128)S(1)}) custom-call(bf16[40,2,15,32,128]{4,3,2,1,0:T(8,128)(2,1)} %model_hbm.11, s32[15,32,128]{2,1,0:T(8,128)S(1)} %copy-done.1, f32[328,128]{1,0:T(8,128)S(1)} %collective-permute-done.5.unused_in), custom_call_target="tpu_custom_call", output_to_operand_aliasing={{1}: (2, {})} | custom-call | bytes 73800000 | tf_op jit(solution)/shard_map/pallas_call | solution.py:480
  22.8 3.4 %collective-permute-start.12 = (f32[328,128]{1,0:T(8,128)S(1)}, f32[328,128]{1,0:T(8,128)S(1)}, u32[]{:S(2)}, u32[]{:S(2)}) collective-permute-start(f32[328,128]{1,0:T(8,128)S(1)} %collective-permute-done.7.rest_12_), channel_id=1, source_target_pairs={{0,1},{1,0},{2,3},{3,2},{4,5},{5,4},{6,7},{7,6},{8,9},{9,8},{10,11... | collective-permute-start | bytes 503816 | tf_op jit(solution)/shard_map/ppermute | solution.py:445
  28.3 10.9 %shard_map.89 = f32[16,120,128]{2,1,0:T(8,128)} custom-call(s32[30]{0:T(128)S(1)} %pad_add_fusion.ends_ref, bf16[40,2,15,32,128]{4,3,2,1,0:T(8,128)(2,1)} %model_hbm.11, f32[2,15,32,128]{3,2,1,0:T(8,128)S(1)} %copy-done, s32[15,32,128]{2,1,0:T(8,128)S(1)} %copy-done.2, f32[8,88,128]{2,1,0:T(8,128)S(1)} %get-tuple-element.17.power_ref, ...), custom_call_target="tpu_custom_call" | custom-call | bytes 33210000 | tf_op jit(solution)/shard_map/pallas_call | solution.py:480
  44.6 5.6 %all-to-all-start = ((f32[16,120,128]{2,1,0:T(8,128)}), f32[16,120,128]{2,1,0:T(8,128)S(1)}, u32[]{:S(2)}, u32[]{:S(2)}) async-start(f32[16,120,128]{2,1,0:T(8,128)} %shard_map.89), calls=%async_computation | async-start | bytes 1966080 | tf_op jit(solution)/shard_map/all_to_all | solution.py:440
  50.2 0.9 copy-done.4
  51.1 0.9 copy-done.6
  52.0 0.9 copy-done.8
  52.9 0.9 copy-done.10
  53.9 0.9 copy-done.12
  54.8 0.9 copy-done.14
  55.7 0.9 copy-done.16
  56.6 0.9 copy-done.18
  58.5 15.2 %all-to-all-done.sums = f32[16,120,128]{2,1,0:T(8,128)S(1)} async-done(((f32[16,120,128]{2,1,0:T(8,128)}), f32[16,120,128]{2,1,0:T(8,128)S(1)}, u32[]{:S(2)}, u32[]{:S(2)}) %all-to-all-start) | async-done | bytes 983072 | tf_op jit(solution)/shard_map/all_to_all | solution.py:440
  73.7 0.9 copy-done.20
  74.6 1.5 shard_map.90.g_ref.rest_0_.g_in
  76.2 1.0 collective-permute-start.21
  77.3 1.6 collective-permute-start.18
  78.8 1.1 collective-permute-start.17
  79.9 2.5 %collective-permute-done.15.rest_4_ = f32[328,128]{1,0:T(8,128)S(1)} collective-permute-done((f32[328,128]{1,0:T(8,128)S(1)}, f32[328,128]{1,0:T(8,128)S(1)}, u32[]{:S(2)}, u32[]{:S(2)}) %collective-permute-start.15) | collective-permute-done | bytes 167968 | tf_op jit(solution)/shard_map/ppermute | solution.py:445
  83.1 3.5 %collective-permute-start.24 = (f32[328,128]{1,0:T(8,128)S(1)}, f32[328,128]{1,0:T(8,128)S(1)}, u32[]{:S(2)}, u32[]{:S(2)}) collective-permute-start(f32[328,128]{1,0:T(8,128)S(1)} %collective-permute-done.21.rest_6_), channel_id=1, source_target_pairs={{0,4},{1,5},{2,6},{3,7},{4,0},{5,1},{6,2},{7,3},{8,12},{9,13},{10,... | collective-permute-start | bytes 503816 | tf_op jit(solution)/shard_map/ppermute | solution.py:445
  86.6 2.1 %collective-permute-start.20 = (f32[328,128]{1,0:T(8,128)S(1)}, f32[328,128]{1,0:T(8,128)S(1)}, u32[]{:S(2)}, u32[]{:S(2)}) collective-permute-start(f32[328,128]{1,0:T(8,128)S(1)} %collective-permute-done.15.rest_4_), channel_id=1, source_target_pairs={{0,1},{1,0},{2,3},{3,2},{4,5},{5,4},{6,7},{7,6},{8,9},{9,8},{10,11... | collective-permute-start | bytes 503816 | tf_op jit(solution)/shard_map/ppermute | solution.py:445
  89.5 1.2 collective-permute-start.26
  90.7 4.5 %shard_map.92 = (f32[2,15,32,128]{3,2,1,0:T(8,128)S(1)}, f32[4,88,128]{2,1,0:T(8,128)S(1)}, f32[4,88,128]{2,1,0:T(8,128)S(1)}, f32[328,128]{1,0:T(8,128)S(1)}) custom-call(s32[30]{0:T(128)S(1)} %pad_add_fusion.ends_ref, bf16[40,2,15,32,128]{4,3,2,1,0:T(8,128)(2,1)} %model_hbm.11, f32[2,15,32,128]{3,2,1,0:T(8,128)S(1)} %copy-done, ...), custom_call_target="tpu_custom_call", output_to_operand_aliasing={{3}: (3, {})} | custom-call | bytes 3690000 | tf_op jit(solution)/shard_map/pallas_call | solution.py:480
  95.2 2.8 %collective-permute-start.23 = (f32[328,128]{1,0:T(8,128)S(1)}, f32[328,128]{1,0:T(8,128)S(1)}, u32[]{:S(2)}, u32[]{:S(2)}) collective-permute-start(f32[328,128]{1,0:T(8,128)S(1)} %get-tuple-element.21.rest_0_), channel_id=1, source_target_pairs={{0,1},{1,0},{2,3},{3,2},{4,5},{5,4},{6,7},{7,6},{8,9},{9,8},{10,11... | collective-permute-start | bytes 503816 | tf_op jit(solution)/shard_map/ppermute | solution.py:445
  99.6 0.9 collective-permute-done.27.rest_5_
  100.5 9.1 %shard_map.93 = f32[16,80,128]{2,1,0:T(8,128)} custom-call(s32[30]{0:T(128)S(1)} %pad_add_fusion.ends_ref, bf16[40,2,15,32,128]{4,3,2,1,0:T(8,128)(2,1)} %model_hbm.11, s32[15,32,128]{2,1,0:T(8,128)S(1)} %copy-done.2, f32[8,88,128]{2,1,0:T(8,128)S(1)} %get-tuple-element.17.power_ref, f32[2,15,32,128]{3,2,1,0:T(8,128)S(1)} %get-tuple-element.18.acc_ref, ...), custom_call_target="tpu_custom_call" | custom-call | bytes 25830000 | tf_op jit(solution)/shard_map/pallas_call | solution.py:480
  109.6 5.1 %all-to-all-start.1 = ((f32[16,80,128]{2,1,0:T(8,128)}), f32[16,80,128]{2,1,0:T(8,128)S(1)}, u32[]{:S(2)}, u32[]{:S(2)}) async-start(f32[16,80,128]{2,1,0:T(8,128)} %shard_map.93), calls=%async_computation.1 | async-start | bytes 1310720 | tf_op jit(solution)/shard_map/all_to_all | solution.py:440
  114.7 1.0 shard_map.91.den_ref
  115.8 15.8 %all-to-all-done.1.sums = f32[16,80,128]{2,1,0:T(8,128)S(1)} async-done(((f32[16,80,128]{2,1,0:T(8,128)}), f32[16,80,128]{2,1,0:T(8,128)S(1)}, u32[]{:S(2)}, u32[]{:S(2)}) %all-to-all-start.1) | async-done | bytes 655392 | tf_op jit(solution)/shard_map/all_to_all | solution.py:440
  131.6 1.0 shard_map.94.rest_0_.rest_8_
  133.3 1.6 %collective-permute-start.33 = (f32[328,128]{1,0:T(8,128)S(1)}, f32[328,128]{1,0:T(8,128)S(1)}, u32[]{:S(2)}, u32[]{:S(2)}) collective-permute-start(f32[328,128]{1,0:T(8,128)S(1)} %shard_map.94.rest_0_.rest_8_), channel_id=1, source_target_pairs={{0,2},{1,3},{2,0},{3,1},{4,6},{5,7},{6,4},{7,5},{8,10},{9,11},{10,... | collective-permute-start | bytes 503816 | tf_op jit(solution)/shard_map/ppermute | solution.py:445
  134.9 1.1 collective-permute-start.32
  136.0 2.8 %collective-permute-done.30.rest_4_.rest_12_ = f32[328,128]{1,0:T(8,128)S(1)} collective-permute-done((f32[328,128]{1,0:T(8,128)S(1)}, f32[328,128]{1,0:T(8,128)S(1)}, u32[]{:S(2)}, u32[]{:S(2)}) %collective-permute-start.30) | collective-permute-done | bytes 167968 | tf_op jit(solution)/shard_map/ppermute | solution.py:445
  139.8 2.4 %collective-permute-start.39 = (f32[328,128]{1,0:T(8,128)S(1)}, f32[328,128]{1,0:T(8,128)S(1)}, u32[]{:S(2)}, u32[]{:S(2)}) collective-permute-start(f32[328,128]{1,0:T(8,128)S(1)} %collective-permute-done.36.rest_6_.rest_14_), channel_id=1, source_target_pairs={{0,4},{1,5},{2,6},{3,7},{4,0},{5,1},{6,2},{7,3},{8,12},{9,13},{10,... | collective-permute-start | bytes 503816 | tf_op jit(solution)/shard_map/ppermute | solution.py:445
  142.2 2.2 %collective-permute-start.35 = (f32[328,128]{1,0:T(8,128)S(1)}, f32[328,128]{1,0:T(8,128)S(1)}, u32[]{:S(2)}, u32[]{:S(2)}) collective-permute-start(f32[328,128]{1,0:T(8,128)S(1)} %collective-permute-done.30.rest_4_.rest_12_), channel_id=1, source_target_pairs={{0,1},{1,0},{2,3},{3,2},{4,5},{5,4},{6,7},{7,6},{8,9},{9,8},{10,11... | collective-permute-start | bytes 503816 | tf_op jit(solution)/shard_map/ppermute | solution.py:445
  145.6 1.0 collective-permute-start.41
  146.6 4.8 %shard_map.95 = (f32[2,15,32,128]{3,2,1,0:T(8,128)S(1)}, f32[4,88,128]{2,1,0:T(8,128)}, f32[4,88,128]{2,1,0:T(8,128)}, f32[328,128]{1,0:T(8,128)S(1)}) custom-call(s32[30]{0:T(128)S(1)} %pad_add_fusion.ends_ref, bf16[40,2,15,32,128]{4,3,2,1,0:T(8,128)(2,1)} %model_hbm.11, f32[2,15,32,128]{3,2,1,0:T(8,128)S(1)} %copy-done, ...), custom_call_target="tpu_custom_call", output_to_operand_aliasing={{3}: (3, {})} | custom-call | bytes 3690000 | tf_op jit(solution)/shard_map/pallas_call | solution.py:480
  151.4 3.0 %collective-permute-start.38 = (f32[328,128]{1,0:T(8,128)S(1)}, f32[328,128]{1,0:T(8,128)S(1)}, u32[]{:S(2)}, u32[]{:S(2)}) collective-permute-start(f32[328,128]{1,0:T(8,128)S(1)} %get-tuple-element.23.rest_0_), channel_id=1, source_target_pairs={{0,1},{1,0},{2,3},{3,2},{4,5},{5,4},{6,7},{7,6},{8,9},{9,8},{10,11... | collective-permute-start | bytes 503816 | tf_op jit(solution)/shard_map/ppermute | solution.py:445
  156.3 5.0 %shard_map.96 = (f32[2,15,32,128]{3,2,1,0:T(8,128)}, f32[2,160,128]{2,1,0:T(8,128)}) custom-call(s32[30]{0:T(128)S(1)} %pad_add_fusion.ends_ref, bf16[40,2,15,32,128]{4,3,2,1,0:T(8,128)(2,1)} %model_hbm.11, s32[15,32,128]{2,1,0:T(8,128)S(1)} %copy-done.2, f32[2,15,32,128]{3,2,1,0:T(8,128)S(1)} %get-tuple-element.22.acc_ref, ...), custom_call_target="tpu_custom_call" | custom-call | bytes 14760000 | tf_op jit(solution)/shard_map/pallas_call | solution.py:480
  (104 shorter events, 17.3 us)
Async XLA Ops:
  0.6 27.7 %copy-start = (f32[2,15,32,128]{3,2,1,0:T(8,128)S(1)}, f32[2,15,32,128]{3,2,1,0:T(8,128)}, u32[]{:S(2)}) copy-start(f32[2,15,32,128]{3,2,1,0:T(8,128)} %vis_ref.5) | copy-start | bytes 1474564
  1.8 5.2 %collective-permute-start.3 = (f32[328,128]{1,0:T(8,128)S(1)}, f32[328,128]{1,0:T(8,128)S(1)}, u32[]{:S(2)}, u32[]{:S(2)}) collective-permute-start(f32[328,128]{1,0:T(8,128)S(1)} %shard_map.86.rest_0_), channel_id=1, source_target_pairs={{0,4},{1,5},{2,6},{3,7},{4,0},{5,1},{6,2},{7,3},{8,12},{9,13},{10,... | collective-permute-start | bytes 503816 | tf_op jit(solution)/shard_map/ppermute | solution.py:445
  1.8 6.4 %collective-permute-start.7 = (f32[328,128]{1,0:T(8,128)S(1)}, f32[328,128]{1,0:T(8,128)S(1)}, u32[]{:S(2)}, u32[]{:S(2)}) collective-permute-start(f32[328,128]{1,0:T(8,128)S(1)} %shard_map.86.rest_0_), channel_id=1, source_target_pairs={{0,12},{1,13},{2,14},{3,15},{4,8},{5,9},{6,10},{7,11},{8,4},{9,5},... | collective-permute-start | bytes 503816 | tf_op jit(solution)/shard_map/ppermute | solution.py:445
  4.4 10.3 %collective-permute-start.1 = (f32[328,128]{1,0:T(8,128)S(1)}, f32[328,128]{1,0:T(8,128)S(1)}, u32[]{:S(2)}, u32[]{:S(2)}) collective-permute-start(f32[328,128]{1,0:T(8,128)S(1)} %shard_map.86.rest_0_), channel_id=1, source_target_pairs={{0,2},{1,3},{2,0},{3,1},{4,6},{5,7},{6,4},{7,5},{8,10},{9,11},{10,... | collective-permute-start | bytes 503816 | tf_op jit(solution)/shard_map/ppermute | solution.py:445
  7.0 8.2 %collective-permute-start.5 = (f32[328,128]{1,0:T(8,128)S(1)}, f32[328,128]{1,0:T(8,128)S(1)}, u32[]{:S(2)}, u32[]{:S(2)}) collective-permute-start(f32[328,128]{1,0:T(8,128)S(1)} %collective-permute-done.3.rest_4_), channel_id=1, source_target_pairs={{0,2},{1,3},{2,0},{3,1},{4,6},{5,7},{6,4},{7,5},{8,10},{9,11},{10,... | collective-permute-start | bytes 503816 | tf_op jit(solution)/shard_map/ppermute | solution.py:445
  8.2 8.2 %collective-permute-start.8 = (f32[328,128]{1,0:T(8,128)S(1)}, f32[328,128]{1,0:T(8,128)S(1)}, u32[]{:S(2)}, u32[]{:S(2)}) collective-permute-start(f32[328,128]{1,0:T(8,128)S(1)} %collective-permute-done.7.rest_12_), channel_id=1, source_target_pairs={{0,4},{1,5},{2,6},{3,7},{4,0},{5,1},{6,2},{7,3},{8,12},{9,13},{10,... | collective-permute-start | bytes 503816 | tf_op jit(solution)/shard_map/ppermute | solution.py:445
  12.8 9.9 %collective-permute-start = (f32[328,128]{1,0:T(8,128)S(1)}, f32[328,128]{1,0:T(8,128)S(1)}, u32[]{:S(2)}, u32[]{:S(2)}) collective-permute-start(f32[328,128]{1,0:T(8,128)S(1)} %shard_map.86.rest_0_), channel_id=1, source_target_pairs={{0,1},{1,0},{2,3},{3,2},{4,5},{5,4},{6,7},{7,6},{8,9},{9,8},{10,11... | collective-permute-start | bytes 503816 | tf_op jit(solution)/shard_map/ppermute | solution.py:445
  14.7 11.5 %collective-permute-start.2 = (f32[328,128]{1,0:T(8,128)S(1)}, f32[328,128]{1,0:T(8,128)S(1)}, u32[]{:S(2)}, u32[]{:S(2)}) collective-permute-start(f32[328,128]{1,0:T(8,128)S(1)} %collective-permute-done.1.rest_2_), channel_id=1, source_target_pairs={{0,1},{1,0},{2,3},{3,2},{4,5},{5,4},{6,7},{7,6},{8,9},{9,8},{10,11... | collective-permute-start | bytes 503816 | tf_op jit(solution)/shard_map/ppermute | solution.py:445
  14.7 11.5 %collective-permute-start.4 = (f32[328,128]{1,0:T(8,128)S(1)}, f32[328,128]{1,0:T(8,128)S(1)}, u32[]{:S(2)}, u32[]{:S(2)}) collective-permute-start(f32[328,128]{1,0:T(8,128)S(1)} %collective-permute-done.3.rest_4_), channel_id=1, source_target_pairs={{0,1},{1,0},{2,3},{3,2},{4,5},{5,4},{6,7},{7,6},{8,9},{9,8},{10,11... | collective-permute-start | bytes 503816 | tf_op jit(solution)/shard_map/ppermute | solution.py:445
  15.2 11.5 %collective-permute-start.13 = (f32[328,128]{1,0:T(8,128)S(1)}, f32[328,128]{1,0:T(8,128)S(1)}, u32[]{:S(2)}, u32[]{:S(2)}) collective-permute-start(f32[328,128]{1,0:T(8,128)S(1)} %collective-permute-done.7.rest_12_), channel_id=1, source_target_pairs={{0,2},{1,3},{2,0},{3,1},{4,6},{5,7},{6,4},{7,5},{8,10},{9,11},{10,... | collective-permute-start | bytes 503816 | tf_op jit(solution)/shard_map/ppermute | solution.py:445
  16.5 10.3 %collective-permute-start.10 = (f32[328,128]{1,0:T(8,128)S(1)}, f32[328,128]{1,0:T(8,128)S(1)}, u32[]{:S(2)}, u32[]{:S(2)}) collective-permute-start(f32[328,128]{1,0:T(8,128)S(1)} %collective-permute-done.8.rest_8_), channel_id=1, source_target_pairs={{0,2},{1,3},{2,0},{3,1},{4,6},{5,7},{6,4},{7,5},{8,10},{9,11},{10,... | collective-permute-start | bytes 503816 | tf_op jit(solution)/shard_map/ppermute | solution.py:445
  22.8 4.5 %collective-permute-start.12 = (f32[328,128]{1,0:T(8,128)S(1)}, f32[328,128]{1,0:T(8,128)S(1)}, u32[]{:S(2)}, u32[]{:S(2)}) collective-permute-start(f32[328,128]{1,0:T(8,128)S(1)} %collective-permute-done.7.rest_12_), channel_id=1, source_target_pairs={{0,1},{1,0},{2,3},{3,2},{4,5},{5,4},{6,7},{7,6},{8,9},{9,8},{10,11... | collective-permute-start | bytes 503816 | tf_op jit(solution)/shard_map/ppermute | solution.py:445
  26.2 1.4 collective-permute-start.6
  26.3 1.6 collective-permute-start.9
  26.7 1.4 collective-permute-start.14
  26.8 1.6 collective-permute-start.11
  44.6 29.1 %all-to-all-start = ((f32[16,120,128]{2,1,0:T(8,128)}), f32[16,120,128]{2,1,0:T(8,128)S(1)}, u32[]{:S(2)}, u32[]{:S(2)}) async-start(f32[16,120,128]{2,1,0:T(8,128)} %shard_map.89), calls=%async_computation | async-start | bytes 1966080 | tf_op jit(solution)/shard_map/all_to_all | solution.py:440
  76.2 6.2 %collective-permute-start.15 = (f32[328,128]{1,0:T(8,128)S(1)}, f32[328,128]{1,0:T(8,128)S(1)}, u32[]{:S(2)}, u32[]{:S(2)}) collective-permute-start(f32[328,128]{1,0:T(8,128)S(1)} %shard_map.90.g_ref.rest_0_.g_in), channel_id=1, source_target_pairs={{0,4},{1,5},{2,6},{3,7},{4,0},{5,1},{6,2},{7,3},{8,12},{9,13},{10,... | collective-permute-start | bytes 503816 | tf_op jit(solution)/shard_map/ppermute | solution.py:445
  76.2 6.8 %collective-permute-start.21 = (f32[328,128]{1,0:T(8,128)S(1)}, f32[328,128]{1,0:T(8,128)S(1)}, u32[]{:S(2)}, u32[]{:S(2)}) collective-permute-start(f32[328,128]{1,0:T(8,128)S(1)} %shard_map.90.g_ref.rest_0_.g_in), channel_id=1, source_target_pairs={{0,12},{1,13},{2,14},{3,15},{4,8},{5,9},{6,10},{7,11},{8,4},{9,5},... | collective-permute-start | bytes 503816 | tf_op jit(solution)/shard_map/ppermute | solution.py:445
  77.3 11.4 %collective-permute-start.18 = (f32[328,128]{1,0:T(8,128)S(1)}, f32[328,128]{1,0:T(8,128)S(1)}, u32[]{:S(2)}, u32[]{:S(2)}) collective-permute-start(f32[328,128]{1,0:T(8,128)S(1)} %shard_map.90.g_ref.rest_0_.g_in), channel_id=1, source_target_pairs={{0,2},{1,3},{2,0},{3,1},{4,6},{5,7},{6,4},{7,5},{8,10},{9,11},{10,... | collective-permute-start | bytes 503816 | tf_op jit(solution)/shard_map/ppermute | solution.py:445
  78.8 9.8 %collective-permute-start.17 = (f32[328,128]{1,0:T(8,128)S(1)}, f32[328,128]{1,0:T(8,128)S(1)}, u32[]{:S(2)}, u32[]{:S(2)}) collective-permute-start(f32[328,128]{1,0:T(8,128)S(1)} %shard_map.90.g_ref.rest_0_.g_in), channel_id=1, source_target_pairs={{0,1},{1,0},{2,3},{3,2},{4,5},{5,4},{6,7},{7,6},{8,9},{9,8},{10,11... | collective-permute-start | bytes 503816 | tf_op jit(solution)/shard_map/ppermute | solution.py:445
  82.3 6.8 %collective-permute-start.16 = (f32[328,128]{1,0:T(8,128)S(1)}, f32[328,128]{1,0:T(8,128)S(1)}, u32[]{:S(2)}, u32[]{:S(2)}) collective-permute-start(f32[328,128]{1,0:T(8,128)S(1)} %collective-permute-done.15.rest_4_), channel_id=1, source_target_pairs={{0,2},{1,3},{2,0},{3,1},{4,6},{5,7},{6,4},{7,5},{8,10},{9,11},{10,... | collective-permute-start | bytes 503816 | tf_op jit(solution)/shard_map/ppermute | solution.py:445
  83.1 6.4 %collective-permute-start.24 = (f32[328,128]{1,0:T(8,128)S(1)}, f32[328,128]{1,0:T(8,128)S(1)}, u32[]{:S(2)}, u32[]{:S(2)}) collective-permute-start(f32[328,128]{1,0:T(8,128)S(1)} %collective-permute-done.21.rest_6_), channel_id=1, source_target_pairs={{0,4},{1,5},{2,6},{3,7},{4,0},{5,1},{6,2},{7,3},{8,12},{9,13},{10,... | collective-permute-start | bytes 503816 | tf_op jit(solution)/shard_map/ppermute | solution.py:445
  86.6 4.1 %collective-permute-start.20 = (f32[328,128]{1,0:T(8,128)S(1)}, f32[328,128]{1,0:T(8,128)S(1)}, u32[]{:S(2)}, u32[]{:S(2)}) collective-permute-start(f32[328,128]{1,0:T(8,128)S(1)} %collective-permute-done.15.rest_4_), channel_id=1, source_target_pairs={{0,1},{1,0},{2,3},{3,2},{4,5},{5,4},{6,7},{7,6},{8,9},{9,8},{10,11... | collective-permute-start | bytes 503816 | tf_op jit(solution)/shard_map/ppermute | solution.py:445
  88.7 2.0 %collective-permute-start.19 = (f32[328,128]{1,0:T(8,128)S(1)}, f32[328,128]{1,0:T(8,128)S(1)}, u32[]{:S(2)}, u32[]{:S(2)}) collective-permute-start(f32[328,128]{1,0:T(8,128)S(1)} %collective-permute-done.18.rest_2_), channel_id=1, source_target_pairs={{0,1},{1,0},{2,3},{3,2},{4,5},{5,4},{6,7},{7,6},{8,9},{9,8},{10,11... | collective-permute-start | bytes 503816 | tf_op jit(solution)/shard_map/ppermute | solution.py:445
  88.7 2.0 %collective-permute-start.22 = (f32[328,128]{1,0:T(8,128)S(1)}, f32[328,128]{1,0:T(8,128)S(1)}, u32[]{:S(2)}, u32[]{:S(2)}) collective-permute-start(f32[328,128]{1,0:T(8,128)S(1)} %collective-permute-done.21.rest_6_), channel_id=1, source_target_pairs={{0,1},{1,0},{2,3},{3,2},{4,5},{5,4},{6,7},{7,6},{8,9},{9,8},{10,11... | collective-permute-start | bytes 503816 | tf_op jit(solution)/shard_map/ppermute | solution.py:445
  89.2 8.9 %collective-permute-start.28 = (f32[328,128]{1,0:T(8,128)S(1)}, f32[328,128]{1,0:T(8,128)S(1)}, u32[]{:S(2)}, u32[]{:S(2)}) collective-permute-start(f32[328,128]{1,0:T(8,128)S(1)} %collective-permute-done.21.rest_6_), channel_id=1, source_target_pairs={{0,2},{1,3},{2,0},{3,1},{4,6},{5,7},{6,4},{7,5},{8,10},{9,11},{10,... | collective-permute-start | bytes 503816 | tf_op jit(solution)/shard_map/ppermute | solution.py:445
  89.5 9.1 %collective-permute-start.26 = (f32[328,128]{1,0:T(8,128)S(1)}, f32[328,128]{1,0:T(8,128)S(1)}, u32[]{:S(2)}, u32[]{:S(2)}) collective-permute-start(f32[328,128]{1,0:T(8,128)S(1)} %collective-permute-done.24.rest_2_), channel_id=1, source_target_pairs={{0,2},{1,3},{2,0},{3,1},{4,6},{5,7},{6,4},{7,5},{8,10},{9,11},{10,... | collective-permute-start | bytes 503816 | tf_op jit(solution)/shard_map/ppermute | solution.py:445
  95.2 4.3 %collective-permute-start.23 = (f32[328,128]{1,0:T(8,128)S(1)}, f32[328,128]{1,0:T(8,128)S(1)}, u32[]{:S(2)}, u32[]{:S(2)}) collective-permute-start(f32[328,128]{1,0:T(8,128)S(1)} %get-tuple-element.21.rest_0_), channel_id=1, source_target_pairs={{0,1},{1,0},{2,3},{3,2},{4,5},{5,4},{6,7},{7,6},{8,9},{9,8},{10,11... | collective-permute-start | bytes 503816 | tf_op jit(solution)/shard_map/ppermute | solution.py:445
  98.0 1.5 collective-permute-start.25
  98.1 1.6 collective-permute-start.29
  98.6 1.9 %collective-permute-start.27 = (f32[328,128]{1,0:T(8,128)S(1)}, f32[328,128]{1,0:T(8,128)S(1)}, u32[]{:S(2)}, u32[]{:S(2)}) collective-permute-start(f32[328,128]{1,0:T(8,128)S(1)} %collective-permute-done.26.rest_4_), channel_id=1, source_target_pairs={{0,1},{1,0},{2,3},{3,2},{4,5},{5,4},{6,7},{7,6},{8,9},{9,8},{10,11... | collective-permute-start | bytes 503816 | tf_op jit(solution)/shard_map/ppermute | solution.py:445
  109.6 22.0 %all-to-all-start.1 = ((f32[16,80,128]{2,1,0:T(8,128)}), f32[16,80,128]{2,1,0:T(8,128)S(1)}, u32[]{:S(2)}, u32[]{:S(2)}) async-start(f32[16,80,128]{2,1,0:T(8,128)} %shard_map.93), calls=%async_computation.1 | async-start | bytes 1310720 | tf_op jit(solution)/shard_map/all_to_all | solution.py:440
  132.7 6.1 %collective-permute-start.30 = (f32[328,128]{1,0:T(8,128)S(1)}, f32[328,128]{1,0:T(8,128)S(1)}, u32[]{:S(2)}, u32[]{:S(2)}) collective-permute-start(f32[328,128]{1,0:T(8,128)S(1)} %shard_map.94.rest_0_.rest_8_), channel_id=1, source_target_pairs={{0,4},{1,5},{2,6},{3,7},{4,0},{5,1},{6,2},{7,3},{8,12},{9,13},{10,... | collective-permute-start | bytes 503816 | tf_op jit(solution)/shard_map/ppermute | solution.py:445
  132.7 7.1 %collective-permute-start.36 = (f32[328,128]{1,0:T(8,128)S(1)}, f32[328,128]{1,0:T(8,128)S(1)}, u32[]{:S(2)}, u32[]{:S(2)}) collective-permute-start(f32[328,128]{1,0:T(8,128)S(1)} %shard_map.94.rest_0_.rest_8_), channel_id=1, source_target_pairs={{0,12},{1,13},{2,14},{3,15},{4,8},{5,9},{6,10},{7,11},{8,4},{9,5},... | collective-permute-start | bytes 503816 | tf_op jit(solution)/shard_map/ppermute | solution.py:445
  133.3 11.2 %collective-permute-start.33 = (f32[328,128]{1,0:T(8,128)S(1)}, f32[328,128]{1,0:T(8,128)S(1)}, u32[]{:S(2)}, u32[]{:S(2)}) collective-permute-start(f32[328,128]{1,0:T(8,128)S(1)} %shard_map.94.rest_0_.rest_8_), channel_id=1, source_target_pairs={{0,2},{1,3},{2,0},{3,1},{4,6},{5,7},{6,4},{7,5},{8,10},{9,11},{10,... | collective-permute-start | bytes 503816 | tf_op jit(solution)/shard_map/ppermute | solution.py:445
  134.9 9.6 %collective-permute-start.32 = (f32[328,128]{1,0:T(8,128)S(1)}, f32[328,128]{1,0:T(8,128)S(1)}, u32[]{:S(2)}, u32[]{:S(2)}) collective-permute-start(f32[328,128]{1,0:T(8,128)S(1)} %shard_map.94.rest_0_.rest_8_), channel_id=1, source_target_pairs={{0,1},{1,0},{2,3},{3,2},{4,5},{5,4},{6,7},{7,6},{8,9},{9,8},{10,11... | collective-permute-start | bytes 503816 | tf_op jit(solution)/shard_map/ppermute | solution.py:445
  138.8 6.2 %collective-permute-start.31 = (f32[328,128]{1,0:T(8,128)S(1)}, f32[328,128]{1,0:T(8,128)S(1)}, u32[]{:S(2)}, u32[]{:S(2)}) collective-permute-start(f32[328,128]{1,0:T(8,128)S(1)} %collective-permute-done.30.rest_4_.rest_12_), channel_id=1, source_target_pairs={{0,2},{1,3},{2,0},{3,1},{4,6},{5,7},{6,4},{7,5},{8,10},{9,11},{10,... | collective-permute-start | bytes 503816 | tf_op jit(solution)/shard_map/ppermute | solution.py:445
  139.8 5.7 %collective-permute-start.39 = (f32[328,128]{1,0:T(8,128)S(1)}, f32[328,128]{1,0:T(8,128)S(1)}, u32[]{:S(2)}, u32[]{:S(2)}) collective-permute-start(f32[328,128]{1,0:T(8,128)S(1)} %collective-permute-done.36.rest_6_.rest_14_), channel_id=1, source_target_pairs={{0,4},{1,5},{2,6},{3,7},{4,0},{5,1},{6,2},{7,3},{8,12},{9,13},{10,... | collective-permute-start | bytes 503816 | tf_op jit(solution)/shard_map/ppermute | solution.py:445
  142.2 4.4 %collective-permute-start.35 = (f32[328,128]{1,0:T(8,128)S(1)}, f32[328,128]{1,0:T(8,128)S(1)}, u32[]{:S(2)}, u32[]{:S(2)}) collective-permute-start(f32[328,128]{1,0:T(8,128)S(1)} %collective-permute-done.30.rest_4_.rest_12_), channel_id=1, source_target_pairs={{0,1},{1,0},{2,3},{3,2},{4,5},{5,4},{6,7},{7,6},{8,9},{9,8},{10,11... | collective-permute-start | bytes 503816 | tf_op jit(solution)/shard_map/ppermute | solution.py:445
  144.5 2.1 %collective-permute-start.34 = (f32[328,128]{1,0:T(8,128)S(1)}, f32[328,128]{1,0:T(8,128)S(1)}, u32[]{:S(2)}, u32[]{:S(2)}) collective-permute-start(f32[328,128]{1,0:T(8,128)S(1)} %collective-permute-done.33.rest_2_.rest_10_), channel_id=1, source_target_pairs={{0,1},{1,0},{2,3},{3,2},{4,5},{5,4},{6,7},{7,6},{8,9},{9,8},{10,11... | collective-permute-start | bytes 503816 | tf_op jit(solution)/shard_map/ppermute | solution.py:445
  144.5 2.1 %collective-permute-start.37 = (f32[328,128]{1,0:T(8,128)S(1)}, f32[328,128]{1,0:T(8,128)S(1)}, u32[]{:S(2)}, u32[]{:S(2)}) collective-permute-start(f32[328,128]{1,0:T(8,128)S(1)} %collective-permute-done.36.rest_6_.rest_14_), channel_id=1, source_target_pairs={{0,1},{1,0},{2,3},{3,2},{4,5},{5,4},{6,7},{7,6},{8,9},{9,8},{10,11... | collective-permute-start | bytes 503816 | tf_op jit(solution)/shard_map/ppermute | solution.py:445
  145.0 9.5 %collective-permute-start.43 = (f32[328,128]{1,0:T(8,128)S(1)}, f32[328,128]{1,0:T(8,128)S(1)}, u32[]{:S(2)}, u32[]{:S(2)}) collective-permute-start(f32[328,128]{1,0:T(8,128)S(1)} %collective-permute-done.36.rest_6_.rest_14_), channel_id=1, source_target_pairs={{0,2},{1,3},{2,0},{3,1},{4,6},{5,7},{6,4},{7,5},{8,10},{9,11},{10,... | collective-permute-start | bytes 503816 | tf_op jit(solution)/shard_map/ppermute | solution.py:445
  145.6 9.3 %collective-permute-start.41 = (f32[328,128]{1,0:T(8,128)S(1)}, f32[328,128]{1,0:T(8,128)S(1)}, u32[]{:S(2)}, u32[]{:S(2)}) collective-permute-start(f32[328,128]{1,0:T(8,128)S(1)} %collective-permute-done.39.rest_2_), channel_id=1, source_target_pairs={{0,2},{1,3},{2,0},{3,1},{4,6},{5,7},{6,4},{7,5},{8,10},{9,11},{10,... | collective-permute-start | bytes 503816 | tf_op jit(solution)/shard_map/ppermute | solution.py:445
  151.4 4.0 %collective-permute-start.38 = (f32[328,128]{1,0:T(8,128)S(1)}, f32[328,128]{1,0:T(8,128)S(1)}, u32[]{:S(2)}, u32[]{:S(2)}) collective-permute-start(f32[328,128]{1,0:T(8,128)S(1)} %get-tuple-element.23.rest_0_), channel_id=1, source_target_pairs={{0,1},{1,0},{2,3},{3,2},{4,5},{5,4},{6,7},{7,6},{8,9},{9,8},{10,11... | collective-permute-start | bytes 503816 | tf_op jit(solution)/shard_map/ppermute | solution.py:445
  154.4 1.4 collective-permute-start.40
  154.5 1.6 collective-permute-start.44
  154.9 1.4 collective-permute-start.42
  (22 other events, 44.7 us)

commit v11 on v10

--- a/solution.py
+++ b/solution.py
@@ -44,6 +44,7 @@
 
 
 TILE = 8
+TRIP = 2
 
 
 def pack_kernel(n, dpc, first_hbm, second_hbm, re_hbm, im_hbm, out_ref, first_ref, second_ref, sems):
@@ -89,9 +90,11 @@
         def part(i, carry):
             for copy in self.part(i):
                 copy.wait()
-            for u in range(self.size):
+            def one(u, carry):
                 body(i * self.size + u)
-            return carry
+                return carry
+
+            return lax.fori_loop(0, self.size, one, carry)
 
         lax.fori_loop(0, self.pairs // self.size, part, 0)
 
@@ -121,9 +124,7 @@
     ref[STATIONS * dpc :, :] = jnp.zeros((TILE, 128), F32)
 
 
-def first_own_kernel(n, dpc, *rest):
-    ins, (g_ref, onehot_ref, split, lines) = rest[:n], rest[n:]
-    me = lax.axis_index("bl")
+def first_own(n, dpc, me, ins, g_ref, onehot_ref, split, lines):
     k, c = lax.div(me, 2), lax.rem(me, 2)
     per = STATIONS // n
     rows = per * SOURCE_COUNT
@@ -255,19 +256,22 @@
     clear(dpc, pairs, hre, him)
 
 
-def predict(dpc, b, acc, chips, model_ref, hre, him):
-    tiles = [slice(t, t + TILE) for t in range(0, acc[0].shape[0], TILE)]
-    acc_re, acc_im = ([x[t] for t in tiles] for x in acc)
-    for m, k in enumerate(chips):
-        for dd in range(dpc):
-            mr = model_ref[k * dpc + dd, 0, b].astype(F32)
-            mi = model_ref[k * dpc + dd, 1, b].astype(F32)
-            row = pl.ds(b * dpc + dd, TILE, stride=0)
+def predict(dpc, b, acc, first, chips, model_ref, hre, him):
+    def trip(i, acc):
+        tiles = [slice(t, t + TILE) for t in range(0, acc[0].shape[0], TILE)]
+        acc_re, acc_im = ([x[t] for t in tiles] for x in acc)
+        for u in range(TRIP * dpc):
+            d = first + i * TRIP * dpc + u
+            mr = model_ref[d, 0, b].astype(F32)
+            mi = model_ref[d, 1, b].astype(F32)
+            m, row = i * TRIP + u // dpc, pl.ds(b * dpc + u % dpc, TILE, stride=0)
             hr, hi = hre[m, row, :], him[m, row, :]
-            for i, t in enumerate(tiles):
-                acc_re[i] = acc_re[i] - (hr * mr[t] - hi * mi[t])
-                acc_im[i] = acc_im[i] - (hr * mi[t] + hi * mr[t])
-    return jnp.concatenate(acc_re, 0), jnp.concatenate(acc_im, 0)
+            for j, t in enumerate(tiles):
+                acc_re[j] = acc_re[j] - (hr * mr[t] - hi * mi[t])
+                acc_im[j] = acc_im[j] - (hr * mi[t] + hi * mr[t])
+        return jnp.concatenate(acc_re, 0), jnp.concatenate(acc_im, 0)
+
+    return lax.fori_loop(0, chips // TRIP, trip, acc)
 
 
 def weighted(b, acc, mask_ref):
@@ -302,15 +306,22 @@
 
 def correlate(dpc, b, res, chips, model_ref, cre, cim):
     res_re, res_im = res
-    for m, k in enumerate(chips):
-        re, im = [], []
-        for dd in range(dpc):
-            mr = model_ref[k * dpc + dd, 0, b].astype(F32)
-            mi = model_ref[k * dpc + dd, 1, b].astype(F32)
-            re.append(tile_sum(mr * res_re + mi * res_im))
-            im.append(tile_sum(mr * res_im - mi * res_re))
-        cre[m, pl.ds(b * dpc, TILE), :] = row_sums(re)
-        cim[m, pl.ds(b * dpc, TILE), :] = row_sums(im)
+
+    def trip(i, carry):
+        for v in range(TRIP):
+            re, im = [], []
+            for dd in range(dpc):
+                d = (i * TRIP + v) * dpc + dd
+                mr = model_ref[d, 0, b].astype(F32)
+                mi = model_ref[d, 1, b].astype(F32)
+                re.append(tile_sum(mr * res_re + mi * res_im))
+                im.append(tile_sum(mr * res_im - mi * res_re))
+            rows = pl.ds(b * dpc, TILE)
+            cre[i * TRIP + v, rows, :] = row_sums(re)
+            cim[i * TRIP + v, rows, :] = row_sums(im)
+        return carry
+
+    lax.fori_loop(0, chips // TRIP, trip, 0)
 
 
 def write_sums(dpc, chips, cre, cim, tiles, power_ref, out_ref, start):
@@ -334,19 +345,20 @@
 
 
 def first_pass_kernel(n, dpc, ends_ref, model_hbm, vis_ref, mask_ref, power_ref, *rest):
-    ins, (out_ref, model_ref, sems, hre, him, cre, cim, stack) = rest[:n], rest[n:]
+    ins, (out_ref, g_ref, onehot_ref, model_ref, sems, hre, him, cre, cim, stack, split, lines) = rest[:n], rest[n:]
     fetch = Fetch(model_hbm, model_ref, sems)
-    products_first(n, dpc, lax.axis_index("bl"), mask_ref.shape[0], ends_ref, ins, hre, him, stack)
-    chips = range(n // 2)
+    me = lax.axis_index("bl")
+    pairs, chips = mask_ref.shape[0], n // 2
+    products_first(n, dpc, me, pairs, ends_ref, ins, hre, him, stack)
+    first_own(n, dpc, me, ins, g_ref, onehot_ref, split, lines)
 
     def pair(b):
-        acc = predict(dpc, b, (vis_ref[0, b], vis_ref[1, b]), chips, model_ref, hre, him)
+        acc = predict(dpc, b, (vis_ref[0, b], vis_ref[1, b]), 0, chips, model_ref, hre, him)
         correlate(dpc, b, weighted(b, acc, mask_ref), chips, model_ref, cre, cim)
 
     fetch.each(pair)
-
-    clear(dpc, mask_ref.shape[0], cre, cim)
-    write_sums(dpc, chips, cre, cim, lambda m: (hre, him, m), power_ref, out_ref, True)
+    clear(dpc, pairs, cre, cim)
+    write_sums(dpc, range(chips), cre, cim, lambda m: (hre, him, m), power_ref, out_ref, True)
 
 
 NEAR, FAR = (0, 1, 2, 6), (3, 4, 5, 7)
@@ -364,7 +376,7 @@
 
     def pair(b):
         acc = vis_ref[0, b], vis_ref[1, b]
-        acc_ref[0, b], acc_ref[1, b] = predict(dpc, b, acc, range(len(NEAR)), model_ref, hre, him)
+        acc_ref[0, b], acc_ref[1, b] = predict(dpc, b, acc, 0, len(NEAR), model_ref, hre, him)
 
     fetch.each(pair)
 
@@ -382,15 +394,14 @@
     *rest,
 ):
     ins, (out_ref, model_ref, sems, hre, him, cre, cim) = rest[: 2 * len(FAR)], rest[2 * len(FAR) :]
-    fetch = Fetch(model_hbm, model_ref, sems)
     me = lax.axis_index("bl")
+    chips = chips_of(me, NEAR + FAR)
+    fetch = Fetch(model_hbm, model_ref, sems, [k * dpc for k in chips])
     products(dpc, me, model_hbm.shape[2], ends_ref, ins, hre, him)
-    far = chips_of(me, FAR)
-    chips = chips_of(me, NEAR) + far
 
     def pair(b):
-        acc = predict(dpc, b, (acc_ref[0, b], acc_ref[1, b]), far, model_ref, hre, him)
-        correlate(dpc, b, weighted(b, acc, mask_ref), chips, model_ref, cre, cim)
+        acc = predict(dpc, b, (acc_ref[0, b], acc_ref[1, b]), len(NEAR) * dpc, len(FAR), model_ref, hre, him)
+        correlate(dpc, b, weighted(b, acc, mask_ref), len(chips), model_ref, cre, cim)
 
     fetch.each(pair)
 
@@ -421,7 +432,7 @@
 
     def pair(b):
         acc = acc_ref[0, b], acc_ref[1, b]
-        acc = predict(dpc, b, acc, range(len(FAR)), model_ref, hre, him)
+        acc = predict(dpc, b, acc, 0, len(FAR), model_ref, hre, him)
         res_ref[0, b], res_ref[1, b] = weighted(b, acc, mask_ref)
 
     fetch.each(pair)
@@ -467,7 +478,7 @@
     half = (len(FAR), ROWS * dpc + TILE, channels)
     lots = n * 2 * ROWS
     mine = (STATIONS * dpc + TILE, channels)
-    sems = pltpu.SemaphoreType.DMA((pairs, n // 4))
+    sems = pltpu.SemaphoreType.DMA((pairs, n // 2))
     held = [pltpu.VMEM(model.shape, BF16), sems]
     held_half = [pltpu.VMEM((SOURCE_COUNT // 2,) + model.shape[1:], BF16), sems]
 
@@ -506,18 +517,15 @@
         return x
 
     got = gather(n, piece, powers_beside)
-    g, onehot = call(
-        first_own_kernel,
-        got,
-        [shape(*mine), shape(STATIONS, lots, dtype=BF16)],
-        [(STATIONS * TILE, channels), (n, channels)],
-        micros=2,
-    )
-    (sums,) = call(
+    sums, g, onehot = call(
         first_pass_kernel,
         (ends, model, vis, mask, power, *got),
-        [shape(n, (ROWS + TILE) * dpc, channels)],
-        held + [plane] * 4 + [(n,) + piece.shape],
+        [
+            shape(n, (ROWS + TILE) * dpc, channels),
+            shape(*mine),
+            shape(STATIONS, lots, dtype=BF16),
+        ],
+        held + [plane] * 4 + [(n,) + piece.shape, (STATIONS * TILE, channels), (n, channels)],
         micros=9,
     )
     powers = exchange(sums)

time: 164 us -> 167 us (1.018)
  blocking collectives: 0 us -> 27.2 us
  starting transfers between devices: 59.1 us -> 44.2 us
  local copies, waits for them, and re-layouts: 15.2 us -> 0.96 us
  Pallas kernels: 44.4 us -> 48.7 us
    all_to_all x0 -> x1, blocking collectives: none -> 27.2 us  [exchange(): return lax.all_to_all(x, 'bl', split_axis=0, concat_axis=0, tiled=True)]
    ppermute x45, waiting for transfers between devices: 10.7 us -> 27 us  [send(): return lax.ppermute(x, 'bl', [(i, i ^ o) for i in range(n)])]
    all_to_all x2 -> x1, waiting for transfers between devices: 31.1 us -> 15.8 us  [exchange(): return lax.all_to_all(x, 'bl', split_axis=0, concat_axis=0, tiled=True)]
    unnamed x46 -> x10, local copies, waits for them, and re-layouts: 15.2 us -> 0.96 us
    ppermute x45, starting transfers between devices: 48.4 us -> 38.5 us  [send(): return lax.ppermute(x, 'bl', [(i, i ^ o) for i in range(n)])]
    all_to_all x2 -> x1, starting transfers between devices: 10.7 us -> 5.69 us  [exchange(): return lax.all_to_all(x, 'bl', split_axis=0, concat_axis=0, tiled=True)]
    pallas_call x11 -> x10, Pallas kernels: 44.4 us -> 48.7 us  [call(): pl.pallas_call(functools.partial(kernel, n, dpc), in_specs=[place(x) for...]
  transfers between devices with their start and end apart: 47 -> 46, of which waited for: 17 -> 16; matrix products, arithmetic and copies ran while one was open for 0% -> 0% of each run, Pallas kernels for 10% -> 10%
where the time goes in v11:
time: 167 us; the launch traced here: 165 us
  Pallas kernels  48.7 us (29%)
  starting transfers between devices  44.2 us (26%)
  waiting for transfers between devices  42.8 us (26%)
  blocking collectives  27.2 us (16%)
    pallas_call x10, Pallas kernels, call(): pl.pallas_call(functools.partial(kernel, n, dpc), in_specs=[place(x) for...  48.7 us
    ppermute x45, starting transfers between devices, send(): return lax.ppermute(x, 'bl', [(i, i ^ o) for i in range(n)])  38.5 us
    all_to_all x1, blocking collectives, exchange(): return lax.all_to_all(x, 'bl', split_axis=0, concat_axis=0, tiled=True)  27.2 us
    ppermute x45, waiting for transfers between devices, send(): return lax.ppermute(x, 'bl', [(i, i ^ o) for i in range(n)])  27 us
    all_to_all x1, waiting for transfers between devices, exchange(): return lax.all_to_all(x, 'bl', split_axis=0, concat_axis=0, tiled=True)  15.8 us
    all_to_all x1, starting transfers between devices, exchange(): return lax.all_to_all(x, 'bl', split_axis=0, concat_axis=0, tiled=True)  5.69 us
  transfers between devices with their start and end apart: 46, of which 16 were waited for; matrix products, arithmetic and copies ran while one was open for 0% of the time, Pallas kernels for 10%

profile of v11, /device:TPU:9, one launch (start us, length us, event | category | flops | bytes accessed | tf_op | source)
XLA Modules:
  0.0 164.7 jit_solution(14022327530304787060)
XLA Ops:
  0.6 1.1 shard_map.86.rest_0_
  1.8 1.4 collective-permute-start.7
  3.1 2.2 %collective-permute-start = (f32[328,128]{1,0:T(8,128)S(1)}, f32[328,128]{1,0:T(8,128)S(1)}, u32[]{:S(2)}, u32[]{:S(2)}) collective-permute-start(f32[328,128]{1,0:T(8,128)S(1)} %shard_map.86.rest_0_), channel_id=1, source_target_pairs={{0,4},{1,5},{2,6},{3,7},{4,0},{5,1},{6,2},{7,3},{8,12},{9,13},{10,... | collective-permute-start | bytes 503816 | tf_op jit(solution)/shard_map/ppermute | solution.py:456
  5.3 1.2 collective-permute-start.3
  6.5 4.2 %collective-permute-done.7.rest_12_ = f32[328,128]{1,0:T(8,128)S(1)} collective-permute-done((f32[328,128]{1,0:T(8,128)S(1)}, f32[328,128]{1,0:T(8,128)S(1)}, u32[]{:S(2)}, u32[]{:S(2)}) %collective-permute-start.7) | collective-permute-done | bytes 167968 | tf_op jit(solution)/shard_map/ppermute | solution.py:456
  10.8 1.9 %collective-permute-done.rest_4_ = f32[328,128]{1,0:T(8,128)S(1)} collective-permute-done((f32[328,128]{1,0:T(8,128)S(1)}, f32[328,128]{1,0:T(8,128)S(1)}, u32[]{:S(2)}, u32[]{:S(2)}) %collective-permute-start) | collective-permute-done | bytes 167968 | tf_op jit(solution)/shard_map/ppermute | solution.py:456
  12.7 1.2 collective-permute-start.1
  13.9 2.0 %collective-permute-start.2 = (f32[328,128]{1,0:T(8,128)S(1)}, f32[328,128]{1,0:T(8,128)S(1)}, u32[]{:S(2)}, u32[]{:S(2)}) collective-permute-start(f32[328,128]{1,0:T(8,128)S(1)} %shard_map.86.rest_0_), channel_id=1, source_target_pairs={{0,1},{1,0},{2,3},{3,2},{4,5},{5,4},{6,7},{7,6},{8,9},{9,8},{10,11... | collective-permute-start | bytes 503816 | tf_op jit(solution)/shard_map/ppermute | solution.py:456
  16.5 1.3 collective-permute-start.4
  17.8 1.2 collective-permute-start.10
  19.0 0.9 copy-done.1
  20.0 5.6 %shard_map.87 = (f32[8,88,128]{2,1,0:T(8,128)S(1)}, f32[328,128]{1,0:T(8,128)S(1)}) custom-call(bf16[40,2,15,32,128]{4,3,2,1,0:T(8,128)(2,1)} %model_hbm.11, s32[15,32,128]{2,1,0:T(8,128)S(1)} %copy-done.1, f32[328,128]{1,0:T(8,128)S(1)} %collective-permute-done.1.unused_in), custom_call_target="tpu_custom_call", output_to_operand_aliasing={{1}: (2, {})} | custom-call | bytes 73800000 | tf_op jit(solution)/shard_map/pallas_call | solution.py:491
  25.6 4.1 %collective-permute-start.5 = (f32[328,128]{1,0:T(8,128)S(1)}, f32[328,128]{1,0:T(8,128)S(1)}, u32[]{:S(2)}, u32[]{:S(2)}) collective-permute-start(f32[328,128]{1,0:T(8,128)S(1)} %collective-permute-done.rest_4_), channel_id=1, source_target_pairs={{0,1},{1,0},{2,3},{3,2},{4,5},{5,4},{6,7},{7,6},{8,9},{9,8},{10,11... | collective-permute-start | bytes 503816 | tf_op jit(solution)/shard_map/ppermute | solution.py:456
  30.8 0.5 collective-permute-done.14.rest_15_
  31.8 11.6 %shard_map.88 = (f32[16,120,128]{2,1,0:T(8,128)S(1)}, f32[328,128]{1,0:T(8,128)S(1)}, bf16[64,512]{1,0:T(8,128)(2,1)S(1)}) custom-call(s32[30]{0:T(128)S(1)} %pad_add_fusion.ends_ref, bf16[40,2,15,32,128]{4,3,2,1,0:T(8,128)(2,1)} %model_hbm.11, f32[2,15,32,128]{3,2,1,0:T(8,128)S(1)} %copy-done, s32[15,32,128]{2,1,0:T(8,128)S(1)} %copy-done.2, ...), custom_call_target="tpu_custom_call" | custom-call | bytes 33210000 | tf_op jit(solution)/shard_map/pallas_call | solution.py:491
  43.4 27.2 %all_to_all.10.sums = f32[16,120,128]{2,1,0:T(8,128)S(1)} all-to-all(f32[16,120,128]{2,1,0:T(8,128)S(1)} %get-tuple-element.19), channel_id=1, replica_groups=mesh['grp'=2,'bl'=16] {'bl'}, dimensions={0} | all-to-all | bytes 1966080 | tf_op jit(solution)/shard_map/all_to_all | solution.py:451
  70.6 1.6 shard_map.89.g_ref.rest_0_.g_in
  72.4 0.5 collective-permute-start.18
  72.9 2.3 %collective-permute-start.15 = (f32[328,128]{1,0:T(8,128)S(1)}, f32[328,128]{1,0:T(8,128)S(1)}, u32[]{:S(2)}, u32[]{:S(2)}) collective-permute-start(f32[328,128]{1,0:T(8,128)S(1)} %shard_map.89.g_ref.rest_0_.g_in), channel_id=1, source_target_pairs={{0,4},{1,5},{2,6},{3,7},{4,0},{5,1},{6,2},{7,3},{8,12},{9,13},{10,... | collective-permute-start | bytes 503816 | tf_op jit(solution)/shard_map/ppermute | solution.py:456
  75.2 1.0 collective-permute-start.17
  76.3 5.6 %collective-permute-done.21.rest_6_ = f32[328,128]{1,0:T(8,128)S(1)} collective-permute-done((f32[328,128]{1,0:T(8,128)S(1)}, f32[328,128]{1,0:T(8,128)S(1)}, u32[]{:S(2)}, u32[]{:S(2)}) %collective-permute-start.21) | collective-permute-done | bytes 167968 | tf_op jit(solution)/shard_map/ppermute | solution.py:456
  81.9 0.7 collective-permute-start.22
  82.6 0.4 collective-permute-start.20
  83.1 1.1 collective-permute-start.16
  84.2 2.9 %collective-permute-done.24.rest_2_ = f32[328,128]{1,0:T(8,128)S(1)} collective-permute-done((f32[328,128]{1,0:T(8,128)S(1)}, f32[328,128]{1,0:T(8,128)S(1)}, u32[]{:S(2)}, u32[]{:S(2)}) %collective-permute-start.24) | collective-permute-done | bytes 167968 | tf_op jit(solution)/shard_map/ppermute | solution.py:456
  87.0 1.5 collective-permute-start.26
  88.9 4.9 %shard_map.91 = (f32[2,15,32,128]{3,2,1,0:T(8,128)S(1)}, f32[4,88,128]{2,1,0:T(8,128)S(1)}, f32[4,88,128]{2,1,0:T(8,128)S(1)}, f32[328,128]{1,0:T(8,128)S(1)}) custom-call(s32[30]{0:T(128)S(1)} %pad_add_fusion.ends_ref, bf16[40,2,15,32,128]{4,3,2,1,0:T(8,128)(2,1)} %model_hbm.11, f32[2,15,32,128]{3,2,1,0:T(8,128)S(1)} %copy-done, ...), custom_call_target="tpu_custom_call", output_to_operand_aliasing={{3}: (3, {})} | custom-call | bytes 3690000 | tf_op jit(solution)/shard_map/pallas_call | solution.py:491
  93.8 1.8 %collective-permute-start.23 = (f32[328,128]{1,0:T(8,128)S(1)}, f32[328,128]{1,0:T(8,128)S(1)}, u32[]{:S(2)}, u32[]{:S(2)}) collective-permute-start(f32[328,128]{1,0:T(8,128)S(1)} %get-tuple-element.23.rest_0_), channel_id=1, source_target_pairs={{0,1},{1,0},{2,3},{3,2},{4,5},{5,4},{6,7},{7,6},{8,9},{9,8},{10,11... | collective-permute-start | bytes 503816 | tf_op jit(solution)/shard_map/ppermute | solution.py:456
  96.1 1.3 collective-permute-start.27
  97.4 1.0 collective-permute-done.27.rest_5_
  98.4 10.6 %shard_map.92 = f32[16,80,128]{2,1,0:T(8,128)} custom-call(s32[30]{0:T(128)S(1)} %pad_add_fusion.ends_ref, bf16[40,2,15,32,128]{4,3,2,1,0:T(8,128)(2,1)} %model_hbm.11, s32[15,32,128]{2,1,0:T(8,128)S(1)} %copy-done.2, f32[8,88,128]{2,1,0:T(8,128)S(1)} %get-tuple-element.15.power_ref, f32[2,15,32,128]{3,2,1,0:T(8,128)S(1)} %get-tuple-element.20.acc_ref, ...), custom_call_target="tpu_custom_call" | custom-call | bytes 25830000 | tf_op jit(solution)/shard_map/pallas_call | solution.py:491
  109.0 5.7 %all-to-all-start.1 = ((f32[16,80,128]{2,1,0:T(8,128)}), f32[16,80,128]{2,1,0:T(8,128)S(1)}, u32[]{:S(2)}, u32[]{:S(2)}) async-start(f32[16,80,128]{2,1,0:T(8,128)} %shard_map.92), calls=%async_computation.1 | async-start | bytes 1310720 | tf_op jit(solution)/shard_map/all_to_all | solution.py:451
  114.7 1.1 shard_map.90.den_ref
  115.7 15.8 %all-to-all-done.1.sums = f32[16,80,128]{2,1,0:T(8,128)S(1)} async-done(((f32[16,80,128]{2,1,0:T(8,128)}), f32[16,80,128]{2,1,0:T(8,128)S(1)}, u32[]{:S(2)}, u32[]{:S(2)}) %all-to-all-start.1) | async-done | bytes 655392 | tf_op jit(solution)/shard_map/all_to_all | solution.py:451
  131.6 1.0 shard_map.93.rest_0_.rest_8_
  132.9 0.6 collective-permute-start.33
  133.5 2.3 %collective-permute-start.30 = (f32[328,128]{1,0:T(8,128)S(1)}, f32[328,128]{1,0:T(8,128)S(1)}, u32[]{:S(2)}, u32[]{:S(2)}) collective-permute-start(f32[328,128]{1,0:T(8,128)S(1)} %shard_map.93.rest_0_.rest_8_), channel_id=1, source_target_pairs={{0,4},{1,5},{2,6},{3,7},{4,0},{5,1},{6,2},{7,3},{8,12},{9,13},{10,... | collective-permute-start | bytes 503816 | tf_op jit(solution)/shard_map/ppermute | solution.py:456
  135.8 1.1 collective-permute-start.32
  136.8 5.6 %collective-permute-done.36.rest_6_.rest_14_ = f32[328,128]{1,0:T(8,128)S(1)} collective-permute-done((f32[328,128]{1,0:T(8,128)S(1)}, f32[328,128]{1,0:T(8,128)S(1)}, u32[]{:S(2)}, u32[]{:S(2)}) %collective-permute-start.36) | collective-permute-done | bytes 167968 | tf_op jit(solution)/shard_map/ppermute | solution.py:456
  142.4 0.6 collective-permute-start.37
  143.5 1.1 collective-permute-start.31
  144.6 3.0 %collective-permute-done.39.rest_2_ = f32[328,128]{1,0:T(8,128)S(1)} collective-permute-done((f32[328,128]{1,0:T(8,128)S(1)}, f32[328,128]{1,0:T(8,128)S(1)}, u32[]{:S(2)}, u32[]{:S(2)}) %collective-permute-start.39) | collective-permute-done | bytes 167968 | tf_op jit(solution)/shard_map/ppermute | solution.py:456
  147.7 1.5 collective-permute-start.41
  149.3 5.6 %shard_map.94 = (f32[2,15,32,128]{3,2,1,0:T(8,128)S(1)}, f32[4,88,128]{2,1,0:T(8,128)}, f32[4,88,128]{2,1,0:T(8,128)}, f32[328,128]{1,0:T(8,128)S(1)}) custom-call(s32[30]{0:T(128)S(1)} %pad_add_fusion.ends_ref, bf16[40,2,15,32,128]{4,3,2,1,0:T(8,128)(2,1)} %model_hbm.11, f32[2,15,32,128]{3,2,1,0:T(8,128)S(1)} %copy-done, ...), custom_call_target="tpu_custom_call", output_to_operand_aliasing={{3}: (3, {})} | custom-call | bytes 3690000 | tf_op jit(solution)/shard_map/pallas_call | solution.py:491
  154.9 1.9 %collective-permute-start.38 = (f32[328,128]{1,0:T(8,128)S(1)}, f32[328,128]{1,0:T(8,128)S(1)}, u32[]{:S(2)}, u32[]{:S(2)}) collective-permute-start(f32[328,128]{1,0:T(8,128)S(1)} %get-tuple-element.25.rest_0_), channel_id=1, source_target_pairs={{0,1},{1,0},{2,3},{3,2},{4,5},{5,4},{6,7},{7,6},{8,9},{9,8},{10,11... | collective-permute-start | bytes 503816 | tf_op jit(solution)/shard_map/ppermute | solution.py:456
  157.3 0.6 collective-permute-start.42
  158.5 0.5 collective-permute-done.42.rest_5_
  159.0 5.7 %shard_map.95 = (f32[2,15,32,128]{3,2,1,0:T(8,128)}, f32[2,160,128]{2,1,0:T(8,128)}) custom-call(s32[30]{0:T(128)S(1)} %pad_add_fusion.ends_ref, bf16[40,2,15,32,128]{4,3,2,1,0:T(8,128)(2,1)} %model_hbm.11, s32[15,32,128]{2,1,0:T(8,128)S(1)} %copy-done.2, f32[2,15,32,128]{3,2,1,0:T(8,128)S(1)} %get-tuple-element.24.acc_ref, ...), custom_call_target="tpu_custom_call" | custom-call | bytes 14760000 | tf_op jit(solution)/shard_map/pallas_call | solution.py:491
  (66 shorter events, 5.4 us)
Async XLA Ops:
  0.6 31.2 %copy-start = (f32[2,15,32,128]{3,2,1,0:T(8,128)S(1)}, f32[2,15,32,128]{3,2,1,0:T(8,128)}, u32[]{:S(2)}) copy-start(f32[2,15,32,128]{3,2,1,0:T(8,128)} %vis_ref.5) | copy-start | bytes 1474564
  1.8 9.0 %collective-permute-start.7 = (f32[328,128]{1,0:T(8,128)S(1)}, f32[328,128]{1,0:T(8,128)S(1)}, u32[]{:S(2)}, u32[]{:S(2)}) collective-permute-start(f32[328,128]{1,0:T(8,128)S(1)} %shard_map.86.rest_0_), channel_id=1, source_target_pairs={{0,12},{1,13},{2,14},{3,15},{4,8},{5,9},{6,10},{7,11},{8,4},{9,5},... | collective-permute-start | bytes 503816 | tf_op jit(solution)/shard_map/ppermute | solution.py:456
  3.1 9.6 %collective-permute-start = (f32[328,128]{1,0:T(8,128)S(1)}, f32[328,128]{1,0:T(8,128)S(1)}, u32[]{:S(2)}, u32[]{:S(2)}) collective-permute-start(f32[328,128]{1,0:T(8,128)S(1)} %shard_map.86.rest_0_), channel_id=1, source_target_pairs={{0,4},{1,5},{2,6},{3,7},{4,0},{5,1},{6,2},{7,3},{8,12},{9,13},{10,... | collective-permute-start | bytes 503816 | tf_op jit(solution)/shard_map/ppermute | solution.py:456
  5.3 10.9 %collective-permute-start.3 = (f32[328,128]{1,0:T(8,128)S(1)}, f32[328,128]{1,0:T(8,128)S(1)}, u32[]{:S(2)}, u32[]{:S(2)}) collective-permute-start(f32[328,128]{1,0:T(8,128)S(1)} %shard_map.86.rest_0_), channel_id=1, source_target_pairs={{0,2},{1,3},{2,0},{3,1},{4,6},{5,7},{6,4},{7,5},{8,10},{9,11},{10,... | collective-permute-start | bytes 503816 | tf_op jit(solution)/shard_map/ppermute | solution.py:456
  10.8 5.7 %collective-permute-start.8 = (f32[328,128]{1,0:T(8,128)S(1)}, f32[328,128]{1,0:T(8,128)S(1)}, u32[]{:S(2)}, u32[]{:S(2)}) collective-permute-start(f32[328,128]{1,0:T(8,128)S(1)} %collective-permute-done.7.rest_12_), channel_id=1, source_target_pairs={{0,4},{1,5},{2,6},{3,7},{4,0},{5,1},{6,2},{7,3},{8,12},{9,13},{10,... | collective-permute-start | bytes 503816 | tf_op jit(solution)/shard_map/ppermute | solution.py:456
  12.7 5.1 %collective-permute-start.1 = (f32[328,128]{1,0:T(8,128)S(1)}, f32[328,128]{1,0:T(8,128)S(1)}, u32[]{:S(2)}, u32[]{:S(2)}) collective-permute-start(f32[328,128]{1,0:T(8,128)S(1)} %collective-permute-done.rest_4_), channel_id=1, source_target_pairs={{0,2},{1,3},{2,0},{3,1},{4,6},{5,7},{6,4},{7,5},{8,10},{9,11},{10,... | collective-permute-start | bytes 503816 | tf_op jit(solution)/shard_map/ppermute | solution.py:456
  13.9 11.6 %collective-permute-start.2 = (f32[328,128]{1,0:T(8,128)S(1)}, f32[328,128]{1,0:T(8,128)S(1)}, u32[]{:S(2)}, u32[]{:S(2)}) collective-permute-start(f32[328,128]{1,0:T(8,128)S(1)} %shard_map.86.rest_0_), channel_id=1, source_target_pairs={{0,1},{1,0},{2,3},{3,2},{4,5},{5,4},{6,7},{7,6},{8,9},{9,8},{10,11... | collective-permute-start | bytes 503816 | tf_op jit(solution)/shard_map/ppermute | solution.py:456
  16.0 13.7 %collective-permute-start.13 = (f32[328,128]{1,0:T(8,128)S(1)}, f32[328,128]{1,0:T(8,128)S(1)}, u32[]{:S(2)}, u32[]{:S(2)}) collective-permute-start(f32[328,128]{1,0:T(8,128)S(1)} %collective-permute-done.7.rest_12_), channel_id=1, source_target_pairs={{0,2},{1,3},{2,0},{3,1},{4,6},{5,7},{6,4},{7,5},{8,10},{9,11},{10,... | collective-permute-start | bytes 503816 | tf_op jit(solution)/shard_map/ppermute | solution.py:456
  16.2 13.5 %collective-permute-start.12 = (f32[328,128]{1,0:T(8,128)S(1)}, f32[328,128]{1,0:T(8,128)S(1)}, u32[]{:S(2)}, u32[]{:S(2)}) collective-permute-start(f32[328,128]{1,0:T(8,128)S(1)} %collective-permute-done.7.rest_12_), channel_id=1, source_target_pairs={{0,1},{1,0},{2,3},{3,2},{4,5},{5,4},{6,7},{7,6},{8,9},{9,8},{10,11... | collective-permute-start | bytes 503816 | tf_op jit(solution)/shard_map/ppermute | solution.py:456
  16.5 13.7 %collective-permute-start.4 = (f32[328,128]{1,0:T(8,128)S(1)}, f32[328,128]{1,0:T(8,128)S(1)}, u32[]{:S(2)}, u32[]{:S(2)}) collective-permute-start(f32[328,128]{1,0:T(8,128)S(1)} %collective-permute-done.3.rest_2_), channel_id=1, source_target_pairs={{0,1},{1,0},{2,3},{3,2},{4,5},{5,4},{6,7},{7,6},{8,9},{9,8},{10,11... | collective-permute-start | bytes 503816 | tf_op jit(solution)/shard_map/ppermute | solution.py:456
  17.8 12.4 %collective-permute-start.10 = (f32[328,128]{1,0:T(8,128)S(1)}, f32[328,128]{1,0:T(8,128)S(1)}, u32[]{:S(2)}, u32[]{:S(2)}) collective-permute-start(f32[328,128]{1,0:T(8,128)S(1)} %collective-permute-done.8.rest_8_), channel_id=1, source_target_pairs={{0,2},{1,3},{2,0},{3,1},{4,6},{5,7},{6,4},{7,5},{8,10},{9,11},{10,... | collective-permute-start | bytes 503816 | tf_op jit(solution)/shard_map/ppermute | solution.py:456
  20.0 11.8 %copy-start.2 = (s32[15,32,128]{2,1,0:T(8,128)S(1)}, s32[15,32,128]{2,1,0:T(8,128)}, u32[]{:S(2)}) copy-start(s32[15,32,128]{2,1,0:T(8,128)} %mask_ref.7) | copy-start | bytes 737284
  25.6 5.2 %collective-permute-start.5 = (f32[328,128]{1,0:T(8,128)S(1)}, f32[328,128]{1,0:T(8,128)S(1)}, u32[]{:S(2)}, u32[]{:S(2)}) collective-permute-start(f32[328,128]{1,0:T(8,128)S(1)} %collective-permute-done.rest_4_), channel_id=1, source_target_pairs={{0,1},{1,0},{2,3},{3,2},{4,5},{5,4},{6,7},{7,6},{8,9},{9,8},{10,11... | collective-permute-start | bytes 503816 | tf_op jit(solution)/shard_map/ppermute | solution.py:456
  29.7 1.9 %collective-permute-start.6 = (f32[328,128]{1,0:T(8,128)S(1)}, f32[328,128]{1,0:T(8,128)S(1)}, u32[]{:S(2)}, u32[]{:S(2)}) collective-permute-start(f32[328,128]{1,0:T(8,128)S(1)} %get-tuple-element.16.rest_6_), channel_id=1, source_target_pairs={{0,1},{1,0},{2,3},{3,2},{4,5},{5,4},{6,7},{7,6},{8,9},{9,8},{10,11... | collective-permute-start | bytes 503816 | tf_op jit(solution)/shard_map/ppermute | solution.py:456
  29.7 1.6 collective-permute-start.14
  30.2 1.4 collective-permute-start.9
  30.3 1.6 collective-permute-start.11
  72.2 9.7 %collective-permute-start.21 = (f32[328,128]{1,0:T(8,128)S(1)}, f32[328,128]{1,0:T(8,128)S(1)}, u32[]{:S(2)}, u32[]{:S(2)}) collective-permute-start(f32[328,128]{1,0:T(8,128)S(1)} %shard_map.89.g_ref.rest_0_.g_in), channel_id=1, source_target_pairs={{0,12},{1,13},{2,14},{3,15},{4,8},{5,9},{6,10},{7,11},{8,4},{9,5},... | collective-permute-start | bytes 503816 | tf_op jit(solution)/shard_map/ppermute | solution.py:456
  72.4 10.1 %collective-permute-start.18 = (f32[328,128]{1,0:T(8,128)S(1)}, f32[328,128]{1,0:T(8,128)S(1)}, u32[]{:S(2)}, u32[]{:S(2)}) collective-permute-start(f32[328,128]{1,0:T(8,128)S(1)} %shard_map.89.g_ref.rest_0_.g_in), channel_id=1, source_target_pairs={{0,2},{1,3},{2,0},{3,1},{4,6},{5,7},{6,4},{7,5},{8,10},{9,11},{10,... | collective-permute-start | bytes 503816 | tf_op jit(solution)/shard_map/ppermute | solution.py:456
  72.9 9.7 %collective-permute-start.15 = (f32[328,128]{1,0:T(8,128)S(1)}, f32[328,128]{1,0:T(8,128)S(1)}, u32[]{:S(2)}, u32[]{:S(2)}) collective-permute-start(f32[328,128]{1,0:T(8,128)S(1)} %shard_map.89.g_ref.rest_0_.g_in), channel_id=1, source_target_pairs={{0,4},{1,5},{2,6},{3,7},{4,0},{5,1},{6,2},{7,3},{8,12},{9,13},{10,... | collective-permute-start | bytes 503816 | tf_op jit(solution)/shard_map/ppermute | solution.py:456
  75.2 7.8 %collective-permute-start.17 = (f32[328,128]{1,0:T(8,128)S(1)}, f32[328,128]{1,0:T(8,128)S(1)}, u32[]{:S(2)}, u32[]{:S(2)}) collective-permute-start(f32[328,128]{1,0:T(8,128)S(1)} %shard_map.89.g_ref.rest_0_.g_in), channel_id=1, source_target_pairs={{0,1},{1,0},{2,3},{3,2},{4,5},{5,4},{6,7},{7,6},{8,9},{9,8},{10,11... | collective-permute-start | bytes 503816 | tf_op jit(solution)/shard_map/ppermute | solution.py:456
  81.9 5.2 %collective-permute-start.24 = (f32[328,128]{1,0:T(8,128)S(1)}, f32[328,128]{1,0:T(8,128)S(1)}, u32[]{:S(2)}, u32[]{:S(2)}) collective-permute-start(f32[328,128]{1,0:T(8,128)S(1)} %collective-permute-done.21.rest_6_), channel_id=1, source_target_pairs={{0,4},{1,5},{2,6},{3,7},{4,0},{5,1},{6,2},{7,3},{8,12},{9,13},{10,... | collective-permute-start | bytes 503816 | tf_op jit(solution)/shard_map/ppermute | solution.py:456
  81.9 5.2 %collective-permute-start.22 = (f32[328,128]{1,0:T(8,128)S(1)}, f32[328,128]{1,0:T(8,128)S(1)}, u32[]{:S(2)}, u32[]{:S(2)}) collective-permute-start(f32[328,128]{1,0:T(8,128)S(1)} %collective-permute-done.21.rest_6_), channel_id=1, source_target_pairs={{0,1},{1,0},{2,3},{3,2},{4,5},{5,4},{6,7},{7,6},{8,9},{9,8},{10,11... | collective-permute-start | bytes 503816 | tf_op jit(solution)/shard_map/ppermute | solution.py:456
  82.6 6.0 %collective-permute-start.19 = (f32[328,128]{1,0:T(8,128)S(1)}, f32[328,128]{1,0:T(8,128)S(1)}, u32[]{:S(2)}, u32[]{:S(2)}) collective-permute-start(f32[328,128]{1,0:T(8,128)S(1)} %collective-permute-done.18.rest_2_), channel_id=1, source_target_pairs={{0,1},{1,0},{2,3},{3,2},{4,5},{5,4},{6,7},{7,6},{8,9},{9,8},{10,11... | collective-permute-start | bytes 503816 | tf_op jit(solution)/shard_map/ppermute | solution.py:456
  82.6 5.9 %collective-permute-start.20 = (f32[328,128]{1,0:T(8,128)S(1)}, f32[328,128]{1,0:T(8,128)S(1)}, u32[]{:S(2)}, u32[]{:S(2)}) collective-permute-start(f32[328,128]{1,0:T(8,128)S(1)} %collective-permute-done.15.rest_4_), channel_id=1, source_target_pairs={{0,1},{1,0},{2,3},{3,2},{4,5},{5,4},{6,7},{7,6},{8,9},{9,8},{10,11... | collective-permute-start | bytes 503816 | tf_op jit(solution)/shard_map/ppermute | solution.py:456
  83.1 5.8 %collective-permute-start.16 = (f32[328,128]{1,0:T(8,128)S(1)}, f32[328,128]{1,0:T(8,128)S(1)}, u32[]{:S(2)}, u32[]{:S(2)}) collective-permute-start(f32[328,128]{1,0:T(8,128)S(1)} %collective-permute-done.15.rest_4_), channel_id=1, source_target_pairs={{0,2},{1,3},{2,0},{3,1},{4,6},{5,7},{6,4},{7,5},{8,10},{9,11},{10,... | collective-permute-start | bytes 503816 | tf_op jit(solution)/shard_map/ppermute | solution.py:456
  87.0 8.5 %collective-permute-start.28 = (f32[328,128]{1,0:T(8,128)S(1)}, f32[328,128]{1,0:T(8,128)S(1)}, u32[]{:S(2)}, u32[]{:S(2)}) collective-permute-start(f32[328,128]{1,0:T(8,128)S(1)} %collective-permute-done.21.rest_6_), channel_id=1, source_target_pairs={{0,2},{1,3},{2,0},{3,1},{4,6},{5,7},{6,4},{7,5},{8,10},{9,11},{10,... | collective-permute-start | bytes 503816 | tf_op jit(solution)/shard_map/ppermute | solution.py:456
  87.0 9.0 %collective-permute-start.26 = (f32[328,128]{1,0:T(8,128)S(1)}, f32[328,128]{1,0:T(8,128)S(1)}, u32[]{:S(2)}, u32[]{:S(2)}) collective-permute-start(f32[328,128]{1,0:T(8,128)S(1)} %collective-permute-done.24.rest_2_), channel_id=1, source_target_pairs={{0,2},{1,3},{2,0},{3,1},{4,6},{5,7},{6,4},{7,5},{8,10},{9,11},{10,... | collective-permute-start | bytes 503816 | tf_op jit(solution)/shard_map/ppermute | solution.py:456
  93.8 3.6 %collective-permute-start.23 = (f32[328,128]{1,0:T(8,128)S(1)}, f32[328,128]{1,0:T(8,128)S(1)}, u32[]{:S(2)}, u32[]{:S(2)}) collective-permute-start(f32[328,128]{1,0:T(8,128)S(1)} %get-tuple-element.23.rest_0_), channel_id=1, source_target_pairs={{0,1},{1,0},{2,3},{3,2},{4,5},{5,4},{6,7},{7,6},{8,9},{9,8},{10,11... | collective-permute-start | bytes 503816 | tf_op jit(solution)/shard_map/ppermute | solution.py:456
  95.6 1.8 %collective-permute-start.29 = (f32[328,128]{1,0:T(8,128)S(1)}, f32[328,128]{1,0:T(8,128)S(1)}, u32[]{:S(2)}, u32[]{:S(2)}) collective-permute-start(f32[328,128]{1,0:T(8,128)S(1)} %collective-permute-done.28.rest_6_), channel_id=1, source_target_pairs={{0,1},{1,0},{2,3},{3,2},{4,5},{5,4},{6,7},{7,6},{8,9},{9,8},{10,11... | collective-permute-start | bytes 503816 | tf_op jit(solution)/shard_map/ppermute | solution.py:456
  95.7 1.7 %collective-permute-start.25 = (f32[328,128]{1,0:T(8,128)S(1)}, f32[328,128]{1,0:T(8,128)S(1)}, u32[]{:S(2)}, u32[]{:S(2)}) collective-permute-start(f32[328,128]{1,0:T(8,128)S(1)} %collective-permute-done.24.rest_2_), channel_id=1, source_target_pairs={{0,1},{1,0},{2,3},{3,2},{4,5},{5,4},{6,7},{7,6},{8,9},{9,8},{10,11... | collective-permute-start | bytes 503816 | tf_op jit(solution)/shard_map/ppermute | solution.py:456
  96.1 2.3 %collective-permute-start.27 = (f32[328,128]{1,0:T(8,128)S(1)}, f32[328,128]{1,0:T(8,128)S(1)}, u32[]{:S(2)}, u32[]{:S(2)}) collective-permute-start(f32[328,128]{1,0:T(8,128)S(1)} %collective-permute-done.26.rest_4_), channel_id=1, source_target_pairs={{0,1},{1,0},{2,3},{3,2},{4,5},{5,4},{6,7},{7,6},{8,9},{9,8},{10,11... | collective-permute-start | bytes 503816 | tf_op jit(solution)/shard_map/ppermute | solution.py:456
  109.0 22.6 %all-to-all-start.1 = ((f32[16,80,128]{2,1,0:T(8,128)}), f32[16,80,128]{2,1,0:T(8,128)S(1)}, u32[]{:S(2)}, u32[]{:S(2)}) async-start(f32[16,80,128]{2,1,0:T(8,128)} %shard_map.92), calls=%async_computation.1 | async-start | bytes 1310720 | tf_op jit(solution)/shard_map/all_to_all | solution.py:451
  132.6 9.8 %collective-permute-start.36 = (f32[328,128]{1,0:T(8,128)S(1)}, f32[328,128]{1,0:T(8,128)S(1)}, u32[]{:S(2)}, u32[]{:S(2)}) collective-permute-start(f32[328,128]{1,0:T(8,128)S(1)} %shard_map.93.rest_0_.rest_8_), channel_id=1, source_target_pairs={{0,12},{1,13},{2,14},{3,15},{4,8},{5,9},{6,10},{7,11},{8,4},{9,5},... | collective-permute-start | bytes 503816 | tf_op jit(solution)/shard_map/ppermute | solution.py:456
  132.9 10.1 %collective-permute-start.33 = (f32[328,128]{1,0:T(8,128)S(1)}, f32[328,128]{1,0:T(8,128)S(1)}, u32[]{:S(2)}, u32[]{:S(2)}) collective-permute-start(f32[328,128]{1,0:T(8,128)S(1)} %shard_map.93.rest_0_.rest_8_), channel_id=1, source_target_pairs={{0,2},{1,3},{2,0},{3,1},{4,6},{5,7},{6,4},{7,5},{8,10},{9,11},{10,... | collective-permute-start | bytes 503816 | tf_op jit(solution)/shard_map/ppermute | solution.py:456
  133.5 9.6 %collective-permute-start.30 = (f32[328,128]{1,0:T(8,128)S(1)}, f32[328,128]{1,0:T(8,128)S(1)}, u32[]{:S(2)}, u32[]{:S(2)}) collective-permute-start(f32[328,128]{1,0:T(8,128)S(1)} %shard_map.93.rest_0_.rest_8_), channel_id=1, source_target_pairs={{0,4},{1,5},{2,6},{3,7},{4,0},{5,1},{6,2},{7,3},{8,12},{9,13},{10,... | collective-permute-start | bytes 503816 | tf_op jit(solution)/shard_map/ppermute | solution.py:456
  135.8 7.8 %collective-permute-start.32 = (f32[328,128]{1,0:T(8,128)S(1)}, f32[328,128]{1,0:T(8,128)S(1)}, u32[]{:S(2)}, u32[]{:S(2)}) collective-permute-start(f32[328,128]{1,0:T(8,128)S(1)} %shard_map.93.rest_0_.rest_8_), channel_id=1, source_target_pairs={{0,1},{1,0},{2,3},{3,2},{4,5},{5,4},{6,7},{7,6},{8,9},{9,8},{10,11... | collective-permute-start | bytes 503816 | tf_op jit(solution)/shard_map/ppermute | solution.py:456
  142.4 5.3 %collective-permute-start.39 = (f32[328,128]{1,0:T(8,128)S(1)}, f32[328,128]{1,0:T(8,128)S(1)}, u32[]{:S(2)}, u32[]{:S(2)}) collective-permute-start(f32[328,128]{1,0:T(8,128)S(1)} %collective-permute-done.36.rest_6_.rest_14_), channel_id=1, source_target_pairs={{0,4},{1,5},{2,6},{3,7},{4,0},{5,1},{6,2},{7,3},{8,12},{9,13},{10,... | collective-permute-start | bytes 503816 | tf_op jit(solution)/shard_map/ppermute | solution.py:456
  142.4 5.3 %collective-permute-start.37 = (f32[328,128]{1,0:T(8,128)S(1)}, f32[328,128]{1,0:T(8,128)S(1)}, u32[]{:S(2)}, u32[]{:S(2)}) collective-permute-start(f32[328,128]{1,0:T(8,128)S(1)} %collective-permute-done.36.rest_6_.rest_14_), channel_id=1, source_target_pairs={{0,1},{1,0},{2,3},{3,2},{4,5},{5,4},{6,7},{7,6},{8,9},{9,8},{10,11... | collective-permute-start | bytes 503816 | tf_op jit(solution)/shard_map/ppermute | solution.py:456
  143.0 6.2 %collective-permute-start.34 = (f32[328,128]{1,0:T(8,128)S(1)}, f32[328,128]{1,0:T(8,128)S(1)}, u32[]{:S(2)}, u32[]{:S(2)}) collective-permute-start(f32[328,128]{1,0:T(8,128)S(1)} %collective-permute-done.33.rest_2_.rest_10_), channel_id=1, source_target_pairs={{0,1},{1,0},{2,3},{3,2},{4,5},{5,4},{6,7},{7,6},{8,9},{9,8},{10,11... | collective-permute-start | bytes 503816 | tf_op jit(solution)/shard_map/ppermute | solution.py:456
  143.1 6.1 %collective-permute-start.35 = (f32[328,128]{1,0:T(8,128)S(1)}, f32[328,128]{1,0:T(8,128)S(1)}, u32[]{:S(2)}, u32[]{:S(2)}) collective-permute-start(f32[328,128]{1,0:T(8,128)S(1)} %collective-permute-done.30.rest_4_.rest_12_), channel_id=1, source_target_pairs={{0,1},{1,0},{2,3},{3,2},{4,5},{5,4},{6,7},{7,6},{8,9},{9,8},{10,11... | collective-permute-start | bytes 503816 | tf_op jit(solution)/shard_map/ppermute | solution.py:456
  143.5 5.8 %collective-permute-start.31 = (f32[328,128]{1,0:T(8,128)S(1)}, f32[328,128]{1,0:T(8,128)S(1)}, u32[]{:S(2)}, u32[]{:S(2)}) collective-permute-start(f32[328,128]{1,0:T(8,128)S(1)} %collective-permute-done.30.rest_4_.rest_12_), channel_id=1, source_target_pairs={{0,2},{1,3},{2,0},{3,1},{4,6},{5,7},{6,4},{7,5},{8,10},{9,11},{10,... | collective-permute-start | bytes 503816 | tf_op jit(solution)/shard_map/ppermute | solution.py:456
  147.7 9.1 %collective-permute-start.43 = (f32[328,128]{1,0:T(8,128)S(1)}, f32[328,128]{1,0:T(8,128)S(1)}, u32[]{:S(2)}, u32[]{:S(2)}) collective-permute-start(f32[328,128]{1,0:T(8,128)S(1)} %collective-permute-done.36.rest_6_.rest_14_), channel_id=1, source_target_pairs={{0,2},{1,3},{2,0},{3,1},{4,6},{5,7},{6,4},{7,5},{8,10},{9,11},{10,... | collective-permute-start | bytes 503816 | tf_op jit(solution)/shard_map/ppermute | solution.py:456
  147.7 9.6 %collective-permute-start.41 = (f32[328,128]{1,0:T(8,128)S(1)}, f32[328,128]{1,0:T(8,128)S(1)}, u32[]{:S(2)}, u32[]{:S(2)}) collective-permute-start(f32[328,128]{1,0:T(8,128)S(1)} %collective-permute-done.39.rest_2_), channel_id=1, source_target_pairs={{0,2},{1,3},{2,0},{3,1},{4,6},{5,7},{6,4},{7,5},{8,10},{9,11},{10,... | collective-permute-start | bytes 503816 | tf_op jit(solution)/shard_map/ppermute | solution.py:456
  154.9 3.5 %collective-permute-start.38 = (f32[328,128]{1,0:T(8,128)S(1)}, f32[328,128]{1,0:T(8,128)S(1)}, u32[]{:S(2)}, u32[]{:S(2)}) collective-permute-start(f32[328,128]{1,0:T(8,128)S(1)} %get-tuple-element.25.rest_0_), channel_id=1, source_target_pairs={{0,1},{1,0},{2,3},{3,2},{4,5},{5,4},{6,7},{7,6},{8,9},{9,8},{10,11... | collective-permute-start | bytes 503816 | tf_op jit(solution)/shard_map/ppermute | solution.py:456
  156.8 1.4 collective-permute-start.44
  156.9 1.6 collective-permute-start.40
  157.3 1.7 %collective-permute-start.42 = (f32[328,128]{1,0:T(8,128)S(1)}, f32[328,128]{1,0:T(8,128)S(1)}, u32[]{:S(2)}, u32[]{:S(2)}) collective-permute-start(f32[328,128]{1,0:T(8,128)S(1)} %collective-permute-done.41.rest_4_), channel_id=1, source_target_pairs={{0,1},{1,0},{2,3},{3,2},{4,5},{5,4},{6,7},{7,6},{8,9},{9,8},{10,11... | collective-permute-start | bytes 503816 | tf_op jit(solution)/shard_map/ppermute | solution.py:456
  (3 other events, 22.4 us)

commit v12 on v11

--- a/solution.py
+++ b/solution.py
@@ -44,7 +44,6 @@
 
 
 TILE = 8
-TRIP = 2
 
 
 def pack_kernel(n, dpc, first_hbm, second_hbm, re_hbm, im_hbm, out_ref, first_ref, second_ref, sems):
@@ -86,7 +85,7 @@
             for j, first in enumerate(self.firsts)
         ]
 
-    def each(self, body):
+    def each(self, body, after=lambda i: None):
         def part(i, carry):
             for copy in self.part(i):
                 copy.wait()
@@ -94,13 +93,17 @@
                 body(i * self.size + u)
                 return carry
 
-            return lax.fori_loop(0, self.size, one, carry)
+            carry = lax.fori_loop(0, self.size, one, carry)
+            after(i)
+            return carry
 
         lax.fori_loop(0, self.pairs // self.size, part, 0)
 
 
-def power_kernel(n, dpc, model_hbm, mask_ref, unused_in, out_ref, unused_out, model_ref, sems):
+def power_kernel(n, dpc, ends_in, model_hbm, mask_ref, unused_in, ends_ref, out_ref, unused_out, model_ref, sems):
     fetch = Fetch(model_hbm, model_ref, sems)
+    for i in range(ends_in.shape[0]):
+        ends_ref[i] = ends_in[i]
     out_ref[...] = jnp.zeros_like(out_ref)
 
     def pair(b):
@@ -257,21 +260,19 @@
 
 
 def predict(dpc, b, acc, first, chips, model_ref, hre, him):
-    def trip(i, acc):
-        tiles = [slice(t, t + TILE) for t in range(0, acc[0].shape[0], TILE)]
-        acc_re, acc_im = ([x[t] for t in tiles] for x in acc)
-        for u in range(TRIP * dpc):
-            d = first + i * TRIP * dpc + u
+    tiles = [slice(t, t + TILE) for t in range(0, acc[0].shape[0], TILE)]
+    acc_re, acc_im = ([x[t] for t in tiles] for x in acc)
+    for m in range(chips):
+        for dd in range(dpc):
+            d = first + m * dpc + dd
             mr = model_ref[d, 0, b].astype(F32)
             mi = model_ref[d, 1, b].astype(F32)
-            m, row = i * TRIP + u // dpc, pl.ds(b * dpc + u % dpc, TILE, stride=0)
+            row = pl.ds(b * dpc + dd, TILE, stride=0)
             hr, hi = hre[m, row, :], him[m, row, :]
             for j, t in enumerate(tiles):
                 acc_re[j] = acc_re[j] - (hr * mr[t] - hi * mi[t])
                 acc_im[j] = acc_im[j] - (hr * mi[t] + hi * mr[t])
-        return jnp.concatenate(acc_re, 0), jnp.concatenate(acc_im, 0)
-
-    return lax.fori_loop(0, chips // TRIP, trip, acc)
+    return jnp.concatenate(acc_re, 0), jnp.concatenate(acc_im, 0)
 
 
 def weighted(b, acc, mask_ref):
@@ -306,33 +307,27 @@
 
 def correlate(dpc, b, res, chips, model_ref, cre, cim):
     res_re, res_im = res
-
-    def trip(i, carry):
-        for v in range(TRIP):
-            re, im = [], []
-            for dd in range(dpc):
-                d = (i * TRIP + v) * dpc + dd
-                mr = model_ref[d, 0, b].astype(F32)
-                mi = model_ref[d, 1, b].astype(F32)
-                re.append(tile_sum(mr * res_re + mi * res_im))
-                im.append(tile_sum(mr * res_im - mi * res_re))
-            rows = pl.ds(b * dpc, TILE)
-            cre[i * TRIP + v, rows, :] = row_sums(re)
-            cim[i * TRIP + v, rows, :] = row_sums(im)
-        return carry
-
-    lax.fori_loop(0, chips // TRIP, trip, 0)
-
-
-def write_sums(dpc, chips, cre, cim, tiles, power_ref, out_ref, start):
+    for m in range(chips):
+        re, im = [], []
+        for dd in range(dpc):
+            mr = model_ref[m * dpc + dd, 0, b].astype(F32)
+            mi = model_ref[m * dpc + dd, 1, b].astype(F32)
+            re.append(tile_sum(mr * res_re + mi * res_im))
+            im.append(tile_sum(mr * res_im - mi * res_re))
+        cre[m, pl.ds(b * dpc, TILE), :] = row_sums(re)
+        cim[m, pl.ds(b * dpc, TILE), :] = row_sums(im)
+
+
+def write_sums(dpc, chips, cre, cim, tiles, power_ref, out_ref, out_hbm, sems, start):
+    copies = []
     for m, k in enumerate(chips):
         re, im, at = tiles(m)
         for t in range(ROWS * dpc // TILE):
             rows = slice(t * TILE, (t + 1) * TILE)
             w = power_ref[k, rows, :]
             x0, x1 = cross(cre[m, rows, :] + re[at, rows, :] * w, cim[m, rows, :] + im[at, rows, :] * w)
-            out_ref[2 * k, rows, :] = x0
-            out_ref[2 * k + 1, rows, :] = x1
+            out_ref[2 * m, rows, :] = x0
+            out_ref[2 * m + 1, rows, :] = x1
         if start:
             for t in range(dpc):
                 x0, x1 = cross(
@@ -340,12 +335,19 @@
                     power_ref[k, (t + dpc) * TILE : (t + dpc + 1) * TILE, :],
                 )
                 rows = slice(ROWS * dpc + t * TILE, ROWS * dpc + (t + 1) * TILE)
-                out_ref[2 * k, rows, :] = x0
-                out_ref[2 * k + 1, rows, :] = x1
+                out_ref[2 * m, rows, :] = x0
+                out_ref[2 * m + 1, rows, :] = x1
+        copies.append(
+            pltpu.make_async_copy(out_ref.at[pl.ds(2 * m, 2)], out_hbm.at[pl.ds(2 * k, 2)], sems.at[m])
+        )
+        copies[-1].start()
+    for copy in copies:
+        copy.wait()
 
 
 def first_pass_kernel(n, dpc, ends_ref, model_hbm, vis_ref, mask_ref, power_ref, *rest):
-    ins, (out_ref, g_ref, onehot_ref, model_ref, sems, hre, him, cre, cim, stack, split, lines) = rest[:n], rest[n:]
+    ins, rest = rest[:n], rest[n:]
+    out_hbm, g_ref, onehot_ref, out_ref, out_sems, model_ref, sems, hre, him, cre, cim, stack, split, lines = rest
     fetch = Fetch(model_hbm, model_ref, sems)
     me = lax.axis_index("bl")
     pairs, chips = mask_ref.shape[0], n // 2
@@ -358,7 +360,7 @@
 
     fetch.each(pair)
     clear(dpc, pairs, cre, cim)
-    write_sums(dpc, range(chips), cre, cim, lambda m: (hre, him, m), power_ref, out_ref, True)
+    write_sums(dpc, range(chips), cre, cim, lambda m: (hre, him, m), power_ref, out_ref, out_hbm, out_sems, True)
 
 
 NEAR, FAR = (0, 1, 2, 6), (3, 4, 5, 7)
@@ -393,7 +395,8 @@
     near_im,
     *rest,
 ):
-    ins, (out_ref, model_ref, sems, hre, him, cre, cim) = rest[: 2 * len(FAR)], rest[2 * len(FAR) :]
+    ins, rest = rest[: 2 * len(FAR)], rest[2 * len(FAR) :]
+    out_hbm, out_ref, out_sems, model_ref, sems, hre, him, cre, cim = rest
     me = lax.axis_index("bl")
     chips = chips_of(me, NEAR + FAR)
     fetch = Fetch(model_hbm, model_ref, sems, [k * dpc for k in chips])
@@ -412,11 +415,11 @@
             m -= len(pairs)
 
     clear(dpc, mask_ref.shape[0], cre, cim)
-    write_sums(dpc, chips, cre, cim, tiles, power_ref, out_ref, False)
+    write_sums(dpc, chips, cre, cim, tiles, power_ref, out_ref, out_hbm, out_sems, False)
 
 
 def last_kernel(n, dpc, ends_ref, model_hbm, mask_ref, acc_ref, *rest):
-    ins, (res_ref, gains_ref, model_ref, sems, hre, him) = rest[:n], rest[n:]
+    ins, (res_hbm, gains_ref, res_ref, res_sems, model_ref, sems, hre, him) = rest[:n], rest[n:]
     me = lax.axis_index("bl")
     fetch = Fetch(model_hbm, model_ref, sems, [k * dpc for k in chips_of(me, FAR)])
     products(dpc, me, model_hbm.shape[2], ends_ref, ins[: 2 * len(FAR)], hre, him)
@@ -435,12 +438,19 @@
         acc = predict(dpc, b, acc, 0, len(FAR), model_ref, hre, him)
         res_ref[0, b], res_ref[1, b] = weighted(b, acc, mask_ref)
 
-    fetch.each(pair)
+    def leave(i):
+        part = pl.ds(i * fetch.size, fetch.size)
+        return pltpu.make_async_copy(res_ref.at[:, part], res_hbm.at[:, part], res_sems.at[i])
+
+    fetch.each(pair, lambda i: leave(i).start())
+    for i in range(mask_ref.shape[0] // fetch.size):
+        leave(i).wait()
 
 
 SMEM = pl.BlockSpec(memory_space=pltpu.SMEM)
 VMEM = pl.BlockSpec(memory_space=pltpu.VMEM)
 HBM = pl.BlockSpec(memory_space=pltpu.HBM)
+ANY = pl.BlockSpec(memory_space=pl.ANY)
 
 
 def shape(*dims, dtype=F32):
@@ -479,10 +489,11 @@
     lots = n * 2 * ROWS
     mine = (STATIONS * dpc + TILE, channels)
     sems = pltpu.SemaphoreType.DMA((pairs, n // 2))
+    few = pltpu.SemaphoreType.DMA((n // 2,))
     held = [pltpu.VMEM(model.shape, BF16), sems]
     held_half = [pltpu.VMEM((SOURCE_COUNT // 2,) + model.shape[1:], BF16), sems]
 
-    def call(kernel, args, outs, scratch=(), micros=1, aliases={}):
+    def call(kernel, args, outs, scratch=(), micros=1, aliases={}, away=()):
         def place(x):
             if x is model or any(x is y for y in starts):
                 return HBM
@@ -491,7 +502,7 @@
         return pl.pallas_call(
             functools.partial(kernel, n, dpc),
             in_specs=[place(x) for x in args],
-            out_specs=[VMEM for o in outs],
+            out_specs=[ANY if i in away else SMEM if o.dtype == jnp.int32 else VMEM for i, o in enumerate(outs)],
             out_shape=outs,
             scratch_shapes=[pltpu.VMEM(x, F32) if isinstance(x, tuple) else x for x in scratch],
             compiler_params=params,
@@ -510,10 +521,9 @@
     power = None
 
     def powers_beside(x, got):
-        nonlocal power
-        power, x = call(
-            power_kernel, (model, mask, x), [shape(*plane), shape(*x.shape)], held, micros=20, aliases={2: 1}
-        )
+        nonlocal power, ends
+        outs = [pltpu.SMEM(ends.shape, jnp.int32), shape(*plane), shape(*x.shape)]
+        ends, power, x = call(power_kernel, (ends, model, mask, x), outs, held, micros=20, aliases={3: 2})
         return x
 
     got = gather(n, piece, powers_beside)
@@ -525,8 +535,12 @@
             shape(*mine),
             shape(STATIONS, lots, dtype=BF16),
         ],
-        held + [plane] * 4 + [(n,) + piece.shape, (STATIONS * TILE, channels), (n, channels)],
+        [(n, (ROWS + TILE) * dpc, channels), few]
+        + held
+        + [plane] * 4
+        + [(n,) + piece.shape, (STATIONS * TILE, channels), (n, channels)],
         micros=9,
+        away=(0,),
     )
     powers = exchange(sums)
     (g,) = call(
@@ -565,8 +579,9 @@
             later_pass_kernel,
             (ends, model, mask, power, *near, *got[: 2 * len(FAR)]),
             [shape(n, ROWS * dpc, channels)],
-            held + [half] * 2 + [plane] * 2,
+            [(n, ROWS * dpc, channels), few] + held + [half] * 2 + [plane] * 2,
             micros=7,
+            away=(0,),
         )
         sums = exchange(sums)
         (g,) = call(
@@ -580,8 +595,9 @@
         last_kernel,
         (ends, model, mask, near[0], *got),
         [shape(*vis.shape), shape(2, *gre.shape)],
-        held_half + [half] * 2,
+        [vis.shape, pltpu.SemaphoreType.DMA((pairs,))] + held_half + [half] * 2,
         micros=4,
+        away=(0,),
     )
     return gains, residual
 

time: 167 us -> 168 us (level)
  transfers between devices with their start and end apart: 46 -> 46, of which waited for: 16 -> 15; matrix products, arithmetic and copies ran while one was open for 0% -> 0% of each run, Pallas kernels for 10% -> 10%
where the time goes in v12:
time: 168 us; the launch traced here: 165 us
  Pallas kernels  47.6 us (28%)
  starting transfers between devices  45 us (27%)
  waiting for transfers between devices  42.9 us (26%)
  blocking collectives  27.2 us (16%)
    pallas_call x10, Pallas kernels, call(): pl.pallas_call(functools.partial(kernel, n, dpc), in_specs=[place(x) for...  47.6 us
    ppermute x45, starting transfers between devices, send(): return lax.ppermute(x, 'bl', [(i, i ^ o) for i in range(n)])  39.3 us
    all_to_all x1, blocking collectives, exchange(): return lax.all_to_all(x, 'bl', split_axis=0, concat_axis=0, tiled=True)  27.2 us
    ppermute x45, waiting for transfers between devices, send(): return lax.ppermute(x, 'bl', [(i, i ^ o) for i in range(n)])  27.1 us
    all_to_all x1, waiting for transfers between devices, exchange(): return lax.all_to_all(x, 'bl', split_axis=0, concat_axis=0, tiled=True)  15.8 us
    all_to_all x1, starting transfers between devices, exchange(): return lax.all_to_all(x, 'bl', split_axis=0, concat_axis=0, tiled=True)  5.7 us
  transfers between devices with their start and end apart: 46, of which 15 were waited for; matrix products, arithmetic and copies ran while one was open for 0% of the time, Pallas kernels for 10%

profile of v12, /device:TPU:9, one launch (start us, length us, event | category | flops | bytes accessed | tf_op | source)
XLA Modules:
  0.0 165.3 jit_solution(4056405077206629562)
XLA Ops:
  0.6 1.1 shard_map.86.rest_0_
  1.8 1.4 collective-permute-start.7
  3.1 2.2 %collective-permute-start = (f32[328,128]{1,0:T(8,128)S(1)}, f32[328,128]{1,0:T(8,128)S(1)}, u32[]{:S(2)}, u32[]{:S(2)}) collective-permute-start(f32[328,128]{1,0:T(8,128)S(1)} %shard_map.86.rest_0_), channel_id=1, source_target_pairs={{0,4},{1,5},{2,6},{3,7},{4,0},{5,1},{6,2},{7,3},{8,12},{9,13},{10,... | collective-permute-start | bytes 503816 | tf_op jit(solution)/shard_map/ppermute | solution.py:466
  5.3 1.2 collective-permute-start.3
  6.5 4.2 %collective-permute-done.7.rest_12_ = f32[328,128]{1,0:T(8,128)S(1)} collective-permute-done((f32[328,128]{1,0:T(8,128)S(1)}, f32[328,128]{1,0:T(8,128)S(1)}, u32[]{:S(2)}, u32[]{:S(2)}) %collective-permute-start.7) | collective-permute-done | bytes 167968 | tf_op jit(solution)/shard_map/ppermute | solution.py:466
  10.8 1.9 %collective-permute-done.rest_4_ = f32[328,128]{1,0:T(8,128)S(1)} collective-permute-done((f32[328,128]{1,0:T(8,128)S(1)}, f32[328,128]{1,0:T(8,128)S(1)}, u32[]{:S(2)}, u32[]{:S(2)}) %collective-permute-start) | collective-permute-done | bytes 167968 | tf_op jit(solution)/shard_map/ppermute | solution.py:466
  12.7 1.2 collective-permute-start.1
  13.9 2.0 %collective-permute-start.2 = (f32[328,128]{1,0:T(8,128)S(1)}, f32[328,128]{1,0:T(8,128)S(1)}, u32[]{:S(2)}, u32[]{:S(2)}) collective-permute-start(f32[328,128]{1,0:T(8,128)S(1)} %shard_map.86.rest_0_), channel_id=1, source_target_pairs={{0,1},{1,0},{2,3},{3,2},{4,5},{5,4},{6,7},{7,6},{8,9},{9,8},{10,11... | collective-permute-start | bytes 503816 | tf_op jit(solution)/shard_map/ppermute | solution.py:466
  16.5 1.3 collective-permute-start.4
  17.8 1.2 collective-permute-start.10
  19.0 0.7 pad_add_fusion.ends_in
  19.8 0.9 copy-done.1
  20.7 6.1 %shard_map.87 = (s32[30]{0:T(128)S(4)}, f32[8,88,128]{2,1,0:T(8,128)S(1)}, f32[328,128]{1,0:T(8,128)S(1)}) custom-call(s32[30]{0:T(128)S(1)} %pad_add_fusion.ends_in, bf16[40,2,15,32,128]{4,3,2,1,0:T(8,128)(2,1)} %model_hbm.11, s32[15,32,128]{2,1,0:T(8,128)S(1)} %copy-done.1, ...), custom_call_target="tpu_custom_call", output_to_operand_aliasing={{2}: (3, {})} | custom-call | bytes 73800000 | tf_op jit(solution)/shard_map/pallas_call | solution.py:502
  26.8 4.1 %collective-permute-start.5 = (f32[328,128]{1,0:T(8,128)S(1)}, f32[328,128]{1,0:T(8,128)S(1)}, u32[]{:S(2)}, u32[]{:S(2)}) collective-permute-start(f32[328,128]{1,0:T(8,128)S(1)} %collective-permute-done.rest_4_), channel_id=1, source_target_pairs={{0,1},{1,0},{2,3},{3,2},{4,5},{5,4},{6,7},{7,6},{8,9},{9,8},{10,11... | collective-permute-start | bytes 503816 | tf_op jit(solution)/shard_map/ppermute | solution.py:466
  31.9 0.6 collective-permute-done.14.rest_15_
  33.1 12.2 %shard_map.88 = (f32[16,120,128]{2,1,0:T(8,128)S(1)}, f32[328,128]{1,0:T(8,128)S(1)}, bf16[64,512]{1,0:T(8,128)(2,1)S(1)}) custom-call(s32[30]{0:T(128)S(4)} %get-tuple-element.16.ends_ref, bf16[40,2,15,32,128]{4,3,2,1,0:T(8,128)(2,1)} %model_hbm.11, f32[2,15,32,128]{3,2,1,0:T(8,128)S(1)} %copy-done, s32[15,32,128]{2,1,0:T(8,128)S(1)} %copy-done.2, ...), custom_call_target="tpu_custom_call" | custom-call | bytes 33210000 | tf_op jit(solution)/shard_map/pallas_call | solution.py:502
  45.3 27.2 %all_to_all.10.sums = f32[16,120,128]{2,1,0:T(8,128)S(1)} all-to-all(f32[16,120,128]{2,1,0:T(8,128)S(1)} %get-tuple-element.21), channel_id=1, replica_groups=mesh['grp'=2,'bl'=16] {'bl'}, dimensions={0} | all-to-all | bytes 1966080 | tf_op jit(solution)/shard_map/all_to_all | solution.py:461
  72.5 1.6 shard_map.89.g_ref.rest_0_.g_in
  74.3 0.5 collective-permute-start.18
  74.8 2.3 %collective-permute-start.15 = (f32[328,128]{1,0:T(8,128)S(1)}, f32[328,128]{1,0:T(8,128)S(1)}, u32[]{:S(2)}, u32[]{:S(2)}) collective-permute-start(f32[328,128]{1,0:T(8,128)S(1)} %shard_map.89.g_ref.rest_0_.g_in), channel_id=1, source_target_pairs={{0,4},{1,5},{2,6},{3,7},{4,0},{5,1},{6,2},{7,3},{8,12},{9,13},{10,... | collective-permute-start | bytes 503816 | tf_op jit(solution)/shard_map/ppermute | solution.py:466
  77.1 1.1 collective-permute-start.17
  78.1 5.6 %collective-permute-done.21.rest_6_ = f32[328,128]{1,0:T(8,128)S(1)} collective-permute-done((f32[328,128]{1,0:T(8,128)S(1)}, f32[328,128]{1,0:T(8,128)S(1)}, u32[]{:S(2)}, u32[]{:S(2)}) %collective-permute-start.21) | collective-permute-done | bytes 167968 | tf_op jit(solution)/shard_map/ppermute | solution.py:466
  83.7 0.7 collective-permute-start.22
  84.9 1.1 collective-permute-start.16
  86.0 2.8 %collective-permute-done.24.rest_2_ = f32[328,128]{1,0:T(8,128)S(1)} collective-permute-done((f32[328,128]{1,0:T(8,128)S(1)}, f32[328,128]{1,0:T(8,128)S(1)}, u32[]{:S(2)}, u32[]{:S(2)}) %collective-permute-start.24) | collective-permute-done | bytes 167968 | tf_op jit(solution)/shard_map/ppermute | solution.py:466
  88.9 1.5 collective-permute-start.26
  90.8 4.5 %shard_map.91 = (f32[2,15,32,128]{3,2,1,0:T(8,128)S(1)}, f32[4,88,128]{2,1,0:T(8,128)S(1)}, f32[4,88,128]{2,1,0:T(8,128)S(1)}, f32[328,128]{1,0:T(8,128)S(1)}) custom-call(s32[30]{0:T(128)S(4)} %get-tuple-element.16.ends_ref, bf16[40,2,15,32,128]{4,3,2,1,0:T(8,128)(2,1)} %model_hbm.11, ...), custom_call_target="tpu_custom_call", output_to_operand_aliasing={{3}: (3, {})} | custom-call | bytes 3690000 | tf_op jit(solution)/shard_map/pallas_call | solution.py:502
  95.2 1.8 %collective-permute-start.23 = (f32[328,128]{1,0:T(8,128)S(1)}, f32[328,128]{1,0:T(8,128)S(1)}, u32[]{:S(2)}, u32[]{:S(2)}) collective-permute-start(f32[328,128]{1,0:T(8,128)S(1)} %get-tuple-element.25.rest_0_), channel_id=1, source_target_pairs={{0,1},{1,0},{2,3},{3,2},{4,5},{5,4},{6,7},{7,6},{8,9},{9,8},{10,11... | collective-permute-start | bytes 503816 | tf_op jit(solution)/shard_map/ppermute | solution.py:466
  97.5 1.6 collective-permute-start.27
  99.2 1.0 collective-permute-done.27.rest_5_
  100.2 9.2 %shard_map.92 = f32[16,80,128]{2,1,0:T(8,128)} custom-call(s32[30]{0:T(128)S(4)} %get-tuple-element.16.ends_ref, bf16[40,2,15,32,128]{4,3,2,1,0:T(8,128)(2,1)} %model_hbm.11, s32[15,32,128]{2,1,0:T(8,128)S(1)} %copy-done.2, f32[8,88,128]{2,1,0:T(8,128)S(1)} %get-tuple-element.17.power_ref, f32[2,15,32,128]{3,2,1,0:T(8,128)S(1)} %get-tuple-element.22.acc_ref, ...), custom_call_target="tpu_custom_call" | custom-call | bytes 25830000 | tf_op jit(solution)/shard_map/pallas_call | solution.py:502
  109.4 5.7 %all-to-all-start.1 = ((f32[16,80,128]{2,1,0:T(8,128)}), f32[16,80,128]{2,1,0:T(8,128)S(1)}, u32[]{:S(2)}, u32[]{:S(2)}) async-start(f32[16,80,128]{2,1,0:T(8,128)} %shard_map.92), calls=%async_computation.1 | async-start | bytes 1310720 | tf_op jit(solution)/shard_map/all_to_all | solution.py:461
  115.1 1.0 shard_map.90.den_ref
  116.1 15.8 %all-to-all-done.1.sums = f32[16,80,128]{2,1,0:T(8,128)S(1)} async-done(((f32[16,80,128]{2,1,0:T(8,128)}), f32[16,80,128]{2,1,0:T(8,128)S(1)}, u32[]{:S(2)}, u32[]{:S(2)}) %all-to-all-start.1) | async-done | bytes 655392 | tf_op jit(solution)/shard_map/all_to_all | solution.py:461
  132.0 1.0 shard_map.93.rest_0_.rest_8_
  133.3 0.6 collective-permute-start.33
  133.9 2.3 %collective-permute-start.30 = (f32[328,128]{1,0:T(8,128)S(1)}, f32[328,128]{1,0:T(8,128)S(1)}, u32[]{:S(2)}, u32[]{:S(2)}) collective-permute-start(f32[328,128]{1,0:T(8,128)S(1)} %shard_map.93.rest_0_.rest_8_), channel_id=1, source_target_pairs={{0,4},{1,5},{2,6},{3,7},{4,0},{5,1},{6,2},{7,3},{8,12},{9,13},{10,... | collective-permute-start | bytes 503816 | tf_op jit(solution)/shard_map/ppermute | solution.py:466
  136.2 1.1 collective-permute-start.32
  137.2 5.6 %collective-permute-done.36.rest_6_.rest_14_ = f32[328,128]{1,0:T(8,128)S(1)} collective-permute-done((f32[328,128]{1,0:T(8,128)S(1)}, f32[328,128]{1,0:T(8,128)S(1)}, u32[]{:S(2)}, u32[]{:S(2)}) %collective-permute-start.36) | collective-permute-done | bytes 167968 | tf_op jit(solution)/shard_map/ppermute | solution.py:466
  142.8 0.6 collective-permute-start.37
  143.9 1.1 collective-permute-start.31
  145.1 3.0 %collective-permute-done.39.rest_2_ = f32[328,128]{1,0:T(8,128)S(1)} collective-permute-done((f32[328,128]{1,0:T(8,128)S(1)}, f32[328,128]{1,0:T(8,128)S(1)}, u32[]{:S(2)}, u32[]{:S(2)}) %collective-permute-start.39) | collective-permute-done | bytes 167968 | tf_op jit(solution)/shard_map/ppermute | solution.py:466
  148.1 1.5 collective-permute-start.41
  149.8 5.2 %shard_map.94 = (f32[2,15,32,128]{3,2,1,0:T(8,128)S(1)}, f32[4,88,128]{2,1,0:T(8,128)}, f32[4,88,128]{2,1,0:T(8,128)}, f32[328,128]{1,0:T(8,128)S(1)}) custom-call(s32[30]{0:T(128)S(4)} %get-tuple-element.16.ends_ref, bf16[40,2,15,32,128]{4,3,2,1,0:T(8,128)(2,1)} %model_hbm.11, f32[2,15,32,128]{3,2,1,0:T(8,128)S(1)} %copy-done, ...), custom_call_target="tpu_custom_call", output_to_operand_aliasing={{3}: (3, {})} | custom-call | bytes 3690000 | tf_op jit(solution)/shard_map/pallas_call | solution.py:502
  154.9 1.9 %collective-permute-start.38 = (f32[328,128]{1,0:T(8,128)S(1)}, f32[328,128]{1,0:T(8,128)S(1)}, u32[]{:S(2)}, u32[]{:S(2)}) collective-permute-start(f32[328,128]{1,0:T(8,128)S(1)} %get-tuple-element.27.rest_0_), channel_id=1, source_target_pairs={{0,1},{1,0},{2,3},{3,2},{4,5},{5,4},{6,7},{7,6},{8,9},{9,8},{10,11... | collective-permute-start | bytes 503816 | tf_op jit(solution)/shard_map/ppermute | solution.py:466
  157.3 1.1 collective-permute-start.42
  158.5 1.0 collective-permute-done.42.rest_5_
  159.4 5.7 %shard_map.95 = (f32[2,15,32,128]{3,2,1,0:T(8,128)}, f32[2,160,128]{2,1,0:T(8,128)}) custom-call(s32[30]{0:T(128)S(4)} %get-tuple-element.16.ends_ref, bf16[40,2,15,32,128]{4,3,2,1,0:T(8,128)(2,1)} %model_hbm.11, s32[15,32,128]{2,1,0:T(8,128)S(1)} %copy-done.2, f32[2,15,32,128]{3,2,1,0:T(8,128)S(1)} %get-tuple-element.26.acc_ref, ...), custom_call_target="tpu_custom_call" | custom-call | bytes 14760000 | tf_op jit(solution)/shard_map/pallas_call | solution.py:502
  (62 shorter events, 5.4 us)
Async XLA Ops:
  0.6 32.4 %copy-start = (f32[2,15,32,128]{3,2,1,0:T(8,128)S(1)}, f32[2,15,32,128]{3,2,1,0:T(8,128)}, u32[]{:S(2)}) copy-start(f32[2,15,32,128]{3,2,1,0:T(8,128)} %vis_ref.5) | copy-start | bytes 1474564
  1.8 9.0 %collective-permute-start.7 = (f32[328,128]{1,0:T(8,128)S(1)}, f32[328,128]{1,0:T(8,128)S(1)}, u32[]{:S(2)}, u32[]{:S(2)}) collective-permute-start(f32[328,128]{1,0:T(8,128)S(1)} %shard_map.86.rest_0_), channel_id=1, source_target_pairs={{0,12},{1,13},{2,14},{3,15},{4,8},{5,9},{6,10},{7,11},{8,4},{9,5},... | collective-permute-start | bytes 503816 | tf_op jit(solution)/shard_map/ppermute | solution.py:466
  3.1 9.6 %collective-permute-start = (f32[328,128]{1,0:T(8,128)S(1)}, f32[328,128]{1,0:T(8,128)S(1)}, u32[]{:S(2)}, u32[]{:S(2)}) collective-permute-start(f32[328,128]{1,0:T(8,128)S(1)} %shard_map.86.rest_0_), channel_id=1, source_target_pairs={{0,4},{1,5},{2,6},{3,7},{4,0},{5,1},{6,2},{7,3},{8,12},{9,13},{10,... | collective-permute-start | bytes 503816 | tf_op jit(solution)/shard_map/ppermute | solution.py:466
  5.3 10.9 %collective-permute-start.3 = (f32[328,128]{1,0:T(8,128)S(1)}, f32[328,128]{1,0:T(8,128)S(1)}, u32[]{:S(2)}, u32[]{:S(2)}) collective-permute-start(f32[328,128]{1,0:T(8,128)S(1)} %shard_map.86.rest_0_), channel_id=1, source_target_pairs={{0,2},{1,3},{2,0},{3,1},{4,6},{5,7},{6,4},{7,5},{8,10},{9,11},{10,... | collective-permute-start | bytes 503816 | tf_op jit(solution)/shard_map/ppermute | solution.py:466
  10.8 5.7 %collective-permute-start.8 = (f32[328,128]{1,0:T(8,128)S(1)}, f32[328,128]{1,0:T(8,128)S(1)}, u32[]{:S(2)}, u32[]{:S(2)}) collective-permute-start(f32[328,128]{1,0:T(8,128)S(1)} %collective-permute-done.7.rest_12_), channel_id=1, source_target_pairs={{0,4},{1,5},{2,6},{3,7},{4,0},{5,1},{6,2},{7,3},{8,12},{9,13},{10,... | collective-permute-start | bytes 503816 | tf_op jit(solution)/shard_map/ppermute | solution.py:466
  12.7 5.1 %collective-permute-start.1 = (f32[328,128]{1,0:T(8,128)S(1)}, f32[328,128]{1,0:T(8,128)S(1)}, u32[]{:S(2)}, u32[]{:S(2)}) collective-permute-start(f32[328,128]{1,0:T(8,128)S(1)} %collective-permute-done.rest_4_), channel_id=1, source_target_pairs={{0,2},{1,3},{2,0},{3,1},{4,6},{5,7},{6,4},{7,5},{8,10},{9,11},{10,... | collective-permute-start | bytes 503816 | tf_op jit(solution)/shard_map/ppermute | solution.py:466
  13.9 12.9 %collective-permute-start.2 = (f32[328,128]{1,0:T(8,128)S(1)}, f32[328,128]{1,0:T(8,128)S(1)}, u32[]{:S(2)}, u32[]{:S(2)}) collective-permute-start(f32[328,128]{1,0:T(8,128)S(1)} %shard_map.86.rest_0_), channel_id=1, source_target_pairs={{0,1},{1,0},{2,3},{3,2},{4,5},{5,4},{6,7},{7,6},{8,9},{9,8},{10,11... | collective-permute-start | bytes 503816 | tf_op jit(solution)/shard_map/ppermute | solution.py:466
  16.0 14.9 %collective-permute-start.13 = (f32[328,128]{1,0:T(8,128)S(1)}, f32[328,128]{1,0:T(8,128)S(1)}, u32[]{:S(2)}, u32[]{:S(2)}) collective-permute-start(f32[328,128]{1,0:T(8,128)S(1)} %collective-permute-done.7.rest_12_), channel_id=1, source_target_pairs={{0,2},{1,3},{2,0},{3,1},{4,6},{5,7},{6,4},{7,5},{8,10},{9,11},{10,... | collective-permute-start | bytes 503816 | tf_op jit(solution)/shard_map/ppermute | solution.py:466
  16.2 14.8 %collective-permute-start.12 = (f32[328,128]{1,0:T(8,128)S(1)}, f32[328,128]{1,0:T(8,128)S(1)}, u32[]{:S(2)}, u32[]{:S(2)}) collective-permute-start(f32[328,128]{1,0:T(8,128)S(1)} %collective-permute-done.7.rest_12_), channel_id=1, source_target_pairs={{0,1},{1,0},{2,3},{3,2},{4,5},{5,4},{6,7},{7,6},{8,9},{9,8},{10,11... | collective-permute-start | bytes 503816 | tf_op jit(solution)/shard_map/ppermute | solution.py:466
  16.5 14.9 %collective-permute-start.4 = (f32[328,128]{1,0:T(8,128)S(1)}, f32[328,128]{1,0:T(8,128)S(1)}, u32[]{:S(2)}, u32[]{:S(2)}) collective-permute-start(f32[328,128]{1,0:T(8,128)S(1)} %collective-permute-done.3.rest_2_), channel_id=1, source_target_pairs={{0,1},{1,0},{2,3},{3,2},{4,5},{5,4},{6,7},{7,6},{8,9},{9,8},{10,11... | collective-permute-start | bytes 503816 | tf_op jit(solution)/shard_map/ppermute | solution.py:466
  17.8 13.7 %collective-permute-start.10 = (f32[328,128]{1,0:T(8,128)S(1)}, f32[328,128]{1,0:T(8,128)S(1)}, u32[]{:S(2)}, u32[]{:S(2)}) collective-permute-start(f32[328,128]{1,0:T(8,128)S(1)} %collective-permute-done.8.rest_8_), channel_id=1, source_target_pairs={{0,2},{1,3},{2,0},{3,1},{4,6},{5,7},{6,4},{7,5},{8,10},{9,11},{10,... | collective-permute-start | bytes 503816 | tf_op jit(solution)/shard_map/ppermute | solution.py:466
  20.7 12.3 %copy-start.2 = (s32[15,32,128]{2,1,0:T(8,128)S(1)}, s32[15,32,128]{2,1,0:T(8,128)}, u32[]{:S(2)}) copy-start(s32[15,32,128]{2,1,0:T(8,128)} %mask_ref.7) | copy-start | bytes 737284
  26.8 5.1 %collective-permute-start.5 = (f32[328,128]{1,0:T(8,128)S(1)}, f32[328,128]{1,0:T(8,128)S(1)}, u32[]{:S(2)}, u32[]{:S(2)}) collective-permute-start(f32[328,128]{1,0:T(8,128)S(1)} %collective-permute-done.rest_4_), channel_id=1, source_target_pairs={{0,1},{1,0},{2,3},{3,2},{4,5},{5,4},{6,7},{7,6},{8,9},{9,8},{10,11... | collective-permute-start | bytes 503816 | tf_op jit(solution)/shard_map/ppermute | solution.py:466
  30.9 1.9 %collective-permute-start.6 = (f32[328,128]{1,0:T(8,128)S(1)}, f32[328,128]{1,0:T(8,128)S(1)}, u32[]{:S(2)}, u32[]{:S(2)}) collective-permute-start(f32[328,128]{1,0:T(8,128)S(1)} %get-tuple-element.18.rest_6_), channel_id=1, source_target_pairs={{0,1},{1,0},{2,3},{3,2},{4,5},{5,4},{6,7},{7,6},{8,9},{9,8},{10,11... | collective-permute-start | bytes 503816 | tf_op jit(solution)/shard_map/ppermute | solution.py:466
  31.0 1.6 collective-permute-start.14
  31.4 1.4 collective-permute-start.9
  31.5 1.6 collective-permute-start.11
  74.0 9.7 %collective-permute-start.21 = (f32[328,128]{1,0:T(8,128)S(1)}, f32[328,128]{1,0:T(8,128)S(1)}, u32[]{:S(2)}, u32[]{:S(2)}) collective-permute-start(f32[328,128]{1,0:T(8,128)S(1)} %shard_map.89.g_ref.rest_0_.g_in), channel_id=1, source_target_pairs={{0,12},{1,13},{2,14},{3,15},{4,8},{5,9},{6,10},{7,11},{8,4},{9,5},... | collective-permute-start | bytes 503816 | tf_op jit(solution)/shard_map/ppermute | solution.py:466
  74.3 10.1 %collective-permute-start.18 = (f32[328,128]{1,0:T(8,128)S(1)}, f32[328,128]{1,0:T(8,128)S(1)}, u32[]{:S(2)}, u32[]{:S(2)}) collective-permute-start(f32[328,128]{1,0:T(8,128)S(1)} %shard_map.89.g_ref.rest_0_.g_in), channel_id=1, source_target_pairs={{0,2},{1,3},{2,0},{3,1},{4,6},{5,7},{6,4},{7,5},{8,10},{9,11},{10,... | collective-permute-start | bytes 503816 | tf_op jit(solution)/shard_map/ppermute | solution.py:466
  74.8 9.7 %collective-permute-start.15 = (f32[328,128]{1,0:T(8,128)S(1)}, f32[328,128]{1,0:T(8,128)S(1)}, u32[]{:S(2)}, u32[]{:S(2)}) collective-permute-start(f32[328,128]{1,0:T(8,128)S(1)} %shard_map.89.g_ref.rest_0_.g_in), channel_id=1, source_target_pairs={{0,4},{1,5},{2,6},{3,7},{4,0},{5,1},{6,2},{7,3},{8,12},{9,13},{10,... | collective-permute-start | bytes 503816 | tf_op jit(solution)/shard_map/ppermute | solution.py:466
  77.1 7.8 %collective-permute-start.17 = (f32[328,128]{1,0:T(8,128)S(1)}, f32[328,128]{1,0:T(8,128)S(1)}, u32[]{:S(2)}, u32[]{:S(2)}) collective-permute-start(f32[328,128]{1,0:T(8,128)S(1)} %shard_map.89.g_ref.rest_0_.g_in), channel_id=1, source_target_pairs={{0,1},{1,0},{2,3},{3,2},{4,5},{5,4},{6,7},{7,6},{8,9},{9,8},{10,11... | collective-permute-start | bytes 503816 | tf_op jit(solution)/shard_map/ppermute | solution.py:466
  83.7 5.2 %collective-permute-start.24 = (f32[328,128]{1,0:T(8,128)S(1)}, f32[328,128]{1,0:T(8,128)S(1)}, u32[]{:S(2)}, u32[]{:S(2)}) collective-permute-start(f32[328,128]{1,0:T(8,128)S(1)} %collective-permute-done.21.rest_6_), channel_id=1, source_target_pairs={{0,4},{1,5},{2,6},{3,7},{4,0},{5,1},{6,2},{7,3},{8,12},{9,13},{10,... | collective-permute-start | bytes 503816 | tf_op jit(solution)/shard_map/ppermute | solution.py:466
  83.7 5.2 %collective-permute-start.22 = (f32[328,128]{1,0:T(8,128)S(1)}, f32[328,128]{1,0:T(8,128)S(1)}, u32[]{:S(2)}, u32[]{:S(2)}) collective-permute-start(f32[328,128]{1,0:T(8,128)S(1)} %collective-permute-done.21.rest_6_), channel_id=1, source_target_pairs={{0,1},{1,0},{2,3},{3,2},{4,5},{5,4},{6,7},{7,6},{8,9},{9,8},{10,11... | collective-permute-start | bytes 503816 | tf_op jit(solution)/shard_map/ppermute | solution.py:466
  84.4 5.9 %collective-permute-start.19 = (f32[328,128]{1,0:T(8,128)S(1)}, f32[328,128]{1,0:T(8,128)S(1)}, u32[]{:S(2)}, u32[]{:S(2)}) collective-permute-start(f32[328,128]{1,0:T(8,128)S(1)} %collective-permute-done.18.rest_2_), channel_id=1, source_target_pairs={{0,1},{1,0},{2,3},{3,2},{4,5},{5,4},{6,7},{7,6},{8,9},{9,8},{10,11... | collective-permute-start | bytes 503816 | tf_op jit(solution)/shard_map/ppermute | solution.py:466
  84.5 5.9 %collective-permute-start.20 = (f32[328,128]{1,0:T(8,128)S(1)}, f32[328,128]{1,0:T(8,128)S(1)}, u32[]{:S(2)}, u32[]{:S(2)}) collective-permute-start(f32[328,128]{1,0:T(8,128)S(1)} %collective-permute-done.15.rest_4_), channel_id=1, source_target_pairs={{0,1},{1,0},{2,3},{3,2},{4,5},{5,4},{6,7},{7,6},{8,9},{9,8},{10,11... | collective-permute-start | bytes 503816 | tf_op jit(solution)/shard_map/ppermute | solution.py:466
  84.9 5.8 %collective-permute-start.16 = (f32[328,128]{1,0:T(8,128)S(1)}, f32[328,128]{1,0:T(8,128)S(1)}, u32[]{:S(2)}, u32[]{:S(2)}) collective-permute-start(f32[328,128]{1,0:T(8,128)S(1)} %collective-permute-done.15.rest_4_), channel_id=1, source_target_pairs={{0,2},{1,3},{2,0},{3,1},{4,6},{5,7},{6,4},{7,5},{8,10},{9,11},{10,... | collective-permute-start | bytes 503816 | tf_op jit(solution)/shard_map/ppermute | solution.py:466
  88.9 8.1 %collective-permute-start.28 = (f32[328,128]{1,0:T(8,128)S(1)}, f32[328,128]{1,0:T(8,128)S(1)}, u32[]{:S(2)}, u32[]{:S(2)}) collective-permute-start(f32[328,128]{1,0:T(8,128)S(1)} %collective-permute-done.21.rest_6_), channel_id=1, source_target_pairs={{0,2},{1,3},{2,0},{3,1},{4,6},{5,7},{6,4},{7,5},{8,10},{9,11},{10,... | collective-permute-start | bytes 503816 | tf_op jit(solution)/shard_map/ppermute | solution.py:466
  88.9 8.7 %collective-permute-start.26 = (f32[328,128]{1,0:T(8,128)S(1)}, f32[328,128]{1,0:T(8,128)S(1)}, u32[]{:S(2)}, u32[]{:S(2)}) collective-permute-start(f32[328,128]{1,0:T(8,128)S(1)} %collective-permute-done.24.rest_2_), channel_id=1, source_target_pairs={{0,2},{1,3},{2,0},{3,1},{4,6},{5,7},{6,4},{7,5},{8,10},{9,11},{10,... | collective-permute-start | bytes 503816 | tf_op jit(solution)/shard_map/ppermute | solution.py:466
  95.2 3.9 %collective-permute-start.23 = (f32[328,128]{1,0:T(8,128)S(1)}, f32[328,128]{1,0:T(8,128)S(1)}, u32[]{:S(2)}, u32[]{:S(2)}) collective-permute-start(f32[328,128]{1,0:T(8,128)S(1)} %get-tuple-element.25.rest_0_), channel_id=1, source_target_pairs={{0,1},{1,0},{2,3},{3,2},{4,5},{5,4},{6,7},{7,6},{8,9},{9,8},{10,11... | collective-permute-start | bytes 503816 | tf_op jit(solution)/shard_map/ppermute | solution.py:466
  97.0 2.2 %collective-permute-start.29 = (f32[328,128]{1,0:T(8,128)S(1)}, f32[328,128]{1,0:T(8,128)S(1)}, u32[]{:S(2)}, u32[]{:S(2)}) collective-permute-start(f32[328,128]{1,0:T(8,128)S(1)} %collective-permute-done.28.rest_6_), channel_id=1, source_target_pairs={{0,1},{1,0},{2,3},{3,2},{4,5},{5,4},{6,7},{7,6},{8,9},{9,8},{10,11... | collective-permute-start | bytes 503816 | tf_op jit(solution)/shard_map/ppermute | solution.py:466
  97.4 1.8 %collective-permute-start.25 = (f32[328,128]{1,0:T(8,128)S(1)}, f32[328,128]{1,0:T(8,128)S(1)}, u32[]{:S(2)}, u32[]{:S(2)}) collective-permute-start(f32[328,128]{1,0:T(8,128)S(1)} %collective-permute-done.24.rest_2_), channel_id=1, source_target_pairs={{0,1},{1,0},{2,3},{3,2},{4,5},{5,4},{6,7},{7,6},{8,9},{9,8},{10,11... | collective-permute-start | bytes 503816 | tf_op jit(solution)/shard_map/ppermute | solution.py:466
  97.5 2.7 %collective-permute-start.27 = (f32[328,128]{1,0:T(8,128)S(1)}, f32[328,128]{1,0:T(8,128)S(1)}, u32[]{:S(2)}, u32[]{:S(2)}) collective-permute-start(f32[328,128]{1,0:T(8,128)S(1)} %collective-permute-done.26.rest_4_), channel_id=1, source_target_pairs={{0,1},{1,0},{2,3},{3,2},{4,5},{5,4},{6,7},{7,6},{8,9},{9,8},{10,11... | collective-permute-start | bytes 503816 | tf_op jit(solution)/shard_map/ppermute | solution.py:466
  109.4 22.6 %all-to-all-start.1 = ((f32[16,80,128]{2,1,0:T(8,128)}), f32[16,80,128]{2,1,0:T(8,128)S(1)}, u32[]{:S(2)}, u32[]{:S(2)}) async-start(f32[16,80,128]{2,1,0:T(8,128)} %shard_map.92), calls=%async_computation.1 | async-start | bytes 1310720 | tf_op jit(solution)/shard_map/all_to_all | solution.py:461
  133.0 9.8 %collective-permute-start.36 = (f32[328,128]{1,0:T(8,128)S(1)}, f32[328,128]{1,0:T(8,128)S(1)}, u32[]{:S(2)}, u32[]{:S(2)}) collective-permute-start(f32[328,128]{1,0:T(8,128)S(1)} %shard_map.93.rest_0_.rest_8_), channel_id=1, source_target_pairs={{0,12},{1,13},{2,14},{3,15},{4,8},{5,9},{6,10},{7,11},{8,4},{9,5},... | collective-permute-start | bytes 503816 | tf_op jit(solution)/shard_map/ppermute | solution.py:466
  133.3 10.1 %collective-permute-start.33 = (f32[328,128]{1,0:T(8,128)S(1)}, f32[328,128]{1,0:T(8,128)S(1)}, u32[]{:S(2)}, u32[]{:S(2)}) collective-permute-start(f32[328,128]{1,0:T(8,128)S(1)} %shard_map.93.rest_0_.rest_8_), channel_id=1, source_target_pairs={{0,2},{1,3},{2,0},{3,1},{4,6},{5,7},{6,4},{7,5},{8,10},{9,11},{10,... | collective-permute-start | bytes 503816 | tf_op jit(solution)/shard_map/ppermute | solution.py:466
  133.9 9.6 %collective-permute-start.30 = (f32[328,128]{1,0:T(8,128)S(1)}, f32[328,128]{1,0:T(8,128)S(1)}, u32[]{:S(2)}, u32[]{:S(2)}) collective-permute-start(f32[328,128]{1,0:T(8,128)S(1)} %shard_map.93.rest_0_.rest_8_), channel_id=1, source_target_pairs={{0,4},{1,5},{2,6},{3,7},{4,0},{5,1},{6,2},{7,3},{8,12},{9,13},{10,... | collective-permute-start | bytes 503816 | tf_op jit(solution)/shard_map/ppermute | solution.py:466
  136.2 7.8 %collective-permute-start.32 = (f32[328,128]{1,0:T(8,128)S(1)}, f32[328,128]{1,0:T(8,128)S(1)}, u32[]{:S(2)}, u32[]{:S(2)}) collective-permute-start(f32[328,128]{1,0:T(8,128)S(1)} %shard_map.93.rest_0_.rest_8_), channel_id=1, source_target_pairs={{0,1},{1,0},{2,3},{3,2},{4,5},{5,4},{6,7},{7,6},{8,9},{9,8},{10,11... | collective-permute-start | bytes 503816 | tf_op jit(solution)/shard_map/ppermute | solution.py:466
  142.8 5.3 %collective-permute-start.39 = (f32[328,128]{1,0:T(8,128)S(1)}, f32[328,128]{1,0:T(8,128)S(1)}, u32[]{:S(2)}, u32[]{:S(2)}) collective-permute-start(f32[328,128]{1,0:T(8,128)S(1)} %collective-permute-done.36.rest_6_.rest_14_), channel_id=1, source_target_pairs={{0,4},{1,5},{2,6},{3,7},{4,0},{5,1},{6,2},{7,3},{8,12},{9,13},{10,... | collective-permute-start | bytes 503816 | tf_op jit(solution)/shard_map/ppermute | solution.py:466
  142.8 5.3 %collective-permute-start.37 = (f32[328,128]{1,0:T(8,128)S(1)}, f32[328,128]{1,0:T(8,128)S(1)}, u32[]{:S(2)}, u32[]{:S(2)}) collective-permute-start(f32[328,128]{1,0:T(8,128)S(1)} %collective-permute-done.36.rest_6_.rest_14_), channel_id=1, source_target_pairs={{0,1},{1,0},{2,3},{3,2},{4,5},{5,4},{6,7},{7,6},{8,9},{9,8},{10,11... | collective-permute-start | bytes 503816 | tf_op jit(solution)/shard_map/ppermute | solution.py:466
  143.4 6.2 %collective-permute-start.34 = (f32[328,128]{1,0:T(8,128)S(1)}, f32[328,128]{1,0:T(8,128)S(1)}, u32[]{:S(2)}, u32[]{:S(2)}) collective-permute-start(f32[328,128]{1,0:T(8,128)S(1)} %collective-permute-done.33.rest_2_.rest_10_), channel_id=1, source_target_pairs={{0,1},{1,0},{2,3},{3,2},{4,5},{5,4},{6,7},{7,6},{8,9},{9,8},{10,11... | collective-permute-start | bytes 503816 | tf_op jit(solution)/shard_map/ppermute | solution.py:466
  143.5 6.1 %collective-permute-start.35 = (f32[328,128]{1,0:T(8,128)S(1)}, f32[328,128]{1,0:T(8,128)S(1)}, u32[]{:S(2)}, u32[]{:S(2)}) collective-permute-start(f32[328,128]{1,0:T(8,128)S(1)} %collective-permute-done.30.rest_4_.rest_12_), channel_id=1, source_target_pairs={{0,1},{1,0},{2,3},{3,2},{4,5},{5,4},{6,7},{7,6},{8,9},{9,8},{10,11... | collective-permute-start | bytes 503816 | tf_op jit(solution)/shard_map/ppermute | solution.py:466
  143.9 5.8 %collective-permute-start.31 = (f32[328,128]{1,0:T(8,128)S(1)}, f32[328,128]{1,0:T(8,128)S(1)}, u32[]{:S(2)}, u32[]{:S(2)}) collective-permute-start(f32[328,128]{1,0:T(8,128)S(1)} %collective-permute-done.30.rest_4_.rest_12_), channel_id=1, source_target_pairs={{0,2},{1,3},{2,0},{3,1},{4,6},{5,7},{6,4},{7,5},{8,10},{9,11},{10,... | collective-permute-start | bytes 503816 | tf_op jit(solution)/shard_map/ppermute | solution.py:466
  148.1 8.7 %collective-permute-start.43 = (f32[328,128]{1,0:T(8,128)S(1)}, f32[328,128]{1,0:T(8,128)S(1)}, u32[]{:S(2)}, u32[]{:S(2)}) collective-permute-start(f32[328,128]{1,0:T(8,128)S(1)} %collective-permute-done.36.rest_6_.rest_14_), channel_id=1, source_target_pairs={{0,2},{1,3},{2,0},{3,1},{4,6},{5,7},{6,4},{7,5},{8,10},{9,11},{10,... | collective-permute-start | bytes 503816 | tf_op jit(solution)/shard_map/ppermute | solution.py:466
  148.1 9.2 %collective-permute-start.41 = (f32[328,128]{1,0:T(8,128)S(1)}, f32[328,128]{1,0:T(8,128)S(1)}, u32[]{:S(2)}, u32[]{:S(2)}) collective-permute-start(f32[328,128]{1,0:T(8,128)S(1)} %collective-permute-done.39.rest_2_), channel_id=1, source_target_pairs={{0,2},{1,3},{2,0},{3,1},{4,6},{5,7},{6,4},{7,5},{8,10},{9,11},{10,... | collective-permute-start | bytes 503816 | tf_op jit(solution)/shard_map/ppermute | solution.py:466
  154.9 3.5 %collective-permute-start.38 = (f32[328,128]{1,0:T(8,128)S(1)}, f32[328,128]{1,0:T(8,128)S(1)}, u32[]{:S(2)}, u32[]{:S(2)}) collective-permute-start(f32[328,128]{1,0:T(8,128)S(1)} %get-tuple-element.27.rest_0_), channel_id=1, source_target_pairs={{0,1},{1,0},{2,3},{3,2},{4,5},{5,4},{6,7},{7,6},{8,9},{9,8},{10,11... | collective-permute-start | bytes 503816 | tf_op jit(solution)/shard_map/ppermute | solution.py:466
  156.8 1.6 collective-permute-start.44
  156.9 1.6 collective-permute-start.40
  157.3 2.1 %collective-permute-start.42 = (f32[328,128]{1,0:T(8,128)S(1)}, f32[328,128]{1,0:T(8,128)S(1)}, u32[]{:S(2)}, u32[]{:S(2)}) collective-permute-start(f32[328,128]{1,0:T(8,128)S(1)} %collective-permute-done.41.rest_4_), channel_id=1, source_target_pairs={{0,1},{1,0},{2,3},{3,2},{4,5},{5,4},{6,7},{7,6},{8,9},{9,8},{10,11... | collective-permute-start | bytes 503816 | tf_op jit(solution)/shard_map/ppermute | solution.py:466
  (1 other events, 0.9 us)

commit v13 on v8

--- a/solution.py
+++ b/solution.py
@@ -127,11 +127,14 @@
     for o in range(n):
         peer = jnp.bitwise_xor(me, o)
         lines[pl.ds(peer, 1), :] = ins[o][2 * rows : 2 * rows + 1, :]
+        done = []
         for s in range(per):
             at = s * SOURCE_COUNT + k * dpc
             x0, x1 = cross(ins[o][pl.ds(at, TILE), :], ins[o][pl.ds(rows + at, TILE), :])
+            done.append(jnp.where(c == 0, x0, x1))
+        for s in range(per):
             to = pl.multiple_of((peer * per + s) * TILE, TILE)
-            split[pl.ds(to, TILE), :] = jnp.where(c == 0, x0, x1)
+            split[pl.ds(to, TILE), :] = done[s]
     g = jnp.concatenate([split[pl.ds(dd, STATIONS, stride=TILE), :] for dd in range(dpc)], axis=1)
     put(g_ref, g, dpc)
     across = 128 // (2 * ROWS)
@@ -213,21 +216,34 @@
     for o in range(n):
         stack[jnp.bitwise_xor(me, o)] = ins[o][...]
 
-    def pair(b, carry):
+    def block(station, k, part):
+        at = lax.rem(station, per) * SOURCE_COUNT + k * dpc + part * rows
+        return stack[lax.div(station, per), pl.ds(at, TILE), :]
+
+    def one(b, k):
         p, q = first_ref[b], second_ref[b]
-
-        def block(station, k, part):
-            at = lax.rem(station, per) * SOURCE_COUNT + k * dpc + part * rows
-            return stack[lax.div(station, per), pl.ds(at, TILE), :]
-
-        for k in range(n // 2):
-            pr, pi, qr, qi = block(p, k, 0), block(p, k, 1), block(q, k, 0), block(q, k, 1)
-            hre[k, pl.ds(b * dpc, TILE), :] = pr * qr + pi * qi
-            him[k, pl.ds(b * dpc, TILE), :] = pi * qr - pr * qi
+        return block(p, k, 0), block(p, k, 1), block(q, k, 0), block(q, k, 1)
+
+    assemble(dpc, first_ref.shape[0], range(n // 2), one, hre, him)
+
+
+def assemble(dpc, pairs, chips, one, hre, him):
+    size = 3 if pairs % 3 == 0 else 1
+
+    def group(i, carry):
+        done = []
+        for u in range(size):
+            for m in chips:
+                pr, pi, qr, qi = one(i * size + u, m)
+                done.append((u, m, pr * qr + pi * qi, pi * qr - pr * qi))
+        for u, m, re, im in done:
+            rows = pl.ds((i * size + u) * dpc, TILE)
+            hre[m, rows, :] = re
+            him[m, rows, :] = im
         return carry
 
-    lax.fori_loop(0, first_ref.shape[0], pair, 0)
-    clear(dpc, first_ref.shape[0], hre, him)
+    lax.fori_loop(0, pairs // size, group, 0)
+    clear(dpc, pairs, hre, him)
 
 
 def piece_pair(dpc, even, ins, m, station):
@@ -239,17 +255,10 @@
 def products(dpc, me, first_ref, second_ref, ins, hre, him):
     even = lax.rem(me, 2) == 0
 
-    def pair(b, carry):
-        p, q = first_ref[b], second_ref[b]
-        for m in range(len(ins) // 2):
-            pr, pi = piece_pair(dpc, even, ins, m, p)
-            qr, qi = piece_pair(dpc, even, ins, m, q)
-            hre[m, pl.ds(b * dpc, TILE), :] = pr * qr + pi * qi
-            him[m, pl.ds(b * dpc, TILE), :] = pi * qr - pr * qi
-        return carry
-
-    lax.fori_loop(0, first_ref.shape[0], pair, 0)
-    clear(dpc, first_ref.shape[0], hre, him)
+    def one(b, m):
+        return *piece_pair(dpc, even, ins, m, first_ref[b]), *piece_pair(dpc, even, ins, m, second_ref[b])
+
+    assemble(dpc, first_ref.shape[0], range(len(ins) // 2), one, hre, him)
 
 
 def predict(dpc, b, acc, chips, model_ref, hre, him):
@@ -299,6 +308,7 @@
 
 def correlate(dpc, b, res, chips, model_ref, cre, cim):
     res_re, res_im = res
+    done = []
     for m, k in enumerate(chips):
         re, im = [], []
         for dd in range(dpc):
@@ -306,28 +316,28 @@
             mi = model_ref[k * dpc + dd, 1, b].astype(F32)
             re.append(tile_sum(mr * res_re + mi * res_im))
             im.append(tile_sum(mr * res_im - mi * res_re))
-        cre[m, pl.ds(b * dpc, TILE), :] = row_sums(re)
-        cim[m, pl.ds(b * dpc, TILE), :] = row_sums(im)
+        done.append((m, row_sums(re), row_sums(im)))
+    for m, re, im in done:
+        cre[m, pl.ds(b * dpc, TILE), :] = re
+        cim[m, pl.ds(b * dpc, TILE), :] = im
 
 
 def write_sums(dpc, chips, cre, cim, tiles, power_ref, out_ref, start):
     for m, k in enumerate(chips):
         re, im, at = tiles(m)
+        done = []
         for t in range(ROWS * dpc // TILE):
             rows = slice(t * TILE, (t + 1) * TILE)
             w = power_ref[k, rows, :]
-            x0, x1 = cross(cre[m, rows, :] + re[at, rows, :] * w, cim[m, rows, :] + im[at, rows, :] * w)
+            done.append(cross(cre[m, rows, :] + re[at, rows, :] * w, cim[m, rows, :] + im[at, rows, :] * w))
+        if start:
+            for t in range(dpc):
+                low, high = (slice(u * TILE, (u + 1) * TILE) for u in (t, t + dpc))
+                done.append(cross(power_ref[k, low, :], power_ref[k, high, :]))
+        for t, (x0, x1) in enumerate(done):
+            rows = slice(t * TILE, (t + 1) * TILE)
             out_ref[2 * k, rows, :] = x0
             out_ref[2 * k + 1, rows, :] = x1
-        if start:
-            for t in range(dpc):
-                x0, x1 = cross(
-                    power_ref[k, t * TILE : (t + 1) * TILE, :],
-                    power_ref[k, (t + dpc) * TILE : (t + dpc + 1) * TILE, :],
-                )
-                rows = slice(ROWS * dpc + t * TILE, ROWS * dpc + (t + 1) * TILE)
-                out_ref[2 * k, rows, :] = x0
-                out_ref[2 * k + 1, rows, :] = x1
 
 
 def first_pass_kernel(
@@ -416,12 +426,12 @@
     per = STATIONS // n
     even = lax.rem(me, 2) == 0
     for m, k in enumerate(chips_of(me, FAR + NEAR)):
-        for s in range(per):
-            re, im = piece_pair(dpc, even, ins, m, me * per + s)
+        done = [piece_pair(dpc, even, ins, m, me * per + s) for s in range(per)]
+        for s, parts in enumerate(done):
             for dd in range(dpc):
                 at = s * SOURCE_COUNT + k * dpc + dd
-                gains_ref[0, pl.ds(at, 1), :] = re[dd : dd + 1]
-                gains_ref[1, pl.ds(at, 1), :] = im[dd : dd + 1]
+                gains_ref[0, pl.ds(at, 1), :] = parts[0][dd : dd + 1]
+                gains_ref[1, pl.ds(at, 1), :] = parts[1][dd : dd + 1]
 
     def pair(b, carry):
         acc = acc_ref[0, b], acc_ref[1, b]

time: 161 us -> 160 us (level)
  no operation moved by 1% of the time
where the time goes in v13:
time: 160 us; the launch traced here: 157 us
  starting transfers between devices  58.8 us (37%)
  Pallas kernels  45 us (28%)
  waiting for transfers between devices  43.9 us (27%)
  local copies, waits for them, and re-layouts  8.44 us (5%)
    ppermute x45, starting transfers between devices, send(): return lax.ppermute(x, 'bl', [(i, i ^ o) for i in range(n)])  48.3 us
    pallas_call x11, Pallas kernels, call(): pl.pallas_call(functools.partial(kernel, n, dpc), in_specs=[place(x) for...  45 us
    all_to_all x2, waiting for transfers between devices, exchange(): return lax.all_to_all(x, 'bl', split_axis=0, concat_axis=0, tiled=True)  32.7 us
    ppermute x45, waiting for transfers between devices, send(): return lax.ppermute(x, 'bl', [(i, i ^ o) for i in range(n)])  11.2 us
    all_to_all x2, starting transfers between devices, exchange(): return lax.all_to_all(x, 'bl', split_axis=0, concat_axis=0, tiled=True)  10.5 us
    unnamed x38, local copies, waits for them, and re-layouts  8.44 us
  transfers between devices with their start and end apart: 47, of which 16 were waited for; matrix products, arithmetic and copies ran while one was open for 0% of the time, Pallas kernels for 11%

profile of v13, /device:TPU:9, one launch (start us, length us, event | category | flops | bytes accessed | tf_op | source)
XLA Modules:
  0.0 157.2 jit_solution(10592999313189765372)
XLA Ops:
  1.9 1.5 shard_map.86.rest_0_
  3.5 2.6 %collective-permute-start.7 = (f32[328,128]{1,0:T(8,128)S(1)}, f32[328,128]{1,0:T(8,128)S(1)}, u32[]{:S(2)}, u32[]{:S(2)}) collective-permute-start(f32[328,128]{1,0:T(8,128)S(1)} %shard_map.86.rest_0_), channel_id=1, source_target_pairs={{0,12},{1,13},{2,14},{3,15},{4,8},{5,9},{6,10},{7,11},{8,4},{9,5},... | collective-permute-start | bytes 503816 | tf_op jit(solution)/shard_map/ppermute | solution.py:460
  6.1 1.2 collective-permute-start.1
  7.3 1.4 collective-permute-done.3.rest_4_
  8.7 1.2 collective-permute-start.5
  9.9 4.6 %collective-permute-start.8 = (f32[328,128]{1,0:T(8,128)S(1)}, f32[328,128]{1,0:T(8,128)S(1)}, u32[]{:S(2)}, u32[]{:S(2)}) collective-permute-start(f32[328,128]{1,0:T(8,128)S(1)} %collective-permute-done.7.rest_12_), channel_id=1, source_target_pairs={{0,4},{1,5},{2,6},{3,7},{4,0},{5,1},{6,2},{7,3},{8,12},{9,13},{10,... | collective-permute-start | bytes 503816 | tf_op jit(solution)/shard_map/ppermute | solution.py:460
  14.5 1.9 %collective-permute-start = (f32[328,128]{1,0:T(8,128)S(1)}, f32[328,128]{1,0:T(8,128)S(1)}, u32[]{:S(2)}, u32[]{:S(2)}) collective-permute-start(f32[328,128]{1,0:T(8,128)S(1)} %shard_map.86.rest_0_), channel_id=1, source_target_pairs={{0,1},{1,0},{2,3},{3,2},{4,5},{5,4},{6,7},{7,6},{8,9},{9,8},{10,11... | collective-permute-start | bytes 503816 | tf_op jit(solution)/shard_map/ppermute | solution.py:460
  16.9 1.2 collective-permute-start.13
  18.5 0.9 copy-done.1
  19.4 5.6 %shard_map.87 = (f32[8,88,128]{2,1,0:T(8,128)S(1)}, f32[328,128]{1,0:T(8,128)S(1)}) custom-call(bf16[40,2,15,32,128]{4,3,2,1,0:T(8,128)(2,1)} %model_hbm.11, s32[15,32,128]{2,1,0:T(8,128)S(1)} %copy-done.1, f32[328,128]{1,0:T(8,128)S(1)} %collective-permute-done.5.unused_in), custom_call_target="tpu_custom_call", output_to_operand_aliasing={{1}: (2, {})} | custom-call | bytes 73800000 | tf_op jit(solution)/shard_map/pallas_call | solution.py:494
  25.0 3.4 %collective-permute-start.12 = (f32[328,128]{1,0:T(8,128)S(1)}, f32[328,128]{1,0:T(8,128)S(1)}, u32[]{:S(2)}, u32[]{:S(2)}) collective-permute-start(f32[328,128]{1,0:T(8,128)S(1)} %collective-permute-done.7.rest_12_), channel_id=1, source_target_pairs={{0,1},{1,0},{2,3},{3,2},{4,5},{5,4},{6,7},{7,6},{8,9},{9,8},{10,11... | collective-permute-start | bytes 503816 | tf_op jit(solution)/shard_map/ppermute | solution.py:460
  30.7 10.3 %shard_map.89 = f32[16,120,128]{2,1,0:T(8,128)} custom-call(s32[1]{0:T(128)} %bitcast.me_ref, s32[15]{0:T(128)S(1)} %copy-done.16, s32[15]{0:T(128)S(1)} %copy-done.18, bf16[40,2,15,32,128]{4,3,2,1,0:T(8,128)(2,1)} %model_hbm.11, f32[2,15,32,128]{3,2,1,0:T(8,128)S(1)} %copy-done, s32[15,32,128]{2,1,0:T(8,128)S(1)} %copy-done.2, ...), custom_call_target="tpu_custom_call" | custom-call | bytes 33210000 | tf_op jit(solution)/shard_map/pallas_call | solution.py:494
  41.0 5.6 %all-to-all-start = ((f32[16,120,128]{2,1,0:T(8,128)}), f32[16,120,128]{2,1,0:T(8,128)S(1)}, u32[]{:S(2)}, u32[]{:S(2)}) async-start(f32[16,120,128]{2,1,0:T(8,128)} %shard_map.89), calls=%async_computation | async-start | bytes 1966080 | tf_op jit(solution)/shard_map/all_to_all | solution.py:455
  46.7 0.9 copy-done.4
  47.6 0.9 copy-done.6
  48.5 0.9 copy-done.8
  49.4 0.9 copy-done.10
  50.3 0.9 copy-done.12
  51.2 1.3 shard_map.88
  53.3 16.9 %all-to-all-done.sums = f32[16,120,128]{2,1,0:T(8,128)S(1)} async-done(((f32[16,120,128]{2,1,0:T(8,128)}), f32[16,120,128]{2,1,0:T(8,128)S(1)}, u32[]{:S(2)}, u32[]{:S(2)}) %all-to-all-start) | async-done | bytes 983072 | tf_op jit(solution)/shard_map/all_to_all | solution.py:455
  70.2 0.9 copy-done.14
  71.1 1.5 shard_map.90.g_ref.rest_0_.g_in
  72.7 1.0 collective-permute-start.21
  73.7 1.6 collective-permute-start.18
  75.3 1.1 collective-permute-start.17
  76.3 2.5 %collective-permute-done.15.rest_4_ = f32[328,128]{1,0:T(8,128)S(1)} collective-permute-done((f32[328,128]{1,0:T(8,128)S(1)}, f32[328,128]{1,0:T(8,128)S(1)}, u32[]{:S(2)}, u32[]{:S(2)}) %collective-permute-start.15) | collective-permute-done | bytes 167968 | tf_op jit(solution)/shard_map/ppermute | solution.py:460
  78.8 0.7 collective-permute-start.16
  79.5 3.5 %collective-permute-start.24 = (f32[328,128]{1,0:T(8,128)S(1)}, f32[328,128]{1,0:T(8,128)S(1)}, u32[]{:S(2)}, u32[]{:S(2)}) collective-permute-start(f32[328,128]{1,0:T(8,128)S(1)} %collective-permute-done.21.rest_6_), channel_id=1, source_target_pairs={{0,4},{1,5},{2,6},{3,7},{4,0},{5,1},{6,2},{7,3},{8,12},{9,13},{10,... | collective-permute-start | bytes 503816 | tf_op jit(solution)/shard_map/ppermute | solution.py:460
  83.1 2.1 %collective-permute-start.20 = (f32[328,128]{1,0:T(8,128)S(1)}, f32[328,128]{1,0:T(8,128)S(1)}, u32[]{:S(2)}, u32[]{:S(2)}) collective-permute-start(f32[328,128]{1,0:T(8,128)S(1)} %collective-permute-done.15.rest_4_), channel_id=1, source_target_pairs={{0,1},{1,0},{2,3},{3,2},{4,5},{5,4},{6,7},{7,6},{8,9},{9,8},{10,11... | collective-permute-start | bytes 503816 | tf_op jit(solution)/shard_map/ppermute | solution.py:460
  85.9 1.2 collective-permute-start.26
  87.1 4.3 %shard_map.92 = (f32[2,15,32,128]{3,2,1,0:T(8,128)S(1)}, f32[4,88,128]{2,1,0:T(8,128)S(1)}, f32[4,88,128]{2,1,0:T(8,128)S(1)}, f32[328,128]{1,0:T(8,128)S(1)}) custom-call(s32[1]{0:T(128)} %bitcast.me_ref, s32[15]{0:T(128)S(1)} %copy-done.16, s32[15]{0:T(128)S(1)} %copy-done.18, ...), custom_call_target="tpu_custom_call", output_to_operand_aliasing={{3}: (5, {})} | custom-call | bytes 3690000 | tf_op jit(solution)/shard_map/pallas_call | solution.py:494
  91.4 2.8 %collective-permute-start.23 = (f32[328,128]{1,0:T(8,128)S(1)}, f32[328,128]{1,0:T(8,128)S(1)}, u32[]{:S(2)}, u32[]{:S(2)}) collective-permute-start(f32[328,128]{1,0:T(8,128)S(1)} %get-tuple-element.21.rest_0_), channel_id=1, source_target_pairs={{0,1},{1,0},{2,3},{3,2},{4,5},{5,4},{6,7},{7,6},{8,9},{9,8},{10,11... | collective-permute-start | bytes 503816 | tf_op jit(solution)/shard_map/ppermute | solution.py:460
  95.1 0.9 collective-permute-start.27
  96.0 1.0 collective-permute-done.27.rest_5_
  97.0 8.5 %shard_map.93 = f32[16,80,128]{2,1,0:T(8,128)} custom-call(s32[1]{0:T(128)} %bitcast.me_ref, s32[15]{0:T(128)S(1)} %copy-done.16, s32[15]{0:T(128)S(1)} %copy-done.18, bf16[40,2,15,32,128]{4,3,2,1,0:T(8,128)(2,1)} %model_hbm.11, s32[15,32,128]{2,1,0:T(8,128)S(1)} %copy-done.2, f32[8,88,128]{2,1,0:T(8,128)S(1)} %get-tuple-element.17.power_ref, ...), custom_call_target="tpu_custom_call" | custom-call | bytes 25830000 | tf_op jit(solution)/shard_map/pallas_call | solution.py:494
  105.5 4.9 %all-to-all-start.1 = ((f32[16,80,128]{2,1,0:T(8,128)}), f32[16,80,128]{2,1,0:T(8,128)S(1)}, u32[]{:S(2)}, u32[]{:S(2)}) async-start(f32[16,80,128]{2,1,0:T(8,128)} %shard_map.93), calls=%async_computation.1 | async-start | bytes 1310720 | tf_op jit(solution)/shard_map/all_to_all | solution.py:455
  110.4 1.0 shard_map.91.den_ref
  111.4 15.8 %all-to-all-done.1.sums = f32[16,80,128]{2,1,0:T(8,128)S(1)} async-done(((f32[16,80,128]{2,1,0:T(8,128)}), f32[16,80,128]{2,1,0:T(8,128)S(1)}, u32[]{:S(2)}, u32[]{:S(2)}) %all-to-all-start.1) | async-done | bytes 655392 | tf_op jit(solution)/shard_map/all_to_all | solution.py:455
  127.3 1.0 shard_map.94.rest_0_.rest_8_
  128.9 1.6 %collective-permute-start.33 = (f32[328,128]{1,0:T(8,128)S(1)}, f32[328,128]{1,0:T(8,128)S(1)}, u32[]{:S(2)}, u32[]{:S(2)}) collective-permute-start(f32[328,128]{1,0:T(8,128)S(1)} %shard_map.94.rest_0_.rest_8_), channel_id=1, source_target_pairs={{0,2},{1,3},{2,0},{3,1},{4,6},{5,7},{6,4},{7,5},{8,10},{9,11},{10,... | collective-permute-start | bytes 503816 | tf_op jit(solution)/shard_map/ppermute | solution.py:460
  130.6 1.1 collective-permute-start.32
  131.6 2.8 %collective-permute-done.30.rest_4_.rest_12_ = f32[328,128]{1,0:T(8,128)S(1)} collective-permute-done((f32[328,128]{1,0:T(8,128)S(1)}, f32[328,128]{1,0:T(8,128)S(1)}, u32[]{:S(2)}, u32[]{:S(2)}) %collective-permute-start.30) | collective-permute-done | bytes 167968 | tf_op jit(solution)/shard_map/ppermute | solution.py:460
  135.5 2.4 %collective-permute-start.39 = (f32[328,128]{1,0:T(8,128)S(1)}, f32[328,128]{1,0:T(8,128)S(1)}, u32[]{:S(2)}, u32[]{:S(2)}) collective-permute-start(f32[328,128]{1,0:T(8,128)S(1)} %collective-permute-done.36.rest_6_.rest_14_), channel_id=1, source_target_pairs={{0,4},{1,5},{2,6},{3,7},{4,0},{5,1},{6,2},{7,3},{8,12},{9,13},{10,... | collective-permute-start | bytes 503816 | tf_op jit(solution)/shard_map/ppermute | solution.py:460
  137.9 2.2 %collective-permute-start.35 = (f32[328,128]{1,0:T(8,128)S(1)}, f32[328,128]{1,0:T(8,128)S(1)}, u32[]{:S(2)}, u32[]{:S(2)}) collective-permute-start(f32[328,128]{1,0:T(8,128)S(1)} %collective-permute-done.30.rest_4_.rest_12_), channel_id=1, source_target_pairs={{0,1},{1,0},{2,3},{3,2},{4,5},{5,4},{6,7},{7,6},{8,9},{9,8},{10,11... | collective-permute-start | bytes 503816 | tf_op jit(solution)/shard_map/ppermute | solution.py:460
  141.2 1.0 collective-permute-start.41
  142.3 4.9 %shard_map.95 = (f32[2,15,32,128]{3,2,1,0:T(8,128)S(1)}, f32[4,88,128]{2,1,0:T(8,128)}, f32[4,88,128]{2,1,0:T(8,128)}, f32[328,128]{1,0:T(8,128)S(1)}) custom-call(s32[1]{0:T(128)} %bitcast.me_ref, s32[15]{0:T(128)S(1)} %copy-done.16, s32[15]{0:T(128)S(1)} %copy-done.18, bf16[40,2,15,32,128]{4,3,2,1,0:T(8,128)(2,1)} %model_hbm.11, ...), custom_call_target="tpu_custom_call", output_to_operand_aliasing={{3}: (5, {})} | custom-call | bytes 3690000 | tf_op jit(solution)/shard_map/pallas_call | solution.py:494
  147.2 3.0 %collective-permute-start.38 = (f32[328,128]{1,0:T(8,128)S(1)}, f32[328,128]{1,0:T(8,128)S(1)}, u32[]{:S(2)}, u32[]{:S(2)}) collective-permute-start(f32[328,128]{1,0:T(8,128)S(1)} %get-tuple-element.23.rest_0_), channel_id=1, source_target_pairs={{0,1},{1,0},{2,3},{3,2},{4,5},{5,4},{6,7},{7,6},{8,9},{9,8},{10,11... | collective-permute-start | bytes 503816 | tf_op jit(solution)/shard_map/ppermute | solution.py:460
  152.1 5.0 %shard_map.96 = (f32[2,15,32,128]{3,2,1,0:T(8,128)}, f32[2,160,128]{2,1,0:T(8,128)}) custom-call(s32[1]{0:T(128)} %bitcast.me_ref, s32[15]{0:T(128)S(1)} %copy-done.16, s32[15]{0:T(128)S(1)} %copy-done.18, bf16[40,2,15,32,128]{4,3,2,1,0:T(8,128)(2,1)} %model_hbm.11, s32[15,32,128]{2,1,0:T(8,128)S(1)} %copy-done.2, ...), custom_call_target="tpu_custom_call" | custom-call | bytes 14760000 | tf_op jit(solution)/shard_map/pallas_call | solution.py:494
  (95 shorter events, 11.6 us)
Async XLA Ops:
  1.9 28.8 %copy-start = (f32[2,15,32,128]{3,2,1,0:T(8,128)S(1)}, f32[2,15,32,128]{3,2,1,0:T(8,128)}, u32[]{:S(2)}) copy-start(f32[2,15,32,128]{3,2,1,0:T(8,128)} %vis_ref.5) | copy-start | bytes 1474564
  3.4 5.2 %collective-permute-start.3 = (f32[328,128]{1,0:T(8,128)S(1)}, f32[328,128]{1,0:T(8,128)S(1)}, u32[]{:S(2)}, u32[]{:S(2)}) collective-permute-start(f32[328,128]{1,0:T(8,128)S(1)} %shard_map.86.rest_0_), channel_id=1, source_target_pairs={{0,4},{1,5},{2,6},{3,7},{4,0},{5,1},{6,2},{7,3},{8,12},{9,13},{10,... | collective-permute-start | bytes 503816 | tf_op jit(solution)/shard_map/ppermute | solution.py:460
  3.5 6.4 %collective-permute-start.7 = (f32[328,128]{1,0:T(8,128)S(1)}, f32[328,128]{1,0:T(8,128)S(1)}, u32[]{:S(2)}, u32[]{:S(2)}) collective-permute-start(f32[328,128]{1,0:T(8,128)S(1)} %shard_map.86.rest_0_), channel_id=1, source_target_pairs={{0,12},{1,13},{2,14},{3,15},{4,8},{5,9},{6,10},{7,11},{8,4},{9,5},... | collective-permute-start | bytes 503816 | tf_op jit(solution)/shard_map/ppermute | solution.py:460
  6.1 10.3 %collective-permute-start.1 = (f32[328,128]{1,0:T(8,128)S(1)}, f32[328,128]{1,0:T(8,128)S(1)}, u32[]{:S(2)}, u32[]{:S(2)}) collective-permute-start(f32[328,128]{1,0:T(8,128)S(1)} %shard_map.86.rest_0_), channel_id=1, source_target_pairs={{0,2},{1,3},{2,0},{3,1},{4,6},{5,7},{6,4},{7,5},{8,10},{9,11},{10,... | collective-permute-start | bytes 503816 | tf_op jit(solution)/shard_map/ppermute | solution.py:460
  8.7 8.2 %collective-permute-start.5 = (f32[328,128]{1,0:T(8,128)S(1)}, f32[328,128]{1,0:T(8,128)S(1)}, u32[]{:S(2)}, u32[]{:S(2)}) collective-permute-start(f32[328,128]{1,0:T(8,128)S(1)} %collective-permute-done.3.rest_4_), channel_id=1, source_target_pairs={{0,2},{1,3},{2,0},{3,1},{4,6},{5,7},{6,4},{7,5},{8,10},{9,11},{10,... | collective-permute-start | bytes 503816 | tf_op jit(solution)/shard_map/ppermute | solution.py:460
  9.9 8.2 %collective-permute-start.8 = (f32[328,128]{1,0:T(8,128)S(1)}, f32[328,128]{1,0:T(8,128)S(1)}, u32[]{:S(2)}, u32[]{:S(2)}) collective-permute-start(f32[328,128]{1,0:T(8,128)S(1)} %collective-permute-done.7.rest_12_), channel_id=1, source_target_pairs={{0,4},{1,5},{2,6},{3,7},{4,0},{5,1},{6,2},{7,3},{8,12},{9,13},{10,... | collective-permute-start | bytes 503816 | tf_op jit(solution)/shard_map/ppermute | solution.py:460
  14.5 10.5 %collective-permute-start = (f32[328,128]{1,0:T(8,128)S(1)}, f32[328,128]{1,0:T(8,128)S(1)}, u32[]{:S(2)}, u32[]{:S(2)}) collective-permute-start(f32[328,128]{1,0:T(8,128)S(1)} %shard_map.86.rest_0_), channel_id=1, source_target_pairs={{0,1},{1,0},{2,3},{3,2},{4,5},{5,4},{6,7},{7,6},{8,9},{9,8},{10,11... | collective-permute-start | bytes 503816 | tf_op jit(solution)/shard_map/ppermute | solution.py:460
  16.4 12.0 %collective-permute-start.2 = (f32[328,128]{1,0:T(8,128)S(1)}, f32[328,128]{1,0:T(8,128)S(1)}, u32[]{:S(2)}, u32[]{:S(2)}) collective-permute-start(f32[328,128]{1,0:T(8,128)S(1)} %collective-permute-done.1.rest_2_), channel_id=1, source_target_pairs={{0,1},{1,0},{2,3},{3,2},{4,5},{5,4},{6,7},{7,6},{8,9},{9,8},{10,11... | collective-permute-start | bytes 503816 | tf_op jit(solution)/shard_map/ppermute | solution.py:460
  16.4 12.1 %collective-permute-start.4 = (f32[328,128]{1,0:T(8,128)S(1)}, f32[328,128]{1,0:T(8,128)S(1)}, u32[]{:S(2)}, u32[]{:S(2)}) collective-permute-start(f32[328,128]{1,0:T(8,128)S(1)} %collective-permute-done.3.rest_4_), channel_id=1, source_target_pairs={{0,1},{1,0},{2,3},{3,2},{4,5},{5,4},{6,7},{7,6},{8,9},{9,8},{10,11... | collective-permute-start | bytes 503816 | tf_op jit(solution)/shard_map/ppermute | solution.py:460
  16.9 12.0 %collective-permute-start.13 = (f32[328,128]{1,0:T(8,128)S(1)}, f32[328,128]{1,0:T(8,128)S(1)}, u32[]{:S(2)}, u32[]{:S(2)}) collective-permute-start(f32[328,128]{1,0:T(8,128)S(1)} %collective-permute-done.7.rest_12_), channel_id=1, source_target_pairs={{0,2},{1,3},{2,0},{3,1},{4,6},{5,7},{6,4},{7,5},{8,10},{9,11},{10,... | collective-permute-start | bytes 503816 | tf_op jit(solution)/shard_map/ppermute | solution.py:460
  18.1 10.9 %collective-permute-start.10 = (f32[328,128]{1,0:T(8,128)S(1)}, f32[328,128]{1,0:T(8,128)S(1)}, u32[]{:S(2)}, u32[]{:S(2)}) collective-permute-start(f32[328,128]{1,0:T(8,128)S(1)} %collective-permute-done.8.rest_8_), channel_id=1, source_target_pairs={{0,2},{1,3},{2,0},{3,1},{4,6},{5,7},{6,4},{7,5},{8,10},{9,11},{10,... | collective-permute-start | bytes 503816 | tf_op jit(solution)/shard_map/ppermute | solution.py:460
  25.0 4.4 %collective-permute-start.12 = (f32[328,128]{1,0:T(8,128)S(1)}, f32[328,128]{1,0:T(8,128)S(1)}, u32[]{:S(2)}, u32[]{:S(2)}) collective-permute-start(f32[328,128]{1,0:T(8,128)S(1)} %collective-permute-done.7.rest_12_), channel_id=1, source_target_pairs={{0,1},{1,0},{2,3},{3,2},{4,5},{5,4},{6,7},{7,6},{8,9},{9,8},{10,11... | collective-permute-start | bytes 503816 | tf_op jit(solution)/shard_map/ppermute | solution.py:460
  28.4 1.4 collective-permute-start.6
  28.5 1.7 %collective-permute-start.9 = (f32[328,128]{1,0:T(8,128)S(1)}, f32[328,128]{1,0:T(8,128)}, u32[]{:S(2)}, u32[]{:S(2)}) collective-permute-start(f32[328,128]{1,0:T(8,128)S(1)} %collective-permute-done.8.rest_8_), channel_id=1, source_target_pairs={{0,1},{1,0},{2,3},{3,2},{4,5},{5,4},{6,7},{7,6},{8,9},{9,8},{10,11... | collective-permute-start | bytes 503816 | tf_op jit(solution)/shard_map/ppermute | solution.py:460
  28.9 1.5 collective-permute-start.14
  29.0 1.7 %collective-permute-start.11 = (f32[328,128]{1,0:T(8,128)S(1)}, f32[328,128]{1,0:T(8,128)}, u32[]{:S(2)}, u32[]{:S(2)}) collective-permute-start(f32[328,128]{1,0:T(8,128)S(1)} %collective-permute-done.10.rest_10_), channel_id=1, source_target_pairs={{0,1},{1,0},{2,3},{3,2},{4,5},{5,4},{6,7},{7,6},{8,9},{9,8},{10,11... | collective-permute-start | bytes 503816 | tf_op jit(solution)/shard_map/ppermute | solution.py:460
  41.0 29.1 %all-to-all-start = ((f32[16,120,128]{2,1,0:T(8,128)}), f32[16,120,128]{2,1,0:T(8,128)S(1)}, u32[]{:S(2)}, u32[]{:S(2)}) async-start(f32[16,120,128]{2,1,0:T(8,128)} %shard_map.89), calls=%async_computation | async-start | bytes 1966080 | tf_op jit(solution)/shard_map/all_to_all | solution.py:455
  72.6 6.2 %collective-permute-start.15 = (f32[328,128]{1,0:T(8,128)S(1)}, f32[328,128]{1,0:T(8,128)S(1)}, u32[]{:S(2)}, u32[]{:S(2)}) collective-permute-start(f32[328,128]{1,0:T(8,128)S(1)} %shard_map.90.g_ref.rest_0_.g_in), channel_id=1, source_target_pairs={{0,4},{1,5},{2,6},{3,7},{4,0},{5,1},{6,2},{7,3},{8,12},{9,13},{10,... | collective-permute-start | bytes 503816 | tf_op jit(solution)/shard_map/ppermute | solution.py:460
  72.7 6.8 %collective-permute-start.21 = (f32[328,128]{1,0:T(8,128)S(1)}, f32[328,128]{1,0:T(8,128)S(1)}, u32[]{:S(2)}, u32[]{:S(2)}) collective-permute-start(f32[328,128]{1,0:T(8,128)S(1)} %shard_map.90.g_ref.rest_0_.g_in), channel_id=1, source_target_pairs={{0,12},{1,13},{2,14},{3,15},{4,8},{5,9},{6,10},{7,11},{8,4},{9,5},... | collective-permute-start | bytes 503816 | tf_op jit(solution)/shard_map/ppermute | solution.py:460
  73.7 11.4 %collective-permute-start.18 = (f32[328,128]{1,0:T(8,128)S(1)}, f32[328,128]{1,0:T(8,128)S(1)}, u32[]{:S(2)}, u32[]{:S(2)}) collective-permute-start(f32[328,128]{1,0:T(8,128)S(1)} %shard_map.90.g_ref.rest_0_.g_in), channel_id=1, source_target_pairs={{0,2},{1,3},{2,0},{3,1},{4,6},{5,7},{6,4},{7,5},{8,10},{9,11},{10,... | collective-permute-start | bytes 503816 | tf_op jit(solution)/shard_map/ppermute | solution.py:460
  75.3 9.9 %collective-permute-start.17 = (f32[328,128]{1,0:T(8,128)S(1)}, f32[328,128]{1,0:T(8,128)S(1)}, u32[]{:S(2)}, u32[]{:S(2)}) collective-permute-start(f32[328,128]{1,0:T(8,128)S(1)} %shard_map.90.g_ref.rest_0_.g_in), channel_id=1, source_target_pairs={{0,1},{1,0},{2,3},{3,2},{4,5},{5,4},{6,7},{7,6},{8,9},{9,8},{10,11... | collective-permute-start | bytes 503816 | tf_op jit(solution)/shard_map/ppermute | solution.py:460
  78.8 6.8 %collective-permute-start.16 = (f32[328,128]{1,0:T(8,128)S(1)}, f32[328,128]{1,0:T(8,128)S(1)}, u32[]{:S(2)}, u32[]{:S(2)}) collective-permute-start(f32[328,128]{1,0:T(8,128)S(1)} %collective-permute-done.15.rest_4_), channel_id=1, source_target_pairs={{0,2},{1,3},{2,0},{3,1},{4,6},{5,7},{6,4},{7,5},{8,10},{9,11},{10,... | collective-permute-start | bytes 503816 | tf_op jit(solution)/shard_map/ppermute | solution.py:460
  79.5 6.4 %collective-permute-start.24 = (f32[328,128]{1,0:T(8,128)S(1)}, f32[328,128]{1,0:T(8,128)S(1)}, u32[]{:S(2)}, u32[]{:S(2)}) collective-permute-start(f32[328,128]{1,0:T(8,128)S(1)} %collective-permute-done.21.rest_6_), channel_id=1, source_target_pairs={{0,4},{1,5},{2,6},{3,7},{4,0},{5,1},{6,2},{7,3},{8,12},{9,13},{10,... | collective-permute-start | bytes 503816 | tf_op jit(solution)/shard_map/ppermute | solution.py:460
  83.1 4.1 %collective-permute-start.20 = (f32[328,128]{1,0:T(8,128)S(1)}, f32[328,128]{1,0:T(8,128)S(1)}, u32[]{:S(2)}, u32[]{:S(2)}) collective-permute-start(f32[328,128]{1,0:T(8,128)S(1)} %collective-permute-done.15.rest_4_), channel_id=1, source_target_pairs={{0,1},{1,0},{2,3},{3,2},{4,5},{5,4},{6,7},{7,6},{8,9},{9,8},{10,11... | collective-permute-start | bytes 503816 | tf_op jit(solution)/shard_map/ppermute | solution.py:460
  85.1 2.0 %collective-permute-start.19 = (f32[328,128]{1,0:T(8,128)S(1)}, f32[328,128]{1,0:T(8,128)S(1)}, u32[]{:S(2)}, u32[]{:S(2)}) collective-permute-start(f32[328,128]{1,0:T(8,128)S(1)} %collective-permute-done.18.rest_2_), channel_id=1, source_target_pairs={{0,1},{1,0},{2,3},{3,2},{4,5},{5,4},{6,7},{7,6},{8,9},{9,8},{10,11... | collective-permute-start | bytes 503816 | tf_op jit(solution)/shard_map/ppermute | solution.py:460
  85.1 2.0 %collective-permute-start.22 = (f32[328,128]{1,0:T(8,128)S(1)}, f32[328,128]{1,0:T(8,128)S(1)}, u32[]{:S(2)}, u32[]{:S(2)}) collective-permute-start(f32[328,128]{1,0:T(8,128)S(1)} %collective-permute-done.21.rest_6_), channel_id=1, source_target_pairs={{0,1},{1,0},{2,3},{3,2},{4,5},{5,4},{6,7},{7,6},{8,9},{9,8},{10,11... | collective-permute-start | bytes 503816 | tf_op jit(solution)/shard_map/ppermute | solution.py:460
  85.6 8.7 %collective-permute-start.28 = (f32[328,128]{1,0:T(8,128)S(1)}, f32[328,128]{1,0:T(8,128)S(1)}, u32[]{:S(2)}, u32[]{:S(2)}) collective-permute-start(f32[328,128]{1,0:T(8,128)S(1)} %collective-permute-done.21.rest_6_), channel_id=1, source_target_pairs={{0,2},{1,3},{2,0},{3,1},{4,6},{5,7},{6,4},{7,5},{8,10},{9,11},{10,... | collective-permute-start | bytes 503816 | tf_op jit(solution)/shard_map/ppermute | solution.py:460
  85.9 9.2 %collective-permute-start.26 = (f32[328,128]{1,0:T(8,128)S(1)}, f32[328,128]{1,0:T(8,128)S(1)}, u32[]{:S(2)}, u32[]{:S(2)}) collective-permute-start(f32[328,128]{1,0:T(8,128)S(1)} %collective-permute-done.24.rest_2_), channel_id=1, source_target_pairs={{0,2},{1,3},{2,0},{3,1},{4,6},{5,7},{6,4},{7,5},{8,10},{9,11},{10,... | collective-permute-start | bytes 503816 | tf_op jit(solution)/shard_map/ppermute | solution.py:460
  91.4 4.5 %collective-permute-start.23 = (f32[328,128]{1,0:T(8,128)S(1)}, f32[328,128]{1,0:T(8,128)S(1)}, u32[]{:S(2)}, u32[]{:S(2)}) collective-permute-start(f32[328,128]{1,0:T(8,128)S(1)} %get-tuple-element.21.rest_0_), channel_id=1, source_target_pairs={{0,1},{1,0},{2,3},{3,2},{4,5},{5,4},{6,7},{7,6},{8,9},{9,8},{10,11... | collective-permute-start | bytes 503816 | tf_op jit(solution)/shard_map/ppermute | solution.py:460
  94.2 1.7 %collective-permute-start.25 = (f32[328,128]{1,0:T(8,128)S(1)}, f32[328,128]{1,0:T(8,128)S(1)}, u32[]{:S(2)}, u32[]{:S(2)}) collective-permute-start(f32[328,128]{1,0:T(8,128)S(1)} %collective-permute-done.24.rest_2_), channel_id=1, source_target_pairs={{0,1},{1,0},{2,3},{3,2},{4,5},{5,4},{6,7},{7,6},{8,9},{9,8},{10,11... | collective-permute-start | bytes 503816 | tf_op jit(solution)/shard_map/ppermute | solution.py:460
  94.3 1.6 %collective-permute-start.29 = (f32[328,128]{1,0:T(8,128)S(1)}, f32[328,128]{1,0:T(8,128)S(1)}, u32[]{:S(2)}, u32[]{:S(2)}) collective-permute-start(f32[328,128]{1,0:T(8,128)S(1)} %collective-permute-done.28.rest_6_), channel_id=1, source_target_pairs={{0,1},{1,0},{2,3},{3,2},{4,5},{5,4},{6,7},{7,6},{8,9},{9,8},{10,11... | collective-permute-start | bytes 503816 | tf_op jit(solution)/shard_map/ppermute | solution.py:460
  95.1 1.9 %collective-permute-start.27 = (f32[328,128]{1,0:T(8,128)S(1)}, f32[328,128]{1,0:T(8,128)S(1)}, u32[]{:S(2)}, u32[]{:S(2)}) collective-permute-start(f32[328,128]{1,0:T(8,128)S(1)} %collective-permute-done.26.rest_4_), channel_id=1, source_target_pairs={{0,1},{1,0},{2,3},{3,2},{4,5},{5,4},{6,7},{7,6},{8,9},{9,8},{10,11... | collective-permute-start | bytes 503816 | tf_op jit(solution)/shard_map/ppermute | solution.py:460
  105.5 21.8 %all-to-all-start.1 = ((f32[16,80,128]{2,1,0:T(8,128)}), f32[16,80,128]{2,1,0:T(8,128)S(1)}, u32[]{:S(2)}, u32[]{:S(2)}) async-start(f32[16,80,128]{2,1,0:T(8,128)} %shard_map.93), calls=%async_computation.1 | async-start | bytes 1310720 | tf_op jit(solution)/shard_map/all_to_all | solution.py:455
  128.3 6.1 %collective-permute-start.30 = (f32[328,128]{1,0:T(8,128)S(1)}, f32[328,128]{1,0:T(8,128)S(1)}, u32[]{:S(2)}, u32[]{:S(2)}) collective-permute-start(f32[328,128]{1,0:T(8,128)S(1)} %shard_map.94.rest_0_.rest_8_), channel_id=1, source_target_pairs={{0,4},{1,5},{2,6},{3,7},{4,0},{5,1},{6,2},{7,3},{8,12},{9,13},{10,... | collective-permute-start | bytes 503816 | tf_op jit(solution)/shard_map/ppermute | solution.py:460
  128.4 7.1 %collective-permute-start.36 = (f32[328,128]{1,0:T(8,128)S(1)}, f32[328,128]{1,0:T(8,128)S(1)}, u32[]{:S(2)}, u32[]{:S(2)}) collective-permute-start(f32[328,128]{1,0:T(8,128)S(1)} %shard_map.94.rest_0_.rest_8_), channel_id=1, source_target_pairs={{0,12},{1,13},{2,14},{3,15},{4,8},{5,9},{6,10},{7,11},{8,4},{9,5},... | collective-permute-start | bytes 503816 | tf_op jit(solution)/shard_map/ppermute | solution.py:460
  128.9 11.2 %collective-permute-start.33 = (f32[328,128]{1,0:T(8,128)S(1)}, f32[328,128]{1,0:T(8,128)S(1)}, u32[]{:S(2)}, u32[]{:S(2)}) collective-permute-start(f32[328,128]{1,0:T(8,128)S(1)} %shard_map.94.rest_0_.rest_8_), channel_id=1, source_target_pairs={{0,2},{1,3},{2,0},{3,1},{4,6},{5,7},{6,4},{7,5},{8,10},{9,11},{10,... | collective-permute-start | bytes 503816 | tf_op jit(solution)/shard_map/ppermute | solution.py:460
  130.6 9.6 %collective-permute-start.32 = (f32[328,128]{1,0:T(8,128)S(1)}, f32[328,128]{1,0:T(8,128)S(1)}, u32[]{:S(2)}, u32[]{:S(2)}) collective-permute-start(f32[328,128]{1,0:T(8,128)S(1)} %shard_map.94.rest_0_.rest_8_), channel_id=1, source_target_pairs={{0,1},{1,0},{2,3},{3,2},{4,5},{5,4},{6,7},{7,6},{8,9},{9,8},{10,11... | collective-permute-start | bytes 503816 | tf_op jit(solution)/shard_map/ppermute | solution.py:460
  134.5 6.2 %collective-permute-start.31 = (f32[328,128]{1,0:T(8,128)S(1)}, f32[328,128]{1,0:T(8,128)S(1)}, u32[]{:S(2)}, u32[]{:S(2)}) collective-permute-start(f32[328,128]{1,0:T(8,128)S(1)} %collective-permute-done.30.rest_4_.rest_12_), channel_id=1, source_target_pairs={{0,2},{1,3},{2,0},{3,1},{4,6},{5,7},{6,4},{7,5},{8,10},{9,11},{10,... | collective-permute-start | bytes 503816 | tf_op jit(solution)/shard_map/ppermute | solution.py:460
  135.5 5.7 %collective-permute-start.39 = (f32[328,128]{1,0:T(8,128)S(1)}, f32[328,128]{1,0:T(8,128)S(1)}, u32[]{:S(2)}, u32[]{:S(2)}) collective-permute-start(f32[328,128]{1,0:T(8,128)S(1)} %collective-permute-done.36.rest_6_.rest_14_), channel_id=1, source_target_pairs={{0,4},{1,5},{2,6},{3,7},{4,0},{5,1},{6,2},{7,3},{8,12},{9,13},{10,... | collective-permute-start | bytes 503816 | tf_op jit(solution)/shard_map/ppermute | solution.py:460
  137.9 4.4 %collective-permute-start.35 = (f32[328,128]{1,0:T(8,128)S(1)}, f32[328,128]{1,0:T(8,128)S(1)}, u32[]{:S(2)}, u32[]{:S(2)}) collective-permute-start(f32[328,128]{1,0:T(8,128)S(1)} %collective-permute-done.30.rest_4_.rest_12_), channel_id=1, source_target_pairs={{0,1},{1,0},{2,3},{3,2},{4,5},{5,4},{6,7},{7,6},{8,9},{9,8},{10,11... | collective-permute-start | bytes 503816 | tf_op jit(solution)/shard_map/ppermute | solution.py:460
  140.1 2.1 %collective-permute-start.34 = (f32[328,128]{1,0:T(8,128)S(1)}, f32[328,128]{1,0:T(8,128)S(1)}, u32[]{:S(2)}, u32[]{:S(2)}) collective-permute-start(f32[328,128]{1,0:T(8,128)S(1)} %collective-permute-done.33.rest_2_.rest_10_), channel_id=1, source_target_pairs={{0,1},{1,0},{2,3},{3,2},{4,5},{5,4},{6,7},{7,6},{8,9},{9,8},{10,11... | collective-permute-start | bytes 503816 | tf_op jit(solution)/shard_map/ppermute | solution.py:460
  140.1 2.1 %collective-permute-start.37 = (f32[328,128]{1,0:T(8,128)S(1)}, f32[328,128]{1,0:T(8,128)S(1)}, u32[]{:S(2)}, u32[]{:S(2)}) collective-permute-start(f32[328,128]{1,0:T(8,128)S(1)} %collective-permute-done.36.rest_6_.rest_14_), channel_id=1, source_target_pairs={{0,1},{1,0},{2,3},{3,2},{4,5},{5,4},{6,7},{7,6},{8,9},{9,8},{10,11... | collective-permute-start | bytes 503816 | tf_op jit(solution)/shard_map/ppermute | solution.py:460
  140.7 9.6 %collective-permute-start.43 = (f32[328,128]{1,0:T(8,128)S(1)}, f32[328,128]{1,0:T(8,128)S(1)}, u32[]{:S(2)}, u32[]{:S(2)}) collective-permute-start(f32[328,128]{1,0:T(8,128)S(1)} %collective-permute-done.36.rest_6_.rest_14_), channel_id=1, source_target_pairs={{0,2},{1,3},{2,0},{3,1},{4,6},{5,7},{6,4},{7,5},{8,10},{9,11},{10,... | collective-permute-start | bytes 503816 | tf_op jit(solution)/shard_map/ppermute | solution.py:460
  141.2 9.4 %collective-permute-start.41 = (f32[328,128]{1,0:T(8,128)S(1)}, f32[328,128]{1,0:T(8,128)S(1)}, u32[]{:S(2)}, u32[]{:S(2)}) collective-permute-start(f32[328,128]{1,0:T(8,128)S(1)} %collective-permute-done.39.rest_2_), channel_id=1, source_target_pairs={{0,2},{1,3},{2,0},{3,1},{4,6},{5,7},{6,4},{7,5},{8,10},{9,11},{10,... | collective-permute-start | bytes 503816 | tf_op jit(solution)/shard_map/ppermute | solution.py:460
  147.2 4.0 %collective-permute-start.38 = (f32[328,128]{1,0:T(8,128)S(1)}, f32[328,128]{1,0:T(8,128)S(1)}, u32[]{:S(2)}, u32[]{:S(2)}) collective-permute-start(f32[328,128]{1,0:T(8,128)S(1)} %get-tuple-element.23.rest_0_), channel_id=1, source_target_pairs={{0,1},{1,0},{2,3},{3,2},{4,5},{5,4},{6,7},{7,6},{8,9},{9,8},{10,11... | collective-permute-start | bytes 503816 | tf_op jit(solution)/shard_map/ppermute | solution.py:460
  150.1 1.4 collective-permute-start.40
  150.2 1.6 collective-permute-start.44
  150.7 1.4 collective-permute-start.42
  (18 other events, 101.7 us)

commit v14 on v13

--- a/solution.py
+++ b/solution.py
@@ -47,22 +47,22 @@
 PARTS = (1, 3, 7, ROWS)
 
 
-def pack_kernel(n, dpc, first_ref, second_ref, re_ref, im_ref, out_ref, sems):
-    rows = re_ref.shape[0]
+def pack_kernel(n, dpc, first_hbm, second_hbm, re_hbm, im_hbm, out_ref, first_ref, second_ref, sems):
+    rows = re_hbm.shape[0]
     copies = [
-        pltpu.make_async_copy(re_ref, out_ref.at[pl.ds(0, rows)], sems.at[0]),
-        pltpu.make_async_copy(im_ref, out_ref.at[pl.ds(rows, rows)], sems.at[1]),
+        pltpu.make_async_copy(first_hbm, first_ref, sems.at[0]),
+        pltpu.make_async_copy(second_hbm, second_ref, sems.at[1]),
+        pltpu.make_async_copy(re_hbm, out_ref.at[pl.ds(0, rows)], sems.at[2]),
+        pltpu.make_async_copy(im_hbm, out_ref.at[pl.ds(rows, rows)], sems.at[3]),
     ]
     for copy in copies:
         copy.start()
-    lane = lax.broadcasted_iota(jnp.int32, (TILE, 128), 1)
-    marks = jnp.zeros((TILE, 128), F32)
-    for r in range(first_ref.shape[0]):
-        marks = jnp.where(lane == r, (first_ref[r] + 1).astype(F32), marks)
-        marks = jnp.where(lane == ROWS + r, (second_ref[r] + 1).astype(F32), marks)
-    out_ref[2 * rows :] = marks
+    out_ref[2 * rows :] = jnp.zeros((TILE, 128), F32)
     for copy in copies:
         copy.wait()
+    pairs = first_ref.shape[1]
+    out_ref[2 * rows : 2 * rows + 1, :pairs] = (first_ref[...] + 1).astype(F32)
+    out_ref[2 * rows : 2 * rows + 1, ROWS : ROWS + pairs] = (second_ref[...] + 1).astype(F32)
 
 
 class Fetch:
@@ -98,7 +98,7 @@
 
     def pair(b, carry):
         weight = mask_ref[b].astype(F32)
-        for d in range(SOURCE_COUNT):
+        for d in range(model_ref.shape[0]):
             mr = model_ref[d, 0, b].astype(F32)
             mi = model_ref[d, 1, b].astype(F32)
             row = pl.ds(b * dpc + d % dpc, 1)
@@ -306,20 +306,24 @@
     return total
 
 
-def correlate(dpc, b, res, chips, model_ref, cre, cim):
+def correlate(dpc, b, res, chips, model_ref, cre, cim, weight=None, power_ref=None):
     res_re, res_im = res
     done = []
     for m, k in enumerate(chips):
-        re, im = [], []
+        re, im, power = [], [], []
         for dd in range(dpc):
             mr = model_ref[k * dpc + dd, 0, b].astype(F32)
             mi = model_ref[k * dpc + dd, 1, b].astype(F32)
             re.append(tile_sum(mr * res_re + mi * res_im))
             im.append(tile_sum(mr * res_im - mi * res_re))
-        done.append((m, row_sums(re), row_sums(im)))
-    for m, re, im in done:
+            if weight is not None and m >= len(chips) // 2:
+                power.append(tile_sum(weight * (mr * mr + mi * mi)))
+        done.append((m, row_sums(re), row_sums(im), row_sums(power) if power else None))
+    for m, re, im, power in done:
         cre[m, pl.ds(b * dpc, TILE), :] = re
         cim[m, pl.ds(b * dpc, TILE), :] = im
+        if power is not None:
+            power_ref[m, pl.ds(b * dpc, TILE), :] = power
 
 
 def write_sums(dpc, chips, cre, cim, tiles, power_ref, out_ref, start):
@@ -341,21 +345,22 @@
 
 
 def first_pass_kernel(
-    n, dpc, me_ref, first_ref, second_ref, model_hbm, vis_ref, mask_ref, power_ref, *rest
+    n, dpc, me_ref, first_ref, second_ref, model_hbm, vis_ref, mask_ref, power_in, *rest
 ):
-    ins, (out_ref, model_ref, sems, hre, him, cre, cim, stack) = rest[:n], rest[n:]
+    ins, (out_ref, power_ref, model_ref, sems, hre, him, cre, cim, stack) = rest[:n], rest[n:]
     fetch = Fetch(model_hbm, model_ref, sems)
     products_first(n, dpc, me_ref[0], first_ref, second_ref, ins, hre, him, stack)
     chips = range(n // 2)
+    power_ref[: n // 4] = power_in[...]
 
     def pair(b, carry):
         acc = predict(dpc, b, (vis_ref[0, b], vis_ref[1, b]), chips, model_ref, hre, him)
-        correlate(dpc, b, weighted(b, acc, mask_ref), chips, model_ref, cre, cim)
+        weight = mask_ref[b].astype(F32)
+        correlate(dpc, b, weighted(b, acc, mask_ref), chips, model_ref, cre, cim, weight, power_ref)
         return carry
 
     fetch.each(pair)
-
-    clear(dpc, mask_ref.shape[0], cre, cim)
+    clear(dpc, mask_ref.shape[0], cre, cim, power_ref)
     write_sums(dpc, chips, cre, cim, lambda m: (hre, him, m), power_ref, out_ref, True)
 
 
@@ -471,7 +476,8 @@
 
 
 def fast_body(n, vis, model, mask, first, second, gre, gim):
-    model, gre, gim = (pltpu.with_memory_space_constraint(x, pltpu.HBM) for x in (model, gre, gim))
+    starts = (first.reshape(1, -1), second.reshape(1, -1), gre, gim)
+    model, *starts = (pltpu.with_memory_space_constraint(x, pltpu.HBM) for x in (model, *starts))
     dpc = SOURCE_COUNT // (n // 2)
     width = dpc * 128
     pairs, times, channels = mask.shape
@@ -487,7 +493,7 @@
 
     def call(kernel, args, outs, scratch=(), micros=1, aliases={}):
         def place(x):
-            if x is model or x is gre or x is gim:
+            if x is model or any(x is y for y in starts):
                 return HBM
             return SMEM if x.ndim == 1 else VMEM
 
@@ -506,17 +512,16 @@
 
     (piece,) = call(
         pack_kernel,
-        (first, second, gre, gim),
+        starts,
         [shape(2 * gre.shape[0] + TILE, channels)],
-        [pltpu.SemaphoreType.DMA((2,))],
+        [pltpu.VMEM((1, pairs), jnp.int32)] * 2 + [pltpu.SemaphoreType.DMA((4,))],
     )
     power = None
 
     def powers_beside(x, got):
         nonlocal power
-        power, x = call(
-            power_kernel, (model, mask, x), [shape(*plane), shape(*x.shape)], held, micros=20, aliases={2: 1}
-        )
+        outs = [shape(*half), shape(*x.shape)]
+        power, x = call(power_kernel, (model, mask, x), outs, held_half, micros=20, aliases={2: 1})
         return x
 
     got = gather(n, piece, powers_beside)
@@ -527,10 +532,10 @@
         [(STATIONS * TILE, channels), (n, channels)],
         micros=2,
     )
-    (sums,) = call(
+    sums, power = call(
         first_pass_kernel,
         (me, first, second, model, vis, mask, power, *got),
-        [shape(n, (ROWS + TILE) * dpc, channels)],
+        [shape(n, (ROWS + TILE) * dpc, channels), shape(*plane)],
         held + [plane] * 4 + [(n,) + piece.shape],
         micros=9,
     )

time: 160 us -> 159 us (level)
  Pallas kernels: 45 us -> 43.1 us
    pallas_call x11, Pallas kernels: 45 us -> 43.1 us  [call(): pl.pallas_call(functools.partial(kernel, n, dpc), in_specs=[place(x) for...]
    unnamed x38 -> x42, local copies, waits for them, and re-layouts: 8.44 us -> 9.45 us
  transfers between devices with their start and end apart: 47 -> 47, of which waited for: 16 -> 16; matrix products, arithmetic and copies ran while one was open for 0% -> 0% of each run, Pallas kernels for 11% -> 10%
where the time goes in v14:
time: 159 us; the launch traced here: 156 us
  starting transfers between devices  58.7 us (37%)
  waiting for transfers between devices  44.1 us (28%)
  Pallas kernels  43.1 us (27%)
  local copies, waits for them, and re-layouts  9.45 us (6%)
    ppermute x45, starting transfers between devices, send(): return lax.ppermute(x, 'bl', [(i, i ^ o) for i in range(n)])  48.2 us
    pallas_call x11, Pallas kernels, call(): pl.pallas_call(functools.partial(kernel, n, dpc), in_specs=[place(x) for...  43.1 us
    all_to_all x2, waiting for transfers between devices, exchange(): return lax.all_to_all(x, 'bl', split_axis=0, concat_axis=0, tiled=True)  32.9 us
    ppermute x45, waiting for transfers between devices, send(): return lax.ppermute(x, 'bl', [(i, i ^ o) for i in range(n)])  11.2 us
    all_to_all x2, starting transfers between devices, exchange(): return lax.all_to_all(x, 'bl', split_axis=0, concat_axis=0, tiled=True)  10.5 us
    unnamed x42, local copies, waits for them, and re-layouts  9.45 us
  transfers between devices with their start and end apart: 47, of which 16 were waited for; matrix products, arithmetic and copies ran while one was open for 0% of the time, Pallas kernels for 10%

profile of v14, /device:TPU:9, one launch (start us, length us, event | category | flops | bytes accessed | tf_op | source)
XLA Modules:
  0.0 156.4 jit_solution(12566904266235126453)
XLA Ops:
  0.6 1.1 shard_map.86.rest_0_
  1.8 2.6 %collective-permute-start.7 = (f32[328,128]{1,0:T(8,128)S(1)}, f32[328,128]{1,0:T(8,128)S(1)}, u32[]{:S(2)}, u32[]{:S(2)}) collective-permute-start(f32[328,128]{1,0:T(8,128)S(1)} %shard_map.86.rest_0_), channel_id=1, source_target_pairs={{0,12},{1,13},{2,14},{3,15},{4,8},{5,9},{6,10},{7,11},{8,4},{9,5},... | collective-permute-start | bytes 503816 | tf_op jit(solution)/shard_map/ppermute | solution.py:465
  4.4 1.2 collective-permute-start.1
  5.6 1.4 collective-permute-done.3.rest_4_
  7.0 1.2 collective-permute-start.5
  8.2 4.6 %collective-permute-start.8 = (f32[328,128]{1,0:T(8,128)S(1)}, f32[328,128]{1,0:T(8,128)S(1)}, u32[]{:S(2)}, u32[]{:S(2)}) collective-permute-start(f32[328,128]{1,0:T(8,128)S(1)} %collective-permute-done.7.rest_12_), channel_id=1, source_target_pairs={{0,4},{1,5},{2,6},{3,7},{4,0},{5,1},{6,2},{7,3},{8,12},{9,13},{10,... | collective-permute-start | bytes 503816 | tf_op jit(solution)/shard_map/ppermute | solution.py:465
  12.8 1.9 %collective-permute-start = (f32[328,128]{1,0:T(8,128)S(1)}, f32[328,128]{1,0:T(8,128)S(1)}, u32[]{:S(2)}, u32[]{:S(2)}) collective-permute-start(f32[328,128]{1,0:T(8,128)S(1)} %shard_map.86.rest_0_), channel_id=1, source_target_pairs={{0,1},{1,0},{2,3},{3,2},{4,5},{5,4},{6,7},{7,6},{8,9},{9,8},{10,11... | collective-permute-start | bytes 503816 | tf_op jit(solution)/shard_map/ppermute | solution.py:465
  15.2 1.2 collective-permute-start.13
  16.8 0.9 copy-done.1
  17.7 3.4 %shard_map.87 = (f32[4,88,128]{2,1,0:T(8,128)S(1)}, f32[328,128]{1,0:T(8,128)S(1)}) custom-call(bf16[40,2,15,32,128]{4,3,2,1,0:T(8,128)(2,1)} %model_hbm.11, s32[15,32,128]{2,1,0:T(8,128)S(1)} %copy-done.1, f32[328,128]{1,0:T(8,128)S(1)} %collective-permute-done.5.unused_in), custom_call_target="tpu_custom_call", output_to_operand_aliasing={{1}: (2, {})} | custom-call | bytes 73800000 | tf_op jit(solution)/shard_map/pallas_call | solution.py:500
  21.8 3.3 %collective-permute-start.12 = (f32[328,128]{1,0:T(8,128)S(1)}, f32[328,128]{1,0:T(8,128)S(1)}, u32[]{:S(2)}, u32[]{:S(2)}) collective-permute-start(f32[328,128]{1,0:T(8,128)S(1)} %collective-permute-done.7.rest_12_), channel_id=1, source_target_pairs={{0,1},{1,0},{2,3},{3,2},{4,5},{5,4},{6,7},{7,6},{8,9},{9,8},{10,11... | collective-permute-start | bytes 503816 | tf_op jit(solution)/shard_map/ppermute | solution.py:465
  27.5 0.9 copy-done.16
  28.4 11.0 %shard_map.89 = (f32[16,120,128]{2,1,0:T(8,128)}, f32[8,88,128]{2,1,0:T(8,128)S(1)}) custom-call(s32[1]{0:T(128)} %bitcast.me_ref, s32[15]{0:T(128)S(1)} %copy-done.19, s32[15]{0:T(128)S(1)} %copy-done.20, bf16[40,2,15,32,128]{4,3,2,1,0:T(8,128)(2,1)} %model_hbm.11, f32[2,15,32,128]{3,2,1,0:T(8,128)S(1)} %copy-done, s32[15,32,128]{2,1,0:T(8,128)S(1)} %copy-done.2, ...), custom_call_target="tpu_custom_call" | custom-call | bytes 33210000 | tf_op jit(solution)/shard_map/pallas_call | solution.py:500
  40.2 5.6 %all-to-all-start = ((f32[16,120,128]{2,1,0:T(8,128)}), f32[16,120,128]{2,1,0:T(8,128)S(1)}, u32[]{:S(2)}, u32[]{:S(2)}) async-start(f32[16,120,128]{2,1,0:T(8,128)} %get-tuple-element.20), calls=%async_computation | async-start | bytes 1966080 | tf_op jit(solution)/shard_map/all_to_all | solution.py:460
  45.8 0.9 copy-done.4
  46.7 0.9 copy-done.6
  47.7 0.9 copy-done.8
  48.6 0.9 copy-done.10
  49.5 0.9 copy-done.12
  50.4 1.2 shard_map.88
  52.3 17.1 %all-to-all-done.sums = f32[16,120,128]{2,1,0:T(8,128)S(1)} async-done(((f32[16,120,128]{2,1,0:T(8,128)}), f32[16,120,128]{2,1,0:T(8,128)S(1)}, u32[]{:S(2)}, u32[]{:S(2)}) %all-to-all-start) | async-done | bytes 983072 | tf_op jit(solution)/shard_map/all_to_all | solution.py:460
  69.3 0.9 copy-done.18
  70.3 1.5 shard_map.90.g_ref.rest_0_.g_in
  71.9 1.0 collective-permute-start.21
  72.9 1.6 collective-permute-start.18
  74.5 1.0 collective-permute-start.17
  75.5 2.5 %collective-permute-done.15.rest_4_ = f32[328,128]{1,0:T(8,128)S(1)} collective-permute-done((f32[328,128]{1,0:T(8,128)S(1)}, f32[328,128]{1,0:T(8,128)S(1)}, u32[]{:S(2)}, u32[]{:S(2)}) %collective-permute-start.15) | collective-permute-done | bytes 167968 | tf_op jit(solution)/shard_map/ppermute | solution.py:465
  78.7 3.6 %collective-permute-start.24 = (f32[328,128]{1,0:T(8,128)S(1)}, f32[328,128]{1,0:T(8,128)S(1)}, u32[]{:S(2)}, u32[]{:S(2)}) collective-permute-start(f32[328,128]{1,0:T(8,128)S(1)} %collective-permute-done.21.rest_6_), channel_id=1, source_target_pairs={{0,4},{1,5},{2,6},{3,7},{4,0},{5,1},{6,2},{7,3},{8,12},{9,13},{10,... | collective-permute-start | bytes 503816 | tf_op jit(solution)/shard_map/ppermute | solution.py:465
  82.2 2.1 %collective-permute-start.20 = (f32[328,128]{1,0:T(8,128)S(1)}, f32[328,128]{1,0:T(8,128)S(1)}, u32[]{:S(2)}, u32[]{:S(2)}) collective-permute-start(f32[328,128]{1,0:T(8,128)S(1)} %collective-permute-done.15.rest_4_), channel_id=1, source_target_pairs={{0,1},{1,0},{2,3},{3,2},{4,5},{5,4},{6,7},{7,6},{8,9},{9,8},{10,11... | collective-permute-start | bytes 503816 | tf_op jit(solution)/shard_map/ppermute | solution.py:465
  85.1 1.2 collective-permute-start.26
  86.3 4.3 %shard_map.92 = (f32[2,15,32,128]{3,2,1,0:T(8,128)S(1)}, f32[4,88,128]{2,1,0:T(8,128)S(1)}, f32[4,88,128]{2,1,0:T(8,128)S(1)}, f32[328,128]{1,0:T(8,128)S(1)}) custom-call(s32[1]{0:T(128)} %bitcast.me_ref, s32[15]{0:T(128)S(1)} %copy-done.19, s32[15]{0:T(128)S(1)} %copy-done.20, ...), custom_call_target="tpu_custom_call", output_to_operand_aliasing={{3}: (5, {})} | custom-call | bytes 3690000 | tf_op jit(solution)/shard_map/pallas_call | solution.py:500
  90.6 2.8 %collective-permute-start.23 = (f32[328,128]{1,0:T(8,128)S(1)}, f32[328,128]{1,0:T(8,128)S(1)}, u32[]{:S(2)}, u32[]{:S(2)}) collective-permute-start(f32[328,128]{1,0:T(8,128)S(1)} %get-tuple-element.25.rest_0_), channel_id=1, source_target_pairs={{0,1},{1,0},{2,3},{3,2},{4,5},{5,4},{6,7},{7,6},{8,9},{9,8},{10,11... | collective-permute-start | bytes 503816 | tf_op jit(solution)/shard_map/ppermute | solution.py:465
  94.3 0.9 collective-permute-start.27
  95.1 1.0 collective-permute-done.27.rest_5_
  96.2 8.5 %shard_map.93 = f32[16,80,128]{2,1,0:T(8,128)} custom-call(s32[1]{0:T(128)} %bitcast.me_ref, s32[15]{0:T(128)S(1)} %copy-done.19, s32[15]{0:T(128)S(1)} %copy-done.20, bf16[40,2,15,32,128]{4,3,2,1,0:T(8,128)(2,1)} %model_hbm.11, s32[15,32,128]{2,1,0:T(8,128)S(1)} %copy-done.2, f32[8,88,128]{2,1,0:T(8,128)S(1)} %copy-done.14, ...), custom_call_target="tpu_custom_call" | custom-call | bytes 25830000 | tf_op jit(solution)/shard_map/pallas_call | solution.py:500
  104.6 4.9 %all-to-all-start.1 = ((f32[16,80,128]{2,1,0:T(8,128)}), f32[16,80,128]{2,1,0:T(8,128)S(1)}, u32[]{:S(2)}, u32[]{:S(2)}) async-start(f32[16,80,128]{2,1,0:T(8,128)} %shard_map.93), calls=%async_computation.1 | async-start | bytes 1310720 | tf_op jit(solution)/shard_map/all_to_all | solution.py:460
  109.5 1.0 shard_map.91.den_ref
  110.6 15.8 %all-to-all-done.1.sums = f32[16,80,128]{2,1,0:T(8,128)S(1)} async-done(((f32[16,80,128]{2,1,0:T(8,128)}), f32[16,80,128]{2,1,0:T(8,128)S(1)}, u32[]{:S(2)}, u32[]{:S(2)}) %all-to-all-start.1) | async-done | bytes 655392 | tf_op jit(solution)/shard_map/all_to_all | solution.py:460
  126.4 1.0 shard_map.94.rest_0_.rest_8_
  128.1 1.6 %collective-permute-start.33 = (f32[328,128]{1,0:T(8,128)S(1)}, f32[328,128]{1,0:T(8,128)S(1)}, u32[]{:S(2)}, u32[]{:S(2)}) collective-permute-start(f32[328,128]{1,0:T(8,128)S(1)} %shard_map.94.rest_0_.rest_8_), channel_id=1, source_target_pairs={{0,2},{1,3},{2,0},{3,1},{4,6},{5,7},{6,4},{7,5},{8,10},{9,11},{10,... | collective-permute-start | bytes 503816 | tf_op jit(solution)/shard_map/ppermute | solution.py:465
  129.7 1.1 collective-permute-start.32
  130.8 2.8 %collective-permute-done.30.rest_4_.rest_12_ = f32[328,128]{1,0:T(8,128)S(1)} collective-permute-done((f32[328,128]{1,0:T(8,128)S(1)}, f32[328,128]{1,0:T(8,128)S(1)}, u32[]{:S(2)}, u32[]{:S(2)}) %collective-permute-start.30) | collective-permute-done | bytes 167968 | tf_op jit(solution)/shard_map/ppermute | solution.py:465
  134.7 2.4 %collective-permute-start.39 = (f32[328,128]{1,0:T(8,128)S(1)}, f32[328,128]{1,0:T(8,128)S(1)}, u32[]{:S(2)}, u32[]{:S(2)}) collective-permute-start(f32[328,128]{1,0:T(8,128)S(1)} %collective-permute-done.36.rest_6_.rest_14_), channel_id=1, source_target_pairs={{0,4},{1,5},{2,6},{3,7},{4,0},{5,1},{6,2},{7,3},{8,12},{9,13},{10,... | collective-permute-start | bytes 503816 | tf_op jit(solution)/shard_map/ppermute | solution.py:465
  137.1 2.2 %collective-permute-start.35 = (f32[328,128]{1,0:T(8,128)S(1)}, f32[328,128]{1,0:T(8,128)S(1)}, u32[]{:S(2)}, u32[]{:S(2)}) collective-permute-start(f32[328,128]{1,0:T(8,128)S(1)} %collective-permute-done.30.rest_4_.rest_12_), channel_id=1, source_target_pairs={{0,1},{1,0},{2,3},{3,2},{4,5},{5,4},{6,7},{7,6},{8,9},{9,8},{10,11... | collective-permute-start | bytes 503816 | tf_op jit(solution)/shard_map/ppermute | solution.py:465
  140.4 1.0 collective-permute-start.41
  141.4 4.9 %shard_map.95 = (f32[2,15,32,128]{3,2,1,0:T(8,128)S(1)}, f32[4,88,128]{2,1,0:T(8,128)}, f32[4,88,128]{2,1,0:T(8,128)}, f32[328,128]{1,0:T(8,128)S(1)}) custom-call(s32[1]{0:T(128)} %bitcast.me_ref, s32[15]{0:T(128)S(1)} %copy-done.19, s32[15]{0:T(128)S(1)} %copy-done.20, bf16[40,2,15,32,128]{4,3,2,1,0:T(8,128)(2,1)} %model_hbm.11, ...), custom_call_target="tpu_custom_call", output_to_operand_aliasing={{3}: (5, {})} | custom-call | bytes 3690000 | tf_op jit(solution)/shard_map/pallas_call | solution.py:500
  146.4 2.9 %collective-permute-start.38 = (f32[328,128]{1,0:T(8,128)S(1)}, f32[328,128]{1,0:T(8,128)S(1)}, u32[]{:S(2)}, u32[]{:S(2)}) collective-permute-start(f32[328,128]{1,0:T(8,128)S(1)} %get-tuple-element.27.rest_0_), channel_id=1, source_target_pairs={{0,1},{1,0},{2,3},{3,2},{4,5},{5,4},{6,7},{7,6},{8,9},{9,8},{10,11... | collective-permute-start | bytes 503816 | tf_op jit(solution)/shard_map/ppermute | solution.py:465
  151.2 5.0 %shard_map.96 = (f32[2,15,32,128]{3,2,1,0:T(8,128)}, f32[2,160,128]{2,1,0:T(8,128)}) custom-call(s32[1]{0:T(128)} %bitcast.me_ref, s32[15]{0:T(128)S(1)} %copy-done.19, s32[15]{0:T(128)S(1)} %copy-done.20, bf16[40,2,15,32,128]{4,3,2,1,0:T(8,128)(2,1)} %model_hbm.11, s32[15,32,128]{2,1,0:T(8,128)S(1)} %copy-done.2, ...), custom_call_target="tpu_custom_call" | custom-call | bytes 14760000 | tf_op jit(solution)/shard_map/pallas_call | solution.py:500
  (99 shorter events, 12.4 us)
Async XLA Ops:
  1.8 5.2 %collective-permute-start.3 = (f32[328,128]{1,0:T(8,128)S(1)}, f32[328,128]{1,0:T(8,128)S(1)}, u32[]{:S(2)}, u32[]{:S(2)}) collective-permute-start(f32[328,128]{1,0:T(8,128)S(1)} %shard_map.86.rest_0_), channel_id=1, source_target_pairs={{0,4},{1,5},{2,6},{3,7},{4,0},{5,1},{6,2},{7,3},{8,12},{9,13},{10,... | collective-permute-start | bytes 503816 | tf_op jit(solution)/shard_map/ppermute | solution.py:465
  1.8 6.4 %collective-permute-start.7 = (f32[328,128]{1,0:T(8,128)S(1)}, f32[328,128]{1,0:T(8,128)S(1)}, u32[]{:S(2)}, u32[]{:S(2)}) collective-permute-start(f32[328,128]{1,0:T(8,128)S(1)} %shard_map.86.rest_0_), channel_id=1, source_target_pairs={{0,12},{1,13},{2,14},{3,15},{4,8},{5,9},{6,10},{7,11},{8,4},{9,5},... | collective-permute-start | bytes 503816 | tf_op jit(solution)/shard_map/ppermute | solution.py:465
  4.4 10.3 %collective-permute-start.1 = (f32[328,128]{1,0:T(8,128)S(1)}, f32[328,128]{1,0:T(8,128)S(1)}, u32[]{:S(2)}, u32[]{:S(2)}) collective-permute-start(f32[328,128]{1,0:T(8,128)S(1)} %shard_map.86.rest_0_), channel_id=1, source_target_pairs={{0,2},{1,3},{2,0},{3,1},{4,6},{5,7},{6,4},{7,5},{8,10},{9,11},{10,... | collective-permute-start | bytes 503816 | tf_op jit(solution)/shard_map/ppermute | solution.py:465
  7.0 8.2 %collective-permute-start.5 = (f32[328,128]{1,0:T(8,128)S(1)}, f32[328,128]{1,0:T(8,128)S(1)}, u32[]{:S(2)}, u32[]{:S(2)}) collective-permute-start(f32[328,128]{1,0:T(8,128)S(1)} %collective-permute-done.3.rest_4_), channel_id=1, source_target_pairs={{0,2},{1,3},{2,0},{3,1},{4,6},{5,7},{6,4},{7,5},{8,10},{9,11},{10,... | collective-permute-start | bytes 503816 | tf_op jit(solution)/shard_map/ppermute | solution.py:465
  8.2 8.2 %collective-permute-start.8 = (f32[328,128]{1,0:T(8,128)S(1)}, f32[328,128]{1,0:T(8,128)S(1)}, u32[]{:S(2)}, u32[]{:S(2)}) collective-permute-start(f32[328,128]{1,0:T(8,128)S(1)} %collective-permute-done.7.rest_12_), channel_id=1, source_target_pairs={{0,4},{1,5},{2,6},{3,7},{4,0},{5,1},{6,2},{7,3},{8,12},{9,13},{10,... | collective-permute-start | bytes 503816 | tf_op jit(solution)/shard_map/ppermute | solution.py:465
  12.8 9.0 %collective-permute-start = (f32[328,128]{1,0:T(8,128)S(1)}, f32[328,128]{1,0:T(8,128)S(1)}, u32[]{:S(2)}, u32[]{:S(2)}) collective-permute-start(f32[328,128]{1,0:T(8,128)S(1)} %shard_map.86.rest_0_), channel_id=1, source_target_pairs={{0,1},{1,0},{2,3},{3,2},{4,5},{5,4},{6,7},{7,6},{8,9},{9,8},{10,11... | collective-permute-start | bytes 503816 | tf_op jit(solution)/shard_map/ppermute | solution.py:465
  14.7 10.5 %collective-permute-start.2 = (f32[328,128]{1,0:T(8,128)S(1)}, f32[328,128]{1,0:T(8,128)S(1)}, u32[]{:S(2)}, u32[]{:S(2)}) collective-permute-start(f32[328,128]{1,0:T(8,128)S(1)} %collective-permute-done.1.rest_2_), channel_id=1, source_target_pairs={{0,1},{1,0},{2,3},{3,2},{4,5},{5,4},{6,7},{7,6},{8,9},{9,8},{10,11... | collective-permute-start | bytes 503816 | tf_op jit(solution)/shard_map/ppermute | solution.py:465
  14.7 10.5 %collective-permute-start.4 = (f32[328,128]{1,0:T(8,128)S(1)}, f32[328,128]{1,0:T(8,128)S(1)}, u32[]{:S(2)}, u32[]{:S(2)}) collective-permute-start(f32[328,128]{1,0:T(8,128)S(1)} %collective-permute-done.3.rest_4_), channel_id=1, source_target_pairs={{0,1},{1,0},{2,3},{3,2},{4,5},{5,4},{6,7},{7,6},{8,9},{9,8},{10,11... | collective-permute-start | bytes 503816 | tf_op jit(solution)/shard_map/ppermute | solution.py:465
  15.2 10.5 %collective-permute-start.13 = (f32[328,128]{1,0:T(8,128)S(1)}, f32[328,128]{1,0:T(8,128)S(1)}, u32[]{:S(2)}, u32[]{:S(2)}) collective-permute-start(f32[328,128]{1,0:T(8,128)S(1)} %collective-permute-done.7.rest_12_), channel_id=1, source_target_pairs={{0,2},{1,3},{2,0},{3,1},{4,6},{5,7},{6,4},{7,5},{8,10},{9,11},{10,... | collective-permute-start | bytes 503816 | tf_op jit(solution)/shard_map/ppermute | solution.py:465
  16.5 9.3 %collective-permute-start.10 = (f32[328,128]{1,0:T(8,128)S(1)}, f32[328,128]{1,0:T(8,128)S(1)}, u32[]{:S(2)}, u32[]{:S(2)}) collective-permute-start(f32[328,128]{1,0:T(8,128)S(1)} %collective-permute-done.8.rest_8_), channel_id=1, source_target_pairs={{0,2},{1,3},{2,0},{3,1},{4,6},{5,7},{6,4},{7,5},{8,10},{9,11},{10,... | collective-permute-start | bytes 503816 | tf_op jit(solution)/shard_map/ppermute | solution.py:465
  21.8 4.4 %collective-permute-start.12 = (f32[328,128]{1,0:T(8,128)S(1)}, f32[328,128]{1,0:T(8,128)S(1)}, u32[]{:S(2)}, u32[]{:S(2)}) collective-permute-start(f32[328,128]{1,0:T(8,128)S(1)} %collective-permute-done.7.rest_12_), channel_id=1, source_target_pairs={{0,1},{1,0},{2,3},{3,2},{4,5},{5,4},{6,7},{7,6},{8,9},{9,8},{10,11... | collective-permute-start | bytes 503816 | tf_op jit(solution)/shard_map/ppermute | solution.py:465
  25.2 1.4 collective-permute-start.6
  25.3 1.6 %collective-permute-start.9 = (f32[328,128]{1,0:T(8,128)S(1)}, f32[328,128]{1,0:T(8,128)S(1)}, u32[]{:S(2)}, u32[]{:S(2)}) collective-permute-start(f32[328,128]{1,0:T(8,128)S(1)} %collective-permute-done.8.rest_8_), channel_id=1, source_target_pairs={{0,1},{1,0},{2,3},{3,2},{4,5},{5,4},{6,7},{7,6},{8,9},{9,8},{10,11... | collective-permute-start | bytes 503816 | tf_op jit(solution)/shard_map/ppermute | solution.py:465
  25.7 1.4 collective-permute-start.14
  25.8 1.7 %collective-permute-start.11 = (f32[328,128]{1,0:T(8,128)S(1)}, f32[328,128]{1,0:T(8,128)}, u32[]{:S(2)}, u32[]{:S(2)}) collective-permute-start(f32[328,128]{1,0:T(8,128)S(1)} %collective-permute-done.10.rest_10_), channel_id=1, source_target_pairs={{0,1},{1,0},{2,3},{3,2},{4,5},{5,4},{6,7},{7,6},{8,9},{9,8},{10,11... | collective-permute-start | bytes 503816 | tf_op jit(solution)/shard_map/ppermute | solution.py:465
  40.2 29.1 %all-to-all-start = ((f32[16,120,128]{2,1,0:T(8,128)}), f32[16,120,128]{2,1,0:T(8,128)S(1)}, u32[]{:S(2)}, u32[]{:S(2)}) async-start(f32[16,120,128]{2,1,0:T(8,128)} %get-tuple-element.20), calls=%async_computation | async-start | bytes 1966080 | tf_op jit(solution)/shard_map/all_to_all | solution.py:460
  52.3 43.9 %copy-start.14 = (f32[8,88,128]{2,1,0:T(8,128)S(1)}, f32[8,88,128]{2,1,0:T(8,128)}, u32[]{:S(2)}) copy-start(f32[8,88,128]{2,1,0:T(8,128)} %copy-done.13) | copy-start | bytes 1081348
  71.8 6.2 %collective-permute-start.15 = (f32[328,128]{1,0:T(8,128)S(1)}, f32[328,128]{1,0:T(8,128)S(1)}, u32[]{:S(2)}, u32[]{:S(2)}) collective-permute-start(f32[328,128]{1,0:T(8,128)S(1)} %shard_map.90.g_ref.rest_0_.g_in), channel_id=1, source_target_pairs={{0,4},{1,5},{2,6},{3,7},{4,0},{5,1},{6,2},{7,3},{8,12},{9,13},{10,... | collective-permute-start | bytes 503816 | tf_op jit(solution)/shard_map/ppermute | solution.py:465
  71.9 6.8 %collective-permute-start.21 = (f32[328,128]{1,0:T(8,128)S(1)}, f32[328,128]{1,0:T(8,128)S(1)}, u32[]{:S(2)}, u32[]{:S(2)}) collective-permute-start(f32[328,128]{1,0:T(8,128)S(1)} %shard_map.90.g_ref.rest_0_.g_in), channel_id=1, source_target_pairs={{0,12},{1,13},{2,14},{3,15},{4,8},{5,9},{6,10},{7,11},{8,4},{9,5},... | collective-permute-start | bytes 503816 | tf_op jit(solution)/shard_map/ppermute | solution.py:465
  72.9 11.4 %collective-permute-start.18 = (f32[328,128]{1,0:T(8,128)S(1)}, f32[328,128]{1,0:T(8,128)S(1)}, u32[]{:S(2)}, u32[]{:S(2)}) collective-permute-start(f32[328,128]{1,0:T(8,128)S(1)} %shard_map.90.g_ref.rest_0_.g_in), channel_id=1, source_target_pairs={{0,2},{1,3},{2,0},{3,1},{4,6},{5,7},{6,4},{7,5},{8,10},{9,11},{10,... | collective-permute-start | bytes 503816 | tf_op jit(solution)/shard_map/ppermute | solution.py:465
  74.5 9.8 %collective-permute-start.17 = (f32[328,128]{1,0:T(8,128)S(1)}, f32[328,128]{1,0:T(8,128)S(1)}, u32[]{:S(2)}, u32[]{:S(2)}) collective-permute-start(f32[328,128]{1,0:T(8,128)S(1)} %shard_map.90.g_ref.rest_0_.g_in), channel_id=1, source_target_pairs={{0,1},{1,0},{2,3},{3,2},{4,5},{5,4},{6,7},{7,6},{8,9},{9,8},{10,11... | collective-permute-start | bytes 503816 | tf_op jit(solution)/shard_map/ppermute | solution.py:465
  78.0 6.8 %collective-permute-start.16 = (f32[328,128]{1,0:T(8,128)S(1)}, f32[328,128]{1,0:T(8,128)S(1)}, u32[]{:S(2)}, u32[]{:S(2)}) collective-permute-start(f32[328,128]{1,0:T(8,128)S(1)} %collective-permute-done.15.rest_4_), channel_id=1, source_target_pairs={{0,2},{1,3},{2,0},{3,1},{4,6},{5,7},{6,4},{7,5},{8,10},{9,11},{10,... | collective-permute-start | bytes 503816 | tf_op jit(solution)/shard_map/ppermute | solution.py:465
  78.7 6.4 %collective-permute-start.24 = (f32[328,128]{1,0:T(8,128)S(1)}, f32[328,128]{1,0:T(8,128)S(1)}, u32[]{:S(2)}, u32[]{:S(2)}) collective-permute-start(f32[328,128]{1,0:T(8,128)S(1)} %collective-permute-done.21.rest_6_), channel_id=1, source_target_pairs={{0,4},{1,5},{2,6},{3,7},{4,0},{5,1},{6,2},{7,3},{8,12},{9,13},{10,... | collective-permute-start | bytes 503816 | tf_op jit(solution)/shard_map/ppermute | solution.py:465
  82.2 4.1 %collective-permute-start.20 = (f32[328,128]{1,0:T(8,128)S(1)}, f32[328,128]{1,0:T(8,128)S(1)}, u32[]{:S(2)}, u32[]{:S(2)}) collective-permute-start(f32[328,128]{1,0:T(8,128)S(1)} %collective-permute-done.15.rest_4_), channel_id=1, source_target_pairs={{0,1},{1,0},{2,3},{3,2},{4,5},{5,4},{6,7},{7,6},{8,9},{9,8},{10,11... | collective-permute-start | bytes 503816 | tf_op jit(solution)/shard_map/ppermute | solution.py:465
  84.3 2.0 %collective-permute-start.19 = (f32[328,128]{1,0:T(8,128)S(1)}, f32[328,128]{1,0:T(8,128)S(1)}, u32[]{:S(2)}, u32[]{:S(2)}) collective-permute-start(f32[328,128]{1,0:T(8,128)S(1)} %collective-permute-done.18.rest_2_), channel_id=1, source_target_pairs={{0,1},{1,0},{2,3},{3,2},{4,5},{5,4},{6,7},{7,6},{8,9},{9,8},{10,11... | collective-permute-start | bytes 503816 | tf_op jit(solution)/shard_map/ppermute | solution.py:465
  84.3 2.0 %collective-permute-start.22 = (f32[328,128]{1,0:T(8,128)S(1)}, f32[328,128]{1,0:T(8,128)S(1)}, u32[]{:S(2)}, u32[]{:S(2)}) collective-permute-start(f32[328,128]{1,0:T(8,128)S(1)} %collective-permute-done.21.rest_6_), channel_id=1, source_target_pairs={{0,1},{1,0},{2,3},{3,2},{4,5},{5,4},{6,7},{7,6},{8,9},{9,8},{10,11... | collective-permute-start | bytes 503816 | tf_op jit(solution)/shard_map/ppermute | solution.py:465
  84.8 8.7 %collective-permute-start.28 = (f32[328,128]{1,0:T(8,128)S(1)}, f32[328,128]{1,0:T(8,128)S(1)}, u32[]{:S(2)}, u32[]{:S(2)}) collective-permute-start(f32[328,128]{1,0:T(8,128)S(1)} %collective-permute-done.21.rest_6_), channel_id=1, source_target_pairs={{0,2},{1,3},{2,0},{3,1},{4,6},{5,7},{6,4},{7,5},{8,10},{9,11},{10,... | collective-permute-start | bytes 503816 | tf_op jit(solution)/shard_map/ppermute | solution.py:465
  85.1 9.1 %collective-permute-start.26 = (f32[328,128]{1,0:T(8,128)S(1)}, f32[328,128]{1,0:T(8,128)S(1)}, u32[]{:S(2)}, u32[]{:S(2)}) collective-permute-start(f32[328,128]{1,0:T(8,128)S(1)} %collective-permute-done.24.rest_2_), channel_id=1, source_target_pairs={{0,2},{1,3},{2,0},{3,1},{4,6},{5,7},{6,4},{7,5},{8,10},{9,11},{10,... | collective-permute-start | bytes 503816 | tf_op jit(solution)/shard_map/ppermute | solution.py:465
  90.6 4.5 %collective-permute-start.23 = (f32[328,128]{1,0:T(8,128)S(1)}, f32[328,128]{1,0:T(8,128)S(1)}, u32[]{:S(2)}, u32[]{:S(2)}) collective-permute-start(f32[328,128]{1,0:T(8,128)S(1)} %get-tuple-element.25.rest_0_), channel_id=1, source_target_pairs={{0,1},{1,0},{2,3},{3,2},{4,5},{5,4},{6,7},{7,6},{8,9},{9,8},{10,11... | collective-permute-start | bytes 503816 | tf_op jit(solution)/shard_map/ppermute | solution.py:465
  93.4 1.7 %collective-permute-start.25 = (f32[328,128]{1,0:T(8,128)S(1)}, f32[328,128]{1,0:T(8,128)S(1)}, u32[]{:S(2)}, u32[]{:S(2)}) collective-permute-start(f32[328,128]{1,0:T(8,128)S(1)} %collective-permute-done.24.rest_2_), channel_id=1, source_target_pairs={{0,1},{1,0},{2,3},{3,2},{4,5},{5,4},{6,7},{7,6},{8,9},{9,8},{10,11... | collective-permute-start | bytes 503816 | tf_op jit(solution)/shard_map/ppermute | solution.py:465
  93.5 1.6 %collective-permute-start.29 = (f32[328,128]{1,0:T(8,128)S(1)}, f32[328,128]{1,0:T(8,128)S(1)}, u32[]{:S(2)}, u32[]{:S(2)}) collective-permute-start(f32[328,128]{1,0:T(8,128)S(1)} %collective-permute-done.28.rest_6_), channel_id=1, source_target_pairs={{0,1},{1,0},{2,3},{3,2},{4,5},{5,4},{6,7},{7,6},{8,9},{9,8},{10,11... | collective-permute-start | bytes 503816 | tf_op jit(solution)/shard_map/ppermute | solution.py:465
  94.3 1.9 %collective-permute-start.27 = (f32[328,128]{1,0:T(8,128)S(1)}, f32[328,128]{1,0:T(8,128)S(1)}, u32[]{:S(2)}, u32[]{:S(2)}) collective-permute-start(f32[328,128]{1,0:T(8,128)S(1)} %collective-permute-done.26.rest_4_), channel_id=1, source_target_pairs={{0,1},{1,0},{2,3},{3,2},{4,5},{5,4},{6,7},{7,6},{8,9},{9,8},{10,11... | collective-permute-start | bytes 503816 | tf_op jit(solution)/shard_map/ppermute | solution.py:465
  104.6 21.8 %all-to-all-start.1 = ((f32[16,80,128]{2,1,0:T(8,128)}), f32[16,80,128]{2,1,0:T(8,128)S(1)}, u32[]{:S(2)}, u32[]{:S(2)}) async-start(f32[16,80,128]{2,1,0:T(8,128)} %shard_map.93), calls=%async_computation.1 | async-start | bytes 1310720 | tf_op jit(solution)/shard_map/all_to_all | solution.py:460
  127.5 6.1 %collective-permute-start.30 = (f32[328,128]{1,0:T(8,128)S(1)}, f32[328,128]{1,0:T(8,128)S(1)}, u32[]{:S(2)}, u32[]{:S(2)}) collective-permute-start(f32[328,128]{1,0:T(8,128)S(1)} %shard_map.94.rest_0_.rest_8_), channel_id=1, source_target_pairs={{0,4},{1,5},{2,6},{3,7},{4,0},{5,1},{6,2},{7,3},{8,12},{9,13},{10,... | collective-permute-start | bytes 503816 | tf_op jit(solution)/shard_map/ppermute | solution.py:465
  127.6 7.1 %collective-permute-start.36 = (f32[328,128]{1,0:T(8,128)S(1)}, f32[328,128]{1,0:T(8,128)S(1)}, u32[]{:S(2)}, u32[]{:S(2)}) collective-permute-start(f32[328,128]{1,0:T(8,128)S(1)} %shard_map.94.rest_0_.rest_8_), channel_id=1, source_target_pairs={{0,12},{1,13},{2,14},{3,15},{4,8},{5,9},{6,10},{7,11},{8,4},{9,5},... | collective-permute-start | bytes 503816 | tf_op jit(solution)/shard_map/ppermute | solution.py:465
  128.1 11.2 %collective-permute-start.33 = (f32[328,128]{1,0:T(8,128)S(1)}, f32[328,128]{1,0:T(8,128)S(1)}, u32[]{:S(2)}, u32[]{:S(2)}) collective-permute-start(f32[328,128]{1,0:T(8,128)S(1)} %shard_map.94.rest_0_.rest_8_), channel_id=1, source_target_pairs={{0,2},{1,3},{2,0},{3,1},{4,6},{5,7},{6,4},{7,5},{8,10},{9,11},{10,... | collective-permute-start | bytes 503816 | tf_op jit(solution)/shard_map/ppermute | solution.py:465
  129.7 9.6 %collective-permute-start.32 = (f32[328,128]{1,0:T(8,128)S(1)}, f32[328,128]{1,0:T(8,128)S(1)}, u32[]{:S(2)}, u32[]{:S(2)}) collective-permute-start(f32[328,128]{1,0:T(8,128)S(1)} %shard_map.94.rest_0_.rest_8_), channel_id=1, source_target_pairs={{0,1},{1,0},{2,3},{3,2},{4,5},{5,4},{6,7},{7,6},{8,9},{9,8},{10,11... | collective-permute-start | bytes 503816 | tf_op jit(solution)/shard_map/ppermute | solution.py:465
  133.6 6.2 %collective-permute-start.31 = (f32[328,128]{1,0:T(8,128)S(1)}, f32[328,128]{1,0:T(8,128)S(1)}, u32[]{:S(2)}, u32[]{:S(2)}) collective-permute-start(f32[328,128]{1,0:T(8,128)S(1)} %collective-permute-done.30.rest_4_.rest_12_), channel_id=1, source_target_pairs={{0,2},{1,3},{2,0},{3,1},{4,6},{5,7},{6,4},{7,5},{8,10},{9,11},{10,... | collective-permute-start | bytes 503816 | tf_op jit(solution)/shard_map/ppermute | solution.py:465
  134.7 5.7 %collective-permute-start.39 = (f32[328,128]{1,0:T(8,128)S(1)}, f32[328,128]{1,0:T(8,128)S(1)}, u32[]{:S(2)}, u32[]{:S(2)}) collective-permute-start(f32[328,128]{1,0:T(8,128)S(1)} %collective-permute-done.36.rest_6_.rest_14_), channel_id=1, source_target_pairs={{0,4},{1,5},{2,6},{3,7},{4,0},{5,1},{6,2},{7,3},{8,12},{9,13},{10,... | collective-permute-start | bytes 503816 | tf_op jit(solution)/shard_map/ppermute | solution.py:465
  137.1 4.4 %collective-permute-start.35 = (f32[328,128]{1,0:T(8,128)S(1)}, f32[328,128]{1,0:T(8,128)S(1)}, u32[]{:S(2)}, u32[]{:S(2)}) collective-permute-start(f32[328,128]{1,0:T(8,128)S(1)} %collective-permute-done.30.rest_4_.rest_12_), channel_id=1, source_target_pairs={{0,1},{1,0},{2,3},{3,2},{4,5},{5,4},{6,7},{7,6},{8,9},{9,8},{10,11... | collective-permute-start | bytes 503816 | tf_op jit(solution)/shard_map/ppermute | solution.py:465
  139.3 2.1 %collective-permute-start.34 = (f32[328,128]{1,0:T(8,128)S(1)}, f32[328,128]{1,0:T(8,128)S(1)}, u32[]{:S(2)}, u32[]{:S(2)}) collective-permute-start(f32[328,128]{1,0:T(8,128)S(1)} %collective-permute-done.33.rest_2_.rest_10_), channel_id=1, source_target_pairs={{0,1},{1,0},{2,3},{3,2},{4,5},{5,4},{6,7},{7,6},{8,9},{9,8},{10,11... | collective-permute-start | bytes 503816 | tf_op jit(solution)/shard_map/ppermute | solution.py:465
  139.3 2.1 %collective-permute-start.37 = (f32[328,128]{1,0:T(8,128)S(1)}, f32[328,128]{1,0:T(8,128)S(1)}, u32[]{:S(2)}, u32[]{:S(2)}) collective-permute-start(f32[328,128]{1,0:T(8,128)S(1)} %collective-permute-done.36.rest_6_.rest_14_), channel_id=1, source_target_pairs={{0,1},{1,0},{2,3},{3,2},{4,5},{5,4},{6,7},{7,6},{8,9},{9,8},{10,11... | collective-permute-start | bytes 503816 | tf_op jit(solution)/shard_map/ppermute | solution.py:465
  139.8 9.6 %collective-permute-start.43 = (f32[328,128]{1,0:T(8,128)S(1)}, f32[328,128]{1,0:T(8,128)S(1)}, u32[]{:S(2)}, u32[]{:S(2)}) collective-permute-start(f32[328,128]{1,0:T(8,128)S(1)} %collective-permute-done.36.rest_6_.rest_14_), channel_id=1, source_target_pairs={{0,2},{1,3},{2,0},{3,1},{4,6},{5,7},{6,4},{7,5},{8,10},{9,11},{10,... | collective-permute-start | bytes 503816 | tf_op jit(solution)/shard_map/ppermute | solution.py:465
  140.4 9.4 %collective-permute-start.41 = (f32[328,128]{1,0:T(8,128)S(1)}, f32[328,128]{1,0:T(8,128)S(1)}, u32[]{:S(2)}, u32[]{:S(2)}) collective-permute-start(f32[328,128]{1,0:T(8,128)S(1)} %collective-permute-done.39.rest_2_), channel_id=1, source_target_pairs={{0,2},{1,3},{2,0},{3,1},{4,6},{5,7},{6,4},{7,5},{8,10},{9,11},{10,... | collective-permute-start | bytes 503816 | tf_op jit(solution)/shard_map/ppermute | solution.py:465
  146.4 4.0 %collective-permute-start.38 = (f32[328,128]{1,0:T(8,128)S(1)}, f32[328,128]{1,0:T(8,128)S(1)}, u32[]{:S(2)}, u32[]{:S(2)}) collective-permute-start(f32[328,128]{1,0:T(8,128)S(1)} %get-tuple-element.27.rest_0_), channel_id=1, source_target_pairs={{0,1},{1,0},{2,3},{3,2},{4,5},{5,4},{6,7},{7,6},{8,9},{9,8},{10,11... | collective-permute-start | bytes 503816 | tf_op jit(solution)/shard_map/ppermute | solution.py:465
  149.3 1.4 collective-permute-start.40
  149.4 1.6 collective-permute-start.44
  149.8 1.4 collective-permute-start.42
  (20 other events, 134.1 us)

commit v15 on v14

--- a/solution.py
+++ b/solution.py
@@ -92,7 +92,17 @@
             lax.fori_loop(self.ends[i], self.ends[i + 1], body, 0)
 
 
-def power_kernel(n, dpc, model_hbm, mask_ref, unused_in, out_ref, unused_out, model_ref, sems):
+def bring(pairs, sems):
+    copies = [pltpu.make_async_copy(*pair, sems.at[i]) for i, pair in enumerate(pairs)]
+    for copy in copies:
+        copy.start()
+    return copies
+
+
+def power_kernel(
+    n, dpc, model_hbm, mask_hbm, unused_in, out_ref, unused_out, mask_ref, side, model_ref, sems
+):
+    (mask_copy,) = bring([(mask_hbm, mask_ref)], side)
     fetch = Fetch(model_hbm, model_ref, sems)
     out_ref[...] = jnp.zeros_like(out_ref)
 
@@ -105,6 +115,7 @@
             out_ref[d // dpc, row, :] = jnp.sum(weight * (mr * mr + mi * mi), axis=0, keepdims=True)
         return carry
 
+    mask_copy.wait()
     fetch.each(pair)
 
 
@@ -118,9 +129,9 @@
     ref[STATIONS * dpc :, :] = jnp.zeros((TILE, 128), F32)
 
 
-def first_own_kernel(n, dpc, me_ref, *rest):
+def first_own_kernel(n, dpc, *rest):
     ins, (g_ref, onehot_ref, split, lines) = rest[:n], rest[n:]
-    me = me_ref[0]
+    me = lax.axis_index("bl")
     k, c = lax.div(me, 2), lax.rem(me, 2)
     per = STATIONS // n
     rows = per * SOURCE_COUNT
@@ -344,12 +355,14 @@
             out_ref[2 * k + 1, rows, :] = x1
 
 
-def first_pass_kernel(
-    n, dpc, me_ref, first_ref, second_ref, model_hbm, vis_ref, mask_ref, power_in, *rest
-):
-    ins, (out_ref, power_ref, model_ref, sems, hre, him, cre, cim, stack) = rest[:n], rest[n:]
+def first_pass_kernel(n, dpc, first_ref, second_ref, model_hbm, vis_hbm, mask_hbm, power_in, *rest):
+    ins, rest = rest[:n], rest[n:]
+    out_ref, power_ref, vis_ref, mask_ref, side, model_ref, sems, hre, him, cre, cim, stack = rest
+    copies = bring([(vis_hbm, vis_ref), (mask_hbm, mask_ref)], side)
     fetch = Fetch(model_hbm, model_ref, sems)
-    products_first(n, dpc, me_ref[0], first_ref, second_ref, ins, hre, him, stack)
+    products_first(n, dpc, lax.axis_index("bl"), first_ref, second_ref, ins, hre, him, stack)
+    for copy in copies:
+        copy.wait()
     chips = range(n // 2)
     power_ref[: n // 4] = power_in[...]
 
@@ -371,11 +384,15 @@
     return [jnp.bitwise_xor(lax.div(me, 2), m) for m in pairs]
 
 
-def early_kernel(n, dpc, me_ref, first_ref, second_ref, model_hbm, vis_ref, unused_in, *rest):
-    ins, (acc_ref, hre, him, unused_out, model_ref, sems) = rest[: 2 * len(NEAR)], rest[2 * len(NEAR) :]
-    me = me_ref[0]
+def early_kernel(n, dpc, first_ref, second_ref, model_hbm, vis_hbm, unused_in, *rest):
+    ins, rest = rest[: 2 * len(NEAR)], rest[2 * len(NEAR) :]
+    acc_ref, hre, him, unused_out, vis_ref, side, model_ref, sems = rest
+    me = lax.axis_index("bl")
+    (vis_copy,) = bring([(vis_hbm, vis_ref)], side)
     fetch = Fetch(model_hbm, model_ref, sems, [k * dpc for k in chips_of(me, NEAR)])
     products(dpc, me, first_ref, second_ref, ins, hre, him)
+
+    vis_copy.wait()
 
     def pair(b, carry):
         acc = vis_ref[0, b], vis_ref[1, b]
@@ -388,23 +405,26 @@
 def later_pass_kernel(
     n,
     dpc,
-    me_ref,
     first_ref,
     second_ref,
     model_hbm,
-    mask_ref,
+    mask_hbm,
     power_ref,
     acc_ref,
     near_re,
     near_im,
     *rest,
 ):
-    ins, (out_ref, model_ref, sems, hre, him, cre, cim) = rest[: 2 * len(FAR)], rest[2 * len(FAR) :]
+    ins, rest = rest[: 2 * len(FAR)], rest[2 * len(FAR) :]
+    out_ref, mask_ref, side, model_ref, sems, hre, him, cre, cim = rest
+    (mask_copy,) = bring([(mask_hbm, mask_ref)], side)
     fetch = Fetch(model_hbm, model_ref, sems)
-    me = me_ref[0]
+    me = lax.axis_index("bl")
     products(dpc, me, first_ref, second_ref, ins, hre, him)
     far = chips_of(me, FAR)
     chips = chips_of(me, NEAR) + far
+
+    mask_copy.wait()
 
     def pair(b, carry):
         acc = predict(dpc, b, (acc_ref[0, b], acc_ref[1, b]), far, model_ref, hre, him)
@@ -423,9 +443,10 @@
     write_sums(dpc, chips, cre, cim, tiles, power_ref, out_ref, False)
 
 
-def last_kernel(n, dpc, me_ref, first_ref, second_ref, model_hbm, mask_ref, acc_ref, *rest):
-    ins, (res_ref, gains_ref, model_ref, sems, hre, him) = rest[:n], rest[n:]
-    me = me_ref[0]
+def last_kernel(n, dpc, first_ref, second_ref, model_hbm, mask_hbm, acc_ref, *rest):
+    ins, (res_ref, gains_ref, mask_ref, side, model_ref, sems, hre, him) = rest[:n], rest[n:]
+    (mask_copy,) = bring([(mask_hbm, mask_ref)], side)
+    me = lax.axis_index("bl")
     fetch = Fetch(model_hbm, model_ref, sems, [k * dpc for k in chips_of(me, FAR)])
     products(dpc, me, first_ref, second_ref, ins[: 2 * len(FAR)], hre, him)
     per = STATIONS // n
@@ -438,6 +459,8 @@
                 gains_ref[0, pl.ds(at, 1), :] = parts[0][dd : dd + 1]
                 gains_ref[1, pl.ds(at, 1), :] = parts[1][dd : dd + 1]
 
+    mask_copy.wait()
+
     def pair(b, carry):
         acc = acc_ref[0, b], acc_ref[1, b]
         acc = predict(dpc, b, acc, range(len(FAR)), model_ref, hre, him)
@@ -477,23 +500,26 @@
 
 def fast_body(n, vis, model, mask, first, second, gre, gim):
     starts = (first.reshape(1, -1), second.reshape(1, -1), gre, gim)
-    model, *starts = (pltpu.with_memory_space_constraint(x, pltpu.HBM) for x in (model, *starts))
+    model, vis, mask, *starts = (
+        pltpu.with_memory_space_constraint(x, pltpu.HBM) for x in (model, vis, mask, *starts)
+    )
     dpc = SOURCE_COUNT // (n // 2)
     width = dpc * 128
     pairs, times, channels = mask.shape
-    me = lax.axis_index("bl").astype(jnp.int32).reshape(1)
     params = pltpu.CompilerParams(vmem_limit_bytes=VMEM_LIMIT)
     plane = (n // 2, ROWS * dpc + TILE, channels)
     half = (len(FAR), ROWS * dpc + TILE, channels)
     lots = n * 2 * ROWS
     mine = (STATIONS * dpc + TILE, channels)
     sems = pltpu.SemaphoreType.DMA((len(PARTS), n // 4))
+    side = pltpu.SemaphoreType.DMA((2,))
+    mask_held = [pltpu.VMEM(mask.shape, jnp.int32), side]
     held = [pltpu.VMEM(model.shape, BF16), sems]
     held_half = [pltpu.VMEM((SOURCE_COUNT // 2,) + model.shape[1:], BF16), sems]
 
     def call(kernel, args, outs, scratch=(), micros=1, aliases={}):
         def place(x):
-            if x is model or any(x is y for y in starts):
+            if any(x is y for y in (model, vis, mask, *starts)):
                 return HBM
             return SMEM if x.ndim == 1 else VMEM
 
@@ -521,22 +547,22 @@
     def powers_beside(x, got):
         nonlocal power
         outs = [shape(*half), shape(*x.shape)]
-        power, x = call(power_kernel, (model, mask, x), outs, held_half, micros=20, aliases={2: 1})
+        power, x = call(power_kernel, (model, mask, x), outs, mask_held + held_half, micros=20, aliases={2: 1})
         return x
 
     got = gather(n, piece, powers_beside)
     g, onehot = call(
         first_own_kernel,
-        (me, *got),
+        got,
         [shape(*mine), shape(STATIONS, lots, dtype=BF16)],
         [(STATIONS * TILE, channels), (n, channels)],
         micros=2,
     )
     sums, power = call(
         first_pass_kernel,
-        (me, first, second, model, vis, mask, power, *got),
-        [shape(n, (ROWS + TILE) * dpc, channels), shape(*plane)],
-        held + [plane] * 4 + [(n,) + piece.shape],
+        (first, second, model, vis, mask, power, *got),
+        [shape(n, (ROWS + TILE) * dpc, channels), pltpu.HBM(plane, F32)],
+        [vis.shape] + mask_held + held + [plane] * 4 + [(n,) + piece.shape],
         micros=9,
     )
     powers = exchange(sums)
@@ -555,9 +581,9 @@
 
         def beside(x, got):
             nonlocal near
-            args = (me, first, second, model, vis, x, *slots(got, NEAR))
+            args = (first, second, model, vis, x, *slots(got, NEAR))
             outs = [shape(*vis.shape), shape(*half), shape(*half), shape(*x.shape)]
-            *near, x = call(early_kernel, args, outs, held_half, aliases={5: 3})
+            *near, x = call(early_kernel, args, outs, [vis.shape, side] + held_half, aliases={4: 3})
             return x
 
         got = gather(n, g, beside)
@@ -574,9 +600,9 @@
         )
         (sums,) = call(
             later_pass_kernel,
-            (me, first, second, model, mask, power, *near, *got[: 2 * len(FAR)]),
+            (first, second, model, mask, power, *near, *got[: 2 * len(FAR)]),
             [shape(n, ROWS * dpc, channels)],
-            held + [half] * 2 + [plane] * 2,
+            mask_held + held + [half] * 2 + [plane] * 2,
             micros=7,
         )
         sums = exchange(sums)
@@ -589,9 +615,9 @@
     near, got = gather_near(g)
     residual, gains = call(
         last_kernel,
-        (me, first, second, model, mask, near[0], *got),
+        (first, second, model, mask, near[0], *got),
         [shape(*vis.shape), shape(2, *gre.shape)],
-        held_half + [half] * 2,
+        mask_held + held_half + [half] * 2,
         micros=4,
     )
     return gains, residual

time: 159 us -> 161 us (1.013)
  local copies, waits for them, and re-layouts: 9.45 us -> 4.66 us
  waiting for transfers between devices: 44.1 us -> 48.3 us
  Pallas kernels: 43.1 us -> 45.8 us
    unnamed x42 -> x20, local copies, waits for them, and re-layouts: 9.45 us -> 4.66 us
    all_to_all x2, waiting for transfers between devices: 32.9 us -> 36.8 us  [exchange(): return lax.all_to_all(x, 'bl', split_axis=0, concat_axis=0, tiled=True)]
    pallas_call x11, Pallas kernels: 43.1 us -> 45.8 us  [call(): pl.pallas_call(functools.partial(kernel, n, dpc), in_specs=[place(x) for...]
  transfers between devices with their start and end apart: 47 -> 47, of which waited for: 16 -> 17; matrix products, arithmetic and copies ran while one was open for 0% -> 0% of each run, Pallas kernels for 10% -> 10%
where the time goes in v15:
time: 161 us; the launch traced here: 159 us
  starting transfers between devices  58.9 us (37%)
  waiting for transfers between devices  48.3 us (30%)
  Pallas kernels  45.8 us (28%)
  local copies, waits for them, and re-layouts  4.66 us (3%)
    ppermute x45, starting transfers between devices, send(): return lax.ppermute(x, 'bl', [(i, i ^ o) for i in range(n)])  47.8 us
    pallas_call x11, Pallas kernels, call(): pl.pallas_call(functools.partial(kernel, n, dpc), in_specs=[place(x) for...  45.8 us
    all_to_all x2, waiting for transfers between devices, exchange(): return lax.all_to_all(x, 'bl', split_axis=0, concat_axis=0, tiled=True)  36.8 us
    ppermute x45, waiting for transfers between devices, send(): return lax.ppermute(x, 'bl', [(i, i ^ o) for i in range(n)])  11.4 us
    all_to_all x2, starting transfers between devices, exchange(): return lax.all_to_all(x, 'bl', split_axis=0, concat_axis=0, tiled=True)  11.2 us
    unnamed x20, local copies, waits for them, and re-layouts  4.66 us
  transfers between devices with their start and end apart: 47, of which 17 were waited for; matrix products, arithmetic and copies ran while one was open for 0% of the time, Pallas kernels for 10%

profile of v15, /device:TPU:9, one launch (start us, length us, event | category | flops | bytes accessed | tf_op | source)
XLA Modules:
  0.0 158.7 jit_solution(13874460003445458600)
XLA Ops:
  0.7 1.1 shard_map.86.rest_0_
  1.8 2.6 %collective-permute-start.7 = (f32[328,128]{1,0:T(8,128)S(1)}, f32[328,128]{1,0:T(8,128)S(1)}, u32[]{:S(2)}, u32[]{:S(2)}) collective-permute-start(f32[328,128]{1,0:T(8,128)S(1)} %shard_map.86.rest_0_), channel_id=1, source_target_pairs={{0,12},{1,13},{2,14},{3,15},{4,8},{5,9},{6,10},{7,11},{8,4},{9,5},... | collective-permute-start | bytes 503816 | tf_op jit(solution)/shard_map/ppermute | solution.py:488
  4.4 1.2 collective-permute-start.1
  5.6 1.4 collective-permute-done.3.rest_4_
  7.0 1.2 collective-permute-start.5
  8.2 4.6 %collective-permute-start.8 = (f32[328,128]{1,0:T(8,128)S(1)}, f32[328,128]{1,0:T(8,128)S(1)}, u32[]{:S(2)}, u32[]{:S(2)}) collective-permute-start(f32[328,128]{1,0:T(8,128)S(1)} %collective-permute-done.7.rest_12_), channel_id=1, source_target_pairs={{0,4},{1,5},{2,6},{3,7},{4,0},{5,1},{6,2},{7,3},{8,12},{9,13},{10,... | collective-permute-start | bytes 503816 | tf_op jit(solution)/shard_map/ppermute | solution.py:488
  12.8 1.9 %collective-permute-start = (f32[328,128]{1,0:T(8,128)S(1)}, f32[328,128]{1,0:T(8,128)S(1)}, u32[]{:S(2)}, u32[]{:S(2)}) collective-permute-start(f32[328,128]{1,0:T(8,128)S(1)} %shard_map.86.rest_0_), channel_id=1, source_target_pairs={{0,1},{1,0},{2,3},{3,2},{4,5},{5,4},{6,7},{7,6},{8,9},{9,8},{10,11... | collective-permute-start | bytes 503816 | tf_op jit(solution)/shard_map/ppermute | solution.py:488
  15.2 1.2 collective-permute-start.13
  16.8 3.5 %shard_map.87 = (f32[4,88,128]{2,1,0:T(8,128)S(1)}, f32[328,128]{1,0:T(8,128)S(1)}) custom-call(bf16[40,2,15,32,128]{4,3,2,1,0:T(8,128)(2,1)} %model_hbm.11, s32[15,32,128]{2,1,0:T(8,128)} %mask_hbm.7, f32[328,128]{1,0:T(8,128)S(1)} %collective-permute-done.5.unused_in), custom_call_target="tpu_custom_call", output_to_operand_aliasing={{1}: (2, {})} | custom-call | bytes 73800000 | tf_op jit(solution)/shard_map/pallas_call | solution.py:526
  20.3 3.4 %collective-permute-start.12 = (f32[328,128]{1,0:T(8,128)S(1)}, f32[328,128]{1,0:T(8,128)S(1)}, u32[]{:S(2)}, u32[]{:S(2)}) collective-permute-start(f32[328,128]{1,0:T(8,128)S(1)} %collective-permute-done.7.rest_12_), channel_id=1, source_target_pairs={{0,1},{1,0},{2,3},{3,2},{4,5},{5,4},{6,7},{7,6},{8,9},{9,8},{10,11... | collective-permute-start | bytes 503816 | tf_op jit(solution)/shard_map/ppermute | solution.py:488
  24.7 0.8 collective-permute-start.11
  25.6 0.9 collective-permute-done.11.rest_11_
  26.5 10.9 %shard_map.89 = (f32[16,120,128]{2,1,0:T(8,128)}, f32[8,88,128]{2,1,0:T(8,128)}) custom-call(s32[15]{0:T(128)S(1)} %copy-done.8, s32[15]{0:T(128)S(1)} %copy-done.9, bf16[40,2,15,32,128]{4,3,2,1,0:T(8,128)(2,1)} %model_hbm.11, f32[2,15,32,128]{3,2,1,0:T(8,128)} %vis_hbm.5, s32[15,32,128]{2,1,0:T(8,128)} %mask_hbm.7, ...), custom_call_target="tpu_custom_call" | custom-call | bytes 33210000 | tf_op jit(solution)/shard_map/pallas_call | solution.py:526
  37.4 0.7 copy-done
  38.1 5.4 %all-to-all-start = ((f32[16,120,128]{2,1,0:T(8,128)}), f32[16,120,128]{2,1,0:T(8,128)S(1)}, u32[]{:S(2)}, u32[]{:S(2)}) async-start(f32[16,120,128]{2,1,0:T(8,128)} %get-tuple-element.20), calls=%async_computation | async-start | bytes 1966080 | tf_op jit(solution)/shard_map/all_to_all | solution.py:483
  43.5 0.9 copy-done.1
  44.7 0.6 copy-done.2
  45.4 0.7 copy-done.6
  46.0 21.0 %all-to-all-done.sums = f32[16,120,128]{2,1,0:T(8,128)S(1)} async-done(((f32[16,120,128]{2,1,0:T(8,128)}), f32[16,120,128]{2,1,0:T(8,128)S(1)}, u32[]{:S(2)}, u32[]{:S(2)}) %all-to-all-start) | async-done | bytes 983072 | tf_op jit(solution)/shard_map/all_to_all | solution.py:483
  67.0 0.8 copy-done.3
  67.9 0.9 copy-done.7
  68.8 1.6 shard_map.90.g_ref.rest_0_.g_in
  70.5 1.0 collective-permute-start.21
  71.5 1.6 collective-permute-start.18
  73.0 1.0 collective-permute-start.17
  74.1 2.5 %collective-permute-done.15.rest_4_ = f32[328,128]{1,0:T(8,128)S(1)} collective-permute-done((f32[328,128]{1,0:T(8,128)S(1)}, f32[328,128]{1,0:T(8,128)S(1)}, u32[]{:S(2)}, u32[]{:S(2)}) %collective-permute-start.15) | collective-permute-done | bytes 167968 | tf_op jit(solution)/shard_map/ppermute | solution.py:488
  76.6 0.7 collective-permute-start.16
  77.3 3.5 %collective-permute-start.24 = (f32[328,128]{1,0:T(8,128)S(1)}, f32[328,128]{1,0:T(8,128)S(1)}, u32[]{:S(2)}, u32[]{:S(2)}) collective-permute-start(f32[328,128]{1,0:T(8,128)S(1)} %collective-permute-done.21.rest_6_), channel_id=1, source_target_pairs={{0,4},{1,5},{2,6},{3,7},{4,0},{5,1},{6,2},{7,3},{8,12},{9,13},{10,... | collective-permute-start | bytes 503816 | tf_op jit(solution)/shard_map/ppermute | solution.py:488
  80.8 2.1 %collective-permute-start.20 = (f32[328,128]{1,0:T(8,128)S(1)}, f32[328,128]{1,0:T(8,128)S(1)}, u32[]{:S(2)}, u32[]{:S(2)}) collective-permute-start(f32[328,128]{1,0:T(8,128)S(1)} %collective-permute-done.15.rest_4_), channel_id=1, source_target_pairs={{0,1},{1,0},{2,3},{3,2},{4,5},{5,4},{6,7},{7,6},{8,9},{9,8},{10,11... | collective-permute-start | bytes 503816 | tf_op jit(solution)/shard_map/ppermute | solution.py:488
  83.7 1.2 collective-permute-start.26
  84.9 5.3 %shard_map.92 = (f32[2,15,32,128]{3,2,1,0:T(8,128)S(1)}, f32[4,88,128]{2,1,0:T(8,128)S(1)}, f32[4,88,128]{2,1,0:T(8,128)S(1)}, f32[328,128]{1,0:T(8,128)S(1)}) custom-call(s32[15]{0:T(128)S(1)} %copy-done.8, s32[15]{0:T(128)S(1)} %copy-done.9, bf16[40,2,15,32,128]{4,3,2,1,0:T(8,128)(2,1)} %model_hbm.11, ...), custom_call_target="tpu_custom_call", output_to_operand_aliasing={{3}: (4, {})} | custom-call | bytes 3690000 | tf_op jit(solution)/shard_map/pallas_call | solution.py:526
  90.2 2.8 %collective-permute-start.23 = (f32[328,128]{1,0:T(8,128)S(1)}, f32[328,128]{1,0:T(8,128)S(1)}, u32[]{:S(2)}, u32[]{:S(2)}) collective-permute-start(f32[328,128]{1,0:T(8,128)S(1)} %get-tuple-element.25.rest_0_), channel_id=1, source_target_pairs={{0,1},{1,0},{2,3},{3,2},{4,5},{5,4},{6,7},{7,6},{8,9},{9,8},{10,11... | collective-permute-start | bytes 503816 | tf_op jit(solution)/shard_map/ppermute | solution.py:488
  94.9 9.3 %shard_map.93 = f32[16,80,128]{2,1,0:T(8,128)} custom-call(s32[15]{0:T(128)S(1)} %copy-done.8, s32[15]{0:T(128)S(1)} %copy-done.9, bf16[40,2,15,32,128]{4,3,2,1,0:T(8,128)(2,1)} %model_hbm.11, s32[15,32,128]{2,1,0:T(8,128)} %mask_hbm.7, f32[8,88,128]{2,1,0:T(8,128)S(1)} %copy-done.5, f32[2,15,32,128]{3,2,1,0:T(8,128)S(1)} %get-tuple-element.22.acc_ref, ...), custom_call_target="tpu_custom_call" | custom-call | bytes 25830000 | tf_op jit(solution)/shard_map/pallas_call | solution.py:526
  104.2 5.7 %all-to-all-start.1 = ((f32[16,80,128]{2,1,0:T(8,128)}), f32[16,80,128]{2,1,0:T(8,128)S(1)}, u32[]{:S(2)}, u32[]{:S(2)}) async-start(f32[16,80,128]{2,1,0:T(8,128)} %shard_map.93), calls=%async_computation.1 | async-start | bytes 1310720 | tf_op jit(solution)/shard_map/all_to_all | solution.py:483
  110.0 1.1 shard_map.91.den_ref
  111.0 15.8 %all-to-all-done.1.sums = f32[16,80,128]{2,1,0:T(8,128)S(1)} async-done(((f32[16,80,128]{2,1,0:T(8,128)}), f32[16,80,128]{2,1,0:T(8,128)S(1)}, u32[]{:S(2)}, u32[]{:S(2)}) %all-to-all-start.1) | async-done | bytes 655392 | tf_op jit(solution)/shard_map/all_to_all | solution.py:483
  126.8 1.0 shard_map.94.rest_0_.rest_8_
  128.5 1.6 %collective-permute-start.33 = (f32[328,128]{1,0:T(8,128)S(1)}, f32[328,128]{1,0:T(8,128)S(1)}, u32[]{:S(2)}, u32[]{:S(2)}) collective-permute-start(f32[328,128]{1,0:T(8,128)S(1)} %shard_map.94.rest_0_.rest_8_), channel_id=1, source_target_pairs={{0,2},{1,3},{2,0},{3,1},{4,6},{5,7},{6,4},{7,5},{8,10},{9,11},{10,... | collective-permute-start | bytes 503816 | tf_op jit(solution)/shard_map/ppermute | solution.py:488
  130.1 1.1 collective-permute-start.32
  131.2 2.8 %collective-permute-done.30.rest_4_.rest_12_ = f32[328,128]{1,0:T(8,128)S(1)} collective-permute-done((f32[328,128]{1,0:T(8,128)S(1)}, f32[328,128]{1,0:T(8,128)S(1)}, u32[]{:S(2)}, u32[]{:S(2)}) %collective-permute-start.30) | collective-permute-done | bytes 167968 | tf_op jit(solution)/shard_map/ppermute | solution.py:488
  134.4 0.7 collective-permute-done.36.rest_6_.rest_14_
  135.1 2.4 %collective-permute-start.39 = (f32[328,128]{1,0:T(8,128)S(1)}, f32[328,128]{1,0:T(8,128)S(1)}, u32[]{:S(2)}, u32[]{:S(2)}) collective-permute-start(f32[328,128]{1,0:T(8,128)S(1)} %collective-permute-done.36.rest_6_.rest_14_), channel_id=1, source_target_pairs={{0,4},{1,5},{2,6},{3,7},{4,0},{5,1},{6,2},{7,3},{8,12},{9,13},{10,... | collective-permute-start | bytes 503816 | tf_op jit(solution)/shard_map/ppermute | solution.py:488
  137.5 2.2 %collective-permute-start.35 = (f32[328,128]{1,0:T(8,128)S(1)}, f32[328,128]{1,0:T(8,128)S(1)}, u32[]{:S(2)}, u32[]{:S(2)}) collective-permute-start(f32[328,128]{1,0:T(8,128)S(1)} %collective-permute-done.30.rest_4_.rest_12_), channel_id=1, source_target_pairs={{0,1},{1,0},{2,3},{3,2},{4,5},{5,4},{6,7},{7,6},{8,9},{9,8},{10,11... | collective-permute-start | bytes 503816 | tf_op jit(solution)/shard_map/ppermute | solution.py:488
  140.2 0.6 collective-permute-start.43
  140.8 1.0 collective-permute-start.41
  141.8 5.9 %shard_map.95 = (f32[2,15,32,128]{3,2,1,0:T(8,128)S(1)}, f32[4,88,128]{2,1,0:T(8,128)}, f32[4,88,128]{2,1,0:T(8,128)}, f32[328,128]{1,0:T(8,128)S(1)}) custom-call(s32[15]{0:T(128)S(1)} %copy-done.8, s32[15]{0:T(128)S(1)} %copy-done.9, bf16[40,2,15,32,128]{4,3,2,1,0:T(8,128)(2,1)} %model_hbm.11, ...), custom_call_target="tpu_custom_call", output_to_operand_aliasing={{3}: (4, {})} | custom-call | bytes 3690000 | tf_op jit(solution)/shard_map/pallas_call | solution.py:526
  147.7 3.0 %collective-permute-start.38 = (f32[328,128]{1,0:T(8,128)S(1)}, f32[328,128]{1,0:T(8,128)S(1)}, u32[]{:S(2)}, u32[]{:S(2)}) collective-permute-start(f32[328,128]{1,0:T(8,128)S(1)} %get-tuple-element.27.rest_0_), channel_id=1, source_target_pairs={{0,1},{1,0},{2,3},{3,2},{4,5},{5,4},{6,7},{7,6},{8,9},{9,8},{10,11... | collective-permute-start | bytes 503816 | tf_op jit(solution)/shard_map/ppermute | solution.py:488
  152.6 6.0 %shard_map.96 = (f32[2,15,32,128]{3,2,1,0:T(8,128)}, f32[2,160,128]{2,1,0:T(8,128)}) custom-call(s32[15]{0:T(128)S(1)} %copy-done.8, s32[15]{0:T(128)S(1)} %copy-done.9, bf16[40,2,15,32,128]{4,3,2,1,0:T(8,128)(2,1)} %model_hbm.11, s32[15,32,128]{2,1,0:T(8,128)} %mask_hbm.7, f32[2,15,32,128]{3,2,1,0:T(8,128)S(1)} %get-tuple-element.26.acc_ref, ...), custom_call_target="tpu_custom_call" | custom-call | bytes 14760000 | tf_op jit(solution)/shard_map/pallas_call | solution.py:526
  (77 shorter events, 8.6 us)
Async XLA Ops:
  1.7 5.2 %collective-permute-start.3 = (f32[328,128]{1,0:T(8,128)S(1)}, f32[328,128]{1,0:T(8,128)S(1)}, u32[]{:S(2)}, u32[]{:S(2)}) collective-permute-start(f32[328,128]{1,0:T(8,128)S(1)} %shard_map.86.rest_0_), channel_id=1, source_target_pairs={{0,4},{1,5},{2,6},{3,7},{4,0},{5,1},{6,2},{7,3},{8,12},{9,13},{10,... | collective-permute-start | bytes 503816 | tf_op jit(solution)/shard_map/ppermute | solution.py:488
  1.8 6.4 %collective-permute-start.7 = (f32[328,128]{1,0:T(8,128)S(1)}, f32[328,128]{1,0:T(8,128)S(1)}, u32[]{:S(2)}, u32[]{:S(2)}) collective-permute-start(f32[328,128]{1,0:T(8,128)S(1)} %shard_map.86.rest_0_), channel_id=1, source_target_pairs={{0,12},{1,13},{2,14},{3,15},{4,8},{5,9},{6,10},{7,11},{8,4},{9,5},... | collective-permute-start | bytes 503816 | tf_op jit(solution)/shard_map/ppermute | solution.py:488
  4.4 10.3 %collective-permute-start.1 = (f32[328,128]{1,0:T(8,128)S(1)}, f32[328,128]{1,0:T(8,128)S(1)}, u32[]{:S(2)}, u32[]{:S(2)}) collective-permute-start(f32[328,128]{1,0:T(8,128)S(1)} %shard_map.86.rest_0_), channel_id=1, source_target_pairs={{0,2},{1,3},{2,0},{3,1},{4,6},{5,7},{6,4},{7,5},{8,10},{9,11},{10,... | collective-permute-start | bytes 503816 | tf_op jit(solution)/shard_map/ppermute | solution.py:488
  7.0 8.2 %collective-permute-start.5 = (f32[328,128]{1,0:T(8,128)S(1)}, f32[328,128]{1,0:T(8,128)S(1)}, u32[]{:S(2)}, u32[]{:S(2)}) collective-permute-start(f32[328,128]{1,0:T(8,128)S(1)} %collective-permute-done.3.rest_4_), channel_id=1, source_target_pairs={{0,2},{1,3},{2,0},{3,1},{4,6},{5,7},{6,4},{7,5},{8,10},{9,11},{10,... | collective-permute-start | bytes 503816 | tf_op jit(solution)/shard_map/ppermute | solution.py:488
  8.2 8.2 %collective-permute-start.8 = (f32[328,128]{1,0:T(8,128)S(1)}, f32[328,128]{1,0:T(8,128)S(1)}, u32[]{:S(2)}, u32[]{:S(2)}) collective-permute-start(f32[328,128]{1,0:T(8,128)S(1)} %collective-permute-done.7.rest_12_), channel_id=1, source_target_pairs={{0,4},{1,5},{2,6},{3,7},{4,0},{5,1},{6,2},{7,3},{8,12},{9,13},{10,... | collective-permute-start | bytes 503816 | tf_op jit(solution)/shard_map/ppermute | solution.py:488
  12.8 7.5 %collective-permute-start = (f32[328,128]{1,0:T(8,128)S(1)}, f32[328,128]{1,0:T(8,128)S(1)}, u32[]{:S(2)}, u32[]{:S(2)}) collective-permute-start(f32[328,128]{1,0:T(8,128)S(1)} %shard_map.86.rest_0_), channel_id=1, source_target_pairs={{0,1},{1,0},{2,3},{3,2},{4,5},{5,4},{6,7},{7,6},{8,9},{9,8},{10,11... | collective-permute-start | bytes 503816 | tf_op jit(solution)/shard_map/ppermute | solution.py:488
  14.7 9.0 %collective-permute-start.2 = (f32[328,128]{1,0:T(8,128)S(1)}, f32[328,128]{1,0:T(8,128)S(1)}, u32[]{:S(2)}, u32[]{:S(2)}) collective-permute-start(f32[328,128]{1,0:T(8,128)S(1)} %collective-permute-done.1.rest_2_), channel_id=1, source_target_pairs={{0,1},{1,0},{2,3},{3,2},{4,5},{5,4},{6,7},{7,6},{8,9},{9,8},{10,11... | collective-permute-start | bytes 503816 | tf_op jit(solution)/shard_map/ppermute | solution.py:488
  14.7 9.1 %collective-permute-start.4 = (f32[328,128]{1,0:T(8,128)S(1)}, f32[328,128]{1,0:T(8,128)S(1)}, u32[]{:S(2)}, u32[]{:S(2)}) collective-permute-start(f32[328,128]{1,0:T(8,128)S(1)} %collective-permute-done.3.rest_4_), channel_id=1, source_target_pairs={{0,1},{1,0},{2,3},{3,2},{4,5},{5,4},{6,7},{7,6},{8,9},{9,8},{10,11... | collective-permute-start | bytes 503816 | tf_op jit(solution)/shard_map/ppermute | solution.py:488
  15.2 9.0 %collective-permute-start.13 = (f32[328,128]{1,0:T(8,128)S(1)}, f32[328,128]{1,0:T(8,128)S(1)}, u32[]{:S(2)}, u32[]{:S(2)}) collective-permute-start(f32[328,128]{1,0:T(8,128)S(1)} %collective-permute-done.7.rest_12_), channel_id=1, source_target_pairs={{0,2},{1,3},{2,0},{3,1},{4,6},{5,7},{6,4},{7,5},{8,10},{9,11},{10,... | collective-permute-start | bytes 503816 | tf_op jit(solution)/shard_map/ppermute | solution.py:488
  16.4 8.3 %collective-permute-start.10 = (f32[328,128]{1,0:T(8,128)S(1)}, f32[328,128]{1,0:T(8,128)S(1)}, u32[]{:S(2)}, u32[]{:S(2)}) collective-permute-start(f32[328,128]{1,0:T(8,128)S(1)} %collective-permute-done.8.rest_8_), channel_id=1, source_target_pairs={{0,2},{1,3},{2,0},{3,1},{4,6},{5,7},{6,4},{7,5},{8,10},{9,11},{10,... | collective-permute-start | bytes 503816 | tf_op jit(solution)/shard_map/ppermute | solution.py:488
  20.3 5.2 %collective-permute-start.12 = (f32[328,128]{1,0:T(8,128)S(1)}, f32[328,128]{1,0:T(8,128)S(1)}, u32[]{:S(2)}, u32[]{:S(2)}) collective-permute-start(f32[328,128]{1,0:T(8,128)S(1)} %collective-permute-done.7.rest_12_), channel_id=1, source_target_pairs={{0,1},{1,0},{2,3},{3,2},{4,5},{5,4},{6,7},{7,6},{8,9},{9,8},{10,11... | collective-permute-start | bytes 503816 | tf_op jit(solution)/shard_map/ppermute | solution.py:488
  23.7 1.8 %collective-permute-start.6 = (f32[328,128]{1,0:T(8,128)S(1)}, f32[328,128]{1,0:T(8,128)S(1)}, u32[]{:S(2)}, u32[]{:S(2)}) collective-permute-start(f32[328,128]{1,0:T(8,128)S(1)} %get-tuple-element.16.rest_6_), channel_id=1, source_target_pairs={{0,1},{1,0},{2,3},{3,2},{4,5},{5,4},{6,7},{7,6},{8,9},{9,8},{10,11... | collective-permute-start | bytes 503816 | tf_op jit(solution)/shard_map/ppermute | solution.py:488
  23.8 1.7 %collective-permute-start.9 = (f32[328,128]{1,0:T(8,128)S(1)}, f32[328,128]{1,0:T(8,128)S(1)}, u32[]{:S(2)}, u32[]{:S(2)}) collective-permute-start(f32[328,128]{1,0:T(8,128)S(1)} %collective-permute-done.8.rest_8_), channel_id=1, source_target_pairs={{0,1},{1,0},{2,3},{3,2},{4,5},{5,4},{6,7},{7,6},{8,9},{9,8},{10,11... | collective-permute-start | bytes 503816 | tf_op jit(solution)/shard_map/ppermute | solution.py:488
  24.2 1.4 collective-permute-start.14
  24.7 1.8 %collective-permute-start.11 = (f32[328,128]{1,0:T(8,128)S(1)}, f32[328,128]{1,0:T(8,128)S(1)}, u32[]{:S(2)}, u32[]{:S(2)}) collective-permute-start(f32[328,128]{1,0:T(8,128)S(1)} %collective-permute-done.10.rest_10_), channel_id=1, source_target_pairs={{0,1},{1,0},{2,3},{3,2},{4,5},{5,4},{6,7},{7,6},{8,9},{9,8},{10,11... | collective-permute-start | bytes 503816 | tf_op jit(solution)/shard_map/ppermute | solution.py:488
  38.1 28.9 %all-to-all-start = ((f32[16,120,128]{2,1,0:T(8,128)}), f32[16,120,128]{2,1,0:T(8,128)S(1)}, u32[]{:S(2)}, u32[]{:S(2)}) async-start(f32[16,120,128]{2,1,0:T(8,128)} %get-tuple-element.20), calls=%async_computation | async-start | bytes 1966080 | tf_op jit(solution)/shard_map/all_to_all | solution.py:483
  68.8 26.1 %copy-start.5 = (f32[8,88,128]{2,1,0:T(8,128)S(1)}, f32[8,88,128]{2,1,0:T(8,128)}, u32[]{:S(2)}) copy-start(f32[8,88,128]{2,1,0:T(8,128)} %get-tuple-element.21.power_ref) | copy-start | bytes 1081348
  70.4 6.2 %collective-permute-start.15 = (f32[328,128]{1,0:T(8,128)S(1)}, f32[328,128]{1,0:T(8,128)S(1)}, u32[]{:S(2)}, u32[]{:S(2)}) collective-permute-start(f32[328,128]{1,0:T(8,128)S(1)} %shard_map.90.g_ref.rest_0_.g_in), channel_id=1, source_target_pairs={{0,4},{1,5},{2,6},{3,7},{4,0},{5,1},{6,2},{7,3},{8,12},{9,13},{10,... | collective-permute-start | bytes 503816 | tf_op jit(solution)/shard_map/ppermute | solution.py:488
  70.5 6.8 %collective-permute-start.21 = (f32[328,128]{1,0:T(8,128)S(1)}, f32[328,128]{1,0:T(8,128)S(1)}, u32[]{:S(2)}, u32[]{:S(2)}) collective-permute-start(f32[328,128]{1,0:T(8,128)S(1)} %shard_map.90.g_ref.rest_0_.g_in), channel_id=1, source_target_pairs={{0,12},{1,13},{2,14},{3,15},{4,8},{5,9},{6,10},{7,11},{8,4},{9,5},... | collective-permute-start | bytes 503816 | tf_op jit(solution)/shard_map/ppermute | solution.py:488
  71.5 11.4 %collective-permute-start.18 = (f32[328,128]{1,0:T(8,128)S(1)}, f32[328,128]{1,0:T(8,128)S(1)}, u32[]{:S(2)}, u32[]{:S(2)}) collective-permute-start(f32[328,128]{1,0:T(8,128)S(1)} %shard_map.90.g_ref.rest_0_.g_in), channel_id=1, source_target_pairs={{0,2},{1,3},{2,0},{3,1},{4,6},{5,7},{6,4},{7,5},{8,10},{9,11},{10,... | collective-permute-start | bytes 503816 | tf_op jit(solution)/shard_map/ppermute | solution.py:488
  73.0 9.8 %collective-permute-start.17 = (f32[328,128]{1,0:T(8,128)S(1)}, f32[328,128]{1,0:T(8,128)S(1)}, u32[]{:S(2)}, u32[]{:S(2)}) collective-permute-start(f32[328,128]{1,0:T(8,128)S(1)} %shard_map.90.g_ref.rest_0_.g_in), channel_id=1, source_target_pairs={{0,1},{1,0},{2,3},{3,2},{4,5},{5,4},{6,7},{7,6},{8,9},{9,8},{10,11... | collective-permute-start | bytes 503816 | tf_op jit(solution)/shard_map/ppermute | solution.py:488
  76.6 6.8 %collective-permute-start.16 = (f32[328,128]{1,0:T(8,128)S(1)}, f32[328,128]{1,0:T(8,128)S(1)}, u32[]{:S(2)}, u32[]{:S(2)}) collective-permute-start(f32[328,128]{1,0:T(8,128)S(1)} %collective-permute-done.15.rest_4_), channel_id=1, source_target_pairs={{0,2},{1,3},{2,0},{3,1},{4,6},{5,7},{6,4},{7,5},{8,10},{9,11},{10,... | collective-permute-start | bytes 503816 | tf_op jit(solution)/shard_map/ppermute | solution.py:488
  77.3 6.4 %collective-permute-start.24 = (f32[328,128]{1,0:T(8,128)S(1)}, f32[328,128]{1,0:T(8,128)S(1)}, u32[]{:S(2)}, u32[]{:S(2)}) collective-permute-start(f32[328,128]{1,0:T(8,128)S(1)} %collective-permute-done.21.rest_6_), channel_id=1, source_target_pairs={{0,4},{1,5},{2,6},{3,7},{4,0},{5,1},{6,2},{7,3},{8,12},{9,13},{10,... | collective-permute-start | bytes 503816 | tf_op jit(solution)/shard_map/ppermute | solution.py:488
  80.8 4.1 %collective-permute-start.20 = (f32[328,128]{1,0:T(8,128)S(1)}, f32[328,128]{1,0:T(8,128)S(1)}, u32[]{:S(2)}, u32[]{:S(2)}) collective-permute-start(f32[328,128]{1,0:T(8,128)S(1)} %collective-permute-done.15.rest_4_), channel_id=1, source_target_pairs={{0,1},{1,0},{2,3},{3,2},{4,5},{5,4},{6,7},{7,6},{8,9},{9,8},{10,11... | collective-permute-start | bytes 503816 | tf_op jit(solution)/shard_map/ppermute | solution.py:488
  82.9 2.0 %collective-permute-start.19 = (f32[328,128]{1,0:T(8,128)S(1)}, f32[328,128]{1,0:T(8,128)S(1)}, u32[]{:S(2)}, u32[]{:S(2)}) collective-permute-start(f32[328,128]{1,0:T(8,128)S(1)} %collective-permute-done.18.rest_2_), channel_id=1, source_target_pairs={{0,1},{1,0},{2,3},{3,2},{4,5},{5,4},{6,7},{7,6},{8,9},{9,8},{10,11... | collective-permute-start | bytes 503816 | tf_op jit(solution)/shard_map/ppermute | solution.py:488
  82.9 2.0 %collective-permute-start.22 = (f32[328,128]{1,0:T(8,128)S(1)}, f32[328,128]{1,0:T(8,128)S(1)}, u32[]{:S(2)}, u32[]{:S(2)}) collective-permute-start(f32[328,128]{1,0:T(8,128)S(1)} %collective-permute-done.21.rest_6_), channel_id=1, source_target_pairs={{0,1},{1,0},{2,3},{3,2},{4,5},{5,4},{6,7},{7,6},{8,9},{9,8},{10,11... | collective-permute-start | bytes 503816 | tf_op jit(solution)/shard_map/ppermute | solution.py:488
  83.4 9.7 %collective-permute-start.28 = (f32[328,128]{1,0:T(8,128)S(1)}, f32[328,128]{1,0:T(8,128)S(1)}, u32[]{:S(2)}, u32[]{:S(2)}) collective-permute-start(f32[328,128]{1,0:T(8,128)S(1)} %collective-permute-done.21.rest_6_), channel_id=1, source_target_pairs={{0,2},{1,3},{2,0},{3,1},{4,6},{5,7},{6,4},{7,5},{8,10},{9,11},{10,... | collective-permute-start | bytes 503816 | tf_op jit(solution)/shard_map/ppermute | solution.py:488
  83.7 9.8 %collective-permute-start.26 = (f32[328,128]{1,0:T(8,128)S(1)}, f32[328,128]{1,0:T(8,128)S(1)}, u32[]{:S(2)}, u32[]{:S(2)}) collective-permute-start(f32[328,128]{1,0:T(8,128)S(1)} %collective-permute-done.24.rest_2_), channel_id=1, source_target_pairs={{0,2},{1,3},{2,0},{3,1},{4,6},{5,7},{6,4},{7,5},{8,10},{9,11},{10,... | collective-permute-start | bytes 503816 | tf_op jit(solution)/shard_map/ppermute | solution.py:488
  90.2 3.8 %collective-permute-start.23 = (f32[328,128]{1,0:T(8,128)S(1)}, f32[328,128]{1,0:T(8,128)S(1)}, u32[]{:S(2)}, u32[]{:S(2)}) collective-permute-start(f32[328,128]{1,0:T(8,128)S(1)} %get-tuple-element.25.rest_0_), channel_id=1, source_target_pairs={{0,1},{1,0},{2,3},{3,2},{4,5},{5,4},{6,7},{7,6},{8,9},{9,8},{10,11... | collective-permute-start | bytes 503816 | tf_op jit(solution)/shard_map/ppermute | solution.py:488
  93.0 1.4 collective-permute-start.25
  93.1 1.6 collective-permute-start.29
  93.5 1.4 collective-permute-start.27
  104.2 22.6 %all-to-all-start.1 = ((f32[16,80,128]{2,1,0:T(8,128)}), f32[16,80,128]{2,1,0:T(8,128)S(1)}, u32[]{:S(2)}, u32[]{:S(2)}) async-start(f32[16,80,128]{2,1,0:T(8,128)} %shard_map.93), calls=%async_computation.1 | async-start | bytes 1310720 | tf_op jit(solution)/shard_map/all_to_all | solution.py:483
  127.9 6.1 %collective-permute-start.30 = (f32[328,128]{1,0:T(8,128)S(1)}, f32[328,128]{1,0:T(8,128)S(1)}, u32[]{:S(2)}, u32[]{:S(2)}) collective-permute-start(f32[328,128]{1,0:T(8,128)S(1)} %shard_map.94.rest_0_.rest_8_), channel_id=1, source_target_pairs={{0,4},{1,5},{2,6},{3,7},{4,0},{5,1},{6,2},{7,3},{8,12},{9,13},{10,... | collective-permute-start | bytes 503816 | tf_op jit(solution)/shard_map/ppermute | solution.py:488
  128.0 7.1 %collective-permute-start.36 = (f32[328,128]{1,0:T(8,128)S(1)}, f32[328,128]{1,0:T(8,128)S(1)}, u32[]{:S(2)}, u32[]{:S(2)}) collective-permute-start(f32[328,128]{1,0:T(8,128)S(1)} %shard_map.94.rest_0_.rest_8_), channel_id=1, source_target_pairs={{0,12},{1,13},{2,14},{3,15},{4,8},{5,9},{6,10},{7,11},{8,4},{9,5},... | collective-permute-start | bytes 503816 | tf_op jit(solution)/shard_map/ppermute | solution.py:488
  128.5 11.2 %collective-permute-start.33 = (f32[328,128]{1,0:T(8,128)S(1)}, f32[328,128]{1,0:T(8,128)S(1)}, u32[]{:S(2)}, u32[]{:S(2)}) collective-permute-start(f32[328,128]{1,0:T(8,128)S(1)} %shard_map.94.rest_0_.rest_8_), channel_id=1, source_target_pairs={{0,2},{1,3},{2,0},{3,1},{4,6},{5,7},{6,4},{7,5},{8,10},{9,11},{10,... | collective-permute-start | bytes 503816 | tf_op jit(solution)/shard_map/ppermute | solution.py:488
  130.1 9.6 %collective-permute-start.32 = (f32[328,128]{1,0:T(8,128)S(1)}, f32[328,128]{1,0:T(8,128)S(1)}, u32[]{:S(2)}, u32[]{:S(2)}) collective-permute-start(f32[328,128]{1,0:T(8,128)S(1)} %shard_map.94.rest_0_.rest_8_), channel_id=1, source_target_pairs={{0,1},{1,0},{2,3},{3,2},{4,5},{5,4},{6,7},{7,6},{8,9},{9,8},{10,11... | collective-permute-start | bytes 503816 | tf_op jit(solution)/shard_map/ppermute | solution.py:488
  134.0 6.2 %collective-permute-start.31 = (f32[328,128]{1,0:T(8,128)S(1)}, f32[328,128]{1,0:T(8,128)S(1)}, u32[]{:S(2)}, u32[]{:S(2)}) collective-permute-start(f32[328,128]{1,0:T(8,128)S(1)} %collective-permute-done.30.rest_4_.rest_12_), channel_id=1, source_target_pairs={{0,2},{1,3},{2,0},{3,1},{4,6},{5,7},{6,4},{7,5},{8,10},{9,11},{10,... | collective-permute-start | bytes 503816 | tf_op jit(solution)/shard_map/ppermute | solution.py:488
  135.1 5.7 %collective-permute-start.39 = (f32[328,128]{1,0:T(8,128)S(1)}, f32[328,128]{1,0:T(8,128)S(1)}, u32[]{:S(2)}, u32[]{:S(2)}) collective-permute-start(f32[328,128]{1,0:T(8,128)S(1)} %collective-permute-done.36.rest_6_.rest_14_), channel_id=1, source_target_pairs={{0,4},{1,5},{2,6},{3,7},{4,0},{5,1},{6,2},{7,3},{8,12},{9,13},{10,... | collective-permute-start | bytes 503816 | tf_op jit(solution)/shard_map/ppermute | solution.py:488
  137.5 4.4 %collective-permute-start.35 = (f32[328,128]{1,0:T(8,128)S(1)}, f32[328,128]{1,0:T(8,128)S(1)}, u32[]{:S(2)}, u32[]{:S(2)}) collective-permute-start(f32[328,128]{1,0:T(8,128)S(1)} %collective-permute-done.30.rest_4_.rest_12_), channel_id=1, source_target_pairs={{0,1},{1,0},{2,3},{3,2},{4,5},{5,4},{6,7},{7,6},{8,9},{9,8},{10,11... | collective-permute-start | bytes 503816 | tf_op jit(solution)/shard_map/ppermute | solution.py:488
  139.7 2.1 %collective-permute-start.34 = (f32[328,128]{1,0:T(8,128)S(1)}, f32[328,128]{1,0:T(8,128)S(1)}, u32[]{:S(2)}, u32[]{:S(2)}) collective-permute-start(f32[328,128]{1,0:T(8,128)S(1)} %collective-permute-done.33.rest_2_.rest_10_), channel_id=1, source_target_pairs={{0,1},{1,0},{2,3},{3,2},{4,5},{5,4},{6,7},{7,6},{8,9},{9,8},{10,11... | collective-permute-start | bytes 503816 | tf_op jit(solution)/shard_map/ppermute | solution.py:488
  139.7 2.1 %collective-permute-start.37 = (f32[328,128]{1,0:T(8,128)S(1)}, f32[328,128]{1,0:T(8,128)S(1)}, u32[]{:S(2)}, u32[]{:S(2)}) collective-permute-start(f32[328,128]{1,0:T(8,128)S(1)} %collective-permute-done.36.rest_6_.rest_14_), channel_id=1, source_target_pairs={{0,1},{1,0},{2,3},{3,2},{4,5},{5,4},{6,7},{7,6},{8,9},{9,8},{10,11... | collective-permute-start | bytes 503816 | tf_op jit(solution)/shard_map/ppermute | solution.py:488
  140.2 10.5 %collective-permute-start.43 = (f32[328,128]{1,0:T(8,128)S(1)}, f32[328,128]{1,0:T(8,128)S(1)}, u32[]{:S(2)}, u32[]{:S(2)}) collective-permute-start(f32[328,128]{1,0:T(8,128)S(1)} %collective-permute-done.36.rest_6_.rest_14_), channel_id=1, source_target_pairs={{0,2},{1,3},{2,0},{3,1},{4,6},{5,7},{6,4},{7,5},{8,10},{9,11},{10,... | collective-permute-start | bytes 503816 | tf_op jit(solution)/shard_map/ppermute | solution.py:488
  140.8 10.4 %collective-permute-start.41 = (f32[328,128]{1,0:T(8,128)S(1)}, f32[328,128]{1,0:T(8,128)S(1)}, u32[]{:S(2)}, u32[]{:S(2)}) collective-permute-start(f32[328,128]{1,0:T(8,128)S(1)} %collective-permute-done.39.rest_2_), channel_id=1, source_target_pairs={{0,2},{1,3},{2,0},{3,1},{4,6},{5,7},{6,4},{7,5},{8,10},{9,11},{10,... | collective-permute-start | bytes 503816 | tf_op jit(solution)/shard_map/ppermute | solution.py:488
  147.7 4.0 %collective-permute-start.38 = (f32[328,128]{1,0:T(8,128)S(1)}, f32[328,128]{1,0:T(8,128)S(1)}, u32[]{:S(2)}, u32[]{:S(2)}) collective-permute-start(f32[328,128]{1,0:T(8,128)S(1)} %get-tuple-element.27.rest_0_), channel_id=1, source_target_pairs={{0,1},{1,0},{2,3},{3,2},{4,5},{5,4},{6,7},{7,6},{8,9},{9,8},{10,11... | collective-permute-start | bytes 503816 | tf_op jit(solution)/shard_map/ppermute | solution.py:488
  150.7 1.4 collective-permute-start.40
  150.7 1.6 collective-permute-start.44
  151.2 1.4 collective-permute-start.42
  (9 other events, 76.3 us)

commit v16 on v15

--- a/solution.py
+++ b/solution.py
@@ -384,15 +384,12 @@
     return [jnp.bitwise_xor(lax.div(me, 2), m) for m in pairs]
 
 
-def early_kernel(n, dpc, first_ref, second_ref, model_hbm, vis_hbm, unused_in, *rest):
+def early_kernel(n, dpc, first_ref, second_ref, model_hbm, vis_ref, unused_in, *rest):
     ins, rest = rest[: 2 * len(NEAR)], rest[2 * len(NEAR) :]
-    acc_ref, hre, him, unused_out, vis_ref, side, model_ref, sems = rest
+    acc_ref, hre, him, unused_out, model_ref, sems = rest
     me = lax.axis_index("bl")
-    (vis_copy,) = bring([(vis_hbm, vis_ref)], side)
     fetch = Fetch(model_hbm, model_ref, sems, [k * dpc for k in chips_of(me, NEAR)])
     products(dpc, me, first_ref, second_ref, ins, hre, him)
-
-    vis_copy.wait()
 
     def pair(b, carry):
         acc = vis_ref[0, b], vis_ref[1, b]
@@ -408,7 +405,7 @@
     first_ref,
     second_ref,
     model_hbm,
-    mask_hbm,
+    mask_ref,
     power_ref,
     acc_ref,
     near_re,
@@ -416,16 +413,13 @@
     *rest,
 ):
     ins, rest = rest[: 2 * len(FAR)], rest[2 * len(FAR) :]
-    out_ref, mask_ref, side, model_ref, sems, hre, him, cre, cim = rest
-    (mask_copy,) = bring([(mask_hbm, mask_ref)], side)
+    out_ref, model_ref, sems, hre, him, cre, cim = rest
     fetch = Fetch(model_hbm, model_ref, sems)
     me = lax.axis_index("bl")
     products(dpc, me, first_ref, second_ref, ins, hre, him)
     far = chips_of(me, FAR)
     chips = chips_of(me, NEAR) + far
 
-    mask_copy.wait()
-
     def pair(b, carry):
         acc = predict(dpc, b, (acc_ref[0, b], acc_ref[1, b]), far, model_ref, hre, him)
         correlate(dpc, b, weighted(b, acc, mask_ref), chips, model_ref, cre, cim)
@@ -443,9 +437,8 @@
     write_sums(dpc, chips, cre, cim, tiles, power_ref, out_ref, False)
 
 
-def last_kernel(n, dpc, first_ref, second_ref, model_hbm, mask_hbm, acc_ref, *rest):
-    ins, (res_ref, gains_ref, mask_ref, side, model_ref, sems, hre, him) = rest[:n], rest[n:]
-    (mask_copy,) = bring([(mask_hbm, mask_ref)], side)
+def last_kernel(n, dpc, first_ref, second_ref, model_hbm, mask_ref, acc_ref, *rest):
+    ins, (res_ref, gains_ref, model_ref, sems, hre, him) = rest[:n], rest[n:]
     me = lax.axis_index("bl")
     fetch = Fetch(model_hbm, model_ref, sems, [k * dpc for k in chips_of(me, FAR)])
     products(dpc, me, first_ref, second_ref, ins[: 2 * len(FAR)], hre, him)
@@ -459,8 +452,6 @@
                 gains_ref[0, pl.ds(at, 1), :] = parts[0][dd : dd + 1]
                 gains_ref[1, pl.ds(at, 1), :] = parts[1][dd : dd + 1]
 
-    mask_copy.wait()
-
     def pair(b, carry):
         acc = acc_ref[0, b], acc_ref[1, b]
         acc = predict(dpc, b, acc, range(len(FAR)), model_ref, hre, him)
@@ -500,7 +491,7 @@
 
 def fast_body(n, vis, model, mask, first, second, gre, gim):
     starts = (first.reshape(1, -1), second.reshape(1, -1), gre, gim)
-    model, vis, mask, *starts = (
+    model, far_vis, far_mask, *starts = (
         pltpu.with_memory_space_constraint(x, pltpu.HBM) for x in (model, vis, mask, *starts)
     )
     dpc = SOURCE_COUNT // (n // 2)
@@ -519,7 +510,7 @@
 
     def call(kernel, args, outs, scratch=(), micros=1, aliases={}):
         def place(x):
-            if any(x is y for y in (model, vis, mask, *starts)):
+            if any(x is y for y in (model, far_vis, far_mask, *starts)):
                 return HBM
             return SMEM if x.ndim == 1 else VMEM
 
@@ -547,7 +538,7 @@
     def powers_beside(x, got):
         nonlocal power
         outs = [shape(*half), shape(*x.shape)]
-        power, x = call(power_kernel, (model, mask, x), outs, mask_held + held_half, micros=20, aliases={2: 1})
+        power, x = call(power_kernel, (model, far_mask, x), outs, mask_held + held_half, micros=20, aliases={2: 1})
         return x
 
     got = gather(n, piece, powers_beside)
@@ -560,7 +551,7 @@
     )
     sums, power = call(
         first_pass_kernel,
-        (first, second, model, vis, mask, power, *got),
+        (first, second, model, far_vis, far_mask, power, *got),
         [shape(n, (ROWS + TILE) * dpc, channels), pltpu.HBM(plane, F32)],
         [vis.shape] + mask_held + held + [plane] * 4 + [(n,) + piece.shape],
         micros=9,
@@ -583,7 +574,7 @@
             nonlocal near
             args = (first, second, model, vis, x, *slots(got, NEAR))
             outs = [shape(*vis.shape), shape(*half), shape(*half), shape(*x.shape)]
-            *near, x = call(early_kernel, args, outs, [vis.shape, side] + held_half, aliases={4: 3})
+            *near, x = call(early_kernel, args, outs, held_half, aliases={4: 3})
             return x
 
         got = gather(n, g, beside)
@@ -602,7 +593,7 @@
             later_pass_kernel,
             (first, second, model, mask, power, *near, *got[: 2 * len(FAR)]),
             [shape(n, ROWS * dpc, channels)],
-            mask_held + held + [half] * 2 + [plane] * 2,
+            held + [half] * 2 + [plane] * 2,
             micros=7,
         )
         sums = exchange(sums)
@@ -617,7 +608,7 @@
         last_kernel,
         (first, second, model, mask, near[0], *got),
         [shape(*vis.shape), shape(2, *gre.shape)],
-        mask_held + held_half + [half] * 2,
+        held_half + [half] * 2,
         micros=4,
     )
     return gains, residual

time: 161 us -> 158 us (0.981)
  waiting for transfers between devices: 48.3 us -> 44.2 us
  local copies, waits for them, and re-layouts: 4.66 us -> 8.47 us
  Pallas kernels: 45.8 us -> 42.1 us
    all_to_all x2, waiting for transfers between devices: 36.8 us -> 32.9 us  [exchange(): return lax.all_to_all(x, 'bl', split_axis=0, concat_axis=0, tiled=True)]
    unnamed x20 -> x38, local copies, waits for them, and re-layouts: 4.66 us -> 8.47 us
    pallas_call x11, Pallas kernels: 45.8 us -> 42.1 us  [call(): pl.pallas_call(functools.partial(kernel, n, dpc), in_specs=[place(x) for...]
  transfers between devices with their start and end apart: 47 -> 47, of which waited for: 17 -> 15; matrix products, arithmetic and copies ran while one was open for 0% -> 0% of each run, Pallas kernels for 10% -> 9%
where the time goes in v16:
time: 158 us; the launch traced here: 155 us
  starting transfers between devices  59.1 us (37%)
  waiting for transfers between devices  44.2 us (28%)
  Pallas kernels  42.1 us (27%)
  local copies, waits for them, and re-layouts  8.47 us (5%)
    ppermute x45, starting transfers between devices, send(): return lax.ppermute(x, 'bl', [(i, i ^ o) for i in range(n)])  48.6 us
    pallas_call x11, Pallas kernels, call(): pl.pallas_call(functools.partial(kernel, n, dpc), in_specs=[place(x) for...  42.1 us
    all_to_all x2, waiting for transfers between devices, exchange(): return lax.all_to_all(x, 'bl', split_axis=0, concat_axis=0, tiled=True)  32.9 us
    ppermute x45, waiting for transfers between devices, send(): return lax.ppermute(x, 'bl', [(i, i ^ o) for i in range(n)])  11.3 us
    all_to_all x2, starting transfers between devices, exchange(): return lax.all_to_all(x, 'bl', split_axis=0, concat_axis=0, tiled=True)  10.5 us
    unnamed x38, local copies, waits for them, and re-layouts  8.47 us
  transfers between devices with their start and end apart: 47, of which 15 were waited for; matrix products, arithmetic and copies ran while one was open for 0% of the time, Pallas kernels for 9%

profile of v16, /device:TPU:9, one launch (start us, length us, event | category | flops | bytes accessed | tf_op | source)
XLA Modules:
  0.0 155.0 jit_solution(17793847258801748890)
XLA Ops:
  0.7 1.1 shard_map.86.rest_0_
  1.8 2.6 %collective-permute-start.7 = (f32[328,128]{1,0:T(8,128)S(1)}, f32[328,128]{1,0:T(8,128)S(1)}, u32[]{:S(2)}, u32[]{:S(2)}) collective-permute-start(f32[328,128]{1,0:T(8,128)S(1)} %shard_map.86.rest_0_), channel_id=1, source_target_pairs={{0,12},{1,13},{2,14},{3,15},{4,8},{5,9},{6,10},{7,11},{8,4},{9,5},... | collective-permute-start | bytes 503816 | tf_op jit(solution)/shard_map/ppermute | solution.py:479
  4.4 1.2 collective-permute-start.1
  5.6 1.4 collective-permute-done.3.rest_4_
  7.0 1.2 collective-permute-start.5
  8.2 4.6 %collective-permute-start.8 = (f32[328,128]{1,0:T(8,128)S(1)}, f32[328,128]{1,0:T(8,128)S(1)}, u32[]{:S(2)}, u32[]{:S(2)}) collective-permute-start(f32[328,128]{1,0:T(8,128)S(1)} %collective-permute-done.7.rest_12_), channel_id=1, source_target_pairs={{0,4},{1,5},{2,6},{3,7},{4,0},{5,1},{6,2},{7,3},{8,12},{9,13},{10,... | collective-permute-start | bytes 503816 | tf_op jit(solution)/shard_map/ppermute | solution.py:479
  12.8 1.9 %collective-permute-start = (f32[328,128]{1,0:T(8,128)S(1)}, f32[328,128]{1,0:T(8,128)S(1)}, u32[]{:S(2)}, u32[]{:S(2)}) collective-permute-start(f32[328,128]{1,0:T(8,128)S(1)} %shard_map.86.rest_0_), channel_id=1, source_target_pairs={{0,1},{1,0},{2,3},{3,2},{4,5},{5,4},{6,7},{7,6},{8,9},{9,8},{10,11... | collective-permute-start | bytes 503816 | tf_op jit(solution)/shard_map/ppermute | solution.py:479
  15.2 1.2 collective-permute-start.13
  16.8 3.5 %shard_map.87 = (f32[4,88,128]{2,1,0:T(8,128)S(1)}, f32[328,128]{1,0:T(8,128)S(1)}) custom-call(bf16[40,2,15,32,128]{4,3,2,1,0:T(8,128)(2,1)} %model_hbm.11, s32[15,32,128]{2,1,0:T(8,128)} %mask_ref.3, f32[328,128]{1,0:T(8,128)S(1)} %collective-permute-done.5.unused_in), custom_call_target="tpu_custom_call", output_to_operand_aliasing={{1}: (2, {})} | custom-call | bytes 73800000 | tf_op jit(solution)/shard_map/pallas_call | solution.py:517
  20.3 3.4 %collective-permute-start.12 = (f32[328,128]{1,0:T(8,128)S(1)}, f32[328,128]{1,0:T(8,128)S(1)}, u32[]{:S(2)}, u32[]{:S(2)}) collective-permute-start(f32[328,128]{1,0:T(8,128)S(1)} %collective-permute-done.7.rest_12_), channel_id=1, source_target_pairs={{0,1},{1,0},{2,3},{3,2},{4,5},{5,4},{6,7},{7,6},{8,9},{9,8},{10,11... | collective-permute-start | bytes 503816 | tf_op jit(solution)/shard_map/ppermute | solution.py:479
  24.7 0.8 collective-permute-start.11
  25.6 0.9 collective-permute-done.11.rest_11_
  26.5 10.9 %shard_map.89 = (f32[16,120,128]{2,1,0:T(8,128)}, f32[8,88,128]{2,1,0:T(8,128)}) custom-call(s32[15]{0:T(128)S(1)} %copy-done.17, s32[15]{0:T(128)S(1)} %copy-done.18, bf16[40,2,15,32,128]{4,3,2,1,0:T(8,128)(2,1)} %model_hbm.11, f32[2,15,32,128]{3,2,1,0:T(8,128)} %vis_ref.3, s32[15,32,128]{2,1,0:T(8,128)} %mask_ref.3, ...), custom_call_target="tpu_custom_call" | custom-call | bytes 33210000 | tf_op jit(solution)/shard_map/pallas_call | solution.py:517
  38.8 5.6 %all-to-all-start = ((f32[16,120,128]{2,1,0:T(8,128)}), f32[16,120,128]{2,1,0:T(8,128)S(1)}, u32[]{:S(2)}, u32[]{:S(2)}) async-start(f32[16,120,128]{2,1,0:T(8,128)} %get-tuple-element.20), calls=%async_computation | async-start | bytes 1966080 | tf_op jit(solution)/shard_map/all_to_all | solution.py:474
  44.4 0.9 copy-done.3
  45.3 0.9 copy-done.5
  46.2 0.9 copy-done.7
  47.2 0.9 copy-done.9
  48.1 0.9 copy-done.11
  49.0 0.9 copy-done.13
  50.9 17.0 %all-to-all-done.sums = f32[16,120,128]{2,1,0:T(8,128)S(1)} async-done(((f32[16,120,128]{2,1,0:T(8,128)}), f32[16,120,128]{2,1,0:T(8,128)S(1)}, u32[]{:S(2)}, u32[]{:S(2)}) %all-to-all-start) | async-done | bytes 983072 | tf_op jit(solution)/shard_map/all_to_all | solution.py:474
  67.9 0.9 copy-done.16
  68.8 1.5 shard_map.90.g_ref.rest_0_.g_in
  70.5 1.0 collective-permute-start.21
  71.5 1.6 %collective-permute-start.18 = (f32[328,128]{1,0:T(8,128)S(1)}, f32[328,128]{1,0:T(8,128)S(1)}, u32[]{:S(2)}, u32[]{:S(2)}) collective-permute-start(f32[328,128]{1,0:T(8,128)S(1)} %shard_map.90.g_ref.rest_0_.g_in), channel_id=1, source_target_pairs={{0,2},{1,3},{2,0},{3,1},{4,6},{5,7},{6,4},{7,5},{8,10},{9,11},{10,... | collective-permute-start | bytes 503816 | tf_op jit(solution)/shard_map/ppermute | solution.py:479
  73.0 1.1 collective-permute-start.17
  74.1 2.5 %collective-permute-done.15.rest_4_ = f32[328,128]{1,0:T(8,128)S(1)} collective-permute-done((f32[328,128]{1,0:T(8,128)S(1)}, f32[328,128]{1,0:T(8,128)S(1)}, u32[]{:S(2)}, u32[]{:S(2)}) %collective-permute-start.15) | collective-permute-done | bytes 167968 | tf_op jit(solution)/shard_map/ppermute | solution.py:479
  77.3 3.5 %collective-permute-start.24 = (f32[328,128]{1,0:T(8,128)S(1)}, f32[328,128]{1,0:T(8,128)S(1)}, u32[]{:S(2)}, u32[]{:S(2)}) collective-permute-start(f32[328,128]{1,0:T(8,128)S(1)} %collective-permute-done.21.rest_6_), channel_id=1, source_target_pairs={{0,4},{1,5},{2,6},{3,7},{4,0},{5,1},{6,2},{7,3},{8,12},{9,13},{10,... | collective-permute-start | bytes 503816 | tf_op jit(solution)/shard_map/ppermute | solution.py:479
  80.8 2.1 %collective-permute-start.20 = (f32[328,128]{1,0:T(8,128)S(1)}, f32[328,128]{1,0:T(8,128)S(1)}, u32[]{:S(2)}, u32[]{:S(2)}) collective-permute-start(f32[328,128]{1,0:T(8,128)S(1)} %collective-permute-done.15.rest_4_), channel_id=1, source_target_pairs={{0,1},{1,0},{2,3},{3,2},{4,5},{5,4},{6,7},{7,6},{8,9},{9,8},{10,11... | collective-permute-start | bytes 503816 | tf_op jit(solution)/shard_map/ppermute | solution.py:479
  83.7 1.2 collective-permute-start.26
  84.9 4.3 %shard_map.92 = (f32[2,15,32,128]{3,2,1,0:T(8,128)S(1)}, f32[4,88,128]{2,1,0:T(8,128)S(1)}, f32[4,88,128]{2,1,0:T(8,128)S(1)}, f32[328,128]{1,0:T(8,128)S(1)}) custom-call(s32[15]{0:T(128)S(1)} %copy-done.17, s32[15]{0:T(128)S(1)} %copy-done.18, bf16[40,2,15,32,128]{4,3,2,1,0:T(8,128)(2,1)} %model_hbm.11, ...), custom_call_target="tpu_custom_call", output_to_operand_aliasing={{3}: (4, {})} | custom-call | bytes 3690000 | tf_op jit(solution)/shard_map/pallas_call | solution.py:517
  89.2 2.8 %collective-permute-start.23 = (f32[328,128]{1,0:T(8,128)S(1)}, f32[328,128]{1,0:T(8,128)S(1)}, u32[]{:S(2)}, u32[]{:S(2)}) collective-permute-start(f32[328,128]{1,0:T(8,128)S(1)} %get-tuple-element.25.rest_0_), channel_id=1, source_target_pairs={{0,1},{1,0},{2,3},{3,2},{4,5},{5,4},{6,7},{7,6},{8,9},{9,8},{10,11... | collective-permute-start | bytes 503816 | tf_op jit(solution)/shard_map/ppermute | solution.py:479
  92.8 0.9 collective-permute-start.27
  93.7 1.0 collective-permute-done.27.rest_5_
  94.7 8.5 %shard_map.93 = f32[16,80,128]{2,1,0:T(8,128)} custom-call(s32[15]{0:T(128)S(1)} %copy-done.17, s32[15]{0:T(128)S(1)} %copy-done.18, bf16[40,2,15,32,128]{4,3,2,1,0:T(8,128)(2,1)} %model_hbm.11, s32[15,32,128]{2,1,0:T(8,128)S(1)} %copy-done.1, f32[8,88,128]{2,1,0:T(8,128)S(1)} %copy-done.14, f32[2,15,32,128]{3,2,1,0:T(8,128)S(1)} %get-tuple-element.22.acc_ref, ...), custom_call_target="tpu_custom_call" | custom-call | bytes 25830000 | tf_op jit(solution)/shard_map/pallas_call | solution.py:517
  103.2 4.9 %all-to-all-start.1 = ((f32[16,80,128]{2,1,0:T(8,128)}), f32[16,80,128]{2,1,0:T(8,128)S(1)}, u32[]{:S(2)}, u32[]{:S(2)}) async-start(f32[16,80,128]{2,1,0:T(8,128)} %shard_map.93), calls=%async_computation.1 | async-start | bytes 1310720 | tf_op jit(solution)/shard_map/all_to_all | solution.py:474
  108.2 1.0 shard_map.91.den_ref
  109.2 15.8 %all-to-all-done.1.sums = f32[16,80,128]{2,1,0:T(8,128)S(1)} async-done(((f32[16,80,128]{2,1,0:T(8,128)}), f32[16,80,128]{2,1,0:T(8,128)S(1)}, u32[]{:S(2)}, u32[]{:S(2)}) %all-to-all-start.1) | async-done | bytes 655392 | tf_op jit(solution)/shard_map/all_to_all | solution.py:474
  125.0 1.0 shard_map.94.rest_0_.rest_8_
  126.7 1.6 %collective-permute-start.33 = (f32[328,128]{1,0:T(8,128)S(1)}, f32[328,128]{1,0:T(8,128)S(1)}, u32[]{:S(2)}, u32[]{:S(2)}) collective-permute-start(f32[328,128]{1,0:T(8,128)S(1)} %shard_map.94.rest_0_.rest_8_), channel_id=1, source_target_pairs={{0,2},{1,3},{2,0},{3,1},{4,6},{5,7},{6,4},{7,5},{8,10},{9,11},{10,... | collective-permute-start | bytes 503816 | tf_op jit(solution)/shard_map/ppermute | solution.py:479
  128.3 1.1 collective-permute-start.32
  129.4 2.8 %collective-permute-done.30.rest_4_.rest_12_ = f32[328,128]{1,0:T(8,128)S(1)} collective-permute-done((f32[328,128]{1,0:T(8,128)S(1)}, f32[328,128]{1,0:T(8,128)S(1)}, u32[]{:S(2)}, u32[]{:S(2)}) %collective-permute-start.30) | collective-permute-done | bytes 167968 | tf_op jit(solution)/shard_map/ppermute | solution.py:479
  133.3 2.4 %collective-permute-start.39 = (f32[328,128]{1,0:T(8,128)S(1)}, f32[328,128]{1,0:T(8,128)S(1)}, u32[]{:S(2)}, u32[]{:S(2)}) collective-permute-start(f32[328,128]{1,0:T(8,128)S(1)} %collective-permute-done.36.rest_6_.rest_14_), channel_id=1, source_target_pairs={{0,4},{1,5},{2,6},{3,7},{4,0},{5,1},{6,2},{7,3},{8,12},{9,13},{10,... | collective-permute-start | bytes 503816 | tf_op jit(solution)/shard_map/ppermute | solution.py:479
  135.7 2.2 %collective-permute-start.35 = (f32[328,128]{1,0:T(8,128)S(1)}, f32[328,128]{1,0:T(8,128)S(1)}, u32[]{:S(2)}, u32[]{:S(2)}) collective-permute-start(f32[328,128]{1,0:T(8,128)S(1)} %collective-permute-done.30.rest_4_.rest_12_), channel_id=1, source_target_pairs={{0,1},{1,0},{2,3},{3,2},{4,5},{5,4},{6,7},{7,6},{8,9},{9,8},{10,11... | collective-permute-start | bytes 503816 | tf_op jit(solution)/shard_map/ppermute | solution.py:479
  139.0 1.0 collective-permute-start.41
  140.0 4.9 %shard_map.95 = (f32[2,15,32,128]{3,2,1,0:T(8,128)S(1)}, f32[4,88,128]{2,1,0:T(8,128)}, f32[4,88,128]{2,1,0:T(8,128)}, f32[328,128]{1,0:T(8,128)S(1)}) custom-call(s32[15]{0:T(128)S(1)} %copy-done.17, s32[15]{0:T(128)S(1)} %copy-done.18, bf16[40,2,15,32,128]{4,3,2,1,0:T(8,128)(2,1)} %model_hbm.11, ...), custom_call_target="tpu_custom_call", output_to_operand_aliasing={{3}: (4, {})} | custom-call | bytes 3690000 | tf_op jit(solution)/shard_map/pallas_call | solution.py:517
  145.0 3.0 %collective-permute-start.38 = (f32[328,128]{1,0:T(8,128)S(1)}, f32[328,128]{1,0:T(8,128)S(1)}, u32[]{:S(2)}, u32[]{:S(2)}) collective-permute-start(f32[328,128]{1,0:T(8,128)S(1)} %get-tuple-element.27.rest_0_), channel_id=1, source_target_pairs={{0,1},{1,0},{2,3},{3,2},{4,5},{5,4},{6,7},{7,6},{8,9},{9,8},{10,11... | collective-permute-start | bytes 503816 | tf_op jit(solution)/shard_map/ppermute | solution.py:479
  149.8 5.0 %shard_map.96 = (f32[2,15,32,128]{3,2,1,0:T(8,128)}, f32[2,160,128]{2,1,0:T(8,128)}) custom-call(s32[15]{0:T(128)S(1)} %copy-done.17, s32[15]{0:T(128)S(1)} %copy-done.18, bf16[40,2,15,32,128]{4,3,2,1,0:T(8,128)(2,1)} %model_hbm.11, s32[15,32,128]{2,1,0:T(8,128)S(1)} %copy-done.1, f32[2,15,32,128]{3,2,1,0:T(8,128)S(1)} %get-tuple-element.26.acc_ref, ...), custom_call_target="tpu_custom_call" | custom-call | bytes 14760000 | tf_op jit(solution)/shard_map/pallas_call | solution.py:517
  (95 shorter events, 11.5 us)
Async XLA Ops:
  1.7 5.2 %collective-permute-start.3 = (f32[328,128]{1,0:T(8,128)S(1)}, f32[328,128]{1,0:T(8,128)S(1)}, u32[]{:S(2)}, u32[]{:S(2)}) collective-permute-start(f32[328,128]{1,0:T(8,128)S(1)} %shard_map.86.rest_0_), channel_id=1, source_target_pairs={{0,4},{1,5},{2,6},{3,7},{4,0},{5,1},{6,2},{7,3},{8,12},{9,13},{10,... | collective-permute-start | bytes 503816 | tf_op jit(solution)/shard_map/ppermute | solution.py:479
  1.8 6.4 %collective-permute-start.7 = (f32[328,128]{1,0:T(8,128)S(1)}, f32[328,128]{1,0:T(8,128)S(1)}, u32[]{:S(2)}, u32[]{:S(2)}) collective-permute-start(f32[328,128]{1,0:T(8,128)S(1)} %shard_map.86.rest_0_), channel_id=1, source_target_pairs={{0,12},{1,13},{2,14},{3,15},{4,8},{5,9},{6,10},{7,11},{8,4},{9,5},... | collective-permute-start | bytes 503816 | tf_op jit(solution)/shard_map/ppermute | solution.py:479
  4.4 10.3 %collective-permute-start.1 = (f32[328,128]{1,0:T(8,128)S(1)}, f32[328,128]{1,0:T(8,128)S(1)}, u32[]{:S(2)}, u32[]{:S(2)}) collective-permute-start(f32[328,128]{1,0:T(8,128)S(1)} %shard_map.86.rest_0_), channel_id=1, source_target_pairs={{0,2},{1,3},{2,0},{3,1},{4,6},{5,7},{6,4},{7,5},{8,10},{9,11},{10,... | collective-permute-start | bytes 503816 | tf_op jit(solution)/shard_map/ppermute | solution.py:479
  7.0 8.2 %collective-permute-start.5 = (f32[328,128]{1,0:T(8,128)S(1)}, f32[328,128]{1,0:T(8,128)S(1)}, u32[]{:S(2)}, u32[]{:S(2)}) collective-permute-start(f32[328,128]{1,0:T(8,128)S(1)} %collective-permute-done.3.rest_4_), channel_id=1, source_target_pairs={{0,2},{1,3},{2,0},{3,1},{4,6},{5,7},{6,4},{7,5},{8,10},{9,11},{10,... | collective-permute-start | bytes 503816 | tf_op jit(solution)/shard_map/ppermute | solution.py:479
  8.2 8.2 %collective-permute-start.8 = (f32[328,128]{1,0:T(8,128)S(1)}, f32[328,128]{1,0:T(8,128)S(1)}, u32[]{:S(2)}, u32[]{:S(2)}) collective-permute-start(f32[328,128]{1,0:T(8,128)S(1)} %collective-permute-done.7.rest_12_), channel_id=1, source_target_pairs={{0,4},{1,5},{2,6},{3,7},{4,0},{5,1},{6,2},{7,3},{8,12},{9,13},{10,... | collective-permute-start | bytes 503816 | tf_op jit(solution)/shard_map/ppermute | solution.py:479
  12.8 7.5 %collective-permute-start = (f32[328,128]{1,0:T(8,128)S(1)}, f32[328,128]{1,0:T(8,128)S(1)}, u32[]{:S(2)}, u32[]{:S(2)}) collective-permute-start(f32[328,128]{1,0:T(8,128)S(1)} %shard_map.86.rest_0_), channel_id=1, source_target_pairs={{0,1},{1,0},{2,3},{3,2},{4,5},{5,4},{6,7},{7,6},{8,9},{9,8},{10,11... | collective-permute-start | bytes 503816 | tf_op jit(solution)/shard_map/ppermute | solution.py:479
  14.7 9.0 %collective-permute-start.2 = (f32[328,128]{1,0:T(8,128)S(1)}, f32[328,128]{1,0:T(8,128)S(1)}, u32[]{:S(2)}, u32[]{:S(2)}) collective-permute-start(f32[328,128]{1,0:T(8,128)S(1)} %collective-permute-done.1.rest_2_), channel_id=1, source_target_pairs={{0,1},{1,0},{2,3},{3,2},{4,5},{5,4},{6,7},{7,6},{8,9},{9,8},{10,11... | collective-permute-start | bytes 503816 | tf_op jit(solution)/shard_map/ppermute | solution.py:479
  14.7 9.1 %collective-permute-start.4 = (f32[328,128]{1,0:T(8,128)S(1)}, f32[328,128]{1,0:T(8,128)S(1)}, u32[]{:S(2)}, u32[]{:S(2)}) collective-permute-start(f32[328,128]{1,0:T(8,128)S(1)} %collective-permute-done.3.rest_4_), channel_id=1, source_target_pairs={{0,1},{1,0},{2,3},{3,2},{4,5},{5,4},{6,7},{7,6},{8,9},{9,8},{10,11... | collective-permute-start | bytes 503816 | tf_op jit(solution)/shard_map/ppermute | solution.py:479
  15.2 9.0 %collective-permute-start.13 = (f32[328,128]{1,0:T(8,128)S(1)}, f32[328,128]{1,0:T(8,128)S(1)}, u32[]{:S(2)}, u32[]{:S(2)}) collective-permute-start(f32[328,128]{1,0:T(8,128)S(1)} %collective-permute-done.7.rest_12_), channel_id=1, source_target_pairs={{0,2},{1,3},{2,0},{3,1},{4,6},{5,7},{6,4},{7,5},{8,10},{9,11},{10,... | collective-permute-start | bytes 503816 | tf_op jit(solution)/shard_map/ppermute | solution.py:479
  16.4 8.3 %collective-permute-start.10 = (f32[328,128]{1,0:T(8,128)S(1)}, f32[328,128]{1,0:T(8,128)S(1)}, u32[]{:S(2)}, u32[]{:S(2)}) collective-permute-start(f32[328,128]{1,0:T(8,128)S(1)} %collective-permute-done.8.rest_8_), channel_id=1, source_target_pairs={{0,2},{1,3},{2,0},{3,1},{4,6},{5,7},{6,4},{7,5},{8,10},{9,11},{10,... | collective-permute-start | bytes 503816 | tf_op jit(solution)/shard_map/ppermute | solution.py:479
  20.3 64.6 %copy-start = (f32[2,15,32,128]{3,2,1,0:T(8,128)S(1)}, f32[2,15,32,128]{3,2,1,0:T(8,128)}, u32[]{:S(2)}) copy-start(f32[2,15,32,128]{3,2,1,0:T(8,128)} %vis_ref.3) | copy-start | bytes 1474564
  20.3 5.2 %collective-permute-start.12 = (f32[328,128]{1,0:T(8,128)S(1)}, f32[328,128]{1,0:T(8,128)S(1)}, u32[]{:S(2)}, u32[]{:S(2)}) collective-permute-start(f32[328,128]{1,0:T(8,128)S(1)} %collective-permute-done.7.rest_12_), channel_id=1, source_target_pairs={{0,1},{1,0},{2,3},{3,2},{4,5},{5,4},{6,7},{7,6},{8,9},{9,8},{10,11... | collective-permute-start | bytes 503816 | tf_op jit(solution)/shard_map/ppermute | solution.py:479
  23.7 1.8 %collective-permute-start.6 = (f32[328,128]{1,0:T(8,128)S(1)}, f32[328,128]{1,0:T(8,128)S(1)}, u32[]{:S(2)}, u32[]{:S(2)}) collective-permute-start(f32[328,128]{1,0:T(8,128)S(1)} %get-tuple-element.16.rest_6_), channel_id=1, source_target_pairs={{0,1},{1,0},{2,3},{3,2},{4,5},{5,4},{6,7},{7,6},{8,9},{9,8},{10,11... | collective-permute-start | bytes 503816 | tf_op jit(solution)/shard_map/ppermute | solution.py:479
  23.8 1.7 %collective-permute-start.9 = (f32[328,128]{1,0:T(8,128)S(1)}, f32[328,128]{1,0:T(8,128)S(1)}, u32[]{:S(2)}, u32[]{:S(2)}) collective-permute-start(f32[328,128]{1,0:T(8,128)S(1)} %collective-permute-done.8.rest_8_), channel_id=1, source_target_pairs={{0,1},{1,0},{2,3},{3,2},{4,5},{5,4},{6,7},{7,6},{8,9},{9,8},{10,11... | collective-permute-start | bytes 503816 | tf_op jit(solution)/shard_map/ppermute | solution.py:479
  24.2 1.4 collective-permute-start.14
  24.7 1.8 %collective-permute-start.11 = (f32[328,128]{1,0:T(8,128)S(1)}, f32[328,128]{1,0:T(8,128)S(1)}, u32[]{:S(2)}, u32[]{:S(2)}) collective-permute-start(f32[328,128]{1,0:T(8,128)S(1)} %collective-permute-done.10.rest_10_), channel_id=1, source_target_pairs={{0,1},{1,0},{2,3},{3,2},{4,5},{5,4},{6,7},{7,6},{8,9},{9,8},{10,11... | collective-permute-start | bytes 503816 | tf_op jit(solution)/shard_map/ppermute | solution.py:479
  38.8 29.1 %all-to-all-start = ((f32[16,120,128]{2,1,0:T(8,128)}), f32[16,120,128]{2,1,0:T(8,128)S(1)}, u32[]{:S(2)}, u32[]{:S(2)}) async-start(f32[16,120,128]{2,1,0:T(8,128)} %get-tuple-element.20), calls=%async_computation | async-start | bytes 1966080 | tf_op jit(solution)/shard_map/all_to_all | solution.py:474
  70.4 6.2 %collective-permute-start.15 = (f32[328,128]{1,0:T(8,128)S(1)}, f32[328,128]{1,0:T(8,128)S(1)}, u32[]{:S(2)}, u32[]{:S(2)}) collective-permute-start(f32[328,128]{1,0:T(8,128)S(1)} %shard_map.90.g_ref.rest_0_.g_in), channel_id=1, source_target_pairs={{0,4},{1,5},{2,6},{3,7},{4,0},{5,1},{6,2},{7,3},{8,12},{9,13},{10,... | collective-permute-start | bytes 503816 | tf_op jit(solution)/shard_map/ppermute | solution.py:479
  70.5 6.8 %collective-permute-start.21 = (f32[328,128]{1,0:T(8,128)S(1)}, f32[328,128]{1,0:T(8,128)S(1)}, u32[]{:S(2)}, u32[]{:S(2)}) collective-permute-start(f32[328,128]{1,0:T(8,128)S(1)} %shard_map.90.g_ref.rest_0_.g_in), channel_id=1, source_target_pairs={{0,12},{1,13},{2,14},{3,15},{4,8},{5,9},{6,10},{7,11},{8,4},{9,5},... | collective-permute-start | bytes 503816 | tf_op jit(solution)/shard_map/ppermute | solution.py:479
  71.5 11.4 %collective-permute-start.18 = (f32[328,128]{1,0:T(8,128)S(1)}, f32[328,128]{1,0:T(8,128)S(1)}, u32[]{:S(2)}, u32[]{:S(2)}) collective-permute-start(f32[328,128]{1,0:T(8,128)S(1)} %shard_map.90.g_ref.rest_0_.g_in), channel_id=1, source_target_pairs={{0,2},{1,3},{2,0},{3,1},{4,6},{5,7},{6,4},{7,5},{8,10},{9,11},{10,... | collective-permute-start | bytes 503816 | tf_op jit(solution)/shard_map/ppermute | solution.py:479
  73.0 9.8 %collective-permute-start.17 = (f32[328,128]{1,0:T(8,128)S(1)}, f32[328,128]{1,0:T(8,128)S(1)}, u32[]{:S(2)}, u32[]{:S(2)}) collective-permute-start(f32[328,128]{1,0:T(8,128)S(1)} %shard_map.90.g_ref.rest_0_.g_in), channel_id=1, source_target_pairs={{0,1},{1,0},{2,3},{3,2},{4,5},{5,4},{6,7},{7,6},{8,9},{9,8},{10,11... | collective-permute-start | bytes 503816 | tf_op jit(solution)/shard_map/ppermute | solution.py:479
  76.5 6.8 %collective-permute-start.16 = (f32[328,128]{1,0:T(8,128)S(1)}, f32[328,128]{1,0:T(8,128)S(1)}, u32[]{:S(2)}, u32[]{:S(2)}) collective-permute-start(f32[328,128]{1,0:T(8,128)S(1)} %collective-permute-done.15.rest_4_), channel_id=1, source_target_pairs={{0,2},{1,3},{2,0},{3,1},{4,6},{5,7},{6,4},{7,5},{8,10},{9,11},{10,... | collective-permute-start | bytes 503816 | tf_op jit(solution)/shard_map/ppermute | solution.py:479
  77.3 6.4 %collective-permute-start.24 = (f32[328,128]{1,0:T(8,128)S(1)}, f32[328,128]{1,0:T(8,128)S(1)}, u32[]{:S(2)}, u32[]{:S(2)}) collective-permute-start(f32[328,128]{1,0:T(8,128)S(1)} %collective-permute-done.21.rest_6_), channel_id=1, source_target_pairs={{0,4},{1,5},{2,6},{3,7},{4,0},{5,1},{6,2},{7,3},{8,12},{9,13},{10,... | collective-permute-start | bytes 503816 | tf_op jit(solution)/shard_map/ppermute | solution.py:479
  80.8 4.1 %collective-permute-start.20 = (f32[328,128]{1,0:T(8,128)S(1)}, f32[328,128]{1,0:T(8,128)S(1)}, u32[]{:S(2)}, u32[]{:S(2)}) collective-permute-start(f32[328,128]{1,0:T(8,128)S(1)} %collective-permute-done.15.rest_4_), channel_id=1, source_target_pairs={{0,1},{1,0},{2,3},{3,2},{4,5},{5,4},{6,7},{7,6},{8,9},{9,8},{10,11... | collective-permute-start | bytes 503816 | tf_op jit(solution)/shard_map/ppermute | solution.py:479
  82.9 2.0 %collective-permute-start.19 = (f32[328,128]{1,0:T(8,128)S(1)}, f32[328,128]{1,0:T(8,128)S(1)}, u32[]{:S(2)}, u32[]{:S(2)}) collective-permute-start(f32[328,128]{1,0:T(8,128)S(1)} %collective-permute-done.18.rest_2_), channel_id=1, source_target_pairs={{0,1},{1,0},{2,3},{3,2},{4,5},{5,4},{6,7},{7,6},{8,9},{9,8},{10,11... | collective-permute-start | bytes 503816 | tf_op jit(solution)/shard_map/ppermute | solution.py:479
  82.9 2.0 %collective-permute-start.22 = (f32[328,128]{1,0:T(8,128)S(1)}, f32[328,128]{1,0:T(8,128)S(1)}, u32[]{:S(2)}, u32[]{:S(2)}) collective-permute-start(f32[328,128]{1,0:T(8,128)S(1)} %collective-permute-done.21.rest_6_), channel_id=1, source_target_pairs={{0,1},{1,0},{2,3},{3,2},{4,5},{5,4},{6,7},{7,6},{8,9},{9,8},{10,11... | collective-permute-start | bytes 503816 | tf_op jit(solution)/shard_map/ppermute | solution.py:479
  83.4 8.7 %collective-permute-start.28 = (f32[328,128]{1,0:T(8,128)S(1)}, f32[328,128]{1,0:T(8,128)S(1)}, u32[]{:S(2)}, u32[]{:S(2)}) collective-permute-start(f32[328,128]{1,0:T(8,128)S(1)} %collective-permute-done.21.rest_6_), channel_id=1, source_target_pairs={{0,2},{1,3},{2,0},{3,1},{4,6},{5,7},{6,4},{7,5},{8,10},{9,11},{10,... | collective-permute-start | bytes 503816 | tf_op jit(solution)/shard_map/ppermute | solution.py:479
  83.7 9.1 %collective-permute-start.26 = (f32[328,128]{1,0:T(8,128)S(1)}, f32[328,128]{1,0:T(8,128)S(1)}, u32[]{:S(2)}, u32[]{:S(2)}) collective-permute-start(f32[328,128]{1,0:T(8,128)S(1)} %collective-permute-done.24.rest_2_), channel_id=1, source_target_pairs={{0,2},{1,3},{2,0},{3,1},{4,6},{5,7},{6,4},{7,5},{8,10},{9,11},{10,... | collective-permute-start | bytes 503816 | tf_op jit(solution)/shard_map/ppermute | solution.py:479
  89.2 4.5 %collective-permute-start.23 = (f32[328,128]{1,0:T(8,128)S(1)}, f32[328,128]{1,0:T(8,128)S(1)}, u32[]{:S(2)}, u32[]{:S(2)}) collective-permute-start(f32[328,128]{1,0:T(8,128)S(1)} %get-tuple-element.25.rest_0_), channel_id=1, source_target_pairs={{0,1},{1,0},{2,3},{3,2},{4,5},{5,4},{6,7},{7,6},{8,9},{9,8},{10,11... | collective-permute-start | bytes 503816 | tf_op jit(solution)/shard_map/ppermute | solution.py:479
  92.0 1.7 %collective-permute-start.25 = (f32[328,128]{1,0:T(8,128)S(1)}, f32[328,128]{1,0:T(8,128)S(1)}, u32[]{:S(2)}, u32[]{:S(2)}) collective-permute-start(f32[328,128]{1,0:T(8,128)S(1)} %collective-permute-done.24.rest_2_), channel_id=1, source_target_pairs={{0,1},{1,0},{2,3},{3,2},{4,5},{5,4},{6,7},{7,6},{8,9},{9,8},{10,11... | collective-permute-start | bytes 503816 | tf_op jit(solution)/shard_map/ppermute | solution.py:479
  92.1 1.6 %collective-permute-start.29 = (f32[328,128]{1,0:T(8,128)S(1)}, f32[328,128]{1,0:T(8,128)S(1)}, u32[]{:S(2)}, u32[]{:S(2)}) collective-permute-start(f32[328,128]{1,0:T(8,128)S(1)} %collective-permute-done.28.rest_6_), channel_id=1, source_target_pairs={{0,1},{1,0},{2,3},{3,2},{4,5},{5,4},{6,7},{7,6},{8,9},{9,8},{10,11... | collective-permute-start | bytes 503816 | tf_op jit(solution)/shard_map/ppermute | solution.py:479
  92.8 1.9 %collective-permute-start.27 = (f32[328,128]{1,0:T(8,128)S(1)}, f32[328,128]{1,0:T(8,128)S(1)}, u32[]{:S(2)}, u32[]{:S(2)}) collective-permute-start(f32[328,128]{1,0:T(8,128)S(1)} %collective-permute-done.26.rest_4_), channel_id=1, source_target_pairs={{0,1},{1,0},{2,3},{3,2},{4,5},{5,4},{6,7},{7,6},{8,9},{9,8},{10,11... | collective-permute-start | bytes 503816 | tf_op jit(solution)/shard_map/ppermute | solution.py:479
  103.2 21.8 %all-to-all-start.1 = ((f32[16,80,128]{2,1,0:T(8,128)}), f32[16,80,128]{2,1,0:T(8,128)S(1)}, u32[]{:S(2)}, u32[]{:S(2)}) async-start(f32[16,80,128]{2,1,0:T(8,128)} %shard_map.93), calls=%async_computation.1 | async-start | bytes 1310720 | tf_op jit(solution)/shard_map/all_to_all | solution.py:474
  126.1 6.1 %collective-permute-start.30 = (f32[328,128]{1,0:T(8,128)S(1)}, f32[328,128]{1,0:T(8,128)S(1)}, u32[]{:S(2)}, u32[]{:S(2)}) collective-permute-start(f32[328,128]{1,0:T(8,128)S(1)} %shard_map.94.rest_0_.rest_8_), channel_id=1, source_target_pairs={{0,4},{1,5},{2,6},{3,7},{4,0},{5,1},{6,2},{7,3},{8,12},{9,13},{10,... | collective-permute-start | bytes 503816 | tf_op jit(solution)/shard_map/ppermute | solution.py:479
  126.2 7.1 %collective-permute-start.36 = (f32[328,128]{1,0:T(8,128)S(1)}, f32[328,128]{1,0:T(8,128)S(1)}, u32[]{:S(2)}, u32[]{:S(2)}) collective-permute-start(f32[328,128]{1,0:T(8,128)S(1)} %shard_map.94.rest_0_.rest_8_), channel_id=1, source_target_pairs={{0,12},{1,13},{2,14},{3,15},{4,8},{5,9},{6,10},{7,11},{8,4},{9,5},... | collective-permute-start | bytes 503816 | tf_op jit(solution)/shard_map/ppermute | solution.py:479
  126.7 11.2 %collective-permute-start.33 = (f32[328,128]{1,0:T(8,128)S(1)}, f32[328,128]{1,0:T(8,128)S(1)}, u32[]{:S(2)}, u32[]{:S(2)}) collective-permute-start(f32[328,128]{1,0:T(8,128)S(1)} %shard_map.94.rest_0_.rest_8_), channel_id=1, source_target_pairs={{0,2},{1,3},{2,0},{3,1},{4,6},{5,7},{6,4},{7,5},{8,10},{9,11},{10,... | collective-permute-start | bytes 503816 | tf_op jit(solution)/shard_map/ppermute | solution.py:479
  128.3 9.6 %collective-permute-start.32 = (f32[328,128]{1,0:T(8,128)S(1)}, f32[328,128]{1,0:T(8,128)S(1)}, u32[]{:S(2)}, u32[]{:S(2)}) collective-permute-start(f32[328,128]{1,0:T(8,128)S(1)} %shard_map.94.rest_0_.rest_8_), channel_id=1, source_target_pairs={{0,1},{1,0},{2,3},{3,2},{4,5},{5,4},{6,7},{7,6},{8,9},{9,8},{10,11... | collective-permute-start | bytes 503816 | tf_op jit(solution)/shard_map/ppermute | solution.py:479
  132.2 6.2 %collective-permute-start.31 = (f32[328,128]{1,0:T(8,128)S(1)}, f32[328,128]{1,0:T(8,128)S(1)}, u32[]{:S(2)}, u32[]{:S(2)}) collective-permute-start(f32[328,128]{1,0:T(8,128)S(1)} %collective-permute-done.30.rest_4_.rest_12_), channel_id=1, source_target_pairs={{0,2},{1,3},{2,0},{3,1},{4,6},{5,7},{6,4},{7,5},{8,10},{9,11},{10,... | collective-permute-start | bytes 503816 | tf_op jit(solution)/shard_map/ppermute | solution.py:479
  133.3 5.7 %collective-permute-start.39 = (f32[328,128]{1,0:T(8,128)S(1)}, f32[328,128]{1,0:T(8,128)S(1)}, u32[]{:S(2)}, u32[]{:S(2)}) collective-permute-start(f32[328,128]{1,0:T(8,128)S(1)} %collective-permute-done.36.rest_6_.rest_14_), channel_id=1, source_target_pairs={{0,4},{1,5},{2,6},{3,7},{4,0},{5,1},{6,2},{7,3},{8,12},{9,13},{10,... | collective-permute-start | bytes 503816 | tf_op jit(solution)/shard_map/ppermute | solution.py:479
  135.7 4.4 %collective-permute-start.35 = (f32[328,128]{1,0:T(8,128)S(1)}, f32[328,128]{1,0:T(8,128)S(1)}, u32[]{:S(2)}, u32[]{:S(2)}) collective-permute-start(f32[328,128]{1,0:T(8,128)S(1)} %collective-permute-done.30.rest_4_.rest_12_), channel_id=1, source_target_pairs={{0,1},{1,0},{2,3},{3,2},{4,5},{5,4},{6,7},{7,6},{8,9},{9,8},{10,11... | collective-permute-start | bytes 503816 | tf_op jit(solution)/shard_map/ppermute | solution.py:479
  137.9 2.1 %collective-permute-start.34 = (f32[328,128]{1,0:T(8,128)S(1)}, f32[328,128]{1,0:T(8,128)S(1)}, u32[]{:S(2)}, u32[]{:S(2)}) collective-permute-start(f32[328,128]{1,0:T(8,128)S(1)} %collective-permute-done.33.rest_2_.rest_10_), channel_id=1, source_target_pairs={{0,1},{1,0},{2,3},{3,2},{4,5},{5,4},{6,7},{7,6},{8,9},{9,8},{10,11... | collective-permute-start | bytes 503816 | tf_op jit(solution)/shard_map/ppermute | solution.py:479
  137.9 2.1 %collective-permute-start.37 = (f32[328,128]{1,0:T(8,128)S(1)}, f32[328,128]{1,0:T(8,128)S(1)}, u32[]{:S(2)}, u32[]{:S(2)}) collective-permute-start(f32[328,128]{1,0:T(8,128)S(1)} %collective-permute-done.36.rest_6_.rest_14_), channel_id=1, source_target_pairs={{0,1},{1,0},{2,3},{3,2},{4,5},{5,4},{6,7},{7,6},{8,9},{9,8},{10,11... | collective-permute-start | bytes 503816 | tf_op jit(solution)/shard_map/ppermute | solution.py:479
  138.4 9.6 %collective-permute-start.43 = (f32[328,128]{1,0:T(8,128)S(1)}, f32[328,128]{1,0:T(8,128)S(1)}, u32[]{:S(2)}, u32[]{:S(2)}) collective-permute-start(f32[328,128]{1,0:T(8,128)S(1)} %collective-permute-done.36.rest_6_.rest_14_), channel_id=1, source_target_pairs={{0,2},{1,3},{2,0},{3,1},{4,6},{5,7},{6,4},{7,5},{8,10},{9,11},{10,... | collective-permute-start | bytes 503816 | tf_op jit(solution)/shard_map/ppermute | solution.py:479
  139.0 9.5 %collective-permute-start.41 = (f32[328,128]{1,0:T(8,128)S(1)}, f32[328,128]{1,0:T(8,128)S(1)}, u32[]{:S(2)}, u32[]{:S(2)}) collective-permute-start(f32[328,128]{1,0:T(8,128)S(1)} %collective-permute-done.39.rest_2_), channel_id=1, source_target_pairs={{0,2},{1,3},{2,0},{3,1},{4,6},{5,7},{6,4},{7,5},{8,10},{9,11},{10,... | collective-permute-start | bytes 503816 | tf_op jit(solution)/shard_map/ppermute | solution.py:479
  145.0 4.0 %collective-permute-start.38 = (f32[328,128]{1,0:T(8,128)S(1)}, f32[328,128]{1,0:T(8,128)S(1)}, u32[]{:S(2)}, u32[]{:S(2)}) collective-permute-start(f32[328,128]{1,0:T(8,128)S(1)} %get-tuple-element.27.rest_0_), channel_id=1, source_target_pairs={{0,1},{1,0},{2,3},{3,2},{4,5},{5,4},{6,7},{7,6},{8,9},{9,8},{10,11... | collective-permute-start | bytes 503816 | tf_op jit(solution)/shard_map/ppermute | solution.py:479
  147.9 1.4 collective-permute-start.40
  148.0 1.6 %collective-permute-start.44 = (f32[328,128]{1,0:T(8,128)S(1)}, f32[328,128]{1,0:T(8,128)S(1)}, u32[]{:S(2)}, u32[]{:S(2)}) collective-permute-start(f32[328,128]{1,0:T(8,128)S(1)} %collective-permute-done.43.rest_6_), channel_id=1, source_target_pairs={{0,1},{1,0},{2,3},{3,2},{4,5},{5,4},{6,7},{7,6},{8,9},{9,8},{10,11... | collective-permute-start | bytes 503816 | tf_op jit(solution)/shard_map/ppermute | solution.py:479
  148.4 1.4 collective-permute-start.42
  (18 other events, 206.6 us)

commit v17 on v16

--- a/solution.py
+++ b/solution.py
@@ -130,7 +130,7 @@
 
 
 def first_own_kernel(n, dpc, *rest):
-    ins, (g_ref, onehot_ref, split, lines) = rest[:n], rest[n:]
+    ins, (g_ref, onehot_ref, unused_out, split, lines) = rest[:n], rest[n:]
     me = lax.axis_index("bl")
     k, c = lax.div(me, 2), lax.rem(me, 2)
     per = STATIONS // n
@@ -542,12 +542,13 @@
         return x
 
     got = gather(n, piece, powers_beside)
-    g, onehot = call(
+    g, onehot, got[0] = call(
         first_own_kernel,
         got,
-        [shape(*mine), shape(STATIONS, lots, dtype=BF16)],
+        [shape(*mine), shape(STATIONS, lots, dtype=BF16), shape(*piece.shape)],
         [(STATIONS * TILE, channels), (n, channels)],
         micros=2,
+        aliases={0: 2},
     )
     sums, power = call(
         first_pass_kernel,

time: 158 us -> 155 us (0.981)
  blocking collectives: 0 us -> 29.4 us
  waiting for transfers between devices: 44.2 us -> 28.6 us
  local copies, waits for them, and re-layouts: 8.47 us -> 0.03 us
  starting transfers between devices: 59.1 us -> 52.1 us
    all_to_all x0 -> x1, blocking collectives: none -> 29.4 us  [exchange(): return lax.all_to_all(x, 'bl', split_axis=0, concat_axis=0, tiled=True)]
    all_to_all x2 -> x1, waiting for transfers between devices: 32.9 us -> 15.8 us  [exchange(): return lax.all_to_all(x, 'bl', split_axis=0, concat_axis=0, tiled=True)]
    unnamed x38 -> x10, local copies, waits for them, and re-layouts: 8.47 us -> 0.03 us
    all_to_all x2 -> x1, starting transfers between devices: 10.5 us -> 5.3 us  [exchange(): return lax.all_to_all(x, 'bl', split_axis=0, concat_axis=0, tiled=True)]
    ppermute x45, starting transfers between devices: 48.6 us -> 46.8 us  [send(): return lax.ppermute(x, 'bl', [(i, i ^ o) for i in range(n)])]
  transfers between devices with their start and end apart: 47 -> 46, of which waited for: 15 -> 17; matrix products, arithmetic and copies ran while one was open for 0% -> 0% of each run, Pallas kernels for 9% -> 9%
where the time goes in v17:
time: 155 us; the launch traced here: 153 us
  starting transfers between devices  52.1 us (34%)
  Pallas kernels  41.5 us (27%)
  blocking collectives  29.4 us (19%)
  waiting for transfers between devices  28.6 us (18%)
    ppermute x45, starting transfers between devices, send(): return lax.ppermute(x, 'bl', [(i, i ^ o) for i in range(n)])  46.8 us
    pallas_call x11, Pallas kernels, call(): pl.pallas_call(functools.partial(kernel, n, dpc), in_specs=[place(x) for...  41.5 us
    all_to_all x1, blocking collectives, exchange(): return lax.all_to_all(x, 'bl', split_axis=0, concat_axis=0, tiled=True)  29.4 us
    all_to_all x1, waiting for transfers between devices, exchange(): return lax.all_to_all(x, 'bl', split_axis=0, concat_axis=0, tiled=True)  15.8 us
    ppermute x45, waiting for transfers between devices, send(): return lax.ppermute(x, 'bl', [(i, i ^ o) for i in range(n)])  12.8 us
    all_to_all x1, starting transfers between devices, exchange(): return lax.all_to_all(x, 'bl', split_axis=0, concat_axis=0, tiled=True)  5.3 us
  transfers between devices with their start and end apart: 46, of which 17 were waited for; matrix products, arithmetic and copies ran while one was open for 0% of the time, Pallas kernels for 9%

profile of v17, /device:TPU:9, one launch (start us, length us, event | category | flops | bytes accessed | tf_op | source)
XLA Modules:
  0.0 152.7 jit_solution(16892295654571231009)
XLA Ops:
  0.7 1.1 shard_map.86.rest_0_
  1.8 2.6 %collective-permute-start.7 = (f32[328,128]{1,0:T(8,128)S(1)}, f32[328,128]{1,0:T(8,128)S(1)}, u32[]{:S(2)}, u32[]{:S(2)}) collective-permute-start(f32[328,128]{1,0:T(8,128)S(1)} %shard_map.86.rest_0_), channel_id=1, source_target_pairs={{0,12},{1,13},{2,14},{3,15},{4,8},{5,9},{6,10},{7,11},{8,4},{9,5},... | collective-permute-start | bytes 503816 | tf_op jit(solution)/shard_map/ppermute | solution.py:479
  4.4 1.2 collective-permute-start.1
  5.6 1.4 collective-permute-done.3.rest_4_
  7.0 1.2 collective-permute-start.5
  8.2 4.6 %collective-permute-start.8 = (f32[328,128]{1,0:T(8,128)S(1)}, f32[328,128]{1,0:T(8,128)S(1)}, u32[]{:S(2)}, u32[]{:S(2)}) collective-permute-start(f32[328,128]{1,0:T(8,128)S(1)} %collective-permute-done.7.rest_12_), channel_id=1, source_target_pairs={{0,4},{1,5},{2,6},{3,7},{4,0},{5,1},{6,2},{7,3},{8,12},{9,13},{10,... | collective-permute-start | bytes 503816 | tf_op jit(solution)/shard_map/ppermute | solution.py:479
  12.8 1.9 %collective-permute-start = (f32[328,128]{1,0:T(8,128)S(1)}, f32[328,128]{1,0:T(8,128)S(1)}, u32[]{:S(2)}, u32[]{:S(2)}) collective-permute-start(f32[328,128]{1,0:T(8,128)S(1)} %shard_map.86.rest_0_), channel_id=1, source_target_pairs={{0,1},{1,0},{2,3},{3,2},{4,5},{5,4},{6,7},{7,6},{8,9},{9,8},{10,11... | collective-permute-start | bytes 503816 | tf_op jit(solution)/shard_map/ppermute | solution.py:479
  14.7 0.5 collective-permute-start.4
  15.2 1.2 collective-permute-start.13
  16.8 3.5 %shard_map.87 = (f32[4,88,128]{2,1,0:T(8,128)S(1)}, f32[328,128]{1,0:T(8,128)S(1)}) custom-call(bf16[40,2,15,32,128]{4,3,2,1,0:T(8,128)(2,1)} %model_hbm.11, s32[15,32,128]{2,1,0:T(8,128)} %mask_ref.3, f32[328,128]{1,0:T(8,128)S(1)} %collective-permute-done.5.unused_in), custom_call_target="tpu_custom_call", output_to_operand_aliasing={{1}: (2, {})} | custom-call | bytes 73800000 | tf_op jit(solution)/shard_map/pallas_call | solution.py:517
  20.3 3.4 %collective-permute-start.12 = (f32[328,128]{1,0:T(8,128)S(1)}, f32[328,128]{1,0:T(8,128)S(1)}, u32[]{:S(2)}, u32[]{:S(2)}) collective-permute-start(f32[328,128]{1,0:T(8,128)S(1)} %collective-permute-done.7.rest_12_), channel_id=1, source_target_pairs={{0,1},{1,0},{2,3},{3,2},{4,5},{5,4},{6,7},{7,6},{8,9},{9,8},{10,11... | collective-permute-start | bytes 503816 | tf_op jit(solution)/shard_map/ppermute | solution.py:479
  24.7 0.8 collective-permute-start.11
  25.6 0.9 collective-permute-done.11.rest_11_
  26.8 10.3 %shard_map.89 = (f32[16,120,128]{2,1,0:T(8,128)S(1)}, f32[8,88,128]{2,1,0:T(8,128)}) custom-call(s32[15]{0:T(128)S(1)} %copy-done.3, s32[15]{0:T(128)S(1)} %copy-done.4, bf16[40,2,15,32,128]{4,3,2,1,0:T(8,128)(2,1)} %model_hbm.11, f32[2,15,32,128]{3,2,1,0:T(8,128)} %vis_ref.3, s32[15,32,128]{2,1,0:T(8,128)} %mask_ref.3, ...), custom_call_target="tpu_custom_call" | custom-call | bytes 33210000 | tf_op jit(solution)/shard_map/pallas_call | solution.py:517
  37.2 29.4 %all_to_all.10.sums = f32[16,120,128]{2,1,0:T(8,128)S(1)} all-to-all(f32[16,120,128]{2,1,0:T(8,128)S(1)} %get-tuple-element.22), channel_id=1, replica_groups=mesh['grp'=2,'bl'=16] {'bl'}, dimensions={0} | all-to-all | bytes 1966080 | tf_op jit(solution)/shard_map/all_to_all | solution.py:474
  66.6 1.6 %shard_map.90.g_ref.rest_0_.g_in = f32[328,128]{1,0:T(8,128)S(1)} custom-call(f32[328,128]{1,0:T(8,128)S(1)} %get-tuple-element.18.g_in, bf16[64,512]{1,0:T(8,128)(2,1)S(1)} %get-tuple-element.19.onehot_ref, f32[16,120,128]{2,1,0:T(8,128)S(1)} %all_to_all.10.sums), custom_call_target="tpu_custom_call" | custom-call | bytes 3690000 | tf_op jit(solution)/shard_map/pallas_call | solution.py:517
  68.3 0.8 collective-permute-start.21
  69.1 1.2 collective-permute-start.18
  70.3 1.1 collective-permute-start.17
  71.4 2.9 %collective-permute-done.15.rest_4_ = f32[328,128]{1,0:T(8,128)S(1)} collective-permute-done((f32[328,128]{1,0:T(8,128)S(1)}, f32[328,128]{1,0:T(8,128)S(1)}, u32[]{:S(2)}, u32[]{:S(2)}) %collective-permute-start.15) | collective-permute-done | bytes 167968 | tf_op jit(solution)/shard_map/ppermute | solution.py:479
  74.5 1.0 collective-permute-done.21.rest_6_
  75.5 2.2 %collective-permute-start.24 = (f32[328,128]{1,0:T(8,128)S(1)}, f32[328,128]{1,0:T(8,128)S(1)}, u32[]{:S(2)}, u32[]{:S(2)}) collective-permute-start(f32[328,128]{1,0:T(8,128)S(1)} %collective-permute-done.21.rest_6_), channel_id=1, source_target_pairs={{0,4},{1,5},{2,6},{3,7},{4,0},{5,1},{6,2},{7,3},{8,12},{9,13},{10,... | collective-permute-start | bytes 503816 | tf_op jit(solution)/shard_map/ppermute | solution.py:479
  77.7 2.2 %collective-permute-start.20 = (f32[328,128]{1,0:T(8,128)S(1)}, f32[328,128]{1,0:T(8,128)S(1)}, u32[]{:S(2)}, u32[]{:S(2)}) collective-permute-start(f32[328,128]{1,0:T(8,128)S(1)} %collective-permute-done.15.rest_4_), channel_id=1, source_target_pairs={{0,1},{1,0},{2,3},{3,2},{4,5},{5,4},{6,7},{7,6},{8,9},{9,8},{10,11... | collective-permute-start | bytes 503816 | tf_op jit(solution)/shard_map/ppermute | solution.py:479
  79.9 0.5 collective-permute-start.22
  80.4 0.5 collective-permute-start.28
  80.9 2.8 %collective-permute-start.26 = (f32[328,128]{1,0:T(8,128)S(1)}, f32[328,128]{1,0:T(8,128)S(1)}, u32[]{:S(2)}, u32[]{:S(2)}) collective-permute-start(f32[328,128]{1,0:T(8,128)S(1)} %collective-permute-done.24.rest_2_), channel_id=1, source_target_pairs={{0,2},{1,3},{2,0},{3,1},{4,6},{5,7},{6,4},{7,5},{8,10},{9,11},{10,... | collective-permute-start | bytes 503816 | tf_op jit(solution)/shard_map/ppermute | solution.py:479
  83.8 4.3 %shard_map.92 = (f32[2,15,32,128]{3,2,1,0:T(8,128)S(1)}, f32[4,88,128]{2,1,0:T(8,128)S(1)}, f32[4,88,128]{2,1,0:T(8,128)S(1)}, f32[328,128]{1,0:T(8,128)S(1)}) custom-call(s32[15]{0:T(128)S(1)} %copy-done.3, s32[15]{0:T(128)S(1)} %copy-done.4, bf16[40,2,15,32,128]{4,3,2,1,0:T(8,128)(2,1)} %model_hbm.11, ...), custom_call_target="tpu_custom_call", output_to_operand_aliasing={{3}: (4, {})} | custom-call | bytes 3690000 | tf_op jit(solution)/shard_map/pallas_call | solution.py:517
  88.1 2.0 %collective-permute-start.23 = (f32[328,128]{1,0:T(8,128)S(1)}, f32[328,128]{1,0:T(8,128)S(1)}, u32[]{:S(2)}, u32[]{:S(2)}) collective-permute-start(f32[328,128]{1,0:T(8,128)S(1)} %get-tuple-element.27.rest_0_), channel_id=1, source_target_pairs={{0,1},{1,0},{2,3},{3,2},{4,5},{5,4},{6,7},{7,6},{8,9},{9,8},{10,11... | collective-permute-start | bytes 503816 | tf_op jit(solution)/shard_map/ppermute | solution.py:479
  90.2 0.4 collective-permute-start.29
  92.0 8.5 %shard_map.93 = f32[16,80,128]{2,1,0:T(8,128)} custom-call(s32[15]{0:T(128)S(1)} %copy-done.3, s32[15]{0:T(128)S(1)} %copy-done.4, bf16[40,2,15,32,128]{4,3,2,1,0:T(8,128)(2,1)} %model_hbm.11, s32[15,32,128]{2,1,0:T(8,128)S(1)} %copy-done.1, f32[8,88,128]{2,1,0:T(8,128)S(1)} %copy-done.2, f32[2,15,32,128]{3,2,1,0:T(8,128)S(1)} %get-tuple-element.24.acc_ref, ...), custom_call_target="tpu_custom_call" | custom-call | bytes 25830000 | tf_op jit(solution)/shard_map/pallas_call | solution.py:517
  100.5 5.3 %all-to-all-start.1 = ((f32[16,80,128]{2,1,0:T(8,128)}), f32[16,80,128]{2,1,0:T(8,128)S(1)}, u32[]{:S(2)}, u32[]{:S(2)}) async-start(f32[16,80,128]{2,1,0:T(8,128)} %shard_map.93), calls=%async_computation.1 | async-start | bytes 1310720 | tf_op jit(solution)/shard_map/all_to_all | solution.py:474
  105.8 1.1 shard_map.91.den_ref
  106.9 15.8 %all-to-all-done.1.sums = f32[16,80,128]{2,1,0:T(8,128)S(1)} async-done(((f32[16,80,128]{2,1,0:T(8,128)}), f32[16,80,128]{2,1,0:T(8,128)S(1)}, u32[]{:S(2)}, u32[]{:S(2)}) %all-to-all-start.1) | async-done | bytes 655392 | tf_op jit(solution)/shard_map/all_to_all | solution.py:474
  122.7 1.0 shard_map.94.rest_0_.rest_8_
  123.8 0.5 collective-permute-start.36
  124.4 1.6 %collective-permute-start.33 = (f32[328,128]{1,0:T(8,128)S(1)}, f32[328,128]{1,0:T(8,128)S(1)}, u32[]{:S(2)}, u32[]{:S(2)}) collective-permute-start(f32[328,128]{1,0:T(8,128)S(1)} %shard_map.94.rest_0_.rest_8_), channel_id=1, source_target_pairs={{0,2},{1,3},{2,0},{3,1},{4,6},{5,7},{6,4},{7,5},{8,10},{9,11},{10,... | collective-permute-start | bytes 503816 | tf_op jit(solution)/shard_map/ppermute | solution.py:479
  126.0 1.1 collective-permute-start.32
  127.0 2.8 %collective-permute-done.30.rest_4_.rest_12_ = f32[328,128]{1,0:T(8,128)S(1)} collective-permute-done((f32[328,128]{1,0:T(8,128)S(1)}, f32[328,128]{1,0:T(8,128)S(1)}, u32[]{:S(2)}, u32[]{:S(2)}) %collective-permute-start.30) | collective-permute-done | bytes 167968 | tf_op jit(solution)/shard_map/ppermute | solution.py:479
  130.2 0.7 collective-permute-done.36.rest_6_.rest_14_
  130.9 2.4 %collective-permute-start.39 = (f32[328,128]{1,0:T(8,128)S(1)}, f32[328,128]{1,0:T(8,128)S(1)}, u32[]{:S(2)}, u32[]{:S(2)}) collective-permute-start(f32[328,128]{1,0:T(8,128)S(1)} %collective-permute-done.36.rest_6_.rest_14_), channel_id=1, source_target_pairs={{0,4},{1,5},{2,6},{3,7},{4,0},{5,1},{6,2},{7,3},{8,12},{9,13},{10,... | collective-permute-start | bytes 503816 | tf_op jit(solution)/shard_map/ppermute | solution.py:479
  133.3 2.2 %collective-permute-start.35 = (f32[328,128]{1,0:T(8,128)S(1)}, f32[328,128]{1,0:T(8,128)S(1)}, u32[]{:S(2)}, u32[]{:S(2)}) collective-permute-start(f32[328,128]{1,0:T(8,128)S(1)} %collective-permute-done.30.rest_4_.rest_12_), channel_id=1, source_target_pairs={{0,1},{1,0},{2,3},{3,2},{4,5},{5,4},{6,7},{7,6},{8,9},{9,8},{10,11... | collective-permute-start | bytes 503816 | tf_op jit(solution)/shard_map/ppermute | solution.py:479
  135.6 0.5 collective-permute-start.37
  136.1 0.6 collective-permute-start.43
  136.7 1.0 collective-permute-start.41
  137.7 4.9 %shard_map.95 = (f32[2,15,32,128]{3,2,1,0:T(8,128)S(1)}, f32[4,88,128]{2,1,0:T(8,128)}, f32[4,88,128]{2,1,0:T(8,128)}, f32[328,128]{1,0:T(8,128)S(1)}) custom-call(s32[15]{0:T(128)S(1)} %copy-done.3, s32[15]{0:T(128)S(1)} %copy-done.4, bf16[40,2,15,32,128]{4,3,2,1,0:T(8,128)(2,1)} %model_hbm.11, ...), custom_call_target="tpu_custom_call", output_to_operand_aliasing={{3}: (4, {})} | custom-call | bytes 3690000 | tf_op jit(solution)/shard_map/pallas_call | solution.py:517
  142.6 3.0 %collective-permute-start.38 = (f32[328,128]{1,0:T(8,128)S(1)}, f32[328,128]{1,0:T(8,128)S(1)}, u32[]{:S(2)}, u32[]{:S(2)}) collective-permute-start(f32[328,128]{1,0:T(8,128)S(1)} %get-tuple-element.29.rest_0_), channel_id=1, source_target_pairs={{0,1},{1,0},{2,3},{3,2},{4,5},{5,4},{6,7},{7,6},{8,9},{9,8},{10,11... | collective-permute-start | bytes 503816 | tf_op jit(solution)/shard_map/ppermute | solution.py:479
  145.7 0.4 collective-permute-start.44
  147.5 5.0 %shard_map.96 = (f32[2,15,32,128]{3,2,1,0:T(8,128)}, f32[2,160,128]{2,1,0:T(8,128)}) custom-call(s32[15]{0:T(128)S(1)} %copy-done.3, s32[15]{0:T(128)S(1)} %copy-done.4, bf16[40,2,15,32,128]{4,3,2,1,0:T(8,128)(2,1)} %model_hbm.11, s32[15,32,128]{2,1,0:T(8,128)S(1)} %copy-done.1, f32[2,15,32,128]{3,2,1,0:T(8,128)S(1)} %get-tuple-element.28.acc_ref, ...), custom_call_target="tpu_custom_call" | custom-call | bytes 14760000 | tf_op jit(solution)/shard_map/pallas_call | solution.py:517
  (66 shorter events, 5.7 us)
Async XLA Ops:
  1.7 5.2 %collective-permute-start.3 = (f32[328,128]{1,0:T(8,128)S(1)}, f32[328,128]{1,0:T(8,128)S(1)}, u32[]{:S(2)}, u32[]{:S(2)}) collective-permute-start(f32[328,128]{1,0:T(8,128)S(1)} %shard_map.86.rest_0_), channel_id=1, source_target_pairs={{0,4},{1,5},{2,6},{3,7},{4,0},{5,1},{6,2},{7,3},{8,12},{9,13},{10,... | collective-permute-start | bytes 503816 | tf_op jit(solution)/shard_map/ppermute | solution.py:479
  1.8 6.4 %collective-permute-start.7 = (f32[328,128]{1,0:T(8,128)S(1)}, f32[328,128]{1,0:T(8,128)S(1)}, u32[]{:S(2)}, u32[]{:S(2)}) collective-permute-start(f32[328,128]{1,0:T(8,128)S(1)} %shard_map.86.rest_0_), channel_id=1, source_target_pairs={{0,12},{1,13},{2,14},{3,15},{4,8},{5,9},{6,10},{7,11},{8,4},{9,5},... | collective-permute-start | bytes 503816 | tf_op jit(solution)/shard_map/ppermute | solution.py:479
  4.4 10.3 %collective-permute-start.1 = (f32[328,128]{1,0:T(8,128)S(1)}, f32[328,128]{1,0:T(8,128)S(1)}, u32[]{:S(2)}, u32[]{:S(2)}) collective-permute-start(f32[328,128]{1,0:T(8,128)S(1)} %shard_map.86.rest_0_), channel_id=1, source_target_pairs={{0,2},{1,3},{2,0},{3,1},{4,6},{5,7},{6,4},{7,5},{8,10},{9,11},{10,... | collective-permute-start | bytes 503816 | tf_op jit(solution)/shard_map/ppermute | solution.py:479
  7.0 8.2 %collective-permute-start.5 = (f32[328,128]{1,0:T(8,128)S(1)}, f32[328,128]{1,0:T(8,128)S(1)}, u32[]{:S(2)}, u32[]{:S(2)}) collective-permute-start(f32[328,128]{1,0:T(8,128)S(1)} %collective-permute-done.3.rest_4_), channel_id=1, source_target_pairs={{0,2},{1,3},{2,0},{3,1},{4,6},{5,7},{6,4},{7,5},{8,10},{9,11},{10,... | collective-permute-start | bytes 503816 | tf_op jit(solution)/shard_map/ppermute | solution.py:479
  8.2 8.2 %collective-permute-start.8 = (f32[328,128]{1,0:T(8,128)S(1)}, f32[328,128]{1,0:T(8,128)S(1)}, u32[]{:S(2)}, u32[]{:S(2)}) collective-permute-start(f32[328,128]{1,0:T(8,128)S(1)} %collective-permute-done.7.rest_12_), channel_id=1, source_target_pairs={{0,4},{1,5},{2,6},{3,7},{4,0},{5,1},{6,2},{7,3},{8,12},{9,13},{10,... | collective-permute-start | bytes 503816 | tf_op jit(solution)/shard_map/ppermute | solution.py:479
  12.8 7.5 %collective-permute-start = (f32[328,128]{1,0:T(8,128)S(1)}, f32[328,128]{1,0:T(8,128)S(1)}, u32[]{:S(2)}, u32[]{:S(2)}) collective-permute-start(f32[328,128]{1,0:T(8,128)S(1)} %shard_map.86.rest_0_), channel_id=1, source_target_pairs={{0,1},{1,0},{2,3},{3,2},{4,5},{5,4},{6,7},{7,6},{8,9},{9,8},{10,11... | collective-permute-start | bytes 503816 | tf_op jit(solution)/shard_map/ppermute | solution.py:479
  14.7 9.0 %collective-permute-start.2 = (f32[328,128]{1,0:T(8,128)S(1)}, f32[328,128]{1,0:T(8,128)S(1)}, u32[]{:S(2)}, u32[]{:S(2)}) collective-permute-start(f32[328,128]{1,0:T(8,128)S(1)} %collective-permute-done.1.rest_2_), channel_id=1, source_target_pairs={{0,1},{1,0},{2,3},{3,2},{4,5},{5,4},{6,7},{7,6},{8,9},{9,8},{10,11... | collective-permute-start | bytes 503816 | tf_op jit(solution)/shard_map/ppermute | solution.py:479
  14.7 9.1 %collective-permute-start.4 = (f32[328,128]{1,0:T(8,128)S(1)}, f32[328,128]{1,0:T(8,128)S(1)}, u32[]{:S(2)}, u32[]{:S(2)}) collective-permute-start(f32[328,128]{1,0:T(8,128)S(1)} %collective-permute-done.3.rest_4_), channel_id=1, source_target_pairs={{0,1},{1,0},{2,3},{3,2},{4,5},{5,4},{6,7},{7,6},{8,9},{9,8},{10,11... | collective-permute-start | bytes 503816 | tf_op jit(solution)/shard_map/ppermute | solution.py:479
  15.2 9.0 %collective-permute-start.13 = (f32[328,128]{1,0:T(8,128)S(1)}, f32[328,128]{1,0:T(8,128)S(1)}, u32[]{:S(2)}, u32[]{:S(2)}) collective-permute-start(f32[328,128]{1,0:T(8,128)S(1)} %collective-permute-done.7.rest_12_), channel_id=1, source_target_pairs={{0,2},{1,3},{2,0},{3,1},{4,6},{5,7},{6,4},{7,5},{8,10},{9,11},{10,... | collective-permute-start | bytes 503816 | tf_op jit(solution)/shard_map/ppermute | solution.py:479
  16.4 8.3 %collective-permute-start.10 = (f32[328,128]{1,0:T(8,128)S(1)}, f32[328,128]{1,0:T(8,128)S(1)}, u32[]{:S(2)}, u32[]{:S(2)}) collective-permute-start(f32[328,128]{1,0:T(8,128)S(1)} %collective-permute-done.8.rest_8_), channel_id=1, source_target_pairs={{0,2},{1,3},{2,0},{3,1},{4,6},{5,7},{6,4},{7,5},{8,10},{9,11},{10,... | collective-permute-start | bytes 503816 | tf_op jit(solution)/shard_map/ppermute | solution.py:479
  20.3 63.5 %copy-start = (f32[2,15,32,128]{3,2,1,0:T(8,128)S(1)}, f32[2,15,32,128]{3,2,1,0:T(8,128)}, u32[]{:S(2)}) copy-start(f32[2,15,32,128]{3,2,1,0:T(8,128)} %vis_ref.3) | copy-start | bytes 1474564
  20.3 5.2 %collective-permute-start.12 = (f32[328,128]{1,0:T(8,128)S(1)}, f32[328,128]{1,0:T(8,128)S(1)}, u32[]{:S(2)}, u32[]{:S(2)}) collective-permute-start(f32[328,128]{1,0:T(8,128)S(1)} %collective-permute-done.7.rest_12_), channel_id=1, source_target_pairs={{0,1},{1,0},{2,3},{3,2},{4,5},{5,4},{6,7},{7,6},{8,9},{9,8},{10,11... | collective-permute-start | bytes 503816 | tf_op jit(solution)/shard_map/ppermute | solution.py:479
  23.7 1.8 %collective-permute-start.6 = (f32[328,128]{1,0:T(8,128)S(1)}, f32[328,128]{1,0:T(8,128)S(1)}, u32[]{:S(2)}, u32[]{:S(2)}) collective-permute-start(f32[328,128]{1,0:T(8,128)S(1)} %get-tuple-element.17.rest_6_), channel_id=1, source_target_pairs={{0,1},{1,0},{2,3},{3,2},{4,5},{5,4},{6,7},{7,6},{8,9},{9,8},{10,11... | collective-permute-start | bytes 503816 | tf_op jit(solution)/shard_map/ppermute | solution.py:479
  23.8 1.7 %collective-permute-start.9 = (f32[328,128]{1,0:T(8,128)S(1)}, f32[328,128]{1,0:T(8,128)S(1)}, u32[]{:S(2)}, u32[]{:S(2)}) collective-permute-start(f32[328,128]{1,0:T(8,128)S(1)} %collective-permute-done.8.rest_8_), channel_id=1, source_target_pairs={{0,1},{1,0},{2,3},{3,2},{4,5},{5,4},{6,7},{7,6},{8,9},{9,8},{10,11... | collective-permute-start | bytes 503816 | tf_op jit(solution)/shard_map/ppermute | solution.py:479
  24.2 1.4 collective-permute-start.14
  24.7 1.8 %collective-permute-start.11 = (f32[328,128]{1,0:T(8,128)S(1)}, f32[328,128]{1,0:T(8,128)S(1)}, u32[]{:S(2)}, u32[]{:S(2)}) collective-permute-start(f32[328,128]{1,0:T(8,128)S(1)} %collective-permute-done.10.rest_10_), channel_id=1, source_target_pairs={{0,1},{1,0},{2,3},{3,2},{4,5},{5,4},{6,7},{7,6},{8,9},{9,8},{10,11... | collective-permute-start | bytes 503816 | tf_op jit(solution)/shard_map/ppermute | solution.py:479
  37.1 54.9 %copy-start.1 = (s32[15,32,128]{2,1,0:T(8,128)S(1)}, s32[15,32,128]{2,1,0:T(8,128)}, u32[]{:S(2)}) copy-start(s32[15,32,128]{2,1,0:T(8,128)} %mask_ref.3) | copy-start | bytes 737284
  68.1 6.1 %collective-permute-start.15 = (f32[328,128]{1,0:T(8,128)S(1)}, f32[328,128]{1,0:T(8,128)S(1)}, u32[]{:S(2)}, u32[]{:S(2)}) collective-permute-start(f32[328,128]{1,0:T(8,128)S(1)} %shard_map.90.g_ref.rest_0_.g_in), channel_id=1, source_target_pairs={{0,4},{1,5},{2,6},{3,7},{4,0},{5,1},{6,2},{7,3},{8,12},{9,13},{10,... | collective-permute-start | bytes 503816 | tf_op jit(solution)/shard_map/ppermute | solution.py:479
  68.3 7.2 %collective-permute-start.21 = (f32[328,128]{1,0:T(8,128)S(1)}, f32[328,128]{1,0:T(8,128)S(1)}, u32[]{:S(2)}, u32[]{:S(2)}) collective-permute-start(f32[328,128]{1,0:T(8,128)S(1)} %shard_map.90.g_ref.rest_0_.g_in), channel_id=1, source_target_pairs={{0,12},{1,13},{2,14},{3,15},{4,8},{5,9},{6,10},{7,11},{8,4},{9,5},... | collective-permute-start | bytes 503816 | tf_op jit(solution)/shard_map/ppermute | solution.py:479
  69.1 10.8 %collective-permute-start.18 = (f32[328,128]{1,0:T(8,128)S(1)}, f32[328,128]{1,0:T(8,128)S(1)}, u32[]{:S(2)}, u32[]{:S(2)}) collective-permute-start(f32[328,128]{1,0:T(8,128)S(1)} %shard_map.90.g_ref.rest_0_.g_in), channel_id=1, source_target_pairs={{0,2},{1,3},{2,0},{3,1},{4,6},{5,7},{6,4},{7,5},{8,10},{9,11},{10,... | collective-permute-start | bytes 503816 | tf_op jit(solution)/shard_map/ppermute | solution.py:479
  70.3 9.6 %collective-permute-start.17 = (f32[328,128]{1,0:T(8,128)S(1)}, f32[328,128]{1,0:T(8,128)S(1)}, u32[]{:S(2)}, u32[]{:S(2)}) collective-permute-start(f32[328,128]{1,0:T(8,128)S(1)} %shard_map.90.g_ref.rest_0_.g_in), channel_id=1, source_target_pairs={{0,1},{1,0},{2,3},{3,2},{4,5},{5,4},{6,7},{7,6},{8,9},{9,8},{10,11... | collective-permute-start | bytes 503816 | tf_op jit(solution)/shard_map/ppermute | solution.py:479
  74.2 6.2 %collective-permute-start.16 = (f32[328,128]{1,0:T(8,128)S(1)}, f32[328,128]{1,0:T(8,128)S(1)}, u32[]{:S(2)}, u32[]{:S(2)}) collective-permute-start(f32[328,128]{1,0:T(8,128)S(1)} %collective-permute-done.15.rest_4_), channel_id=1, source_target_pairs={{0,2},{1,3},{2,0},{3,1},{4,6},{5,7},{6,4},{7,5},{8,10},{9,11},{10,... | collective-permute-start | bytes 503816 | tf_op jit(solution)/shard_map/ppermute | solution.py:479
  75.5 5.5 %collective-permute-start.24 = (f32[328,128]{1,0:T(8,128)S(1)}, f32[328,128]{1,0:T(8,128)S(1)}, u32[]{:S(2)}, u32[]{:S(2)}) collective-permute-start(f32[328,128]{1,0:T(8,128)S(1)} %collective-permute-done.21.rest_6_), channel_id=1, source_target_pairs={{0,4},{1,5},{2,6},{3,7},{4,0},{5,1},{6,2},{7,3},{8,12},{9,13},{10,... | collective-permute-start | bytes 503816 | tf_op jit(solution)/shard_map/ppermute | solution.py:479
  77.7 6.0 %collective-permute-start.20 = (f32[328,128]{1,0:T(8,128)S(1)}, f32[328,128]{1,0:T(8,128)S(1)}, u32[]{:S(2)}, u32[]{:S(2)}) collective-permute-start(f32[328,128]{1,0:T(8,128)S(1)} %collective-permute-done.15.rest_4_), channel_id=1, source_target_pairs={{0,1},{1,0},{2,3},{3,2},{4,5},{5,4},{6,7},{7,6},{8,9},{9,8},{10,11... | collective-permute-start | bytes 503816 | tf_op jit(solution)/shard_map/ppermute | solution.py:479
  79.9 3.8 %collective-permute-start.19 = (f32[328,128]{1,0:T(8,128)S(1)}, f32[328,128]{1,0:T(8,128)S(1)}, u32[]{:S(2)}, u32[]{:S(2)}) collective-permute-start(f32[328,128]{1,0:T(8,128)S(1)} %collective-permute-done.18.rest_2_), channel_id=1, source_target_pairs={{0,1},{1,0},{2,3},{3,2},{4,5},{5,4},{6,7},{7,6},{8,9},{9,8},{10,11... | collective-permute-start | bytes 503816 | tf_op jit(solution)/shard_map/ppermute | solution.py:479
  79.9 3.8 %collective-permute-start.22 = (f32[328,128]{1,0:T(8,128)S(1)}, f32[328,128]{1,0:T(8,128)S(1)}, u32[]{:S(2)}, u32[]{:S(2)}) collective-permute-start(f32[328,128]{1,0:T(8,128)S(1)} %collective-permute-done.21.rest_6_), channel_id=1, source_target_pairs={{0,1},{1,0},{2,3},{3,2},{4,5},{5,4},{6,7},{7,6},{8,9},{9,8},{10,11... | collective-permute-start | bytes 503816 | tf_op jit(solution)/shard_map/ppermute | solution.py:479
  80.4 9.8 %collective-permute-start.28 = (f32[328,128]{1,0:T(8,128)S(1)}, f32[328,128]{1,0:T(8,128)S(1)}, u32[]{:S(2)}, u32[]{:S(2)}) collective-permute-start(f32[328,128]{1,0:T(8,128)S(1)} %collective-permute-done.21.rest_6_), channel_id=1, source_target_pairs={{0,2},{1,3},{2,0},{3,1},{4,6},{5,7},{6,4},{7,5},{8,10},{9,11},{10,... | collective-permute-start | bytes 503816 | tf_op jit(solution)/shard_map/ppermute | solution.py:479
  80.9 9.7 %collective-permute-start.26 = (f32[328,128]{1,0:T(8,128)S(1)}, f32[328,128]{1,0:T(8,128)S(1)}, u32[]{:S(2)}, u32[]{:S(2)}) collective-permute-start(f32[328,128]{1,0:T(8,128)S(1)} %collective-permute-done.24.rest_2_), channel_id=1, source_target_pairs={{0,2},{1,3},{2,0},{3,1},{4,6},{5,7},{6,4},{7,5},{8,10},{9,11},{10,... | collective-permute-start | bytes 503816 | tf_op jit(solution)/shard_map/ppermute | solution.py:479
  88.1 3.1 %collective-permute-start.23 = (f32[328,128]{1,0:T(8,128)S(1)}, f32[328,128]{1,0:T(8,128)S(1)}, u32[]{:S(2)}, u32[]{:S(2)}) collective-permute-start(f32[328,128]{1,0:T(8,128)S(1)} %get-tuple-element.27.rest_0_), channel_id=1, source_target_pairs={{0,1},{1,0},{2,3},{3,2},{4,5},{5,4},{6,7},{7,6},{8,9},{9,8},{10,11... | collective-permute-start | bytes 503816 | tf_op jit(solution)/shard_map/ppermute | solution.py:479
  90.1 1.4 collective-permute-start.25
  90.2 1.6 %collective-permute-start.29 = (f32[328,128]{1,0:T(8,128)S(1)}, f32[328,128]{1,0:T(8,128)S(1)}, u32[]{:S(2)}, u32[]{:S(2)}) collective-permute-start(f32[328,128]{1,0:T(8,128)S(1)} %collective-permute-done.28.rest_6_), channel_id=1, source_target_pairs={{0,1},{1,0},{2,3},{3,2},{4,5},{5,4},{6,7},{7,6},{8,9},{9,8},{10,11... | collective-permute-start | bytes 503816 | tf_op jit(solution)/shard_map/ppermute | solution.py:479
  90.6 1.4 collective-permute-start.27
  100.5 22.2 %all-to-all-start.1 = ((f32[16,80,128]{2,1,0:T(8,128)}), f32[16,80,128]{2,1,0:T(8,128)S(1)}, u32[]{:S(2)}, u32[]{:S(2)}) async-start(f32[16,80,128]{2,1,0:T(8,128)} %shard_map.93), calls=%async_computation.1 | async-start | bytes 1310720 | tf_op jit(solution)/shard_map/all_to_all | solution.py:474
  123.8 6.1 %collective-permute-start.30 = (f32[328,128]{1,0:T(8,128)S(1)}, f32[328,128]{1,0:T(8,128)S(1)}, u32[]{:S(2)}, u32[]{:S(2)}) collective-permute-start(f32[328,128]{1,0:T(8,128)S(1)} %shard_map.94.rest_0_.rest_8_), channel_id=1, source_target_pairs={{0,4},{1,5},{2,6},{3,7},{4,0},{5,1},{6,2},{7,3},{8,12},{9,13},{10,... | collective-permute-start | bytes 503816 | tf_op jit(solution)/shard_map/ppermute | solution.py:479
  123.8 7.1 %collective-permute-start.36 = (f32[328,128]{1,0:T(8,128)S(1)}, f32[328,128]{1,0:T(8,128)S(1)}, u32[]{:S(2)}, u32[]{:S(2)}) collective-permute-start(f32[328,128]{1,0:T(8,128)S(1)} %shard_map.94.rest_0_.rest_8_), channel_id=1, source_target_pairs={{0,12},{1,13},{2,14},{3,15},{4,8},{5,9},{6,10},{7,11},{8,4},{9,5},... | collective-permute-start | bytes 503816 | tf_op jit(solution)/shard_map/ppermute | solution.py:479
  124.4 11.2 %collective-permute-start.33 = (f32[328,128]{1,0:T(8,128)S(1)}, f32[328,128]{1,0:T(8,128)S(1)}, u32[]{:S(2)}, u32[]{:S(2)}) collective-permute-start(f32[328,128]{1,0:T(8,128)S(1)} %shard_map.94.rest_0_.rest_8_), channel_id=1, source_target_pairs={{0,2},{1,3},{2,0},{3,1},{4,6},{5,7},{6,4},{7,5},{8,10},{9,11},{10,... | collective-permute-start | bytes 503816 | tf_op jit(solution)/shard_map/ppermute | solution.py:479
  126.0 9.6 %collective-permute-start.32 = (f32[328,128]{1,0:T(8,128)S(1)}, f32[328,128]{1,0:T(8,128)S(1)}, u32[]{:S(2)}, u32[]{:S(2)}) collective-permute-start(f32[328,128]{1,0:T(8,128)S(1)} %shard_map.94.rest_0_.rest_8_), channel_id=1, source_target_pairs={{0,1},{1,0},{2,3},{3,2},{4,5},{5,4},{6,7},{7,6},{8,9},{9,8},{10,11... | collective-permute-start | bytes 503816 | tf_op jit(solution)/shard_map/ppermute | solution.py:479
  129.9 6.2 %collective-permute-start.31 = (f32[328,128]{1,0:T(8,128)S(1)}, f32[328,128]{1,0:T(8,128)S(1)}, u32[]{:S(2)}, u32[]{:S(2)}) collective-permute-start(f32[328,128]{1,0:T(8,128)S(1)} %collective-permute-done.30.rest_4_.rest_12_), channel_id=1, source_target_pairs={{0,2},{1,3},{2,0},{3,1},{4,6},{5,7},{6,4},{7,5},{8,10},{9,11},{10,... | collective-permute-start | bytes 503816 | tf_op jit(solution)/shard_map/ppermute | solution.py:479
  130.9 5.7 %collective-permute-start.39 = (f32[328,128]{1,0:T(8,128)S(1)}, f32[328,128]{1,0:T(8,128)S(1)}, u32[]{:S(2)}, u32[]{:S(2)}) collective-permute-start(f32[328,128]{1,0:T(8,128)S(1)} %collective-permute-done.36.rest_6_.rest_14_), channel_id=1, source_target_pairs={{0,4},{1,5},{2,6},{3,7},{4,0},{5,1},{6,2},{7,3},{8,12},{9,13},{10,... | collective-permute-start | bytes 503816 | tf_op jit(solution)/shard_map/ppermute | solution.py:479
  133.3 4.4 %collective-permute-start.35 = (f32[328,128]{1,0:T(8,128)S(1)}, f32[328,128]{1,0:T(8,128)S(1)}, u32[]{:S(2)}, u32[]{:S(2)}) collective-permute-start(f32[328,128]{1,0:T(8,128)S(1)} %collective-permute-done.30.rest_4_.rest_12_), channel_id=1, source_target_pairs={{0,1},{1,0},{2,3},{3,2},{4,5},{5,4},{6,7},{7,6},{8,9},{9,8},{10,11... | collective-permute-start | bytes 503816 | tf_op jit(solution)/shard_map/ppermute | solution.py:479
  135.6 2.1 %collective-permute-start.34 = (f32[328,128]{1,0:T(8,128)S(1)}, f32[328,128]{1,0:T(8,128)S(1)}, u32[]{:S(2)}, u32[]{:S(2)}) collective-permute-start(f32[328,128]{1,0:T(8,128)S(1)} %collective-permute-done.33.rest_2_.rest_10_), channel_id=1, source_target_pairs={{0,1},{1,0},{2,3},{3,2},{4,5},{5,4},{6,7},{7,6},{8,9},{9,8},{10,11... | collective-permute-start | bytes 503816 | tf_op jit(solution)/shard_map/ppermute | solution.py:479
  135.6 2.1 %collective-permute-start.37 = (f32[328,128]{1,0:T(8,128)S(1)}, f32[328,128]{1,0:T(8,128)S(1)}, u32[]{:S(2)}, u32[]{:S(2)}) collective-permute-start(f32[328,128]{1,0:T(8,128)S(1)} %collective-permute-done.36.rest_6_.rest_14_), channel_id=1, source_target_pairs={{0,1},{1,0},{2,3},{3,2},{4,5},{5,4},{6,7},{7,6},{8,9},{9,8},{10,11... | collective-permute-start | bytes 503816 | tf_op jit(solution)/shard_map/ppermute | solution.py:479
  136.1 9.6 %collective-permute-start.43 = (f32[328,128]{1,0:T(8,128)S(1)}, f32[328,128]{1,0:T(8,128)S(1)}, u32[]{:S(2)}, u32[]{:S(2)}) collective-permute-start(f32[328,128]{1,0:T(8,128)S(1)} %collective-permute-done.36.rest_6_.rest_14_), channel_id=1, source_target_pairs={{0,2},{1,3},{2,0},{3,1},{4,6},{5,7},{6,4},{7,5},{8,10},{9,11},{10,... | collective-permute-start | bytes 503816 | tf_op jit(solution)/shard_map/ppermute | solution.py:479
  136.7 9.5 %collective-permute-start.41 = (f32[328,128]{1,0:T(8,128)S(1)}, f32[328,128]{1,0:T(8,128)S(1)}, u32[]{:S(2)}, u32[]{:S(2)}) collective-permute-start(f32[328,128]{1,0:T(8,128)S(1)} %collective-permute-done.39.rest_2_), channel_id=1, source_target_pairs={{0,2},{1,3},{2,0},{3,1},{4,6},{5,7},{6,4},{7,5},{8,10},{9,11},{10,... | collective-permute-start | bytes 503816 | tf_op jit(solution)/shard_map/ppermute | solution.py:479
  142.6 4.0 %collective-permute-start.38 = (f32[328,128]{1,0:T(8,128)S(1)}, f32[328,128]{1,0:T(8,128)S(1)}, u32[]{:S(2)}, u32[]{:S(2)}) collective-permute-start(f32[328,128]{1,0:T(8,128)S(1)} %get-tuple-element.29.rest_0_), channel_id=1, source_target_pairs={{0,1},{1,0},{2,3},{3,2},{4,5},{5,4},{6,7},{7,6},{8,9},{9,8},{10,11... | collective-permute-start | bytes 503816 | tf_op jit(solution)/shard_map/ppermute | solution.py:479
  145.6 1.4 collective-permute-start.40
  145.7 1.6 %collective-permute-start.44 = (f32[328,128]{1,0:T(8,128)S(1)}, f32[328,128]{1,0:T(8,128)S(1)}, u32[]{:S(2)}, u32[]{:S(2)}) collective-permute-start(f32[328,128]{1,0:T(8,128)S(1)} %collective-permute-done.43.rest_6_), channel_id=1, source_target_pairs={{0,1},{1,0},{2,3},{3,2},{4,5},{5,4},{6,7},{7,6},{8,9},{9,8},{10,11... | collective-permute-start | bytes 503816 | tf_op jit(solution)/shard_map/ppermute | solution.py:479
  146.1 1.4 collective-permute-start.42
  (3 other events, 107.2 us)

commit v18 on v17

--- a/solution.py
+++ b/solution.py
@@ -386,7 +386,7 @@
 
 def early_kernel(n, dpc, first_ref, second_ref, model_hbm, vis_ref, unused_in, *rest):
     ins, rest = rest[: 2 * len(NEAR)], rest[2 * len(NEAR) :]
-    acc_ref, hre, him, unused_out, model_ref, sems = rest
+    acc_ref, unused_out, hre, him, model_ref, sems = rest
     me = lax.axis_index("bl")
     fetch = Fetch(model_hbm, model_ref, sems, [k * dpc for k in chips_of(me, NEAR)])
     products(dpc, me, first_ref, second_ref, ins, hre, him)
@@ -568,21 +568,26 @@
     def slots(got, pairs):
         return [got[2 * m + c] for m in pairs for c in (0, 1)]
 
-    def gather_near(g):
+    def gather_near(g, last):
         near = None
 
         def beside(x, got):
             nonlocal near
             args = (first, second, model, vis, x, *slots(got, NEAR))
-            outs = [shape(*vis.shape), shape(*half), shape(*half), shape(*x.shape)]
-            *near, x = call(early_kernel, args, outs, held_half, aliases={4: 3})
+            outs = [shape(*vis.shape), shape(*x.shape)]
+            if last:
+                near, x = call(early_kernel, args, outs, [half, half] + held_half, aliases={4: 1})
+            else:
+                outs += [shape(*half), shape(*half)]
+                acc, x, *tiles = call(early_kernel, args, outs, held_half, aliases={4: 1})
+                near = (acc, *tiles)
             return x
 
         got = gather(n, g, beside)
         return near, slots(got, FAR + NEAR)
 
     for step in range(1, ITERS):
-        near, got = gather_near(g)
+        near, got = gather_near(g, False)
         (den,) = call(
             prepare_kernel,
             (g, onehot, powers),
@@ -604,10 +609,10 @@
             [shape(*mine)],
             [(lots, width)] * 2,
         )
-    near, got = gather_near(g)
+    near, got = gather_near(g, True)
     residual, gains = call(
         last_kernel,
-        (first, second, model, mask, near[0], *got),
+        (first, second, model, mask, near, *got),
         [shape(*vis.shape), shape(2, *gre.shape)],
         held_half + [half] * 2,
         micros=4,

time: 155 us -> 155 us (level)
  transfers between devices with their start and end apart: 46 -> 46, of which waited for: 17 -> 15; matrix products, arithmetic and copies ran while one was open for 0% -> 0% of each run, Pallas kernels for 9% -> 9%
where the time goes in v18:
time: 155 us; the launch traced here: 153 us
  starting transfers between devices  52.7 us (34%)
  Pallas kernels  40.9 us (26%)
  blocking collectives  29.4 us (19%)
  waiting for transfers between devices  28.5 us (18%)
    ppermute x45, starting transfers between devices, send(): return lax.ppermute(x, 'bl', [(i, i ^ o) for i in range(n)])  47.4 us
    pallas_call x11, Pallas kernels, call(): pl.pallas_call(functools.partial(kernel, n, dpc), in_specs=[place(x) for...  40.9 us
    all_to_all x1, blocking collectives, exchange(): return lax.all_to_all(x, 'bl', split_axis=0, concat_axis=0, tiled=True)  29.4 us
    all_to_all x1, waiting for transfers between devices, exchange(): return lax.all_to_all(x, 'bl', split_axis=0, concat_axis=0, tiled=True)  15.8 us
    ppermute x45, waiting for transfers between devices, send(): return lax.ppermute(x, 'bl', [(i, i ^ o) for i in range(n)])  12.7 us
    all_to_all x1, starting transfers between devices, exchange(): return lax.all_to_all(x, 'bl', split_axis=0, concat_axis=0, tiled=True)  5.3 us
  transfers between devices with their start and end apart: 46, of which 15 were waited for; matrix products, arithmetic and copies ran while one was open for 0% of the time, Pallas kernels for 9%

profile of v18, /device:TPU:9, one launch (start us, length us, event | category | flops | bytes accessed | tf_op | source)
XLA Modules:
  0.0 152.6 jit_solution(2325190352478313256)
XLA Ops:
  0.7 1.1 shard_map.86.rest_0_
  1.8 2.6 %collective-permute-start.7 = (f32[328,128]{1,0:T(8,128)S(1)}, f32[328,128]{1,0:T(8,128)S(1)}, u32[]{:S(2)}, u32[]{:S(2)}) collective-permute-start(f32[328,128]{1,0:T(8,128)S(1)} %shard_map.86.rest_0_), channel_id=1, source_target_pairs={{0,12},{1,13},{2,14},{3,15},{4,8},{5,9},{6,10},{7,11},{8,4},{9,5},... | collective-permute-start | bytes 503816 | tf_op jit(solution)/shard_map/ppermute | solution.py:479
  4.4 1.2 collective-permute-start.1
  5.6 1.4 collective-permute-done.3.rest_4_
  7.0 1.2 collective-permute-start.5
  8.2 4.6 %collective-permute-start.8 = (f32[328,128]{1,0:T(8,128)S(1)}, f32[328,128]{1,0:T(8,128)S(1)}, u32[]{:S(2)}, u32[]{:S(2)}) collective-permute-start(f32[328,128]{1,0:T(8,128)S(1)} %collective-permute-done.7.rest_12_), channel_id=1, source_target_pairs={{0,4},{1,5},{2,6},{3,7},{4,0},{5,1},{6,2},{7,3},{8,12},{9,13},{10,... | collective-permute-start | bytes 503816 | tf_op jit(solution)/shard_map/ppermute | solution.py:479
  12.8 1.9 %collective-permute-start = (f32[328,128]{1,0:T(8,128)S(1)}, f32[328,128]{1,0:T(8,128)S(1)}, u32[]{:S(2)}, u32[]{:S(2)}) collective-permute-start(f32[328,128]{1,0:T(8,128)S(1)} %shard_map.86.rest_0_), channel_id=1, source_target_pairs={{0,1},{1,0},{2,3},{3,2},{4,5},{5,4},{6,7},{7,6},{8,9},{9,8},{10,11... | collective-permute-start | bytes 503816 | tf_op jit(solution)/shard_map/ppermute | solution.py:479
  14.7 0.5 collective-permute-start.4
  15.2 1.2 collective-permute-start.13
  16.8 3.5 %shard_map.87 = (f32[4,88,128]{2,1,0:T(8,128)S(1)}, f32[328,128]{1,0:T(8,128)S(1)}) custom-call(bf16[40,2,15,32,128]{4,3,2,1,0:T(8,128)(2,1)} %model_hbm.11, s32[15,32,128]{2,1,0:T(8,128)} %mask_ref.3, f32[328,128]{1,0:T(8,128)S(1)} %collective-permute-done.5.unused_in), custom_call_target="tpu_custom_call", output_to_operand_aliasing={{1}: (2, {})} | custom-call | bytes 73800000 | tf_op jit(solution)/shard_map/pallas_call | solution.py:517
  20.3 3.4 %collective-permute-start.12 = (f32[328,128]{1,0:T(8,128)S(1)}, f32[328,128]{1,0:T(8,128)S(1)}, u32[]{:S(2)}, u32[]{:S(2)}) collective-permute-start(f32[328,128]{1,0:T(8,128)S(1)} %collective-permute-done.7.rest_12_), channel_id=1, source_target_pairs={{0,1},{1,0},{2,3},{3,2},{4,5},{5,4},{6,7},{7,6},{8,9},{9,8},{10,11... | collective-permute-start | bytes 503816 | tf_op jit(solution)/shard_map/ppermute | solution.py:479
  24.7 0.8 collective-permute-start.11
  25.6 0.9 collective-permute-done.11.rest_11_
  26.8 10.3 %shard_map.89 = (f32[16,120,128]{2,1,0:T(8,128)S(1)}, f32[8,88,128]{2,1,0:T(8,128)}) custom-call(s32[15]{0:T(128)S(1)} %copy-done.3, s32[15]{0:T(128)S(1)} %copy-done.4, bf16[40,2,15,32,128]{4,3,2,1,0:T(8,128)(2,1)} %model_hbm.11, f32[2,15,32,128]{3,2,1,0:T(8,128)} %vis_ref.3, s32[15,32,128]{2,1,0:T(8,128)} %mask_ref.3, ...), custom_call_target="tpu_custom_call" | custom-call | bytes 33210000 | tf_op jit(solution)/shard_map/pallas_call | solution.py:517
  37.2 29.4 %all_to_all.10.sums = f32[16,120,128]{2,1,0:T(8,128)S(1)} all-to-all(f32[16,120,128]{2,1,0:T(8,128)S(1)} %get-tuple-element.22), channel_id=1, replica_groups=mesh['grp'=2,'bl'=16] {'bl'}, dimensions={0} | all-to-all | bytes 1966080 | tf_op jit(solution)/shard_map/all_to_all | solution.py:474
  66.6 1.6 %shard_map.90.g_ref.rest_0_.g_in = f32[328,128]{1,0:T(8,128)S(1)} custom-call(f32[328,128]{1,0:T(8,128)S(1)} %get-tuple-element.18.g_in, bf16[64,512]{1,0:T(8,128)(2,1)S(1)} %get-tuple-element.19.onehot_ref, f32[16,120,128]{2,1,0:T(8,128)S(1)} %all_to_all.10.sums), custom_call_target="tpu_custom_call" | custom-call | bytes 3690000 | tf_op jit(solution)/shard_map/pallas_call | solution.py:517
  68.3 0.8 collective-permute-start.21
  69.1 1.2 collective-permute-start.18
  70.3 1.1 collective-permute-start.17
  71.4 2.9 %collective-permute-done.15.rest_4_ = f32[328,128]{1,0:T(8,128)S(1)} collective-permute-done((f32[328,128]{1,0:T(8,128)S(1)}, f32[328,128]{1,0:T(8,128)S(1)}, u32[]{:S(2)}, u32[]{:S(2)}) %collective-permute-start.15) | collective-permute-done | bytes 167968 | tf_op jit(solution)/shard_map/ppermute | solution.py:479
  74.5 1.0 collective-permute-done.21.rest_6_
  75.5 2.2 %collective-permute-start.24 = (f32[328,128]{1,0:T(8,128)S(1)}, f32[328,128]{1,0:T(8,128)S(1)}, u32[]{:S(2)}, u32[]{:S(2)}) collective-permute-start(f32[328,128]{1,0:T(8,128)S(1)} %collective-permute-done.21.rest_6_), channel_id=1, source_target_pairs={{0,4},{1,5},{2,6},{3,7},{4,0},{5,1},{6,2},{7,3},{8,12},{9,13},{10,... | collective-permute-start | bytes 503816 | tf_op jit(solution)/shard_map/ppermute | solution.py:479
  77.7 2.2 %collective-permute-start.20 = (f32[328,128]{1,0:T(8,128)S(1)}, f32[328,128]{1,0:T(8,128)S(1)}, u32[]{:S(2)}, u32[]{:S(2)}) collective-permute-start(f32[328,128]{1,0:T(8,128)S(1)} %collective-permute-done.15.rest_4_), channel_id=1, source_target_pairs={{0,1},{1,0},{2,3},{3,2},{4,5},{5,4},{6,7},{7,6},{8,9},{9,8},{10,11... | collective-permute-start | bytes 503816 | tf_op jit(solution)/shard_map/ppermute | solution.py:479
  79.9 0.5 collective-permute-start.22
  80.4 0.5 collective-permute-start.28
  80.9 2.8 %collective-permute-start.26 = (f32[328,128]{1,0:T(8,128)S(1)}, f32[328,128]{1,0:T(8,128)S(1)}, u32[]{:S(2)}, u32[]{:S(2)}) collective-permute-start(f32[328,128]{1,0:T(8,128)S(1)} %collective-permute-done.24.rest_2_), channel_id=1, source_target_pairs={{0,2},{1,3},{2,0},{3,1},{4,6},{5,7},{6,4},{7,5},{8,10},{9,11},{10,... | collective-permute-start | bytes 503816 | tf_op jit(solution)/shard_map/ppermute | solution.py:479
  83.8 4.3 %shard_map.92 = (f32[2,15,32,128]{3,2,1,0:T(8,128)S(1)}, f32[328,128]{1,0:T(8,128)S(1)}, f32[4,88,128]{2,1,0:T(8,128)S(1)}, f32[4,88,128]{2,1,0:T(8,128)S(1)}) custom-call(s32[15]{0:T(128)S(1)} %copy-done.3, s32[15]{0:T(128)S(1)} %copy-done.4, bf16[40,2,15,32,128]{4,3,2,1,0:T(8,128)(2,1)} %model_hbm.11, ...), custom_call_target="tpu_custom_call", output_to_operand_aliasing={{1}: (4, {})} | custom-call | bytes 3690000 | tf_op jit(solution)/shard_map/pallas_call | solution.py:517
  88.1 2.0 %collective-permute-start.23 = (f32[328,128]{1,0:T(8,128)S(1)}, f32[328,128]{1,0:T(8,128)S(1)}, u32[]{:S(2)}, u32[]{:S(2)}) collective-permute-start(f32[328,128]{1,0:T(8,128)S(1)} %get-tuple-element.27.rest_0_), channel_id=1, source_target_pairs={{0,1},{1,0},{2,3},{3,2},{4,5},{5,4},{6,7},{7,6},{8,9},{9,8},{10,11... | collective-permute-start | bytes 503816 | tf_op jit(solution)/shard_map/ppermute | solution.py:479
  92.0 8.5 %shard_map.93 = f32[16,80,128]{2,1,0:T(8,128)} custom-call(s32[15]{0:T(128)S(1)} %copy-done.3, s32[15]{0:T(128)S(1)} %copy-done.4, bf16[40,2,15,32,128]{4,3,2,1,0:T(8,128)(2,1)} %model_hbm.11, s32[15,32,128]{2,1,0:T(8,128)S(1)} %copy-done.1, f32[8,88,128]{2,1,0:T(8,128)S(1)} %copy-done.2, f32[2,15,32,128]{3,2,1,0:T(8,128)S(1)} %get-tuple-element.24.acc_ref, ...), custom_call_target="tpu_custom_call" | custom-call | bytes 25830000 | tf_op jit(solution)/shard_map/pallas_call | solution.py:517
  100.5 5.3 %all-to-all-start.1 = ((f32[16,80,128]{2,1,0:T(8,128)}), f32[16,80,128]{2,1,0:T(8,128)S(1)}, u32[]{:S(2)}, u32[]{:S(2)}) async-start(f32[16,80,128]{2,1,0:T(8,128)} %shard_map.93), calls=%async_computation.1 | async-start | bytes 1310720 | tf_op jit(solution)/shard_map/all_to_all | solution.py:474
  105.8 1.1 shard_map.91.den_ref
  106.9 15.8 %all-to-all-done.1.sums = f32[16,80,128]{2,1,0:T(8,128)S(1)} async-done(((f32[16,80,128]{2,1,0:T(8,128)}), f32[16,80,128]{2,1,0:T(8,128)S(1)}, u32[]{:S(2)}, u32[]{:S(2)}) %all-to-all-start.1) | async-done | bytes 655392 | tf_op jit(solution)/shard_map/all_to_all | solution.py:474
  122.7 1.0 shard_map.94.rest_0_.rest_8_
  123.8 0.5 collective-permute-start.36
  124.4 1.6 %collective-permute-start.33 = (f32[328,128]{1,0:T(8,128)S(1)}, f32[328,128]{1,0:T(8,128)S(1)}, u32[]{:S(2)}, u32[]{:S(2)}) collective-permute-start(f32[328,128]{1,0:T(8,128)S(1)} %shard_map.94.rest_0_.rest_8_), channel_id=1, source_target_pairs={{0,2},{1,3},{2,0},{3,1},{4,6},{5,7},{6,4},{7,5},{8,10},{9,11},{10,... | collective-permute-start | bytes 503816 | tf_op jit(solution)/shard_map/ppermute | solution.py:479
  126.0 1.1 collective-permute-start.32
  127.0 2.8 %collective-permute-done.30.rest_4_.rest_12_ = f32[328,128]{1,0:T(8,128)S(1)} collective-permute-done((f32[328,128]{1,0:T(8,128)S(1)}, f32[328,128]{1,0:T(8,128)S(1)}, u32[]{:S(2)}, u32[]{:S(2)}) %collective-permute-start.30) | collective-permute-done | bytes 167968 | tf_op jit(solution)/shard_map/ppermute | solution.py:479
  130.2 0.7 collective-permute-done.36.rest_6_.rest_14_
  130.9 2.4 %collective-permute-start.39 = (f32[328,128]{1,0:T(8,128)S(1)}, f32[328,128]{1,0:T(8,128)S(1)}, u32[]{:S(2)}, u32[]{:S(2)}) collective-permute-start(f32[328,128]{1,0:T(8,128)S(1)} %collective-permute-done.36.rest_6_.rest_14_), channel_id=1, source_target_pairs={{0,4},{1,5},{2,6},{3,7},{4,0},{5,1},{6,2},{7,3},{8,12},{9,13},{10,... | collective-permute-start | bytes 503816 | tf_op jit(solution)/shard_map/ppermute | solution.py:479
  133.3 2.2 %collective-permute-start.35 = (f32[328,128]{1,0:T(8,128)S(1)}, f32[328,128]{1,0:T(8,128)S(1)}, u32[]{:S(2)}, u32[]{:S(2)}) collective-permute-start(f32[328,128]{1,0:T(8,128)S(1)} %collective-permute-done.30.rest_4_.rest_12_), channel_id=1, source_target_pairs={{0,1},{1,0},{2,3},{3,2},{4,5},{5,4},{6,7},{7,6},{8,9},{9,8},{10,11... | collective-permute-start | bytes 503816 | tf_op jit(solution)/shard_map/ppermute | solution.py:479
  135.6 0.5 collective-permute-start.37
  136.1 0.6 collective-permute-start.43
  136.7 1.0 collective-permute-start.41
  137.7 4.3 %shard_map.95 = (f32[2,15,32,128]{3,2,1,0:T(8,128)S(1)}, f32[328,128]{1,0:T(8,128)S(1)}) custom-call(s32[15]{0:T(128)S(1)} %copy-done.3, s32[15]{0:T(128)S(1)} %copy-done.4, bf16[40,2,15,32,128]{4,3,2,1,0:T(8,128)(2,1)} %model_hbm.11, f32[2,15,32,128]{3,2,1,0:T(8,128)S(1)} %copy-done, ...), custom_call_target="tpu_custom_call", output_to_operand_aliasing={{1}: (4, {})} | custom-call | bytes 3690000 | tf_op jit(solution)/shard_map/pallas_call | solution.py:517
  142.0 3.0 %collective-permute-start.38 = (f32[328,128]{1,0:T(8,128)S(1)}, f32[328,128]{1,0:T(8,128)S(1)}, u32[]{:S(2)}, u32[]{:S(2)}) collective-permute-start(f32[328,128]{1,0:T(8,128)S(1)} %get-tuple-element.29.rest_0_), channel_id=1, source_target_pairs={{0,1},{1,0},{2,3},{3,2},{4,5},{5,4},{6,7},{7,6},{8,9},{9,8},{10,11... | collective-permute-start | bytes 503816 | tf_op jit(solution)/shard_map/ppermute | solution.py:479
  145.5 0.9 collective-permute-start.42
  146.6 0.8 collective-permute-done.42.rest_5_
  147.4 5.0 %shard_map.96 = (f32[2,15,32,128]{3,2,1,0:T(8,128)}, f32[2,160,128]{2,1,0:T(8,128)}) custom-call(s32[15]{0:T(128)S(1)} %copy-done.3, s32[15]{0:T(128)S(1)} %copy-done.4, bf16[40,2,15,32,128]{4,3,2,1,0:T(8,128)(2,1)} %model_hbm.11, s32[15,32,128]{2,1,0:T(8,128)S(1)} %copy-done.1, f32[2,15,32,128]{3,2,1,0:T(8,128)S(1)} %get-tuple-element.28.acc_ref, ...), custom_call_target="tpu_custom_call" | custom-call | bytes 14760000 | tf_op jit(solution)/shard_map/pallas_call | solution.py:517
  (66 shorter events, 5.4 us)
Async XLA Ops:
  1.7 5.2 %collective-permute-start.3 = (f32[328,128]{1,0:T(8,128)S(1)}, f32[328,128]{1,0:T(8,128)S(1)}, u32[]{:S(2)}, u32[]{:S(2)}) collective-permute-start(f32[328,128]{1,0:T(8,128)S(1)} %shard_map.86.rest_0_), channel_id=1, source_target_pairs={{0,4},{1,5},{2,6},{3,7},{4,0},{5,1},{6,2},{7,3},{8,12},{9,13},{10,... | collective-permute-start | bytes 503816 | tf_op jit(solution)/shard_map/ppermute | solution.py:479
  1.8 6.4 %collective-permute-start.7 = (f32[328,128]{1,0:T(8,128)S(1)}, f32[328,128]{1,0:T(8,128)S(1)}, u32[]{:S(2)}, u32[]{:S(2)}) collective-permute-start(f32[328,128]{1,0:T(8,128)S(1)} %shard_map.86.rest_0_), channel_id=1, source_target_pairs={{0,12},{1,13},{2,14},{3,15},{4,8},{5,9},{6,10},{7,11},{8,4},{9,5},... | collective-permute-start | bytes 503816 | tf_op jit(solution)/shard_map/ppermute | solution.py:479
  4.4 10.3 %collective-permute-start.1 = (f32[328,128]{1,0:T(8,128)S(1)}, f32[328,128]{1,0:T(8,128)S(1)}, u32[]{:S(2)}, u32[]{:S(2)}) collective-permute-start(f32[328,128]{1,0:T(8,128)S(1)} %shard_map.86.rest_0_), channel_id=1, source_target_pairs={{0,2},{1,3},{2,0},{3,1},{4,6},{5,7},{6,4},{7,5},{8,10},{9,11},{10,... | collective-permute-start | bytes 503816 | tf_op jit(solution)/shard_map/ppermute | solution.py:479
  7.0 8.2 %collective-permute-start.5 = (f32[328,128]{1,0:T(8,128)S(1)}, f32[328,128]{1,0:T(8,128)S(1)}, u32[]{:S(2)}, u32[]{:S(2)}) collective-permute-start(f32[328,128]{1,0:T(8,128)S(1)} %collective-permute-done.3.rest_4_), channel_id=1, source_target_pairs={{0,2},{1,3},{2,0},{3,1},{4,6},{5,7},{6,4},{7,5},{8,10},{9,11},{10,... | collective-permute-start | bytes 503816 | tf_op jit(solution)/shard_map/ppermute | solution.py:479
  8.2 8.2 %collective-permute-start.8 = (f32[328,128]{1,0:T(8,128)S(1)}, f32[328,128]{1,0:T(8,128)S(1)}, u32[]{:S(2)}, u32[]{:S(2)}) collective-permute-start(f32[328,128]{1,0:T(8,128)S(1)} %collective-permute-done.7.rest_12_), channel_id=1, source_target_pairs={{0,4},{1,5},{2,6},{3,7},{4,0},{5,1},{6,2},{7,3},{8,12},{9,13},{10,... | collective-permute-start | bytes 503816 | tf_op jit(solution)/shard_map/ppermute | solution.py:479
  12.8 7.5 %collective-permute-start = (f32[328,128]{1,0:T(8,128)S(1)}, f32[328,128]{1,0:T(8,128)S(1)}, u32[]{:S(2)}, u32[]{:S(2)}) collective-permute-start(f32[328,128]{1,0:T(8,128)S(1)} %shard_map.86.rest_0_), channel_id=1, source_target_pairs={{0,1},{1,0},{2,3},{3,2},{4,5},{5,4},{6,7},{7,6},{8,9},{9,8},{10,11... | collective-permute-start | bytes 503816 | tf_op jit(solution)/shard_map/ppermute | solution.py:479
  14.7 9.0 %collective-permute-start.2 = (f32[328,128]{1,0:T(8,128)S(1)}, f32[328,128]{1,0:T(8,128)S(1)}, u32[]{:S(2)}, u32[]{:S(2)}) collective-permute-start(f32[328,128]{1,0:T(8,128)S(1)} %collective-permute-done.1.rest_2_), channel_id=1, source_target_pairs={{0,1},{1,0},{2,3},{3,2},{4,5},{5,4},{6,7},{7,6},{8,9},{9,8},{10,11... | collective-permute-start | bytes 503816 | tf_op jit(solution)/shard_map/ppermute | solution.py:479
  14.7 9.1 %collective-permute-start.4 = (f32[328,128]{1,0:T(8,128)S(1)}, f32[328,128]{1,0:T(8,128)S(1)}, u32[]{:S(2)}, u32[]{:S(2)}) collective-permute-start(f32[328,128]{1,0:T(8,128)S(1)} %collective-permute-done.3.rest_4_), channel_id=1, source_target_pairs={{0,1},{1,0},{2,3},{3,2},{4,5},{5,4},{6,7},{7,6},{8,9},{9,8},{10,11... | collective-permute-start | bytes 503816 | tf_op jit(solution)/shard_map/ppermute | solution.py:479
  15.2 9.0 %collective-permute-start.13 = (f32[328,128]{1,0:T(8,128)S(1)}, f32[328,128]{1,0:T(8,128)S(1)}, u32[]{:S(2)}, u32[]{:S(2)}) collective-permute-start(f32[328,128]{1,0:T(8,128)S(1)} %collective-permute-done.7.rest_12_), channel_id=1, source_target_pairs={{0,2},{1,3},{2,0},{3,1},{4,6},{5,7},{6,4},{7,5},{8,10},{9,11},{10,... | collective-permute-start | bytes 503816 | tf_op jit(solution)/shard_map/ppermute | solution.py:479
  16.4 8.3 %collective-permute-start.10 = (f32[328,128]{1,0:T(8,128)S(1)}, f32[328,128]{1,0:T(8,128)S(1)}, u32[]{:S(2)}, u32[]{:S(2)}) collective-permute-start(f32[328,128]{1,0:T(8,128)S(1)} %collective-permute-done.8.rest_8_), channel_id=1, source_target_pairs={{0,2},{1,3},{2,0},{3,1},{4,6},{5,7},{6,4},{7,5},{8,10},{9,11},{10,... | collective-permute-start | bytes 503816 | tf_op jit(solution)/shard_map/ppermute | solution.py:479
  20.3 63.5 %copy-start = (f32[2,15,32,128]{3,2,1,0:T(8,128)S(1)}, f32[2,15,32,128]{3,2,1,0:T(8,128)}, u32[]{:S(2)}) copy-start(f32[2,15,32,128]{3,2,1,0:T(8,128)} %vis_ref.3) | copy-start | bytes 1474564
  20.3 5.2 %collective-permute-start.12 = (f32[328,128]{1,0:T(8,128)S(1)}, f32[328,128]{1,0:T(8,128)S(1)}, u32[]{:S(2)}, u32[]{:S(2)}) collective-permute-start(f32[328,128]{1,0:T(8,128)S(1)} %collective-permute-done.7.rest_12_), channel_id=1, source_target_pairs={{0,1},{1,0},{2,3},{3,2},{4,5},{5,4},{6,7},{7,6},{8,9},{9,8},{10,11... | collective-permute-start | bytes 503816 | tf_op jit(solution)/shard_map/ppermute | solution.py:479
  23.7 1.8 %collective-permute-start.6 = (f32[328,128]{1,0:T(8,128)S(1)}, f32[328,128]{1,0:T(8,128)S(1)}, u32[]{:S(2)}, u32[]{:S(2)}) collective-permute-start(f32[328,128]{1,0:T(8,128)S(1)} %get-tuple-element.17.rest_6_), channel_id=1, source_target_pairs={{0,1},{1,0},{2,3},{3,2},{4,5},{5,4},{6,7},{7,6},{8,9},{9,8},{10,11... | collective-permute-start | bytes 503816 | tf_op jit(solution)/shard_map/ppermute | solution.py:479
  23.8 1.7 %collective-permute-start.9 = (f32[328,128]{1,0:T(8,128)S(1)}, f32[328,128]{1,0:T(8,128)S(1)}, u32[]{:S(2)}, u32[]{:S(2)}) collective-permute-start(f32[328,128]{1,0:T(8,128)S(1)} %collective-permute-done.8.rest_8_), channel_id=1, source_target_pairs={{0,1},{1,0},{2,3},{3,2},{4,5},{5,4},{6,7},{7,6},{8,9},{9,8},{10,11... | collective-permute-start | bytes 503816 | tf_op jit(solution)/shard_map/ppermute | solution.py:479
  24.2 1.4 collective-permute-start.14
  24.7 1.8 %collective-permute-start.11 = (f32[328,128]{1,0:T(8,128)S(1)}, f32[328,128]{1,0:T(8,128)S(1)}, u32[]{:S(2)}, u32[]{:S(2)}) collective-permute-start(f32[328,128]{1,0:T(8,128)S(1)} %collective-permute-done.10.rest_10_), channel_id=1, source_target_pairs={{0,1},{1,0},{2,3},{3,2},{4,5},{5,4},{6,7},{7,6},{8,9},{9,8},{10,11... | collective-permute-start | bytes 503816 | tf_op jit(solution)/shard_map/ppermute | solution.py:479
  37.1 54.9 %copy-start.1 = (s32[15,32,128]{2,1,0:T(8,128)S(1)}, s32[15,32,128]{2,1,0:T(8,128)}, u32[]{:S(2)}) copy-start(s32[15,32,128]{2,1,0:T(8,128)} %mask_ref.3) | copy-start | bytes 737284
  68.1 6.1 %collective-permute-start.15 = (f32[328,128]{1,0:T(8,128)S(1)}, f32[328,128]{1,0:T(8,128)S(1)}, u32[]{:S(2)}, u32[]{:S(2)}) collective-permute-start(f32[328,128]{1,0:T(8,128)S(1)} %shard_map.90.g_ref.rest_0_.g_in), channel_id=1, source_target_pairs={{0,4},{1,5},{2,6},{3,7},{4,0},{5,1},{6,2},{7,3},{8,12},{9,13},{10,... | collective-permute-start | bytes 503816 | tf_op jit(solution)/shard_map/ppermute | solution.py:479
  68.3 7.2 %collective-permute-start.21 = (f32[328,128]{1,0:T(8,128)S(1)}, f32[328,128]{1,0:T(8,128)S(1)}, u32[]{:S(2)}, u32[]{:S(2)}) collective-permute-start(f32[328,128]{1,0:T(8,128)S(1)} %shard_map.90.g_ref.rest_0_.g_in), channel_id=1, source_target_pairs={{0,12},{1,13},{2,14},{3,15},{4,8},{5,9},{6,10},{7,11},{8,4},{9,5},... | collective-permute-start | bytes 503816 | tf_op jit(solution)/shard_map/ppermute | solution.py:479
  69.1 10.8 %collective-permute-start.18 = (f32[328,128]{1,0:T(8,128)S(1)}, f32[328,128]{1,0:T(8,128)S(1)}, u32[]{:S(2)}, u32[]{:S(2)}) collective-permute-start(f32[328,128]{1,0:T(8,128)S(1)} %shard_map.90.g_ref.rest_0_.g_in), channel_id=1, source_target_pairs={{0,2},{1,3},{2,0},{3,1},{4,6},{5,7},{6,4},{7,5},{8,10},{9,11},{10,... | collective-permute-start | bytes 503816 | tf_op jit(solution)/shard_map/ppermute | solution.py:479
  70.3 9.6 %collective-permute-start.17 = (f32[328,128]{1,0:T(8,128)S(1)}, f32[328,128]{1,0:T(8,128)S(1)}, u32[]{:S(2)}, u32[]{:S(2)}) collective-permute-start(f32[328,128]{1,0:T(8,128)S(1)} %shard_map.90.g_ref.rest_0_.g_in), channel_id=1, source_target_pairs={{0,1},{1,0},{2,3},{3,2},{4,5},{5,4},{6,7},{7,6},{8,9},{9,8},{10,11... | collective-permute-start | bytes 503816 | tf_op jit(solution)/shard_map/ppermute | solution.py:479
  74.2 6.2 %collective-permute-start.16 = (f32[328,128]{1,0:T(8,128)S(1)}, f32[328,128]{1,0:T(8,128)S(1)}, u32[]{:S(2)}, u32[]{:S(2)}) collective-permute-start(f32[328,128]{1,0:T(8,128)S(1)} %collective-permute-done.15.rest_4_), channel_id=1, source_target_pairs={{0,2},{1,3},{2,0},{3,1},{4,6},{5,7},{6,4},{7,5},{8,10},{9,11},{10,... | collective-permute-start | bytes 503816 | tf_op jit(solution)/shard_map/ppermute | solution.py:479
  75.5 5.5 %collective-permute-start.24 = (f32[328,128]{1,0:T(8,128)S(1)}, f32[328,128]{1,0:T(8,128)S(1)}, u32[]{:S(2)}, u32[]{:S(2)}) collective-permute-start(f32[328,128]{1,0:T(8,128)S(1)} %collective-permute-done.21.rest_6_), channel_id=1, source_target_pairs={{0,4},{1,5},{2,6},{3,7},{4,0},{5,1},{6,2},{7,3},{8,12},{9,13},{10,... | collective-permute-start | bytes 503816 | tf_op jit(solution)/shard_map/ppermute | solution.py:479
  77.7 6.0 %collective-permute-start.20 = (f32[328,128]{1,0:T(8,128)S(1)}, f32[328,128]{1,0:T(8,128)S(1)}, u32[]{:S(2)}, u32[]{:S(2)}) collective-permute-start(f32[328,128]{1,0:T(8,128)S(1)} %collective-permute-done.15.rest_4_), channel_id=1, source_target_pairs={{0,1},{1,0},{2,3},{3,2},{4,5},{5,4},{6,7},{7,6},{8,9},{9,8},{10,11... | collective-permute-start | bytes 503816 | tf_op jit(solution)/shard_map/ppermute | solution.py:479
  79.9 3.8 %collective-permute-start.19 = (f32[328,128]{1,0:T(8,128)S(1)}, f32[328,128]{1,0:T(8,128)S(1)}, u32[]{:S(2)}, u32[]{:S(2)}) collective-permute-start(f32[328,128]{1,0:T(8,128)S(1)} %collective-permute-done.18.rest_2_), channel_id=1, source_target_pairs={{0,1},{1,0},{2,3},{3,2},{4,5},{5,4},{6,7},{7,6},{8,9},{9,8},{10,11... | collective-permute-start | bytes 503816 | tf_op jit(solution)/shard_map/ppermute | solution.py:479
  79.9 3.8 %collective-permute-start.22 = (f32[328,128]{1,0:T(8,128)S(1)}, f32[328,128]{1,0:T(8,128)S(1)}, u32[]{:S(2)}, u32[]{:S(2)}) collective-permute-start(f32[328,128]{1,0:T(8,128)S(1)} %collective-permute-done.21.rest_6_), channel_id=1, source_target_pairs={{0,1},{1,0},{2,3},{3,2},{4,5},{5,4},{6,7},{7,6},{8,9},{9,8},{10,11... | collective-permute-start | bytes 503816 | tf_op jit(solution)/shard_map/ppermute | solution.py:479
  80.4 9.8 %collective-permute-start.28 = (f32[328,128]{1,0:T(8,128)S(1)}, f32[328,128]{1,0:T(8,128)S(1)}, u32[]{:S(2)}, u32[]{:S(2)}) collective-permute-start(f32[328,128]{1,0:T(8,128)S(1)} %collective-permute-done.21.rest_6_), channel_id=1, source_target_pairs={{0,2},{1,3},{2,0},{3,1},{4,6},{5,7},{6,4},{7,5},{8,10},{9,11},{10,... | collective-permute-start | bytes 503816 | tf_op jit(solution)/shard_map/ppermute | solution.py:479
  80.9 9.7 %collective-permute-start.26 = (f32[328,128]{1,0:T(8,128)S(1)}, f32[328,128]{1,0:T(8,128)S(1)}, u32[]{:S(2)}, u32[]{:S(2)}) collective-permute-start(f32[328,128]{1,0:T(8,128)S(1)} %collective-permute-done.24.rest_2_), channel_id=1, source_target_pairs={{0,2},{1,3},{2,0},{3,1},{4,6},{5,7},{6,4},{7,5},{8,10},{9,11},{10,... | collective-permute-start | bytes 503816 | tf_op jit(solution)/shard_map/ppermute | solution.py:479
  88.1 3.1 %collective-permute-start.23 = (f32[328,128]{1,0:T(8,128)S(1)}, f32[328,128]{1,0:T(8,128)S(1)}, u32[]{:S(2)}, u32[]{:S(2)}) collective-permute-start(f32[328,128]{1,0:T(8,128)S(1)} %get-tuple-element.27.rest_0_), channel_id=1, source_target_pairs={{0,1},{1,0},{2,3},{3,2},{4,5},{5,4},{6,7},{7,6},{8,9},{9,8},{10,11... | collective-permute-start | bytes 503816 | tf_op jit(solution)/shard_map/ppermute | solution.py:479
  90.1 1.4 collective-permute-start.25
  90.2 1.6 %collective-permute-start.29 = (f32[328,128]{1,0:T(8,128)S(1)}, f32[328,128]{1,0:T(8,128)S(1)}, u32[]{:S(2)}, u32[]{:S(2)}) collective-permute-start(f32[328,128]{1,0:T(8,128)S(1)} %collective-permute-done.28.rest_6_), channel_id=1, source_target_pairs={{0,1},{1,0},{2,3},{3,2},{4,5},{5,4},{6,7},{7,6},{8,9},{9,8},{10,11... | collective-permute-start | bytes 503816 | tf_op jit(solution)/shard_map/ppermute | solution.py:479
  90.6 1.4 collective-permute-start.27
  100.5 22.2 %all-to-all-start.1 = ((f32[16,80,128]{2,1,0:T(8,128)}), f32[16,80,128]{2,1,0:T(8,128)S(1)}, u32[]{:S(2)}, u32[]{:S(2)}) async-start(f32[16,80,128]{2,1,0:T(8,128)} %shard_map.93), calls=%async_computation.1 | async-start | bytes 1310720 | tf_op jit(solution)/shard_map/all_to_all | solution.py:474
  123.8 6.1 %collective-permute-start.30 = (f32[328,128]{1,0:T(8,128)S(1)}, f32[328,128]{1,0:T(8,128)S(1)}, u32[]{:S(2)}, u32[]{:S(2)}) collective-permute-start(f32[328,128]{1,0:T(8,128)S(1)} %shard_map.94.rest_0_.rest_8_), channel_id=1, source_target_pairs={{0,4},{1,5},{2,6},{3,7},{4,0},{5,1},{6,2},{7,3},{8,12},{9,13},{10,... | collective-permute-start | bytes 503816 | tf_op jit(solution)/shard_map/ppermute | solution.py:479
  123.8 7.1 %collective-permute-start.36 = (f32[328,128]{1,0:T(8,128)S(1)}, f32[328,128]{1,0:T(8,128)S(1)}, u32[]{:S(2)}, u32[]{:S(2)}) collective-permute-start(f32[328,128]{1,0:T(8,128)S(1)} %shard_map.94.rest_0_.rest_8_), channel_id=1, source_target_pairs={{0,12},{1,13},{2,14},{3,15},{4,8},{5,9},{6,10},{7,11},{8,4},{9,5},... | collective-permute-start | bytes 503816 | tf_op jit(solution)/shard_map/ppermute | solution.py:479
  124.4 11.2 %collective-permute-start.33 = (f32[328,128]{1,0:T(8,128)S(1)}, f32[328,128]{1,0:T(8,128)S(1)}, u32[]{:S(2)}, u32[]{:S(2)}) collective-permute-start(f32[328,128]{1,0:T(8,128)S(1)} %shard_map.94.rest_0_.rest_8_), channel_id=1, source_target_pairs={{0,2},{1,3},{2,0},{3,1},{4,6},{5,7},{6,4},{7,5},{8,10},{9,11},{10,... | collective-permute-start | bytes 503816 | tf_op jit(solution)/shard_map/ppermute | solution.py:479
  126.0 9.6 %collective-permute-start.32 = (f32[328,128]{1,0:T(8,128)S(1)}, f32[328,128]{1,0:T(8,128)S(1)}, u32[]{:S(2)}, u32[]{:S(2)}) collective-permute-start(f32[328,128]{1,0:T(8,128)S(1)} %shard_map.94.rest_0_.rest_8_), channel_id=1, source_target_pairs={{0,1},{1,0},{2,3},{3,2},{4,5},{5,4},{6,7},{7,6},{8,9},{9,8},{10,11... | collective-permute-start | bytes 503816 | tf_op jit(solution)/shard_map/ppermute | solution.py:479
  129.9 6.2 %collective-permute-start.31 = (f32[328,128]{1,0:T(8,128)S(1)}, f32[328,128]{1,0:T(8,128)S(1)}, u32[]{:S(2)}, u32[]{:S(2)}) collective-permute-start(f32[328,128]{1,0:T(8,128)S(1)} %collective-permute-done.30.rest_4_.rest_12_), channel_id=1, source_target_pairs={{0,2},{1,3},{2,0},{3,1},{4,6},{5,7},{6,4},{7,5},{8,10},{9,11},{10,... | collective-permute-start | bytes 503816 | tf_op jit(solution)/shard_map/ppermute | solution.py:479
  130.9 5.7 %collective-permute-start.39 = (f32[328,128]{1,0:T(8,128)S(1)}, f32[328,128]{1,0:T(8,128)S(1)}, u32[]{:S(2)}, u32[]{:S(2)}) collective-permute-start(f32[328,128]{1,0:T(8,128)S(1)} %collective-permute-done.36.rest_6_.rest_14_), channel_id=1, source_target_pairs={{0,4},{1,5},{2,6},{3,7},{4,0},{5,1},{6,2},{7,3},{8,12},{9,13},{10,... | collective-permute-start | bytes 503816 | tf_op jit(solution)/shard_map/ppermute | solution.py:479
  133.3 4.4 %collective-permute-start.35 = (f32[328,128]{1,0:T(8,128)S(1)}, f32[328,128]{1,0:T(8,128)S(1)}, u32[]{:S(2)}, u32[]{:S(2)}) collective-permute-start(f32[328,128]{1,0:T(8,128)S(1)} %collective-permute-done.30.rest_4_.rest_12_), channel_id=1, source_target_pairs={{0,1},{1,0},{2,3},{3,2},{4,5},{5,4},{6,7},{7,6},{8,9},{9,8},{10,11... | collective-permute-start | bytes 503816 | tf_op jit(solution)/shard_map/ppermute | solution.py:479
  135.6 2.1 %collective-permute-start.34 = (f32[328,128]{1,0:T(8,128)S(1)}, f32[328,128]{1,0:T(8,128)S(1)}, u32[]{:S(2)}, u32[]{:S(2)}) collective-permute-start(f32[328,128]{1,0:T(8,128)S(1)} %collective-permute-done.33.rest_2_.rest_10_), channel_id=1, source_target_pairs={{0,1},{1,0},{2,3},{3,2},{4,5},{5,4},{6,7},{7,6},{8,9},{9,8},{10,11... | collective-permute-start | bytes 503816 | tf_op jit(solution)/shard_map/ppermute | solution.py:479
  135.6 2.1 %collective-permute-start.37 = (f32[328,128]{1,0:T(8,128)S(1)}, f32[328,128]{1,0:T(8,128)S(1)}, u32[]{:S(2)}, u32[]{:S(2)}) collective-permute-start(f32[328,128]{1,0:T(8,128)S(1)} %collective-permute-done.36.rest_6_.rest_14_), channel_id=1, source_target_pairs={{0,1},{1,0},{2,3},{3,2},{4,5},{5,4},{6,7},{7,6},{8,9},{9,8},{10,11... | collective-permute-start | bytes 503816 | tf_op jit(solution)/shard_map/ppermute | solution.py:479
  136.1 8.9 %collective-permute-start.43 = (f32[328,128]{1,0:T(8,128)S(1)}, f32[328,128]{1,0:T(8,128)S(1)}, u32[]{:S(2)}, u32[]{:S(2)}) collective-permute-start(f32[328,128]{1,0:T(8,128)S(1)} %collective-permute-done.36.rest_6_.rest_14_), channel_id=1, source_target_pairs={{0,2},{1,3},{2,0},{3,1},{4,6},{5,7},{6,4},{7,5},{8,10},{9,11},{10,... | collective-permute-start | bytes 503816 | tf_op jit(solution)/shard_map/ppermute | solution.py:479
  136.7 8.8 %collective-permute-start.41 = (f32[328,128]{1,0:T(8,128)S(1)}, f32[328,128]{1,0:T(8,128)S(1)}, u32[]{:S(2)}, u32[]{:S(2)}) collective-permute-start(f32[328,128]{1,0:T(8,128)S(1)} %collective-permute-done.39.rest_2_), channel_id=1, source_target_pairs={{0,2},{1,3},{2,0},{3,1},{4,6},{5,7},{6,4},{7,5},{8,10},{9,11},{10,... | collective-permute-start | bytes 503816 | tf_op jit(solution)/shard_map/ppermute | solution.py:479
  142.0 4.4 %collective-permute-start.38 = (f32[328,128]{1,0:T(8,128)S(1)}, f32[328,128]{1,0:T(8,128)S(1)}, u32[]{:S(2)}, u32[]{:S(2)}) collective-permute-start(f32[328,128]{1,0:T(8,128)S(1)} %get-tuple-element.29.rest_0_), channel_id=1, source_target_pairs={{0,1},{1,0},{2,3},{3,2},{4,5},{5,4},{6,7},{7,6},{8,9},{9,8},{10,11... | collective-permute-start | bytes 503816 | tf_op jit(solution)/shard_map/ppermute | solution.py:479
  144.9 1.5 collective-permute-start.40
  145.0 1.6 %collective-permute-start.44 = (f32[328,128]{1,0:T(8,128)S(1)}, f32[328,128]{1,0:T(8,128)S(1)}, u32[]{:S(2)}, u32[]{:S(2)}) collective-permute-start(f32[328,128]{1,0:T(8,128)S(1)} %collective-permute-done.43.rest_6_), channel_id=1, source_target_pairs={{0,1},{1,0},{2,3},{3,2},{4,5},{5,4},{6,7},{7,6},{8,9},{9,8},{10,11... | collective-permute-start | bytes 503816 | tf_op jit(solution)/shard_map/ppermute | solution.py:479
  145.5 2.0 %collective-permute-start.42 = (f32[328,128]{1,0:T(8,128)S(1)}, f32[328,128]{1,0:T(8,128)S(1)}, u32[]{:S(2)}, u32[]{:S(2)}) collective-permute-start(f32[328,128]{1,0:T(8,128)S(1)} %collective-permute-done.41.rest_4_), channel_id=1, source_target_pairs={{0,1},{1,0},{2,3},{3,2},{4,5},{5,4},{6,7},{7,6},{8,9},{9,8},{10,11... | collective-permute-start | bytes 503816 | tf_op jit(solution)/shard_map/ppermute | solution.py:479
  (3 other events, 107.2 us)

commit v19 on v18

--- a/solution.py
+++ b/solution.py
@@ -44,7 +44,7 @@
 
 
 TILE = 8
-PARTS = (1, 3, 7, ROWS)
+PARTS = (1, 3, 6, 9, 12, ROWS)
 
 
 def pack_kernel(n, dpc, first_hbm, second_hbm, re_hbm, im_hbm, out_ref, first_ref, second_ref, sems):

time: 155 us -> 154 us (level)
  transfers between devices with their start and end apart: 46 -> 46, of which waited for: 15 -> 13; matrix products, arithmetic and copies ran while one was open for 0% -> 0% of each run, Pallas kernels for 9% -> 8%
where the time goes in v19:
time: 154 us; the launch traced here: 152 us
  starting transfers between devices  53.3 us (35%)
  Pallas kernels  39.4 us (26%)
  blocking collectives  29.4 us (19%)
  waiting for transfers between devices  28.7 us (19%)
    ppermute x45, starting transfers between devices, send(): return lax.ppermute(x, 'bl', [(i, i ^ o) for i in range(n)])  48 us
    pallas_call x11, Pallas kernels, call(): pl.pallas_call(functools.partial(kernel, n, dpc), in_specs=[place(x) for...  39.4 us
    all_to_all x1, blocking collectives, exchange(): return lax.all_to_all(x, 'bl', split_axis=0, concat_axis=0, tiled=True)  29.4 us
    all_to_all x1, waiting for transfers between devices, exchange(): return lax.all_to_all(x, 'bl', split_axis=0, concat_axis=0, tiled=True)  15.8 us
    ppermute x45, waiting for transfers between devices, send(): return lax.ppermute(x, 'bl', [(i, i ^ o) for i in range(n)])  12.9 us
    all_to_all x1, starting transfers between devices, exchange(): return lax.all_to_all(x, 'bl', split_axis=0, concat_axis=0, tiled=True)  5.3 us
  transfers between devices with their start and end apart: 46, of which 13 were waited for; matrix products, arithmetic and copies ran while one was open for 0% of the time, Pallas kernels for 8%

profile of v19, /device:TPU:9, one launch (start us, length us, event | category | flops | bytes accessed | tf_op | source)
XLA Modules:
  0.0 151.8 jit_solution(15720426993297884311)
XLA Ops:
  0.7 1.1 shard_map.86.rest_0_
  1.8 2.6 %collective-permute-start.7 = (f32[328,128]{1,0:T(8,128)S(1)}, f32[328,128]{1,0:T(8,128)S(1)}, u32[]{:S(2)}, u32[]{:S(2)}) collective-permute-start(f32[328,128]{1,0:T(8,128)S(1)} %shard_map.86.rest_0_), channel_id=1, source_target_pairs={{0,12},{1,13},{2,14},{3,15},{4,8},{5,9},{6,10},{7,11},{8,4},{9,5},... | collective-permute-start | bytes 503816 | tf_op jit(solution)/shard_map/ppermute | solution.py:479
  4.4 1.2 collective-permute-start.1
  5.6 1.4 collective-permute-done.3.rest_4_
  7.0 1.2 collective-permute-start.5
  8.2 4.6 %collective-permute-start.8 = (f32[328,128]{1,0:T(8,128)S(1)}, f32[328,128]{1,0:T(8,128)S(1)}, u32[]{:S(2)}, u32[]{:S(2)}) collective-permute-start(f32[328,128]{1,0:T(8,128)S(1)} %collective-permute-done.7.rest_12_), channel_id=1, source_target_pairs={{0,4},{1,5},{2,6},{3,7},{4,0},{5,1},{6,2},{7,3},{8,12},{9,13},{10,... | collective-permute-start | bytes 503816 | tf_op jit(solution)/shard_map/ppermute | solution.py:479
  12.8 1.9 %collective-permute-start = (f32[328,128]{1,0:T(8,128)S(1)}, f32[328,128]{1,0:T(8,128)S(1)}, u32[]{:S(2)}, u32[]{:S(2)}) collective-permute-start(f32[328,128]{1,0:T(8,128)S(1)} %shard_map.86.rest_0_), channel_id=1, source_target_pairs={{0,1},{1,0},{2,3},{3,2},{4,5},{5,4},{6,7},{7,6},{8,9},{9,8},{10,11... | collective-permute-start | bytes 503816 | tf_op jit(solution)/shard_map/ppermute | solution.py:479
  14.7 0.5 collective-permute-start.4
  15.2 1.2 collective-permute-start.13
  16.8 3.1 %shard_map.87 = (f32[4,88,128]{2,1,0:T(8,128)S(1)}, f32[328,128]{1,0:T(8,128)S(1)}) custom-call(bf16[40,2,15,32,128]{4,3,2,1,0:T(8,128)(2,1)} %model_hbm.11, s32[15,32,128]{2,1,0:T(8,128)} %mask_ref.3, f32[328,128]{1,0:T(8,128)S(1)} %collective-permute-done.5.unused_in), custom_call_target="tpu_custom_call", output_to_operand_aliasing={{1}: (2, {})} | custom-call | bytes 73800000 | tf_op jit(solution)/shard_map/pallas_call | solution.py:517
  19.9 3.4 %collective-permute-start.12 = (f32[328,128]{1,0:T(8,128)S(1)}, f32[328,128]{1,0:T(8,128)S(1)}, u32[]{:S(2)}, u32[]{:S(2)}) collective-permute-start(f32[328,128]{1,0:T(8,128)S(1)} %collective-permute-done.7.rest_12_), channel_id=1, source_target_pairs={{0,1},{1,0},{2,3},{3,2},{4,5},{5,4},{6,7},{7,6},{8,9},{9,8},{10,11... | collective-permute-start | bytes 503816 | tf_op jit(solution)/shard_map/ppermute | solution.py:479
  23.9 0.9 collective-permute-done.10.rest_10_
  24.7 0.8 collective-permute-start.11
  25.5 1.0 collective-permute-done.11.rest_11_
  26.8 10.4 %shard_map.89 = (f32[16,120,128]{2,1,0:T(8,128)S(1)}, f32[8,88,128]{2,1,0:T(8,128)}) custom-call(s32[15]{0:T(128)S(1)} %copy-done.3, s32[15]{0:T(128)S(1)} %copy-done.4, bf16[40,2,15,32,128]{4,3,2,1,0:T(8,128)(2,1)} %model_hbm.11, f32[2,15,32,128]{3,2,1,0:T(8,128)} %vis_ref.3, s32[15,32,128]{2,1,0:T(8,128)} %mask_ref.3, ...), custom_call_target="tpu_custom_call" | custom-call | bytes 33210000 | tf_op jit(solution)/shard_map/pallas_call | solution.py:517
  37.2 29.4 %all_to_all.10.sums = f32[16,120,128]{2,1,0:T(8,128)S(1)} all-to-all(f32[16,120,128]{2,1,0:T(8,128)S(1)} %get-tuple-element.22), channel_id=1, replica_groups=mesh['grp'=2,'bl'=16] {'bl'}, dimensions={0} | all-to-all | bytes 1966080 | tf_op jit(solution)/shard_map/all_to_all | solution.py:474
  66.6 1.6 %shard_map.90.g_ref.rest_0_.g_in = f32[328,128]{1,0:T(8,128)S(1)} custom-call(f32[328,128]{1,0:T(8,128)S(1)} %get-tuple-element.18.g_in, bf16[64,512]{1,0:T(8,128)(2,1)S(1)} %get-tuple-element.19.onehot_ref, f32[16,120,128]{2,1,0:T(8,128)S(1)} %all_to_all.10.sums), custom_call_target="tpu_custom_call" | custom-call | bytes 3690000 | tf_op jit(solution)/shard_map/pallas_call | solution.py:517
  68.4 0.8 collective-permute-start.21
  69.2 1.2 collective-permute-start.18
  70.4 1.0 collective-permute-start.17
  71.4 2.9 %collective-permute-done.15.rest_4_ = f32[328,128]{1,0:T(8,128)S(1)} collective-permute-done((f32[328,128]{1,0:T(8,128)S(1)}, f32[328,128]{1,0:T(8,128)S(1)}, u32[]{:S(2)}, u32[]{:S(2)}) %collective-permute-start.15) | collective-permute-done | bytes 167968 | tf_op jit(solution)/shard_map/ppermute | solution.py:479
  74.6 1.0 collective-permute-done.21.rest_6_
  75.6 2.2 %collective-permute-start.24 = (f32[328,128]{1,0:T(8,128)S(1)}, f32[328,128]{1,0:T(8,128)S(1)}, u32[]{:S(2)}, u32[]{:S(2)}) collective-permute-start(f32[328,128]{1,0:T(8,128)S(1)} %collective-permute-done.21.rest_6_), channel_id=1, source_target_pairs={{0,4},{1,5},{2,6},{3,7},{4,0},{5,1},{6,2},{7,3},{8,12},{9,13},{10,... | collective-permute-start | bytes 503816 | tf_op jit(solution)/shard_map/ppermute | solution.py:479
  77.8 2.2 %collective-permute-start.20 = (f32[328,128]{1,0:T(8,128)S(1)}, f32[328,128]{1,0:T(8,128)S(1)}, u32[]{:S(2)}, u32[]{:S(2)}) collective-permute-start(f32[328,128]{1,0:T(8,128)S(1)} %collective-permute-done.15.rest_4_), channel_id=1, source_target_pairs={{0,1},{1,0},{2,3},{3,2},{4,5},{5,4},{6,7},{7,6},{8,9},{9,8},{10,11... | collective-permute-start | bytes 503816 | tf_op jit(solution)/shard_map/ppermute | solution.py:479
  80.0 0.5 collective-permute-start.22
  80.5 0.5 collective-permute-start.28
  81.0 2.8 %collective-permute-start.26 = (f32[328,128]{1,0:T(8,128)S(1)}, f32[328,128]{1,0:T(8,128)S(1)}, u32[]{:S(2)}, u32[]{:S(2)}) collective-permute-start(f32[328,128]{1,0:T(8,128)S(1)} %collective-permute-done.24.rest_2_), channel_id=1, source_target_pairs={{0,2},{1,3},{2,0},{3,1},{4,6},{5,7},{6,4},{7,5},{8,10},{9,11},{10,... | collective-permute-start | bytes 503816 | tf_op jit(solution)/shard_map/ppermute | solution.py:479
  83.8 4.0 %shard_map.92 = (f32[2,15,32,128]{3,2,1,0:T(8,128)S(1)}, f32[328,128]{1,0:T(8,128)S(1)}, f32[4,88,128]{2,1,0:T(8,128)S(1)}, f32[4,88,128]{2,1,0:T(8,128)S(1)}) custom-call(s32[15]{0:T(128)S(1)} %copy-done.3, s32[15]{0:T(128)S(1)} %copy-done.4, bf16[40,2,15,32,128]{4,3,2,1,0:T(8,128)(2,1)} %model_hbm.11, ...), custom_call_target="tpu_custom_call", output_to_operand_aliasing={{1}: (4, {})} | custom-call | bytes 3690000 | tf_op jit(solution)/shard_map/pallas_call | solution.py:517
  87.9 2.0 %collective-permute-start.23 = (f32[328,128]{1,0:T(8,128)S(1)}, f32[328,128]{1,0:T(8,128)S(1)}, u32[]{:S(2)}, u32[]{:S(2)}) collective-permute-start(f32[328,128]{1,0:T(8,128)S(1)} %get-tuple-element.27.rest_0_), channel_id=1, source_target_pairs={{0,1},{1,0},{2,3},{3,2},{4,5},{5,4},{6,7},{7,6},{8,9},{9,8},{10,11... | collective-permute-start | bytes 503816 | tf_op jit(solution)/shard_map/ppermute | solution.py:479
  91.8 8.2 %shard_map.93 = f32[16,80,128]{2,1,0:T(8,128)} custom-call(s32[15]{0:T(128)S(1)} %copy-done.3, s32[15]{0:T(128)S(1)} %copy-done.4, bf16[40,2,15,32,128]{4,3,2,1,0:T(8,128)(2,1)} %model_hbm.11, s32[15,32,128]{2,1,0:T(8,128)S(1)} %copy-done.1, f32[8,88,128]{2,1,0:T(8,128)S(1)} %copy-done.2, f32[2,15,32,128]{3,2,1,0:T(8,128)S(1)} %get-tuple-element.24.acc_ref, ...), custom_call_target="tpu_custom_call" | custom-call | bytes 25830000 | tf_op jit(solution)/shard_map/pallas_call | solution.py:517
  100.1 5.3 %all-to-all-start.1 = ((f32[16,80,128]{2,1,0:T(8,128)}), f32[16,80,128]{2,1,0:T(8,128)S(1)}, u32[]{:S(2)}, u32[]{:S(2)}) async-start(f32[16,80,128]{2,1,0:T(8,128)} %shard_map.93), calls=%async_computation.1 | async-start | bytes 1310720 | tf_op jit(solution)/shard_map/all_to_all | solution.py:474
  105.4 1.1 shard_map.91.den_ref
  106.4 15.8 %all-to-all-done.1.sums = f32[16,80,128]{2,1,0:T(8,128)S(1)} async-done(((f32[16,80,128]{2,1,0:T(8,128)}), f32[16,80,128]{2,1,0:T(8,128)S(1)}, u32[]{:S(2)}, u32[]{:S(2)}) %all-to-all-start.1) | async-done | bytes 655392 | tf_op jit(solution)/shard_map/all_to_all | solution.py:474
  122.3 1.0 shard_map.94.rest_0_.rest_8_
  123.4 0.5 collective-permute-start.36
  124.0 1.6 %collective-permute-start.33 = (f32[328,128]{1,0:T(8,128)S(1)}, f32[328,128]{1,0:T(8,128)S(1)}, u32[]{:S(2)}, u32[]{:S(2)}) collective-permute-start(f32[328,128]{1,0:T(8,128)S(1)} %shard_map.94.rest_0_.rest_8_), channel_id=1, source_target_pairs={{0,2},{1,3},{2,0},{3,1},{4,6},{5,7},{6,4},{7,5},{8,10},{9,11},{10,... | collective-permute-start | bytes 503816 | tf_op jit(solution)/shard_map/ppermute | solution.py:479
  125.6 1.1 collective-permute-start.32
  126.6 2.8 %collective-permute-done.30.rest_4_.rest_12_ = f32[328,128]{1,0:T(8,128)S(1)} collective-permute-done((f32[328,128]{1,0:T(8,128)S(1)}, f32[328,128]{1,0:T(8,128)S(1)}, u32[]{:S(2)}, u32[]{:S(2)}) %collective-permute-start.30) | collective-permute-done | bytes 167968 | tf_op jit(solution)/shard_map/ppermute | solution.py:479
  129.8 0.7 collective-permute-done.36.rest_6_.rest_14_
  130.5 2.4 %collective-permute-start.39 = (f32[328,128]{1,0:T(8,128)S(1)}, f32[328,128]{1,0:T(8,128)S(1)}, u32[]{:S(2)}, u32[]{:S(2)}) collective-permute-start(f32[328,128]{1,0:T(8,128)S(1)} %collective-permute-done.36.rest_6_.rest_14_), channel_id=1, source_target_pairs={{0,4},{1,5},{2,6},{3,7},{4,0},{5,1},{6,2},{7,3},{8,12},{9,13},{10,... | collective-permute-start | bytes 503816 | tf_op jit(solution)/shard_map/ppermute | solution.py:479
  132.9 2.2 %collective-permute-start.35 = (f32[328,128]{1,0:T(8,128)S(1)}, f32[328,128]{1,0:T(8,128)S(1)}, u32[]{:S(2)}, u32[]{:S(2)}) collective-permute-start(f32[328,128]{1,0:T(8,128)S(1)} %collective-permute-done.30.rest_4_.rest_12_), channel_id=1, source_target_pairs={{0,1},{1,0},{2,3},{3,2},{4,5},{5,4},{6,7},{7,6},{8,9},{9,8},{10,11... | collective-permute-start | bytes 503816 | tf_op jit(solution)/shard_map/ppermute | solution.py:479
  135.7 0.6 collective-permute-start.43
  136.2 1.0 collective-permute-start.41
  137.3 4.0 %shard_map.95 = (f32[2,15,32,128]{3,2,1,0:T(8,128)S(1)}, f32[328,128]{1,0:T(8,128)S(1)}) custom-call(s32[15]{0:T(128)S(1)} %copy-done.3, s32[15]{0:T(128)S(1)} %copy-done.4, bf16[40,2,15,32,128]{4,3,2,1,0:T(8,128)(2,1)} %model_hbm.11, f32[2,15,32,128]{3,2,1,0:T(8,128)S(1)} %copy-done, ...), custom_call_target="tpu_custom_call", output_to_operand_aliasing={{1}: (4, {})} | custom-call | bytes 3690000 | tf_op jit(solution)/shard_map/pallas_call | solution.py:517
  141.3 2.9 %collective-permute-start.38 = (f32[328,128]{1,0:T(8,128)S(1)}, f32[328,128]{1,0:T(8,128)S(1)}, u32[]{:S(2)}, u32[]{:S(2)}) collective-permute-start(f32[328,128]{1,0:T(8,128)S(1)} %get-tuple-element.29.rest_0_), channel_id=1, source_target_pairs={{0,1},{1,0},{2,3},{3,2},{4,5},{5,4},{6,7},{7,6},{8,9},{9,8},{10,11... | collective-permute-start | bytes 503816 | tf_op jit(solution)/shard_map/ppermute | solution.py:479
  144.8 1.2 collective-permute-start.42
  146.0 1.0 collective-permute-done.42.rest_5_
  147.0 4.7 %shard_map.96 = (f32[2,15,32,128]{3,2,1,0:T(8,128)}, f32[2,160,128]{2,1,0:T(8,128)}) custom-call(s32[15]{0:T(128)S(1)} %copy-done.3, s32[15]{0:T(128)S(1)} %copy-done.4, bf16[40,2,15,32,128]{4,3,2,1,0:T(8,128)(2,1)} %model_hbm.11, s32[15,32,128]{2,1,0:T(8,128)S(1)} %copy-done.1, f32[2,15,32,128]{3,2,1,0:T(8,128)S(1)} %get-tuple-element.28.acc_ref, ...), custom_call_target="tpu_custom_call" | custom-call | bytes 14760000 | tf_op jit(solution)/shard_map/pallas_call | solution.py:517
  (66 shorter events, 5.2 us)
Async XLA Ops:
  1.7 5.2 %collective-permute-start.3 = (f32[328,128]{1,0:T(8,128)S(1)}, f32[328,128]{1,0:T(8,128)S(1)}, u32[]{:S(2)}, u32[]{:S(2)}) collective-permute-start(f32[328,128]{1,0:T(8,128)S(1)} %shard_map.86.rest_0_), channel_id=1, source_target_pairs={{0,4},{1,5},{2,6},{3,7},{4,0},{5,1},{6,2},{7,3},{8,12},{9,13},{10,... | collective-permute-start | bytes 503816 | tf_op jit(solution)/shard_map/ppermute | solution.py:479
  1.8 6.4 %collective-permute-start.7 = (f32[328,128]{1,0:T(8,128)S(1)}, f32[328,128]{1,0:T(8,128)S(1)}, u32[]{:S(2)}, u32[]{:S(2)}) collective-permute-start(f32[328,128]{1,0:T(8,128)S(1)} %shard_map.86.rest_0_), channel_id=1, source_target_pairs={{0,12},{1,13},{2,14},{3,15},{4,8},{5,9},{6,10},{7,11},{8,4},{9,5},... | collective-permute-start | bytes 503816 | tf_op jit(solution)/shard_map/ppermute | solution.py:479
  4.4 10.3 %collective-permute-start.1 = (f32[328,128]{1,0:T(8,128)S(1)}, f32[328,128]{1,0:T(8,128)S(1)}, u32[]{:S(2)}, u32[]{:S(2)}) collective-permute-start(f32[328,128]{1,0:T(8,128)S(1)} %shard_map.86.rest_0_), channel_id=1, source_target_pairs={{0,2},{1,3},{2,0},{3,1},{4,6},{5,7},{6,4},{7,5},{8,10},{9,11},{10,... | collective-permute-start | bytes 503816 | tf_op jit(solution)/shard_map/ppermute | solution.py:479
  7.0 8.2 %collective-permute-start.5 = (f32[328,128]{1,0:T(8,128)S(1)}, f32[328,128]{1,0:T(8,128)S(1)}, u32[]{:S(2)}, u32[]{:S(2)}) collective-permute-start(f32[328,128]{1,0:T(8,128)S(1)} %collective-permute-done.3.rest_4_), channel_id=1, source_target_pairs={{0,2},{1,3},{2,0},{3,1},{4,6},{5,7},{6,4},{7,5},{8,10},{9,11},{10,... | collective-permute-start | bytes 503816 | tf_op jit(solution)/shard_map/ppermute | solution.py:479
  8.2 8.2 %collective-permute-start.8 = (f32[328,128]{1,0:T(8,128)S(1)}, f32[328,128]{1,0:T(8,128)S(1)}, u32[]{:S(2)}, u32[]{:S(2)}) collective-permute-start(f32[328,128]{1,0:T(8,128)S(1)} %collective-permute-done.7.rest_12_), channel_id=1, source_target_pairs={{0,4},{1,5},{2,6},{3,7},{4,0},{5,1},{6,2},{7,3},{8,12},{9,13},{10,... | collective-permute-start | bytes 503816 | tf_op jit(solution)/shard_map/ppermute | solution.py:479
  12.8 7.0 %collective-permute-start = (f32[328,128]{1,0:T(8,128)S(1)}, f32[328,128]{1,0:T(8,128)S(1)}, u32[]{:S(2)}, u32[]{:S(2)}) collective-permute-start(f32[328,128]{1,0:T(8,128)S(1)} %shard_map.86.rest_0_), channel_id=1, source_target_pairs={{0,1},{1,0},{2,3},{3,2},{4,5},{5,4},{6,7},{7,6},{8,9},{9,8},{10,11... | collective-permute-start | bytes 503816 | tf_op jit(solution)/shard_map/ppermute | solution.py:479
  14.7 8.6 %collective-permute-start.2 = (f32[328,128]{1,0:T(8,128)S(1)}, f32[328,128]{1,0:T(8,128)S(1)}, u32[]{:S(2)}, u32[]{:S(2)}) collective-permute-start(f32[328,128]{1,0:T(8,128)S(1)} %collective-permute-done.1.rest_2_), channel_id=1, source_target_pairs={{0,1},{1,0},{2,3},{3,2},{4,5},{5,4},{6,7},{7,6},{8,9},{9,8},{10,11... | collective-permute-start | bytes 503816 | tf_op jit(solution)/shard_map/ppermute | solution.py:479
  14.7 8.6 %collective-permute-start.4 = (f32[328,128]{1,0:T(8,128)S(1)}, f32[328,128]{1,0:T(8,128)S(1)}, u32[]{:S(2)}, u32[]{:S(2)}) collective-permute-start(f32[328,128]{1,0:T(8,128)S(1)} %collective-permute-done.3.rest_4_), channel_id=1, source_target_pairs={{0,1},{1,0},{2,3},{3,2},{4,5},{5,4},{6,7},{7,6},{8,9},{9,8},{10,11... | collective-permute-start | bytes 503816 | tf_op jit(solution)/shard_map/ppermute | solution.py:479
  15.2 8.6 %collective-permute-start.13 = (f32[328,128]{1,0:T(8,128)S(1)}, f32[328,128]{1,0:T(8,128)S(1)}, u32[]{:S(2)}, u32[]{:S(2)}) collective-permute-start(f32[328,128]{1,0:T(8,128)S(1)} %collective-permute-done.7.rest_12_), channel_id=1, source_target_pairs={{0,2},{1,3},{2,0},{3,1},{4,6},{5,7},{6,4},{7,5},{8,10},{9,11},{10,... | collective-permute-start | bytes 503816 | tf_op jit(solution)/shard_map/ppermute | solution.py:479
  16.4 8.3 %collective-permute-start.10 = (f32[328,128]{1,0:T(8,128)S(1)}, f32[328,128]{1,0:T(8,128)S(1)}, u32[]{:S(2)}, u32[]{:S(2)}) collective-permute-start(f32[328,128]{1,0:T(8,128)S(1)} %collective-permute-done.8.rest_8_), channel_id=1, source_target_pairs={{0,2},{1,3},{2,0},{3,1},{4,6},{5,7},{6,4},{7,5},{8,10},{9,11},{10,... | collective-permute-start | bytes 503816 | tf_op jit(solution)/shard_map/ppermute | solution.py:479
  19.8 64.0 %copy-start = (f32[2,15,32,128]{3,2,1,0:T(8,128)S(1)}, f32[2,15,32,128]{3,2,1,0:T(8,128)}, u32[]{:S(2)}) copy-start(f32[2,15,32,128]{3,2,1,0:T(8,128)} %vis_ref.3) | copy-start | bytes 1474564
  19.9 5.7 %collective-permute-start.12 = (f32[328,128]{1,0:T(8,128)S(1)}, f32[328,128]{1,0:T(8,128)S(1)}, u32[]{:S(2)}, u32[]{:S(2)}) collective-permute-start(f32[328,128]{1,0:T(8,128)S(1)} %collective-permute-done.7.rest_12_), channel_id=1, source_target_pairs={{0,1},{1,0},{2,3},{3,2},{4,5},{5,4},{6,7},{7,6},{8,9},{9,8},{10,11... | collective-permute-start | bytes 503816 | tf_op jit(solution)/shard_map/ppermute | solution.py:479
  23.2 2.3 %collective-permute-start.6 = (f32[328,128]{1,0:T(8,128)S(1)}, f32[328,128]{1,0:T(8,128)S(1)}, u32[]{:S(2)}, u32[]{:S(2)}) collective-permute-start(f32[328,128]{1,0:T(8,128)S(1)} %get-tuple-element.17.rest_6_), channel_id=1, source_target_pairs={{0,1},{1,0},{2,3},{3,2},{4,5},{5,4},{6,7},{7,6},{8,9},{9,8},{10,11... | collective-permute-start | bytes 503816 | tf_op jit(solution)/shard_map/ppermute | solution.py:479
  23.3 2.2 %collective-permute-start.9 = (f32[328,128]{1,0:T(8,128)S(1)}, f32[328,128]{1,0:T(8,128)S(1)}, u32[]{:S(2)}, u32[]{:S(2)}) collective-permute-start(f32[328,128]{1,0:T(8,128)S(1)} %collective-permute-done.8.rest_8_), channel_id=1, source_target_pairs={{0,1},{1,0},{2,3},{3,2},{4,5},{5,4},{6,7},{7,6},{8,9},{9,8},{10,11... | collective-permute-start | bytes 503816 | tf_op jit(solution)/shard_map/ppermute | solution.py:479
  23.8 1.8 %collective-permute-start.14 = (f32[328,128]{1,0:T(8,128)S(1)}, f32[328,128]{1,0:T(8,128)S(1)}, u32[]{:S(2)}, u32[]{:S(2)}) collective-permute-start(f32[328,128]{1,0:T(8,128)S(1)} %collective-permute-done.13.rest_14_), channel_id=1, source_target_pairs={{0,1},{1,0},{2,3},{3,2},{4,5},{5,4},{6,7},{7,6},{8,9},{9,8},{10,11... | collective-permute-start | bytes 503816 | tf_op jit(solution)/shard_map/ppermute | solution.py:479
  24.7 1.8 %collective-permute-start.11 = (f32[328,128]{1,0:T(8,128)S(1)}, f32[328,128]{1,0:T(8,128)S(1)}, u32[]{:S(2)}, u32[]{:S(2)}) collective-permute-start(f32[328,128]{1,0:T(8,128)S(1)} %collective-permute-done.10.rest_10_), channel_id=1, source_target_pairs={{0,1},{1,0},{2,3},{3,2},{4,5},{5,4},{6,7},{7,6},{8,9},{9,8},{10,11... | collective-permute-start | bytes 503816 | tf_op jit(solution)/shard_map/ppermute | solution.py:479
  37.2 54.6 %copy-start.1 = (s32[15,32,128]{2,1,0:T(8,128)S(1)}, s32[15,32,128]{2,1,0:T(8,128)}, u32[]{:S(2)}) copy-start(s32[15,32,128]{2,1,0:T(8,128)} %mask_ref.3) | copy-start | bytes 737284
  68.2 6.1 %collective-permute-start.15 = (f32[328,128]{1,0:T(8,128)S(1)}, f32[328,128]{1,0:T(8,128)S(1)}, u32[]{:S(2)}, u32[]{:S(2)}) collective-permute-start(f32[328,128]{1,0:T(8,128)S(1)} %shard_map.90.g_ref.rest_0_.g_in), channel_id=1, source_target_pairs={{0,4},{1,5},{2,6},{3,7},{4,0},{5,1},{6,2},{7,3},{8,12},{9,13},{10,... | collective-permute-start | bytes 503816 | tf_op jit(solution)/shard_map/ppermute | solution.py:479
  68.4 7.2 %collective-permute-start.21 = (f32[328,128]{1,0:T(8,128)S(1)}, f32[328,128]{1,0:T(8,128)S(1)}, u32[]{:S(2)}, u32[]{:S(2)}) collective-permute-start(f32[328,128]{1,0:T(8,128)S(1)} %shard_map.90.g_ref.rest_0_.g_in), channel_id=1, source_target_pairs={{0,12},{1,13},{2,14},{3,15},{4,8},{5,9},{6,10},{7,11},{8,4},{9,5},... | collective-permute-start | bytes 503816 | tf_op jit(solution)/shard_map/ppermute | solution.py:479
  69.2 10.8 %collective-permute-start.18 = (f32[328,128]{1,0:T(8,128)S(1)}, f32[328,128]{1,0:T(8,128)S(1)}, u32[]{:S(2)}, u32[]{:S(2)}) collective-permute-start(f32[328,128]{1,0:T(8,128)S(1)} %shard_map.90.g_ref.rest_0_.g_in), channel_id=1, source_target_pairs={{0,2},{1,3},{2,0},{3,1},{4,6},{5,7},{6,4},{7,5},{8,10},{9,11},{10,... | collective-permute-start | bytes 503816 | tf_op jit(solution)/shard_map/ppermute | solution.py:479
  70.4 9.6 %collective-permute-start.17 = (f32[328,128]{1,0:T(8,128)S(1)}, f32[328,128]{1,0:T(8,128)S(1)}, u32[]{:S(2)}, u32[]{:S(2)}) collective-permute-start(f32[328,128]{1,0:T(8,128)S(1)} %shard_map.90.g_ref.rest_0_.g_in), channel_id=1, source_target_pairs={{0,1},{1,0},{2,3},{3,2},{4,5},{5,4},{6,7},{7,6},{8,9},{9,8},{10,11... | collective-permute-start | bytes 503816 | tf_op jit(solution)/shard_map/ppermute | solution.py:479
  74.3 6.2 %collective-permute-start.16 = (f32[328,128]{1,0:T(8,128)S(1)}, f32[328,128]{1,0:T(8,128)S(1)}, u32[]{:S(2)}, u32[]{:S(2)}) collective-permute-start(f32[328,128]{1,0:T(8,128)S(1)} %collective-permute-done.15.rest_4_), channel_id=1, source_target_pairs={{0,2},{1,3},{2,0},{3,1},{4,6},{5,7},{6,4},{7,5},{8,10},{9,11},{10,... | collective-permute-start | bytes 503816 | tf_op jit(solution)/shard_map/ppermute | solution.py:479
  75.6 5.5 %collective-permute-start.24 = (f32[328,128]{1,0:T(8,128)S(1)}, f32[328,128]{1,0:T(8,128)S(1)}, u32[]{:S(2)}, u32[]{:S(2)}) collective-permute-start(f32[328,128]{1,0:T(8,128)S(1)} %collective-permute-done.21.rest_6_), channel_id=1, source_target_pairs={{0,4},{1,5},{2,6},{3,7},{4,0},{5,1},{6,2},{7,3},{8,12},{9,13},{10,... | collective-permute-start | bytes 503816 | tf_op jit(solution)/shard_map/ppermute | solution.py:479
  77.8 6.0 %collective-permute-start.20 = (f32[328,128]{1,0:T(8,128)S(1)}, f32[328,128]{1,0:T(8,128)S(1)}, u32[]{:S(2)}, u32[]{:S(2)}) collective-permute-start(f32[328,128]{1,0:T(8,128)S(1)} %collective-permute-done.15.rest_4_), channel_id=1, source_target_pairs={{0,1},{1,0},{2,3},{3,2},{4,5},{5,4},{6,7},{7,6},{8,9},{9,8},{10,11... | collective-permute-start | bytes 503816 | tf_op jit(solution)/shard_map/ppermute | solution.py:479
  80.0 3.8 %collective-permute-start.19 = (f32[328,128]{1,0:T(8,128)S(1)}, f32[328,128]{1,0:T(8,128)S(1)}, u32[]{:S(2)}, u32[]{:S(2)}) collective-permute-start(f32[328,128]{1,0:T(8,128)S(1)} %collective-permute-done.18.rest_2_), channel_id=1, source_target_pairs={{0,1},{1,0},{2,3},{3,2},{4,5},{5,4},{6,7},{7,6},{8,9},{9,8},{10,11... | collective-permute-start | bytes 503816 | tf_op jit(solution)/shard_map/ppermute | solution.py:479
  80.0 3.8 %collective-permute-start.22 = (f32[328,128]{1,0:T(8,128)S(1)}, f32[328,128]{1,0:T(8,128)S(1)}, u32[]{:S(2)}, u32[]{:S(2)}) collective-permute-start(f32[328,128]{1,0:T(8,128)S(1)} %collective-permute-done.21.rest_6_), channel_id=1, source_target_pairs={{0,1},{1,0},{2,3},{3,2},{4,5},{5,4},{6,7},{7,6},{8,9},{9,8},{10,11... | collective-permute-start | bytes 503816 | tf_op jit(solution)/shard_map/ppermute | solution.py:479
  80.5 9.5 %collective-permute-start.28 = (f32[328,128]{1,0:T(8,128)S(1)}, f32[328,128]{1,0:T(8,128)S(1)}, u32[]{:S(2)}, u32[]{:S(2)}) collective-permute-start(f32[328,128]{1,0:T(8,128)S(1)} %collective-permute-done.21.rest_6_), channel_id=1, source_target_pairs={{0,2},{1,3},{2,0},{3,1},{4,6},{5,7},{6,4},{7,5},{8,10},{9,11},{10,... | collective-permute-start | bytes 503816 | tf_op jit(solution)/shard_map/ppermute | solution.py:479
  81.0 9.4 %collective-permute-start.26 = (f32[328,128]{1,0:T(8,128)S(1)}, f32[328,128]{1,0:T(8,128)S(1)}, u32[]{:S(2)}, u32[]{:S(2)}) collective-permute-start(f32[328,128]{1,0:T(8,128)S(1)} %collective-permute-done.24.rest_2_), channel_id=1, source_target_pairs={{0,2},{1,3},{2,0},{3,1},{4,6},{5,7},{6,4},{7,5},{8,10},{9,11},{10,... | collective-permute-start | bytes 503816 | tf_op jit(solution)/shard_map/ppermute | solution.py:479
  87.9 3.1 %collective-permute-start.23 = (f32[328,128]{1,0:T(8,128)S(1)}, f32[328,128]{1,0:T(8,128)S(1)}, u32[]{:S(2)}, u32[]{:S(2)}) collective-permute-start(f32[328,128]{1,0:T(8,128)S(1)} %get-tuple-element.27.rest_0_), channel_id=1, source_target_pairs={{0,1},{1,0},{2,3},{3,2},{4,5},{5,4},{6,7},{7,6},{8,9},{9,8},{10,11... | collective-permute-start | bytes 503816 | tf_op jit(solution)/shard_map/ppermute | solution.py:479
  89.9 1.4 collective-permute-start.25
  90.0 1.6 %collective-permute-start.29 = (f32[328,128]{1,0:T(8,128)S(1)}, f32[328,128]{1,0:T(8,128)S(1)}, u32[]{:S(2)}, u32[]{:S(2)}) collective-permute-start(f32[328,128]{1,0:T(8,128)S(1)} %collective-permute-done.28.rest_6_), channel_id=1, source_target_pairs={{0,1},{1,0},{2,3},{3,2},{4,5},{5,4},{6,7},{7,6},{8,9},{9,8},{10,11... | collective-permute-start | bytes 503816 | tf_op jit(solution)/shard_map/ppermute | solution.py:479
  90.4 1.4 collective-permute-start.27
  100.1 22.2 %all-to-all-start.1 = ((f32[16,80,128]{2,1,0:T(8,128)}), f32[16,80,128]{2,1,0:T(8,128)S(1)}, u32[]{:S(2)}, u32[]{:S(2)}) async-start(f32[16,80,128]{2,1,0:T(8,128)} %shard_map.93), calls=%async_computation.1 | async-start | bytes 1310720 | tf_op jit(solution)/shard_map/all_to_all | solution.py:474
  123.3 6.1 %collective-permute-start.30 = (f32[328,128]{1,0:T(8,128)S(1)}, f32[328,128]{1,0:T(8,128)S(1)}, u32[]{:S(2)}, u32[]{:S(2)}) collective-permute-start(f32[328,128]{1,0:T(8,128)S(1)} %shard_map.94.rest_0_.rest_8_), channel_id=1, source_target_pairs={{0,4},{1,5},{2,6},{3,7},{4,0},{5,1},{6,2},{7,3},{8,12},{9,13},{10,... | collective-permute-start | bytes 503816 | tf_op jit(solution)/shard_map/ppermute | solution.py:479
  123.4 7.1 %collective-permute-start.36 = (f32[328,128]{1,0:T(8,128)S(1)}, f32[328,128]{1,0:T(8,128)S(1)}, u32[]{:S(2)}, u32[]{:S(2)}) collective-permute-start(f32[328,128]{1,0:T(8,128)S(1)} %shard_map.94.rest_0_.rest_8_), channel_id=1, source_target_pairs={{0,12},{1,13},{2,14},{3,15},{4,8},{5,9},{6,10},{7,11},{8,4},{9,5},... | collective-permute-start | bytes 503816 | tf_op jit(solution)/shard_map/ppermute | solution.py:479
  124.0 11.2 %collective-permute-start.33 = (f32[328,128]{1,0:T(8,128)S(1)}, f32[328,128]{1,0:T(8,128)S(1)}, u32[]{:S(2)}, u32[]{:S(2)}) collective-permute-start(f32[328,128]{1,0:T(8,128)S(1)} %shard_map.94.rest_0_.rest_8_), channel_id=1, source_target_pairs={{0,2},{1,3},{2,0},{3,1},{4,6},{5,7},{6,4},{7,5},{8,10},{9,11},{10,... | collective-permute-start | bytes 503816 | tf_op jit(solution)/shard_map/ppermute | solution.py:479
  125.6 9.6 %collective-permute-start.32 = (f32[328,128]{1,0:T(8,128)S(1)}, f32[328,128]{1,0:T(8,128)S(1)}, u32[]{:S(2)}, u32[]{:S(2)}) collective-permute-start(f32[328,128]{1,0:T(8,128)S(1)} %shard_map.94.rest_0_.rest_8_), channel_id=1, source_target_pairs={{0,1},{1,0},{2,3},{3,2},{4,5},{5,4},{6,7},{7,6},{8,9},{9,8},{10,11... | collective-permute-start | bytes 503816 | tf_op jit(solution)/shard_map/ppermute | solution.py:479
  129.5 6.2 %collective-permute-start.31 = (f32[328,128]{1,0:T(8,128)S(1)}, f32[328,128]{1,0:T(8,128)S(1)}, u32[]{:S(2)}, u32[]{:S(2)}) collective-permute-start(f32[328,128]{1,0:T(8,128)S(1)} %collective-permute-done.30.rest_4_.rest_12_), channel_id=1, source_target_pairs={{0,2},{1,3},{2,0},{3,1},{4,6},{5,7},{6,4},{7,5},{8,10},{9,11},{10,... | collective-permute-start | bytes 503816 | tf_op jit(solution)/shard_map/ppermute | solution.py:479
  130.5 5.7 %collective-permute-start.39 = (f32[328,128]{1,0:T(8,128)S(1)}, f32[328,128]{1,0:T(8,128)S(1)}, u32[]{:S(2)}, u32[]{:S(2)}) collective-permute-start(f32[328,128]{1,0:T(8,128)S(1)} %collective-permute-done.36.rest_6_.rest_14_), channel_id=1, source_target_pairs={{0,4},{1,5},{2,6},{3,7},{4,0},{5,1},{6,2},{7,3},{8,12},{9,13},{10,... | collective-permute-start | bytes 503816 | tf_op jit(solution)/shard_map/ppermute | solution.py:479
  132.9 4.4 %collective-permute-start.35 = (f32[328,128]{1,0:T(8,128)S(1)}, f32[328,128]{1,0:T(8,128)S(1)}, u32[]{:S(2)}, u32[]{:S(2)}) collective-permute-start(f32[328,128]{1,0:T(8,128)S(1)} %collective-permute-done.30.rest_4_.rest_12_), channel_id=1, source_target_pairs={{0,1},{1,0},{2,3},{3,2},{4,5},{5,4},{6,7},{7,6},{8,9},{9,8},{10,11... | collective-permute-start | bytes 503816 | tf_op jit(solution)/shard_map/ppermute | solution.py:479
  135.1 2.1 %collective-permute-start.34 = (f32[328,128]{1,0:T(8,128)S(1)}, f32[328,128]{1,0:T(8,128)S(1)}, u32[]{:S(2)}, u32[]{:S(2)}) collective-permute-start(f32[328,128]{1,0:T(8,128)S(1)} %collective-permute-done.33.rest_2_.rest_10_), channel_id=1, source_target_pairs={{0,1},{1,0},{2,3},{3,2},{4,5},{5,4},{6,7},{7,6},{8,9},{9,8},{10,11... | collective-permute-start | bytes 503816 | tf_op jit(solution)/shard_map/ppermute | solution.py:479
  135.1 2.1 %collective-permute-start.37 = (f32[328,128]{1,0:T(8,128)S(1)}, f32[328,128]{1,0:T(8,128)S(1)}, u32[]{:S(2)}, u32[]{:S(2)}) collective-permute-start(f32[328,128]{1,0:T(8,128)S(1)} %collective-permute-done.36.rest_6_.rest_14_), channel_id=1, source_target_pairs={{0,1},{1,0},{2,3},{3,2},{4,5},{5,4},{6,7},{7,6},{8,9},{9,8},{10,11... | collective-permute-start | bytes 503816 | tf_op jit(solution)/shard_map/ppermute | solution.py:479
  135.7 8.7 %collective-permute-start.43 = (f32[328,128]{1,0:T(8,128)S(1)}, f32[328,128]{1,0:T(8,128)S(1)}, u32[]{:S(2)}, u32[]{:S(2)}) collective-permute-start(f32[328,128]{1,0:T(8,128)S(1)} %collective-permute-done.36.rest_6_.rest_14_), channel_id=1, source_target_pairs={{0,2},{1,3},{2,0},{3,1},{4,6},{5,7},{6,4},{7,5},{8,10},{9,11},{10,... | collective-permute-start | bytes 503816 | tf_op jit(solution)/shard_map/ppermute | solution.py:479
  136.2 8.5 %collective-permute-start.41 = (f32[328,128]{1,0:T(8,128)S(1)}, f32[328,128]{1,0:T(8,128)S(1)}, u32[]{:S(2)}, u32[]{:S(2)}) collective-permute-start(f32[328,128]{1,0:T(8,128)S(1)} %collective-permute-done.39.rest_2_), channel_id=1, source_target_pairs={{0,2},{1,3},{2,0},{3,1},{4,6},{5,7},{6,4},{7,5},{8,10},{9,11},{10,... | collective-permute-start | bytes 503816 | tf_op jit(solution)/shard_map/ppermute | solution.py:479
  141.3 4.7 %collective-permute-start.38 = (f32[328,128]{1,0:T(8,128)S(1)}, f32[328,128]{1,0:T(8,128)S(1)}, u32[]{:S(2)}, u32[]{:S(2)}) collective-permute-start(f32[328,128]{1,0:T(8,128)S(1)} %get-tuple-element.29.rest_0_), channel_id=1, source_target_pairs={{0,1},{1,0},{2,3},{3,2},{4,5},{5,4},{6,7},{7,6},{8,9},{9,8},{10,11... | collective-permute-start | bytes 503816 | tf_op jit(solution)/shard_map/ppermute | solution.py:479
  144.2 1.7 %collective-permute-start.40 = (f32[328,128]{1,0:T(8,128)S(1)}, f32[328,128]{1,0:T(8,128)S(1)}, u32[]{:S(2)}, u32[]{:S(2)}) collective-permute-start(f32[328,128]{1,0:T(8,128)S(1)} %collective-permute-done.39.rest_2_), channel_id=1, source_target_pairs={{0,1},{1,0},{2,3},{3,2},{4,5},{5,4},{6,7},{7,6},{8,9},{9,8},{10,11... | collective-permute-start | bytes 503816 | tf_op jit(solution)/shard_map/ppermute | solution.py:479
  144.3 1.7 %collective-permute-start.44 = (f32[328,128]{1,0:T(8,128)S(1)}, f32[328,128]{1,0:T(8,128)S(1)}, u32[]{:S(2)}, u32[]{:S(2)}) collective-permute-start(f32[328,128]{1,0:T(8,128)S(1)} %collective-permute-done.43.rest_6_), channel_id=1, source_target_pairs={{0,1},{1,0},{2,3},{3,2},{4,5},{5,4},{6,7},{7,6},{8,9},{9,8},{10,11... | collective-permute-start | bytes 503816 | tf_op jit(solution)/shard_map/ppermute | solution.py:479
  144.8 2.2 %collective-permute-start.42 = (f32[328,128]{1,0:T(8,128)S(1)}, f32[328,128]{1,0:T(8,128)S(1)}, u32[]{:S(2)}, u32[]{:S(2)}) collective-permute-start(f32[328,128]{1,0:T(8,128)S(1)} %collective-permute-done.41.rest_4_), channel_id=1, source_target_pairs={{0,1},{1,0},{2,3},{3,2},{4,5},{5,4},{6,7},{7,6},{8,9},{9,8},{10,11... | collective-permute-start | bytes 503816 | tf_op jit(solution)/shard_map/ppermute | solution.py:479
  (3 other events, 107.0 us)
